TPU v7x, 128 devices: a whole 4x4x4 slice. The times are simulated.
128 devices in a mesh: tok: 32 (over z, x, core), blk: 4 (over y).
Axes of the slice: x: 4, y: 4, z: 4, core: 2. Of those that a mesh axis runs over, the one named last changes fastest.
Arguments:
- resid: bfloat16 [16384, 8192], P('tok', 'blk'), may hold values from -2500 to 2500
- norm_gain: float32 [8192], P('blk'), may hold values from 0.25 to 1.75
- keep_index: int32 [8192], P('tok'), may hold values from 0 to 511, as said below
- counts: int32 [64], P('tok'), may hold values from 0 to 128, as said below
Outputs:
- feature_mean: float32 [8192], P('blk')
- gram_factor: float32 [8192, 8192], P('tok', 'blk')
Inputs may be any that keep to these rules, and one draw needn't show every extreme that they name: `keep_index`: the 256 entries of one index of tok are distinct row numbers among that index's 512 tokens. `counts`: the live slots of a block are its first ones, and within one index of tok each block is full before the next block has a live slot; exactly half of the 8192 slots are live; some index of tok has all its 256 slots live.
All inputs are finite; a program needn't handle non-finite values.
Results may differ from a plain program's by a relative error of at most 0.007.
Values may be sent and summed in bfloat16 or wider, within the bound.
No kernel may reach another device: no remote copies, remote signals or barrier semaphores. Data moves between devices by JAX's collectives and lax.ppermute only.
A program may use at most 192 MiB of HBM per device.

v0:
```python
import jax
import jax.numpy as jnp
from jax import lax
from jax.sharding import PartitionSpec as P

epsilon = 1e-05


def panel_product(left_rows, shard_rows):
    return lax.dot_general(
        left_rows, shard_rows, (((0,), (0,)), ((), ())), preferred_element_type=jnp.float32
    )


def per_device(resid, norm_gain, keep_index, counts):
    col_width = resid.shape[1]
    keep_rows = keep_index.shape[0]
    block_rows = keep_rows // counts.shape[0]
    full_width = col_width * lax.axis_size("blk")
    panel_rows = full_width // lax.axis_size("tok")
    picked = resid[keep_index].astype(jnp.float32)
    live_slot = jnp.arange(keep_rows, dtype=jnp.int32) % block_rows < jnp.repeat(
        counts, block_rows, total_repeat_length=keep_rows
    )
    row_sums = lax.psum(jnp.sum(picked * picked, axis=1), "blk")
    row_scale = lax.rsqrt(row_sums / full_width + epsilon)
    normed = jnp.where(
        live_slot[:, None], picked * row_scale[:, None] * norm_gain[None, :], 0.0
    ).astype(jnp.bfloat16)
    col_sum = jnp.dot(
        jnp.ones((1, keep_rows), jnp.bfloat16), normed, preferred_element_type=jnp.float32
    )[0]
    col_total, kept_total = lax.psum((col_sum, jnp.sum(counts).astype(jnp.float32)), "tok")
    feature_mean = col_total / kept_total
    row_first = lax.axis_index("tok") * panel_rows
    col_first = lax.axis_index("blk") * col_width
    panel_cols = lax.all_to_all(
        lax.all_gather(normed, "blk", axis=1, tiled=True),
        "tok",
        split_axis=1,
        concat_axis=0,
        tiled=True,
    )
    zero_tile = jnp.zeros((panel_rows, col_width), jnp.float32)
    shard_rows = lax.all_gather(normed, "tok", axis=0, tiled=True)
    left_rows = lax.slice_in_dim(panel_cols, 0, shard_rows.shape[0], axis=0)
    gram_tile = zero_tile + panel_product(left_rows, shard_rows)
    row_index = row_first + jnp.arange(panel_rows, dtype=jnp.int32)[:, None]
    col_index = col_first + jnp.arange(col_width, dtype=jnp.int32)[None, :]
    gram_factor = jnp.where(row_index <= col_index, gram_tile / kept_total, 0.0)
    return (feature_mean, gram_factor)


def solution(mesh):
    return jax.shard_map(
        per_device,
        mesh=mesh,
        in_specs=(P("tok", "blk"), P("blk"), P("tok"), P("tok")),
        out_specs=(P("blk"), P("tok", "blk")),
        check_vma=False,
    )
```

profile of v0, /device:TPU:1, one launch (start us, length us, event | category | flops | bytes accessed | tf_op | source)
XLA Modules:
  0.0 259.1 jit_solution(8862910795490816480)
XLA Ops:
  7.2 0.0 copy-start
  7.2 0.0 all-gather.3.cloned.1.call-start
  7.2 0.8 compare_select_fusion.2
  8.1 0.7 copy-done
  8.8 0.0 copy-start.3
  8.8 0.0 copy-start.2
  8.8 1.4 gather_fusion
  10.1 0.3 fusion.1
  10.4 9.6 %psum.21 = f32[256]{0:T(256)S(1)} all-reduce(f32[256]{0:T(256)S(1)} %fusion.1), channel_id=1, replica_groups=mesh['tok'=32,'blk'=4] {'blk'}, use_global_device_ids=true, to_apply=%region_1.2 | all-reduce | flops 256 | bytes 2048 | tf_op jit(solution)/shard_map/psum | solution.py:25
  20.0 0.0 copy-done.3
  20.0 0.6 fusion.11
  20.6 1.3 compare_select_fusion.1
  21.9 0.0 copy-done.2
  21.9 1.3 fusion.4
  23.3 0.0 all-gather.3.cloned.1.call-update
  23.3 0.0 all-gather.5.cloned.1.call-start
  23.3 0.7 all-gather.5.cloned.1.call-update
  24.0 49.7 %all-gather.3.cloned.1.call-done = bf16[256,8192]{1,0:T(8,128)(2,1)} async-done(((bf16[256,2048]{1,0:T(8,128)(2,1)}), bf16[256,8192]{1,0:T(8,128)(2,1)}) %all-gather.3.cloned.1.call-update) | async-done | bytes 4194320 | tf_op jit(solution)/shard_map/all_gather | solution.py:38
  73.8 4.7 %copy.9 = bf16[32,32,8,256]{3,2,0,1:T(8,128)(2,1)} copy(bf16[32,32,8,256]{3,2,1,0:T(8,128)(2,1)} %bitcast.21) | data formatting | bytes 8388608 | tf_op jit(solution)/shard_map/all_to_all | solution.py:37
  78.4 0.0 copy-start.1
  78.4 7.9 %all-to-all-start = ((bf16[256,32,256]{2,0,1:T(8,128)(2,1)}), bf16[256,32,256]{2,0,1:T(8,128)(2,1)}, u32[]{:S(2)}, u32[]{:S(2)}) async-start(bf16[256,32,256]{2,0,1:T(8,128)(2,1)} %bitcast.20), calls=%async_computation | async-start | bytes 8388608 | tf_op jit(solution)/shard_map/all_to_all | solution.py:37
  86.3 0.6 reduce_sum.19
  87.6 0.0 copy-done.1
  87.6 0.2 fusion.8
  87.9 123.9 %all-reduce = (f32[2048]{0:T(1024)S(1)}, f32[]{:T(128)}) all-reduce(f32[2048]{0:T(1024)S(1)} %bitcast.22, f32[]{:T(128)S(6)} %convert_element_type.11), channel_id=1, replica_groups=mesh['tok'=32,'blk'=4] {'tok'}, use_global_device_ids=true, to_apply=%region_2.3 | all-reduce | flops 2049 | bytes 16392 | tf_op jit(solution)/shard_map/psum | solution.py:33
  211.8 1.2 broadcast_divide_fusion
  213.0 0.0 all-to-all-done
  213.0 21.4 %all-gather.5.cloned.1.call-done = bf16[8192,2048]{1,0:T(8,128)(2,1)} async-done(((bf16[256,2048]{1,0:T(8,128)(2,1)}), bf16[8192,2048]{1,0:T(8,128)(2,1)}) %all-gather.5.cloned.1.call-update) | async-done | bytes 33554448 | tf_op jit(solution)/shard_map/all_gather | solution.py:45
  234.4 17.8 %fusion = f32[256,2048]{1,0:T(8,128)} fusion(bf16[8192,256]{1,0:T(8,128)(2,1)} %bitcast.9, bf16[8192,2048]{1,0:T(8,128)(2,1)} %all-gather.5.cloned.1.call-done, f32[]{:T(128)} %get-tuple-element.15, s32[2048]{0:T(1024)S(1)} %iota_add_fusion, s32[256]{0:T(256)S(1)} %iota_add_fusion.1), kind=kOutput, calls=%fused_computation.5 | convolution fusion | flops 8591507456 | bytes 39855108 | tf_op jit(solution)/shard_map/dot_general | solution.py:10
  (7 shorter events, 0.0 us)
Async XLA Ops:
  7.2 1.6 copy-start
  7.2 66.6 %all-gather.3.cloned.1.call-start = ((), (), s32[]{:S(2)}) async-start(), calls=%async_computation.1 | async-start | bytes 5242880 | tf_op jit(solution)/shard_map/all_gather | solution.py:38
  8.8 11.2 %copy-start.3 = (s32[2]{0:T(128)S(1)}, s32[2]{0:T(128)}, u32[]{:S(2)}) copy-start(s32[2]{0:T(128)} %param.9) | copy-start | bytes 28
  8.8 13.1 %copy-start.2 = (f32[2048]{0:T(1024)S(1)}, f32[2048]{0:T(1024)}, u32[]{:S(2)}) copy-start(f32[2048]{0:T(1024)} %param.7) | copy-start | bytes 24580
  23.3 211.1 %all-gather.5.cloned.1.call-start = ((), (), s32[]{:S(2)}) async-start(), calls=%async_computation.2 | async-start | bytes 34603008 | tf_op jit(solution)/shard_map/all_gather | solution.py:45
  78.4 9.2 %copy-start.1 = (bf16[256,2048]{1,0:T(8,128)(2,1)S(1)}, bf16[256,2048]{1,0:T(8,128)(2,1)}, u32[]{:S(2)}) copy-start(bf16[256,2048]{1,0:T(8,128)(2,1)} %fusion.4) | copy-start | bytes 3145732
  78.4 134.6 %all-to-all-start = ((bf16[256,32,256]{2,0,1:T(8,128)(2,1)}), bf16[256,32,256]{2,0,1:T(8,128)(2,1)}, u32[]{:S(2)}, u32[]{:S(2)}) async-start(bf16[256,32,256]{2,0,1:T(8,128)(2,1)} %bitcast.20), calls=%async_computation | async-start | bytes 8388608 | tf_op jit(solution)/shard_map/all_to_all | solution.py:37
Sparse Core Ops, SparseCore 0:
  23.4 50.2 all-gather.2
  76.6 157.7 all-gather.4
where the time goes:
time: 259 us
  blocking collectives  133 us (51%)
  waiting for transfers between devices  71.8 us (28%)
  matrix products  18.1 us (7%)
  between operations  14.8 us (6%)
  starting transfers between devices  7.97 us (3%)
  local copies, waits for them, and re-layouts  7.31 us (3%)
  other arithmetic  5.65 us (2%)
    psum x1, blocking collectives, per_device(): lax.psum((col_sum, jnp.sum(counts).astype(jnp.float32)), 'tok')  124 us
    all_gather x1, waiting for transfers between devices, per_device(): lax.all_gather(normed, 'blk', axis=1, tiled=True)  49.7 us
    all_gather x1, waiting for transfers between devices, per_device(): shard_rows = lax.all_gather(normed, 'tok', axis=0, tiled=True)  21.4 us
    dot_general x1, matrix products, panel_product(): lax.dot_general(left_rows, shard_rows, (((0,), (0,)), ((), ())), preferre...  17.8 us
    psum x1, blocking collectives, per_device(): row_sums = lax.psum(jnp.sum(picked * picked, axis=1), 'blk')  9.56 us
    all_to_all x1, starting transfers between devices, per_device(): lax.all_to_all(lax.all_gather(normed, 'blk', axis=1, tiled=True), 'tok',...  7.89 us
  transfers between devices with their start and end apart: 3, of which 2 were waited for; matrix products, arithmetic and copies ran while one was open for 3% of the time, Pallas kernels for 0%

commit v1 on v0

v1 whole, which is shorter than its diff:
```python
import jax
import jax.numpy as jnp
from jax import lax
from jax.experimental import pallas as pl
from jax.experimental.pallas import tpu as pltpu
from jax.sharding import Mesh, PartitionSpec as P

epsilon = 1e-05
TOK = ("z", "x", "c")
SLOTS = 256
LIVE = 4096
WIDTH = 2048
PIECE = 64
VMEM = 60 * 1024 * 1024
bf16 = jnp.bfloat16
f32 = jnp.float32


def params(**kw):
    return pltpu.CompilerParams(vmem_limit_bytes=VMEM, **kw)


def pick_kernel(index_ref, counts_ref, resid_ref, picked_ref, sums_ref):
    tokens = resid_ref.shape[0]
    token = lax.broadcasted_iota(jnp.int32, (tokens, SLOTS), 0)
    slot = lax.broadcasted_iota(jnp.int32, (1, SLOTS), 1)
    half = SLOTS // 2
    end = jnp.where(slot < half, counts_ref[0], half + counts_ref[1])
    kept = jnp.where(slot < end, index_ref[...], -1)
    one_hot = jnp.where(token == kept, 1.0, 0.0).astype(bf16)
    total = jnp.zeros((1, SLOTS), f32)
    step = 512
    for k in range(WIDTH // step):
        part = lax.dot_general(
            resid_ref[:, k * step : (k + 1) * step],
            one_hot,
            (((0,), (0,)), ((), ())),
            preferred_element_type=f32,
        )
        picked_ref[k * step : (k + 1) * step, :] = part.astype(bf16)
        total += jnp.sum(part * part, axis=0, keepdims=True)
    sums_ref[...] = jnp.broadcast_to(total, sums_ref.shape)


def pick(resid, keep_index, counts):
    return pl.pallas_call(
        pick_kernel,
        out_shape=(
            jax.ShapeDtypeStruct((WIDTH, SLOTS), bf16),
            jax.ShapeDtypeStruct((8, SLOTS), f32),
        ),
        in_specs=[
            pl.BlockSpec(memory_space=pltpu.VMEM),
            pl.BlockSpec(memory_space=pltpu.SMEM),
            pl.BlockSpec(memory_space=pltpu.VMEM),
        ],
        out_specs=(pl.BlockSpec(memory_space=pltpu.VMEM),) * 2,
        compiler_params=params(),
        name="pick",
    )(keep_index[None, :], counts, resid)


def norm_kernel(picked_ref, scale_ref, gain_ref, out_ref):
    scale = scale_ref[0:1, :]
    for x in range(4):
        for c in range(2):
            for z in range(4):
                first = ((x * 2 + c) * 4 + z) * PIECE
                rows = picked_ref[first : first + PIECE, :].astype(f32)
                gain = gain_ref[first : first + PIECE, :]
                out_ref[z * 8 + x * 2 + c] = (rows * scale * gain).astype(bf16)


def norm(picked, scale, gain):
    return pl.pallas_call(
        norm_kernel,
        out_shape=jax.ShapeDtypeStruct((32, PIECE, SLOTS), bf16),
        compiler_params=params(),
        name="norm",
    )(picked, scale, gain)


def pack_kernel(first_ref, in_ref, out_ref, acc_ref):
    acc_ref[...] = jnp.zeros_like(acc_ref)

    def body(t, _):
        first = first_ref[t]
        base = pl.multiple_of((first // 128) * 128, 128)
        wide = jnp.concatenate([in_ref[t].astype(f32), jnp.zeros((PIECE, 128), f32)], axis=1)
        moved = pltpu.roll(wide, first - base, 1)
        acc_ref[:, pl.ds(base, SLOTS + 128)] += moved
        return 0

    lax.fori_loop(0, 32, body, 0)
    out_ref[...] = acc_ref[:, :LIVE].astype(bf16)


def pack(first, pieces):
    return pl.pallas_call(
        pack_kernel,
        out_shape=jax.ShapeDtypeStruct((PIECE, LIVE), bf16),
        in_specs=[pl.BlockSpec(memory_space=pltpu.SMEM), pl.BlockSpec(memory_space=pltpu.VMEM)],
        out_specs=pl.BlockSpec(memory_space=pltpu.VMEM),
        scratch_shapes=[pltpu.VMEM((PIECE, LIVE + SLOTS + 128), f32)],
        compiler_params=params(),
        name="pack",
    )(first, pieces)


def gram_kernel(place, n_arrays, *refs):
    where_ref = refs[0]
    arrays = refs[1 : 1 + n_arrays]
    out_ref, sum_ref, rows, cols, sem = refs[1 + n_arrays :]
    copies = []
    for k, (kind, index, start, height) in enumerate(place):
        target = rows if kind == "r" else cols
        first = pl.multiple_of(where_ref[k], 32)
        source = arrays[index].at[pl.ds(start, height)]
        copies.append(pltpu.make_async_copy(source, target.at[pl.ds(first, height)], sem.at[k]))
    for copy in copies:
        copy.start()
    for copy in copies:
        copy.wait()
    step = 256

    def body(n, _):
        at = pl.multiple_of(n * step, step)
        block = cols[pl.ds(at, step), :]
        out_ref[:, pl.ds(at, step)] = lax.dot_general(
            rows[...], block, (((1,), (1,)), ((), ())), preferred_element_type=f32
        )
        sum_ref[:, pl.ds(at, step)] = lax.dot_general(
            jnp.ones((8, LIVE), bf16), block, (((1,), (1,)), ((), ())), preferred_element_type=f32
        )
        return 0

    lax.fori_loop(0, cols.shape[0] // step, body, 0)


def gram(where, arrays, place):
    n_rows, n_cols = 512, 1024
    return pl.pallas_call(
        lambda *refs: gram_kernel(place, len(arrays), *refs),
        out_shape=(
            jax.ShapeDtypeStruct((n_rows, n_cols), f32),
            jax.ShapeDtypeStruct((8, n_cols), f32),
        ),
        in_specs=[pl.BlockSpec(memory_space=pltpu.SMEM)]
        + [pl.BlockSpec(memory_space=pl.ANY)] * len(arrays),
        out_specs=(pl.BlockSpec(memory_space=pltpu.VMEM),) * 2,
        scratch_shapes=[
            pltpu.VMEM((n_rows, LIVE), bf16),
            pltpu.VMEM((n_cols, LIVE), bf16),
            pltpu.SemaphoreType.DMA((len(place),)),
        ],
        compiler_params=params(),
        cost_estimate=pl.CostEstimate(
            flops=2 * n_rows * n_cols * LIVE, bytes_accessed=14 * 1024 * 1024, transcendentals=0
        ),
        name="gram",
    )(where, *arrays)


def shift(value, axis, by):
    return lax.ppermute(value, axis, [((i + by) % 4, i) for i in range(4)])


def swap(value):
    return lax.ppermute(value, "c", [(0, 1), (1, 0)])


def per_device(resid, norm_gain, keep_index, counts):
    z, x, c, y = (lax.axis_index(a) for a in ("z", "x", "c", "y"))
    all_counts = lax.all_gather(counts, TOK, axis=0, tiled=True)
    loads = jnp.sum(all_counts.reshape(32, 2), axis=1)
    first = jnp.cumsum(loads) - loads
    kept_total = jnp.sum(loads).astype(f32)

    picked, sums = pick(resid, keep_index, counts)
    scale = lax.rsqrt(lax.psum(sums, "y") / 8192 + epsilon)
    normed = norm(picked, scale, norm_gain[:, None])
    pieces = lax.all_to_all(normed, TOK, 0, 0, tiled=True)
    mine = pack(first, pieces)

    half = PIECE // 2
    turned = lax.ppermute(mine, ("z", "y"), [(i * 4 + j, j * 4 + i) for i in range(4) for j in range(4)])
    a0, b0 = mine[:half], mine[half:]
    a = {d: shift(a0, "x", d) for d in (1, 3, 2)}
    b = {d: shift(b0, "z", d) for d in (1, 3, 2)}
    r = {d: shift(turned, "y", d) for d in (1, 3, 2)}
    a4 = jnp.concatenate([a0, a[1], a[3], a[2]], axis=0)
    b4 = jnp.concatenate([b0, b[1], b[3], b[2]], axis=0)
    a_up, a_down = shift(a4, "z", 1), shift(a4, "z", 3)
    b_up, b_down = shift(b4, "x", 1), shift(b4, "x", 3)
    a_far0, a_far1 = shift(a_up[: 2 * half], "z", 1), shift(a_down[2 * half :], "z", 3)
    b_far0, b_far1 = shift(b_up[: 2 * half], "x", 1), shift(b_down[2 * half :], "x", 3)

    place, arrays, where = [], [], []

    def add(kind, value, height, places):
        for k, at in enumerate(places):
            place.append((kind, len(arrays), k * height, height))
            where.append(at)
        arrays.append(value)

    order = (0, 1, 3, 2)
    rows = jnp.concatenate([turned, r[1], r[3], r[2]], axis=0)
    other = swap(rows)
    add("r", rows, PIECE, [((y + d) % 4) * PIECE for d in order])
    add("r", other, PIECE, [256 + ((y + d) % 4) * PIECE for d in order])
    for value, dz, dxs in (
        (a4, 0, order),
        (a_up, 1, order),
        (a_down, 3, order),
        (a_far0, 2, order[:2]),
        (a_far1, 2, order[2:]),
    ):
        add("c", value, half, [((x + dx) % 4) * 256 + ((z + dz) % 4) * PIECE for dx in dxs])
    for value, dx, dzs in (
        (b4, 0, order),
        (b_up, 1, order),
        (b_down, 3, order),
        (b_far0, 2, order[:2]),
        (b_far1, 2, order[2:]),
    ):
        add("c", value, half, [((x + dx) % 4) * 256 + ((z + dz) % 4) * PIECE + half for dz in dzs])
    product, col_sum = gram(jnp.stack(where).astype(jnp.int32), arrays, tuple(place))

    own = jnp.concatenate([product[:256], col_sum], axis=0)
    given = jnp.concatenate([product[256:], col_sum], axis=0)
    got = swap(given)
    low = jnp.where(c == 0, own, got)
    high = jnp.where(c == 0, got, own)
    n = own.shape[0]
    whole = jnp.stack([low.reshape(n, 4, 256), high.reshape(n, 4, 256)], axis=2).reshape(n, WIDTH)
    whole = whole / kept_total
    row_index = (z * 8 + x * 2 + c) * 256 + jnp.arange(256, dtype=jnp.int32)[:, None]
    col_index = y * WIDTH + jnp.arange(WIDTH, dtype=jnp.int32)[None, :]
    gram_factor = jnp.where(row_index <= col_index, whole[:256], 0.0)
    return (whole[256], gram_factor)


def solution(mesh):
    fine = Mesh(mesh.devices.reshape(4, 4, 2, 4), ("z", "x", "c", "y"))
    return jax.shard_map(
        per_device,
        mesh=fine,
        in_specs=(P(TOK, "y"), P("y"), P(TOK), P(TOK)),
        out_specs=(P("y"), P(TOK, "y")),
        check_vma=False,
    )
```

time: 259 us -> 206 us (0.80)
  blocking collectives: 133 us -> 30.6 us
  starting transfers between devices: 7.97 us -> 62.7 us
  Pallas kernels: 0 us -> 26 us
  matrix products: 18.1 us -> 0 us
  waiting for transfers between devices: 71.8 us -> 55.7 us
  local copies, waits for them, and re-layouts: 7.31 us -> 20.5 us
  between operations: 14.8 us -> 2.26 us
    psum x2 -> x1, blocking collectives: 133 us -> 9.77 us  [per_device(): scale = lax.rsqrt(lax.psum(sums, 'y') / 8192 + epsilon)]
    all_gather x2 -> x0, waiting for transfers between devices: 71.1 us -> none  [the longest x1 49.7 us: per_device(): lax.all_gather(normed, 'blk', axis=1, tiled=True)]
    ppermute x0 -> x20, waiting for transfers between devices: none -> 55.7 us  [the longest x17 54.7 us: shift(): return lax.ppermute(value, axis, [((i + by) % 4, i) for i in range(4)])]
    ppermute x0 -> x20, starting transfers between devices: none -> 52.1 us  [the longest x17 44.5 us: shift(): return lax.ppermute(value, axis, [((i + by) % 4, i) for i in range(4)])]
    pallas_call x0 -> x4, Pallas kernels: none -> 26 us  [the longest x1 14.2 us: gram(): pl.pallas_call(lambda *refs: gram_kernel(place, len(arrays), *refs), out_...]
    unnamed x0 -> x1, blocking collectives: none -> 20.8 us
    dot_general x2 -> x0, matrix products: 18.1 us -> none  [the longest x1 17.8 us: panel_product(): lax.dot_general(left_rows, shard_rows, (((0,), (0,)), ((), ())), preferre...]
    slice x0 -> x8, local copies, waits for them, and re-layouts: none -> 7.86 us  [the longest x2 4.97 us: per_device(): gram_factor = jnp.where(row_index <= col_index, whole[:256], 0.0)]
  transfers between devices with their start and end apart: 3 -> 21, of which waited for: 2 -> 8; matrix products, arithmetic and copies ran while one was open for 3% -> 4% of each run, Pallas kernels for 0% -> 0%
where the time goes in v1:
time: 206 us; the launch traced here: 205 us
  starting transfers between devices  62.7 us (30%)
  waiting for transfers between devices  55.7 us (27%)
  blocking collectives  30.6 us (15%)
  Pallas kernels  26 us (13%)
  local copies, waits for them, and re-layouts  20.5 us (10%)
  other arithmetic  7.36 us (4%)
  between operations  2.26 us (1%)
    ppermute x17, waiting for transfers between devices, shift(): return lax.ppermute(value, axis, [((i + by) % 4, i) for i in range(4)])  54.7 us
    ppermute x17, starting transfers between devices, shift(): return lax.ppermute(value, axis, [((i + by) % 4, i) for i in range(4)])  44.5 us
    unnamed x1, blocking collectives  20.8 us
    pallas_call x1, Pallas kernels, gram(): pl.pallas_call(lambda *refs: gram_kernel(place, len(arrays), *refs), out_...  14.2 us
    all_to_all x1, starting transfers between devices, per_device(): pieces = lax.all_to_all(normed, TOK, 0, 0, tiled=True)  10.6 us
    psum x1, blocking collectives, per_device(): scale = lax.rsqrt(lax.psum(sums, 'y') / 8192 + epsilon)  9.77 us
    unnamed x32, local copies, waits for them, and re-layouts  7.02 us
    ppermute x2, starting transfers between devices, swap(): return lax.ppermute(value, 'c', [(0, 1), (1, 0)])  5.91 us
  transfers between devices with their start and end apart: 21, of which 8 were waited for; matrix products, arithmetic and copies ran while one was open for 4% of the time, Pallas kernels for 0%

profile of v1, /device:TPU:1, one launch (start us, length us, event | category | flops | bytes accessed | tf_op | source)
XLA Modules:
  0.0 205.1 jit_solution(7217850057913372457)
XLA Ops:
  0.6 3.4 %pick.1 = (bf16[2048,256]{1,0:T(8,128)(2,1)}, f32[8,256]{1,0:T(8,128)}) custom-call(s32[1,256]{1,0:T(1,128)} %bitcast.50, s32[2]{0:T(128)} %counts_ref.1, bf16[512,2048]{1,0:T(8,128)(2,1)} %resid_ref.1), custom_call_target="tpu_custom_call" | custom-call | tf_op jit(solution)/shard_map/pick/pallas_call | solution.py:46
  4.0 9.8 %psum.7 = f32[8,256]{1,0:T(8,128)S(1)} all-reduce(f32[8,256]{1,0:T(8,128)} %get-tuple-element.7), channel_id=1, replica_groups=mesh['z'=4,'x'=4,'c'=2,'y'=4] {'y'}, use_global_device_ids=true, to_apply=%region_2.3 | all-reduce | flops 2048 | bytes 16384 | tf_op jit(solution)/shard_map/psum | solution.py:180
  13.8 0.6 add_rsqrt_fusion.scale_ref
  14.4 1.4 copy.9.gain_ref
  15.7 2.9 %norm.1 = bf16[32,64,256]{2,1,0:T(8,128)(2,1)} custom-call(bf16[2048,256]{1,0:T(8,128)(2,1)} %get-tuple-element.6.picked_ref, f32[8,256]{1,0:T(8,128)} %add_rsqrt_fusion.scale_ref, f32[2048,1]{1,0:T(8,128)} %copy.9.gain_ref), custom_call_target="tpu_custom_call" | custom-call | tf_op jit(solution)/shard_map/norm/pallas_call | solution.py:75
  18.6 10.6 %all-to-all-start = ((bf16[32,64,256]{2,1,0:T(8,128)(2,1)}), bf16[32,64,256]{2,1,0:T(8,128)(2,1)S(1)}, u32[]{:S(2)}, u32[]{:S(2)}) async-start(bf16[32,64,256]{2,1,0:T(8,128)(2,1)} %norm.1), calls=%async_computation | async-start | bytes 2097152 | tf_op jit(solution)/shard_map/all_to_all | solution.py:182
  30.8 20.8 %all-reduce = s32[64]{0:T(128)S(1)} all-reduce(s32[64]{0:T(128)S(1)} %dynamic-update-slice), channel_id=1, replica_groups=mesh['z'=4,'x'=4,'c'=2,'y'=4] {'z','x','c'}, use_global_device_ids=true, to_apply=%add | all-reduce | flops 64 | bytes 512
  52.6 1.0 copy-done
  53.6 5.5 %pack.1 = bf16[64,4096]{1,0:T(8,128)(2,1)} custom-call(s32[32]{0:T(128)} %sub.3.first_ref, bf16[32,64,256]{2,1,0:T(8,128)(2,1)} %copy-done), custom_call_target="tpu_custom_call" | custom-call | tf_op jit(solution)/shard_map/pack/pallas_call | solution.py:99
  59.1 1.7 collective-permute-start
  60.8 27.2 %collective-permute-start.1 = (bf16[64,4096]{1,0:T(8,128)(2,1)S(1)}, bf16[64,4096]{1,0:T(8,128)(2,1)S(1)}, u32[]{:S(2)}, u32[]{:S(2)}) collective-permute-start(bf16[64,4096]{1,0:T(8,128)(2,1)S(1)} %collective-permute-done), channel_id=1, source_target_pairs={{1,0},{2,1},{3,2},{0,3},{5,4},{6,5},{7,6},{4,7},{9,8},{10,9},{11,1... | collective-permute-start | bytes 1572872 | tf_op jit(solution)/shard_map/ppermute | solution.py:165
  88.0 1.1 fusion.3
  89.1 1.4 collective-permute-start.12
  90.6 1.2 collective-permute-start.14
  91.8 1.5 collective-permute-start.2
  93.2 0.8 constant_dynamic-update-slice_fusion.3
  94.1 3.6 %collective-permute-done.1 = bf16[64,4096]{1,0:T(8,128)(2,1)S(1)} collective-permute-done((bf16[64,4096]{1,0:T(8,128)(2,1)S(1)}, bf16[64,4096]{1,0:T(8,128)(2,1)S(1)}, u32[]{:S(2)}, u32[]{:S(2)}) %collective-permute-start.1) | collective-permute-done | bytes 524320 | tf_op jit(solution)/shard_map/ppermute | solution.py:165
  97.7 2.2 %collective-permute-start.3 = (bf16[64,4096]{1,0:T(8,128)(2,1)S(1)}, bf16[64,4096]{1,0:T(8,128)(2,1)S(1)}, u32[]{:S(2)}, u32[]{:S(2)}) collective-permute-start(bf16[64,4096]{1,0:T(8,128)(2,1)S(1)} %collective-permute-done), channel_id=1, source_target_pairs={{2,0},{3,1},{0,2},{1,3},{6,4},{7,5},{4,6},{5,7},{10,8},{11,9},{8,1... | collective-permute-start | bytes 1572872 | tf_op jit(solution)/shard_map/ppermute | solution.py:165
  99.9 0.8 constant_dynamic-update-slice_fusion.2
  100.7 14.9 %collective-permute-done.2 = bf16[64,4096]{1,0:T(8,128)(2,1)S(1)} collective-permute-done((bf16[64,4096]{1,0:T(8,128)(2,1)S(1)}, bf16[64,4096]{1,0:T(8,128)(2,1)S(1)}, u32[]{:S(2)}, u32[]{:S(2)}) %collective-permute-start.2) | collective-permute-done | bytes 524320 | tf_op jit(solution)/shard_map/ppermute | solution.py:165
  115.6 0.8 constant_dynamic-update-slice_fusion.1
  116.5 1.5 collective-permute-start.6
  117.9 0.8 constant_dynamic-update-slice_fusion.refs_1_
  118.8 0.7 collective-permute-start.7
  119.5 3.8 %collective-permute-start.4 = (bf16[256,4096]{1,0:T(8,128)(2,1)}, bf16[256,4096]{1,0:T(8,128)(2,1)}, u32[]{:S(2)}, u32[]{:S(2)}) collective-permute-start(bf16[256,4096]{1,0:T(8,128)(2,1)} %constant_dynamic-update-slice_fusion.refs_1_), channel_id=1, source_target_pairs={{0,4},{4,0},{1,5},{5,1},{2,6},{6,2},{3,7},{7,3},{8,12},{12,8},{9,1... | collective-permute-start | bytes 6291464 | tf_op jit(solution)/shard_map/ppermute | solution.py:169
  123.4 2.0 collective-permute-start.15
  125.4 2.4 %collective-permute-done.7 = bf16[32,4096]{1,0:T(8,128)(2,1)S(1)} collective-permute-done((bf16[32,4096]{1,0:T(8,128)(2,1)S(1)}, bf16[32,4096]{1,0:T(8,128)(2,1)S(1)}, u32[]{:S(2)}, u32[]{:S(2)}) %collective-permute-start.7) | collective-permute-done | bytes 262176 | tf_op jit(solution)/shard_map/ppermute | solution.py:165
  128.0 1.5 collective-permute-start.9
  129.4 21.7 %collective-permute-done.15.refs_9_ = bf16[128,4096]{1,0:T(8,128)(2,1)S(1)} collective-permute-done((bf16[128,4096]{1,0:T(8,128)(2,1)S(1)}, bf16[128,4096]{1,0:T(8,128)(2,1)S(1)}, u32[]{:S(2)}, u32[]{:S(2)}) %collective-permute-start.15) | collective-permute-done | bytes 1048608 | tf_op jit(solution)/shard_map/ppermute | solution.py:165
  151.2 3.5 %collective-permute-start.17 = (bf16[64,4096]{1,0:T(8,128)(2,1)S(1)}, bf16[64,4096]{1,0:T(8,128)(2,1)}, u32[]{:S(2)}, u32[]{:S(2)}) collective-permute-start(bf16[64,4096]{1,0:T(8,128)(2,1)S(1)} %slice.49), channel_id=1, source_target_pairs={{8,0},{16,8},{24,16},{0,24},{9,1},{17,9},{25,17},{1,25},{10,2},{18... | collective-permute-start | bytes 1572872 | tf_op jit(solution)/shard_map/ppermute | solution.py:165
  156.7 1.1 collective-permute-start.11
  157.7 0.7 stack.166.refs_0_
  158.4 6.9 %collective-permute-done.17.refs_11_ = bf16[64,4096]{1,0:T(8,128)(2,1)} collective-permute-done((bf16[64,4096]{1,0:T(8,128)(2,1)S(1)}, bf16[64,4096]{1,0:T(8,128)(2,1)}, u32[]{:S(2)}, u32[]{:S(2)}) %collective-permute-start.17) | collective-permute-done | bytes 524320 | tf_op jit(solution)/shard_map/ppermute | solution.py:165
  165.3 3.3 %collective-permute-done.18.refs_12_ = bf16[64,4096]{1,0:T(8,128)(2,1)} collective-permute-done((bf16[64,4096]{1,0:T(8,128)(2,1)S(1)}, bf16[64,4096]{1,0:T(8,128)(2,1)}, u32[]{:S(2)}, u32[]{:S(2)}) %collective-permute-start.18) | collective-permute-done | bytes 524320 | tf_op jit(solution)/shard_map/ppermute | solution.py:165
  168.6 1.8 collective-permute-done.11.refs_7_
  170.4 14.2 %gram.1 = (f32[512,1024]{1,0:T(8,128)}, f32[8,1024]{1,0:T(8,128)}) custom-call(s32[40]{0:T(128)} %stack.166.refs_0_, bf16[256,4096]{1,0:T(8,128)(2,1)} %constant_dynamic-update-slice_fusion.refs_1_, bf16[256,4096]{1,0:T(8,128)(2,1)} %collective-permute-done.4.refs_2_, bf16[128,4096]{1,0:T(8,128)(2,1)} %copy-done.3, bf16[128,4096]{1,0:T(8,128)(2,1)} %copy-done.6, ...), custom_call_target="tpu_custom_call" | custom-call | flops 4294967296 | bytes 14680064 | tf_op jit(solution)/shard_map/gram/pallas_call | solution.py:142
  184.6 1.7 fusion.2
  186.5 2.2 %collective-permute-start.19 = (f32[264,1024]{1,0:T(8,128)S(1)}, f32[264,1024]{1,0:T(8,128)S(1)}, u32[]{:S(2)}, u32[]{:S(2)}) collective-permute-start(f32[264,1024]{1,0:T(8,128)S(1)} %pad_maximum_fusion), channel_id=1, source_target_pairs={{0,4},{4,0},{1,5},{5,1},{2,6},{6,2},{3,7},{7,3},{8,12},{12,8},{9,1... | collective-permute-start | bytes 3244040 | tf_op jit(solution)/shard_map/ppermute | solution.py:169
  188.6 0.6 reduce_sum.19
  189.9 1.0 collective-permute-done.19
  190.9 1.0 copy-done.1
  191.9 1.5 fusion.1
  193.4 1.3 stack_reshape.8
  194.7 1.3 stack_reshape.9
  196.0 2.0 maximum_divide_fusion
  198.0 2.0 slice.52
  200.1 2.9 %slice.44 = f32[256,2048]{1,0:T(8,128)S(1)} reshape(f32[256,4,2,256]{3,2,1,0:T(2,128)} %slice.52) | data formatting | bytes 4194304 | tf_op jit(solution)/shard_map/slice | solution.py:239
  203.6 1.5 compare_select_fusion
  (61 shorter events, 4.9 us)
Async XLA Ops:
  0.6 13.8 %copy-start.9 = (f32[2048]{0:T(1024)S(1)}, f32[2048]{0:T(1024)}, u32[]{:S(2)}) copy-start(f32[2048]{0:T(1024)} %param.5) | copy-start | bytes 24580
  15.7 13.5 %copy-start.11 = (u32[128]{0:T(128)S(1)}, u32[128]{0:T(128)}, u32[]{:S(2)}) copy-start(u32[128]{0:T(128)} %constant.222) | copy-start | bytes 1540
  15.7 14.8 %copy-start.10 = (s32[2]{0:T(128)S(1)}, s32[2]{0:T(128)}, u32[]{:S(2)}) copy-start(s32[2]{0:T(128)} %counts_ref.1) | copy-start | bytes 28
  18.6 34.0 %all-to-all-start = ((bf16[32,64,256]{2,1,0:T(8,128)(2,1)}), bf16[32,64,256]{2,1,0:T(8,128)(2,1)S(1)}, u32[]{:S(2)}, u32[]{:S(2)}) async-start(bf16[32,64,256]{2,1,0:T(8,128)(2,1)} %norm.1), calls=%async_computation | async-start | bytes 2097152 | tf_op jit(solution)/shard_map/all_to_all | solution.py:182
  52.6 1.0 copy-start
  59.1 1.7 collective-permute-start
  60.8 36.9 %collective-permute-start.1 = (bf16[64,4096]{1,0:T(8,128)(2,1)S(1)}, bf16[64,4096]{1,0:T(8,128)(2,1)S(1)}, u32[]{:S(2)}, u32[]{:S(2)}) collective-permute-start(bf16[64,4096]{1,0:T(8,128)(2,1)S(1)} %collective-permute-done), channel_id=1, source_target_pairs={{1,0},{2,1},{3,2},{0,3},{5,4},{6,5},{7,6},{4,7},{9,8},{10,9},{11,1... | collective-permute-start | bytes 1572872 | tf_op jit(solution)/shard_map/ppermute | solution.py:165
  89.1 29.7 %collective-permute-start.12 = (bf16[32,4096]{1,0:T(8,128)(2,1)S(1)}, bf16[32,4096]{1,0:T(8,128)(2,1)S(1)}, u32[]{:S(2)}, u32[]{:S(2)}) collective-permute-start(bf16[32,4096]{1,0:T(8,128)(2,1)S(1)} %get-tuple-element.14), channel_id=1, source_target_pairs={{32,0},{64,32},{96,64},{0,96},{33,1},{65,33},{97,65},{1,97},{34,2}... | collective-permute-start | bytes 786440 | tf_op jit(solution)/shard_map/ppermute | solution.py:165
  90.5 29.0 %collective-permute-start.13 = (bf16[32,4096]{1,0:T(8,128)(2,1)S(1)}, bf16[32,4096]{1,0:T(8,128)(2,1)S(1)}, u32[]{:S(2)}, u32[]{:S(2)}) collective-permute-start(bf16[32,4096]{1,0:T(8,128)(2,1)S(1)} %get-tuple-element.14), channel_id=1, source_target_pairs={{96,0},{0,32},{32,64},{64,96},{97,1},{1,33},{33,65},{65,97},{98,2}... | collective-permute-start | bytes 786440 | tf_op jit(solution)/shard_map/ppermute | solution.py:165
  90.6 32.7 %collective-permute-start.14 = (bf16[32,4096]{1,0:T(8,128)(2,1)S(1)}, bf16[32,4096]{1,0:T(8,128)(2,1)S(1)}, u32[]{:S(2)}, u32[]{:S(2)}) collective-permute-start(bf16[32,4096]{1,0:T(8,128)(2,1)S(1)} %get-tuple-element.14), channel_id=1, source_target_pairs={{64,0},{96,32},{0,64},{32,96},{65,1},{97,33},{1,65},{33,97},{66,2}... | collective-permute-start | bytes 786440 | tf_op jit(solution)/shard_map/ppermute | solution.py:165
  91.8 23.9 %collective-permute-start.2 = (bf16[64,4096]{1,0:T(8,128)(2,1)S(1)}, bf16[64,4096]{1,0:T(8,128)(2,1)S(1)}, u32[]{:S(2)}, u32[]{:S(2)}) collective-permute-start(bf16[64,4096]{1,0:T(8,128)(2,1)S(1)} %collective-permute-done), channel_id=1, source_target_pairs={{3,0},{0,1},{1,2},{2,3},{7,4},{4,5},{5,6},{6,7},{11,8},{8,9},{9,10... | collective-permute-start | bytes 1572872 | tf_op jit(solution)/shard_map/ppermute | solution.py:165
  97.7 18.8 %collective-permute-start.3 = (bf16[64,4096]{1,0:T(8,128)(2,1)S(1)}, bf16[64,4096]{1,0:T(8,128)(2,1)S(1)}, u32[]{:S(2)}, u32[]{:S(2)}) collective-permute-start(bf16[64,4096]{1,0:T(8,128)(2,1)S(1)} %collective-permute-done), channel_id=1, source_target_pairs={{2,0},{3,1},{0,2},{1,3},{6,4},{7,5},{4,6},{5,7},{10,8},{11,9},{8,1... | collective-permute-start | bytes 1572872 | tf_op jit(solution)/shard_map/ppermute | solution.py:165
  115.6 9.8 %collective-permute-start.5 = (bf16[32,4096]{1,0:T(8,128)(2,1)S(1)}, bf16[32,4096]{1,0:T(8,128)(2,1)S(1)}, u32[]{:S(2)}, u32[]{:S(2)}) collective-permute-start(bf16[32,4096]{1,0:T(8,128)(2,1)S(1)} %get-tuple-element.15), channel_id=1, source_target_pairs={{8,0},{16,8},{24,16},{0,24},{9,1},{17,9},{25,17},{1,25},{10,2},{18... | collective-permute-start | bytes 786440 | tf_op jit(solution)/shard_map/ppermute | solution.py:165
  116.5 8.9 %collective-permute-start.6 = (bf16[32,4096]{1,0:T(8,128)(2,1)S(1)}, bf16[32,4096]{1,0:T(8,128)(2,1)S(1)}, u32[]{:S(2)}, u32[]{:S(2)}) collective-permute-start(bf16[32,4096]{1,0:T(8,128)(2,1)S(1)} %get-tuple-element.15), channel_id=1, source_target_pairs={{24,0},{0,8},{8,16},{16,24},{25,1},{1,9},{9,17},{17,25},{26,2},{2,... | collective-permute-start | bytes 786440 | tf_op jit(solution)/shard_map/ppermute | solution.py:165
  118.8 9.0 %collective-permute-start.7 = (bf16[32,4096]{1,0:T(8,128)(2,1)S(1)}, bf16[32,4096]{1,0:T(8,128)(2,1)S(1)}, u32[]{:S(2)}, u32[]{:S(2)}) collective-permute-start(bf16[32,4096]{1,0:T(8,128)(2,1)S(1)} %get-tuple-element.15), channel_id=1, source_target_pairs={{16,0},{24,8},{0,16},{8,24},{17,1},{25,9},{1,17},{9,25},{18,2},{26... | collective-permute-start | bytes 786440 | tf_op jit(solution)/shard_map/ppermute | solution.py:165
  119.5 50.9 %collective-permute-start.4 = (bf16[256,4096]{1,0:T(8,128)(2,1)}, bf16[256,4096]{1,0:T(8,128)(2,1)}, u32[]{:S(2)}, u32[]{:S(2)}) collective-permute-start(bf16[256,4096]{1,0:T(8,128)(2,1)} %constant_dynamic-update-slice_fusion.refs_1_), channel_id=1, source_target_pairs={{0,4},{4,0},{1,5},{5,1},{2,6},{6,2},{3,7},{7,3},{8,12},{12,8},{9,1... | collective-permute-start | bytes 6291464 | tf_op jit(solution)/shard_map/ppermute | solution.py:169
  123.4 31.4 %copy-start.2 = (bf16[128,4096]{1,0:T(8,128)(2,1)}, bf16[128,4096]{1,0:T(8,128)(2,1)S(1)}, u32[]{:S(2)}) copy-start(bf16[128,4096]{1,0:T(8,128)(2,1)S(1)} %pad_maximum_fusion.3.refs_8_) | copy-start | bytes 3145732
  123.4 27.8 %collective-permute-start.15 = (bf16[128,4096]{1,0:T(8,128)(2,1)S(1)}, bf16[128,4096]{1,0:T(8,128)(2,1)S(1)}, u32[]{:S(2)}, u32[]{:S(2)}) collective-permute-start(bf16[128,4096]{1,0:T(8,128)(2,1)S(1)} %pad_maximum_fusion.3.refs_8_), channel_id=1, source_target_pairs={{8,0},{16,8},{24,16},{0,24},{9,1},{17,9},{25,17},{1,25},{10,2},{18... | collective-permute-start | bytes 3145736 | tf_op jit(solution)/shard_map/ppermute | solution.py:165
  125.4 29.3 %collective-permute-start.16 = (bf16[128,4096]{1,0:T(8,128)(2,1)S(1)}, bf16[128,4096]{1,0:T(8,128)(2,1)S(1)}, u32[]{:S(2)}, u32[]{:S(2)}) collective-permute-start(bf16[128,4096]{1,0:T(8,128)(2,1)S(1)} %pad_maximum_fusion.3.refs_8_), channel_id=1, source_target_pairs={{24,0},{0,8},{8,16},{16,24},{25,1},{1,9},{9,17},{17,25},{26,2},{2,... | collective-permute-start | bytes 3145736 | tf_op jit(solution)/shard_map/ppermute | solution.py:165
  127.9 27.9 %copy-start.3 = (bf16[128,4096]{1,0:T(8,128)(2,1)}, bf16[128,4096]{1,0:T(8,128)(2,1)S(1)}, u32[]{:S(2)}) copy-start(bf16[128,4096]{1,0:T(8,128)(2,1)S(1)} %pad_maximum_fusion.2.refs_3_) | copy-start | bytes 3145732
  127.9 26.9 %collective-permute-start.8 = (bf16[128,4096]{1,0:T(8,128)(2,1)S(1)}, bf16[128,4096]{1,0:T(8,128)(2,1)S(1)}, u32[]{:S(2)}, u32[]{:S(2)}) collective-permute-start(bf16[128,4096]{1,0:T(8,128)(2,1)S(1)} %pad_maximum_fusion.2.refs_3_), channel_id=1, source_target_pairs={{32,0},{64,32},{96,64},{0,96},{33,1},{65,33},{97,65},{1,97},{34,2}... | collective-permute-start | bytes 3145736 | tf_op jit(solution)/shard_map/ppermute | solution.py:165
  128.0 27.5 %collective-permute-start.9 = (bf16[128,4096]{1,0:T(8,128)(2,1)S(1)}, bf16[128,4096]{1,0:T(8,128)(2,1)S(1)}, u32[]{:S(2)}, u32[]{:S(2)}) collective-permute-start(bf16[128,4096]{1,0:T(8,128)(2,1)S(1)} %pad_maximum_fusion.2.refs_3_), channel_id=1, source_target_pairs={{96,0},{0,32},{32,64},{64,96},{97,1},{1,33},{33,65},{65,97},{98,2}... | collective-permute-start | bytes 3145736 | tf_op jit(solution)/shard_map/ppermute | solution.py:165
  151.2 4.6 %copy-start.4 = (bf16[128,4096]{1,0:T(8,128)(2,1)}, bf16[128,4096]{1,0:T(8,128)(2,1)S(1)}, u32[]{:S(2)}) copy-start(bf16[128,4096]{1,0:T(8,128)(2,1)S(1)} %collective-permute-done.15.refs_9_) | copy-start | bytes 3145732
  151.2 14.1 %collective-permute-start.17 = (bf16[64,4096]{1,0:T(8,128)(2,1)S(1)}, bf16[64,4096]{1,0:T(8,128)(2,1)}, u32[]{:S(2)}, u32[]{:S(2)}) collective-permute-start(bf16[64,4096]{1,0:T(8,128)(2,1)S(1)} %slice.49), channel_id=1, source_target_pairs={{8,0},{16,8},{24,16},{0,24},{9,1},{17,9},{25,17},{1,25},{10,2},{18... | collective-permute-start | bytes 1572872 | tf_op jit(solution)/shard_map/ppermute | solution.py:165
  154.7 1.0 copy-start.5
  154.7 13.9 %collective-permute-start.18 = (bf16[64,4096]{1,0:T(8,128)(2,1)S(1)}, bf16[64,4096]{1,0:T(8,128)(2,1)}, u32[]{:S(2)}, u32[]{:S(2)}) collective-permute-start(bf16[64,4096]{1,0:T(8,128)(2,1)S(1)} %slice.50), channel_id=1, source_target_pairs={{24,0},{0,8},{8,16},{16,24},{25,1},{1,9},{9,17},{17,25},{26,2},{2,... | collective-permute-start | bytes 1572872 | tf_op jit(solution)/shard_map/ppermute | solution.py:165
  154.8 1.2 copy-start.6
  154.9 13.7 %collective-permute-start.10 = (bf16[64,4096]{1,0:T(8,128)(2,1)S(1)}, bf16[64,4096]{1,0:T(8,128)(2,1)}, u32[]{:S(2)}, u32[]{:S(2)}) collective-permute-start(bf16[64,4096]{1,0:T(8,128)(2,1)S(1)} %slice.46), channel_id=1, source_target_pairs={{32,0},{64,32},{96,64},{0,96},{33,1},{65,33},{97,65},{1,97},{34,2}... | collective-permute-start | bytes 1572872 | tf_op jit(solution)/shard_map/ppermute | solution.py:165
  155.7 1.0 copy-start.7
  156.7 13.7 %collective-permute-start.11 = (bf16[64,4096]{1,0:T(8,128)(2,1)S(1)}, bf16[64,4096]{1,0:T(8,128)(2,1)}, u32[]{:S(2)}, u32[]{:S(2)}) collective-permute-start(bf16[64,4096]{1,0:T(8,128)(2,1)S(1)} %slice.47), channel_id=1, source_target_pairs={{96,0},{0,32},{32,64},{64,96},{97,1},{1,33},{33,65},{65,97},{98,2}... | collective-permute-start | bytes 1572872 | tf_op jit(solution)/shard_map/ppermute | solution.py:165
  184.6 1.7 copy-start.8
  186.5 4.5 %collective-permute-start.19 = (f32[264,1024]{1,0:T(8,128)S(1)}, f32[264,1024]{1,0:T(8,128)S(1)}, u32[]{:S(2)}, u32[]{:S(2)}) collective-permute-start(f32[264,1024]{1,0:T(8,128)S(1)} %pad_maximum_fusion), channel_id=1, source_target_pairs={{0,4},{4,0},{1,5},{5,1},{2,6},{6,2},{3,7},{7,3},{8,12},{12,8},{9,1... | collective-permute-start | bytes 3244040 | tf_op jit(solution)/shard_map/ppermute | solution.py:169
  190.9 1.0 copy-start.1

commit v2 on v0

v2 whole, which is shorter than its diff:
```python
import jax
import jax.numpy as jnp
from jax import lax
from jax.experimental import pallas as pl
from jax.experimental.pallas import tpu as pltpu
from jax.sharding import Mesh, PartitionSpec as P

epsilon = 1e-05
TOK = ("z", "x", "c")
SLOTS = 256
LIVE = 4096
WIDTH = 2048
PIECE = 64
EXTRA = 16
VMEM = 60 * 1024 * 1024
bf16 = jnp.bfloat16
f32 = jnp.float32


def params(**kw):
    return pltpu.CompilerParams(vmem_limit_bytes=VMEM, **kw)


def pick_kernel(index_ref, counts_ref, resid_ref, out_ref):
    tokens = resid_ref.shape[0]
    token = lax.broadcasted_iota(jnp.int32, (tokens, SLOTS), 0)
    slot = lax.broadcasted_iota(jnp.int32, (1, SLOTS), 1)
    half = SLOTS // 2
    end = jnp.where(slot < half, counts_ref[0], half + counts_ref[1])
    kept = jnp.where(slot < end, index_ref[...], -1)
    one_hot = jnp.where(token == kept, 1.0, 0.0).astype(bf16)
    total = jnp.zeros((1, SLOTS), f32)
    step = 512
    for x in range(4):
        part = lax.dot_general(
            resid_ref[:, x * step : (x + 1) * step],
            one_hot,
            (((0,), (0,)), ((), ())),
            preferred_element_type=f32,
        )
        total += jnp.sum(part * part, axis=0, keepdims=True)
        short = part.astype(bf16)
        for c in range(2):
            for z in range(4):
                first = (c * 4 + z) * PIECE
                out_ref[z * 8 + x * 2 + c, :PIECE, :] = short[first : first + PIECE, :]
    live = (counts_ref[0] + counts_ref[1]).astype(f32)
    high = total.astype(bf16).astype(f32)
    middle = (total - high).astype(bf16).astype(f32)
    low = total - high - middle
    row = lax.broadcasted_iota(jnp.int32, (EXTRA, SLOTS), 0)
    extra = jnp.where(row == 0, live, 0.0)
    for k, term in enumerate((high, middle, low)):
        extra = jnp.where(row == k + 1, term, extra)
    extra = extra.astype(bf16)
    for t in range(32):
        out_ref[t, PIECE:, :] = extra


def pick(resid, keep_index, counts):
    return pl.pallas_call(
        pick_kernel,
        out_shape=jax.ShapeDtypeStruct((32, PIECE + EXTRA, SLOTS), bf16),
        in_specs=[
            pl.BlockSpec(memory_space=pltpu.VMEM),
            pl.BlockSpec(memory_space=pltpu.SMEM),
            pl.BlockSpec(memory_space=pltpu.VMEM),
        ],
        out_specs=pl.BlockSpec(memory_space=pltpu.VMEM),
        compiler_params=params(),
        name="pick",
    )(keep_index[None, :], counts, resid)


def pack_kernel(first_ref, in_ref, scale_ref, gain_ref, out_ref, acc_ref):
    acc_ref[...] = jnp.zeros_like(acc_ref)
    gain = gain_ref[...]
    group = 4

    def body(g, _):
        moved = []
        for k in range(group):
            t = g * group + k
            rows = in_ref[t, :PIECE, :].astype(f32) * scale_ref[pl.ds(t, 1), :] * gain
            first = first_ref[t]
            base = pl.multiple_of((first // 128) * 128, 128)
            wide = jnp.concatenate([rows, jnp.zeros((PIECE, 128), f32)], axis=1)
            moved.append((base, pltpu.roll(wide, first - base, 1)))
        for base, rows in moved:
            acc_ref[:, pl.ds(base, SLOTS + 128)] += rows
        return 0

    lax.fori_loop(0, 32 // group, body, 0)
    out_ref[...] = acc_ref[:, :LIVE].astype(bf16)


def pack(first, pieces, scale, gain):
    return pl.pallas_call(
        pack_kernel,
        out_shape=jax.ShapeDtypeStruct((PIECE, LIVE), bf16),
        in_specs=[pl.BlockSpec(memory_space=pltpu.SMEM)] + [pl.BlockSpec(memory_space=pltpu.VMEM)] * 3,
        out_specs=pl.BlockSpec(memory_space=pltpu.VMEM),
        scratch_shapes=[pltpu.VMEM((PIECE, LIVE + SLOTS + 128), f32)],
        compiler_params=params(),
        name="pack",
    )(first, pieces, scale, gain)


def gram_kernel(place, n_arrays, *refs):
    where_ref, block_ref, rows_in = refs[:3]
    arrays = refs[3 : 3 + n_arrays]
    out_ref, rows, cols, row_sem, sem = refs[3 + n_arrays :]
    row_copy = pltpu.make_async_copy(rows_in, rows.at[pl.ds(0, 256)], row_sem)
    row_copy.start()
    copies = []
    for k, (index, start, height, block) in enumerate(place):
        first = pl.multiple_of(where_ref[k], 16)
        source = arrays[index].at[pl.ds(start, height)]
        copies.append(
            (block, pltpu.make_async_copy(source, cols.at[pl.ds(first, height)], sem.at[k]))
        )
    for block in range(4):
        for at, copy in copies:
            if at == block:
                copy.start()
    rows[256:, :] = jnp.ones((16, LIVE), bf16)
    row_copy.wait()
    for block in range(4):
        for at, copy in copies:
            if at == block:
                copy.wait()
        at = pl.multiple_of(block_ref[block], 256)
        out_ref[:, pl.ds(at, 256)] = lax.dot_general(
            rows[...], cols[pl.ds(at, 256), :], (((1,), (1,)), ((), ())), preferred_element_type=f32
        )


def gram(where, blocks, rows, arrays, place):
    n_rows, n_cols = 272, 1024
    return pl.pallas_call(
        lambda *refs: gram_kernel(place, len(arrays), *refs),
        out_shape=jax.ShapeDtypeStruct((n_rows, n_cols), f32),
        in_specs=[pl.BlockSpec(memory_space=pltpu.SMEM)] * 2
        + [pl.BlockSpec(memory_space=pl.ANY)] * (1 + len(arrays)),
        out_specs=pl.BlockSpec(memory_space=pltpu.VMEM),
        scratch_shapes=[
            pltpu.VMEM((n_rows, LIVE), bf16),
            pltpu.VMEM((n_cols, LIVE), bf16),
            pltpu.SemaphoreType.DMA,
            pltpu.SemaphoreType.DMA((len(place),)),
        ],
        compiler_params=params(),
        cost_estimate=pl.CostEstimate(
            flops=2 * n_rows * n_cols * LIVE, bytes_accessed=12 * 1024 * 1024, transcendentals=0
        ),
        name="gram",
    )(where, blocks, rows, *arrays)


def finish_kernel(info_ref, total_ref, own_ref, got_ref, mean_ref, out_ref):
    core, row_first, col_first = info_ref[0], info_ref[1], info_ref[2]
    total = total_ref[0]
    row = row_first + lax.broadcasted_iota(jnp.int32, (256, 256), 0)
    col = col_first + lax.broadcasted_iota(jnp.int32, (256, 256), 1)
    for k in range(8):
        x = k // 2

        def put(ref):
            values = ref[:256, x * 256 : (x + 1) * 256] / total
            out_ref[:, k * 256 : (k + 1) * 256] = jnp.where(row <= col + k * 256, values, 0.0)
            mean_ref[:, k * 256 : (k + 1) * 256] = ref[256:264, x * 256 : (x + 1) * 256] / total

        @pl.when(core == k % 2)
        def _():
            put(own_ref)

        @pl.when(core != k % 2)
        def _():
            put(got_ref)


def finish(info, total, own, got):
    return pl.pallas_call(
        finish_kernel,
        out_shape=(
            jax.ShapeDtypeStruct((8, WIDTH), f32),
            jax.ShapeDtypeStruct((256, WIDTH), f32),
        ),
        in_specs=[pl.BlockSpec(memory_space=pltpu.SMEM)] * 2 + [pl.BlockSpec(memory_space=pltpu.VMEM)] * 2,
        out_specs=(pl.BlockSpec(memory_space=pltpu.VMEM),) * 2,
        compiler_params=params(),
        name="finish",
    )(info, total, own, got)


def shift(value, axis, by):
    return lax.ppermute(value, axis, [((i + by) % 4, i) for i in range(4)])


def swap(value):
    return lax.ppermute(value, "c", [(0, 1), (1, 0)])


def per_device(resid, norm_gain, keep_index, counts):
    z, x, c, y = (lax.axis_index(a) for a in ("z", "x", "c", "y"))
    pieces = lax.all_to_all(pick(resid, keep_index, counts), TOK, 0, 0, tiled=True)

    extra = pieces[:, PIECE : PIECE + 4, :].astype(f32)
    loads = extra[:, 0, 0].astype(jnp.int32)
    first = jnp.cumsum(loads) - loads
    kept_total = jnp.sum(loads).astype(f32)
    sums = extra[:, 1, :] + extra[:, 2, :] + extra[:, 3, :]
    squares = (sums + shift(sums, "y", 2)) + (shift(sums, "y", 1) + shift(sums, "y", 3))
    scale = lax.rsqrt(squares / 8192 + epsilon)
    gain = lax.dynamic_slice_in_dim(norm_gain, ((x * 2 + c) * 4 + z) * PIECE, PIECE)[:, None]
    mine = pack(first, pieces, scale, gain)

    half = PIECE // 2
    order = (1, 3, 2)
    turned = lax.ppermute(mine, ("z", "y"), [(i * 4 + j, j * 4 + i) for i in range(4) for j in range(4)])
    from_x = {d: shift(mine, "x", d) for d in order}
    from_z = {d: shift(mine, "z", d) for d in order}
    a3 = jnp.concatenate([from_x[d][:half] for d in order], axis=0)
    b3 = jnp.concatenate([from_z[d][half:] for d in order], axis=0)
    a3, b3, turned = lax.optimization_barrier((a3, b3, turned))
    rows = lax.all_gather(turned, "y", axis=0, tiled=True)
    a_up, b_up = shift(a3, "z", 1), shift(b3, "x", 1)
    a_down, b_down = shift(a3, "z", 3), shift(b3, "x", 3)
    a_far0, a_far1 = shift(a_up[:48], "z", 1), shift(a_down[48:], "z", 3)
    b_far0, b_far1 = shift(b_up[:48], "x", 1), shift(b_down[48:], "x", 3)

    held = [(mine, [(0, 0, 0, PIECE)])]
    for d in order:
        held.append((from_x[d], [(d, 0, 0, PIECE)]))
        held.append((from_z[d], [(0, d, 0, PIECE)]))
    for d, value in ((1, a_up), (3, a_down)):
        held.append((value, [(e, d, 0, half) for e in order]))
    held.append((a_far0, [(1, 2, 0, half), (3, 2, 0, 16)]))
    held.append((a_far1, [(3, 2, 16, 16), (2, 2, 0, half)]))
    for d, value in ((1, b_up), (3, b_down)):
        held.append((value, [(d, e, half, half) for e in order]))
    held.append((b_far0, [(2, 1, half, half), (2, 3, half, 16)]))
    held.append((b_far1, [(2, 3, half + 16, 16), (2, 2, half, half)]))

    place, where = [], []
    for index, (_, parts) in enumerate(held):
        start = 0
        for dx, dz, row, height in parts:
            place.append((index, start, height, dx))
            where.append(((x + dx) % 4) * 256 + ((z + dz) % 4) * PIECE + row)
            start += height
    where = jnp.stack(where).astype(jnp.int32)
    blocks = jnp.stack([((x + d) % 4) * 256 for d in range(4)]).astype(jnp.int32)
    arrays = [value for value, _ in held]
    given = gram(where, blocks, swap(rows), arrays, tuple(place))
    got = swap(given)
    own = gram(where, blocks, rows, arrays, tuple(place))
    info = jnp.stack([c, (z * 8 + x * 2 + c) * 256, y * WIDTH]).astype(jnp.int32)
    mean, gram_factor = finish(info, kept_total[None], own, got)
    return (mean[0], gram_factor)


def solution(mesh):
    fine = Mesh(mesh.devices.reshape(4, 4, 2, 4), ("z", "x", "c", "y"))
    return jax.shard_map(
        per_device,
        mesh=fine,
        in_specs=(P(TOK, "y"), P("y"), P(TOK), P(TOK)),
        out_specs=(P("y"), P(TOK, "y")),
        check_vma=False,
    )
```

time: 259 us -> 212 us (0.82)
  blocking collectives: 133 us -> 0 us
  waiting for transfers between devices: 71.8 us -> 110 us
  Pallas kernels: 0 us -> 33.5 us
  starting transfers between devices: 7.97 us -> 39.4 us
  matrix products: 18.1 us -> 0 us
    psum x2 -> x0, blocking collectives: 133 us -> none  [the longest x1 124 us: per_device(): lax.psum((col_sum, jnp.sum(counts).astype(jnp.float32)), 'tok')]
    ppermute x0 -> x20, waiting for transfers between devices: none -> 52.1 us  [the longest x17 52.1 us: shift(): return lax.ppermute(value, axis, [((i + by) % 4, i) for i in range(4)])]
    pallas_call x0 -> x5, Pallas kernels: none -> 33.5 us  [the longest x2 22.7 us: gram(): pl.pallas_call(lambda *refs: gram_kernel(place, len(arrays), *refs), out_...]
    all_gather x2 -> x1, waiting for transfers between devices: 71.1 us -> 40.1 us  [per_device(): rows = lax.all_gather(turned, 'y', axis=0, tiled=True)]
    ppermute x0 -> x20, starting transfers between devices: none -> 29.9 us  [the longest x17 21.6 us: shift(): return lax.ppermute(value, axis, [((i + by) % 4, i) for i in range(4)])]
    all_to_all x1, waiting for transfers between devices: 0.01 us -> 18.2 us  [per_device(): lax.all_to_all(pick(resid, keep_index, counts), TOK, 0, 0, tiled=True)]
    dot_general x2 -> x0, matrix products: 18.1 us -> none  [the longest x1 17.8 us: panel_product(): lax.dot_general(left_rows, shard_rows, (((0,), (0,)), ((), ())), preferre...]
    slice x0 -> x12, local copies, waits for them, and re-layouts: none -> 4.99 us  [the longest x2 1.74 us: per_device(): b_far0, b_far1 = (shift(b_up[:48], 'x', 1), shift(b_down[48:], 'x', 3))]
  transfers between devices with their start and end apart: 3 -> 22, of which waited for: 2 -> 10; matrix products, arithmetic and copies ran while one was open for 3% -> 5% of each run, Pallas kernels for 0% -> 5%
where the time goes in v2:
time: 212 us; the launch traced here: 211 us
  waiting for transfers between devices  110 us (52%)
  starting transfers between devices  39.4 us (19%)
  Pallas kernels  33.5 us (16%)
  between operations  14.9 us (7%)
  local copies, waits for them, and re-layouts  7.46 us (4%)
  other arithmetic  5.28 us (2%)
    ppermute x17, waiting for transfers between devices, shift(): return lax.ppermute(value, axis, [((i + by) % 4, i) for i in range(4)])  52.1 us
    all_gather x1, waiting for transfers between devices, per_device(): rows = lax.all_gather(turned, 'y', axis=0, tiled=True)  40.1 us
    pallas_call x2, Pallas kernels, gram(): pl.pallas_call(lambda *refs: gram_kernel(place, len(arrays), *refs), out_...  22.7 us
    ppermute x17, starting transfers between devices, shift(): return lax.ppermute(value, axis, [((i + by) % 4, i) for i in range(4)])  21.6 us
    all_to_all x1, waiting for transfers between devices, per_device(): lax.all_to_all(pick(resid, keep_index, counts), TOK, 0, 0, tiled=True)  18.2 us
    all_to_all x1, starting transfers between devices, per_device(): lax.all_to_all(pick(resid, keep_index, counts), TOK, 0, 0, tiled=True)  9.43 us
    ppermute x1, starting transfers between devices, per_device(): lax.ppermute(mine, ('z', 'y'), [(i * 4 + j, j * 4 + i) for i in range(4)...  5.34 us
  transfers between devices with their start and end apart: 22, of which 10 were waited for; matrix products, arithmetic and copies ran while one was open for 5% of the time, Pallas kernels for 5%

profile of v2, /device:TPU:1, one launch (start us, length us, event | category | flops | bytes accessed | tf_op | source)
XLA Modules:
  0.0 211.0 jit_solution(18288295813342602432)
XLA Ops:
  7.2 3.5 %pick.1 = bf16[32,80,256]{2,1,0:T(8,128)(2,1)} custom-call(s32[1,256]{1,0:T(1,128)} %bitcast.46, s32[2]{0:T(128)} %counts_ref.1, bf16[512,2048]{1,0:T(8,128)(2,1)} %resid_ref.1), custom_call_target="tpu_custom_call" | custom-call | tf_op jit(solution)/shard_map/pick/pallas_call | solution.py:61
  10.6 9.4 %all-to-all-start = ((bf16[32,80,256]{2,1,0:T(8,128)(2,1)}), bf16[32,80,256]{2,1,0:T(8,128)(2,1)S(1)}, u32[]{:S(2)}, u32[]{:S(2)}) async-start(bf16[32,80,256]{2,1,0:T(8,128)(2,1)} %pick.1), calls=%async_computation | async-start | bytes 2621440 | tf_op jit(solution)/shard_map/all_to_all | solution.py:206
  20.2 0.1 dynamic-slice_bitcast_fusion
  20.2 0.7 copy.16.gain_ref
  20.9 18.2 %all-to-all-done.in_ref = bf16[32,80,256]{2,1,0:T(8,128)(2,1)S(1)} async-done(((bf16[32,80,256]{2,1,0:T(8,128)(2,1)}), bf16[32,80,256]{2,1,0:T(8,128)(2,1)S(1)}, u32[]{:S(2)}, u32[]{:S(2)}) %all-to-all-start) | async-done | bytes 1310752 | tf_op jit(solution)/shard_map/all_to_all | solution.py:206
  39.2 3.0 %collective-permute-start = (f32[32,256]{1,0:T(8,128)S(1)}, f32[32,256]{1,0:T(8,128)S(1)}, u32[]{:S(2)}, u32[]{:S(2)}) collective-permute-start(f32[32,256]{1,0:T(8,128)S(1)} %fusion), channel_id=1, source_target_pairs={{2,0},{3,1},{0,2},{1,3},{6,4},{7,5},{4,6},{5,7},{10,8},{11,9},{8,1... | collective-permute-start | bytes 98312 | tf_op jit(solution)/shard_map/ppermute | solution.py:197
  42.2 0.8 collective-permute-start.1
  43.0 0.7 collective-permute-start.2
  43.7 0.6 fusion.1
  44.4 0.1 reduce.1
  44.5 0.5 sub.3.first_ref
  45.0 1.9 collective-permute-done.2
  47.0 0.6 add_rsqrt_fusion.scale_ref
  47.6 4.1 %pack.1.refs_3_ = bf16[64,4096]{1,0:T(8,128)(2,1)} custom-call(s32[32]{0:T(128)} %sub.3.first_ref, bf16[32,80,256]{2,1,0:T(8,128)(2,1)} %copy-done.1, f32[32,256]{1,0:T(8,128)} %add_rsqrt_fusion.scale_ref, f32[64,1]{1,0:T(8,128)} %copy.16.gain_ref), custom_call_target="tpu_custom_call" | custom-call | tf_op jit(solution)/shard_map/pack/pallas_call | solution.py:98
  51.7 1.6 collective-permute-start.6
  53.2 2.4 %collective-permute-start.8 = (bf16[64,4096]{1,0:T(8,128)(2,1)}, bf16[64,4096]{1,0:T(8,128)(2,1)S(1)}, u32[]{:S(2)}, u32[]{:S(2)}) collective-permute-start(bf16[64,4096]{1,0:T(8,128)(2,1)} %pack.1.refs_3_), channel_id=1, source_target_pairs={{64,0},{96,32},{0,64},{32,96},{65,1},{97,33},{1,65},{33,97},{66,2}... | collective-permute-start | bytes 1572872 | tf_op jit(solution)/shard_map/ppermute | solution.py:197
  55.6 0.4 collective-permute-start.3
  56.0 1.1 collective-permute-start.4
  57.1 7.0 %collective-permute-done.6.refs_5_ = bf16[64,4096]{1,0:T(8,128)(2,1)S(1)} collective-permute-done((bf16[64,4096]{1,0:T(8,128)(2,1)}, bf16[64,4096]{1,0:T(8,128)(2,1)S(1)}, u32[]{:S(2)}, u32[]{:S(2)}) %collective-permute-start.6) | collective-permute-done | bytes 524320 | tf_op jit(solution)/shard_map/ppermute | solution.py:197
  64.1 0.9 collective-permute-start.5
  65.0 0.7 collective-permute-done.7.refs_7_
  65.7 5.3 %collective-permute-start.9 = (bf16[64,4096]{1,0:T(8,128)(2,1)}, bf16[64,4096]{1,0:T(8,128)(2,1)}, u32[]{:S(2)}, u32[]{:S(2)}) collective-permute-start(bf16[64,4096]{1,0:T(8,128)(2,1)} %pack.1.refs_3_), channel_id=1, source_target_pairs={{0,0},{1,32},{2,64},{3,96},{32,1},{33,33},{34,65},{35,97},{64,2},{... | collective-permute-start | bytes 1572872 | tf_op jit(solution)/shard_map/ppermute | solution.py:220
  71.1 18.0 %collective-permute-done.8.refs_9_ = bf16[64,4096]{1,0:T(8,128)(2,1)S(1)} collective-permute-done((bf16[64,4096]{1,0:T(8,128)(2,1)}, bf16[64,4096]{1,0:T(8,128)(2,1)S(1)}, u32[]{:S(2)}, u32[]{:S(2)}) %collective-permute-start.8) | collective-permute-done | bytes 524320 | tf_op jit(solution)/shard_map/ppermute | solution.py:197
  89.1 1.0 pad_maximum_fusion.1
  90.3 1.1 pad_maximum_fusion
  91.4 40.1 %all-gather.2.cloned.1.call-done.refs_2_ = bf16[256,4096]{1,0:T(8,128)(2,1)} async-done(((bf16[64,4096]{1,0:T(8,128)(2,1)}), bf16[256,4096]{1,0:T(8,128)(2,1)}) %all-gather.2.cloned.1.call-update) | async-done | bytes 2097168 | tf_op jit(solution)/shard_map/all_gather | solution.py:226
  131.5 0.7 collective-permute-start.18
  132.2 2.7 %collective-permute-start.10 = (bf16[96,4096]{1,0:T(8,128)(2,1)}, bf16[96,4096]{1,0:T(8,128)(2,1)S(1)}, u32[]{:S(2)}, u32[]{:S(2)}) collective-permute-start(bf16[96,4096]{1,0:T(8,128)(2,1)} %pad_maximum_fusion), channel_id=1, source_target_pairs={{32,0},{64,32},{96,64},{0,96},{33,1},{65,33},{97,65},{1,97},{34,2}... | collective-permute-start | bytes 2359304 | tf_op jit(solution)/shard_map/ppermute | solution.py:197
  134.9 2.4 %collective-permute-start.14 = (bf16[96,4096]{1,0:T(8,128)(2,1)}, bf16[96,4096]{1,0:T(8,128)(2,1)S(1)}, u32[]{:S(2)}, u32[]{:S(2)}) collective-permute-start(bf16[96,4096]{1,0:T(8,128)(2,1)} %pad_maximum_fusion.1), channel_id=1, source_target_pairs={{8,0},{16,8},{24,16},{0,24},{9,1},{17,9},{25,17},{1,25},{10,2},{18... | collective-permute-start | bytes 2359304 | tf_op jit(solution)/shard_map/ppermute | solution.py:197
  137.3 14.9 %collective-permute-done.10.refs_10_ = bf16[96,4096]{1,0:T(8,128)(2,1)S(1)} collective-permute-done((bf16[96,4096]{1,0:T(8,128)(2,1)}, bf16[96,4096]{1,0:T(8,128)(2,1)S(1)}, u32[]{:S(2)}, u32[]{:S(2)}) %collective-permute-start.10) | collective-permute-done | bytes 786464 | tf_op jit(solution)/shard_map/ppermute | solution.py:197
  152.2 0.8 slice.75
  153.0 3.3 %collective-permute-start.12 = (bf16[48,4096]{1,0:T(8,128)(2,1)}, bf16[48,4096]{1,0:T(8,128)(2,1)S(1)}, u32[]{:S(2)}, u32[]{:S(2)}) collective-permute-start(bf16[48,4096]{1,0:T(8,128)(2,1)} %slice.75), channel_id=1, source_target_pairs={{32,0},{64,32},{96,64},{0,96},{33,1},{65,33},{97,65},{1,97},{34,2}... | collective-permute-start | bytes 1179656 | tf_op jit(solution)/shard_map/ppermute | solution.py:197
  156.3 0.8 slice.76
  157.2 0.9 slice.77
  158.0 2.4 %collective-permute-start.16 = (bf16[48,4096]{1,0:T(8,128)(2,1)}, bf16[48,4096]{1,0:T(8,128)(2,1)S(1)}, u32[]{:S(2)}, u32[]{:S(2)}) collective-permute-start(bf16[48,4096]{1,0:T(8,128)(2,1)} %slice.77), channel_id=1, source_target_pairs={{8,0},{16,8},{24,16},{0,24},{9,1},{17,9},{25,17},{1,25},{10,2},{18... | collective-permute-start | bytes 1179656 | tf_op jit(solution)/shard_map/ppermute | solution.py:197
  160.4 0.9 slice.78
  161.3 0.6 stack.142.refs_0_
  162.0 0.6 pad_add_fusion.1.refs_1_
  162.5 1.8 collective-permute-done.12.refs_12_
  164.3 3.9 %collective-permute-done.13.refs_13_ = bf16[48,4096]{1,0:T(8,128)(2,1)S(1)} collective-permute-done((bf16[48,4096]{1,0:T(8,128)(2,1)}, bf16[48,4096]{1,0:T(8,128)(2,1)S(1)}, u32[]{:S(2)}, u32[]{:S(2)}) %collective-permute-start.13) | collective-permute-done | bytes 393248 | tf_op jit(solution)/shard_map/ppermute | solution.py:197
  168.2 3.9 %collective-permute-done.17.refs_17_ = bf16[48,4096]{1,0:T(8,128)(2,1)} collective-permute-done((bf16[48,4096]{1,0:T(8,128)(2,1)}, bf16[48,4096]{1,0:T(8,128)(2,1)}, u32[]{:S(2)}, u32[]{:S(2)}) %collective-permute-start.17) | collective-permute-done | bytes 393248 | tf_op jit(solution)/shard_map/ppermute | solution.py:197
  172.2 11.3 %gram.3 = f32[272,1024]{1,0:T(8,128)} custom-call(s32[27]{0:T(128)} %stack.142.refs_0_, s32[4]{0:T(128)} %pad_add_fusion.1.refs_1_, bf16[256,4096]{1,0:T(8,128)(2,1)} %collective-permute-done.18.refs_2_, bf16[64,4096]{1,0:T(8,128)(2,1)} %pack.1.refs_3_, bf16[64,4096]{1,0:T(8,128)(2,1)} %copy-done.9, bf16[64,4096]{1,0:T(8,128)(2,1)} %copy-done.6, ...), custom_call_target="tpu_custom_call" | custom-call | flops 2281701376 | bytes 12582912 | tf_op jit(solution)/shard_map/gram/pallas_call | solution.py:140
  183.5 2.3 %collective-permute-start.19 = (f32[272,1024]{1,0:T(8,128)}, f32[272,1024]{1,0:T(8,128)S(1)}, u32[]{:S(2)}, u32[]{:S(2)}) collective-permute-start(f32[272,1024]{1,0:T(8,128)} %gram.3), channel_id=1, source_target_pairs={{0,4},{4,0},{1,5},{5,1},{2,6},{6,2},{3,7},{7,3},{8,12},{12,8},{9,1... | collective-permute-start | bytes 3342344 | tf_op jit(solution)/shard_map/ppermute | solution.py:201
  185.9 0.6 pad_add_fusion.info_ref
  187.1 11.4 %gram.2.own_ref = f32[272,1024]{1,0:T(8,128)} custom-call(s32[27]{0:T(128)} %stack.142.refs_0_, s32[4]{0:T(128)} %pad_add_fusion.1.refs_1_, bf16[256,4096]{1,0:T(8,128)(2,1)} %all-gather.2.cloned.1.call-done.refs_2_, bf16[64,4096]{1,0:T(8,128)(2,1)} %pack.1.refs_3_, bf16[64,4096]{1,0:T(8,128)(2,1)} %copy-done.9, bf16[64,4096]{1,0:T(8,128)(2,1)} %copy-done.6, ...), custom_call_target="tpu_custom_call" | custom-call | flops 2281701376 | bytes 12582912 | tf_op jit(solution)/shard_map/gram/pallas_call | solution.py:140
  198.4 1.0 copy-done.15
  199.4 3.3 %finish.1 = (f32[8,2048]{1,0:T(8,128)}, f32[256,2048]{1,0:T(8,128)}) custom-call(s32[3]{0:T(128)} %pad_add_fusion.info_ref, f32[1]{0:T(128)} %bitcast.4.total_ref, f32[272,1024]{1,0:T(8,128)} %gram.2.own_ref, f32[272,1024]{1,0:T(8,128)} %copy-done.15), custom_call_target="tpu_custom_call" | custom-call | tf_op jit(solution)/shard_map/finish/pallas_call | solution.py:183
  202.7 1.4 slice.63
  (61 shorter events, 0.4 us)
Async XLA Ops:
  7.2 13.0 %copy-start = (f32[2048]{0:T(1024)S(1)}, f32[2048]{0:T(1024)}, u32[]{:S(2)}) copy-start(f32[2048]{0:T(1024)} %param.5) | copy-start | bytes 24580
  10.6 28.5 %all-to-all-start = ((bf16[32,80,256]{2,1,0:T(8,128)(2,1)}), bf16[32,80,256]{2,1,0:T(8,128)(2,1)S(1)}, u32[]{:S(2)}, u32[]{:S(2)}) async-start(bf16[32,80,256]{2,1,0:T(8,128)(2,1)} %pick.1), calls=%async_computation | async-start | bytes 2621440 | tf_op jit(solution)/shard_map/all_to_all | solution.py:206
  20.1 111.4 %all-gather.2.cloned.1.call-start = ((), (), s32[]{:S(2)}) async-start(), calls=%async_computation.1 | async-start | bytes 2621440 | tf_op jit(solution)/shard_map/all_gather | solution.py:226
  39.2 8.4 %copy-start.1 = (bf16[32,80,256]{2,1,0:T(8,128)(2,1)}, bf16[32,80,256]{2,1,0:T(8,128)(2,1)S(1)}, u32[]{:S(2)}) copy-start(bf16[32,80,256]{2,1,0:T(8,128)(2,1)S(1)} %all-to-all-done.in_ref) | copy-start | bytes 3932164
  39.2 5.8 %collective-permute-start = (f32[32,256]{1,0:T(8,128)S(1)}, f32[32,256]{1,0:T(8,128)S(1)}, u32[]{:S(2)}, u32[]{:S(2)}) collective-permute-start(f32[32,256]{1,0:T(8,128)S(1)} %fusion), channel_id=1, source_target_pairs={{2,0},{3,1},{0,2},{1,3},{6,4},{7,5},{4,6},{5,7},{10,8},{11,9},{8,1... | collective-permute-start | bytes 98312 | tf_op jit(solution)/shard_map/ppermute | solution.py:197
  42.2 2.8 %collective-permute-start.1 = (f32[32,256]{1,0:T(8,128)S(1)}, f32[32,256]{1,0:T(8,128)S(1)}, u32[]{:S(2)}, u32[]{:S(2)}) collective-permute-start(f32[32,256]{1,0:T(8,128)S(1)} %fusion), channel_id=1, source_target_pairs={{1,0},{2,1},{3,2},{0,3},{5,4},{6,5},{7,6},{4,7},{9,8},{10,9},{11,1... | collective-permute-start | bytes 98312 | tf_op jit(solution)/shard_map/ppermute | solution.py:197
  43.0 4.0 %collective-permute-start.2 = (f32[32,256]{1,0:T(8,128)S(1)}, f32[32,256]{1,0:T(8,128)S(1)}, u32[]{:S(2)}, u32[]{:S(2)}) collective-permute-start(f32[32,256]{1,0:T(8,128)S(1)} %fusion), channel_id=1, source_target_pairs={{3,0},{0,1},{1,2},{2,3},{7,4},{4,5},{5,6},{6,7},{11,8},{8,9},{9,10... | collective-permute-start | bytes 98312 | tf_op jit(solution)/shard_map/ppermute | solution.py:197
  51.7 12.4 %collective-permute-start.6 = (bf16[64,4096]{1,0:T(8,128)(2,1)}, bf16[64,4096]{1,0:T(8,128)(2,1)S(1)}, u32[]{:S(2)}, u32[]{:S(2)}) collective-permute-start(bf16[64,4096]{1,0:T(8,128)(2,1)} %pack.1.refs_3_), channel_id=1, source_target_pairs={{32,0},{64,32},{96,64},{0,96},{33,1},{65,33},{97,65},{1,97},{34,2}... | collective-permute-start | bytes 1572872 | tf_op jit(solution)/shard_map/ppermute | solution.py:197
  53.2 12.5 %collective-permute-start.7 = (bf16[64,4096]{1,0:T(8,128)(2,1)}, bf16[64,4096]{1,0:T(8,128)(2,1)S(1)}, u32[]{:S(2)}, u32[]{:S(2)}) collective-permute-start(bf16[64,4096]{1,0:T(8,128)(2,1)} %pack.1.refs_3_), channel_id=1, source_target_pairs={{96,0},{0,32},{32,64},{64,96},{97,1},{1,33},{33,65},{65,97},{98,2}... | collective-permute-start | bytes 1572872 | tf_op jit(solution)/shard_map/ppermute | solution.py:197
  53.2 35.8 %collective-permute-start.8 = (bf16[64,4096]{1,0:T(8,128)(2,1)}, bf16[64,4096]{1,0:T(8,128)(2,1)S(1)}, u32[]{:S(2)}, u32[]{:S(2)}) collective-permute-start(bf16[64,4096]{1,0:T(8,128)(2,1)} %pack.1.refs_3_), channel_id=1, source_target_pairs={{64,0},{96,32},{0,64},{32,96},{65,1},{97,33},{1,65},{33,97},{66,2}... | collective-permute-start | bytes 1572872 | tf_op jit(solution)/shard_map/ppermute | solution.py:197
  55.6 34.5 %collective-permute-start.3 = (bf16[64,4096]{1,0:T(8,128)(2,1)}, bf16[64,4096]{1,0:T(8,128)(2,1)S(1)}, u32[]{:S(2)}, u32[]{:S(2)}) collective-permute-start(bf16[64,4096]{1,0:T(8,128)(2,1)} %pack.1.refs_3_), channel_id=1, source_target_pairs={{8,0},{16,8},{24,16},{0,24},{9,1},{17,9},{25,17},{1,25},{10,2},{18... | collective-permute-start | bytes 1572872 | tf_op jit(solution)/shard_map/ppermute | solution.py:197
  56.0 34.2 %collective-permute-start.4 = (bf16[64,4096]{1,0:T(8,128)(2,1)}, bf16[64,4096]{1,0:T(8,128)(2,1)S(1)}, u32[]{:S(2)}, u32[]{:S(2)}) collective-permute-start(bf16[64,4096]{1,0:T(8,128)(2,1)} %pack.1.refs_3_), channel_id=1, source_target_pairs={{24,0},{0,8},{8,16},{16,24},{25,1},{1,9},{9,17},{17,25},{26,2},{2,... | collective-permute-start | bytes 1572872 | tf_op jit(solution)/shard_map/ppermute | solution.py:197
  64.1 26.0 %copy-start.6 = (bf16[64,4096]{1,0:T(8,128)(2,1)}, bf16[64,4096]{1,0:T(8,128)(2,1)S(1)}, u32[]{:S(2)}) copy-start(bf16[64,4096]{1,0:T(8,128)(2,1)S(1)} %collective-permute-done.6.refs_5_) | copy-start | bytes 1572868
  64.1 26.1 %collective-permute-start.5 = (bf16[64,4096]{1,0:T(8,128)(2,1)}, bf16[64,4096]{1,0:T(8,128)(2,1)S(1)}, u32[]{:S(2)}, u32[]{:S(2)}) collective-permute-start(bf16[64,4096]{1,0:T(8,128)(2,1)} %pack.1.refs_3_), channel_id=1, source_target_pairs={{16,0},{24,8},{0,16},{8,24},{17,1},{25,9},{1,17},{9,25},{18,2},{26... | collective-permute-start | bytes 1572872 | tf_op jit(solution)/shard_map/ppermute | solution.py:197
  65.7 24.5 %copy-start.7 = (bf16[64,4096]{1,0:T(8,128)(2,1)}, bf16[64,4096]{1,0:T(8,128)(2,1)S(1)}, u32[]{:S(2)}) copy-start(bf16[64,4096]{1,0:T(8,128)(2,1)S(1)} %collective-permute-done.7.refs_7_) | copy-start | bytes 1572868
  65.7 25.7 %collective-permute-start.9 = (bf16[64,4096]{1,0:T(8,128)(2,1)}, bf16[64,4096]{1,0:T(8,128)(2,1)}, u32[]{:S(2)}, u32[]{:S(2)}) collective-permute-start(bf16[64,4096]{1,0:T(8,128)(2,1)} %pack.1.refs_3_), channel_id=1, source_target_pairs={{0,0},{1,32},{2,64},{3,96},{32,1},{33,33},{34,65},{35,97},{64,2},{... | collective-permute-start | bytes 1572872 | tf_op jit(solution)/shard_map/ppermute | solution.py:220
  89.1 1.1 copy-start.8
  90.1 1.3 copy-start.9
  90.2 1.2 copy-start.10
  90.2 44.7 %copy-start.11 = (bf16[64,4096]{1,0:T(8,128)(2,1)}, bf16[64,4096]{1,0:T(8,128)(2,1)S(1)}, u32[]{:S(2)}) copy-start(bf16[64,4096]{1,0:T(8,128)(2,1)S(1)} %collective-permute-done.5.refs_8_) | copy-start | bytes 1572868
  131.5 40.6 %collective-permute-start.18 = (bf16[256,4096]{1,0:T(8,128)(2,1)}, bf16[256,4096]{1,0:T(8,128)(2,1)}, u32[]{:S(2)}, u32[]{:S(2)}) collective-permute-start(bf16[256,4096]{1,0:T(8,128)(2,1)} %all-gather.2.cloned.1.call-done.refs_2_), channel_id=1, source_target_pairs={{0,4},{4,0},{1,5},{5,1},{2,6},{6,2},{3,7},{7,3},{8,12},{12,8},{9,1... | collective-permute-start | bytes 6291464 | tf_op jit(solution)/shard_map/ppermute | solution.py:201
  132.2 20.0 %collective-permute-start.10 = (bf16[96,4096]{1,0:T(8,128)(2,1)}, bf16[96,4096]{1,0:T(8,128)(2,1)S(1)}, u32[]{:S(2)}, u32[]{:S(2)}) collective-permute-start(bf16[96,4096]{1,0:T(8,128)(2,1)} %pad_maximum_fusion), channel_id=1, source_target_pairs={{32,0},{64,32},{96,64},{0,96},{33,1},{65,33},{97,65},{1,97},{34,2}... | collective-permute-start | bytes 2359304 | tf_op jit(solution)/shard_map/ppermute | solution.py:197
  134.9 21.4 %collective-permute-start.11 = (bf16[96,4096]{1,0:T(8,128)(2,1)}, bf16[96,4096]{1,0:T(8,128)(2,1)S(1)}, u32[]{:S(2)}, u32[]{:S(2)}) collective-permute-start(bf16[96,4096]{1,0:T(8,128)(2,1)} %pad_maximum_fusion), channel_id=1, source_target_pairs={{96,0},{0,32},{32,64},{64,96},{97,1},{1,33},{33,65},{65,97},{98,2}... | collective-permute-start | bytes 2359304 | tf_op jit(solution)/shard_map/ppermute | solution.py:197
  134.9 22.3 %collective-permute-start.14 = (bf16[96,4096]{1,0:T(8,128)(2,1)}, bf16[96,4096]{1,0:T(8,128)(2,1)S(1)}, u32[]{:S(2)}, u32[]{:S(2)}) collective-permute-start(bf16[96,4096]{1,0:T(8,128)(2,1)} %pad_maximum_fusion.1), channel_id=1, source_target_pairs={{8,0},{16,8},{24,16},{0,24},{9,1},{17,9},{25,17},{1,25},{10,2},{18... | collective-permute-start | bytes 2359304 | tf_op jit(solution)/shard_map/ppermute | solution.py:197
  137.3 23.2 %collective-permute-start.15 = (bf16[96,4096]{1,0:T(8,128)(2,1)}, bf16[96,4096]{1,0:T(8,128)(2,1)S(1)}, u32[]{:S(2)}, u32[]{:S(2)}) collective-permute-start(bf16[96,4096]{1,0:T(8,128)(2,1)} %pad_maximum_fusion.1), channel_id=1, source_target_pairs={{24,0},{0,8},{8,16},{16,24},{25,1},{1,9},{9,17},{17,25},{26,2},{2,... | collective-permute-start | bytes 2359304 | tf_op jit(solution)/shard_map/ppermute | solution.py:197
  152.2 9.2 %copy-start.2 = (bf16[96,4096]{1,0:T(8,128)(2,1)}, bf16[96,4096]{1,0:T(8,128)(2,1)S(1)}, u32[]{:S(2)}) copy-start(bf16[96,4096]{1,0:T(8,128)(2,1)S(1)} %collective-permute-done.10.refs_10_) | copy-start | bytes 2359300
  153.0 11.3 %collective-permute-start.12 = (bf16[48,4096]{1,0:T(8,128)(2,1)}, bf16[48,4096]{1,0:T(8,128)(2,1)S(1)}, u32[]{:S(2)}, u32[]{:S(2)}) collective-permute-start(bf16[48,4096]{1,0:T(8,128)(2,1)} %slice.75), channel_id=1, source_target_pairs={{32,0},{64,32},{96,64},{0,96},{33,1},{65,33},{97,65},{1,97},{34,2}... | collective-permute-start | bytes 1179656 | tf_op jit(solution)/shard_map/ppermute | solution.py:197
  156.3 15.8 %copy-start.3 = (bf16[96,4096]{1,0:T(8,128)(2,1)}, bf16[96,4096]{1,0:T(8,128)(2,1)S(1)}, u32[]{:S(2)}) copy-start(bf16[96,4096]{1,0:T(8,128)(2,1)S(1)} %collective-permute-done.11.refs_11_) | copy-start | bytes 2359300
  157.2 11.1 %collective-permute-start.13 = (bf16[48,4096]{1,0:T(8,128)(2,1)}, bf16[48,4096]{1,0:T(8,128)(2,1)S(1)}, u32[]{:S(2)}, u32[]{:S(2)}) collective-permute-start(bf16[48,4096]{1,0:T(8,128)(2,1)} %slice.76), channel_id=1, source_target_pairs={{96,0},{0,32},{32,64},{64,96},{97,1},{1,33},{33,65},{65,97},{98,2}... | collective-permute-start | bytes 1179656 | tf_op jit(solution)/shard_map/ppermute | solution.py:197
  157.2 15.0 %copy-start.4 = (bf16[96,4096]{1,0:T(8,128)(2,1)}, bf16[96,4096]{1,0:T(8,128)(2,1)S(1)}, u32[]{:S(2)}) copy-start(bf16[96,4096]{1,0:T(8,128)(2,1)S(1)} %collective-permute-done.14.refs_14_) | copy-start | bytes 2359300
  158.0 10.2 %collective-permute-start.16 = (bf16[48,4096]{1,0:T(8,128)(2,1)}, bf16[48,4096]{1,0:T(8,128)(2,1)S(1)}, u32[]{:S(2)}, u32[]{:S(2)}) collective-permute-start(bf16[48,4096]{1,0:T(8,128)(2,1)} %slice.77), channel_id=1, source_target_pairs={{8,0},{16,8},{24,16},{0,24},{9,1},{17,9},{25,17},{1,25},{10,2},{18... | collective-permute-start | bytes 1179656 | tf_op jit(solution)/shard_map/ppermute | solution.py:197
  160.4 11.7 %copy-start.5 = (bf16[96,4096]{1,0:T(8,128)(2,1)}, bf16[96,4096]{1,0:T(8,128)(2,1)S(1)}, u32[]{:S(2)}) copy-start(bf16[96,4096]{1,0:T(8,128)(2,1)S(1)} %collective-permute-done.15.refs_15_) | copy-start | bytes 2359300
  161.3 10.8 %collective-permute-start.17 = (bf16[48,4096]{1,0:T(8,128)(2,1)}, bf16[48,4096]{1,0:T(8,128)(2,1)}, u32[]{:S(2)}, u32[]{:S(2)}) collective-permute-start(bf16[48,4096]{1,0:T(8,128)(2,1)} %slice.78), channel_id=1, source_target_pairs={{24,0},{0,8},{8,16},{16,24},{25,1},{1,9},{9,17},{17,25},{26,2},{2,... | collective-permute-start | bytes 1179656 | tf_op jit(solution)/shard_map/ppermute | solution.py:197
  164.3 7.9 %copy-start.12 = (bf16[48,4096]{1,0:T(8,128)(2,1)}, bf16[48,4096]{1,0:T(8,128)(2,1)S(1)}, u32[]{:S(2)}) copy-start(bf16[48,4096]{1,0:T(8,128)(2,1)S(1)} %collective-permute-done.12.refs_12_) | copy-start | bytes 1179652
  168.2 3.9 %copy-start.13 = (bf16[48,4096]{1,0:T(8,128)(2,1)}, bf16[48,4096]{1,0:T(8,128)(2,1)S(1)}, u32[]{:S(2)}) copy-start(bf16[48,4096]{1,0:T(8,128)(2,1)S(1)} %collective-permute-done.13.refs_13_) | copy-start | bytes 1179652
  168.2 3.9 %copy-start.14 = (bf16[48,4096]{1,0:T(8,128)(2,1)}, bf16[48,4096]{1,0:T(8,128)(2,1)S(1)}, u32[]{:S(2)}) copy-start(bf16[48,4096]{1,0:T(8,128)(2,1)S(1)} %collective-permute-done.16.refs_16_) | copy-start | bytes 1179652
  183.5 14.9 %collective-permute-start.19 = (f32[272,1024]{1,0:T(8,128)}, f32[272,1024]{1,0:T(8,128)S(1)}, u32[]{:S(2)}, u32[]{:S(2)}) collective-permute-start(f32[272,1024]{1,0:T(8,128)} %gram.3), channel_id=1, source_target_pairs={{0,4},{4,0},{1,5},{5,1},{2,6},{6,2},{3,7},{7,3},{8,12},{12,8},{9,1... | collective-permute-start | bytes 3342344 | tf_op jit(solution)/shard_map/ppermute | solution.py:201
  198.4 1.0 copy-start.15
Sparse Core Ops, SparseCore 0:
  91.5 39.9 all-gather.1

commit v3 on v2

v3 whole, which is shorter than its diff:
```python
import jax
import jax.numpy as jnp
from jax import lax
from jax.experimental import pallas as pl
from jax.experimental.pallas import tpu as pltpu
from jax.sharding import Mesh, PartitionSpec as P

epsilon = 1e-05
TOK = ("z", "x", "c")
SLOTS = 256
LIVE = 4096
WIDTH = 2048
PIECE = 64
EXTRA = 16
LONG = LIVE + 128
VMEM = 60 * 1024 * 1024
bf16 = jnp.bfloat16
f32 = jnp.float32


def params(**kw):
    return pltpu.CompilerParams(vmem_limit_bytes=VMEM, **kw)


def spread(value, place):
    high = value.astype(bf16).astype(f32)
    middle = (value - high).astype(bf16).astype(f32)
    low = value - high - middle
    rest = jnp.where(place == 2, low, 0.0)
    return jnp.where(place == 0, high, jnp.where(place == 1, middle, rest))


def pick_kernel(index_ref, counts_ref, resid_ref, out_ref):
    tokens = resid_ref.shape[0]
    token = lax.broadcasted_iota(jnp.int32, (tokens, SLOTS), 0)
    slot = lax.broadcasted_iota(jnp.int32, (1, SLOTS), 1)
    half = SLOTS // 2
    end = jnp.where(slot < half, counts_ref[0], half + counts_ref[1])
    kept = jnp.where(slot < end, index_ref[...], -1)
    one_hot = jnp.where(token == kept, 1.0, 0.0).astype(bf16)
    total = jnp.zeros((1, SLOTS), f32)
    step = 512
    for x in range(4):
        part = lax.dot_general(
            resid_ref[:, x * step : (x + 1) * step],
            one_hot,
            (((0,), (0,)), ((), ())),
            preferred_element_type=f32,
        )
        total += jnp.sum(part * part, axis=0, keepdims=True)
        short = part.astype(bf16)
        for c in range(2):
            for z in range(4):
                first = (c * 4 + z) * PIECE
                out_ref[z * 8 + x * 2 + c, :PIECE, :] = short[first : first + PIECE, :]
    live = (counts_ref[0] + counts_ref[1]).astype(f32)
    row = lax.broadcasted_iota(jnp.int32, (EXTRA, SLOTS), 0)
    extra = jnp.where(row == 3, live, spread(total, row)).astype(bf16)
    for t in range(32):
        out_ref[t, PIECE:, :] = extra


def pick(resid, keep_index, counts):
    return pl.pallas_call(
        pick_kernel,
        out_shape=jax.ShapeDtypeStruct((32, PIECE + EXTRA, SLOTS), bf16),
        in_specs=[
            pl.BlockSpec(memory_space=pltpu.VMEM),
            pl.BlockSpec(memory_space=pltpu.SMEM),
            pl.BlockSpec(memory_space=pltpu.VMEM),
        ],
        out_specs=pl.BlockSpec(memory_space=pltpu.VMEM),
        compiler_params=params(),
        name="pick",
    )(keep_index[None, :], counts, resid)


def pack_kernel(first_ref, in_ref, scale_ref, gain_ref, out_ref, acc_ref):
    acc_ref[...] = jnp.zeros_like(acc_ref)
    gain = gain_ref[...]
    group = 4

    def body(g, _):
        moved = []
        for k in range(group):
            t = g * group + k
            rows = in_ref[t, :PIECE, :].astype(f32) * scale_ref[pl.ds(t, 1), :] * gain
            first = first_ref[t]
            base = pl.multiple_of((first // 128) * 128, 128)
            wide = jnp.concatenate([rows, jnp.zeros((PIECE, 128), f32)], axis=1)
            moved.append((base, pltpu.roll(wide, first - base, 1)))
        for base, rows in moved:
            acc_ref[:, pl.ds(base, SLOTS + 128)] += rows
        return 0

    lax.fori_loop(0, 32 // group, body, 0)
    short = acc_ref[:, :LIVE].astype(bf16)
    out_ref[:, :LIVE] = short
    total = jnp.sum(short.astype(f32), axis=1, keepdims=True)
    lane = lax.broadcasted_iota(jnp.int32, (PIECE, 128), 1)
    out_ref[:, LIVE:] = spread(total, lane).astype(bf16)


def pack(first, pieces, scale, gain):
    return pl.pallas_call(
        pack_kernel,
        out_shape=jax.ShapeDtypeStruct((PIECE, LONG), bf16),
        in_specs=[pl.BlockSpec(memory_space=pltpu.SMEM)] + [pl.BlockSpec(memory_space=pltpu.VMEM)] * 3,
        out_specs=pl.BlockSpec(memory_space=pltpu.VMEM),
        scratch_shapes=[pltpu.VMEM((PIECE, LIVE + SLOTS + 128), f32)],
        compiler_params=params(),
        name="pack",
    )(first, pieces, scale, gain)


def gram_kernel(row_place, col_place, row_where, col_where, *refs):
    arrays = refs[: 2 + 8]
    own_ref, given_ref, rows, cols, row_sem, sem = refs[2 + 8 :]
    row_copies = []
    for k, (index, start, height) in enumerate(row_place):
        first = pl.multiple_of(row_where[k], 32)
        source = arrays[index].at[pl.ds(start, height), pl.ds(0, LIVE)]
        row_copies.append(pltpu.make_async_copy(source, rows.at[pl.ds(first, height)], row_sem.at[k]))
    copies = []
    for k, (index, start, height, block) in enumerate(col_place):
        first = pl.multiple_of(col_where[k], 16)
        source = arrays[2 + index].at[pl.ds(start, height)]
        copies.append((block, pltpu.make_async_copy(source, cols.at[pl.ds(first, height)], sem.at[k])))
    copies.sort(key=lambda pair: pair[0])
    for copy in row_copies:
        copy.start()
    for _, copy in copies:
        copy.start()
    for copy in row_copies:
        copy.wait()
    lane = lax.broadcasted_iota(jnp.int32, (16, 128), 1)
    terms = jnp.where(lane < 3, 1.0, 0.0).astype(bf16)
    for block in range(2):
        for at, copy in copies:
            if at == block:
                copy.wait()
        inside = slice(block * 256, (block + 1) * 256)
        product = lax.dot_general(
            rows[...], cols[inside, :LIVE], (((1,), (1,)), ((), ())), preferred_element_type=f32
        )
        own_ref[:256, inside] = product[:256]
        given_ref[:256, inside] = product[256:]
        sums = lax.dot_general(
            terms, cols[inside, LIVE:], (((1,), (1,)), ((), ())), preferred_element_type=f32
        )
        own_ref[256:, inside] = sums[:8]
        given_ref[256:, inside] = sums[:8]


def gram(row_where, col_where, arrays, row_place, col_place):
    n_cols = 512
    return pl.pallas_call(
        lambda *refs: gram_kernel(row_place, col_place, *refs),
        out_shape=(jax.ShapeDtypeStruct((264, n_cols), f32),) * 2,
        in_specs=[pl.BlockSpec(memory_space=pltpu.SMEM)] * 2
        + [pl.BlockSpec(memory_space=pl.ANY)] * len(arrays),
        out_specs=(pl.BlockSpec(memory_space=pltpu.VMEM),) * 2,
        scratch_shapes=[
            pltpu.VMEM((512, LIVE), bf16),
            pltpu.VMEM((n_cols, LONG), bf16),
            pltpu.SemaphoreType.DMA((len(row_place),)),
            pltpu.SemaphoreType.DMA((len(col_place),)),
        ],
        compiler_params=params(),
        cost_estimate=pl.CostEstimate(
            flops=2 * 512 * n_cols * LIVE, bytes_accessed=10 * 1024 * 1024, transcendentals=0
        ),
        name="gram",
    )(row_where, col_where, *arrays)


def finish_kernel(info_ref, total_ref, own0_ref, own1_ref, got0_ref, got1_ref, mean_ref, out_ref):
    core, row_first, col_first, place = info_ref[0], info_ref[1], info_ref[2], info_ref[3]
    total = total_ref[0]
    row = row_first + lax.broadcasted_iota(jnp.int32, (256, 256), 0)
    col = col_first + lax.broadcasted_iota(jnp.int32, (256, 256), 1)
    for k, flip in enumerate((0, 1, 3, 2)):
        x = place ^ flip
        inside = slice((k % 2) * 256, (k % 2 + 1) * 256)
        for ref, side in (
            ((own0_ref, own1_ref)[k // 2], core),
            ((got0_ref, got1_ref)[k // 2], 1 - core),
        ):
            at = pl.multiple_of(x * 512 + side * 256, 256)
            values = ref[:256, inside] / total
            out_ref[:, pl.ds(at, 256)] = jnp.where(row <= col + at, values, 0.0)
            mean_ref[:, pl.ds(at, 256)] = ref[256:264, inside][:1] / total


def finish(info, total, own, got):
    return pl.pallas_call(
        finish_kernel,
        out_shape=(
            jax.ShapeDtypeStruct((1, WIDTH), f32),
            jax.ShapeDtypeStruct((256, WIDTH), f32),
        ),
        in_specs=[pl.BlockSpec(memory_space=pltpu.SMEM)] * 2 + [pl.BlockSpec(memory_space=pltpu.VMEM)] * 4,
        out_specs=(pl.BlockSpec(memory_space=pltpu.VMEM),) * 2,
        compiler_params=params(),
        name="finish",
    )(info, total, *own, *got)


def shift(value, axis, by):
    return lax.ppermute(value, axis, [((i + by) % 4, i) for i in range(4)])


def swap(value):
    return lax.ppermute(value, "c", [(0, 1), (1, 0)])


def trade(value, axis, flip):
    return lax.ppermute(value, axis, [(i, i ^ flip) for i in range(4)])


def join(*values):
    return jnp.concatenate(values, axis=0)


def per_device(resid, norm_gain, keep_index, counts):
    z, x, c, y = (lax.axis_index(a) for a in ("z", "x", "c", "y"))
    pieces = lax.all_to_all(pick(resid, keep_index, counts), TOK, 0, 0, tiled=True)

    extra = pieces[:, PIECE : PIECE + 4, :].astype(f32)
    loads = extra[:, 3, 0].astype(jnp.int32)
    first = jnp.cumsum(loads) - loads
    kept_total = jnp.sum(loads).astype(f32)
    sums = extra[:, 0, :] + extra[:, 1, :] + extra[:, 2, :]
    squares = (sums + shift(sums, "y", 2)) + (shift(sums, "y", 1) + shift(sums, "y", 3))
    scale = lax.rsqrt(squares / 8192 + epsilon)
    gain = lax.dynamic_slice_in_dim(norm_gain, ((x * 2 + c) * 4 + z) * PIECE, PIECE)[:, None]
    mine = pack(first, pieces, scale, gain)

    turned = lax.ppermute(mine, ("z", "y"), [(i * 4 + j, j * 4 + i) for i in range(4) for j in range(4)])

    partners = (("x", 1), ("z", 1), ("x", 3), ("z", 3))
    streams = [mine[s * 16 : (s + 1) * 16] for s in range(4)]
    held = [[(0, 0)]] * 4
    arrays, place, where = [], [[], []], [[], []]
    for step in range(4):
        for s in range(4):
            axis, flip = partners[(s + step) % 4]
            dx, dz = (flip, 0) if axis == "x" else (0, flip)
            got = trade(streams[s], axis, flip)
            told = [(a ^ dx, b ^ dz) for a, b in held[s]]
            if step < 3:
                streams[s] = join(streams[s], got)
                held[s] = held[s] + told
                continue
            for value, tags in ((streams[s], held[s]), (got, told)):
                for k, (a, b) in enumerate(tags):
                    block = (0, 1, 3, 2).index(a)
                    place[block // 2].append((len(arrays), k * 16, 16, block % 2))
                    where[block // 2].append((block % 2) * 256 + (z ^ b) * PIECE + s * 16)
                arrays.append(value)

    low, high = turned[:32], turned[32:]
    low, high = join(low, trade(low, "y", 1)), join(high, trade(high, "y", 3))
    low, high = join(low, trade(low, "y", 3)), join(high, trade(high, "y", 1))
    rows = join(low, high)
    other = swap(rows)
    row_place, row_where = [], []
    for index in range(2):
        for k in range(8):
            flip = ((0, 1, 3, 2), (0, 3, 1, 2))[k // 4][k % 4]
            row_place.append((index, k * 32, 32))
            row_where.append(index * 256 + (y ^ flip) * PIECE + k // 4 * 32)
    row_where = jnp.stack(row_where).astype(jnp.int32)

    own, got = [], []
    for k in range(2):
        col_where = jnp.stack(where[k]).astype(jnp.int32)
        kept, given = gram(row_where, col_where, [rows, other, *arrays], tuple(row_place), tuple(place[k]))
        own.append(kept)
        got.append(swap(given))
    info = jnp.stack([c, (z * 8 + x * 2 + c) * 256, y * WIDTH, x]).astype(jnp.int32)
    mean, gram_factor = finish(info, kept_total[None], own, got)
    return (mean[0], gram_factor)


def solution(mesh):
    fine = Mesh(mesh.devices.reshape(4, 4, 2, 4), ("z", "x", "c", "y"))
    return jax.shard_map(
        per_device,
        mesh=fine,
        in_specs=(P(TOK, "y"), P("y"), P(TOK), P(TOK)),
        out_specs=(P("y"), P(TOK, "y")),
        check_vma=False,
    )
```

time: 212 us -> 177 us (0.83)
  waiting for transfers between devices: 110 us -> 82.4 us
  between operations: 14.9 us -> 1.6 us
  starting transfers between devices: 39.4 us -> 50.2 us
  local copies, waits for them, and re-layouts: 7.46 us -> 4.36 us
    ppermute x0 -> x20, waiting for transfers between devices: none -> 62.1 us  [trade(): return lax.ppermute(value, axis, [(i, i ^ flip) for i in range(4)])]
    ppermute x17 -> x3, waiting for transfers between devices: 52.1 us -> 1.3 us  [shift(): return lax.ppermute(value, axis, [((i + by) % 4, i) for i in range(4)])]
    all_gather x1 -> x0, waiting for transfers between devices: 40.1 us -> none  [per_device(): rows = lax.all_gather(turned, 'y', axis=0, tiled=True)]
    ppermute x0 -> x20, starting transfers between devices: none -> 29.4 us  [trade(): return lax.ppermute(value, axis, [(i, i ^ flip) for i in range(4)])]
    ppermute x17 -> x3, starting transfers between devices: 21.6 us -> 4.45 us  [shift(): return lax.ppermute(value, axis, [((i + by) % 4, i) for i in range(4)])]
    ppermute x1, starting transfers between devices: 5.34 us -> 0.68 us  [per_device(): lax.ppermute(mine, ('z', 'y'), [(i * 4 + j, j * 4 + i) for i in range(4)...]
    slice x11 -> x2, local copies, waits for them, and re-layouts: 4.97 us -> 1.25 us  [the longest x1 1.2 us: per_device(): streams = [mine[s * 16:(s + 1) * 16] for s in range(4)]]
    ppermute x2 -> x3, starting transfers between devices: 3.02 us -> 6.3 us  [swap(): return lax.ppermute(value, 'c', [(0, 1), (1, 0)])]
  transfers between devices with their start and end apart: 22 -> 28, of which waited for: 10 -> 13; matrix products, arithmetic and copies ran while one was open for 5% -> 5% of each run, Pallas kernels for 5% -> 6%
where the time goes in v3:
time: 177 us; the launch traced here: 176 us
  waiting for transfers between devices  82.4 us (47%)
  starting transfers between devices  50.2 us (28%)
  Pallas kernels  31.4 us (18%)
  other arithmetic  6.42 us (4%)
  local copies, waits for them, and re-layouts  4.36 us (2%)
    ppermute x20, waiting for transfers between devices, trade(): return lax.ppermute(value, axis, [(i, i ^ flip) for i in range(4)])  62.1 us
    ppermute x20, starting transfers between devices, trade(): return lax.ppermute(value, axis, [(i, i ^ flip) for i in range(4)])  29.4 us
    pallas_call x2, Pallas kernels, gram(): pl.pallas_call(lambda *refs: gram_kernel(row_place, col_place, *refs), ou...  20.5 us
    all_to_all x1, waiting for transfers between devices, per_device(): lax.all_to_all(pick(resid, keep_index, counts), TOK, 0, 0, tiled=True)  18.3 us
    all_to_all x1, starting transfers between devices, per_device(): lax.all_to_all(pick(resid, keep_index, counts), TOK, 0, 0, tiled=True)  9.43 us
    ppermute x3, starting transfers between devices, swap(): return lax.ppermute(value, 'c', [(0, 1), (1, 0)])  6.3 us
    ppermute x3, starting transfers between devices, shift(): return lax.ppermute(value, axis, [((i + by) % 4, i) for i in range(4)])  4.45 us
    pallas_call x1, Pallas kernels, pack(): pl.pallas_call(pack_kernel, out_shape=jax.ShapeDtypeStruct((PIECE, LONG),...  4.22 us
  transfers between devices with their start and end apart: 28, of which 13 were waited for; matrix products, arithmetic and copies ran while one was open for 5% of the time, Pallas kernels for 6%

profile of v3, /device:TPU:1, one launch (start us, length us, event | category | flops | bytes accessed | tf_op | source)
XLA Modules:
  0.0 176.5 jit_solution(11905106468826304973)
XLA Ops:
  0.6 3.5 %pick.1 = bf16[32,80,256]{2,1,0:T(8,128)(2,1)} custom-call(s32[1,256]{1,0:T(1,128)} %bitcast.63, s32[2]{0:T(128)} %counts_ref.1, bf16[512,2048]{1,0:T(8,128)(2,1)} %resid_ref.1), custom_call_target="tpu_custom_call" | custom-call | tf_op jit(solution)/shard_map/pick/pallas_call | solution.py:64
  4.1 9.4 %all-to-all-start = ((bf16[32,80,256]{2,1,0:T(8,128)(2,1)}), bf16[32,80,256]{2,1,0:T(8,128)(2,1)S(1)}, u32[]{:S(2)}, u32[]{:S(2)}) async-start(bf16[32,80,256]{2,1,0:T(8,128)(2,1)} %pick.1), calls=%async_computation | async-start | bytes 2621440 | tf_op jit(solution)/shard_map/all_to_all | solution.py:227
  13.7 0.7 copy.16.gain_ref
  14.3 18.3 %all-to-all-done.in_ref = bf16[32,80,256]{2,1,0:T(8,128)(2,1)S(1)} async-done(((bf16[32,80,256]{2,1,0:T(8,128)(2,1)}), bf16[32,80,256]{2,1,0:T(8,128)(2,1)S(1)}, u32[]{:S(2)}, u32[]{:S(2)}) %all-to-all-start) | async-done | bytes 1310752 | tf_op jit(solution)/shard_map/all_to_all | solution.py:227
  32.7 2.8 %collective-permute-start.1 = (f32[32,256]{1,0:T(8,128)S(1)}, f32[32,256]{1,0:T(8,128)S(1)}, u32[]{:S(2)}, u32[]{:S(2)}) collective-permute-start(f32[32,256]{1,0:T(8,128)S(1)} %fusion), channel_id=1, source_target_pairs={{1,0},{2,1},{3,2},{0,3},{5,4},{6,5},{7,6},{4,7},{9,8},{10,9},{11,1... | collective-permute-start | bytes 98312 | tf_op jit(solution)/shard_map/ppermute | solution.py:210
  35.5 1.6 collective-permute-start
  37.2 0.7 fusion.1
  38.5 1.0 collective-permute-done.2
  39.8 0.6 add_rsqrt_fusion.scale_ref
  40.5 4.2 %pack.1 = bf16[64,4224]{1,0:T(8,128)(2,1)} custom-call(s32[32]{0:T(128)} %sub.3.first_ref, bf16[32,80,256]{2,1,0:T(8,128)(2,1)} %copy-done.3, f32[32,256]{1,0:T(8,128)} %add_rsqrt_fusion.scale_ref, f32[64,1]{1,0:T(8,128)} %copy.16.gain_ref), custom_call_target="tpu_custom_call" | custom-call | tf_op jit(solution)/shard_map/pack/pallas_call | solution.py:105
  44.7 1.2 fusion.4
  45.9 1.7 collective-permute-start.21
  47.6 0.7 collective-permute-start.3
  48.3 2.4 %collective-permute-start.17 = (bf16[16,4224]{1,0:T(8,128)(2,1)S(1)}, bf16[16,4224]{1,0:T(8,128)(2,1)S(1)}, u32[]{:S(2)}, u32[]{:S(2)}) collective-permute-start(bf16[16,4224]{1,0:T(8,128)(2,1)S(1)} %get-tuple-element.17), channel_id=1, source_target_pairs={{0,24},{8,16},{16,8},{24,0},{1,25},{9,17},{17,9},{25,1},{2,26},{10... | collective-permute-start | bytes 405512 | tf_op jit(solution)/shard_map/ppermute | solution.py:218
  50.7 2.2 %collective-permute-start.13 = (bf16[16,4224]{1,0:T(8,128)(2,1)S(1)}, bf16[16,4224]{1,0:T(8,128)(2,1)S(1)}, u32[]{:S(2)}, u32[]{:S(2)}) collective-permute-start(bf16[16,4224]{1,0:T(8,128)(2,1)S(1)} %get-tuple-element.18), channel_id=1, source_target_pairs={{0,32},{32,0},{64,96},{96,64},{1,33},{33,1},{65,97},{97,65},{2,34}... | collective-permute-start | bytes 405512 | tf_op jit(solution)/shard_map/ppermute | solution.py:218
  53.0 1.5 collective-permute-start.22
  54.6 5.1 %collective-permute-start.18 = (bf16[32,4224]{1,0:T(8,128)(2,1)S(1)}, bf16[32,4224]{1,0:T(8,128)(2,1)S(1)}, u32[]{:S(2)}, u32[]{:S(2)}) collective-permute-start(bf16[32,4224]{1,0:T(8,128)(2,1)S(1)} %pad_maximum_fusion.12), channel_id=1, source_target_pairs={{0,96},{32,64},{64,32},{96,0},{1,97},{33,65},{65,33},{97,1},{2,98}... | collective-permute-start | bytes 811016 | tf_op jit(solution)/shard_map/ppermute | solution.py:218
  59.7 17.7 %collective-permute-done.13 = bf16[16,4224]{1,0:T(8,128)(2,1)S(1)} collective-permute-done((bf16[16,4224]{1,0:T(8,128)(2,1)S(1)}, bf16[16,4224]{1,0:T(8,128)(2,1)S(1)}, u32[]{:S(2)}, u32[]{:S(2)}) %collective-permute-start.13) | collective-permute-done | bytes 135200 | tf_op jit(solution)/shard_map/ppermute | solution.py:218
  77.4 0.6 collective-permute-start.14
  78.0 2.3 %collective-permute-start.10 = (bf16[32,4224]{1,0:T(8,128)(2,1)S(1)}, bf16[32,4224]{1,0:T(8,128)(2,1)S(1)}, u32[]{:S(2)}, u32[]{:S(2)}) collective-permute-start(bf16[32,4224]{1,0:T(8,128)(2,1)S(1)} %pad_maximum_fusion.10), channel_id=1, source_target_pairs={{0,32},{32,0},{64,96},{96,64},{1,33},{33,1},{65,97},{97,65},{2,34}... | collective-permute-start | bytes 811016 | tf_op jit(solution)/shard_map/ppermute | solution.py:218
  80.7 5.6 %collective-permute-done.14 = bf16[32,4224]{1,0:T(8,128)(2,1)S(1)} collective-permute-done((bf16[32,4224]{1,0:T(8,128)(2,1)S(1)}, bf16[32,4224]{1,0:T(8,128)(2,1)S(1)}, u32[]{:S(2)}, u32[]{:S(2)}) %collective-permute-start.14) | collective-permute-done | bytes 270368 | tf_op jit(solution)/shard_map/ppermute | solution.py:218
  86.5 2.0 %collective-permute-start.4 = (bf16[32,4224]{1,0:T(8,128)(2,1)S(1)}, bf16[32,4224]{1,0:T(8,128)(2,1)S(1)}, u32[]{:S(2)}, u32[]{:S(2)}) collective-permute-start(bf16[32,4224]{1,0:T(8,128)(2,1)S(1)} %get-tuple-element.22), channel_id=1, source_target_pairs={{0,1},{1,0},{2,3},{3,2},{4,5},{5,4},{6,7},{7,6},{8,9},{9,8},{10,11... | collective-permute-start | bytes 811016 | tf_op jit(solution)/shard_map/ppermute | solution.py:218
  88.5 2.0 %collective-permute-start.11 = (bf16[64,4224]{1,0:T(8,128)(2,1)S(1)}, bf16[64,4224]{1,0:T(8,128)(2,1)S(1)}, u32[]{:S(2)}, u32[]{:S(2)}) collective-permute-start(bf16[64,4224]{1,0:T(8,128)(2,1)S(1)} %pad_maximum_fusion.6), channel_id=1, source_target_pairs={{0,24},{8,16},{16,8},{24,0},{1,25},{9,17},{17,9},{25,1},{2,26},{10... | collective-permute-start | bytes 1622024 | tf_op jit(solution)/shard_map/ppermute | solution.py:218
  90.6 3.4 %collective-permute-done.4 = bf16[32,4224]{1,0:T(8,128)(2,1)S(1)} collective-permute-done((bf16[32,4224]{1,0:T(8,128)(2,1)S(1)}, bf16[32,4224]{1,0:T(8,128)(2,1)S(1)}, u32[]{:S(2)}, u32[]{:S(2)}) %collective-permute-start.4) | collective-permute-done | bytes 270368 | tf_op jit(solution)/shard_map/ppermute | solution.py:218
  93.9 2.2 %collective-permute-start.6 = (bf16[32,4224]{1,0:T(8,128)(2,1)S(1)}, bf16[32,4224]{1,0:T(8,128)(2,1)S(1)}, u32[]{:S(2)}, u32[]{:S(2)}) collective-permute-start(bf16[32,4224]{1,0:T(8,128)(2,1)S(1)} %get-tuple-element.20), channel_id=1, source_target_pairs={{0,3},{1,2},{2,1},{3,0},{4,7},{5,6},{6,5},{7,4},{8,11},{9,10},{10,... | collective-permute-start | bytes 811016 | tf_op jit(solution)/shard_map/ppermute | solution.py:218
  96.2 5.0 %collective-permute-done.6 = bf16[32,4224]{1,0:T(8,128)(2,1)S(1)} collective-permute-done((bf16[32,4224]{1,0:T(8,128)(2,1)S(1)}, bf16[32,4224]{1,0:T(8,128)(2,1)S(1)}, u32[]{:S(2)}, u32[]{:S(2)}) %collective-permute-start.6) | collective-permute-done | bytes 270368 | tf_op jit(solution)/shard_map/ppermute | solution.py:218
  101.1 1.8 %collective-permute-start.5 = (bf16[64,4224]{1,0:T(8,128)(2,1)S(1)}, bf16[64,4224]{1,0:T(8,128)(2,1)S(1)}, u32[]{:S(2)}, u32[]{:S(2)}) collective-permute-start(bf16[64,4224]{1,0:T(8,128)(2,1)S(1)} %pad_maximum_fusion.4), channel_id=1, source_target_pairs={{0,3},{1,2},{2,1},{3,0},{4,7},{5,6},{6,5},{7,4},{8,11},{9,10},{10,... | collective-permute-start | bytes 1622024 | tf_op jit(solution)/shard_map/ppermute | solution.py:218
  103.3 1.6 collective-permute-start.12
  104.9 1.1 pad_maximum_fusion.1.refs_6_
  105.9 7.4 %collective-permute-done.5 = bf16[64,4224]{1,0:T(8,128)(2,1)S(1)} collective-permute-done((bf16[64,4224]{1,0:T(8,128)(2,1)S(1)}, bf16[64,4224]{1,0:T(8,128)(2,1)S(1)}, u32[]{:S(2)}, u32[]{:S(2)}) %collective-permute-start.5) | collective-permute-done | bytes 540704 | tf_op jit(solution)/shard_map/ppermute | solution.py:218
  113.5 4.4 %collective-permute-start.8 = (bf16[256,4224]{1,0:T(8,128)(2,1)S(1)}, bf16[256,4224]{1,0:T(8,128)(2,1)}, u32[]{:S(2)}, u32[]{:S(2)}) collective-permute-start(bf16[256,4224]{1,0:T(8,128)(2,1)S(1)} %constant_dynamic-update-slice_fusion.refs_2_), channel_id=1, source_target_pairs={{0,4},{4,0},{1,5},{5,1},{2,6},{6,2},{3,7},{7,3},{8,12},{12,8},{9,1... | collective-permute-start | bytes 6488072 | tf_op jit(solution)/shard_map/ppermute | solution.py:214
  118.0 1.1 pad_maximum_fusion.2.refs_8_
  119.1 1.6 collective-permute-start.20
  120.7 1.1 pad_maximum_fusion.3.refs_10_
  121.8 1.8 %collective-permute-start.24 = (bf16[128,4224]{1,0:T(8,128)(2,1)}, bf16[128,4224]{1,0:T(8,128)(2,1)}, u32[]{:S(2)}, u32[]{:S(2)}) collective-permute-start(bf16[128,4224]{1,0:T(8,128)(2,1)} %pad_maximum_fusion.3.refs_10_), channel_id=1, source_target_pairs={{0,24},{8,16},{16,8},{24,0},{1,25},{9,17},{17,9},{25,1},{2,26},{10... | collective-permute-start | bytes 3244040 | tf_op jit(solution)/shard_map/ppermute | solution.py:218
  123.6 0.6 stack.219.refs_0_
  124.2 0.7 stack.252.refs_1_
  124.9 1.4 collective-permute-done.12.refs_5_
  126.2 9.0 %collective-permute-done.16.refs_7_ = bf16[128,4224]{1,0:T(8,128)(2,1)} collective-permute-done((bf16[128,4224]{1,0:T(8,128)(2,1)}, bf16[128,4224]{1,0:T(8,128)(2,1)}, u32[]{:S(2)}, u32[]{:S(2)}) %collective-permute-start.16) | collective-permute-done | bytes 1081376 | tf_op jit(solution)/shard_map/ppermute | solution.py:218
  135.3 9.4 %collective-permute-done.20.refs_9_ = bf16[128,4224]{1,0:T(8,128)(2,1)} collective-permute-done((bf16[128,4224]{1,0:T(8,128)(2,1)}, bf16[128,4224]{1,0:T(8,128)(2,1)}, u32[]{:S(2)}, u32[]{:S(2)}) %collective-permute-start.20) | collective-permute-done | bytes 1081376 | tf_op jit(solution)/shard_map/ppermute | solution.py:218
  144.6 3.3 %collective-permute-done.24.refs_11_ = bf16[128,4224]{1,0:T(8,128)(2,1)} collective-permute-done((bf16[128,4224]{1,0:T(8,128)(2,1)}, bf16[128,4224]{1,0:T(8,128)(2,1)}, u32[]{:S(2)}, u32[]{:S(2)}) %collective-permute-start.24) | collective-permute-done | bytes 1081376 | tf_op jit(solution)/shard_map/ppermute | solution.py:218
  147.9 10.2 %gram.3 = (f32[264,512]{1,0:T(8,128)}, f32[264,512]{1,0:T(8,128)}) custom-call(s32[16]{0:T(128)} %stack.219.refs_0_, s32[32]{0:T(128)} %stack.252.refs_1_, bf16[256,4224]{1,0:T(8,128)(2,1)} %copy-done.1, bf16[256,4224]{1,0:T(8,128)(2,1)} %collective-permute-done.8.refs_3_, bf16[128,4224]{1,0:T(8,128)(2,1)} %copy-done.2, ...), custom_call_target="tpu_custom_call" | custom-call | flops 2147483648 | bytes 10485760 | tf_op jit(solution)/shard_map/gram/pallas_call | solution.py:157
  158.2 1.8 collective-permute-start.26
  159.9 10.3 %gram.2 = (f32[264,512]{1,0:T(8,128)}, f32[264,512]{1,0:T(8,128)}) custom-call(s32[16]{0:T(128)} %stack.219.refs_0_, s32[32]{0:T(128)} %stack.252.refs_1_, bf16[256,4224]{1,0:T(8,128)(2,1)} %copy-done.1, bf16[256,4224]{1,0:T(8,128)(2,1)} %collective-permute-done.8.refs_3_, bf16[128,4224]{1,0:T(8,128)(2,1)} %copy-done.2, ...), custom_call_target="tpu_custom_call" | custom-call | flops 2147483648 | bytes 10485760 | tf_op jit(solution)/shard_map/gram/pallas_call | solution.py:157
  170.3 0.7 pad_add_fusion.info_ref
  171.7 0.7 collective-permute-done.25.got0_ref
  172.5 0.7 copy-done.6
  173.2 3.2 %finish.1 = (f32[1,2048]{1,0:T(1,128)}, f32[256,2048]{1,0:T(8,128)}) custom-call(s32[4]{0:T(128)} %pad_add_fusion.info_ref, f32[1]{0:T(128)} %bitcast.5.total_ref, f32[264,512]{1,0:T(8,128)} %get-tuple-element.8.own0_ref, f32[264,512]{1,0:T(8,128)} %get-tuple-element.9.own1_ref, f32[264,512]{1,0:T(8,128)} %copy-done.6, f32[264,512]{1,0:T(8,128)} %copy-done.5), custom_call_target="tpu_custom_call" | custom-call | tf_op jit(solution)/shard_map/finish/pallas_call | solution.py:196
  (62 shorter events, 2.5 us)
Async XLA Ops:
  0.6 12.9 %copy-start = (f32[2048]{0:T(1024)S(1)}, f32[2048]{0:T(1024)}, u32[]{:S(2)}) copy-start(f32[2048]{0:T(1024)} %param.5) | copy-start | bytes 24580
  4.1 28.5 %all-to-all-start = ((bf16[32,80,256]{2,1,0:T(8,128)(2,1)}), bf16[32,80,256]{2,1,0:T(8,128)(2,1)S(1)}, u32[]{:S(2)}, u32[]{:S(2)}) async-start(bf16[32,80,256]{2,1,0:T(8,128)(2,1)} %pick.1), calls=%async_computation | async-start | bytes 2621440 | tf_op jit(solution)/shard_map/all_to_all | solution.py:227
  32.6 7.8 %copy-start.3 = (bf16[32,80,256]{2,1,0:T(8,128)(2,1)}, bf16[32,80,256]{2,1,0:T(8,128)(2,1)S(1)}, u32[]{:S(2)}) copy-start(bf16[32,80,256]{2,1,0:T(8,128)(2,1)S(1)} %all-to-all-done.in_ref) | copy-start | bytes 3932164
  32.7 5.8 %collective-permute-start.1 = (f32[32,256]{1,0:T(8,128)S(1)}, f32[32,256]{1,0:T(8,128)S(1)}, u32[]{:S(2)}, u32[]{:S(2)}) collective-permute-start(f32[32,256]{1,0:T(8,128)S(1)} %fusion), channel_id=1, source_target_pairs={{1,0},{2,1},{3,2},{0,3},{5,4},{6,5},{7,6},{4,7},{9,8},{10,9},{11,1... | collective-permute-start | bytes 98312 | tf_op jit(solution)/shard_map/ppermute | solution.py:210
  35.5 4.0 %collective-permute-start.2 = (f32[32,256]{1,0:T(8,128)S(1)}, f32[32,256]{1,0:T(8,128)S(1)}, u32[]{:S(2)}, u32[]{:S(2)}) collective-permute-start(f32[32,256]{1,0:T(8,128)S(1)} %fusion), channel_id=1, source_target_pairs={{3,0},{0,1},{1,2},{2,3},{7,4},{4,5},{5,6},{6,7},{11,8},{8,9},{9,10... | collective-permute-start | bytes 98312 | tf_op jit(solution)/shard_map/ppermute | solution.py:210
  35.5 4.3 %collective-permute-start = (f32[32,256]{1,0:T(8,128)S(1)}, f32[32,256]{1,0:T(8,128)S(1)}, u32[]{:S(2)}, u32[]{:S(2)}) collective-permute-start(f32[32,256]{1,0:T(8,128)S(1)} %fusion), channel_id=1, source_target_pairs={{2,0},{3,1},{0,2},{1,3},{6,4},{7,5},{4,6},{5,7},{10,8},{11,9},{8,1... | collective-permute-start | bytes 98312 | tf_op jit(solution)/shard_map/ppermute | solution.py:210
  44.7 2.9 %copy-start.4 = (bf16[64,4224]{1,0:T(8,128)(2,1)S(1)}, bf16[64,4224]{1,0:T(8,128)(2,1)}, u32[]{:S(2)}) copy-start(bf16[64,4224]{1,0:T(8,128)(2,1)} %pack.1) | copy-start | bytes 1622020
  45.9 7.1 %collective-permute-start.21 = (bf16[16,4224]{1,0:T(8,128)(2,1)S(1)}, bf16[16,4224]{1,0:T(8,128)(2,1)S(1)}, u32[]{:S(2)}, u32[]{:S(2)}) collective-permute-start(bf16[16,4224]{1,0:T(8,128)(2,1)S(1)} %get-tuple-element.16), channel_id=1, source_target_pairs={{0,96},{32,64},{64,32},{96,0},{1,97},{33,65},{65,33},{97,1},{2,98}... | collective-permute-start | bytes 405512 | tf_op jit(solution)/shard_map/ppermute | solution.py:218
  47.6 38.8 %collective-permute-start.3 = (bf16[64,4224]{1,0:T(8,128)(2,1)S(1)}, bf16[64,4224]{1,0:T(8,128)(2,1)S(1)}, u32[]{:S(2)}, u32[]{:S(2)}) collective-permute-start(bf16[64,4224]{1,0:T(8,128)(2,1)S(1)} %copy-done.4), channel_id=1, source_target_pairs={{0,0},{1,32},{2,64},{3,96},{32,1},{33,33},{34,65},{35,97},{64,2},{... | collective-permute-start | bytes 1622024 | tf_op jit(solution)/shard_map/ppermute | solution.py:239
  48.3 6.2 %collective-permute-start.17 = (bf16[16,4224]{1,0:T(8,128)(2,1)S(1)}, bf16[16,4224]{1,0:T(8,128)(2,1)S(1)}, u32[]{:S(2)}, u32[]{:S(2)}) collective-permute-start(bf16[16,4224]{1,0:T(8,128)(2,1)S(1)} %get-tuple-element.17), channel_id=1, source_target_pairs={{0,24},{8,16},{16,8},{24,0},{1,25},{9,17},{17,9},{25,1},{2,26},{10... | collective-permute-start | bytes 405512 | tf_op jit(solution)/shard_map/ppermute | solution.py:218
  50.7 26.7 %collective-permute-start.13 = (bf16[16,4224]{1,0:T(8,128)(2,1)S(1)}, bf16[16,4224]{1,0:T(8,128)(2,1)S(1)}, u32[]{:S(2)}, u32[]{:S(2)}) collective-permute-start(bf16[16,4224]{1,0:T(8,128)(2,1)S(1)} %get-tuple-element.18), channel_id=1, source_target_pairs={{0,32},{32,0},{64,96},{96,64},{1,33},{33,1},{65,97},{97,65},{2,34}... | collective-permute-start | bytes 405512 | tf_op jit(solution)/shard_map/ppermute | solution.py:218
  53.0 25.0 %collective-permute-start.9 = (bf16[16,4224]{1,0:T(8,128)(2,1)S(1)}, bf16[16,4224]{1,0:T(8,128)(2,1)S(1)}, u32[]{:S(2)}, u32[]{:S(2)}) collective-permute-start(bf16[16,4224]{1,0:T(8,128)(2,1)S(1)} %get-tuple-element.19), channel_id=1, source_target_pairs={{0,8},{8,0},{16,24},{24,16},{1,9},{9,1},{17,25},{25,17},{2,10},{10... | collective-permute-start | bytes 405512 | tf_op jit(solution)/shard_map/ppermute | solution.py:218
  53.0 27.3 %collective-permute-start.22 = (bf16[32,4224]{1,0:T(8,128)(2,1)S(1)}, bf16[32,4224]{1,0:T(8,128)(2,1)S(1)}, u32[]{:S(2)}, u32[]{:S(2)}) collective-permute-start(bf16[32,4224]{1,0:T(8,128)(2,1)S(1)} %pad_maximum_fusion.13), channel_id=1, source_target_pairs={{0,8},{8,0},{16,24},{24,16},{1,9},{9,1},{17,25},{25,17},{2,10},{10... | collective-permute-start | bytes 811016 | tf_op jit(solution)/shard_map/ppermute | solution.py:218
  54.6 25.9 %collective-permute-start.18 = (bf16[32,4224]{1,0:T(8,128)(2,1)S(1)}, bf16[32,4224]{1,0:T(8,128)(2,1)S(1)}, u32[]{:S(2)}, u32[]{:S(2)}) collective-permute-start(bf16[32,4224]{1,0:T(8,128)(2,1)S(1)} %pad_maximum_fusion.12), channel_id=1, source_target_pairs={{0,96},{32,64},{64,32},{96,0},{1,97},{33,65},{65,33},{97,1},{2,98}... | collective-permute-start | bytes 811016 | tf_op jit(solution)/shard_map/ppermute | solution.py:218
  77.4 8.8 %collective-permute-start.14 = (bf16[32,4224]{1,0:T(8,128)(2,1)S(1)}, bf16[32,4224]{1,0:T(8,128)(2,1)S(1)}, u32[]{:S(2)}, u32[]{:S(2)}) collective-permute-start(bf16[32,4224]{1,0:T(8,128)(2,1)S(1)} %pad_maximum_fusion.11), channel_id=1, source_target_pairs={{0,24},{8,16},{16,8},{24,0},{1,25},{9,17},{17,9},{25,1},{2,26},{10... | collective-permute-start | bytes 811016 | tf_op jit(solution)/shard_map/ppermute | solution.py:218
  78.0 10.5 %collective-permute-start.10 = (bf16[32,4224]{1,0:T(8,128)(2,1)S(1)}, bf16[32,4224]{1,0:T(8,128)(2,1)S(1)}, u32[]{:S(2)}, u32[]{:S(2)}) collective-permute-start(bf16[32,4224]{1,0:T(8,128)(2,1)S(1)} %pad_maximum_fusion.10), channel_id=1, source_target_pairs={{0,32},{32,0},{64,96},{96,64},{1,33},{33,1},{65,97},{97,65},{2,34}... | collective-permute-start | bytes 811016 | tf_op jit(solution)/shard_map/ppermute | solution.py:218
  80.3 40.4 %collective-permute-start.23 = (bf16[64,4224]{1,0:T(8,128)(2,1)S(1)}, bf16[64,4224]{1,0:T(8,128)(2,1)S(1)}, u32[]{:S(2)}, u32[]{:S(2)}) collective-permute-start(bf16[64,4224]{1,0:T(8,128)(2,1)S(1)} %pad_maximum_fusion.9), channel_id=1, source_target_pairs={{0,32},{32,0},{64,96},{96,64},{1,33},{33,1},{65,97},{97,65},{2,34}... | collective-permute-start | bytes 1622024 | tf_op jit(solution)/shard_map/ppermute | solution.py:218
  80.5 37.5 %collective-permute-start.19 = (bf16[64,4224]{1,0:T(8,128)(2,1)S(1)}, bf16[64,4224]{1,0:T(8,128)(2,1)S(1)}, u32[]{:S(2)}, u32[]{:S(2)}) collective-permute-start(bf16[64,4224]{1,0:T(8,128)(2,1)S(1)} %pad_maximum_fusion.8), channel_id=1, source_target_pairs={{0,8},{8,0},{16,24},{24,16},{1,9},{9,1},{17,25},{25,17},{2,10},{10... | collective-permute-start | bytes 1622024 | tf_op jit(solution)/shard_map/ppermute | solution.py:218
  86.3 17.0 %collective-permute-start.15 = (bf16[64,4224]{1,0:T(8,128)(2,1)S(1)}, bf16[64,4224]{1,0:T(8,128)(2,1)S(1)}, u32[]{:S(2)}, u32[]{:S(2)}) collective-permute-start(bf16[64,4224]{1,0:T(8,128)(2,1)S(1)} %pad_maximum_fusion.7), channel_id=1, source_target_pairs={{0,96},{32,64},{64,32},{96,0},{1,97},{33,65},{65,33},{97,1},{2,98}... | collective-permute-start | bytes 1622024 | tf_op jit(solution)/shard_map/ppermute | solution.py:218
  86.5 7.5 %collective-permute-start.4 = (bf16[32,4224]{1,0:T(8,128)(2,1)S(1)}, bf16[32,4224]{1,0:T(8,128)(2,1)S(1)}, u32[]{:S(2)}, u32[]{:S(2)}) collective-permute-start(bf16[32,4224]{1,0:T(8,128)(2,1)S(1)} %get-tuple-element.22), channel_id=1, source_target_pairs={{0,1},{1,0},{2,3},{3,2},{4,5},{5,4},{6,7},{7,6},{8,9},{9,8},{10,11... | collective-permute-start | bytes 811016 | tf_op jit(solution)/shard_map/ppermute | solution.py:218
  88.5 14.5 %collective-permute-start.11 = (bf16[64,4224]{1,0:T(8,128)(2,1)S(1)}, bf16[64,4224]{1,0:T(8,128)(2,1)S(1)}, u32[]{:S(2)}, u32[]{:S(2)}) collective-permute-start(bf16[64,4224]{1,0:T(8,128)(2,1)S(1)} %pad_maximum_fusion.6), channel_id=1, source_target_pairs={{0,24},{8,16},{16,8},{24,0},{1,25},{9,17},{17,9},{25,1},{2,26},{10... | collective-permute-start | bytes 1622024 | tf_op jit(solution)/shard_map/ppermute | solution.py:218
  93.9 7.2 %collective-permute-start.6 = (bf16[32,4224]{1,0:T(8,128)(2,1)S(1)}, bf16[32,4224]{1,0:T(8,128)(2,1)S(1)}, u32[]{:S(2)}, u32[]{:S(2)}) collective-permute-start(bf16[32,4224]{1,0:T(8,128)(2,1)S(1)} %get-tuple-element.20), channel_id=1, source_target_pairs={{0,3},{1,2},{2,1},{3,0},{4,7},{5,6},{6,5},{7,4},{8,11},{9,10},{10,... | collective-permute-start | bytes 811016 | tf_op jit(solution)/shard_map/ppermute | solution.py:218
  101.1 12.2 %collective-permute-start.5 = (bf16[64,4224]{1,0:T(8,128)(2,1)S(1)}, bf16[64,4224]{1,0:T(8,128)(2,1)S(1)}, u32[]{:S(2)}, u32[]{:S(2)}) collective-permute-start(bf16[64,4224]{1,0:T(8,128)(2,1)S(1)} %pad_maximum_fusion.4), channel_id=1, source_target_pairs={{0,3},{1,2},{2,1},{3,0},{4,7},{5,6},{6,5},{7,4},{8,11},{9,10},{10,... | collective-permute-start | bytes 1622024 | tf_op jit(solution)/shard_map/ppermute | solution.py:218
  103.1 10.4 %collective-permute-start.7 = (bf16[64,4224]{1,0:T(8,128)(2,1)S(1)}, bf16[64,4224]{1,0:T(8,128)(2,1)S(1)}, u32[]{:S(2)}, u32[]{:S(2)}) collective-permute-start(bf16[64,4224]{1,0:T(8,128)(2,1)S(1)} %pad_maximum_fusion.5), channel_id=1, source_target_pairs={{0,1},{1,0},{2,3},{3,2},{4,5},{5,4},{6,7},{7,6},{8,9},{9,8},{10,11... | collective-permute-start | bytes 1622024 | tf_op jit(solution)/shard_map/ppermute | solution.py:218
  103.3 2.7 %copy-start.2 = (bf16[128,4224]{1,0:T(8,128)(2,1)}, bf16[128,4224]{1,0:T(8,128)(2,1)S(1)}, u32[]{:S(2)}) copy-start(bf16[128,4224]{1,0:T(8,128)(2,1)S(1)} %pad_maximum_fusion.refs_4_) | copy-start | bytes 3244036
  103.3 23.0 %collective-permute-start.12 = (bf16[128,4224]{1,0:T(8,128)(2,1)S(1)}, bf16[128,4224]{1,0:T(8,128)(2,1)}, u32[]{:S(2)}, u32[]{:S(2)}) collective-permute-start(bf16[128,4224]{1,0:T(8,128)(2,1)S(1)} %pad_maximum_fusion.refs_4_), channel_id=1, source_target_pairs={{0,96},{32,64},{64,32},{96,0},{1,97},{33,65},{65,33},{97,1},{2,98}... | collective-permute-start | bytes 3244040 | tf_op jit(solution)/shard_map/ppermute | solution.py:218
  113.3 22.0 %collective-permute-start.16 = (bf16[128,4224]{1,0:T(8,128)(2,1)}, bf16[128,4224]{1,0:T(8,128)(2,1)}, u32[]{:S(2)}, u32[]{:S(2)}) collective-permute-start(bf16[128,4224]{1,0:T(8,128)(2,1)} %pad_maximum_fusion.1.refs_6_), channel_id=1, source_target_pairs={{0,8},{8,0},{16,24},{24,16},{1,9},{9,1},{17,25},{25,17},{2,10},{10... | collective-permute-start | bytes 3244040 | tf_op jit(solution)/shard_map/ppermute | solution.py:218
  113.5 5.6 %copy-start.1 = (bf16[256,4224]{1,0:T(8,128)(2,1)}, bf16[256,4224]{1,0:T(8,128)(2,1)S(1)}, u32[]{:S(2)}) copy-start(bf16[256,4224]{1,0:T(8,128)(2,1)S(1)} %constant_dynamic-update-slice_fusion.refs_2_) | copy-start | bytes 6488068
  113.5 34.4 %collective-permute-start.8 = (bf16[256,4224]{1,0:T(8,128)(2,1)S(1)}, bf16[256,4224]{1,0:T(8,128)(2,1)}, u32[]{:S(2)}, u32[]{:S(2)}) collective-permute-start(bf16[256,4224]{1,0:T(8,128)(2,1)S(1)} %constant_dynamic-update-slice_fusion.refs_2_), channel_id=1, source_target_pairs={{0,4},{4,0},{1,5},{5,1},{2,6},{6,2},{3,7},{7,3},{8,12},{12,8},{9,1... | collective-permute-start | bytes 6488072 | tf_op jit(solution)/shard_map/ppermute | solution.py:214
  119.1 25.5 %collective-permute-start.20 = (bf16[128,4224]{1,0:T(8,128)(2,1)}, bf16[128,4224]{1,0:T(8,128)(2,1)}, u32[]{:S(2)}, u32[]{:S(2)}) collective-permute-start(bf16[128,4224]{1,0:T(8,128)(2,1)} %pad_maximum_fusion.2.refs_8_), channel_id=1, source_target_pairs={{0,32},{32,0},{64,96},{96,64},{1,33},{33,1},{65,97},{97,65},{2,34}... | collective-permute-start | bytes 3244040 | tf_op jit(solution)/shard_map/ppermute | solution.py:218
  121.8 26.1 %collective-permute-start.24 = (bf16[128,4224]{1,0:T(8,128)(2,1)}, bf16[128,4224]{1,0:T(8,128)(2,1)}, u32[]{:S(2)}, u32[]{:S(2)}) collective-permute-start(bf16[128,4224]{1,0:T(8,128)(2,1)} %pad_maximum_fusion.3.refs_10_), channel_id=1, source_target_pairs={{0,24},{8,16},{16,8},{24,0},{1,25},{9,17},{17,9},{25,1},{2,26},{10... | collective-permute-start | bytes 3244040 | tf_op jit(solution)/shard_map/ppermute | solution.py:218
  158.2 13.5 %collective-permute-start.26 = (f32[264,512]{1,0:T(8,128)}, f32[264,512]{1,0:T(8,128)S(1)}, u32[]{:S(2)}, u32[]{:S(2)}) collective-permute-start(f32[264,512]{1,0:T(8,128)} %get-tuple-element.11), channel_id=1, source_target_pairs={{0,4},{4,0},{1,5},{5,1},{2,6},{6,2},{3,7},{7,3},{8,12},{12,8},{9,1... | collective-permute-start | bytes 1622024 | tf_op jit(solution)/shard_map/ppermute | solution.py:214
  170.2 2.2 %collective-permute-start.25 = (f32[264,512]{1,0:T(8,128)}, f32[264,512]{1,0:T(8,128)S(1)}, u32[]{:S(2)}, u32[]{:S(2)}) collective-permute-start(f32[264,512]{1,0:T(8,128)} %get-tuple-element.10), channel_id=1, source_target_pairs={{0,4},{4,0},{1,5},{5,1},{2,6},{6,2},{3,7},{7,3},{8,12},{12,8},{9,1... | collective-permute-start | bytes 1622024 | tf_op jit(solution)/shard_map/ppermute | solution.py:214
  171.7 0.8 copy-start.5
  172.4 0.8 copy-start.6

commit v4 on v3

--- a/solution.py
+++ b/solution.py
@@ -30,7 +30,7 @@
     return jnp.where(place == 0, high, jnp.where(place == 1, middle, rest))
 
 
-def pick_kernel(index_ref, counts_ref, resid_ref, out_ref):
+def pick_kernel(index_ref, counts_ref, resid_ref, picked_ref, sums_ref):
     tokens = resid_ref.shape[0]
     token = lax.broadcasted_iota(jnp.int32, (tokens, SLOTS), 0)
     slot = lax.broadcasted_iota(jnp.int32, (1, SLOTS), 1)
@@ -40,51 +40,106 @@
     one_hot = jnp.where(token == kept, 1.0, 0.0).astype(bf16)
     total = jnp.zeros((1, SLOTS), f32)
     step = 512
-    for x in range(4):
+    for k in range(WIDTH // step):
         part = lax.dot_general(
-            resid_ref[:, x * step : (x + 1) * step],
+            resid_ref[:, k * step : (k + 1) * step],
             one_hot,
             (((0,), (0,)), ((), ())),
             preferred_element_type=f32,
         )
         total += jnp.sum(part * part, axis=0, keepdims=True)
-        short = part.astype(bf16)
-        for c in range(2):
-            for z in range(4):
-                first = (c * 4 + z) * PIECE
-                out_ref[z * 8 + x * 2 + c, :PIECE, :] = short[first : first + PIECE, :]
-    live = (counts_ref[0] + counts_ref[1]).astype(f32)
-    row = lax.broadcasted_iota(jnp.int32, (EXTRA, SLOTS), 0)
-    extra = jnp.where(row == 3, live, spread(total, row)).astype(bf16)
-    for t in range(32):
-        out_ref[t, PIECE:, :] = extra
+        picked_ref[k * step : (k + 1) * step, :] = part.astype(bf16)
+    sums_ref[...] = jnp.broadcast_to(total, sums_ref.shape)
 
 
 def pick(resid, keep_index, counts):
     return pl.pallas_call(
         pick_kernel,
-        out_shape=jax.ShapeDtypeStruct((32, PIECE + EXTRA, SLOTS), bf16),
+        out_shape=(
+            jax.ShapeDtypeStruct((WIDTH, SLOTS), bf16),
+            jax.ShapeDtypeStruct((8, SLOTS), f32),
+        ),
         in_specs=[
             pl.BlockSpec(memory_space=pltpu.VMEM),
             pl.BlockSpec(memory_space=pltpu.SMEM),
             pl.BlockSpec(memory_space=pltpu.VMEM),
         ],
-        out_specs=pl.BlockSpec(memory_space=pltpu.VMEM),
+        out_specs=(pl.BlockSpec(memory_space=pltpu.VMEM),) * 2,
         compiler_params=params(),
         name="pick",
     )(keep_index[None, :], counts, resid)
 
 
-def pack_kernel(first_ref, in_ref, scale_ref, gain_ref, out_ref, acc_ref):
+def norm_kernel(place_ref, counts_ref, picked_ref, gain_ref, s0, s1, s2, s3, out_ref, *turn_refs):
+    squares = (s0[:1, :] + s2[:1, :]) + (s1[:1, :] + s3[:1, :])
+    scale = lax.rsqrt(squares / 8192 + epsilon)
+    y = place_ref[0]
+    live = (counts_ref[0] + counts_ref[1]).astype(f32)
+    extra = jnp.full((EXTRA, SLOTS), live, f32).astype(bf16)
+
+    for x in range(4):
+        for c in range(2):
+            first = (x * 2 + c) * 4 * PIECE
+            rows = picked_ref[first : first + 4 * PIECE, :].astype(f32)
+            short = (rows * scale * gain_ref[first : first + 4 * PIECE, :]).astype(bf16)
+            for q in range(4):
+                piece = short[q * PIECE : (q + 1) * PIECE, :]
+                out_ref[q * 8 + x * 2 + c, :PIECE, :] = piece
+                out_ref[q * 8 + x * 2 + c, PIECE:, :] = extra
+            for k, ref in enumerate(turn_refs):
+                ref[x * 2 + c] = out_ref[(y ^ (k + 1)) * 8 + x * 2 + c, :PIECE, :]
+
+
+def norm(place, counts, picked, gain, sums):
+    return pl.pallas_call(
+        norm_kernel,
+        out_shape=(jax.ShapeDtypeStruct((32, PIECE + EXTRA, SLOTS), bf16),)
+        + (jax.ShapeDtypeStruct((8, PIECE, SLOTS), bf16),) * 3,
+        in_specs=[pl.BlockSpec(memory_space=pltpu.SMEM)] * 2 + [pl.BlockSpec(memory_space=pltpu.VMEM)] * 6,
+        out_specs=(pl.BlockSpec(memory_space=pltpu.VMEM),) * 4,
+        compiler_params=params(),
+        name="norm",
+    )(place, counts, picked, gain, *sums)
+
+
+def order_kernel(place_ref, own_ref, a_ref, b_ref, c_ref, out_ref, sem):
+    y = place_ref[0]
+    copies = [
+        pltpu.make_async_copy(
+            own_ref.at[pl.ds(y * 8, 8), pl.ds(0, PIECE)], out_ref.at[pl.ds(y * 8, 8)], sem.at[0]
+        )
+    ]
+    for k, ref in enumerate((a_ref, b_ref, c_ref)):
+        copies.append(
+            pltpu.make_async_copy(ref, out_ref.at[pl.ds((y ^ (k + 1)) * 8, 8)], sem.at[k + 1])
+        )
+    for copy in copies:
+        copy.start()
+    for copy in copies:
+        copy.wait()
+
+
+def order(place, own, others):
+    return pl.pallas_call(
+        order_kernel,
+        out_shape=jax.ShapeDtypeStruct((32, PIECE, SLOTS), bf16),
+        in_specs=[pl.BlockSpec(memory_space=pltpu.SMEM)] + [pl.BlockSpec(memory_space=pl.ANY)] * 4,
+        out_specs=pl.BlockSpec(memory_space=pl.ANY),
+        scratch_shapes=[pltpu.SemaphoreType.DMA((4,))],
+        compiler_params=params(),
+        name="order",
+    )(place, own, *others)
+
+
+def pack_kernel(first_ref, in_ref, out_ref, acc_ref):
     acc_ref[...] = jnp.zeros_like(acc_ref)
-    gain = gain_ref[...]
     group = 4
 
     def body(g, _):
         moved = []
         for k in range(group):
             t = g * group + k
-            rows = in_ref[t, :PIECE, :].astype(f32) * scale_ref[pl.ds(t, 1), :] * gain
+            rows = in_ref[t, :PIECE, :].astype(f32)
             first = first_ref[t]
             base = pl.multiple_of((first // 128) * 128, 128)
             wide = jnp.concatenate([rows, jnp.zeros((PIECE, 128), f32)], axis=1)
@@ -101,16 +156,16 @@
     out_ref[:, LIVE:] = spread(total, lane).astype(bf16)
 
 
-def pack(first, pieces, scale, gain):
+def pack(first, pieces):
     return pl.pallas_call(
         pack_kernel,
         out_shape=jax.ShapeDtypeStruct((PIECE, LONG), bf16),
-        in_specs=[pl.BlockSpec(memory_space=pltpu.SMEM)] + [pl.BlockSpec(memory_space=pltpu.VMEM)] * 3,
+        in_specs=[pl.BlockSpec(memory_space=pltpu.SMEM)] + [pl.BlockSpec(memory_space=pltpu.VMEM)],
         out_specs=pl.BlockSpec(memory_space=pltpu.VMEM),
         scratch_shapes=[pltpu.VMEM((PIECE, LIVE + SLOTS + 128), f32)],
         compiler_params=params(),
         name="pack",
-    )(first, pieces, scale, gain)
+    )(first, pieces)
 
 
 def gram_kernel(row_place, col_place, row_where, col_where, *refs):
@@ -206,10 +261,6 @@
     )(info, total, *own, *got)
 
 
-def shift(value, axis, by):
-    return lax.ppermute(value, axis, [((i + by) % 4, i) for i in range(4)])
-
-
 def swap(value):
     return lax.ppermute(value, "c", [(0, 1), (1, 0)])
 
@@ -224,19 +275,19 @@
 
 def per_device(resid, norm_gain, keep_index, counts):
     z, x, c, y = (lax.axis_index(a) for a in ("z", "x", "c", "y"))
-    pieces = lax.all_to_all(pick(resid, keep_index, counts), TOK, 0, 0, tiled=True)
-
-    extra = pieces[:, PIECE : PIECE + 4, :].astype(f32)
-    loads = extra[:, 3, 0].astype(jnp.int32)
+    place_y = y[None].astype(jnp.int32)
+    picked, sums = pick(resid, keep_index, counts)
+    all_sums = [sums] + [trade(sums, "y", flip) for flip in (1, 2, 3)]
+    normed, *turns = norm(place_y, counts, picked, norm_gain[:, None], all_sums)
+    pieces = lax.all_to_all(normed, TOK, 0, 0, tiled=True)
+    panel = order(place_y, normed, [trade(turns[k], "y", k + 1) for k in range(3)])
+    panel = lax.all_to_all(panel, TOK, 0, 0, tiled=True)
+
+    loads = pieces[:, PIECE, 0].astype(jnp.int32)
     first = jnp.cumsum(loads) - loads
     kept_total = jnp.sum(loads).astype(f32)
-    sums = extra[:, 0, :] + extra[:, 1, :] + extra[:, 2, :]
-    squares = (sums + shift(sums, "y", 2)) + (shift(sums, "y", 1) + shift(sums, "y", 3))
-    scale = lax.rsqrt(squares / 8192 + epsilon)
-    gain = lax.dynamic_slice_in_dim(norm_gain, ((x * 2 + c) * 4 + z) * PIECE, PIECE)[:, None]
-    mine = pack(first, pieces, scale, gain)
-
-    turned = lax.ppermute(mine, ("z", "y"), [(i * 4 + j, j * 4 + i) for i in range(4) for j in range(4)])
+    mine = pack(first, pieces)
+    turned = pack(first, panel)
 
     partners = (("x", 1), ("z", 1), ("x", 3), ("z", 3))
     streams = [mine[s * 16 : (s + 1) * 16] for s in range(4)]

time: 177 us -> 209 us (1.18)
  Pallas kernels: 31.4 us -> 70.4 us
  waiting for transfers between devices: 82.4 us -> 55.7 us
  other arithmetic: 6.42 us -> 17.6 us
  local copies, waits for them, and re-layouts: 4.36 us -> 8.84 us
  starting transfers between devices: 50.2 us -> 54.3 us
    pallas_call x1 -> x3, Pallas kernels: 3.47 us -> 39.5 us  [the longest x1 32.9 us: order(): pl.pallas_call(order_kernel, out_shape=jax.ShapeDtypeStruct((32, PIECE, S...]
    all_to_all x1 -> x2, waiting for transfers between devices: 18.3 us -> 4.81 us  [the longest x1 4.81 us: per_device(): panel = lax.all_to_all(panel, TOK, 0, 0, tiled=True)]
    ppermute x20 -> x26, waiting for transfers between devices: 62.1 us -> 50.1 us  [trade(): return lax.ppermute(value, axis, [(i, i ^ flip) for i in range(4)])]
    concatenate x14, other arithmetic: 3.73 us -> 15 us  [join(): return jnp.concatenate(values, axis=0)]
    all_to_all x1 -> x2, starting transfers between devices: 9.43 us -> 18.9 us  [the longest x1 10.2 us: per_device(): pieces = lax.all_to_all(normed, TOK, 0, 0, tiled=True)]
    ppermute x4 -> x0, starting transfers between devices: 5.13 us -> none  [the longest x3 4.45 us: shift(): return lax.ppermute(value, axis, [((i + by) % 4, i) for i in range(4)])]
    pallas_call x1 -> x2, Pallas kernels: 4.22 us -> 7.2 us  [pack(): pl.pallas_call(pack_kernel, out_shape=jax.ShapeDtypeStruct((PIECE, LONG),...]
    unnamed x18 -> x38, local copies, waits for them, and re-layouts: 0.98 us -> 3.28 us
  transfers between devices with their start and end apart: 28 -> 31, of which waited for: 13 -> 15; matrix products, arithmetic and copies ran while one was open for 5% -> 11% of each run, Pallas kernels for 6% -> 24%
where the time goes in v4:
time: 209 us; the launch traced here: 208 us
  Pallas kernels  70.4 us (34%)
  waiting for transfers between devices  55.7 us (27%)
  starting transfers between devices  54.3 us (26%)
  other arithmetic  17.6 us (8%)
  local copies, waits for them, and re-layouts  8.84 us (4%)
    ppermute x26, waiting for transfers between devices, trade(): return lax.ppermute(value, axis, [(i, i ^ flip) for i in range(4)])  50.1 us
    pallas_call x1, Pallas kernels, order(): pl.pallas_call(order_kernel, out_shape=jax.ShapeDtypeStruct((32, PIECE, S...  32.9 us
    ppermute x26, starting transfers between devices, trade(): return lax.ppermute(value, axis, [(i, i ^ flip) for i in range(4)])  29.3 us
    pallas_call x2, Pallas kernels, gram(): pl.pallas_call(lambda *refs: gram_kernel(row_place, col_place, *refs), ou...  20.4 us
    concatenate x14, other arithmetic, join(): return jnp.concatenate(values, axis=0)  15 us
    all_to_all x1, starting transfers between devices, per_device(): pieces = lax.all_to_all(normed, TOK, 0, 0, tiled=True)  10.2 us
    all_to_all x1, starting transfers between devices, per_device(): panel = lax.all_to_all(panel, TOK, 0, 0, tiled=True)  8.72 us
    pallas_call x2, Pallas kernels, pack(): pl.pallas_call(pack_kernel, out_shape=jax.ShapeDtypeStruct((PIECE, LONG),...  7.2 us
  transfers between devices with their start and end apart: 31, of which 15 were waited for; matrix products, arithmetic and copies ran while one was open for 11% of the time, Pallas kernels for 24%

profile of v4, /device:TPU:1, one launch (start us, length us, event | category | flops | bytes accessed | tf_op | source)
XLA Modules:
  0.0 208.5 jit_solution(9182155393309736511)
XLA Ops:
  0.6 3.4 %pick.1 = (bf16[2048,256]{1,0:T(8,128)(2,1)}, f32[8,256]{1,0:T(8,128)}) custom-call(s32[1,256]{1,0:T(1,128)} %bitcast.60, s32[2]{0:T(128)} %counts_ref.3, bf16[512,2048]{1,0:T(8,128)(2,1)} %resid_ref.1), custom_call_target="tpu_custom_call" | custom-call | tf_op jit(solution)/shard_map/pick/pallas_call | solution.py:56
  4.0 3.6 %collective-permute-start.2 = (f32[8,256]{1,0:T(8,128)}, f32[8,256]{1,0:T(8,128)S(1)}, u32[]{:S(2)}, u32[]{:S(2)}) collective-permute-start(f32[8,256]{1,0:T(8,128)} %get-tuple-element.15.s0), channel_id=1, source_target_pairs={{0,3},{1,2},{2,1},{3,0},{4,7},{5,6},{6,5},{7,4},{8,11},{9,10},{10,... | collective-permute-start | bytes 24584 | tf_op jit(solution)/shard_map/ppermute | solution.py:269
  8.2 1.4 copy.7.gain_ref
  9.5 2.3 %collective-permute-done.1.s2 = f32[8,256]{1,0:T(8,128)S(1)} collective-permute-done((f32[8,256]{1,0:T(8,128)}, f32[8,256]{1,0:T(8,128)S(1)}, u32[]{:S(2)}, u32[]{:S(2)}) %collective-permute-start.1) | collective-permute-done | bytes 8224 | tf_op jit(solution)/shard_map/ppermute | solution.py:269
  12.4 3.2 %norm.1 = (bf16[32,80,256]{2,1,0:T(8,128)(2,1)}, bf16[8,64,256]{2,1,0:T(8,128)(2,1)}, bf16[8,64,256]{2,1,0:T(8,128)(2,1)}, bf16[8,64,256]{2,1,0:T(8,128)(2,1)}) custom-call(s32[1]{0:T(128)} %bitcast.4.place_ref, s32[2]{0:T(128)} %counts_ref.3, bf16[2048,256]{1,0:T(8,128)(2,1)} %get-tuple-element.14.picked_ref, f32[2048,1]{1,0:T(8,128)} %copy.7.gain_ref, ...), custom_call_target="tpu_custom_call" | custom-call | tf_op jit(solution)/shard_map/norm/pallas_call | solution.py:94
  15.7 10.2 %all-to-all-start = ((bf16[32,80,256]{2,1,0:T(8,128)(2,1)}), bf16[32,80,256]{2,1,0:T(8,128)(2,1)S(1)}, u32[]{:S(2)}, u32[]{:S(2)}) async-start(bf16[32,80,256]{2,1,0:T(8,128)(2,1)} %get-tuple-element.16.own_ref), calls=%async_computation | async-start | bytes 2621440 | tf_op jit(solution)/shard_map/all_to_all | solution.py:282
  25.9 2.2 %collective-permute-start.4 = (bf16[8,64,256]{2,1,0:T(8,128)(2,1)S(1)}, bf16[8,64,256]{2,1,0:T(8,128)(2,1)S(1)}, u32[]{:S(2)}, u32[]{:S(2)}) collective-permute-start(bf16[8,64,256]{2,1,0:T(8,128)(2,1)S(1)} %copy-done.15), channel_id=1, source_target_pairs={{0,2},{1,3},{2,0},{3,1},{4,6},{5,7},{6,4},{7,5},{8,10},{9,11},{10,... | collective-permute-start | bytes 786440 | tf_op jit(solution)/shard_map/ppermute | solution.py:269
  28.1 1.7 collective-permute-start.5
  29.8 3.8 %collective-permute-done.3.a_ref = bf16[8,64,256]{2,1,0:T(8,128)(2,1)S(1)} collective-permute-done((bf16[8,64,256]{2,1,0:T(8,128)(2,1)S(1)}, bf16[8,64,256]{2,1,0:T(8,128)(2,1)S(1)}, u32[]{:S(2)}, u32[]{:S(2)}) %collective-permute-start.3) | collective-permute-done | bytes 262176 | tf_op jit(solution)/shard_map/ppermute | solution.py:269
  33.6 6.4 %collective-permute-done.4.b_ref = bf16[8,64,256]{2,1,0:T(8,128)(2,1)S(1)} collective-permute-done((bf16[8,64,256]{2,1,0:T(8,128)(2,1)S(1)}, bf16[8,64,256]{2,1,0:T(8,128)(2,1)S(1)}, u32[]{:S(2)}, u32[]{:S(2)}) %collective-permute-start.4) | collective-permute-done | bytes 262176 | tf_op jit(solution)/shard_map/ppermute | solution.py:269
  40.0 2.0 collective-permute-done.5.c_ref
  42.7 32.9 %order.1 = bf16[32,64,256]{2,1,0:T(8,128)(2,1)} custom-call(s32[1]{0:T(128)} %bitcast.4.place_ref, bf16[32,80,256]{2,1,0:T(8,128)(2,1)} %get-tuple-element.16.own_ref, bf16[8,64,256]{2,1,0:T(8,128)(2,1)} %copy-done.7, bf16[8,64,256]{2,1,0:T(8,128)(2,1)} %copy-done.8, bf16[8,64,256]{2,1,0:T(8,128)(2,1)} %copy-done.9), custom_call_target="tpu_custom_call" | custom-call | tf_op jit(solution)/shard_map/order/pallas_call | solution.py:123
  75.6 8.7 %all-to-all-start.1 = ((bf16[32,64,256]{2,1,0:T(8,128)(2,1)}), bf16[32,64,256]{2,1,0:T(8,128)(2,1)S(1)}, u32[]{:S(2)}, u32[]{:S(2)}) async-start(bf16[32,64,256]{2,1,0:T(8,128)(2,1)} %order.1), calls=%async_computation.1 | async-start | bytes 2097152 | tf_op jit(solution)/shard_map/all_to_all | solution.py:284
  84.6 1.3 fusion
  86.4 3.7 %pack.3 = bf16[64,4224]{1,0:T(8,128)(2,1)} custom-call(s32[32]{0:T(128)} %sub.3.first_ref, bf16[32,80,256]{2,1,0:T(8,128)(2,1)} %copy-done.2), custom_call_target="tpu_custom_call" | custom-call | tf_op jit(solution)/shard_map/pack/pallas_call | solution.py:160
  90.0 1.8 fusion.2
  91.9 2.6 %collective-permute-start.23 = (bf16[16,4224]{1,0:T(8,128)(2,1)S(1)}, bf16[16,4224]{1,0:T(8,128)(2,1)}, u32[]{:S(2)}, u32[]{:S(2)}) collective-permute-start(bf16[16,4224]{1,0:T(8,128)(2,1)S(1)} %get-tuple-element.28), channel_id=1, source_target_pairs={{0,96},{32,64},{64,32},{96,0},{1,97},{33,65},{65,33},{97,1},{2,98}... | collective-permute-start | bytes 405512 | tf_op jit(solution)/shard_map/ppermute | solution.py:269
  94.5 2.4 %collective-permute-start.19 = (bf16[16,4224]{1,0:T(8,128)(2,1)S(1)}, bf16[16,4224]{1,0:T(8,128)(2,1)}, u32[]{:S(2)}, u32[]{:S(2)}) collective-permute-start(bf16[16,4224]{1,0:T(8,128)(2,1)S(1)} %get-tuple-element.29), channel_id=1, source_target_pairs={{0,24},{8,16},{16,8},{24,0},{1,25},{9,17},{17,9},{25,1},{2,26},{10... | collective-permute-start | bytes 405512 | tf_op jit(solution)/shard_map/ppermute | solution.py:269
  96.9 4.8 %all-to-all-done.1.in_ref = bf16[32,64,256]{2,1,0:T(8,128)(2,1)S(1)} async-done(((bf16[32,64,256]{2,1,0:T(8,128)(2,1)}), bf16[32,64,256]{2,1,0:T(8,128)(2,1)S(1)}, u32[]{:S(2)}, u32[]{:S(2)}) %all-to-all-start.1) | async-done | bytes 1048608 | tf_op jit(solution)/shard_map/all_to_all | solution.py:284
  102.7 3.5 %pack.2 = bf16[64,4224]{1,0:T(8,128)(2,1)} custom-call(s32[32]{0:T(128)} %sub.3.first_ref, bf16[32,64,256]{2,1,0:T(8,128)(2,1)} %copy-done.3), custom_call_target="tpu_custom_call" | custom-call | tf_op jit(solution)/shard_map/pack/pallas_call | solution.py:160
  106.3 1.1 fusion.3
  107.4 1.7 collective-permute-start.8
  111.4 1.0 collective-permute-start.20
  112.4 1.0 pad_maximum_fusion.11
  115.3 1.4 collective-permute-done.6
  117.0 1.2 collective-permute-start.7
  122.8 1.0 pad_maximum_fusion.7
  123.8 1.4 collective-permute-start.17
  125.3 1.0 pad_maximum_fusion.6
  126.3 4.7 %collective-permute-done.7 = bf16[64,4224]{1,0:T(8,128)(2,1)S(1)} collective-permute-done((bf16[64,4224]{1,0:T(8,128)(2,1)S(1)}, bf16[64,4224]{1,0:T(8,128)(2,1)S(1)}, u32[]{:S(2)}, u32[]{:S(2)}) %collective-permute-start.7) | collective-permute-done | bytes 540704 | tf_op jit(solution)/shard_map/ppermute | solution.py:269
  131.0 2.3 %collective-permute-start.13 = (bf16[64,4224]{1,0:T(8,128)(2,1)S(1)}, bf16[64,4224]{1,0:T(8,128)(2,1)S(1)}, u32[]{:S(2)}, u32[]{:S(2)}) collective-permute-start(bf16[64,4224]{1,0:T(8,128)(2,1)S(1)} %pad_maximum_fusion.6), channel_id=1, source_target_pairs={{0,24},{8,16},{16,8},{24,0},{1,25},{9,17},{17,9},{25,1},{2,26},{10... | collective-permute-start | bytes 1622024 | tf_op jit(solution)/shard_map/ppermute | solution.py:269
  133.5 2.1 %collective-permute-start.10 = (bf16[256,4224]{1,0:T(8,128)(2,1)S(1)}, bf16[256,4224]{1,0:T(8,128)(2,1)}, u32[]{:S(2)}, u32[]{:S(2)}) collective-permute-start(bf16[256,4224]{1,0:T(8,128)(2,1)S(1)} %constant_dynamic-update-slice_fusion.refs_2_), channel_id=1, source_target_pairs={{0,4},{4,0},{1,5},{5,1},{2,6},{6,2},{3,7},{7,3},{8,12},{12,8},{9,1... | collective-permute-start | bytes 6488072 | tf_op jit(solution)/shard_map/ppermute | solution.py:265
  135.6 8.4 %collective-permute-done.13 = bf16[64,4224]{1,0:T(8,128)(2,1)S(1)} collective-permute-done((bf16[64,4224]{1,0:T(8,128)(2,1)S(1)}, bf16[64,4224]{1,0:T(8,128)(2,1)S(1)}, u32[]{:S(2)}, u32[]{:S(2)}) %collective-permute-start.13) | collective-permute-done | bytes 540704 | tf_op jit(solution)/shard_map/ppermute | solution.py:269
  144.0 1.0 pad_maximum_fusion.refs_4_
  145.1 1.5 collective-permute-start.14
  146.5 2.0 pad_maximum_fusion.1.refs_6_
  148.6 1.2 collective-permute-start.18
  149.8 2.1 pad_maximum_fusion.2.refs_8_
  151.9 2.0 pad_maximum_fusion.3.refs_10_
  153.9 2.0 collective-permute-start.26
  157.1 11.8 %collective-permute-done.14.refs_5_ = bf16[128,4224]{1,0:T(8,128)(2,1)} collective-permute-done((bf16[128,4224]{1,0:T(8,128)(2,1)S(1)}, bf16[128,4224]{1,0:T(8,128)(2,1)}, u32[]{:S(2)}, u32[]{:S(2)}) %collective-permute-start.14) | collective-permute-done | bytes 1081376 | tf_op jit(solution)/shard_map/ppermute | solution.py:269
  168.9 2.1 %collective-permute-done.18.refs_7_ = bf16[128,4224]{1,0:T(8,128)(2,1)} collective-permute-done((bf16[128,4224]{1,0:T(8,128)(2,1)}, bf16[128,4224]{1,0:T(8,128)(2,1)}, u32[]{:S(2)}, u32[]{:S(2)}) %collective-permute-start.18) | collective-permute-done | bytes 1081376 | tf_op jit(solution)/shard_map/ppermute | solution.py:269
  171.0 3.6 %collective-permute-done.22.refs_9_ = bf16[128,4224]{1,0:T(8,128)(2,1)} collective-permute-done((bf16[128,4224]{1,0:T(8,128)(2,1)}, bf16[128,4224]{1,0:T(8,128)(2,1)}, u32[]{:S(2)}, u32[]{:S(2)}) %collective-permute-start.22) | collective-permute-done | bytes 1081376 | tf_op jit(solution)/shard_map/ppermute | solution.py:269
  174.6 3.2 %collective-permute-done.26.refs_11_ = bf16[128,4224]{1,0:T(8,128)(2,1)} collective-permute-done((bf16[128,4224]{1,0:T(8,128)(2,1)}, bf16[128,4224]{1,0:T(8,128)(2,1)}, u32[]{:S(2)}, u32[]{:S(2)}) %collective-permute-start.26) | collective-permute-done | bytes 1081376 | tf_op jit(solution)/shard_map/ppermute | solution.py:269
  177.8 10.2 %gram.3 = (f32[264,512]{1,0:T(8,128)}, f32[264,512]{1,0:T(8,128)}) custom-call(s32[16]{0:T(128)} %stack.219.refs_0_, s32[32]{0:T(128)} %stack.252.refs_1_, bf16[256,4224]{1,0:T(8,128)(2,1)} %copy-done, bf16[256,4224]{1,0:T(8,128)(2,1)} %collective-permute-done.10.refs_3_, bf16[128,4224]{1,0:T(8,128)(2,1)} %copy-done.1, ...), custom_call_target="tpu_custom_call" | custom-call | flops 2147483648 | bytes 10485760 | tf_op jit(solution)/shard_map/gram/pallas_call | solution.py:212
  188.0 3.9 %collective-permute-start.28 = (f32[264,512]{1,0:T(8,128)}, f32[264,512]{1,0:T(8,128)S(1)}, u32[]{:S(2)}, u32[]{:S(2)}) collective-permute-start(f32[264,512]{1,0:T(8,128)} %get-tuple-element.23), channel_id=1, source_target_pairs={{0,4},{4,0},{1,5},{5,1},{2,6},{6,2},{3,7},{7,3},{8,12},{12,8},{9,1... | collective-permute-start | bytes 1622024 | tf_op jit(solution)/shard_map/ppermute | solution.py:265
  192.0 10.2 %gram.2 = (f32[264,512]{1,0:T(8,128)}, f32[264,512]{1,0:T(8,128)}) custom-call(s32[16]{0:T(128)} %stack.219.refs_0_, s32[32]{0:T(128)} %stack.252.refs_1_, bf16[256,4224]{1,0:T(8,128)(2,1)} %copy-done, bf16[256,4224]{1,0:T(8,128)(2,1)} %collective-permute-done.10.refs_3_, bf16[128,4224]{1,0:T(8,128)(2,1)} %copy-done.1, ...), custom_call_target="tpu_custom_call" | custom-call | flops 2147483648 | bytes 10485760 | tf_op jit(solution)/shard_map/gram/pallas_call | solution.py:212
  205.2 3.2 %finish.1 = (f32[1,2048]{1,0:T(1,128)}, f32[256,2048]{1,0:T(8,128)}) custom-call(s32[4]{0:T(128)} %pad_add_fusion.info_ref, f32[1]{0:T(128)} %bitcast.7.total_ref, f32[264,512]{1,0:T(8,128)} %get-tuple-element.20.own0_ref, f32[264,512]{1,0:T(8,128)} %get-tuple-element.21.own1_ref, f32[264,512]{1,0:T(8,128)} %copy-done.6, f32[264,512]{1,0:T(8,128)} %copy-done.5), custom_call_target="tpu_custom_call" | custom-call | tf_op jit(solution)/shard_map/finish/pallas_call | solution.py:251
  (86 shorter events, 16.6 us)
Async XLA Ops:
  0.6 7.6 %copy-start.10 = (f32[2048]{0:T(1024)S(1)}, f32[2048]{0:T(1024)}, u32[]{:S(2)}) copy-start(f32[2048]{0:T(1024)} %param.5) | copy-start | bytes 24580
  4.0 5.5 %collective-permute-start.2 = (f32[8,256]{1,0:T(8,128)}, f32[8,256]{1,0:T(8,128)S(1)}, u32[]{:S(2)}, u32[]{:S(2)}) collective-permute-start(f32[8,256]{1,0:T(8,128)} %get-tuple-element.15.s0), channel_id=1, source_target_pairs={{0,3},{1,2},{2,1},{3,0},{4,7},{5,6},{6,5},{7,4},{8,11},{9,10},{10,... | collective-permute-start | bytes 24584 | tf_op jit(solution)/shard_map/ppermute | solution.py:269
  7.6 4.2 %collective-permute-start.1 = (f32[8,256]{1,0:T(8,128)}, f32[8,256]{1,0:T(8,128)S(1)}, u32[]{:S(2)}, u32[]{:S(2)}) collective-permute-start(f32[8,256]{1,0:T(8,128)} %get-tuple-element.15.s0), channel_id=1, source_target_pairs={{0,2},{1,3},{2,0},{3,1},{4,6},{5,7},{6,4},{7,5},{8,10},{9,11},{10,... | collective-permute-start | bytes 24584 | tf_op jit(solution)/shard_map/ppermute | solution.py:269
  8.0 3.9 %collective-permute-start = (f32[8,256]{1,0:T(8,128)}, f32[8,256]{1,0:T(8,128)S(1)}, u32[]{:S(2)}, u32[]{:S(2)}) collective-permute-start(f32[8,256]{1,0:T(8,128)} %get-tuple-element.15.s0), channel_id=1, source_target_pairs={{0,1},{1,0},{2,3},{3,2},{4,5},{5,4},{6,7},{7,6},{8,9},{9,8},{10,11... | collective-permute-start | bytes 24584 | tf_op jit(solution)/shard_map/ppermute | solution.py:269
  9.5 2.3 %copy-start.11 = (f32[8,256]{1,0:T(8,128)}, f32[8,256]{1,0:T(8,128)S(1)}, u32[]{:S(2)}) copy-start(f32[8,256]{1,0:T(8,128)S(1)} %collective-permute-done.2.s3) | copy-start | bytes 24580
  11.8 0.6 copy-start.12
  11.8 0.6 copy-start.13
  15.6 10.2 %copy-start.16 = (bf16[8,64,256]{2,1,0:T(8,128)(2,1)S(1)}, bf16[8,64,256]{2,1,0:T(8,128)(2,1)}, u32[]{:S(2)}) copy-start(bf16[8,64,256]{2,1,0:T(8,128)(2,1)} %get-tuple-element.17) | copy-start | bytes 786436
  15.6 10.3 %copy-start.15 = (bf16[8,64,256]{2,1,0:T(8,128)(2,1)S(1)}, bf16[8,64,256]{2,1,0:T(8,128)(2,1)}, u32[]{:S(2)}) copy-start(bf16[8,64,256]{2,1,0:T(8,128)(2,1)} %get-tuple-element.18) | copy-start | bytes 786436
  15.6 12.5 %copy-start.14 = (bf16[8,64,256]{2,1,0:T(8,128)(2,1)S(1)}, bf16[8,64,256]{2,1,0:T(8,128)(2,1)}, u32[]{:S(2)}) copy-start(bf16[8,64,256]{2,1,0:T(8,128)(2,1)} %get-tuple-element.19) | copy-start | bytes 786436
  15.7 60.0 %all-to-all-start = ((bf16[32,80,256]{2,1,0:T(8,128)(2,1)}), bf16[32,80,256]{2,1,0:T(8,128)(2,1)S(1)}, u32[]{:S(2)}, u32[]{:S(2)}) async-start(bf16[32,80,256]{2,1,0:T(8,128)(2,1)} %get-tuple-element.16.own_ref), calls=%async_computation | async-start | bytes 2621440 | tf_op jit(solution)/shard_map/all_to_all | solution.py:282
  25.8 7.8 %collective-permute-start.3 = (bf16[8,64,256]{2,1,0:T(8,128)(2,1)S(1)}, bf16[8,64,256]{2,1,0:T(8,128)(2,1)S(1)}, u32[]{:S(2)}, u32[]{:S(2)}) collective-permute-start(bf16[8,64,256]{2,1,0:T(8,128)(2,1)S(1)} %copy-done.16), channel_id=1, source_target_pairs={{0,1},{1,0},{2,3},{3,2},{4,5},{5,4},{6,7},{7,6},{8,9},{9,8},{10,11... | collective-permute-start | bytes 786440 | tf_op jit(solution)/shard_map/ppermute | solution.py:269
  25.9 14.1 %collective-permute-start.4 = (bf16[8,64,256]{2,1,0:T(8,128)(2,1)S(1)}, bf16[8,64,256]{2,1,0:T(8,128)(2,1)S(1)}, u32[]{:S(2)}, u32[]{:S(2)}) collective-permute-start(bf16[8,64,256]{2,1,0:T(8,128)(2,1)S(1)} %copy-done.15), channel_id=1, source_target_pairs={{0,2},{1,3},{2,0},{3,1},{4,6},{5,7},{6,4},{7,5},{8,10},{9,11},{10,... | collective-permute-start | bytes 786440 | tf_op jit(solution)/shard_map/ppermute | solution.py:269
  28.1 13.9 %collective-permute-start.5 = (bf16[8,64,256]{2,1,0:T(8,128)(2,1)S(1)}, bf16[8,64,256]{2,1,0:T(8,128)(2,1)S(1)}, u32[]{:S(2)}, u32[]{:S(2)}) collective-permute-start(bf16[8,64,256]{2,1,0:T(8,128)(2,1)S(1)} %copy-done.14), channel_id=1, source_target_pairs={{0,3},{1,2},{2,1},{3,0},{4,7},{5,6},{6,5},{7,4},{8,11},{9,10},{10,... | collective-permute-start | bytes 786440 | tf_op jit(solution)/shard_map/ppermute | solution.py:269
  33.6 8.4 %copy-start.7 = (bf16[8,64,256]{2,1,0:T(8,128)(2,1)}, bf16[8,64,256]{2,1,0:T(8,128)(2,1)S(1)}, u32[]{:S(2)}) copy-start(bf16[8,64,256]{2,1,0:T(8,128)(2,1)S(1)} %collective-permute-done.3.a_ref) | copy-start | bytes 786436
  40.0 2.0 copy-start.8
  42.0 0.7 copy-start.9
  75.6 8.9 %copy-start.2 = (bf16[32,80,256]{2,1,0:T(8,128)(2,1)}, bf16[32,80,256]{2,1,0:T(8,128)(2,1)S(1)}, u32[]{:S(2)}) copy-start(bf16[32,80,256]{2,1,0:T(8,128)(2,1)S(1)} %all-to-all-done.in_ref) | copy-start | bytes 3932164
  75.6 26.1 %all-to-all-start.1 = ((bf16[32,64,256]{2,1,0:T(8,128)(2,1)}), bf16[32,64,256]{2,1,0:T(8,128)(2,1)S(1)}, u32[]{:S(2)}, u32[]{:S(2)}) async-start(bf16[32,64,256]{2,1,0:T(8,128)(2,1)} %order.1), calls=%async_computation.1 | async-start | bytes 2097152 | tf_op jit(solution)/shard_map/all_to_all | solution.py:284
  91.9 17.2 %collective-permute-start.23 = (bf16[16,4224]{1,0:T(8,128)(2,1)S(1)}, bf16[16,4224]{1,0:T(8,128)(2,1)}, u32[]{:S(2)}, u32[]{:S(2)}) collective-permute-start(bf16[16,4224]{1,0:T(8,128)(2,1)S(1)} %get-tuple-element.28), channel_id=1, source_target_pairs={{0,96},{32,64},{64,32},{96,0},{1,97},{33,65},{65,33},{97,1},{2,98}... | collective-permute-start | bytes 405512 | tf_op jit(solution)/shard_map/ppermute | solution.py:269
  94.5 15.5 %collective-permute-start.19 = (bf16[16,4224]{1,0:T(8,128)(2,1)S(1)}, bf16[16,4224]{1,0:T(8,128)(2,1)}, u32[]{:S(2)}, u32[]{:S(2)}) collective-permute-start(bf16[16,4224]{1,0:T(8,128)(2,1)S(1)} %get-tuple-element.29), channel_id=1, source_target_pairs={{0,24},{8,16},{16,8},{24,0},{1,25},{9,17},{17,9},{25,1},{2,26},{10... | collective-permute-start | bytes 405512 | tf_op jit(solution)/shard_map/ppermute | solution.py:269
  96.9 14.5 %collective-permute-start.15 = (bf16[16,4224]{1,0:T(8,128)(2,1)}, bf16[16,4224]{1,0:T(8,128)(2,1)}, u32[]{:S(2)}, u32[]{:S(2)}) collective-permute-start(bf16[16,4224]{1,0:T(8,128)(2,1)} %get-tuple-element.30), channel_id=1, source_target_pairs={{0,32},{32,0},{64,96},{96,64},{1,33},{33,1},{65,97},{97,65},{2,34}... | collective-permute-start | bytes 405512 | tf_op jit(solution)/shard_map/ppermute | solution.py:269
  96.9 16.4 %collective-permute-start.11 = (bf16[16,4224]{1,0:T(8,128)(2,1)}, bf16[16,4224]{1,0:T(8,128)(2,1)}, u32[]{:S(2)}, u32[]{:S(2)}) collective-permute-start(bf16[16,4224]{1,0:T(8,128)(2,1)} %get-tuple-element.31), channel_id=1, source_target_pairs={{0,8},{8,0},{16,24},{24,16},{1,9},{9,1},{17,25},{25,17},{2,10},{10... | collective-permute-start | bytes 405512 | tf_op jit(solution)/shard_map/ppermute | solution.py:269
  101.7 1.0 copy-start.3
  107.4 9.6 %collective-permute-start.8 = (bf16[32,4224]{1,0:T(8,128)(2,1)S(1)}, bf16[32,4224]{1,0:T(8,128)(2,1)S(1)}, u32[]{:S(2)}, u32[]{:S(2)}) collective-permute-start(bf16[32,4224]{1,0:T(8,128)(2,1)S(1)} %get-tuple-element.32), channel_id=1, source_target_pairs={{0,3},{1,2},{2,1},{3,0},{4,7},{5,6},{6,5},{7,4},{8,11},{9,10},{10,... | collective-permute-start | bytes 811016 | tf_op jit(solution)/shard_map/ppermute | solution.py:269
  109.1 7.6 %collective-permute-start.6 = (bf16[32,4224]{1,0:T(8,128)(2,1)S(1)}, bf16[32,4224]{1,0:T(8,128)(2,1)S(1)}, u32[]{:S(2)}, u32[]{:S(2)}) collective-permute-start(bf16[32,4224]{1,0:T(8,128)(2,1)S(1)} %get-tuple-element.34), channel_id=1, source_target_pairs={{0,1},{1,0},{2,3},{3,2},{4,5},{5,4},{6,7},{7,6},{8,9},{9,8},{10,11... | collective-permute-start | bytes 811016 | tf_op jit(solution)/shard_map/ppermute | solution.py:269
  110.0 8.2 %collective-permute-start.24 = (bf16[32,4224]{1,0:T(8,128)(2,1)S(1)}, bf16[32,4224]{1,0:T(8,128)(2,1)S(1)}, u32[]{:S(2)}, u32[]{:S(2)}) collective-permute-start(bf16[32,4224]{1,0:T(8,128)(2,1)S(1)} %pad_maximum_fusion.13), channel_id=1, source_target_pairs={{0,8},{8,0},{16,24},{24,16},{1,9},{9,1},{17,25},{25,17},{2,10},{10... | collective-permute-start | bytes 811016 | tf_op jit(solution)/shard_map/ppermute | solution.py:269
  111.4 8.5 %collective-permute-start.20 = (bf16[32,4224]{1,0:T(8,128)(2,1)S(1)}, bf16[32,4224]{1,0:T(8,128)(2,1)S(1)}, u32[]{:S(2)}, u32[]{:S(2)}) collective-permute-start(bf16[32,4224]{1,0:T(8,128)(2,1)S(1)} %pad_maximum_fusion.12), channel_id=1, source_target_pairs={{0,96},{32,64},{64,32},{96,0},{1,97},{33,65},{65,33},{97,1},{2,98}... | collective-permute-start | bytes 811016 | tf_op jit(solution)/shard_map/ppermute | solution.py:269
  113.4 8.5 %collective-permute-start.16 = (bf16[32,4224]{1,0:T(8,128)(2,1)S(1)}, bf16[32,4224]{1,0:T(8,128)(2,1)S(1)}, u32[]{:S(2)}, u32[]{:S(2)}) collective-permute-start(bf16[32,4224]{1,0:T(8,128)(2,1)S(1)} %pad_maximum_fusion.11), channel_id=1, source_target_pairs={{0,24},{8,16},{16,8},{24,0},{1,25},{9,17},{17,9},{25,1},{2,26},{10... | collective-permute-start | bytes 811016 | tf_op jit(solution)/shard_map/ppermute | solution.py:269
  116.7 7.2 %collective-permute-start.12 = (bf16[32,4224]{1,0:T(8,128)(2,1)S(1)}, bf16[32,4224]{1,0:T(8,128)(2,1)S(1)}, u32[]{:S(2)}, u32[]{:S(2)}) collective-permute-start(bf16[32,4224]{1,0:T(8,128)(2,1)S(1)} %pad_maximum_fusion.10), channel_id=1, source_target_pairs={{0,32},{32,0},{64,96},{96,64},{1,33},{33,1},{65,97},{97,65},{2,34}... | collective-permute-start | bytes 811016 | tf_op jit(solution)/shard_map/ppermute | solution.py:269
  117.0 14.0 %collective-permute-start.7 = (bf16[64,4224]{1,0:T(8,128)(2,1)S(1)}, bf16[64,4224]{1,0:T(8,128)(2,1)S(1)}, u32[]{:S(2)}, u32[]{:S(2)}) collective-permute-start(bf16[64,4224]{1,0:T(8,128)(2,1)S(1)} %pad_maximum_fusion.4), channel_id=1, source_target_pairs={{0,3},{1,2},{2,1},{3,0},{4,7},{5,6},{6,5},{7,4},{8,11},{9,10},{10,... | collective-permute-start | bytes 1622024 | tf_op jit(solution)/shard_map/ppermute | solution.py:269
  118.3 15.2 %collective-permute-start.9 = (bf16[64,4224]{1,0:T(8,128)(2,1)S(1)}, bf16[64,4224]{1,0:T(8,128)(2,1)S(1)}, u32[]{:S(2)}, u32[]{:S(2)}) collective-permute-start(bf16[64,4224]{1,0:T(8,128)(2,1)S(1)} %pad_maximum_fusion.5), channel_id=1, source_target_pairs={{0,1},{1,0},{2,3},{3,2},{4,5},{5,4},{6,7},{7,6},{8,9},{9,8},{10,11... | collective-permute-start | bytes 1622024 | tf_op jit(solution)/shard_map/ppermute | solution.py:269
  119.9 32.1 %collective-permute-start.25 = (bf16[64,4224]{1,0:T(8,128)(2,1)S(1)}, bf16[64,4224]{1,0:T(8,128)(2,1)S(1)}, u32[]{:S(2)}, u32[]{:S(2)}) collective-permute-start(bf16[64,4224]{1,0:T(8,128)(2,1)S(1)} %pad_maximum_fusion.9), channel_id=1, source_target_pairs={{0,32},{32,0},{64,96},{96,64},{1,33},{33,1},{65,97},{97,65},{2,34}... | collective-permute-start | bytes 1622024 | tf_op jit(solution)/shard_map/ppermute | solution.py:269
  121.9 27.9 %collective-permute-start.21 = (bf16[64,4224]{1,0:T(8,128)(2,1)S(1)}, bf16[64,4224]{1,0:T(8,128)(2,1)S(1)}, u32[]{:S(2)}, u32[]{:S(2)}) collective-permute-start(bf16[64,4224]{1,0:T(8,128)(2,1)S(1)} %pad_maximum_fusion.8), channel_id=1, source_target_pairs={{0,8},{8,0},{16,24},{24,16},{1,9},{9,1},{17,25},{25,17},{2,10},{10... | collective-permute-start | bytes 1622024 | tf_op jit(solution)/shard_map/ppermute | solution.py:269
  123.8 9.6 %copy-start.4 = (bf16[64,4224]{1,0:T(8,128)(2,1)S(1)}, bf16[64,4224]{1,0:T(8,128)(2,1)}, u32[]{:S(2)}) copy-start(bf16[64,4224]{1,0:T(8,128)(2,1)} %pack.2) | copy-start | bytes 1622020
  123.8 22.7 %collective-permute-start.17 = (bf16[64,4224]{1,0:T(8,128)(2,1)S(1)}, bf16[64,4224]{1,0:T(8,128)(2,1)S(1)}, u32[]{:S(2)}, u32[]{:S(2)}) collective-permute-start(bf16[64,4224]{1,0:T(8,128)(2,1)S(1)} %pad_maximum_fusion.7), channel_id=1, source_target_pairs={{0,96},{32,64},{64,32},{96,0},{1,97},{33,65},{65,33},{97,1},{2,98}... | collective-permute-start | bytes 1622024 | tf_op jit(solution)/shard_map/ppermute | solution.py:269
  131.0 13.0 %collective-permute-start.13 = (bf16[64,4224]{1,0:T(8,128)(2,1)S(1)}, bf16[64,4224]{1,0:T(8,128)(2,1)S(1)}, u32[]{:S(2)}, u32[]{:S(2)}) collective-permute-start(bf16[64,4224]{1,0:T(8,128)(2,1)S(1)} %pad_maximum_fusion.6), channel_id=1, source_target_pairs={{0,24},{8,16},{16,8},{24,0},{1,25},{9,17},{17,9},{25,1},{2,26},{10... | collective-permute-start | bytes 1622024 | tf_op jit(solution)/shard_map/ppermute | solution.py:269
  133.5 11.5 %copy-start = (bf16[256,4224]{1,0:T(8,128)(2,1)}, bf16[256,4224]{1,0:T(8,128)(2,1)S(1)}, u32[]{:S(2)}) copy-start(bf16[256,4224]{1,0:T(8,128)(2,1)S(1)} %constant_dynamic-update-slice_fusion.refs_2_) | copy-start | bytes 6488068
  133.5 44.3 %collective-permute-start.10 = (bf16[256,4224]{1,0:T(8,128)(2,1)S(1)}, bf16[256,4224]{1,0:T(8,128)(2,1)}, u32[]{:S(2)}, u32[]{:S(2)}) collective-permute-start(bf16[256,4224]{1,0:T(8,128)(2,1)S(1)} %constant_dynamic-update-slice_fusion.refs_2_), channel_id=1, source_target_pairs={{0,4},{4,0},{1,5},{5,1},{2,6},{6,2},{3,7},{7,3},{8,12},{12,8},{9,1... | collective-permute-start | bytes 6488072 | tf_op jit(solution)/shard_map/ppermute | solution.py:265
  145.1 3.5 %copy-start.1 = (bf16[128,4224]{1,0:T(8,128)(2,1)}, bf16[128,4224]{1,0:T(8,128)(2,1)S(1)}, u32[]{:S(2)}) copy-start(bf16[128,4224]{1,0:T(8,128)(2,1)S(1)} %pad_maximum_fusion.refs_4_) | copy-start | bytes 3244036
  145.1 23.8 %collective-permute-start.14 = (bf16[128,4224]{1,0:T(8,128)(2,1)S(1)}, bf16[128,4224]{1,0:T(8,128)(2,1)}, u32[]{:S(2)}, u32[]{:S(2)}) collective-permute-start(bf16[128,4224]{1,0:T(8,128)(2,1)S(1)} %pad_maximum_fusion.refs_4_), channel_id=1, source_target_pairs={{0,96},{32,64},{64,32},{96,0},{1,97},{33,65},{65,33},{97,1},{2,98}... | collective-permute-start | bytes 3244040 | tf_op jit(solution)/shard_map/ppermute | solution.py:269
  148.6 22.5 %collective-permute-start.18 = (bf16[128,4224]{1,0:T(8,128)(2,1)}, bf16[128,4224]{1,0:T(8,128)(2,1)}, u32[]{:S(2)}, u32[]{:S(2)}) collective-permute-start(bf16[128,4224]{1,0:T(8,128)(2,1)} %pad_maximum_fusion.1.refs_6_), channel_id=1, source_target_pairs={{0,8},{8,0},{16,24},{24,16},{1,9},{9,1},{17,25},{25,17},{2,10},{10... | collective-permute-start | bytes 3244040 | tf_op jit(solution)/shard_map/ppermute | solution.py:269
  151.9 22.7 %collective-permute-start.22 = (bf16[128,4224]{1,0:T(8,128)(2,1)}, bf16[128,4224]{1,0:T(8,128)(2,1)}, u32[]{:S(2)}, u32[]{:S(2)}) collective-permute-start(bf16[128,4224]{1,0:T(8,128)(2,1)} %pad_maximum_fusion.2.refs_8_), channel_id=1, source_target_pairs={{0,32},{32,0},{64,96},{96,64},{1,33},{33,1},{65,97},{97,65},{2,34}... | collective-permute-start | bytes 3244040 | tf_op jit(solution)/shard_map/ppermute | solution.py:269
  153.9 23.9 %collective-permute-start.26 = (bf16[128,4224]{1,0:T(8,128)(2,1)}, bf16[128,4224]{1,0:T(8,128)(2,1)}, u32[]{:S(2)}, u32[]{:S(2)}) collective-permute-start(bf16[128,4224]{1,0:T(8,128)(2,1)} %pad_maximum_fusion.3.refs_10_), channel_id=1, source_target_pairs={{0,24},{8,16},{16,8},{24,0},{1,25},{9,17},{17,9},{25,1},{2,26},{10... | collective-permute-start | bytes 3244040 | tf_op jit(solution)/shard_map/ppermute | solution.py:269
  188.0 15.6 %collective-permute-start.28 = (f32[264,512]{1,0:T(8,128)}, f32[264,512]{1,0:T(8,128)S(1)}, u32[]{:S(2)}, u32[]{:S(2)}) collective-permute-start(f32[264,512]{1,0:T(8,128)} %get-tuple-element.23), channel_id=1, source_target_pairs={{0,4},{4,0},{1,5},{5,1},{2,6},{6,2},{3,7},{7,3},{8,12},{12,8},{9,1... | collective-permute-start | bytes 1622024 | tf_op jit(solution)/shard_map/ppermute | solution.py:265
  202.2 2.2 %collective-permute-start.27 = (f32[264,512]{1,0:T(8,128)}, f32[264,512]{1,0:T(8,128)S(1)}, u32[]{:S(2)}, u32[]{:S(2)}) collective-permute-start(f32[264,512]{1,0:T(8,128)} %get-tuple-element.22), channel_id=1, source_target_pairs={{0,4},{4,0},{1,5},{5,1},{2,6},{6,2},{3,7},{7,3},{8,12},{12,8},{9,1... | collective-permute-start | bytes 1622024 | tf_op jit(solution)/shard_map/ppermute | solution.py:265
  203.7 0.8 copy-start.5
  204.4 0.8 copy-start.6

commit v5 on v4

v5 whole, which is shorter than its diff:
```python
import jax
import jax.numpy as jnp
from jax import lax
from jax.experimental import pallas as pl
from jax.experimental.pallas import tpu as pltpu
from jax.sharding import Mesh, PartitionSpec as P

epsilon = 1e-05
TOK = ("z", "x", "c")
SLOTS = 256
LIVE = 4096
WIDTH = 2048
PIECE = 64
EXTRA = 16
LONG = LIVE + 128
MIB = 1024 * 1024
bf16 = jnp.bfloat16
f32 = jnp.float32


def params(mib):
    return pltpu.CompilerParams(vmem_limit_bytes=mib * MIB)


def spread(value, place):
    high = value.astype(bf16).astype(f32)
    middle = (value - high).astype(bf16).astype(f32)
    low = value - high - middle
    rest = jnp.where(place == 2, low, 0.0)
    return jnp.where(place == 0, high, jnp.where(place == 1, middle, rest))


def pick_kernel(index_ref, counts_ref, resid_ref, picked_ref, sums_ref):
    tokens = resid_ref.shape[0]
    token = lax.broadcasted_iota(jnp.int32, (tokens, SLOTS), 0)
    slot = lax.broadcasted_iota(jnp.int32, (1, SLOTS), 1)
    half = SLOTS // 2
    end = jnp.where(slot < half, counts_ref[0], half + counts_ref[1])
    kept = jnp.where(slot < end, index_ref[...], -1)
    one_hot = jnp.where(token == kept, 1.0, 0.0).astype(bf16)
    total = jnp.zeros((1, SLOTS), f32)
    step = 512
    for k in range(WIDTH // step):
        part = lax.dot_general(
            resid_ref[:, k * step : (k + 1) * step],
            one_hot,
            (((0,), (0,)), ((), ())),
            preferred_element_type=f32,
        )
        total += jnp.sum(part * part, axis=0, keepdims=True)
        picked_ref[k * step : (k + 1) * step, :] = part.astype(bf16)
    sums_ref[...] = jnp.broadcast_to(total, sums_ref.shape)


def pick(resid, keep_index, counts):
    return pl.pallas_call(
        pick_kernel,
        out_shape=(
            jax.ShapeDtypeStruct((WIDTH, SLOTS), bf16),
            jax.ShapeDtypeStruct((8, SLOTS), f32),
        ),
        in_specs=[
            pl.BlockSpec(memory_space=pltpu.VMEM),
            pl.BlockSpec(memory_space=pltpu.SMEM),
            pl.BlockSpec(memory_space=pltpu.VMEM),
        ],
        out_specs=(pl.BlockSpec(memory_space=pltpu.VMEM),) * 2,
        compiler_params=params(16),
        name="pick",
    )(keep_index[None, :], counts, resid)


PARTNERS = (("x", 1), ("z", 1), ("x", 3), ("z", 3))


def side(place, flip, first):
    if flip == 1 and not first:
        return (place ^ (place >> 1)) & 1
    return place & 1 if flip == 1 else place >> 1


def slot_of(s, x, z):
    at, seen = 0, []
    for step in range(4):
        axis, flip = PARTNERS[(s + step) % 4]
        at += side(x if axis == "x" else z, flip, axis not in seen) << step
        seen.append(axis)
    return at


def norm_kernel(place_ref, counts_ref, picked_ref, gain_ref, s0, s1, s2, s3, out_ref, *refs):
    turn_refs, all_ref = refs[:4], refs[4]
    squares = (s0[:1, :] + s2[:1, :]) + (s1[:1, :] + s3[:1, :])
    scale = lax.rsqrt(squares / 8192 + epsilon)
    y = place_ref[0]
    live = (counts_ref[0] + counts_ref[1]).astype(f32)
    extra = jnp.full((EXTRA, SLOTS), live, f32).astype(bf16)
    for s in range(4):
        for c in range(2):
            first = (s * 2 + c) * 256
            rows = picked_ref[first : first + 256, :].astype(f32)
            short = (rows * scale * gain_ref[first : first + 256, :]).astype(bf16)
            all_ref[first : first + 256, :] = short
            for z in range(4):
                for x in range(4):
                    at = slot_of(s, x, z) * 16
                    out_ref[z * 8 + x * 2 + c, s * 16 : (s + 1) * 16, :] = short[at : at + 16, :]
    for t in range(32):
        out_ref[t, PIECE:, :] = extra
    for flip, ref in enumerate(turn_refs):
        q = y ^ flip
        low = q * 32
        high = 128 + (((q ^ (q >> 1)) & 1) * 2 + (q >> 1)) * 32
        for k in range(8):
            ref[k, :32, :] = all_ref[pl.ds(pl.multiple_of(k * 256 + low, 32), 32), :]
            ref[k, 32:, :] = all_ref[pl.ds(pl.multiple_of(k * 256 + high, 32), 32), :]


def norm(place, counts, picked, gain, sums):
    return pl.pallas_call(
        norm_kernel,
        out_shape=(jax.ShapeDtypeStruct((32, PIECE + EXTRA, SLOTS), bf16),)
        + (jax.ShapeDtypeStruct((8, PIECE, SLOTS), bf16),) * 4,
        in_specs=[pl.BlockSpec(memory_space=pltpu.SMEM)] * 2 + [pl.BlockSpec(memory_space=pltpu.VMEM)] * 6,
        out_specs=(pl.BlockSpec(memory_space=pltpu.VMEM),) * 5,
        scratch_shapes=[pltpu.VMEM((WIDTH, SLOTS), bf16)],
        compiler_params=params(12),
        name="norm",
    )(place, counts, picked, gain, *sums)


def order_kernel(place_ref, own_ref, a_ref, b_ref, c_ref, out_ref):
    y = place_ref[0]
    for k in range(8):
        for flip, ref in enumerate((own_ref, a_ref, b_ref, c_ref)):
            out_ref[(y ^ flip) * 8 + k] = ref[k]


def order(place, blocks):
    return pl.pallas_call(
        order_kernel,
        out_shape=jax.ShapeDtypeStruct((32, PIECE, SLOTS), bf16),
        in_specs=[pl.BlockSpec(memory_space=pltpu.SMEM)] + [pl.BlockSpec(memory_space=pltpu.VMEM)] * 4,
        out_specs=pl.BlockSpec(memory_space=pltpu.VMEM),
        compiler_params=params(8),
        name="order",
    )(place, *blocks)


def pack_kernel(heights, first_ref, in_ref, *refs):
    out_refs, acc_ref = refs[:-1], refs[-1]
    acc_ref[...] = jnp.zeros_like(acc_ref)
    group = 4

    def body(g, _):
        moved = []
        for k in range(group):
            t = g * group + k
            rows = in_ref[t, :PIECE, :].astype(f32)
            first = first_ref[t]
            base = pl.multiple_of((first // 128) * 128, 128)
            wide = jnp.concatenate([rows, jnp.zeros((PIECE, 128), f32)], axis=1)
            moved.append((base, pltpu.roll(wide, first - base, 1)))
        for base, rows in moved:
            acc_ref[:, pl.ds(base, SLOTS + 128)] += rows
        return 0

    lax.fori_loop(0, 32 // group, body, 0)
    start = 0
    for ref, height in zip(out_refs, heights):
        rows = acc_ref[start : start + height, :LIVE]
        ref[:, :LIVE] = rows.astype(bf16)
        total = jnp.sum(rows, axis=1, keepdims=True)
        lane = lax.broadcasted_iota(jnp.int32, (height, 128), 1)
        ref[:, LIVE:] = spread(total, lane).astype(bf16)
        start += height


def pack(first, pieces, heights):
    return pl.pallas_call(
        lambda *refs: pack_kernel(heights, *refs),
        out_shape=tuple(jax.ShapeDtypeStruct((height, LONG), bf16) for height in heights),
        in_specs=[pl.BlockSpec(memory_space=pltpu.SMEM), pl.BlockSpec(memory_space=pltpu.VMEM)],
        out_specs=(pl.BlockSpec(memory_space=pltpu.VMEM),) * len(heights),
        scratch_shapes=[pltpu.VMEM((PIECE, LIVE + SLOTS + 128), f32)],
        compiler_params=params(10),
        name="pack",
    )(first, pieces)


def gram_kernel(rows_ref, cols_ref, own_ref, given_ref):
    product = lax.dot_general(
        rows_ref[:, :LIVE], cols_ref[:, :LIVE], (((1,), (1,)), ((), ())), preferred_element_type=f32
    )
    own_ref[:256, :] = product[:256]
    given_ref[:256, :] = product[256:]
    lane = lax.broadcasted_iota(jnp.int32, (16, 128), 1)
    terms = jnp.where(lane < 3, 1.0, 0.0).astype(bf16)
    sums = lax.dot_general(
        terms, cols_ref[:, LIVE:], (((1,), (1,)), ((), ())), preferred_element_type=f32
    )
    own_ref[256:, :] = sums[:8]
    given_ref[256:, :] = sums[:8]


def gram(rows, cols):
    return pl.pallas_call(
        gram_kernel,
        out_shape=(jax.ShapeDtypeStruct((264, 256), f32),) * 2,
        in_specs=[pl.BlockSpec(memory_space=pltpu.VMEM)] * 2,
        out_specs=(pl.BlockSpec(memory_space=pltpu.VMEM),) * 2,
        compiler_params=params(10),
        cost_estimate=pl.CostEstimate(
            flops=2 * 512 * 256 * LIVE, bytes_accessed=6 * 1024 * 1024, transcendentals=0
        ),
        name="gram",
    )(rows, cols)


def finish_kernel(info_ref, part_ref, *refs):
    own, got, (mean_ref, out_ref) = refs[:4], refs[4:8], refs[8:]
    core, row_first, col_first = info_ref[0], info_ref[1], info_ref[2]
    part = part_ref[0]
    row = row_first + lax.broadcasted_iota(jnp.int32, (256, 256), 0)
    col = col_first + lax.broadcasted_iota(jnp.int32, (256, 256), 1)
    for s in range(4):
        for ref, which in ((own[s], core), (got[s], 1 - core)):
            at = pl.multiple_of(s * 512 + which * 256, 256)
            out_ref[:, pl.ds(at, 256)] = jnp.where(row <= col + at, ref[:256, :] * part, 0.0)
            mean_ref[:, pl.ds(at, 256)] = ref[256:264, :][:1] * part


def finish(info, part, own, got):
    return pl.pallas_call(
        finish_kernel,
        out_shape=(
            jax.ShapeDtypeStruct((1, WIDTH), f32),
            jax.ShapeDtypeStruct((256, WIDTH), f32),
        ),
        in_specs=[pl.BlockSpec(memory_space=pltpu.SMEM)] * 2 + [pl.BlockSpec(memory_space=pltpu.VMEM)] * 8,
        out_specs=(pl.BlockSpec(memory_space=pltpu.VMEM),) * 2,
        compiler_params=params(10),
        name="finish",
    )(info, part, *own, *got)


def swap(value):
    return lax.ppermute(value, "c", [(0, 1), (1, 0)])


def trade(value, axis, flip):
    return lax.ppermute(value, axis, [(i, i ^ flip) for i in range(4)])


def join(*values):
    return jnp.concatenate(values, axis=0)


def meet(value, axis, flip, which):
    got = trade(value, axis, flip)
    return join(jnp.where(which == 0, value, got), jnp.where(which == 0, got, value))


def per_device(resid, norm_gain, keep_index, counts):
    z, x, c, y = (lax.axis_index(a) for a in ("z", "x", "c", "y"))
    place_y = y[None].astype(jnp.int32)
    picked, sums = pick(resid, keep_index, counts)
    all_sums = [sums] + [trade(sums, "y", flip) for flip in (1, 2, 3)]
    normed, *turns = norm(place_y, counts, picked, norm_gain[:, None], all_sums)
    pieces = lax.all_to_all(normed, TOK, 0, 0, tiled=True)
    panel = order(place_y, [turns[0]] + [trade(turns[flip], "y", flip) for flip in (1, 2, 3)])
    panel = lax.all_to_all(panel, TOK, 0, 0, tiled=True)

    loads = pieces[:, PIECE, 0].astype(jnp.int32)
    first = jnp.cumsum(loads) - loads
    part = 1.0 / jnp.sum(loads).astype(f32)

    streams = list(pack(first, pieces, (16, 16, 16, 16)))
    for step in range(4):
        for s in range(4):
            axis, flip = PARTNERS[(s + step) % 4]
            seen = [PARTNERS[(s + k) % 4][0] for k in range(step)]
            which = side(x if axis == "x" else z, flip, axis not in seen)
            streams[s] = meet(streams[s], axis, flip, which)

    low, high = pack(first, panel, (32, 32))
    low, high = meet(low, "y", 1, side(y, 1, True)), meet(high, "y", 3, side(y, 3, True))
    low, high = meet(low, "y", 3, side(y, 3, False)), meet(high, "y", 1, side(y, 1, False))
    rows = join(low, high)
    rows = join(rows, swap(rows))

    own, got = [], []
    for s in range(4):
        kept, given = gram(rows, streams[s])
        own.append(kept)
        got.append(swap(given))
    info = jnp.stack([c, (z * 8 + x * 2 + c) * 256, y * WIDTH]).astype(jnp.int32)
    mean, gram_factor = finish(info, part[None], own, got)
    return (mean[0], gram_factor)


def solution(mesh):
    fine = Mesh(mesh.devices.reshape(4, 4, 2, 4), ("z", "x", "c", "y"))
    return jax.shard_map(
        per_device,
        mesh=fine,
        in_specs=(P(TOK, "y"), P("y"), P(TOK), P(TOK)),
        out_specs=(P("y"), P(TOK, "y")),
        check_vma=False,
    )
```

time: 209 us -> 145 us (0.69)
  Pallas kernels: 70.4 us -> 15.8 us
  other arithmetic: 17.6 us -> 6.42 us
  local copies, waits for them, and re-layouts: 8.84 us -> 3.58 us
  waiting for transfers between devices: 55.7 us -> 60.3 us
  starting transfers between devices: 54.3 us -> 57.2 us
    pallas_call x1, Pallas kernels: 32.9 us -> 1.08 us  [order(): pl.pallas_call(order_kernel, out_shape=jax.ShapeDtypeStruct((32, PIECE, S...]
    pallas_call x4 -> x6, Pallas kernels: 27.6 us -> 9.17 us  [the longest x4 5.12 us: gram(): pl.pallas_call(gram_kernel, out_shape=(jax.ShapeDtypeStruct((264, 256), f...]
    concatenate x14 -> x19, other arithmetic: 15 us -> 1.41 us  [join(): return jnp.concatenate(values, axis=0)]
    ppermute x26, starting transfers between devices: 29.3 us -> 33.2 us  [trade(): return lax.ppermute(value, axis, [(i, i ^ flip) for i in range(4)])]
    slice x2 -> x0, local copies, waits for them, and re-layouts: 2.92 us -> none  [the longest x1 1.83 us: per_device(): streams = [mine[s * 16:(s + 1) * 16] for s in range(4)]]
    all_to_all x1, waiting for transfers between devices: 4.81 us -> 7.72 us  [per_device(): panel = lax.all_to_all(panel, TOK, 0, 0, tiled=True)]
    select_n x0 -> x18, other arithmetic: none -> 2.9 us  [meet(): jnp.where(which == 0, value, got)]
    all_to_all x1, starting transfers between devices: 8.72 us -> 5.83 us  [per_device(): panel = lax.all_to_all(panel, TOK, 0, 0, tiled=True)]
  transfers between devices with their start and end apart: 31 -> 33, of which waited for: 15 -> 19; matrix products, arithmetic and copies ran while one was open for 11% -> 5% of each run, Pallas kernels for 24% -> 4%
where the time goes in v5:
time: 145 us
  waiting for transfers between devices  60.3 us (42%)
  starting transfers between devices  57.2 us (39%)
  Pallas kernels  15.8 us (11%)
  other arithmetic  6.42 us (4%)
  local copies, waits for them, and re-layouts  3.58 us (2%)
  between operations  1.67 us (1%)
    ppermute x26, waiting for transfers between devices, trade(): return lax.ppermute(value, axis, [(i, i ^ flip) for i in range(4)])  48.7 us
    ppermute x26, starting transfers between devices, trade(): return lax.ppermute(value, axis, [(i, i ^ flip) for i in range(4)])  33.2 us
    all_to_all x1, starting transfers between devices, per_device(): pieces = lax.all_to_all(normed, TOK, 0, 0, tiled=True)  10.3 us
    ppermute x5, starting transfers between devices, swap(): return lax.ppermute(value, 'c', [(0, 1), (1, 0)])  7.85 us
    all_to_all x1, waiting for transfers between devices, per_device(): panel = lax.all_to_all(panel, TOK, 0, 0, tiled=True)  7.72 us
    all_to_all x1, starting transfers between devices, per_device(): panel = lax.all_to_all(panel, TOK, 0, 0, tiled=True)  5.83 us
    pallas_call x4, Pallas kernels, gram(): pl.pallas_call(gram_kernel, out_shape=(jax.ShapeDtypeStruct((264, 256), f...  5.12 us
    pallas_call x2, Pallas kernels, pack(): pl.pallas_call(lambda *refs: pack_kernel(heights, *refs), out_shape=tuple...  4.05 us
  transfers between devices with their start and end apart: 33, of which 19 were waited for; matrix products, arithmetic and copies ran while one was open for 5% of the time, Pallas kernels for 4%

profile of v5, /device:TPU:1, one launch (start us, length us, event | category | flops | bytes accessed | tf_op | source)
XLA Modules:
  0.0 145.0 jit_solution(2239491403703421667)
XLA Ops:
  0.6 1.6 %copy-done = bf16[512,2048]{1,0:T(8,128)(2,1)S(1)} copy-done((bf16[512,2048]{1,0:T(8,128)(2,1)S(1)}, bf16[512,2048]{1,0:T(8,128)(2,1)}, u32[]{:S(2)}) %copy-start) | copy-done | bytes 2097176
  2.2 0.7 copy-done.1
  2.9 0.7 copy-done.3
  3.6 1.3 pick.1
  4.9 2.2 %collective-permute-start = (f32[8,256]{1,0:T(8,128)S(1)}, f32[8,256]{1,0:T(8,128)S(1)}, u32[]{:S(2)}, u32[]{:S(2)}) collective-permute-start(f32[8,256]{1,0:T(8,128)S(1)} %get-tuple-element.26.s0), channel_id=1, source_target_pairs={{0,1},{1,0},{2,3},{3,2},{4,5},{5,4},{6,7},{7,6},{8,9},{9,8},{10,11... | collective-permute-start | bytes 24584 | tf_op jit(solution)/shard_map/ppermute | solution.py:252
  7.1 2.6 %collective-permute-start.1 = (f32[8,256]{1,0:T(8,128)S(1)}, f32[8,256]{1,0:T(8,128)S(1)}, u32[]{:S(2)}, u32[]{:S(2)}) collective-permute-start(f32[8,256]{1,0:T(8,128)S(1)} %get-tuple-element.26.s0), channel_id=1, source_target_pairs={{0,2},{1,3},{2,0},{3,1},{4,6},{5,7},{6,4},{7,5},{8,10},{9,11},{10,... | collective-permute-start | bytes 24584 | tf_op jit(solution)/shard_map/ppermute | solution.py:252
  10.1 1.0 collective-permute-done.1.s2
  11.1 2.3 %collective-permute-done.2.s3 = f32[8,256]{1,0:T(8,128)S(1)} collective-permute-done((f32[8,256]{1,0:T(8,128)S(1)}, f32[8,256]{1,0:T(8,128)S(1)}, u32[]{:S(2)}, u32[]{:S(2)}) %collective-permute-start.2) | collective-permute-done | bytes 8224 | tf_op jit(solution)/shard_map/ppermute | solution.py:252
  13.5 2.0 %norm.1 = (bf16[32,80,256]{2,1,0:T(8,128)(2,1)}, bf16[8,64,256]{2,1,0:T(8,128)(2,1)S(1)}, bf16[8,64,256]{2,1,0:T(8,128)(2,1)S(1)}, bf16[8,64,256]{2,1,0:T(8,128)(2,1)S(1)}, bf16[8,64,256]{2,1,0:T(8,128)(2,1)S(1)}) custom-call(s32[1]{0:T(128)} %bitcast.3.place_ref, s32[2]{0:T(128)S(1)} %copy-done.2, bf16[2048,256]{1,0:T(8,128)(2,1)S(1)} %get-tuple-element.25.picked_ref, ...), custom_call_target="tpu_custom_call" | custom-call | tf_op jit(solution)/shard_map/norm/pallas_call | solution.py:120
  15.5 10.3 %all-to-all-start = ((bf16[32,80,256]{2,1,0:T(8,128)(2,1)}), bf16[32,80,256]{2,1,0:T(8,128)(2,1)S(1)}, u32[]{:S(2)}, u32[]{:S(2)}) async-start(bf16[32,80,256]{2,1,0:T(8,128)(2,1)} %get-tuple-element.27), calls=%async_computation | async-start | bytes 2621440 | tf_op jit(solution)/shard_map/all_to_all | solution.py:270
  25.9 1.1 collective-permute-start.4
  27.0 2.7 %collective-permute-start.5 = (bf16[8,64,256]{2,1,0:T(8,128)(2,1)S(1)}, bf16[8,64,256]{2,1,0:T(8,128)(2,1)S(1)}, u32[]{:S(2)}, u32[]{:S(2)}) collective-permute-start(bf16[8,64,256]{2,1,0:T(8,128)(2,1)S(1)} %get-tuple-element.31), channel_id=1, source_target_pairs={{0,3},{1,2},{2,1},{3,0},{4,7},{5,6},{6,5},{7,4},{8,11},{9,10},{10,... | collective-permute-start | bytes 786440 | tf_op jit(solution)/shard_map/ppermute | solution.py:252
  29.7 3.8 %collective-permute-done.3.a_ref = bf16[8,64,256]{2,1,0:T(8,128)(2,1)S(1)} collective-permute-done((bf16[8,64,256]{2,1,0:T(8,128)(2,1)S(1)}, bf16[8,64,256]{2,1,0:T(8,128)(2,1)S(1)}, u32[]{:S(2)}, u32[]{:S(2)}) %collective-permute-start.3) | collective-permute-done | bytes 262176 | tf_op jit(solution)/shard_map/ppermute | solution.py:252
  33.6 5.3 %collective-permute-done.4.b_ref = bf16[8,64,256]{2,1,0:T(8,128)(2,1)S(1)} collective-permute-done((bf16[8,64,256]{2,1,0:T(8,128)(2,1)S(1)}, bf16[8,64,256]{2,1,0:T(8,128)(2,1)S(1)}, u32[]{:S(2)}, u32[]{:S(2)}) %collective-permute-start.4) | collective-permute-done | bytes 262176 | tf_op jit(solution)/shard_map/ppermute | solution.py:252
  38.9 2.1 %collective-permute-done.5.c_ref = bf16[8,64,256]{2,1,0:T(8,128)(2,1)S(1)} collective-permute-done((bf16[8,64,256]{2,1,0:T(8,128)(2,1)S(1)}, bf16[8,64,256]{2,1,0:T(8,128)(2,1)S(1)}, u32[]{:S(2)}, u32[]{:S(2)}) %collective-permute-start.5) | collective-permute-done | bytes 262176 | tf_op jit(solution)/shard_map/ppermute | solution.py:252
  41.0 1.1 order.1
  42.1 2.8 %all-to-all-done.refs_1_ = bf16[32,80,256]{2,1,0:T(8,128)(2,1)S(1)} async-done(((bf16[32,80,256]{2,1,0:T(8,128)(2,1)}), bf16[32,80,256]{2,1,0:T(8,128)(2,1)S(1)}, u32[]{:S(2)}, u32[]{:S(2)}) %all-to-all-start) | async-done | bytes 1310752 | tf_op jit(solution)/shard_map/all_to_all | solution.py:270
  44.9 5.8 %all-to-all-start.1 = ((bf16[32,64,256]{2,1,0:T(8,128)(2,1)}), bf16[32,64,256]{2,1,0:T(8,128)(2,1)S(1)}, u32[]{:S(2)}, u32[]{:S(2)}) async-start(bf16[32,64,256]{2,1,0:T(8,128)(2,1)} %order.1), calls=%async_computation.1 | async-start | bytes 2097152 | tf_op jit(solution)/shard_map/all_to_all | solution.py:272
  50.9 1.2 fusion
  52.1 2.0 %pack.3 = (bf16[16,4224]{1,0:T(8,128)(2,1)S(1)}, bf16[16,4224]{1,0:T(8,128)(2,1)S(1)}, bf16[16,4224]{1,0:T(8,128)(2,1)S(1)}, bf16[16,4224]{1,0:T(8,128)(2,1)S(1)}) custom-call(s32[32]{0:T(128)S(1)} %sub.3.refs_0_, bf16[32,80,256]{2,1,0:T(8,128)(2,1)S(1)} %all-to-all-done.refs_1_), custom_call_target="tpu_custom_call" | custom-call | tf_op jit(solution)/shard_map/pack/pallas_call | solution.py:180
  54.1 1.5 %collective-permute-start.11 = (bf16[16,4224]{1,0:T(8,128)(2,1)S(1)}, bf16[16,4224]{1,0:T(8,128)(2,1)S(1)}, u32[]{:S(2)}, u32[]{:S(2)}) collective-permute-start(bf16[16,4224]{1,0:T(8,128)(2,1)S(1)} %get-tuple-element.34), channel_id=1, source_target_pairs={{0,8},{8,0},{16,24},{24,16},{1,9},{9,1},{17,25},{25,17},{2,10},{10... | collective-permute-start | bytes 405512 | tf_op jit(solution)/shard_map/ppermute | solution.py:252
  55.6 1.2 collective-permute-start.15
  56.8 1.8 %collective-permute-start.19 = (bf16[16,4224]{1,0:T(8,128)(2,1)S(1)}, bf16[16,4224]{1,0:T(8,128)(2,1)S(1)}, u32[]{:S(2)}, u32[]{:S(2)}) collective-permute-start(bf16[16,4224]{1,0:T(8,128)(2,1)S(1)} %get-tuple-element.38), channel_id=1, source_target_pairs={{0,24},{8,16},{16,8},{24,0},{1,25},{9,17},{17,9},{25,1},{2,26},{10... | collective-permute-start | bytes 405512 | tf_op jit(solution)/shard_map/ppermute | solution.py:252
  58.6 1.8 %collective-permute-start.23 = (bf16[16,4224]{1,0:T(8,128)(2,1)S(1)}, bf16[16,4224]{1,0:T(8,128)(2,1)S(1)}, u32[]{:S(2)}, u32[]{:S(2)}) collective-permute-start(bf16[16,4224]{1,0:T(8,128)(2,1)S(1)} %get-tuple-element.40), channel_id=1, source_target_pairs={{0,96},{32,64},{64,32},{96,0},{1,97},{33,65},{65,33},{97,1},{2,98}... | collective-permute-start | bytes 405512 | tf_op jit(solution)/shard_map/ppermute | solution.py:252
  60.4 7.7 %all-to-all-done.1.refs_1_ = bf16[32,64,256]{2,1,0:T(8,128)(2,1)S(1)} async-done(((bf16[32,64,256]{2,1,0:T(8,128)(2,1)}), bf16[32,64,256]{2,1,0:T(8,128)(2,1)S(1)}, u32[]{:S(2)}, u32[]{:S(2)}) %all-to-all-start.1) | async-done | bytes 1048608 | tf_op jit(solution)/shard_map/all_to_all | solution.py:272
  68.1 2.0 %pack.2 = (bf16[32,4224]{1,0:T(8,128)(2,1)S(1)}, bf16[32,4224]{1,0:T(8,128)(2,1)S(1)}) custom-call(s32[32]{0:T(128)S(1)} %sub.3.refs_0_, bf16[32,64,256]{2,1,0:T(8,128)(2,1)S(1)} %all-to-all-done.1.refs_1_), custom_call_target="tpu_custom_call" | custom-call | tf_op jit(solution)/shard_map/pack/pallas_call | solution.py:180
  70.2 2.8 %collective-permute-start.8 = (bf16[32,4224]{1,0:T(8,128)(2,1)S(1)}, bf16[32,4224]{1,0:T(8,128)(2,1)S(1)}, u32[]{:S(2)}, u32[]{:S(2)}) collective-permute-start(bf16[32,4224]{1,0:T(8,128)(2,1)S(1)} %get-tuple-element.33), channel_id=1, source_target_pairs={{0,3},{1,2},{2,1},{3,0},{4,7},{5,6},{6,5},{7,4},{8,11},{9,10},{10,... | collective-permute-start | bytes 811016 | tf_op jit(solution)/shard_map/ppermute | solution.py:252
  73.3 2.0 %collective-permute-start.16 = (bf16[32,4224]{1,0:T(8,128)(2,1)S(1)}, bf16[32,4224]{1,0:T(8,128)(2,1)S(1)}, u32[]{:S(2)}, u32[]{:S(2)}) collective-permute-start(bf16[32,4224]{1,0:T(8,128)(2,1)S(1)} %pad_maximum_fusion.16), channel_id=1, source_target_pairs={{0,24},{8,16},{16,8},{24,0},{1,25},{9,17},{17,9},{25,1},{2,26},{10... | collective-permute-start | bytes 811016 | tf_op jit(solution)/shard_map/ppermute | solution.py:252
  75.3 0.6 collective-permute-start.20
  76.0 2.1 %collective-permute-done.6 = bf16[32,4224]{1,0:T(8,128)(2,1)S(1)} collective-permute-done((bf16[32,4224]{1,0:T(8,128)(2,1)S(1)}, bf16[32,4224]{1,0:T(8,128)(2,1)S(1)}, u32[]{:S(2)}, u32[]{:S(2)}) %collective-permute-start.6) | collective-permute-done | bytes 270368 | tf_op jit(solution)/shard_map/ppermute | solution.py:252
  78.5 1.0 collective-permute-done.8
  79.4 2.7 %collective-permute-start.7 = (bf16[64,4224]{1,0:T(8,128)(2,1)S(1)}, bf16[64,4224]{1,0:T(8,128)(2,1)S(1)}, u32[]{:S(2)}, u32[]{:S(2)}) collective-permute-start(bf16[64,4224]{1,0:T(8,128)(2,1)S(1)} %pad_maximum_fusion.9), channel_id=1, source_target_pairs={{0,3},{1,2},{2,1},{3,0},{4,7},{5,6},{6,5},{7,4},{8,11},{9,10},{10,... | collective-permute-start | bytes 1622024 | tf_op jit(solution)/shard_map/ppermute | solution.py:252
  82.5 2.2 %collective-permute-start.13 = (bf16[64,4224]{1,0:T(8,128)(2,1)S(1)}, bf16[64,4224]{1,0:T(8,128)(2,1)S(1)}, u32[]{:S(2)}, u32[]{:S(2)}) collective-permute-start(bf16[64,4224]{1,0:T(8,128)(2,1)S(1)} %pad_maximum_fusion.11), channel_id=1, source_target_pairs={{0,24},{8,16},{16,8},{24,0},{1,25},{9,17},{17,9},{25,1},{2,26},{10... | collective-permute-start | bytes 1622024 | tf_op jit(solution)/shard_map/ppermute | solution.py:252
  84.8 1.0 collective-permute-start.17
  86.2 7.3 %collective-permute-done.7 = bf16[64,4224]{1,0:T(8,128)(2,1)S(1)} collective-permute-done((bf16[64,4224]{1,0:T(8,128)(2,1)S(1)}, bf16[64,4224]{1,0:T(8,128)(2,1)S(1)}, u32[]{:S(2)}, u32[]{:S(2)}) %collective-permute-start.7) | collective-permute-done | bytes 540704 | tf_op jit(solution)/shard_map/ppermute | solution.py:252
  93.4 0.9 collective-permute-start.25
  95.3 2.5 %collective-permute-start.10 = (bf16[256,4224]{1,0:T(8,128)(2,1)S(1)}, bf16[256,4224]{1,0:T(8,128)(2,1)S(1)}, u32[]{:S(2)}, u32[]{:S(2)}) collective-permute-start(bf16[256,4224]{1,0:T(8,128)(2,1)S(1)} %pad_maximum_fusion), channel_id=1, source_target_pairs={{0,4},{4,0},{1,5},{5,1},{2,6},{6,2},{3,7},{7,3},{8,12},{12,8},{9,1... | collective-permute-start | bytes 6488072 | tf_op jit(solution)/shard_map/ppermute | solution.py:248
  99.2 0.8 collective-permute-start.18
  100.5 4.8 %collective-permute-done.25 = bf16[64,4224]{1,0:T(8,128)(2,1)S(1)} collective-permute-done((bf16[64,4224]{1,0:T(8,128)(2,1)S(1)}, bf16[64,4224]{1,0:T(8,128)(2,1)S(1)}, u32[]{:S(2)}, u32[]{:S(2)}) %collective-permute-start.25) | collective-permute-done | bytes 540704 | tf_op jit(solution)/shard_map/ppermute | solution.py:252
  105.6 4.0 %collective-permute-start.26 = (bf16[128,4224]{1,0:T(8,128)(2,1)S(1)}, bf16[128,4224]{1,0:T(8,128)(2,1)S(1)}, u32[]{:S(2)}, u32[]{:S(2)}) collective-permute-start(bf16[128,4224]{1,0:T(8,128)(2,1)S(1)} %pad_maximum_fusion.8), channel_id=1, source_target_pairs={{0,24},{8,16},{16,8},{24,0},{1,25},{9,17},{17,9},{25,1},{2,26},{10... | collective-permute-start | bytes 3244040 | tf_op jit(solution)/shard_map/ppermute | solution.py:252
  109.6 14.5 %collective-permute-done.14 = bf16[128,4224]{1,0:T(8,128)(2,1)S(1)} collective-permute-done((bf16[128,4224]{1,0:T(8,128)(2,1)S(1)}, bf16[128,4224]{1,0:T(8,128)(2,1)S(1)}, u32[]{:S(2)}, u32[]{:S(2)}) %collective-permute-start.14) | collective-permute-done | bytes 1081376 | tf_op jit(solution)/shard_map/ppermute | solution.py:252
  125.0 3.5 %collective-permute-done.22 = bf16[128,4224]{1,0:T(8,128)(2,1)S(1)} collective-permute-done((bf16[128,4224]{1,0:T(8,128)(2,1)S(1)}, bf16[128,4224]{1,0:T(8,128)(2,1)S(1)}, u32[]{:S(2)}, u32[]{:S(2)}) %collective-permute-start.22) | collective-permute-done | bytes 1081376 | tf_op jit(solution)/shard_map/ppermute | solution.py:252
  130.5 1.3 gram.4
  131.8 1.3 gram.5
  133.1 1.3 gram.6
  134.4 1.3 gram.7
  135.7 4.8 %collective-permute-start.27 = (f32[264,256]{1,0:T(8,128)S(1)}, f32[264,256]{1,0:T(8,128)S(1)}, u32[]{:S(2)}, u32[]{:S(2)}) collective-permute-start(f32[264,256]{1,0:T(8,128)S(1)} %get-tuple-element.42), channel_id=1, source_target_pairs={{0,4},{4,0},{1,5},{5,1},{2,6},{6,2},{3,7},{7,3},{8,12},{12,8},{9,1... | collective-permute-start | bytes 811016 | tf_op jit(solution)/shard_map/ppermute | solution.py:248
  142.8 2.2 %finish.1 = (f32[1,2048]{1,0:T(1,128)}, f32[256,2048]{1,0:T(8,128)}) custom-call(s32[3]{0:T(128)S(1)} %pad_add_fusion.info_ref, f32[1]{0:T(128)} %bitcast.6.part_ref, f32[264,256]{1,0:T(8,128)S(1)} %get-tuple-element.35.refs_0_, f32[264,256]{1,0:T(8,128)S(1)} %get-tuple-element.37.refs_1_, f32[264,256]{1,0:T(8,128)S(1)} %get-tuple-element.39.refs_2_, ...), custom_call_target="tpu_custom_call" | custom-call | tf_op jit(solution)/shard_map/finish/pallas_call | solution.py:234
  (87 shorter events, 9.9 us)
Async XLA Ops:
  0.6 1.6 %copy-start = (bf16[512,2048]{1,0:T(8,128)(2,1)S(1)}, bf16[512,2048]{1,0:T(8,128)(2,1)}, u32[]{:S(2)}) copy-start(bf16[512,2048]{1,0:T(8,128)(2,1)} %resid_ref.1) | copy-start | bytes 6291460
  2.2 0.7 copy-start.1
  2.9 0.7 copy-start.3
  3.6 6.2 %copy-start.4 = (f32[2048]{0:T(1024)S(1)}, f32[2048]{0:T(1024)}, u32[]{:S(2)}) copy-start(f32[2048]{0:T(1024)} %param.5) | copy-start | bytes 24580
  3.6 9.9 %copy-start.2 = (s32[2]{0:T(128)S(1)}, s32[2]{0:T(128)}, u32[]{:S(2)}) copy-start(s32[2]{0:T(128)} %counts_ref.3) | copy-start | bytes 28
  4.9 5.2 %collective-permute-start = (f32[8,256]{1,0:T(8,128)S(1)}, f32[8,256]{1,0:T(8,128)S(1)}, u32[]{:S(2)}, u32[]{:S(2)}) collective-permute-start(f32[8,256]{1,0:T(8,128)S(1)} %get-tuple-element.26.s0), channel_id=1, source_target_pairs={{0,1},{1,0},{2,3},{3,2},{4,5},{5,4},{6,7},{7,6},{8,9},{9,8},{10,11... | collective-permute-start | bytes 24584 | tf_op jit(solution)/shard_map/ppermute | solution.py:252
  7.1 4.0 %collective-permute-start.1 = (f32[8,256]{1,0:T(8,128)S(1)}, f32[8,256]{1,0:T(8,128)S(1)}, u32[]{:S(2)}, u32[]{:S(2)}) collective-permute-start(f32[8,256]{1,0:T(8,128)S(1)} %get-tuple-element.26.s0), channel_id=1, source_target_pairs={{0,2},{1,3},{2,0},{3,1},{4,6},{5,7},{6,4},{7,5},{8,10},{9,11},{10,... | collective-permute-start | bytes 24584 | tf_op jit(solution)/shard_map/ppermute | solution.py:252
  9.7 3.7 %collective-permute-start.2 = (f32[8,256]{1,0:T(8,128)S(1)}, f32[8,256]{1,0:T(8,128)S(1)}, u32[]{:S(2)}, u32[]{:S(2)}) collective-permute-start(f32[8,256]{1,0:T(8,128)S(1)} %get-tuple-element.26.s0), channel_id=1, source_target_pairs={{0,3},{1,2},{2,1},{3,0},{4,7},{5,6},{6,5},{7,4},{8,11},{9,10},{10,... | collective-permute-start | bytes 24584 | tf_op jit(solution)/shard_map/ppermute | solution.py:252
  15.5 29.4 %all-to-all-start = ((bf16[32,80,256]{2,1,0:T(8,128)(2,1)}), bf16[32,80,256]{2,1,0:T(8,128)(2,1)S(1)}, u32[]{:S(2)}, u32[]{:S(2)}) async-start(bf16[32,80,256]{2,1,0:T(8,128)(2,1)} %get-tuple-element.27), calls=%async_computation | async-start | bytes 2621440 | tf_op jit(solution)/shard_map/all_to_all | solution.py:270
  25.8 7.8 %collective-permute-start.3 = (bf16[8,64,256]{2,1,0:T(8,128)(2,1)S(1)}, bf16[8,64,256]{2,1,0:T(8,128)(2,1)S(1)}, u32[]{:S(2)}, u32[]{:S(2)}) collective-permute-start(bf16[8,64,256]{2,1,0:T(8,128)(2,1)S(1)} %get-tuple-element.29), channel_id=1, source_target_pairs={{0,1},{1,0},{2,3},{3,2},{4,5},{5,4},{6,7},{7,6},{8,9},{9,8},{10,11... | collective-permute-start | bytes 786440 | tf_op jit(solution)/shard_map/ppermute | solution.py:252
  25.9 13.0 %collective-permute-start.4 = (bf16[8,64,256]{2,1,0:T(8,128)(2,1)S(1)}, bf16[8,64,256]{2,1,0:T(8,128)(2,1)S(1)}, u32[]{:S(2)}, u32[]{:S(2)}) collective-permute-start(bf16[8,64,256]{2,1,0:T(8,128)(2,1)S(1)} %get-tuple-element.30), channel_id=1, source_target_pairs={{0,2},{1,3},{2,0},{3,1},{4,6},{5,7},{6,4},{7,5},{8,10},{9,11},{10,... | collective-permute-start | bytes 786440 | tf_op jit(solution)/shard_map/ppermute | solution.py:252
  27.0 14.0 %collective-permute-start.5 = (bf16[8,64,256]{2,1,0:T(8,128)(2,1)S(1)}, bf16[8,64,256]{2,1,0:T(8,128)(2,1)S(1)}, u32[]{:S(2)}, u32[]{:S(2)}) collective-permute-start(bf16[8,64,256]{2,1,0:T(8,128)(2,1)S(1)} %get-tuple-element.31), channel_id=1, source_target_pairs={{0,3},{1,2},{2,1},{3,0},{4,7},{5,6},{6,5},{7,4},{8,11},{9,10},{10,... | collective-permute-start | bytes 786440 | tf_op jit(solution)/shard_map/ppermute | solution.py:252
  44.9 23.2 %all-to-all-start.1 = ((bf16[32,64,256]{2,1,0:T(8,128)(2,1)}), bf16[32,64,256]{2,1,0:T(8,128)(2,1)S(1)}, u32[]{:S(2)}, u32[]{:S(2)}) async-start(bf16[32,64,256]{2,1,0:T(8,128)(2,1)} %order.1), calls=%async_computation.1 | async-start | bytes 2097152 | tf_op jit(solution)/shard_map/all_to_all | solution.py:272
  54.1 16.1 %collective-permute-start.11 = (bf16[16,4224]{1,0:T(8,128)(2,1)S(1)}, bf16[16,4224]{1,0:T(8,128)(2,1)S(1)}, u32[]{:S(2)}, u32[]{:S(2)}) collective-permute-start(bf16[16,4224]{1,0:T(8,128)(2,1)S(1)} %get-tuple-element.34), channel_id=1, source_target_pairs={{0,8},{8,0},{16,24},{24,16},{1,9},{9,1},{17,25},{25,17},{2,10},{10... | collective-permute-start | bytes 405512 | tf_op jit(solution)/shard_map/ppermute | solution.py:252
  55.6 17.5 %collective-permute-start.15 = (bf16[16,4224]{1,0:T(8,128)(2,1)S(1)}, bf16[16,4224]{1,0:T(8,128)(2,1)S(1)}, u32[]{:S(2)}, u32[]{:S(2)}) collective-permute-start(bf16[16,4224]{1,0:T(8,128)(2,1)S(1)} %get-tuple-element.36), channel_id=1, source_target_pairs={{0,32},{32,0},{64,96},{96,64},{1,33},{33,1},{65,97},{97,65},{2,34}... | collective-permute-start | bytes 405512 | tf_op jit(solution)/shard_map/ppermute | solution.py:252
  56.8 16.4 %collective-permute-start.19 = (bf16[16,4224]{1,0:T(8,128)(2,1)S(1)}, bf16[16,4224]{1,0:T(8,128)(2,1)S(1)}, u32[]{:S(2)}, u32[]{:S(2)}) collective-permute-start(bf16[16,4224]{1,0:T(8,128)(2,1)S(1)} %get-tuple-element.38), channel_id=1, source_target_pairs={{0,24},{8,16},{16,8},{24,0},{1,25},{9,17},{17,9},{25,1},{2,26},{10... | collective-permute-start | bytes 405512 | tf_op jit(solution)/shard_map/ppermute | solution.py:252
  58.6 16.7 %collective-permute-start.23 = (bf16[16,4224]{1,0:T(8,128)(2,1)S(1)}, bf16[16,4224]{1,0:T(8,128)(2,1)S(1)}, u32[]{:S(2)}, u32[]{:S(2)}) collective-permute-start(bf16[16,4224]{1,0:T(8,128)(2,1)S(1)} %get-tuple-element.40), channel_id=1, source_target_pairs={{0,96},{32,64},{64,32},{96,0},{1,97},{33,65},{65,33},{97,1},{2,98}... | collective-permute-start | bytes 405512 | tf_op jit(solution)/shard_map/ppermute | solution.py:252
  70.1 8.0 %collective-permute-start.6 = (bf16[32,4224]{1,0:T(8,128)(2,1)S(1)}, bf16[32,4224]{1,0:T(8,128)(2,1)S(1)}, u32[]{:S(2)}, u32[]{:S(2)}) collective-permute-start(bf16[32,4224]{1,0:T(8,128)(2,1)S(1)} %get-tuple-element.32), channel_id=1, source_target_pairs={{0,1},{1,0},{2,3},{3,2},{4,5},{5,4},{6,7},{7,6},{8,9},{9,8},{10,11... | collective-permute-start | bytes 811016 | tf_op jit(solution)/shard_map/ppermute | solution.py:252
  70.2 9.2 %collective-permute-start.8 = (bf16[32,4224]{1,0:T(8,128)(2,1)S(1)}, bf16[32,4224]{1,0:T(8,128)(2,1)S(1)}, u32[]{:S(2)}, u32[]{:S(2)}) collective-permute-start(bf16[32,4224]{1,0:T(8,128)(2,1)S(1)} %get-tuple-element.33), channel_id=1, source_target_pairs={{0,3},{1,2},{2,1},{3,0},{4,7},{5,6},{6,5},{7,4},{8,11},{9,10},{10,... | collective-permute-start | bytes 811016 | tf_op jit(solution)/shard_map/ppermute | solution.py:252
  73.1 9.1 %collective-permute-start.12 = (bf16[32,4224]{1,0:T(8,128)(2,1)S(1)}, bf16[32,4224]{1,0:T(8,128)(2,1)S(1)}, u32[]{:S(2)}, u32[]{:S(2)}) collective-permute-start(bf16[32,4224]{1,0:T(8,128)(2,1)S(1)} %pad_maximum_fusion.15), channel_id=1, source_target_pairs={{0,32},{32,0},{64,96},{96,64},{1,33},{33,1},{65,97},{97,65},{2,34}... | collective-permute-start | bytes 811016 | tf_op jit(solution)/shard_map/ppermute | solution.py:252
  73.3 9.2 %collective-permute-start.16 = (bf16[32,4224]{1,0:T(8,128)(2,1)S(1)}, bf16[32,4224]{1,0:T(8,128)(2,1)S(1)}, u32[]{:S(2)}, u32[]{:S(2)}) collective-permute-start(bf16[32,4224]{1,0:T(8,128)(2,1)S(1)} %pad_maximum_fusion.16), channel_id=1, source_target_pairs={{0,24},{8,16},{16,8},{24,0},{1,25},{9,17},{17,9},{25,1},{2,26},{10... | collective-permute-start | bytes 811016 | tf_op jit(solution)/shard_map/ppermute | solution.py:252
  75.3 9.5 %collective-permute-start.20 = (bf16[32,4224]{1,0:T(8,128)(2,1)S(1)}, bf16[32,4224]{1,0:T(8,128)(2,1)S(1)}, u32[]{:S(2)}, u32[]{:S(2)}) collective-permute-start(bf16[32,4224]{1,0:T(8,128)(2,1)S(1)} %pad_maximum_fusion.17), channel_id=1, source_target_pairs={{0,96},{32,64},{64,32},{96,0},{1,97},{33,65},{65,33},{97,1},{2,98}... | collective-permute-start | bytes 811016 | tf_op jit(solution)/shard_map/ppermute | solution.py:252
  78.1 7.8 %collective-permute-start.24 = (bf16[32,4224]{1,0:T(8,128)(2,1)S(1)}, bf16[32,4224]{1,0:T(8,128)(2,1)S(1)}, u32[]{:S(2)}, u32[]{:S(2)}) collective-permute-start(bf16[32,4224]{1,0:T(8,128)(2,1)S(1)} %pad_maximum_fusion.18), channel_id=1, source_target_pairs={{0,8},{8,0},{16,24},{24,16},{1,9},{9,1},{17,25},{25,17},{2,10},{10... | collective-permute-start | bytes 811016 | tf_op jit(solution)/shard_map/ppermute | solution.py:252
  79.4 14.0 %collective-permute-start.7 = (bf16[64,4224]{1,0:T(8,128)(2,1)S(1)}, bf16[64,4224]{1,0:T(8,128)(2,1)S(1)}, u32[]{:S(2)}, u32[]{:S(2)}) collective-permute-start(bf16[64,4224]{1,0:T(8,128)(2,1)S(1)} %pad_maximum_fusion.9), channel_id=1, source_target_pairs={{0,3},{1,2},{2,1},{3,0},{4,7},{5,6},{6,5},{7,4},{8,11},{9,10},{10,... | collective-permute-start | bytes 1622024 | tf_op jit(solution)/shard_map/ppermute | solution.py:252
  82.2 12.6 %collective-permute-start.9 = (bf16[64,4224]{1,0:T(8,128)(2,1)S(1)}, bf16[64,4224]{1,0:T(8,128)(2,1)S(1)}, u32[]{:S(2)}, u32[]{:S(2)}) collective-permute-start(bf16[64,4224]{1,0:T(8,128)(2,1)S(1)} %pad_maximum_fusion.10), channel_id=1, source_target_pairs={{0,1},{1,0},{2,3},{3,2},{4,5},{5,4},{6,7},{7,6},{8,9},{9,8},{10,11... | collective-permute-start | bytes 1622024 | tf_op jit(solution)/shard_map/ppermute | solution.py:252
  82.5 15.3 %collective-permute-start.13 = (bf16[64,4224]{1,0:T(8,128)(2,1)S(1)}, bf16[64,4224]{1,0:T(8,128)(2,1)S(1)}, u32[]{:S(2)}, u32[]{:S(2)}) collective-permute-start(bf16[64,4224]{1,0:T(8,128)(2,1)S(1)} %pad_maximum_fusion.11), channel_id=1, source_target_pairs={{0,24},{8,16},{16,8},{24,0},{1,25},{9,17},{17,9},{25,1},{2,26},{10... | collective-permute-start | bytes 1622024 | tf_op jit(solution)/shard_map/ppermute | solution.py:252
  84.8 14.1 %collective-permute-start.17 = (bf16[64,4224]{1,0:T(8,128)(2,1)S(1)}, bf16[64,4224]{1,0:T(8,128)(2,1)S(1)}, u32[]{:S(2)}, u32[]{:S(2)}) collective-permute-start(bf16[64,4224]{1,0:T(8,128)(2,1)S(1)} %pad_maximum_fusion.12), channel_id=1, source_target_pairs={{0,96},{32,64},{64,32},{96,0},{1,97},{33,65},{65,33},{97,1},{2,98}... | collective-permute-start | bytes 1622024 | tf_op jit(solution)/shard_map/ppermute | solution.py:252
  85.9 14.1 %collective-permute-start.21 = (bf16[64,4224]{1,0:T(8,128)(2,1)S(1)}, bf16[64,4224]{1,0:T(8,128)(2,1)S(1)}, u32[]{:S(2)}, u32[]{:S(2)}) collective-permute-start(bf16[64,4224]{1,0:T(8,128)(2,1)S(1)} %pad_maximum_fusion.13), channel_id=1, source_target_pairs={{0,8},{8,0},{16,24},{24,16},{1,9},{9,1},{17,25},{25,17},{2,10},{10... | collective-permute-start | bytes 1622024 | tf_op jit(solution)/shard_map/ppermute | solution.py:252
  93.4 11.9 %collective-permute-start.25 = (bf16[64,4224]{1,0:T(8,128)(2,1)S(1)}, bf16[64,4224]{1,0:T(8,128)(2,1)S(1)}, u32[]{:S(2)}, u32[]{:S(2)}) collective-permute-start(bf16[64,4224]{1,0:T(8,128)(2,1)S(1)} %pad_maximum_fusion.14), channel_id=1, source_target_pairs={{0,32},{32,0},{64,96},{96,64},{1,33},{33,1},{65,97},{97,65},{2,34}... | collective-permute-start | bytes 1622024 | tf_op jit(solution)/shard_map/ppermute | solution.py:252
  95.3 34.9 %collective-permute-start.10 = (bf16[256,4224]{1,0:T(8,128)(2,1)S(1)}, bf16[256,4224]{1,0:T(8,128)(2,1)S(1)}, u32[]{:S(2)}, u32[]{:S(2)}) collective-permute-start(bf16[256,4224]{1,0:T(8,128)(2,1)S(1)} %pad_maximum_fusion), channel_id=1, source_target_pairs={{0,4},{4,0},{1,5},{5,1},{2,6},{6,2},{3,7},{7,3},{8,12},{12,8},{9,1... | collective-permute-start | bytes 6488072 | tf_op jit(solution)/shard_map/ppermute | solution.py:248
  98.1 26.0 %collective-permute-start.14 = (bf16[128,4224]{1,0:T(8,128)(2,1)S(1)}, bf16[128,4224]{1,0:T(8,128)(2,1)S(1)}, u32[]{:S(2)}, u32[]{:S(2)}) collective-permute-start(bf16[128,4224]{1,0:T(8,128)(2,1)S(1)} %pad_maximum_fusion.5), channel_id=1, source_target_pairs={{0,96},{32,64},{64,32},{96,0},{1,97},{33,65},{65,33},{97,1},{2,98}... | collective-permute-start | bytes 3244040 | tf_op jit(solution)/shard_map/ppermute | solution.py:252
  99.2 25.4 %collective-permute-start.18 = (bf16[128,4224]{1,0:T(8,128)(2,1)S(1)}, bf16[128,4224]{1,0:T(8,128)(2,1)S(1)}, u32[]{:S(2)}, u32[]{:S(2)}) collective-permute-start(bf16[128,4224]{1,0:T(8,128)(2,1)S(1)} %pad_maximum_fusion.6), channel_id=1, source_target_pairs={{0,8},{8,0},{16,24},{24,16},{1,9},{9,1},{17,25},{25,17},{2,10},{10... | collective-permute-start | bytes 3244040 | tf_op jit(solution)/shard_map/ppermute | solution.py:252
  100.3 28.1 %collective-permute-start.22 = (bf16[128,4224]{1,0:T(8,128)(2,1)S(1)}, bf16[128,4224]{1,0:T(8,128)(2,1)S(1)}, u32[]{:S(2)}, u32[]{:S(2)}) collective-permute-start(bf16[128,4224]{1,0:T(8,128)(2,1)S(1)} %pad_maximum_fusion.7), channel_id=1, source_target_pairs={{0,32},{32,0},{64,96},{96,64},{1,33},{33,1},{65,97},{97,65},{2,34}... | collective-permute-start | bytes 3244040 | tf_op jit(solution)/shard_map/ppermute | solution.py:252
  105.6 24.1 %collective-permute-start.26 = (bf16[128,4224]{1,0:T(8,128)(2,1)S(1)}, bf16[128,4224]{1,0:T(8,128)(2,1)S(1)}, u32[]{:S(2)}, u32[]{:S(2)}) collective-permute-start(bf16[128,4224]{1,0:T(8,128)(2,1)S(1)} %pad_maximum_fusion.8), channel_id=1, source_target_pairs={{0,24},{8,16},{16,8},{24,0},{1,25},{9,17},{17,9},{25,1},{2,26},{10... | collective-permute-start | bytes 3244040 | tf_op jit(solution)/shard_map/ppermute | solution.py:252
  135.7 6.1 %collective-permute-start.27 = (f32[264,256]{1,0:T(8,128)S(1)}, f32[264,256]{1,0:T(8,128)S(1)}, u32[]{:S(2)}, u32[]{:S(2)}) collective-permute-start(f32[264,256]{1,0:T(8,128)S(1)} %get-tuple-element.42), channel_id=1, source_target_pairs={{0,4},{4,0},{1,5},{5,1},{2,6},{6,2},{3,7},{7,3},{8,12},{12,8},{9,1... | collective-permute-start | bytes 811016 | tf_op jit(solution)/shard_map/ppermute | solution.py:248
  140.5 1.6 %collective-permute-start.28 = (f32[264,256]{1,0:T(8,128)S(1)}, f32[264,256]{1,0:T(8,128)S(1)}, u32[]{:S(2)}, u32[]{:S(2)}) collective-permute-start(f32[264,256]{1,0:T(8,128)S(1)} %get-tuple-element.43), channel_id=1, source_target_pairs={{0,4},{4,0},{1,5},{5,1},{2,6},{6,2},{3,7},{7,3},{8,12},{12,8},{9,1... | collective-permute-start | bytes 811016 | tf_op jit(solution)/shard_map/ppermute | solution.py:248
  140.6 1.9 %collective-permute-start.29 = (f32[264,256]{1,0:T(8,128)S(1)}, f32[264,256]{1,0:T(8,128)S(1)}, u32[]{:S(2)}, u32[]{:S(2)}) collective-permute-start(f32[264,256]{1,0:T(8,128)S(1)} %get-tuple-element.44), channel_id=1, source_target_pairs={{0,4},{4,0},{1,5},{5,1},{2,6},{6,2},{3,7},{7,3},{8,12},{12,8},{9,1... | collective-permute-start | bytes 811016 | tf_op jit(solution)/shard_map/ppermute | solution.py:248
  141.0 1.8 %collective-permute-start.30 = (f32[264,256]{1,0:T(8,128)S(1)}, f32[264,256]{1,0:T(8,128)S(1)}, u32[]{:S(2)}, u32[]{:S(2)}) collective-permute-start(f32[264,256]{1,0:T(8,128)S(1)} %get-tuple-element.45), channel_id=1, source_target_pairs={{0,4},{4,0},{1,5},{5,1},{2,6},{6,2},{3,7},{7,3},{8,12},{12,8},{9,1... | collective-permute-start | bytes 811016 | tf_op jit(solution)/shard_map/ppermute | solution.py:248

commit v6 on v5

--- a/solution.py
+++ b/solution.py
@@ -30,7 +30,7 @@
     return jnp.where(place == 0, high, jnp.where(place == 1, middle, rest))
 
 
-def pick_kernel(index_ref, counts_ref, resid_ref, picked_ref, sums_ref):
+def pick_kernel(place_ref, index_ref, counts_ref, resid_ref, gain_ref, picked_ref, sums_ref, *turn_refs):
     tokens = resid_ref.shape[0]
     token = lax.broadcasted_iota(jnp.int32, (tokens, SLOTS), 0)
     slot = lax.broadcasted_iota(jnp.int32, (1, SLOTS), 1)
@@ -49,25 +49,34 @@
         )
         total += jnp.sum(part * part, axis=0, keepdims=True)
         picked_ref[k * step : (k + 1) * step, :] = part.astype(bf16)
-    sums_ref[...] = jnp.broadcast_to(total, sums_ref.shape)
-
-
-def pick(resid, keep_index, counts):
+    sums_ref[:8, :] = jnp.broadcast_to(total, (8, SLOTS))
+    sums_ref[8:, :] = gain_ref[...]
+    for flip, ref in zip((1, 2, 3), turn_refs):
+        first = pl.multiple_of((place_ref[0] ^ flip) * PIECE, PIECE)
+        for k in range(8):
+            ref[k] = picked_ref[pl.ds(k * 256 + first, PIECE), :]
+
+
+def pick(place, resid, gain, keep_index, counts):
+    vmem = pl.BlockSpec(memory_space=pltpu.VMEM)
+    smem = pl.BlockSpec(memory_space=pltpu.SMEM)
     return pl.pallas_call(
         pick_kernel,
         out_shape=(
             jax.ShapeDtypeStruct((WIDTH, SLOTS), bf16),
-            jax.ShapeDtypeStruct((8, SLOTS), f32),
-        ),
-        in_specs=[
-            pl.BlockSpec(memory_space=pltpu.VMEM),
-            pl.BlockSpec(memory_space=pltpu.SMEM),
-            pl.BlockSpec(memory_space=pltpu.VMEM),
-        ],
-        out_specs=(pl.BlockSpec(memory_space=pltpu.VMEM),) * 2,
+            jax.ShapeDtypeStruct((16, SLOTS), f32),
+        )
+        + (jax.ShapeDtypeStruct((8, PIECE, SLOTS), bf16),) * 3,
+        in_specs=[smem, vmem, smem, vmem, vmem],
+        out_specs=(vmem,) * 5,
         compiler_params=params(16),
         name="pick",
-    )(keep_index[None, :], counts, resid)
+    )(place, keep_index[None, :], counts, resid, gain)
+
+
+def scale_of(s0, s1, s2, s3):
+    squares = (s0[:1, :] + s2[:1, :]) + (s1[:1, :] + s3[:1, :])
+    return lax.rsqrt(squares / 8192 + epsilon)
 
 
 PARTNERS = (("x", 1), ("z", 1), ("x", 3), ("z", 3))
@@ -88,11 +97,8 @@
     return at
 
 
-def norm_kernel(place_ref, counts_ref, picked_ref, gain_ref, s0, s1, s2, s3, out_ref, *refs):
-    turn_refs, all_ref = refs[:4], refs[4]
-    squares = (s0[:1, :] + s2[:1, :]) + (s1[:1, :] + s3[:1, :])
-    scale = lax.rsqrt(squares / 8192 + epsilon)
-    y = place_ref[0]
+def norm_kernel(counts_ref, picked_ref, gain_ref, s0, s1, s2, s3, out_ref):
+    scale = scale_of(s0, s1, s2, s3)
     live = (counts_ref[0] + counts_ref[1]).astype(f32)
     extra = jnp.full((EXTRA, SLOTS), live, f32).astype(bf16)
     for s in range(4):
@@ -100,51 +106,49 @@
             first = (s * 2 + c) * 256
             rows = picked_ref[first : first + 256, :].astype(f32)
             short = (rows * scale * gain_ref[first : first + 256, :]).astype(bf16)
-            all_ref[first : first + 256, :] = short
             for z in range(4):
                 for x in range(4):
                     at = slot_of(s, x, z) * 16
                     out_ref[z * 8 + x * 2 + c, s * 16 : (s + 1) * 16, :] = short[at : at + 16, :]
     for t in range(32):
         out_ref[t, PIECE:, :] = extra
-    for flip, ref in enumerate(turn_refs):
-        q = y ^ flip
-        low = q * 32
-        high = 128 + (((q ^ (q >> 1)) & 1) * 2 + (q >> 1)) * 32
+
+
+def norm(counts, picked, gain, sums):
+    return pl.pallas_call(
+        norm_kernel,
+        out_shape=jax.ShapeDtypeStruct((32, PIECE + EXTRA, SLOTS), bf16),
+        in_specs=[pl.BlockSpec(memory_space=pltpu.SMEM)] + [pl.BlockSpec(memory_space=pltpu.VMEM)] * 6,
+        out_specs=pl.BlockSpec(memory_space=pltpu.VMEM),
+        compiler_params=params(10),
+        name="norm",
+    )(counts, picked, gain, *sums)
+
+
+def panel_kernel(place_ref, picked_ref, t1, t2, t3, s0, s1, s2, s3, out_ref, gain_ref):
+    scale = scale_of(s0, s1, s2, s3)
+    y = place_ref[0]
+    first = pl.multiple_of(y * PIECE, PIECE)
+    for flip, (turn, sums) in enumerate(((None, s0), (t1, s1), (t2, s2), (t3, s3))):
+        wide = jnp.concatenate([sums[8:, :], jnp.zeros((120, SLOTS), f32)], axis=0)
+        gain_ref[...] = wide.T
         for k in range(8):
-            ref[k, :32, :] = all_ref[pl.ds(pl.multiple_of(k * 256 + low, 32), 32), :]
-            ref[k, 32:, :] = all_ref[pl.ds(pl.multiple_of(k * 256 + high, 32), 32), :]
-
-
-def norm(place, counts, picked, gain, sums):
-    return pl.pallas_call(
-        norm_kernel,
-        out_shape=(jax.ShapeDtypeStruct((32, PIECE + EXTRA, SLOTS), bf16),)
-        + (jax.ShapeDtypeStruct((8, PIECE, SLOTS), bf16),) * 4,
-        in_specs=[pl.BlockSpec(memory_space=pltpu.SMEM)] * 2 + [pl.BlockSpec(memory_space=pltpu.VMEM)] * 6,
-        out_specs=(pl.BlockSpec(memory_space=pltpu.VMEM),) * 5,
-        scratch_shapes=[pltpu.VMEM((WIDTH, SLOTS), bf16)],
-        compiler_params=params(12),
-        name="norm",
-    )(place, counts, picked, gain, *sums)
-
-
-def order_kernel(place_ref, own_ref, a_ref, b_ref, c_ref, out_ref):
-    y = place_ref[0]
-    for k in range(8):
-        for flip, ref in enumerate((own_ref, a_ref, b_ref, c_ref)):
-            out_ref[(y ^ flip) * 8 + k] = ref[k]
-
-
-def order(place, blocks):
-    return pl.pallas_call(
-        order_kernel,
+            at = (y ^ flip) * 8 + k
+            rows = picked_ref[pl.ds(k * 256 + first, PIECE), :] if turn is None else turn[k]
+            gain = gain_ref[pl.ds(first, PIECE), :][:, k : k + 1]
+            out_ref[at] = (rows.astype(f32) * scale * gain).astype(bf16)
+
+
+def panel_pieces(place, picked, turns, sums):
+    return pl.pallas_call(
+        panel_kernel,
         out_shape=jax.ShapeDtypeStruct((32, PIECE, SLOTS), bf16),
-        in_specs=[pl.BlockSpec(memory_space=pltpu.SMEM)] + [pl.BlockSpec(memory_space=pltpu.VMEM)] * 4,
+        in_specs=[pl.BlockSpec(memory_space=pltpu.SMEM)] + [pl.BlockSpec(memory_space=pltpu.VMEM)] * 8,
         out_specs=pl.BlockSpec(memory_space=pltpu.VMEM),
-        compiler_params=params(8),
-        name="order",
-    )(place, *blocks)
+        scratch_shapes=[pltpu.VMEM((SLOTS, 128), f32)],
+        compiler_params=params(10),
+        name="panel",
+    )(place, picked, *turns, *sums)
 
 
 def pack_kernel(heights, first_ref, in_ref, *refs):
@@ -264,11 +268,12 @@
 def per_device(resid, norm_gain, keep_index, counts):
     z, x, c, y = (lax.axis_index(a) for a in ("z", "x", "c", "y"))
     place_y = y[None].astype(jnp.int32)
-    picked, sums = pick(resid, keep_index, counts)
+    picked, sums, *turns = pick(place_y, resid, norm_gain.reshape(8, SLOTS), keep_index, counts)
     all_sums = [sums] + [trade(sums, "y", flip) for flip in (1, 2, 3)]
-    normed, *turns = norm(place_y, counts, picked, norm_gain[:, None], all_sums)
+    turns = [trade(turn, "y", flip) for turn, flip in zip(turns, (1, 2, 3))]
+    normed = norm(counts, picked, norm_gain[:, None], all_sums)
     pieces = lax.all_to_all(normed, TOK, 0, 0, tiled=True)
-    panel = order(place_y, [turns[0]] + [trade(turns[flip], "y", flip) for flip in (1, 2, 3)])
+    panel = panel_pieces(place_y, picked, turns, all_sums)
     panel = lax.all_to_all(panel, TOK, 0, 0, tiled=True)
 
     loads = pieces[:, PIECE, 0].astype(jnp.int32)
@@ -282,11 +287,12 @@
             seen = [PARTNERS[(s + k) % 4][0] for k in range(step)]
             which = side(x if axis == "x" else z, flip, axis not in seen)
             streams[s] = meet(streams[s], axis, flip, which)
-
-    low, high = pack(first, panel, (32, 32))
-    low, high = meet(low, "y", 1, side(y, 1, True)), meet(high, "y", 3, side(y, 3, True))
-    low, high = meet(low, "y", 3, side(y, 3, False)), meet(high, "y", 1, side(y, 1, False))
-    rows = join(low, high)
+        if step == 0:
+            panel, _ = lax.optimization_barrier((panel, streams[3][:8, :128]))
+
+    (rows,) = pack(first, panel, (PIECE,))
+    rows = meet(rows, "y", 1, side(y, 1, True))
+    rows = meet(rows, "y", 3, side(y, 3, False))
     rows = join(rows, swap(rows))
 
     own, got = [], []

time: 145 us -> 140 us (0.966)
  starting transfers between devices: 57.2 us -> 51.3 us
    all_to_all x1, waiting for transfers between devices: 7.72 us -> 12.3 us  [per_device(): panel = lax.all_to_all(panel, TOK, 0, 0, tiled=True)]
    ppermute x26 -> x24, waiting for transfers between devices: 48.7 us -> 44.2 us  [trade(): return lax.ppermute(value, axis, [(i, i ^ flip) for i in range(4)])]
    ppermute x26 -> x24, starting transfers between devices: 33.2 us -> 28.8 us  [trade(): return lax.ppermute(value, axis, [(i, i ^ flip) for i in range(4)])]
    ppermute x5, starting transfers between devices: 7.85 us -> 5.78 us  [swap(): return lax.ppermute(value, 'c', [(0, 1), (1, 0)])]
  transfers between devices with their start and end apart: 33 -> 31, of which waited for: 19 -> 21; matrix products, arithmetic and copies ran while one was open for 5% -> 5% of each run, Pallas kernels for 4% -> 4%
where the time goes in v6:
time: 140 us
  waiting for transfers between devices  59.7 us (43%)
  starting transfers between devices  51.3 us (37%)
  Pallas kernels  16.4 us (12%)
  other arithmetic  6.7 us (5%)
  local copies, waits for them, and re-layouts  4.05 us (3%)
  between operations  1.61 us (1%)
    ppermute x24, waiting for transfers between devices, trade(): return lax.ppermute(value, axis, [(i, i ^ flip) for i in range(4)])  44.2 us
    ppermute x24, starting transfers between devices, trade(): return lax.ppermute(value, axis, [(i, i ^ flip) for i in range(4)])  28.8 us
    all_to_all x1, waiting for transfers between devices, per_device(): panel = lax.all_to_all(panel, TOK, 0, 0, tiled=True)  12.3 us
    all_to_all x1, starting transfers between devices, per_device(): pieces = lax.all_to_all(normed, TOK, 0, 0, tiled=True)  10.3 us
    all_to_all x1, starting transfers between devices, per_device(): panel = lax.all_to_all(panel, TOK, 0, 0, tiled=True)  6.46 us
    ppermute x5, starting transfers between devices, swap(): return lax.ppermute(value, 'c', [(0, 1), (1, 0)])  5.78 us
    pallas_call x4, Pallas kernels, gram(): pl.pallas_call(gram_kernel, out_shape=(jax.ShapeDtypeStruct((264, 256), f...  5.11 us
    pallas_call x2, Pallas kernels, pack(): pl.pallas_call(lambda *refs: pack_kernel(heights, *refs), out_shape=tuple...  4.07 us
  transfers between devices with their start and end apart: 31, of which 21 were waited for; matrix products, arithmetic and copies ran while one was open for 5% of the time, Pallas kernels for 4%

profile of v6, /device:TPU:1, one launch (start us, length us, event | category | flops | bytes accessed | tf_op | source)
XLA Modules:
  0.0 139.9 jit_solution(13156635519158206020)
XLA Ops:
  1.4 1.6 %copy-done = bf16[512,2048]{1,0:T(8,128)(2,1)S(1)} copy-done((bf16[512,2048]{1,0:T(8,128)(2,1)S(1)}, bf16[512,2048]{1,0:T(8,128)(2,1)}, u32[]{:S(2)}) %copy-start) | copy-done | bytes 2097176
  4.3 1.4 pick.1
  5.7 2.2 %collective-permute-start = (f32[16,256]{1,0:T(8,128)S(1)}, f32[16,256]{1,0:T(8,128)S(1)}, u32[]{:S(2)}, u32[]{:S(2)}) collective-permute-start(f32[16,256]{1,0:T(8,128)S(1)} %get-tuple-element.22.s0), channel_id=1, source_target_pairs={{0,1},{1,0},{2,3},{3,2},{4,5},{5,4},{6,7},{7,6},{8,9},{9,8},{10,11... | collective-permute-start | bytes 49160 | tf_op jit(solution)/shard_map/ppermute | solution.py:256
  7.9 2.6 %collective-permute-start.1 = (f32[16,256]{1,0:T(8,128)S(1)}, f32[16,256]{1,0:T(8,128)S(1)}, u32[]{:S(2)}, u32[]{:S(2)}) collective-permute-start(f32[16,256]{1,0:T(8,128)S(1)} %get-tuple-element.22.s0), channel_id=1, source_target_pairs={{0,2},{1,3},{2,0},{3,1},{4,6},{5,7},{6,4},{7,5},{8,10},{9,11},{10,... | collective-permute-start | bytes 49160 | tf_op jit(solution)/shard_map/ppermute | solution.py:256
  10.9 1.1 collective-permute-done.1.s2
  12.0 2.3 %collective-permute-done.2.s3 = f32[16,256]{1,0:T(8,128)S(1)} collective-permute-done((f32[16,256]{1,0:T(8,128)S(1)}, f32[16,256]{1,0:T(8,128)S(1)}, u32[]{:S(2)}, u32[]{:S(2)}) %collective-permute-start.2) | collective-permute-done | bytes 16416 | tf_op jit(solution)/shard_map/ppermute | solution.py:256
  14.4 1.9 %norm.1 = bf16[32,80,256]{2,1,0:T(8,128)(2,1)} custom-call(s32[2]{0:T(128)S(1)} %copy-done.2, bf16[2048,256]{1,0:T(8,128)(2,1)S(1)} %get-tuple-element.21.picked_ref, f32[2048,1]{1,0:T(8,128)S(1)} %copy.7.gain_ref, f32[16,256]{1,0:T(8,128)S(1)} %get-tuple-element.22.s0, f32[16,256]{1,0:T(8,128)S(1)} %collective-permute-done.s1, ...), custom_call_target="tpu_custom_call" | custom-call | tf_op jit(solution)/shard_map/norm/pallas_call | solution.py:118
  16.3 10.3 %all-to-all-start = ((bf16[32,80,256]{2,1,0:T(8,128)(2,1)}), bf16[32,80,256]{2,1,0:T(8,128)(2,1)S(1)}, u32[]{:S(2)}, u32[]{:S(2)}) async-start(bf16[32,80,256]{2,1,0:T(8,128)(2,1)} %norm.1), calls=%async_computation | async-start | bytes 2621440 | tf_op jit(solution)/shard_map/all_to_all | solution.py:275
  26.7 1.1 collective-permute-start.4
  27.8 2.7 %collective-permute-start.5 = (bf16[8,64,256]{2,1,0:T(8,128)(2,1)S(1)}, bf16[8,64,256]{2,1,0:T(8,128)(2,1)S(1)}, u32[]{:S(2)}, u32[]{:S(2)}) collective-permute-start(bf16[8,64,256]{2,1,0:T(8,128)(2,1)S(1)} %get-tuple-element.25), channel_id=1, source_target_pairs={{0,3},{1,2},{2,1},{3,0},{4,7},{5,6},{6,5},{7,4},{8,11},{9,10},{10,... | collective-permute-start | bytes 786440 | tf_op jit(solution)/shard_map/ppermute | solution.py:256
  30.6 3.8 %collective-permute-done.3.t1 = bf16[8,64,256]{2,1,0:T(8,128)(2,1)S(1)} collective-permute-done((bf16[8,64,256]{2,1,0:T(8,128)(2,1)S(1)}, bf16[8,64,256]{2,1,0:T(8,128)(2,1)S(1)}, u32[]{:S(2)}, u32[]{:S(2)}) %collective-permute-start.3) | collective-permute-done | bytes 262176 | tf_op jit(solution)/shard_map/ppermute | solution.py:256
  34.4 5.3 %collective-permute-done.4.t2 = bf16[8,64,256]{2,1,0:T(8,128)(2,1)S(1)} collective-permute-done((bf16[8,64,256]{2,1,0:T(8,128)(2,1)S(1)}, bf16[8,64,256]{2,1,0:T(8,128)(2,1)S(1)}, u32[]{:S(2)}, u32[]{:S(2)}) %collective-permute-start.4) | collective-permute-done | bytes 262176 | tf_op jit(solution)/shard_map/ppermute | solution.py:256
  39.7 2.1 %collective-permute-done.5.t3 = bf16[8,64,256]{2,1,0:T(8,128)(2,1)S(1)} collective-permute-done((bf16[8,64,256]{2,1,0:T(8,128)(2,1)S(1)}, bf16[8,64,256]{2,1,0:T(8,128)(2,1)S(1)}, u32[]{:S(2)}, u32[]{:S(2)}) %collective-permute-start.5) | collective-permute-done | bytes 262176 | tf_op jit(solution)/shard_map/ppermute | solution.py:256
  41.8 1.7 %panel.1 = bf16[32,64,256]{2,1,0:T(8,128)(2,1)} custom-call(s32[1]{0:T(128)} %bitcast.3.place_ref, bf16[2048,256]{1,0:T(8,128)(2,1)S(1)} %get-tuple-element.21.picked_ref, bf16[8,64,256]{2,1,0:T(8,128)(2,1)S(1)} %collective-permute-done.3.t1, bf16[8,64,256]{2,1,0:T(8,128)(2,1)S(1)} %collective-permute-done.4.t2, ...), custom_call_target="tpu_custom_call" | custom-call | tf_op jit(solution)/shard_map/panel/pallas_call | solution.py:143
  43.5 2.2 %all-to-all-done.refs_1_ = bf16[32,80,256]{2,1,0:T(8,128)(2,1)S(1)} async-done(((bf16[32,80,256]{2,1,0:T(8,128)(2,1)}), bf16[32,80,256]{2,1,0:T(8,128)(2,1)S(1)}, u32[]{:S(2)}, u32[]{:S(2)}) %all-to-all-start) | async-done | bytes 1310752 | tf_op jit(solution)/shard_map/all_to_all | solution.py:275
  45.7 6.5 %all-to-all-start.1 = ((bf16[32,64,256]{2,1,0:T(8,128)(2,1)}), bf16[32,64,256]{2,1,0:T(8,128)(2,1)S(1)}, u32[]{:S(2)}, u32[]{:S(2)}) async-start(bf16[32,64,256]{2,1,0:T(8,128)(2,1)} %panel.1), calls=%async_computation.1 | async-start | bytes 2097152 | tf_op jit(solution)/shard_map/all_to_all | solution.py:277
  52.4 1.2 fusion
  53.6 2.0 %pack.3 = (bf16[16,4224]{1,0:T(8,128)(2,1)S(1)}, bf16[16,4224]{1,0:T(8,128)(2,1)S(1)}, bf16[16,4224]{1,0:T(8,128)(2,1)S(1)}, bf16[16,4224]{1,0:T(8,128)(2,1)S(1)}) custom-call(s32[32]{0:T(128)S(1)} %sub.3.refs_0_, bf16[32,80,256]{2,1,0:T(8,128)(2,1)S(1)} %all-to-all-done.refs_1_), custom_call_target="tpu_custom_call" | custom-call | tf_op jit(solution)/shard_map/pack/pallas_call | solution.py:184
  55.6 1.5 %collective-permute-start.9 = (bf16[16,4224]{1,0:T(8,128)(2,1)S(1)}, bf16[16,4224]{1,0:T(8,128)(2,1)S(1)}, u32[]{:S(2)}, u32[]{:S(2)}) collective-permute-start(bf16[16,4224]{1,0:T(8,128)(2,1)S(1)} %get-tuple-element.26), channel_id=1, source_target_pairs={{0,8},{8,0},{16,24},{24,16},{1,9},{9,1},{17,25},{25,17},{2,10},{10... | collective-permute-start | bytes 405512 | tf_op jit(solution)/shard_map/ppermute | solution.py:256
  57.1 12.3 %all-to-all-done.1.refs_1_ = bf16[32,64,256]{2,1,0:T(8,128)(2,1)S(1)} async-done(((bf16[32,64,256]{2,1,0:T(8,128)(2,1)}), bf16[32,64,256]{2,1,0:T(8,128)(2,1)S(1)}, u32[]{:S(2)}, u32[]{:S(2)}) %all-to-all-start.1) | async-done | bytes 1048608 | tf_op jit(solution)/shard_map/all_to_all | solution.py:277
  69.3 2.0 %pack.2 = bf16[64,4224]{1,0:T(8,128)(2,1)S(1)} custom-call(s32[32]{0:T(128)S(1)} %sub.3.refs_0_, bf16[32,64,256]{2,1,0:T(8,128)(2,1)S(1)} %all-to-all-done.1.refs_1_), custom_call_target="tpu_custom_call" | custom-call | tf_op jit(solution)/shard_map/pack/pallas_call | solution.py:184
  71.6 2.1 %collective-permute-start.17 = (bf16[16,4224]{1,0:T(8,128)(2,1)S(1)}, bf16[16,4224]{1,0:T(8,128)(2,1)S(1)}, u32[]{:S(2)}, u32[]{:S(2)}) collective-permute-start(bf16[16,4224]{1,0:T(8,128)(2,1)S(1)} %get-tuple-element.30), channel_id=1, source_target_pairs={{0,24},{8,16},{16,8},{24,0},{1,25},{9,17},{17,9},{25,1},{2,26},{10... | collective-permute-start | bytes 405512 | tf_op jit(solution)/shard_map/ppermute | solution.py:256
  74.4 0.8 collective-permute-start.10
  75.2 1.1 collective-permute-done.13
  76.4 1.8 %collective-permute-start.14 = (bf16[32,4224]{1,0:T(8,128)(2,1)S(1)}, bf16[32,4224]{1,0:T(8,128)(2,1)S(1)}, u32[]{:S(2)}, u32[]{:S(2)}) collective-permute-start(bf16[32,4224]{1,0:T(8,128)(2,1)S(1)} %pad_maximum_fusion.16), channel_id=1, source_target_pairs={{0,24},{8,16},{16,8},{24,0},{1,25},{9,17},{17,9},{25,1},{2,26},{10... | collective-permute-start | bytes 811016 | tf_op jit(solution)/shard_map/ppermute | solution.py:256
  78.2 1.3 collective-permute-start.18
  80.5 1.7 %collective-permute-done.10 = bf16[32,4224]{1,0:T(8,128)(2,1)S(1)} collective-permute-done((bf16[32,4224]{1,0:T(8,128)(2,1)S(1)}, bf16[32,4224]{1,0:T(8,128)(2,1)S(1)}, u32[]{:S(2)}, u32[]{:S(2)}) %collective-permute-start.10) | collective-permute-done | bytes 270368 | tf_op jit(solution)/shard_map/ppermute | solution.py:256
  82.3 1.1 collective-permute-start.11
  83.5 1.0 collective-permute-done.14
  84.6 0.9 collective-permute-start.15
  85.5 1.4 %collective-permute-done.18 = bf16[32,4224]{1,0:T(8,128)(2,1)S(1)} collective-permute-done((bf16[32,4224]{1,0:T(8,128)(2,1)S(1)}, bf16[32,4224]{1,0:T(8,128)(2,1)S(1)}, u32[]{:S(2)}, u32[]{:S(2)}) %collective-permute-start.18) | collective-permute-done | bytes 270368 | tf_op jit(solution)/shard_map/ppermute | solution.py:256
  87.1 0.8 collective-permute-done.22
  88.4 2.8 %collective-permute-start.7 = (bf16[128,4224]{1,0:T(8,128)(2,1)S(1)}, bf16[128,4224]{1,0:T(8,128)(2,1)S(1)}, u32[]{:S(2)}, u32[]{:S(2)}) collective-permute-start(bf16[128,4224]{1,0:T(8,128)(2,1)S(1)} %pad_maximum_fusion.6), channel_id=1, source_target_pairs={{0,3},{1,2},{2,1},{3,0},{4,7},{5,6},{6,5},{7,4},{8,11},{9,10},{10,... | collective-permute-start | bytes 3244040 | tf_op jit(solution)/shard_map/ppermute | solution.py:256
  91.1 5.1 %collective-permute-done.11 = bf16[64,4224]{1,0:T(8,128)(2,1)S(1)} collective-permute-done((bf16[64,4224]{1,0:T(8,128)(2,1)S(1)}, bf16[64,4224]{1,0:T(8,128)(2,1)S(1)}, u32[]{:S(2)}, u32[]{:S(2)}) %collective-permute-start.11) | collective-permute-done | bytes 540704 | tf_op jit(solution)/shard_map/ppermute | solution.py:256
  96.5 2.9 %collective-permute-start.12 = (bf16[128,4224]{1,0:T(8,128)(2,1)S(1)}, bf16[128,4224]{1,0:T(8,128)(2,1)S(1)}, u32[]{:S(2)}, u32[]{:S(2)}) collective-permute-start(bf16[128,4224]{1,0:T(8,128)(2,1)S(1)} %pad_maximum_fusion.7), channel_id=1, source_target_pairs={{0,96},{32,64},{64,32},{96,0},{1,97},{33,65},{65,33},{97,1},{2,98}... | collective-permute-start | bytes 3244040 | tf_op jit(solution)/shard_map/ppermute | solution.py:256
  100.3 0.8 collective-permute-start.20
  101.4 2.7 %collective-permute-start.24 = (bf16[128,4224]{1,0:T(8,128)(2,1)S(1)}, bf16[128,4224]{1,0:T(8,128)(2,1)S(1)}, u32[]{:S(2)}, u32[]{:S(2)}) collective-permute-start(bf16[128,4224]{1,0:T(8,128)(2,1)S(1)} %pad_maximum_fusion.10), channel_id=1, source_target_pairs={{0,24},{8,16},{16,8},{24,0},{1,25},{9,17},{17,9},{25,1},{2,26},{10... | collective-permute-start | bytes 3244040 | tf_op jit(solution)/shard_map/ppermute | solution.py:256
  104.1 9.5 %collective-permute-done.7 = bf16[128,4224]{1,0:T(8,128)(2,1)S(1)} collective-permute-done((bf16[128,4224]{1,0:T(8,128)(2,1)S(1)}, bf16[128,4224]{1,0:T(8,128)(2,1)S(1)}, u32[]{:S(2)}, u32[]{:S(2)}) %collective-permute-start.7) | collective-permute-done | bytes 1081376 | tf_op jit(solution)/shard_map/ppermute | solution.py:256
  114.1 2.4 %collective-permute-start.8 = (bf16[256,4224]{1,0:T(8,128)(2,1)S(1)}, bf16[256,4224]{1,0:T(8,128)(2,1)S(1)}, u32[]{:S(2)}, u32[]{:S(2)}) collective-permute-start(bf16[256,4224]{1,0:T(8,128)(2,1)S(1)} %pad_maximum_fusion.1), channel_id=1, source_target_pairs={{0,4},{4,0},{1,5},{5,1},{2,6},{6,2},{3,7},{7,3},{8,12},{12,8},{9,1... | collective-permute-start | bytes 6488072 | tf_op jit(solution)/shard_map/ppermute | solution.py:252
  116.6 4.8 %collective-permute-done.12 = bf16[128,4224]{1,0:T(8,128)(2,1)S(1)} collective-permute-done((bf16[128,4224]{1,0:T(8,128)(2,1)S(1)}, bf16[128,4224]{1,0:T(8,128)(2,1)S(1)}, u32[]{:S(2)}, u32[]{:S(2)}) %collective-permute-start.12) | collective-permute-done | bytes 1081376 | tf_op jit(solution)/shard_map/ppermute | solution.py:256
  121.9 1.4 %collective-permute-done.16 = bf16[128,4224]{1,0:T(8,128)(2,1)S(1)} collective-permute-done((bf16[128,4224]{1,0:T(8,128)(2,1)S(1)}, bf16[128,4224]{1,0:T(8,128)(2,1)S(1)}, u32[]{:S(2)}, u32[]{:S(2)}) %collective-permute-start.16) | collective-permute-done | bytes 1081376 | tf_op jit(solution)/shard_map/ppermute | solution.py:256
  124.4 1.9 %collective-permute-done.24 = bf16[128,4224]{1,0:T(8,128)(2,1)S(1)} collective-permute-done((bf16[128,4224]{1,0:T(8,128)(2,1)S(1)}, bf16[128,4224]{1,0:T(8,128)(2,1)S(1)}, u32[]{:S(2)}, u32[]{:S(2)}) %collective-permute-start.24) | collective-permute-done | bytes 1081376 | tf_op jit(solution)/shard_map/ppermute | solution.py:256
  127.5 1.3 gram.4
  128.7 1.3 gram.5
  130.0 1.3 gram.6
  131.3 1.3 gram.7
  132.6 2.7 %collective-permute-start.25 = (f32[264,256]{1,0:T(8,128)S(1)}, f32[264,256]{1,0:T(8,128)S(1)}, u32[]{:S(2)}, u32[]{:S(2)}) collective-permute-start(f32[264,256]{1,0:T(8,128)S(1)} %get-tuple-element.34), channel_id=1, source_target_pairs={{0,4},{4,0},{1,5},{5,1},{2,6},{6,2},{3,7},{7,3},{8,12},{12,8},{9,1... | collective-permute-start | bytes 811016 | tf_op jit(solution)/shard_map/ppermute | solution.py:252
  137.7 2.2 %finish.1 = (f32[1,2048]{1,0:T(1,128)}, f32[256,2048]{1,0:T(8,128)}) custom-call(s32[3]{0:T(128)S(1)} %pad_add_fusion.info_ref, f32[1]{0:T(128)} %bitcast.6.part_ref, f32[264,256]{1,0:T(8,128)S(1)} %get-tuple-element.27.refs_0_, f32[264,256]{1,0:T(8,128)S(1)} %get-tuple-element.29.refs_1_, f32[264,256]{1,0:T(8,128)S(1)} %get-tuple-element.31.refs_2_, ...), custom_call_target="tpu_custom_call" | custom-call | tf_op jit(solution)/shard_map/finish/pallas_call | solution.py:238
  (79 shorter events, 11.9 us)
Async XLA Ops:
  0.6 9.9 %copy-start.4 = (f32[2048]{0:T(1024)S(1)}, f32[2048]{0:T(1024)}, u32[]{:S(2)}) copy-start(f32[2048]{0:T(1024)} %param.5) | copy-start | bytes 24580
  1.4 1.6 %copy-start = (bf16[512,2048]{1,0:T(8,128)(2,1)S(1)}, bf16[512,2048]{1,0:T(8,128)(2,1)}, u32[]{:S(2)}) copy-start(bf16[512,2048]{1,0:T(8,128)(2,1)} %resid_ref.1) | copy-start | bytes 6291460
  3.0 0.7 copy-start.1
  3.7 0.7 copy-start.3
  4.3 10.0 %copy-start.2 = (s32[2]{0:T(128)S(1)}, s32[2]{0:T(128)}, u32[]{:S(2)}) copy-start(s32[2]{0:T(128)} %counts_ref.3) | copy-start | bytes 28
  5.7 5.2 %collective-permute-start = (f32[16,256]{1,0:T(8,128)S(1)}, f32[16,256]{1,0:T(8,128)S(1)}, u32[]{:S(2)}, u32[]{:S(2)}) collective-permute-start(f32[16,256]{1,0:T(8,128)S(1)} %get-tuple-element.22.s0), channel_id=1, source_target_pairs={{0,1},{1,0},{2,3},{3,2},{4,5},{5,4},{6,7},{7,6},{8,9},{9,8},{10,11... | collective-permute-start | bytes 49160 | tf_op jit(solution)/shard_map/ppermute | solution.py:256
  7.9 4.1 %collective-permute-start.1 = (f32[16,256]{1,0:T(8,128)S(1)}, f32[16,256]{1,0:T(8,128)S(1)}, u32[]{:S(2)}, u32[]{:S(2)}) collective-permute-start(f32[16,256]{1,0:T(8,128)S(1)} %get-tuple-element.22.s0), channel_id=1, source_target_pairs={{0,2},{1,3},{2,0},{3,1},{4,6},{5,7},{6,4},{7,5},{8,10},{9,11},{10,... | collective-permute-start | bytes 49160 | tf_op jit(solution)/shard_map/ppermute | solution.py:256
  10.6 3.8 %collective-permute-start.2 = (f32[16,256]{1,0:T(8,128)S(1)}, f32[16,256]{1,0:T(8,128)S(1)}, u32[]{:S(2)}, u32[]{:S(2)}) collective-permute-start(f32[16,256]{1,0:T(8,128)S(1)} %get-tuple-element.22.s0), channel_id=1, source_target_pairs={{0,3},{1,2},{2,1},{3,0},{4,7},{5,6},{6,5},{7,4},{8,11},{9,10},{10,... | collective-permute-start | bytes 49160 | tf_op jit(solution)/shard_map/ppermute | solution.py:256
  16.3 29.4 %all-to-all-start = ((bf16[32,80,256]{2,1,0:T(8,128)(2,1)}), bf16[32,80,256]{2,1,0:T(8,128)(2,1)S(1)}, u32[]{:S(2)}, u32[]{:S(2)}) async-start(bf16[32,80,256]{2,1,0:T(8,128)(2,1)} %norm.1), calls=%async_computation | async-start | bytes 2621440 | tf_op jit(solution)/shard_map/all_to_all | solution.py:275
  26.6 7.8 %collective-permute-start.3 = (bf16[8,64,256]{2,1,0:T(8,128)(2,1)S(1)}, bf16[8,64,256]{2,1,0:T(8,128)(2,1)S(1)}, u32[]{:S(2)}, u32[]{:S(2)}) collective-permute-start(bf16[8,64,256]{2,1,0:T(8,128)(2,1)S(1)} %get-tuple-element.23), channel_id=1, source_target_pairs={{0,1},{1,0},{2,3},{3,2},{4,5},{5,4},{6,7},{7,6},{8,9},{9,8},{10,11... | collective-permute-start | bytes 786440 | tf_op jit(solution)/shard_map/ppermute | solution.py:256
  26.7 13.0 %collective-permute-start.4 = (bf16[8,64,256]{2,1,0:T(8,128)(2,1)S(1)}, bf16[8,64,256]{2,1,0:T(8,128)(2,1)S(1)}, u32[]{:S(2)}, u32[]{:S(2)}) collective-permute-start(bf16[8,64,256]{2,1,0:T(8,128)(2,1)S(1)} %get-tuple-element.24), channel_id=1, source_target_pairs={{0,2},{1,3},{2,0},{3,1},{4,6},{5,7},{6,4},{7,5},{8,10},{9,11},{10,... | collective-permute-start | bytes 786440 | tf_op jit(solution)/shard_map/ppermute | solution.py:256
  27.8 14.0 %collective-permute-start.5 = (bf16[8,64,256]{2,1,0:T(8,128)(2,1)S(1)}, bf16[8,64,256]{2,1,0:T(8,128)(2,1)S(1)}, u32[]{:S(2)}, u32[]{:S(2)}) collective-permute-start(bf16[8,64,256]{2,1,0:T(8,128)(2,1)S(1)} %get-tuple-element.25), channel_id=1, source_target_pairs={{0,3},{1,2},{2,1},{3,0},{4,7},{5,6},{6,5},{7,4},{8,11},{9,10},{10,... | collective-permute-start | bytes 786440 | tf_op jit(solution)/shard_map/ppermute | solution.py:256
  45.7 23.6 %all-to-all-start.1 = ((bf16[32,64,256]{2,1,0:T(8,128)(2,1)}), bf16[32,64,256]{2,1,0:T(8,128)(2,1)S(1)}, u32[]{:S(2)}, u32[]{:S(2)}) async-start(bf16[32,64,256]{2,1,0:T(8,128)(2,1)} %panel.1), calls=%async_computation.1 | async-start | bytes 2097152 | tf_op jit(solution)/shard_map/all_to_all | solution.py:277
  55.6 18.7 %collective-permute-start.9 = (bf16[16,4224]{1,0:T(8,128)(2,1)S(1)}, bf16[16,4224]{1,0:T(8,128)(2,1)S(1)}, u32[]{:S(2)}, u32[]{:S(2)}) collective-permute-start(bf16[16,4224]{1,0:T(8,128)(2,1)S(1)} %get-tuple-element.26), channel_id=1, source_target_pairs={{0,8},{8,0},{16,24},{24,16},{1,9},{9,1},{17,25},{25,17},{2,10},{10... | collective-permute-start | bytes 405512 | tf_op jit(solution)/shard_map/ppermute | solution.py:256
  71.4 16.8 %collective-permute-start.6 = (bf16[64,4224]{1,0:T(8,128)(2,1)S(1)}, bf16[64,4224]{1,0:T(8,128)(2,1)S(1)}, u32[]{:S(2)}, u32[]{:S(2)}) collective-permute-start(bf16[64,4224]{1,0:T(8,128)(2,1)S(1)} %pack.2), channel_id=1, source_target_pairs={{0,1},{1,0},{2,3},{3,2},{4,5},{5,4},{6,7},{7,6},{8,9},{9,8},{10,11... | collective-permute-start | bytes 1622024 | tf_op jit(solution)/shard_map/ppermute | solution.py:256
  71.5 4.9 %collective-permute-start.13 = (bf16[16,4224]{1,0:T(8,128)(2,1)S(1)}, bf16[16,4224]{1,0:T(8,128)(2,1)S(1)}, u32[]{:S(2)}, u32[]{:S(2)}) collective-permute-start(bf16[16,4224]{1,0:T(8,128)(2,1)S(1)} %get-tuple-element.28), channel_id=1, source_target_pairs={{0,32},{32,0},{64,96},{96,64},{1,33},{33,1},{65,97},{97,65},{2,34}... | collective-permute-start | bytes 405512 | tf_op jit(solution)/shard_map/ppermute | solution.py:256
  71.6 6.6 %collective-permute-start.17 = (bf16[16,4224]{1,0:T(8,128)(2,1)S(1)}, bf16[16,4224]{1,0:T(8,128)(2,1)S(1)}, u32[]{:S(2)}, u32[]{:S(2)}) collective-permute-start(bf16[16,4224]{1,0:T(8,128)(2,1)S(1)} %get-tuple-element.30), channel_id=1, source_target_pairs={{0,24},{8,16},{16,8},{24,0},{1,25},{9,17},{17,9},{25,1},{2,26},{10... | collective-permute-start | bytes 405512 | tf_op jit(solution)/shard_map/ppermute | solution.py:256
  73.7 6.6 %collective-permute-start.21 = (bf16[16,4224]{1,0:T(8,128)(2,1)S(1)}, bf16[16,4224]{1,0:T(8,128)(2,1)S(1)}, u32[]{:S(2)}, u32[]{:S(2)}) collective-permute-start(bf16[16,4224]{1,0:T(8,128)(2,1)S(1)} %get-tuple-element.32), channel_id=1, source_target_pairs={{0,96},{32,64},{64,32},{96,0},{1,97},{33,65},{65,33},{97,1},{2,98}... | collective-permute-start | bytes 405512 | tf_op jit(solution)/shard_map/ppermute | solution.py:256
  74.4 7.8 %collective-permute-start.10 = (bf16[32,4224]{1,0:T(8,128)(2,1)S(1)}, bf16[32,4224]{1,0:T(8,128)(2,1)S(1)}, u32[]{:S(2)}, u32[]{:S(2)}) collective-permute-start(bf16[32,4224]{1,0:T(8,128)(2,1)S(1)} %pad_maximum_fusion.15), channel_id=1, source_target_pairs={{0,32},{32,0},{64,96},{96,64},{1,33},{33,1},{65,97},{97,65},{2,34}... | collective-permute-start | bytes 811016 | tf_op jit(solution)/shard_map/ppermute | solution.py:256
  76.4 8.1 %collective-permute-start.14 = (bf16[32,4224]{1,0:T(8,128)(2,1)S(1)}, bf16[32,4224]{1,0:T(8,128)(2,1)S(1)}, u32[]{:S(2)}, u32[]{:S(2)}) collective-permute-start(bf16[32,4224]{1,0:T(8,128)(2,1)S(1)} %pad_maximum_fusion.16), channel_id=1, source_target_pairs={{0,24},{8,16},{16,8},{24,0},{1,25},{9,17},{17,9},{25,1},{2,26},{10... | collective-permute-start | bytes 811016 | tf_op jit(solution)/shard_map/ppermute | solution.py:256
  78.2 8.6 %collective-permute-start.18 = (bf16[32,4224]{1,0:T(8,128)(2,1)S(1)}, bf16[32,4224]{1,0:T(8,128)(2,1)S(1)}, u32[]{:S(2)}, u32[]{:S(2)}) collective-permute-start(bf16[32,4224]{1,0:T(8,128)(2,1)S(1)} %pad_maximum_fusion.17), channel_id=1, source_target_pairs={{0,96},{32,64},{64,32},{96,0},{1,97},{33,65},{65,33},{97,1},{2,98}... | collective-permute-start | bytes 811016 | tf_op jit(solution)/shard_map/ppermute | solution.py:256
  80.4 7.5 %collective-permute-start.22 = (bf16[32,4224]{1,0:T(8,128)(2,1)S(1)}, bf16[32,4224]{1,0:T(8,128)(2,1)S(1)}, u32[]{:S(2)}, u32[]{:S(2)}) collective-permute-start(bf16[32,4224]{1,0:T(8,128)(2,1)S(1)} %pad_maximum_fusion.18), channel_id=1, source_target_pairs={{0,8},{8,0},{16,24},{24,16},{1,9},{9,1},{17,25},{25,17},{2,10},{10... | collective-permute-start | bytes 811016 | tf_op jit(solution)/shard_map/ppermute | solution.py:256
  82.3 13.9 %collective-permute-start.11 = (bf16[64,4224]{1,0:T(8,128)(2,1)S(1)}, bf16[64,4224]{1,0:T(8,128)(2,1)S(1)}, u32[]{:S(2)}, u32[]{:S(2)}) collective-permute-start(bf16[64,4224]{1,0:T(8,128)(2,1)S(1)} %pad_maximum_fusion.11), channel_id=1, source_target_pairs={{0,24},{8,16},{16,8},{24,0},{1,25},{9,17},{17,9},{25,1},{2,26},{10... | collective-permute-start | bytes 1622024 | tf_op jit(solution)/shard_map/ppermute | solution.py:256
  84.6 14.8 %collective-permute-start.15 = (bf16[64,4224]{1,0:T(8,128)(2,1)S(1)}, bf16[64,4224]{1,0:T(8,128)(2,1)S(1)}, u32[]{:S(2)}, u32[]{:S(2)}) collective-permute-start(bf16[64,4224]{1,0:T(8,128)(2,1)S(1)} %pad_maximum_fusion.12), channel_id=1, source_target_pairs={{0,96},{32,64},{64,32},{96,0},{1,97},{33,65},{65,33},{97,1},{2,98}... | collective-permute-start | bytes 1622024 | tf_op jit(solution)/shard_map/ppermute | solution.py:256
  87.0 13.0 %collective-permute-start.19 = (bf16[64,4224]{1,0:T(8,128)(2,1)S(1)}, bf16[64,4224]{1,0:T(8,128)(2,1)S(1)}, u32[]{:S(2)}, u32[]{:S(2)}) collective-permute-start(bf16[64,4224]{1,0:T(8,128)(2,1)S(1)} %pad_maximum_fusion.13), channel_id=1, source_target_pairs={{0,8},{8,0},{16,24},{24,16},{1,9},{9,1},{17,25},{25,17},{2,10},{10... | collective-permute-start | bytes 1622024 | tf_op jit(solution)/shard_map/ppermute | solution.py:256
  88.1 13.0 %collective-permute-start.23 = (bf16[64,4224]{1,0:T(8,128)(2,1)S(1)}, bf16[64,4224]{1,0:T(8,128)(2,1)S(1)}, u32[]{:S(2)}, u32[]{:S(2)}) collective-permute-start(bf16[64,4224]{1,0:T(8,128)(2,1)S(1)} %pad_maximum_fusion.14), channel_id=1, source_target_pairs={{0,32},{32,0},{64,96},{96,64},{1,33},{33,1},{65,97},{97,65},{2,34}... | collective-permute-start | bytes 1622024 | tf_op jit(solution)/shard_map/ppermute | solution.py:256
  88.4 25.2 %collective-permute-start.7 = (bf16[128,4224]{1,0:T(8,128)(2,1)S(1)}, bf16[128,4224]{1,0:T(8,128)(2,1)S(1)}, u32[]{:S(2)}, u32[]{:S(2)}) collective-permute-start(bf16[128,4224]{1,0:T(8,128)(2,1)S(1)} %pad_maximum_fusion.6), channel_id=1, source_target_pairs={{0,3},{1,2},{2,1},{3,0},{4,7},{5,6},{6,5},{7,4},{8,11},{9,10},{10,... | collective-permute-start | bytes 3244040 | tf_op jit(solution)/shard_map/ppermute | solution.py:256
  96.5 24.9 %collective-permute-start.12 = (bf16[128,4224]{1,0:T(8,128)(2,1)S(1)}, bf16[128,4224]{1,0:T(8,128)(2,1)S(1)}, u32[]{:S(2)}, u32[]{:S(2)}) collective-permute-start(bf16[128,4224]{1,0:T(8,128)(2,1)S(1)} %pad_maximum_fusion.7), channel_id=1, source_target_pairs={{0,96},{32,64},{64,32},{96,0},{1,97},{33,65},{65,33},{97,1},{2,98}... | collective-permute-start | bytes 3244040 | tf_op jit(solution)/shard_map/ppermute | solution.py:256
  99.7 23.7 %collective-permute-start.16 = (bf16[128,4224]{1,0:T(8,128)(2,1)S(1)}, bf16[128,4224]{1,0:T(8,128)(2,1)S(1)}, u32[]{:S(2)}, u32[]{:S(2)}) collective-permute-start(bf16[128,4224]{1,0:T(8,128)(2,1)S(1)} %pad_maximum_fusion.8), channel_id=1, source_target_pairs={{0,8},{8,0},{16,24},{24,16},{1,9},{9,1},{17,25},{25,17},{2,10},{10... | collective-permute-start | bytes 3244040 | tf_op jit(solution)/shard_map/ppermute | solution.py:256
  100.3 23.5 %collective-permute-start.20 = (bf16[128,4224]{1,0:T(8,128)(2,1)S(1)}, bf16[128,4224]{1,0:T(8,128)(2,1)S(1)}, u32[]{:S(2)}, u32[]{:S(2)}) collective-permute-start(bf16[128,4224]{1,0:T(8,128)(2,1)S(1)} %pad_maximum_fusion.9), channel_id=1, source_target_pairs={{0,32},{32,0},{64,96},{96,64},{1,33},{33,1},{65,97},{97,65},{2,34}... | collective-permute-start | bytes 3244040 | tf_op jit(solution)/shard_map/ppermute | solution.py:256
  101.4 24.9 %collective-permute-start.24 = (bf16[128,4224]{1,0:T(8,128)(2,1)S(1)}, bf16[128,4224]{1,0:T(8,128)(2,1)S(1)}, u32[]{:S(2)}, u32[]{:S(2)}) collective-permute-start(bf16[128,4224]{1,0:T(8,128)(2,1)S(1)} %pad_maximum_fusion.10), channel_id=1, source_target_pairs={{0,24},{8,16},{16,8},{24,0},{1,25},{9,17},{17,9},{25,1},{2,26},{10... | collective-permute-start | bytes 3244040 | tf_op jit(solution)/shard_map/ppermute | solution.py:256
  114.1 12.7 %collective-permute-start.8 = (bf16[256,4224]{1,0:T(8,128)(2,1)S(1)}, bf16[256,4224]{1,0:T(8,128)(2,1)S(1)}, u32[]{:S(2)}, u32[]{:S(2)}) collective-permute-start(bf16[256,4224]{1,0:T(8,128)(2,1)S(1)} %pad_maximum_fusion.1), channel_id=1, source_target_pairs={{0,4},{4,0},{1,5},{5,1},{2,6},{6,2},{3,7},{7,3},{8,12},{12,8},{9,1... | collective-permute-start | bytes 6488072 | tf_op jit(solution)/shard_map/ppermute | solution.py:252
  132.6 4.0 %collective-permute-start.25 = (f32[264,256]{1,0:T(8,128)S(1)}, f32[264,256]{1,0:T(8,128)S(1)}, u32[]{:S(2)}, u32[]{:S(2)}) collective-permute-start(f32[264,256]{1,0:T(8,128)S(1)} %get-tuple-element.34), channel_id=1, source_target_pairs={{0,4},{4,0},{1,5},{5,1},{2,6},{6,2},{3,7},{7,3},{8,12},{12,8},{9,1... | collective-permute-start | bytes 811016 | tf_op jit(solution)/shard_map/ppermute | solution.py:252
  135.3 1.6 %collective-permute-start.26 = (f32[264,256]{1,0:T(8,128)S(1)}, f32[264,256]{1,0:T(8,128)S(1)}, u32[]{:S(2)}, u32[]{:S(2)}) collective-permute-start(f32[264,256]{1,0:T(8,128)S(1)} %get-tuple-element.35), channel_id=1, source_target_pairs={{0,4},{4,0},{1,5},{5,1},{2,6},{6,2},{3,7},{7,3},{8,12},{12,8},{9,1... | collective-permute-start | bytes 811016 | tf_op jit(solution)/shard_map/ppermute | solution.py:252
  135.4 1.9 %collective-permute-start.27 = (f32[264,256]{1,0:T(8,128)S(1)}, f32[264,256]{1,0:T(8,128)S(1)}, u32[]{:S(2)}, u32[]{:S(2)}) collective-permute-start(f32[264,256]{1,0:T(8,128)S(1)} %get-tuple-element.36), channel_id=1, source_target_pairs={{0,4},{4,0},{1,5},{5,1},{2,6},{6,2},{3,7},{7,3},{8,12},{12,8},{9,1... | collective-permute-start | bytes 811016 | tf_op jit(solution)/shard_map/ppermute | solution.py:252
  135.8 1.8 %collective-permute-start.28 = (f32[264,256]{1,0:T(8,128)S(1)}, f32[264,256]{1,0:T(8,128)S(1)}, u32[]{:S(2)}, u32[]{:S(2)}) collective-permute-start(f32[264,256]{1,0:T(8,128)S(1)} %get-tuple-element.37), channel_id=1, source_target_pairs={{0,4},{4,0},{1,5},{5,1},{2,6},{6,2},{3,7},{7,3},{8,12},{12,8},{9,1... | collective-permute-start | bytes 811016 | tf_op jit(solution)/shard_map/ppermute | solution.py:252

commit v7 on v6

--- a/solution.py
+++ b/solution.py
@@ -30,7 +30,22 @@
     return jnp.where(place == 0, high, jnp.where(place == 1, middle, rest))
 
 
-def pick_kernel(place_ref, index_ref, counts_ref, resid_ref, gain_ref, picked_ref, sums_ref, *turn_refs):
+def pick_kernel(place_ref, index_hbm, counts_hbm, resid_hbm, gain_ref, picked_ref, sums_ref, t1, t2, t3, *scratch):
+    index_ref, counts_ref, resid_ref, sem = scratch
+    step = 512
+    parts = [pl.ds(k * step, step) for k in range(WIDTH // step)]
+    small = [
+        pltpu.make_async_copy(index_hbm, index_ref, sem.at[0]),
+        pltpu.make_async_copy(counts_hbm, counts_ref, sem.at[1]),
+    ]
+    large = [
+        pltpu.make_async_copy(resid_hbm.at[:, part], resid_ref.at[:, part], sem.at[2 + k])
+        for k, part in enumerate(parts)
+    ]
+    for copy in small + large:
+        copy.start()
+    for copy in small:
+        copy.wait()
     tokens = resid_ref.shape[0]
     token = lax.broadcasted_iota(jnp.int32, (tokens, SLOTS), 0)
     slot = lax.broadcasted_iota(jnp.int32, (1, SLOTS), 1)
@@ -39,43 +54,55 @@
     kept = jnp.where(slot < end, index_ref[...], -1)
     one_hot = jnp.where(token == kept, 1.0, 0.0).astype(bf16)
     total = jnp.zeros((1, SLOTS), f32)
-    step = 512
-    for k in range(WIDTH // step):
-        part = lax.dot_general(
-            resid_ref[:, k * step : (k + 1) * step],
-            one_hot,
-            (((0,), (0,)), ((), ())),
-            preferred_element_type=f32,
+    for part, copy in zip(parts, large):
+        copy.wait()
+        product = lax.dot_general(
+            resid_ref[:, part], one_hot, (((0,), (0,)), ((), ())), preferred_element_type=f32
         )
-        total += jnp.sum(part * part, axis=0, keepdims=True)
-        picked_ref[k * step : (k + 1) * step, :] = part.astype(bf16)
-    sums_ref[:8, :] = jnp.broadcast_to(total, (8, SLOTS))
-    sums_ref[8:, :] = gain_ref[...]
-    for flip, ref in zip((1, 2, 3), turn_refs):
+        total += jnp.sum(product * product, axis=0, keepdims=True)
+        picked_ref[part, :] = product.astype(bf16)
+    sums_ref[...] = jnp.broadcast_to(total, (8, SLOTS))
+    row = lax.broadcasted_iota(jnp.int32, (EXTRA, SLOTS), 0)
+    sum_terms = spread(total, row)
+    for flip, ref in ((1, t1), (2, t2), (3, t3)):
         first = pl.multiple_of((place_ref[0] ^ flip) * PIECE, PIECE)
         for k in range(8):
-            ref[k] = picked_ref[pl.ds(k * 256 + first, PIECE), :]
+            ref[k, :PIECE, :] = picked_ref[pl.ds(k * 256 + first, PIECE), :]
+            terms = jnp.where(row < 3, sum_terms, spread(gain_ref[k : k + 1, :], row - 3))
+            ref[k, PIECE:, :] = terms.astype(bf16)
 
 
 def pick(place, resid, gain, keep_index, counts):
     vmem = pl.BlockSpec(memory_space=pltpu.VMEM)
     smem = pl.BlockSpec(memory_space=pltpu.SMEM)
+    hbm = pl.BlockSpec(memory_space=pl.ANY)
     return pl.pallas_call(
         pick_kernel,
         out_shape=(
             jax.ShapeDtypeStruct((WIDTH, SLOTS), bf16),
-            jax.ShapeDtypeStruct((16, SLOTS), f32),
+            jax.ShapeDtypeStruct((8, SLOTS), f32),
         )
-        + (jax.ShapeDtypeStruct((8, PIECE, SLOTS), bf16),) * 3,
-        in_specs=[smem, vmem, smem, vmem, vmem],
+        + (jax.ShapeDtypeStruct((8, PIECE + EXTRA, SLOTS), bf16),) * 3,
+        in_specs=[smem, hbm, hbm, hbm, vmem],
         out_specs=(vmem,) * 5,
+        scratch_shapes=[
+            pltpu.VMEM((1, SLOTS), jnp.int32),
+            pltpu.SMEM((2,), jnp.int32),
+            pltpu.VMEM((512, WIDTH), bf16),
+            pltpu.SemaphoreType.DMA((6,)),
+        ],
         compiler_params=params(16),
         name="pick",
     )(place, keep_index[None, :], counts, resid, gain)
 
 
-def scale_of(s0, s1, s2, s3):
-    squares = (s0[:1, :] + s2[:1, :]) + (s1[:1, :] + s3[:1, :])
+def whole_terms(ref, k, first):
+    terms = ref[k, PIECE:, :].astype(f32)
+    return terms[first : first + 1, :] + (terms[first + 1 : first + 2, :] + terms[first + 2 : first + 3, :])
+
+
+def scale_of(sums, t1, t2, t3):
+    squares = (sums[:1, :] + whole_terms(t2, 0, 0)) + (whole_terms(t1, 0, 0) + whole_terms(t3, 0, 0))
     return lax.rsqrt(squares / 8192 + epsilon)
 
 
@@ -97,8 +124,8 @@
     return at
 
 
-def norm_kernel(counts_ref, picked_ref, gain_ref, s0, s1, s2, s3, out_ref):
-    scale = scale_of(s0, s1, s2, s3)
+def norm_kernel(counts_ref, picked_ref, gain_ref, sums, t1, t2, t3, out_ref):
+    scale = scale_of(sums, t1, t2, t3)
     live = (counts_ref[0] + counts_ref[1]).astype(f32)
     extra = jnp.full((EXTRA, SLOTS), live, f32).astype(bf16)
     for s in range(4):
@@ -114,7 +141,7 @@
         out_ref[t, PIECE:, :] = extra
 
 
-def norm(counts, picked, gain, sums):
+def norm(counts, picked, gain, sums, turns):
     return pl.pallas_call(
         norm_kernel,
         out_shape=jax.ShapeDtypeStruct((32, PIECE + EXTRA, SLOTS), bf16),
@@ -122,33 +149,35 @@
         out_specs=pl.BlockSpec(memory_space=pltpu.VMEM),
         compiler_params=params(10),
         name="norm",
-    )(counts, picked, gain, *sums)
-
-
-def panel_kernel(place_ref, picked_ref, t1, t2, t3, s0, s1, s2, s3, out_ref, gain_ref):
-    scale = scale_of(s0, s1, s2, s3)
+    )(counts, picked, gain, sums, *turns)
+
+
+def panel_kernel(place_ref, picked_ref, own_gain_ref, sums, t1, t2, t3, out_ref, gain_ref):
+    scale = scale_of(sums, t1, t2, t3)
     y = place_ref[0]
     first = pl.multiple_of(y * PIECE, PIECE)
-    for flip, (turn, sums) in enumerate(((None, s0), (t1, s1), (t2, s2), (t3, s3))):
-        wide = jnp.concatenate([sums[8:, :], jnp.zeros((120, SLOTS), f32)], axis=0)
-        gain_ref[...] = wide.T
+    for flip, turn in enumerate((None, t1, t2, t3)):
+        if turn is None:
+            gains = own_gain_ref[...]
+        else:
+            gains = jnp.concatenate([whole_terms(turn, k, 3) for k in range(8)], axis=0)
+        gain_ref[...] = jnp.concatenate([gains, jnp.zeros((120, SLOTS), f32)], axis=0).T
         for k in range(8):
-            at = (y ^ flip) * 8 + k
-            rows = picked_ref[pl.ds(k * 256 + first, PIECE), :] if turn is None else turn[k]
+            rows = picked_ref[pl.ds(k * 256 + first, PIECE), :] if turn is None else turn[k, :PIECE, :]
             gain = gain_ref[pl.ds(first, PIECE), :][:, k : k + 1]
-            out_ref[at] = (rows.astype(f32) * scale * gain).astype(bf16)
-
-
-def panel_pieces(place, picked, turns, sums):
+            out_ref[(y ^ flip) * 8 + k] = (rows.astype(f32) * scale * gain).astype(bf16)
+
+
+def panel_pieces(place, picked, gain, sums, turns):
     return pl.pallas_call(
         panel_kernel,
         out_shape=jax.ShapeDtypeStruct((32, PIECE, SLOTS), bf16),
-        in_specs=[pl.BlockSpec(memory_space=pltpu.SMEM)] + [pl.BlockSpec(memory_space=pltpu.VMEM)] * 8,
+        in_specs=[pl.BlockSpec(memory_space=pltpu.SMEM)] + [pl.BlockSpec(memory_space=pltpu.VMEM)] * 6,
         out_specs=pl.BlockSpec(memory_space=pltpu.VMEM),
         scratch_shapes=[pltpu.VMEM((SLOTS, 128), f32)],
         compiler_params=params(10),
         name="panel",
-    )(place, picked, *turns, *sums)
+    )(place, picked, gain, sums, *turns)
 
 
 def pack_kernel(heights, first_ref, in_ref, *refs):
@@ -228,21 +257,27 @@
     row = row_first + lax.broadcasted_iota(jnp.int32, (256, 256), 0)
     col = col_first + lax.broadcasted_iota(jnp.int32, (256, 256), 1)
     for s in range(4):
-        for ref, which in ((own[s], core), (got[s], 1 - core)):
-            at = pl.multiple_of(s * 512 + which * 256, 256)
-            out_ref[:, pl.ds(at, 256)] = jnp.where(row <= col + at, ref[:256, :] * part, 0.0)
-            mean_ref[:, pl.ds(at, 256)] = ref[256:264, :][:1] * part
+
+        @pl.when(pl.program_id(0) == s)
+        def _():
+            for ref, which in ((own[s], core), (got[s], 1 - core)):
+                at = pl.multiple_of(which * 256, 256)
+                values = jnp.where(row <= col + (s * 512 + at), ref[:256, :] * part, 0.0)
+                out_ref[:, pl.ds(at, 256)] = values
+                mean_ref[:, pl.ds(at, 256)] = ref[256:264, :][:1] * part
 
 
 def finish(info, part, own, got):
+    vmem = pl.BlockSpec(memory_space=pltpu.VMEM)
     return pl.pallas_call(
         finish_kernel,
+        grid=(4,),
         out_shape=(
             jax.ShapeDtypeStruct((1, WIDTH), f32),
             jax.ShapeDtypeStruct((256, WIDTH), f32),
         ),
-        in_specs=[pl.BlockSpec(memory_space=pltpu.SMEM)] * 2 + [pl.BlockSpec(memory_space=pltpu.VMEM)] * 8,
-        out_specs=(pl.BlockSpec(memory_space=pltpu.VMEM),) * 2,
+        in_specs=[pl.BlockSpec(memory_space=pltpu.SMEM)] * 2 + [vmem] * 8,
+        out_specs=(pl.BlockSpec((1, 512), lambda s: (0, s)), pl.BlockSpec((256, 512), lambda s: (0, s))),
         compiler_params=params(10),
         name="finish",
     )(info, part, *own, *got)
@@ -268,12 +303,12 @@
 def per_device(resid, norm_gain, keep_index, counts):
     z, x, c, y = (lax.axis_index(a) for a in ("z", "x", "c", "y"))
     place_y = y[None].astype(jnp.int32)
-    picked, sums, *turns = pick(place_y, resid, norm_gain.reshape(8, SLOTS), keep_index, counts)
-    all_sums = [sums] + [trade(sums, "y", flip) for flip in (1, 2, 3)]
+    gain = norm_gain.reshape(8, SLOTS)
+    picked, sums, *turns = pick(place_y, resid, gain, keep_index, counts)
     turns = [trade(turn, "y", flip) for turn, flip in zip(turns, (1, 2, 3))]
-    normed = norm(counts, picked, norm_gain[:, None], all_sums)
+    normed = norm(counts, picked, norm_gain[:, None], sums, turns)
     pieces = lax.all_to_all(normed, TOK, 0, 0, tiled=True)
-    panel = panel_pieces(place_y, picked, turns, all_sums)
+    panel = panel_pieces(place_y, picked, gain, sums, turns)
     panel = lax.all_to_all(panel, TOK, 0, 0, tiled=True)
 
     loads = pieces[:, PIECE, 0].astype(jnp.int32)
@@ -288,7 +323,7 @@
             which = side(x if axis == "x" else z, flip, axis not in seen)
             streams[s] = meet(streams[s], axis, flip, which)
         if step == 0:
-            panel, _ = lax.optimization_barrier((panel, streams[3][:8, :128]))
+            panel = lax.optimization_barrier((panel, *[value[:8, :128] for value in streams]))[0]
 
     (rows,) = pack(first, panel, (PIECE,))
     rows = meet(rows, "y", 1, side(y, 1, True))

time: 140 us -> 154 us (1.10)
  waiting for transfers between devices: 59.7 us -> 78.7 us
  starting transfers between devices: 51.3 us -> 43.8 us
  Pallas kernels: 16.4 us -> 18.7 us
    all_to_all x1, waiting for transfers between devices: 2.19 us -> 17.4 us  [per_device(): pieces = lax.all_to_all(normed, TOK, 0, 0, tiled=True)]
    ppermute x24 -> x21, starting transfers between devices: 28.8 us -> 22.4 us  [trade(): return lax.ppermute(value, axis, [(i, i ^ flip) for i in range(4)])]
    ppermute x24 -> x21, waiting for transfers between devices: 44.2 us -> 48.1 us  [trade(): return lax.ppermute(value, axis, [(i, i ^ flip) for i in range(4)])]
    pallas_call x1, Pallas kernels: 1.39 us -> 3.45 us  [pick(): pl.pallas_call(pick_kernel, out_shape=(jax.ShapeDtypeStruct((WIDTH, SLOTS...]
  transfers between devices with their start and end apart: 31 -> 28, of which waited for: 21 -> 19; matrix products, arithmetic and copies ran while one was open for 5% -> 4% of each run, Pallas kernels for 4% -> 4%
where the time goes in v7:
time: 154 us
  waiting for transfers between devices  78.7 us (51%)
  starting transfers between devices  43.8 us (28%)
  Pallas kernels  18.7 us (12%)
  other arithmetic  6.81 us (4%)
  local copies, waits for them, and re-layouts  4.05 us (3%)
  between operations  1.75 us (1%)
    ppermute x21, waiting for transfers between devices, trade(): return lax.ppermute(value, axis, [(i, i ^ flip) for i in range(4)])  48.1 us
    ppermute x21, starting transfers between devices, trade(): return lax.ppermute(value, axis, [(i, i ^ flip) for i in range(4)])  22.4 us
    all_to_all x1, waiting for transfers between devices, per_device(): pieces = lax.all_to_all(normed, TOK, 0, 0, tiled=True)  17.4 us
    all_to_all x1, waiting for transfers between devices, per_device(): panel = lax.all_to_all(panel, TOK, 0, 0, tiled=True)  12.3 us
    all_to_all x1, starting transfers between devices, per_device(): pieces = lax.all_to_all(normed, TOK, 0, 0, tiled=True)  10.1 us
    ppermute x5, starting transfers between devices, swap(): return lax.ppermute(value, 'c', [(0, 1), (1, 0)])  5.8 us
    all_to_all x1, starting transfers between devices, per_device(): panel = lax.all_to_all(panel, TOK, 0, 0, tiled=True)  5.52 us
    pallas_call x4, Pallas kernels, gram(): pl.pallas_call(gram_kernel, out_shape=(jax.ShapeDtypeStruct((264, 256), f...  5.11 us
  transfers between devices with their start and end apart: 28, of which 19 were waited for; matrix products, arithmetic and copies ran while one was open for 4% of the time, Pallas kernels for 4%

profile of v7, /device:TPU:1, one launch (start us, length us, event | category | flops | bytes accessed | tf_op | source)
XLA Modules:
  0.0 153.8 jit_solution(7285680436659577078)
XLA Ops:
  0.6 0.8 reshape.40.gain_ref.own_gain_ref
  1.4 1.6 %copy-done = bf16[512,2048]{1,0:T(8,128)(2,1)S(1)} copy-done((bf16[512,2048]{1,0:T(8,128)(2,1)S(1)}, bf16[512,2048]{1,0:T(8,128)(2,1)}, u32[]{:S(2)}) %copy-start) | copy-done | bytes 2097176
  3.0 0.7 copy-done.1
  3.7 0.7 copy-done.3
  4.3 3.4 %pick.1 = (bf16[2048,256]{1,0:T(8,128)(2,1)S(1)}, f32[8,256]{1,0:T(8,128)S(1)}, bf16[8,80,256]{2,1,0:T(8,128)(2,1)}, bf16[8,80,256]{2,1,0:T(8,128)(2,1)}, bf16[8,80,256]{2,1,0:T(8,128)(2,1)}) custom-call(s32[1]{0:T(128)} %bitcast.3.place_ref, s32[1,256]{1,0:T(1,128)S(1)} %bitcast.9, s32[2]{0:T(128)S(1)} %copy-done.1, bf16[512,2048]{1,0:T(8,128)(2,1)S(1)} %copy-done, ...), custom_call_target="tpu_custom_call" | custom-call | tf_op jit(solution)/shard_map/pick/pallas_call | solution.py:79
  7.8 2.2 %collective-permute-start = (bf16[8,80,256]{2,1,0:T(8,128)(2,1)}, bf16[8,80,256]{2,1,0:T(8,128)(2,1)S(1)}, u32[]{:S(2)}, u32[]{:S(2)}) collective-permute-start(bf16[8,80,256]{2,1,0:T(8,128)(2,1)} %get-tuple-element.23), channel_id=1, source_target_pairs={{0,1},{1,0},{2,3},{3,2},{4,5},{5,4},{6,7},{7,6},{8,9},{9,8},{10,11... | collective-permute-start | bytes 983048 | tf_op jit(solution)/shard_map/ppermute | solution.py:291
  10.0 2.6 %collective-permute-start.1 = (bf16[8,80,256]{2,1,0:T(8,128)(2,1)}, bf16[8,80,256]{2,1,0:T(8,128)(2,1)S(1)}, u32[]{:S(2)}, u32[]{:S(2)}) collective-permute-start(bf16[8,80,256]{2,1,0:T(8,128)(2,1)} %get-tuple-element.24), channel_id=1, source_target_pairs={{0,2},{1,3},{2,0},{3,1},{4,6},{5,7},{6,4},{7,5},{8,10},{9,11},{10,... | collective-permute-start | bytes 983048 | tf_op jit(solution)/shard_map/ppermute | solution.py:291
  13.0 4.2 %collective-permute-done.t1 = bf16[8,80,256]{2,1,0:T(8,128)(2,1)S(1)} collective-permute-done((bf16[8,80,256]{2,1,0:T(8,128)(2,1)}, bf16[8,80,256]{2,1,0:T(8,128)(2,1)S(1)}, u32[]{:S(2)}, u32[]{:S(2)}) %collective-permute-start) | collective-permute-done | bytes 327712 | tf_op jit(solution)/shard_map/ppermute | solution.py:291
  17.2 9.8 %collective-permute-done.1.t2 = bf16[8,80,256]{2,1,0:T(8,128)(2,1)S(1)} collective-permute-done((bf16[8,80,256]{2,1,0:T(8,128)(2,1)}, bf16[8,80,256]{2,1,0:T(8,128)(2,1)S(1)}, u32[]{:S(2)}, u32[]{:S(2)}) %collective-permute-start.1) | collective-permute-done | bytes 327712 | tf_op jit(solution)/shard_map/ppermute | solution.py:291
  27.0 2.0 %collective-permute-done.2.t3 = bf16[8,80,256]{2,1,0:T(8,128)(2,1)S(1)} collective-permute-done((bf16[8,80,256]{2,1,0:T(8,128)(2,1)}, bf16[8,80,256]{2,1,0:T(8,128)(2,1)S(1)}, u32[]{:S(2)}, u32[]{:S(2)}) %collective-permute-start.2) | collective-permute-done | bytes 327712 | tf_op jit(solution)/shard_map/ppermute | solution.py:291
  29.0 1.9 %norm.1 = bf16[32,80,256]{2,1,0:T(8,128)(2,1)} custom-call(s32[2]{0:T(128)S(1)} %copy-done.2, bf16[2048,256]{1,0:T(8,128)(2,1)S(1)} %get-tuple-element.21.picked_ref, f32[2048,1]{1,0:T(8,128)S(1)} %copy.7.gain_ref, f32[8,256]{1,0:T(8,128)S(1)} %get-tuple-element.22.sums, bf16[8,80,256]{2,1,0:T(8,128)(2,1)S(1)} %collective-permute-done.t1, ...), custom_call_target="tpu_custom_call" | custom-call | tf_op jit(solution)/shard_map/norm/pallas_call | solution.py:145
  31.0 10.1 %all-to-all-start = ((bf16[32,80,256]{2,1,0:T(8,128)(2,1)}), bf16[32,80,256]{2,1,0:T(8,128)(2,1)S(1)}, u32[]{:S(2)}, u32[]{:S(2)}) async-start(bf16[32,80,256]{2,1,0:T(8,128)(2,1)} %norm.1), calls=%async_computation | async-start | bytes 2621440 | tf_op jit(solution)/shard_map/all_to_all | solution.py:310
  41.1 1.7 %panel.1 = bf16[32,64,256]{2,1,0:T(8,128)(2,1)} custom-call(s32[1]{0:T(128)} %bitcast.3.place_ref, bf16[2048,256]{1,0:T(8,128)(2,1)S(1)} %get-tuple-element.21.picked_ref, f32[8,256]{1,0:T(8,128)S(1)} %reshape.40.gain_ref.own_gain_ref, f32[8,256]{1,0:T(8,128)S(1)} %get-tuple-element.22.sums, bf16[8,80,256]{2,1,0:T(8,128)(2,1)S(1)} %collective-permute-done.t1, ...), custom_call_target="tpu_custom_call" | custom-call | tf_op jit(solution)/shard_map/panel/pallas_call | solution.py:172
  42.8 17.4 %all-to-all-done.refs_1_ = bf16[32,80,256]{2,1,0:T(8,128)(2,1)S(1)} async-done(((bf16[32,80,256]{2,1,0:T(8,128)(2,1)}), bf16[32,80,256]{2,1,0:T(8,128)(2,1)S(1)}, u32[]{:S(2)}, u32[]{:S(2)}) %all-to-all-start) | async-done | bytes 1310752 | tf_op jit(solution)/shard_map/all_to_all | solution.py:310
  60.2 5.5 %all-to-all-start.1 = ((bf16[32,64,256]{2,1,0:T(8,128)(2,1)}), bf16[32,64,256]{2,1,0:T(8,128)(2,1)S(1)}, u32[]{:S(2)}, u32[]{:S(2)}) async-start(bf16[32,64,256]{2,1,0:T(8,128)(2,1)} %panel.1), calls=%async_computation.1 | async-start | bytes 2097152 | tf_op jit(solution)/shard_map/all_to_all | solution.py:312
  65.9 1.3 fusion
  67.2 2.0 %pack.3 = (bf16[16,4224]{1,0:T(8,128)(2,1)S(1)}, bf16[16,4224]{1,0:T(8,128)(2,1)S(1)}, bf16[16,4224]{1,0:T(8,128)(2,1)S(1)}, bf16[16,4224]{1,0:T(8,128)(2,1)S(1)}) custom-call(s32[32]{0:T(128)S(1)} %sub.3.refs_0_, bf16[32,80,256]{2,1,0:T(8,128)(2,1)S(1)} %all-to-all-done.refs_1_), custom_call_target="tpu_custom_call" | custom-call | tf_op jit(solution)/shard_map/pack/pallas_call | solution.py:213
  69.2 1.5 collective-permute-start.6
  70.7 12.3 %all-to-all-done.1.refs_1_ = bf16[32,64,256]{2,1,0:T(8,128)(2,1)S(1)} async-done(((bf16[32,64,256]{2,1,0:T(8,128)(2,1)}), bf16[32,64,256]{2,1,0:T(8,128)(2,1)S(1)}, u32[]{:S(2)}, u32[]{:S(2)}) %all-to-all-start.1) | async-done | bytes 1048608 | tf_op jit(solution)/shard_map/all_to_all | solution.py:312
  83.0 2.0 %pack.2 = bf16[64,4224]{1,0:T(8,128)(2,1)S(1)} custom-call(s32[32]{0:T(128)S(1)} %sub.3.refs_0_, bf16[32,64,256]{2,1,0:T(8,128)(2,1)S(1)} %all-to-all-done.1.refs_1_), custom_call_target="tpu_custom_call" | custom-call | tf_op jit(solution)/shard_map/pack/pallas_call | solution.py:213
  85.2 2.1 %collective-permute-start.14 = (bf16[16,4224]{1,0:T(8,128)(2,1)S(1)}, bf16[16,4224]{1,0:T(8,128)(2,1)S(1)}, u32[]{:S(2)}, u32[]{:S(2)}) collective-permute-start(bf16[16,4224]{1,0:T(8,128)(2,1)S(1)} %get-tuple-element.30), channel_id=1, source_target_pairs={{0,24},{8,16},{16,8},{24,0},{1,25},{9,17},{17,9},{25,1},{2,26},{10... | collective-permute-start | bytes 405512 | tf_op jit(solution)/shard_map/ppermute | solution.py:291
  87.9 0.8 collective-permute-start.7
  88.8 1.2 collective-permute-done.10
  90.0 1.8 %collective-permute-start.11 = (bf16[32,4224]{1,0:T(8,128)(2,1)S(1)}, bf16[32,4224]{1,0:T(8,128)(2,1)S(1)}, u32[]{:S(2)}, u32[]{:S(2)}) collective-permute-start(bf16[32,4224]{1,0:T(8,128)(2,1)S(1)} %pad_maximum_fusion.16), channel_id=1, source_target_pairs={{0,24},{8,16},{16,8},{24,0},{1,25},{9,17},{17,9},{25,1},{2,26},{10... | collective-permute-start | bytes 811016 | tf_op jit(solution)/shard_map/ppermute | solution.py:291
  91.9 1.3 collective-permute-start.15
  93.2 0.8 collective-permute-done.18
  94.1 1.7 %collective-permute-done.7 = bf16[32,4224]{1,0:T(8,128)(2,1)S(1)} collective-permute-done((bf16[32,4224]{1,0:T(8,128)(2,1)S(1)}, bf16[32,4224]{1,0:T(8,128)(2,1)S(1)}, u32[]{:S(2)}, u32[]{:S(2)}) %collective-permute-start.7) | collective-permute-done | bytes 270368 | tf_op jit(solution)/shard_map/ppermute | solution.py:291
  95.9 1.2 collective-permute-start.8
  97.1 1.0 collective-permute-done.11
  98.2 0.8 collective-permute-start.12
  99.1 1.4 collective-permute-done.15
  100.7 0.8 collective-permute-done.19
  102.1 7.6 %collective-permute-done.8 = bf16[64,4224]{1,0:T(8,128)(2,1)S(1)} collective-permute-done((bf16[64,4224]{1,0:T(8,128)(2,1)S(1)}, bf16[64,4224]{1,0:T(8,128)(2,1)S(1)}, u32[]{:S(2)}, u32[]{:S(2)}) %collective-permute-start.8) | collective-permute-done | bytes 540704 | tf_op jit(solution)/shard_map/ppermute | solution.py:291
  110.0 3.0 %collective-permute-start.9 = (bf16[128,4224]{1,0:T(8,128)(2,1)S(1)}, bf16[128,4224]{1,0:T(8,128)(2,1)S(1)}, u32[]{:S(2)}, u32[]{:S(2)}) collective-permute-start(bf16[128,4224]{1,0:T(8,128)(2,1)S(1)} %pad_maximum_fusion.7), channel_id=1, source_target_pairs={{0,96},{32,64},{64,32},{96,0},{1,97},{33,65},{65,33},{97,1},{2,98}... | collective-permute-start | bytes 3244040 | tf_op jit(solution)/shard_map/ppermute | solution.py:291
  113.9 0.8 collective-permute-start.17
  115.0 2.7 %collective-permute-start.21 = (bf16[128,4224]{1,0:T(8,128)(2,1)S(1)}, bf16[128,4224]{1,0:T(8,128)(2,1)S(1)}, u32[]{:S(2)}, u32[]{:S(2)}) collective-permute-start(bf16[128,4224]{1,0:T(8,128)(2,1)S(1)} %pad_maximum_fusion.10), channel_id=1, source_target_pairs={{0,24},{8,16},{16,8},{24,0},{1,25},{9,17},{17,9},{25,1},{2,26},{10... | collective-permute-start | bytes 3244040 | tf_op jit(solution)/shard_map/ppermute | solution.py:291
  117.7 9.4 %collective-permute-done.4 = bf16[128,4224]{1,0:T(8,128)(2,1)S(1)} collective-permute-done((bf16[128,4224]{1,0:T(8,128)(2,1)S(1)}, bf16[128,4224]{1,0:T(8,128)(2,1)S(1)}, u32[]{:S(2)}, u32[]{:S(2)}) %collective-permute-start.4) | collective-permute-done | bytes 1081376 | tf_op jit(solution)/shard_map/ppermute | solution.py:291
  127.7 2.5 %collective-permute-start.5 = (bf16[256,4224]{1,0:T(8,128)(2,1)S(1)}, bf16[256,4224]{1,0:T(8,128)(2,1)S(1)}, u32[]{:S(2)}, u32[]{:S(2)}) collective-permute-start(bf16[256,4224]{1,0:T(8,128)(2,1)S(1)} %pad_maximum_fusion.1), channel_id=1, source_target_pairs={{0,4},{4,0},{1,5},{5,1},{2,6},{6,2},{3,7},{7,3},{8,12},{12,8},{9,1... | collective-permute-start | bytes 6488072 | tf_op jit(solution)/shard_map/ppermute | solution.py:287
  130.2 4.9 %collective-permute-done.9 = bf16[128,4224]{1,0:T(8,128)(2,1)S(1)} collective-permute-done((bf16[128,4224]{1,0:T(8,128)(2,1)S(1)}, bf16[128,4224]{1,0:T(8,128)(2,1)S(1)}, u32[]{:S(2)}, u32[]{:S(2)}) %collective-permute-start.9) | collective-permute-done | bytes 1081376 | tf_op jit(solution)/shard_map/ppermute | solution.py:291
  135.6 1.4 collective-permute-done.13
  138.1 1.9 %collective-permute-done.21 = bf16[128,4224]{1,0:T(8,128)(2,1)S(1)} collective-permute-done((bf16[128,4224]{1,0:T(8,128)(2,1)S(1)}, bf16[128,4224]{1,0:T(8,128)(2,1)S(1)}, u32[]{:S(2)}, u32[]{:S(2)}) %collective-permute-start.21) | collective-permute-done | bytes 1081376 | tf_op jit(solution)/shard_map/ppermute | solution.py:291
  140.5 0.6 pad_maximum_fusion.rows_ref
  141.1 1.3 gram.4
  142.4 1.3 gram.5
  143.6 1.3 gram.6
  144.9 1.3 gram.7
  146.2 2.7 %collective-permute-start.22 = (f32[264,256]{1,0:T(8,128)S(1)}, f32[264,256]{1,0:T(8,128)S(1)}, u32[]{:S(2)}, u32[]{:S(2)}) collective-permute-start(f32[264,256]{1,0:T(8,128)S(1)} %get-tuple-element.34), channel_id=1, source_target_pairs={{0,4},{4,0},{1,5},{5,1},{2,6},{6,2},{3,7},{7,3},{8,12},{12,8},{9,1... | collective-permute-start | bytes 811016 | tf_op jit(solution)/shard_map/ppermute | solution.py:287
  151.3 2.5 %finish.1 = (f32[1,2048]{1,0:T(1,128)}, f32[256,2048]{1,0:T(8,128)}) custom-call(s32[3]{0:T(128)S(1)} %pad_add_fusion.info_ref, f32[1]{0:T(128)} %bitcast.6.part_ref, f32[264,256]{1,0:T(8,128)S(1)} %get-tuple-element.27.refs_0_, f32[264,256]{1,0:T(8,128)S(1)} %get-tuple-element.29.refs_1_, f32[264,256]{1,0:T(8,128)S(1)} %get-tuple-element.31.refs_2_, ...), custom_call_target="tpu_custom_call" | custom-call | tf_op jit(solution)/shard_map/finish/pallas_call | solution.py:272
  (73 shorter events, 8.2 us)
Async XLA Ops:
  0.6 12.0 %copy-start.4 = (f32[2048]{0:T(1024)S(1)}, f32[2048]{0:T(1024)}, u32[]{:S(2)}) copy-start(f32[2048]{0:T(1024)} %param.5) | copy-start | bytes 24580
  1.4 1.6 %copy-start = (bf16[512,2048]{1,0:T(8,128)(2,1)S(1)}, bf16[512,2048]{1,0:T(8,128)(2,1)}, u32[]{:S(2)}) copy-start(bf16[512,2048]{1,0:T(8,128)(2,1)} %resid_hbm.1) | copy-start | bytes 6291460
  3.0 0.7 copy-start.1
  3.7 0.7 copy-start.3
  4.3 24.7 %copy-start.2 = (s32[2]{0:T(128)S(1)}, s32[2]{0:T(128)}, u32[]{:S(2)}) copy-start(s32[2]{0:T(128)} %counts_ref.1) | copy-start | bytes 28
  7.8 9.4 %collective-permute-start = (bf16[8,80,256]{2,1,0:T(8,128)(2,1)}, bf16[8,80,256]{2,1,0:T(8,128)(2,1)S(1)}, u32[]{:S(2)}, u32[]{:S(2)}) collective-permute-start(bf16[8,80,256]{2,1,0:T(8,128)(2,1)} %get-tuple-element.23), channel_id=1, source_target_pairs={{0,1},{1,0},{2,3},{3,2},{4,5},{5,4},{6,7},{7,6},{8,9},{9,8},{10,11... | collective-permute-start | bytes 983048 | tf_op jit(solution)/shard_map/ppermute | solution.py:291
  10.0 17.0 %collective-permute-start.1 = (bf16[8,80,256]{2,1,0:T(8,128)(2,1)}, bf16[8,80,256]{2,1,0:T(8,128)(2,1)S(1)}, u32[]{:S(2)}, u32[]{:S(2)}) collective-permute-start(bf16[8,80,256]{2,1,0:T(8,128)(2,1)} %get-tuple-element.24), channel_id=1, source_target_pairs={{0,2},{1,3},{2,0},{3,1},{4,6},{5,7},{6,4},{7,5},{8,10},{9,11},{10,... | collective-permute-start | bytes 983048 | tf_op jit(solution)/shard_map/ppermute | solution.py:291
  12.6 16.4 %collective-permute-start.2 = (bf16[8,80,256]{2,1,0:T(8,128)(2,1)}, bf16[8,80,256]{2,1,0:T(8,128)(2,1)S(1)}, u32[]{:S(2)}, u32[]{:S(2)}) collective-permute-start(bf16[8,80,256]{2,1,0:T(8,128)(2,1)} %get-tuple-element.25), channel_id=1, source_target_pairs={{0,3},{1,2},{2,1},{3,0},{4,7},{5,6},{6,5},{7,4},{8,11},{9,10},{10,... | collective-permute-start | bytes 983048 | tf_op jit(solution)/shard_map/ppermute | solution.py:291
  31.0 29.2 %all-to-all-start = ((bf16[32,80,256]{2,1,0:T(8,128)(2,1)}), bf16[32,80,256]{2,1,0:T(8,128)(2,1)S(1)}, u32[]{:S(2)}, u32[]{:S(2)}) async-start(bf16[32,80,256]{2,1,0:T(8,128)(2,1)} %norm.1), calls=%async_computation | async-start | bytes 2621440 | tf_op jit(solution)/shard_map/all_to_all | solution.py:310
  60.2 22.8 %all-to-all-start.1 = ((bf16[32,64,256]{2,1,0:T(8,128)(2,1)}), bf16[32,64,256]{2,1,0:T(8,128)(2,1)S(1)}, u32[]{:S(2)}, u32[]{:S(2)}) async-start(bf16[32,64,256]{2,1,0:T(8,128)(2,1)} %panel.1), calls=%async_computation.1 | async-start | bytes 2097152 | tf_op jit(solution)/shard_map/all_to_all | solution.py:312
  69.2 18.7 %collective-permute-start.6 = (bf16[16,4224]{1,0:T(8,128)(2,1)S(1)}, bf16[16,4224]{1,0:T(8,128)(2,1)S(1)}, u32[]{:S(2)}, u32[]{:S(2)}) collective-permute-start(bf16[16,4224]{1,0:T(8,128)(2,1)S(1)} %get-tuple-element.26), channel_id=1, source_target_pairs={{0,8},{8,0},{16,24},{24,16},{1,9},{9,1},{17,25},{25,17},{2,10},{10... | collective-permute-start | bytes 405512 | tf_op jit(solution)/shard_map/ppermute | solution.py:291
  85.0 16.8 %collective-permute-start.3 = (bf16[64,4224]{1,0:T(8,128)(2,1)S(1)}, bf16[64,4224]{1,0:T(8,128)(2,1)S(1)}, u32[]{:S(2)}, u32[]{:S(2)}) collective-permute-start(bf16[64,4224]{1,0:T(8,128)(2,1)S(1)} %pack.2), channel_id=1, source_target_pairs={{0,1},{1,0},{2,3},{3,2},{4,5},{5,4},{6,7},{7,6},{8,9},{9,8},{10,11... | collective-permute-start | bytes 1622024 | tf_op jit(solution)/shard_map/ppermute | solution.py:291
  85.1 4.9 %collective-permute-start.10 = (bf16[16,4224]{1,0:T(8,128)(2,1)S(1)}, bf16[16,4224]{1,0:T(8,128)(2,1)S(1)}, u32[]{:S(2)}, u32[]{:S(2)}) collective-permute-start(bf16[16,4224]{1,0:T(8,128)(2,1)S(1)} %get-tuple-element.28), channel_id=1, source_target_pairs={{0,32},{32,0},{64,96},{96,64},{1,33},{33,1},{65,97},{97,65},{2,34}... | collective-permute-start | bytes 405512 | tf_op jit(solution)/shard_map/ppermute | solution.py:291
  85.2 6.6 %collective-permute-start.14 = (bf16[16,4224]{1,0:T(8,128)(2,1)S(1)}, bf16[16,4224]{1,0:T(8,128)(2,1)S(1)}, u32[]{:S(2)}, u32[]{:S(2)}) collective-permute-start(bf16[16,4224]{1,0:T(8,128)(2,1)S(1)} %get-tuple-element.30), channel_id=1, source_target_pairs={{0,24},{8,16},{16,8},{24,0},{1,25},{9,17},{17,9},{25,1},{2,26},{10... | collective-permute-start | bytes 405512 | tf_op jit(solution)/shard_map/ppermute | solution.py:291
  87.3 6.6 %collective-permute-start.18 = (bf16[16,4224]{1,0:T(8,128)(2,1)S(1)}, bf16[16,4224]{1,0:T(8,128)(2,1)S(1)}, u32[]{:S(2)}, u32[]{:S(2)}) collective-permute-start(bf16[16,4224]{1,0:T(8,128)(2,1)S(1)} %get-tuple-element.32), channel_id=1, source_target_pairs={{0,96},{32,64},{64,32},{96,0},{1,97},{33,65},{65,33},{97,1},{2,98}... | collective-permute-start | bytes 405512 | tf_op jit(solution)/shard_map/ppermute | solution.py:291
  87.9 7.8 %collective-permute-start.7 = (bf16[32,4224]{1,0:T(8,128)(2,1)S(1)}, bf16[32,4224]{1,0:T(8,128)(2,1)S(1)}, u32[]{:S(2)}, u32[]{:S(2)}) collective-permute-start(bf16[32,4224]{1,0:T(8,128)(2,1)S(1)} %pad_maximum_fusion.15), channel_id=1, source_target_pairs={{0,32},{32,0},{64,96},{96,64},{1,33},{33,1},{65,97},{97,65},{2,34}... | collective-permute-start | bytes 811016 | tf_op jit(solution)/shard_map/ppermute | solution.py:291
  90.0 8.1 %collective-permute-start.11 = (bf16[32,4224]{1,0:T(8,128)(2,1)S(1)}, bf16[32,4224]{1,0:T(8,128)(2,1)S(1)}, u32[]{:S(2)}, u32[]{:S(2)}) collective-permute-start(bf16[32,4224]{1,0:T(8,128)(2,1)S(1)} %pad_maximum_fusion.16), channel_id=1, source_target_pairs={{0,24},{8,16},{16,8},{24,0},{1,25},{9,17},{17,9},{25,1},{2,26},{10... | collective-permute-start | bytes 811016 | tf_op jit(solution)/shard_map/ppermute | solution.py:291
  91.9 8.6 %collective-permute-start.15 = (bf16[32,4224]{1,0:T(8,128)(2,1)S(1)}, bf16[32,4224]{1,0:T(8,128)(2,1)S(1)}, u32[]{:S(2)}, u32[]{:S(2)}) collective-permute-start(bf16[32,4224]{1,0:T(8,128)(2,1)S(1)} %pad_maximum_fusion.17), channel_id=1, source_target_pairs={{0,96},{32,64},{64,32},{96,0},{1,97},{33,65},{65,33},{97,1},{2,98}... | collective-permute-start | bytes 811016 | tf_op jit(solution)/shard_map/ppermute | solution.py:291
  94.0 7.5 %collective-permute-start.19 = (bf16[32,4224]{1,0:T(8,128)(2,1)S(1)}, bf16[32,4224]{1,0:T(8,128)(2,1)S(1)}, u32[]{:S(2)}, u32[]{:S(2)}) collective-permute-start(bf16[32,4224]{1,0:T(8,128)(2,1)S(1)} %pad_maximum_fusion.18), channel_id=1, source_target_pairs={{0,8},{8,0},{16,24},{24,16},{1,9},{9,1},{17,25},{25,17},{2,10},{10... | collective-permute-start | bytes 811016 | tf_op jit(solution)/shard_map/ppermute | solution.py:291
  95.9 13.8 %collective-permute-start.8 = (bf16[64,4224]{1,0:T(8,128)(2,1)S(1)}, bf16[64,4224]{1,0:T(8,128)(2,1)S(1)}, u32[]{:S(2)}, u32[]{:S(2)}) collective-permute-start(bf16[64,4224]{1,0:T(8,128)(2,1)S(1)} %pad_maximum_fusion.11), channel_id=1, source_target_pairs={{0,24},{8,16},{16,8},{24,0},{1,25},{9,17},{17,9},{25,1},{2,26},{10... | collective-permute-start | bytes 1622024 | tf_op jit(solution)/shard_map/ppermute | solution.py:291
  98.2 14.8 %collective-permute-start.12 = (bf16[64,4224]{1,0:T(8,128)(2,1)S(1)}, bf16[64,4224]{1,0:T(8,128)(2,1)S(1)}, u32[]{:S(2)}, u32[]{:S(2)}) collective-permute-start(bf16[64,4224]{1,0:T(8,128)(2,1)S(1)} %pad_maximum_fusion.12), channel_id=1, source_target_pairs={{0,96},{32,64},{64,32},{96,0},{1,97},{33,65},{65,33},{97,1},{2,98}... | collective-permute-start | bytes 1622024 | tf_op jit(solution)/shard_map/ppermute | solution.py:291
  100.6 12.9 %collective-permute-start.16 = (bf16[64,4224]{1,0:T(8,128)(2,1)S(1)}, bf16[64,4224]{1,0:T(8,128)(2,1)S(1)}, u32[]{:S(2)}, u32[]{:S(2)}) collective-permute-start(bf16[64,4224]{1,0:T(8,128)(2,1)S(1)} %pad_maximum_fusion.13), channel_id=1, source_target_pairs={{0,8},{8,0},{16,24},{24,16},{1,9},{9,1},{17,25},{25,17},{2,10},{10... | collective-permute-start | bytes 1622024 | tf_op jit(solution)/shard_map/ppermute | solution.py:291
  101.7 13.0 %collective-permute-start.20 = (bf16[64,4224]{1,0:T(8,128)(2,1)S(1)}, bf16[64,4224]{1,0:T(8,128)(2,1)S(1)}, u32[]{:S(2)}, u32[]{:S(2)}) collective-permute-start(bf16[64,4224]{1,0:T(8,128)(2,1)S(1)} %pad_maximum_fusion.14), channel_id=1, source_target_pairs={{0,32},{32,0},{64,96},{96,64},{1,33},{33,1},{65,97},{97,65},{2,34}... | collective-permute-start | bytes 1622024 | tf_op jit(solution)/shard_map/ppermute | solution.py:291
  102.0 25.2 %collective-permute-start.4 = (bf16[128,4224]{1,0:T(8,128)(2,1)S(1)}, bf16[128,4224]{1,0:T(8,128)(2,1)S(1)}, u32[]{:S(2)}, u32[]{:S(2)}) collective-permute-start(bf16[128,4224]{1,0:T(8,128)(2,1)S(1)} %pad_maximum_fusion.6), channel_id=1, source_target_pairs={{0,3},{1,2},{2,1},{3,0},{4,7},{5,6},{6,5},{7,4},{8,11},{9,10},{10,... | collective-permute-start | bytes 3244040 | tf_op jit(solution)/shard_map/ppermute | solution.py:291
  110.0 25.1 %collective-permute-start.9 = (bf16[128,4224]{1,0:T(8,128)(2,1)S(1)}, bf16[128,4224]{1,0:T(8,128)(2,1)S(1)}, u32[]{:S(2)}, u32[]{:S(2)}) collective-permute-start(bf16[128,4224]{1,0:T(8,128)(2,1)S(1)} %pad_maximum_fusion.7), channel_id=1, source_target_pairs={{0,96},{32,64},{64,32},{96,0},{1,97},{33,65},{65,33},{97,1},{2,98}... | collective-permute-start | bytes 3244040 | tf_op jit(solution)/shard_map/ppermute | solution.py:291
  113.3 23.7 %collective-permute-start.13 = (bf16[128,4224]{1,0:T(8,128)(2,1)S(1)}, bf16[128,4224]{1,0:T(8,128)(2,1)S(1)}, u32[]{:S(2)}, u32[]{:S(2)}) collective-permute-start(bf16[128,4224]{1,0:T(8,128)(2,1)S(1)} %pad_maximum_fusion.8), channel_id=1, source_target_pairs={{0,8},{8,0},{16,24},{24,16},{1,9},{9,1},{17,25},{25,17},{2,10},{10... | collective-permute-start | bytes 3244040 | tf_op jit(solution)/shard_map/ppermute | solution.py:291
  113.9 23.5 %collective-permute-start.17 = (bf16[128,4224]{1,0:T(8,128)(2,1)S(1)}, bf16[128,4224]{1,0:T(8,128)(2,1)S(1)}, u32[]{:S(2)}, u32[]{:S(2)}) collective-permute-start(bf16[128,4224]{1,0:T(8,128)(2,1)S(1)} %pad_maximum_fusion.9), channel_id=1, source_target_pairs={{0,32},{32,0},{64,96},{96,64},{1,33},{33,1},{65,97},{97,65},{2,34}... | collective-permute-start | bytes 3244040 | tf_op jit(solution)/shard_map/ppermute | solution.py:291
  115.0 24.9 %collective-permute-start.21 = (bf16[128,4224]{1,0:T(8,128)(2,1)S(1)}, bf16[128,4224]{1,0:T(8,128)(2,1)S(1)}, u32[]{:S(2)}, u32[]{:S(2)}) collective-permute-start(bf16[128,4224]{1,0:T(8,128)(2,1)S(1)} %pad_maximum_fusion.10), channel_id=1, source_target_pairs={{0,24},{8,16},{16,8},{24,0},{1,25},{9,17},{17,9},{25,1},{2,26},{10... | collective-permute-start | bytes 3244040 | tf_op jit(solution)/shard_map/ppermute | solution.py:291
  127.7 12.7 %collective-permute-start.5 = (bf16[256,4224]{1,0:T(8,128)(2,1)S(1)}, bf16[256,4224]{1,0:T(8,128)(2,1)S(1)}, u32[]{:S(2)}, u32[]{:S(2)}) collective-permute-start(bf16[256,4224]{1,0:T(8,128)(2,1)S(1)} %pad_maximum_fusion.1), channel_id=1, source_target_pairs={{0,4},{4,0},{1,5},{5,1},{2,6},{6,2},{3,7},{7,3},{8,12},{12,8},{9,1... | collective-permute-start | bytes 6488072 | tf_op jit(solution)/shard_map/ppermute | solution.py:287
  146.2 4.2 %collective-permute-start.22 = (f32[264,256]{1,0:T(8,128)S(1)}, f32[264,256]{1,0:T(8,128)S(1)}, u32[]{:S(2)}, u32[]{:S(2)}) collective-permute-start(f32[264,256]{1,0:T(8,128)S(1)} %get-tuple-element.34), channel_id=1, source_target_pairs={{0,4},{4,0},{1,5},{5,1},{2,6},{6,2},{3,7},{7,3},{8,12},{12,8},{9,1... | collective-permute-start | bytes 811016 | tf_op jit(solution)/shard_map/ppermute | solution.py:287
  148.9 1.6 %collective-permute-start.23 = (f32[264,256]{1,0:T(8,128)S(1)}, f32[264,256]{1,0:T(8,128)S(1)}, u32[]{:S(2)}, u32[]{:S(2)}) collective-permute-start(f32[264,256]{1,0:T(8,128)S(1)} %get-tuple-element.35), channel_id=1, source_target_pairs={{0,4},{4,0},{1,5},{5,1},{2,6},{6,2},{3,7},{7,3},{8,12},{12,8},{9,1... | collective-permute-start | bytes 811016 | tf_op jit(solution)/shard_map/ppermute | solution.py:287
  149.0 1.9 %collective-permute-start.24 = (f32[264,256]{1,0:T(8,128)S(1)}, f32[264,256]{1,0:T(8,128)S(1)}, u32[]{:S(2)}, u32[]{:S(2)}) collective-permute-start(f32[264,256]{1,0:T(8,128)S(1)} %get-tuple-element.36), channel_id=1, source_target_pairs={{0,4},{4,0},{1,5},{5,1},{2,6},{6,2},{3,7},{7,3},{8,12},{12,8},{9,1... | collective-permute-start | bytes 811016 | tf_op jit(solution)/shard_map/ppermute | solution.py:287
  149.5 1.8 %collective-permute-start.25 = (f32[264,256]{1,0:T(8,128)S(1)}, f32[264,256]{1,0:T(8,128)S(1)}, u32[]{:S(2)}, u32[]{:S(2)}) collective-permute-start(f32[264,256]{1,0:T(8,128)S(1)} %get-tuple-element.37), channel_id=1, source_target_pairs={{0,4},{4,0},{1,5},{5,1},{2,6},{6,2},{3,7},{7,3},{8,12},{12,8},{9,1... | collective-permute-start | bytes 811016 | tf_op jit(solution)/shard_map/ppermute | solution.py:287

commit v8 on v6

v8 whole, which is shorter than its diff:
```python
import jax
import jax.numpy as jnp
from jax import lax
from jax.experimental import pallas as pl
from jax.experimental.pallas import tpu as pltpu
from jax.sharding import Mesh, PartitionSpec as P

epsilon = 1e-05
TOK = ("z", "x", "c")
SLOTS = 256
LIVE = 4096
WIDTH = 2048
PIECE = 64
EXTRA = 16
MIB = 1024 * 1024
bf16 = jnp.bfloat16
f32 = jnp.float32


def params(mib):
    return pltpu.CompilerParams(vmem_limit_bytes=mib * MIB)


def spread(value, place):
    high = value.astype(bf16).astype(f32)
    middle = (value - high).astype(bf16).astype(f32)
    low = value - high - middle
    rest = jnp.where(place == 2, low, 0.0)
    return jnp.where(place == 0, high, jnp.where(place == 1, middle, rest))


PARTNERS = (("x", 1), ("z", 1), ("x", 3), ("z", 3))


def side(place, flip, first):
    if flip == 1 and not first:
        return (place ^ (place >> 1)) & 1
    return place & 1 if flip == 1 else place >> 1


def slot_of(s, x, z):
    at, seen = 0, []
    for step in range(4):
        axis, flip = PARTNERS[(s + step) % 4]
        at += side(x if axis == "x" else z, flip, axis not in seen) << step
        seen.append(axis)
    return at


def live_slots(counts_ref):
    slot = lax.broadcasted_iota(jnp.int32, (1, SLOTS), 1)
    half = SLOTS // 2
    return slot < jnp.where(slot < half, counts_ref[0], half + counts_ref[1])


def pick_kernel(place_ref, index_ref, counts_ref, resid_ref, gain_ref, out_ref, *refs):
    turn_refs, picked_ref = refs[:4], refs[4]
    tokens = resid_ref.shape[0]
    token = lax.broadcasted_iota(jnp.int32, (tokens, SLOTS), 0)
    kept = jnp.where(live_slots(counts_ref), index_ref[...], -1)
    one_hot = jnp.where(token == kept, 1.0, 0.0).astype(bf16)
    live = (counts_ref[0] + counts_ref[1]).astype(f32)
    extra = jnp.full((EXTRA, SLOTS), live, f32).astype(bf16)
    for t in range(32):
        out_ref[t, PIECE:, :] = extra
    total = jnp.zeros((1, SLOTS), f32)
    for s in range(4):
        product = lax.dot_general(
            resid_ref[:, s * 512 : (s + 1) * 512],
            one_hot,
            (((0,), (0,)), ((), ())),
            preferred_element_type=f32,
        )
        total += jnp.sum(product * product, axis=0, keepdims=True)
        short = product.astype(bf16)
        picked_ref[s * 512 : (s + 1) * 512, :] = short
        for c in range(2):
            for z in range(4):
                for x in range(4):
                    at = c * 256 + slot_of(s, x, z) * 16
                    out_ref[z * 8 + x * 2 + c, s * 16 : (s + 1) * 16, :] = short[at : at + 16, :]
    row = lax.broadcasted_iota(jnp.int32, (EXTRA, SLOTS), 0)
    sum_terms = spread(total, row)
    for k in range(8):
        terms = jnp.where(row < 3, sum_terms, spread(gain_ref[k : k + 1, :], row - 3)).astype(bf16)
        for flip, ref in enumerate(turn_refs):
            first = pl.multiple_of((place_ref[0] ^ flip) * PIECE, PIECE)
            ref[k, :PIECE, :] = picked_ref[pl.ds(k * 256 + first, PIECE), :]
            ref[k, PIECE:, :] = terms


def pick(place, resid, gain, keep_index, counts):
    vmem = pl.BlockSpec(memory_space=pltpu.VMEM)
    smem = pl.BlockSpec(memory_space=pltpu.SMEM)
    return pl.pallas_call(
        pick_kernel,
        out_shape=(jax.ShapeDtypeStruct((32, PIECE + EXTRA, SLOTS), bf16),)
        + (jax.ShapeDtypeStruct((8, PIECE + EXTRA, SLOTS), bf16),) * 4,
        in_specs=[smem, vmem, smem, vmem, vmem],
        out_specs=(vmem,) * 5,
        scratch_shapes=[pltpu.VMEM((WIDTH, SLOTS), bf16)],
        compiler_params=params(16),
        name="pick",
    )(place, keep_index[None, :], counts, resid, gain)


def whole_terms(ref, k, first):
    terms = ref[k, PIECE:, :].astype(f32)
    return terms[first : first + 1, :] + (terms[first + 1 : first + 2, :] + terms[first + 2 : first + 3, :])


def panel_kernel(place_ref, counts_ref, t0, t1, t2, t3, out_ref, gain_ref):
    sums = [whole_terms(ref, 0, 0) for ref in (t0, t1, t2, t3)]
    scale = lax.rsqrt(((sums[0] + sums[2]) + (sums[1] + sums[3])) / 8192 + epsilon)
    row = lax.broadcasted_iota(jnp.int32, (EXTRA, SLOTS), 0)
    extra = spread(jnp.where(live_slots(counts_ref), scale, 0.0), row).astype(bf16)
    y = place_ref[0]
    first = pl.multiple_of(y * PIECE, PIECE)
    for flip, turn in enumerate((t0, t1, t2, t3)):
        gains = [whole_terms(turn, k, 3) for k in range(8)]
        gain_ref[...] = jnp.concatenate(gains + [jnp.zeros((120, SLOTS), f32)], axis=0).T
        for k in range(8):
            gain = gain_ref[pl.ds(first, PIECE), :][:, k : k + 1]
            rows = turn[k, :PIECE, :].astype(f32)
            out_ref[(y ^ flip) * 8 + k, :PIECE, :] = (rows * scale * gain).astype(bf16)
            out_ref[(y ^ flip) * 8 + k, PIECE:, :] = extra


def panel_pieces(place, counts, turns):
    return pl.pallas_call(
        panel_kernel,
        out_shape=jax.ShapeDtypeStruct((32, PIECE + EXTRA, SLOTS), bf16),
        in_specs=[pl.BlockSpec(memory_space=pltpu.SMEM)] * 2 + [pl.BlockSpec(memory_space=pltpu.VMEM)] * 4,
        out_specs=pl.BlockSpec(memory_space=pltpu.VMEM),
        scratch_shapes=[pltpu.VMEM((SLOTS, 128), f32)],
        compiler_params=params(10),
        name="panel",
    )(place, counts, *turns)


def pack_kernel(heights, scales, first_ref, in_ref, *refs):
    acc_ref, out_refs = refs[-1], refs[-1 - len(heights) - scales : -1]
    n_rows = acc_ref.shape[0]
    acc_ref[...] = jnp.zeros_like(acc_ref)
    group = 4

    def body(g, _):
        moved = []
        for k in range(group):
            t = g * group + k
            rows = in_ref[t, :n_rows, :].astype(f32)
            first = first_ref[t]
            base = pl.multiple_of((first // 128) * 128, 128)
            wide = jnp.concatenate([rows, jnp.zeros((n_rows, 128), f32)], axis=1)
            moved.append((base, pltpu.roll(wide, first - base, 1)))
        for base, rows in moved:
            acc_ref[:, pl.ds(base, SLOTS + 128)] += rows
        return 0

    lax.fori_loop(0, 32 // group, body, 0)
    start = 0
    for ref, height in zip(out_refs, heights):
        ref[...] = acc_ref[start : start + height, :LIVE].astype(bf16)
        start += height
    if scales:
        terms = acc_ref[PIECE : PIECE + 8, :LIVE]
        scale = terms[0:1, :] + (terms[1:2, :] + terms[2:3, :])
        out_refs[-1][...] = jnp.broadcast_to(scale, (8, LIVE))


def pack(first, pieces, heights, scales=False, after=()):
    vmem = pl.BlockSpec(memory_space=pltpu.VMEM)
    n_rows = PIECE + EXTRA if scales else PIECE
    out_shape = [jax.ShapeDtypeStruct((height, LIVE), bf16) for height in heights]
    if scales:
        out_shape.append(jax.ShapeDtypeStruct((8, LIVE), f32))
    return pl.pallas_call(
        lambda *refs: pack_kernel(heights, scales, *refs),
        out_shape=tuple(out_shape),
        in_specs=[pl.BlockSpec(memory_space=pltpu.SMEM), vmem]
        + [pl.BlockSpec(memory_space=pl.ANY)] * len(after),
        out_specs=(vmem,) * len(out_shape),
        scratch_shapes=[pltpu.VMEM((n_rows, LIVE + SLOTS + 128), f32)],
        compiler_params=params(10),
        name="pack",
    )(first, pieces, *after)


def gram_kernel(rows_ref, cols_ref, scale_ref, gain_ref, own_ref, given_ref):
    normed = (cols_ref[...].astype(f32) * scale_ref[0:1, :] * gain_ref[...]).astype(bf16)
    product = lax.dot_general(
        rows_ref[...], normed, (((1,), (1,)), ((), ())), preferred_element_type=f32
    )
    own_ref[:256, :] = product[:256]
    given_ref[:256, :] = product[256:]
    sums = jnp.sum(normed.astype(f32), axis=1, keepdims=True)
    sums = jnp.broadcast_to(sums, (256, 128)).T[:8, :]
    own_ref[256:, :] = sums
    given_ref[256:, :] = sums


def gram(rows, cols, scale, gain):
    return pl.pallas_call(
        gram_kernel,
        out_shape=(jax.ShapeDtypeStruct((264, 256), f32),) * 2,
        in_specs=[pl.BlockSpec(memory_space=pltpu.VMEM)] * 4,
        out_specs=(pl.BlockSpec(memory_space=pltpu.VMEM),) * 2,
        compiler_params=params(16),
        cost_estimate=pl.CostEstimate(
            flops=2 * 512 * 256 * LIVE, bytes_accessed=6 * 1024 * 1024, transcendentals=0
        ),
        name="gram",
    )(rows, cols, scale, gain)


def finish_kernel(info_ref, part_ref, *refs):
    own, got, (mean_ref, out_ref) = refs[:4], refs[4:8], refs[8:]
    core, row_first, col_first = info_ref[0], info_ref[1], info_ref[2]
    part = part_ref[0]
    row = row_first + lax.broadcasted_iota(jnp.int32, (256, 256), 0)
    col = col_first + lax.broadcasted_iota(jnp.int32, (256, 256), 1)
    for s in range(4):

        @pl.when(pl.program_id(0) == s)
        def _():
            for ref, which in ((own[s], core), (got[s], 1 - core)):
                at = pl.multiple_of(which * 256, 256)
                values = jnp.where(row <= col + (s * 512 + at), ref[:256, :] * part, 0.0)
                out_ref[:, pl.ds(at, 256)] = values
                mean_ref[:, pl.ds(at, 256)] = ref[256:264, :][:1] * part


def finish(info, part, own, got):
    vmem = pl.BlockSpec(memory_space=pltpu.VMEM)
    return pl.pallas_call(
        finish_kernel,
        grid=(4,),
        out_shape=(
            jax.ShapeDtypeStruct((1, WIDTH), f32),
            jax.ShapeDtypeStruct((256, WIDTH), f32),
        ),
        in_specs=[pl.BlockSpec(memory_space=pltpu.SMEM)] * 2 + [vmem] * 8,
        out_specs=(pl.BlockSpec((1, 512), lambda s: (0, s)), pl.BlockSpec((256, 512), lambda s: (0, s))),
        compiler_params=params(10),
        name="finish",
    )(info, part, *own, *got)


def swap(value):
    return lax.ppermute(value, "c", [(0, 1), (1, 0)])


def trade(value, axis, flip):
    return lax.ppermute(value, axis, [(i, i ^ flip) for i in range(4)])


def join(*values):
    return jnp.concatenate(values, axis=0)


def meet(value, axis, flip, which):
    got = trade(value, axis, flip)
    return join(jnp.where(which == 0, value, got), jnp.where(which == 0, got, value))


def per_device(resid, norm_gain, keep_index, counts):
    z, x, c, y = (lax.axis_index(a) for a in ("z", "x", "c", "y"))
    place_y = y[None].astype(jnp.int32)
    pieces, *turns = pick(place_y, resid, norm_gain.reshape(8, SLOTS), keep_index, counts)
    pieces = lax.all_to_all(pieces, TOK, 0, 0, tiled=True)
    turns = [turns[0]] + [trade(turns[flip], "y", flip) for flip in (1, 2, 3)]
    panel = lax.all_to_all(panel_pieces(place_y, counts, turns), TOK, 0, 0, tiled=True)

    loads = pieces[:, PIECE, 0].astype(jnp.int32)
    first = jnp.cumsum(loads) - loads
    part = 1.0 / jnp.sum(loads).astype(f32)

    streams = list(pack(first, pieces, (16, 16, 16, 16)))
    for step in range(4):
        for s in range(4):
            axis, flip = PARTNERS[(s + step) % 4]
            seen = [PARTNERS[(s + k) % 4][0] for k in range(step)]
            which = side(x if axis == "x" else z, flip, axis not in seen)
            streams[s] = meet(streams[s], axis, flip, which)
        if step == 1:
            rows, scale = pack(first, panel, (PIECE,), scales=True, after=streams)

    rows = meet(rows, "y", 1, side(y, 1, True))
    rows = meet(rows, "y", 3, side(y, 3, False))
    rows = join(rows, swap(rows))

    gains = lax.dynamic_index_in_dim(norm_gain.reshape(4, 2, 256), c, 1, keepdims=False)[:, :, None]
    own, got = [], []
    for s in range(4):
        kept, given = gram(rows, streams[s], scale, gains[s])
        own.append(kept)
        got.append(swap(given))
    info = jnp.stack([c, (z * 8 + x * 2 + c) * 256, y * WIDTH]).astype(jnp.int32)
    mean, gram_factor = finish(info, part[None], own, got)
    return (mean[0], gram_factor)


def solution(mesh):
    fine = Mesh(mesh.devices.reshape(4, 4, 2, 4), ("z", "x", "c", "y"))
    return jax.shard_map(
        per_device,
        mesh=fine,
        in_specs=(P(TOK, "y"), P("y"), P(TOK), P(TOK)),
        out_specs=(P("y"), P(TOK, "y")),
        check_vma=False,
    )
```

time: 140 us -> 144 us (1.029)
  Pallas kernels: 16.4 us -> 20.8 us
  starting transfers between devices: 51.3 us -> 47.1 us
  other arithmetic: 6.7 us -> 9.32 us
    pallas_call x4, Pallas kernels: 5.11 us -> 8.61 us  [gram(): pl.pallas_call(gram_kernel, out_shape=(jax.ShapeDtypeStruct((264, 256), f...]
    ppermute x24 -> x21, starting transfers between devices: 28.8 us -> 25.3 us  [trade(): return lax.ppermute(value, axis, [(i, i ^ flip) for i in range(4)])]
    ppermute x24 -> x21, waiting for transfers between devices: 44.2 us -> 41.7 us  [trade(): return lax.ppermute(value, axis, [(i, i ^ flip) for i in range(4)])]
    select_n x18, other arithmetic: 3.24 us -> 5.5 us  [meet(): jnp.where(which == 0, value, got)]
    all_to_all x2, starting transfers between devices: 16.8 us -> 15.2 us  [the longest x1 9.57 us: per_device(): pieces = lax.all_to_all(pieces, TOK, 0, 0, tiled=True)]
    pallas_call x6 -> x5, Pallas kernels: 11.3 us -> 12.2 us  [the longest x2 4.8 us: pack(): pl.pallas_call(lambda *refs: pack_kernel(heights, scales, *refs), out_sha...]
    unnamed x10 -> x42, local copies, waits for them, and re-layouts: 2.93 us -> 3.78 us
  transfers between devices with their start and end apart: 31 -> 28, of which waited for: 21 -> 9; matrix products, arithmetic and copies ran while one was open for 5% -> 7% of each run, Pallas kernels for 4% -> 8%
where the time goes in v8:
time: 144 us; the launch traced here: 143 us
  waiting for transfers between devices  58.8 us (41%)
  starting transfers between devices  47.1 us (33%)
  Pallas kernels  20.8 us (14%)
  other arithmetic  9.32 us (6%)
  local copies, waits for them, and re-layouts  5.04 us (4%)
  between operations  2.04 us (1%)
    ppermute x21, waiting for transfers between devices, trade(): return lax.ppermute(value, axis, [(i, i ^ flip) for i in range(4)])  41.7 us
    ppermute x21, starting transfers between devices, trade(): return lax.ppermute(value, axis, [(i, i ^ flip) for i in range(4)])  25.3 us
    all_to_all x1, waiting for transfers between devices, per_device(): pieces = lax.all_to_all(pieces, TOK, 0, 0, tiled=True)  15.1 us
    all_to_all x1, starting transfers between devices, per_device(): pieces = lax.all_to_all(pieces, TOK, 0, 0, tiled=True)  9.57 us
    pallas_call x4, Pallas kernels, gram(): pl.pallas_call(gram_kernel, out_shape=(jax.ShapeDtypeStruct((264, 256), f...  8.61 us
    ppermute x5, starting transfers between devices, swap(): return lax.ppermute(value, 'c', [(0, 1), (1, 0)])  6.59 us
    all_to_all x1, starting transfers between devices, per_device(): lax.all_to_all(panel_pieces(place_y, counts, turns), TOK, 0, 0, tiled=True)  5.62 us
    select_n x18, other arithmetic, meet(): jnp.where(which == 0, value, got)  5.5 us
  transfers between devices with their start and end apart: 28, of which 9 were waited for; matrix products, arithmetic and copies ran while one was open for 7% of the time, Pallas kernels for 8%

profile of v8, /device:TPU:1, one launch (start us, length us, event | category | flops | bytes accessed | tf_op | source)
XLA Modules:
  0.0 143.1 jit_solution(2440007855689365216)
XLA Ops:
  0.6 0.7 reshape.52.gain_ref
  1.3 1.6 %copy-done = bf16[512,2048]{1,0:T(8,128)(2,1)S(1)} copy-done((bf16[512,2048]{1,0:T(8,128)(2,1)S(1)}, bf16[512,2048]{1,0:T(8,128)(2,1)}, u32[]{:S(2)}) %copy-start) | copy-done | bytes 2097176
  2.9 0.7 copy-done.1
  3.6 0.7 copy-done.3
  4.3 2.6 %pick.1 = (bf16[32,80,256]{2,1,0:T(8,128)(2,1)}, bf16[8,80,256]{2,1,0:T(8,128)(2,1)S(1)}, bf16[8,80,256]{2,1,0:T(8,128)(2,1)}, bf16[8,80,256]{2,1,0:T(8,128)(2,1)}, bf16[8,80,256]{2,1,0:T(8,128)(2,1)S(1)}) custom-call(s32[1]{0:T(128)} %bitcast.3.place_ref, s32[1,256]{1,0:T(1,128)S(1)} %bitcast.16, s32[2]{0:T(128)S(1)} %copy-done.1, ...), custom_call_target="tpu_custom_call" | custom-call | tf_op jit(solution)/shard_map/pick/pallas_call | solution.py:95
  6.9 9.6 %all-to-all-start = ((bf16[32,80,256]{2,1,0:T(8,128)(2,1)}), bf16[32,80,256]{2,1,0:T(8,128)(2,1)S(1)}, u32[]{:S(2)}, u32[]{:S(2)}) async-start(bf16[32,80,256]{2,1,0:T(8,128)(2,1)} %get-tuple-element.23), calls=%async_computation | async-start | bytes 2621440 | tf_op jit(solution)/shard_map/all_to_all | solution.py:270
  16.5 1.4 collective-permute-start
  17.8 2.6 %collective-permute-start.1 = (bf16[8,80,256]{2,1,0:T(8,128)(2,1)}, bf16[8,80,256]{2,1,0:T(8,128)(2,1)S(1)}, u32[]{:S(2)}, u32[]{:S(2)}) collective-permute-start(bf16[8,80,256]{2,1,0:T(8,128)(2,1)} %get-tuple-element.26), channel_id=1, source_target_pairs={{0,2},{1,3},{2,0},{3,1},{4,6},{5,7},{6,4},{7,5},{8,10},{9,11},{10,... | collective-permute-start | bytes 983048 | tf_op jit(solution)/shard_map/ppermute | solution.py:254
  20.5 15.1 %all-to-all-done.refs_1_ = bf16[32,80,256]{2,1,0:T(8,128)(2,1)S(1)} async-done(((bf16[32,80,256]{2,1,0:T(8,128)(2,1)}), bf16[32,80,256]{2,1,0:T(8,128)(2,1)S(1)}, u32[]{:S(2)}, u32[]{:S(2)}) %all-to-all-start) | async-done | bytes 1310752 | tf_op jit(solution)/shard_map/all_to_all | solution.py:270
  35.7 1.3 fusion
  37.0 1.9 %pack.2 = (bf16[16,4096]{1,0:T(8,128)(2,1)S(1)}, bf16[16,4096]{1,0:T(8,128)(2,1)S(1)}, bf16[16,4096]{1,0:T(8,128)(2,1)S(1)}, bf16[16,4096]{1,0:T(8,128)(2,1)S(1)}) custom-call(s32[32]{0:T(128)S(1)} %sub.3.refs_0_, bf16[32,80,256]{2,1,0:T(8,128)(2,1)S(1)} %all-to-all-done.refs_1_), custom_call_target="tpu_custom_call" | custom-call | tf_op jit(solution)/shard_map/pack/pallas_call | solution.py:177
  38.9 1.2 collective-permute-start.3
  40.2 2.3 %panel.1 = bf16[32,80,256]{2,1,0:T(8,128)(2,1)} custom-call(s32[1]{0:T(128)} %bitcast.3.place_ref, s32[2]{0:T(128)S(1)} %copy-done.2, bf16[8,80,256]{2,1,0:T(8,128)(2,1)S(1)} %get-tuple-element.24.t0, bf16[8,80,256]{2,1,0:T(8,128)(2,1)S(1)} %collective-permute-done.t1, bf16[8,80,256]{2,1,0:T(8,128)(2,1)S(1)} %collective-permute-done.1.t2, ...), custom_call_target="tpu_custom_call" | custom-call | tf_op jit(solution)/shard_map/panel/pallas_call | solution.py:130
  42.5 5.6 %all-to-all-start.1 = ((bf16[32,80,256]{2,1,0:T(8,128)(2,1)}), bf16[32,80,256]{2,1,0:T(8,128)(2,1)S(1)}, u32[]{:S(2)}, u32[]{:S(2)}) async-start(bf16[32,80,256]{2,1,0:T(8,128)(2,1)} %panel.1), calls=%async_computation.1 | async-start | bytes 2621440 | tf_op jit(solution)/shard_map/all_to_all | solution.py:272
  48.2 1.5 %collective-permute-start.5 = (bf16[16,4096]{1,0:T(8,128)(2,1)S(1)}, bf16[16,4096]{1,0:T(8,128)(2,1)S(1)}, u32[]{:S(2)}, u32[]{:S(2)}) collective-permute-start(bf16[16,4096]{1,0:T(8,128)(2,1)S(1)} %get-tuple-element.29), channel_id=1, source_target_pairs={{0,32},{32,0},{64,96},{96,64},{1,33},{33,1},{65,97},{97,65},{2,34}... | collective-permute-start | bytes 393224 | tf_op jit(solution)/shard_map/ppermute | solution.py:254
  49.6 2.4 %collective-permute-start.7 = (bf16[16,4096]{1,0:T(8,128)(2,1)S(1)}, bf16[16,4096]{1,0:T(8,128)(2,1)S(1)}, u32[]{:S(2)}, u32[]{:S(2)}) collective-permute-start(bf16[16,4096]{1,0:T(8,128)(2,1)S(1)} %get-tuple-element.30), channel_id=1, source_target_pairs={{0,24},{8,16},{16,8},{24,0},{1,25},{9,17},{17,9},{25,1},{2,26},{10... | collective-permute-start | bytes 393224 | tf_op jit(solution)/shard_map/ppermute | solution.py:254
  52.0 1.8 %collective-permute-start.9 = (bf16[16,4096]{1,0:T(8,128)(2,1)S(1)}, bf16[16,4096]{1,0:T(8,128)(2,1)S(1)}, u32[]{:S(2)}, u32[]{:S(2)}) collective-permute-start(bf16[16,4096]{1,0:T(8,128)(2,1)S(1)} %get-tuple-element.31), channel_id=1, source_target_pairs={{0,96},{32,64},{64,32},{96,0},{1,97},{33,65},{65,33},{97,1},{2,98}... | collective-permute-start | bytes 393224 | tf_op jit(solution)/shard_map/ppermute | solution.py:254
  53.8 0.9 broadcast_select_fusion.35
  55.2 11.6 %collective-permute-done.5 = bf16[16,4096]{1,0:T(8,128)(2,1)S(1)} collective-permute-done((bf16[16,4096]{1,0:T(8,128)(2,1)S(1)}, bf16[16,4096]{1,0:T(8,128)(2,1)S(1)}, u32[]{:S(2)}, u32[]{:S(2)}) %collective-permute-start.5) | collective-permute-done | bytes 131104 | tf_op jit(solution)/shard_map/ppermute | solution.py:254
  66.9 3.3 %collective-permute-start.6 = (bf16[32,4096]{1,0:T(8,128)(2,1)S(1)}, bf16[32,4096]{1,0:T(8,128)(2,1)S(1)}, u32[]{:S(2)}, u32[]{:S(2)}) collective-permute-start(bf16[32,4096]{1,0:T(8,128)(2,1)S(1)} %pad_maximum_fusion.16), channel_id=1, source_target_pairs={{0,24},{8,16},{16,8},{24,0},{1,25},{9,17},{17,9},{25,1},{2,26},{10... | collective-permute-start | bytes 786440 | tf_op jit(solution)/shard_map/ppermute | solution.py:254
  70.2 1.5 %collective-permute-start.8 = (bf16[32,4096]{1,0:T(8,128)(2,1)S(1)}, bf16[32,4096]{1,0:T(8,128)(2,1)S(1)}, u32[]{:S(2)}, u32[]{:S(2)}) collective-permute-start(bf16[32,4096]{1,0:T(8,128)(2,1)S(1)} %pad_maximum_fusion.17), channel_id=1, source_target_pairs={{0,96},{32,64},{64,32},{96,0},{1,97},{33,65},{65,33},{97,1},{2,98}... | collective-permute-start | bytes 786440 | tf_op jit(solution)/shard_map/ppermute | solution.py:254
  72.2 0.6 collective-permute-done.4
  73.0 2.2 %collective-permute-done.6 = bf16[32,4096]{1,0:T(8,128)(2,1)S(1)} collective-permute-done((bf16[32,4096]{1,0:T(8,128)(2,1)S(1)}, bf16[32,4096]{1,0:T(8,128)(2,1)S(1)}, u32[]{:S(2)}, u32[]{:S(2)}) %collective-permute-start.6) | collective-permute-done | bytes 262176 | tf_op jit(solution)/shard_map/ppermute | solution.py:254
  75.3 3.1 %collective-permute-done.8 = bf16[32,4096]{1,0:T(8,128)(2,1)S(1)} collective-permute-done((bf16[32,4096]{1,0:T(8,128)(2,1)S(1)}, bf16[32,4096]{1,0:T(8,128)(2,1)S(1)}, u32[]{:S(2)}, u32[]{:S(2)}) %collective-permute-start.8) | collective-permute-done | bytes 262176 | tf_op jit(solution)/shard_map/ppermute | solution.py:254
  79.7 2.9 %pack.3 = (bf16[64,4096]{1,0:T(8,128)(2,1)}, f32[8,4096]{1,0:T(8,128)S(1)}) custom-call(s32[32]{0:T(128)S(1)} %sub.3.refs_0_, bf16[32,80,256]{2,1,0:T(8,128)(2,1)S(1)} %all-to-all-done.1.refs_1_, bf16[64,4096]{1,0:T(8,128)(2,1)S(1)} %get-tuple-element.86.refs_2_, bf16[64,4096]{1,0:T(8,128)(2,1)S(1)} %get-tuple-element.87.refs_3_, ...), custom_call_target="tpu_custom_call" | custom-call | tf_op jit(solution)/shard_map/pack/pallas_call | solution.py:177
  83.6 0.9 collective-permute-start.14
  84.5 0.7 collective-permute-start.16
  85.2 0.6 collective-permute-start.18
  85.8 0.7 collective-permute-start.20
  86.5 7.8 %collective-permute-done.11 = bf16[64,4096]{1,0:T(8,128)(2,1)S(1)} collective-permute-done((bf16[64,4096]{1,0:T(8,128)(2,1)}, bf16[64,4096]{1,0:T(8,128)(2,1)S(1)}, u32[]{:S(2)}, u32[]{:S(2)}) %collective-permute-start.11) | collective-permute-done | bytes 524320 | tf_op jit(solution)/shard_map/ppermute | solution.py:254
  94.3 1.1 broadcast_select_fusion.19
  95.6 1.9 %collective-permute-start.12 = (bf16[128,4096]{1,0:T(8,128)(2,1)S(1)}, bf16[128,4096]{1,0:T(8,128)(2,1)S(1)}, u32[]{:S(2)}, u32[]{:S(2)}) collective-permute-start(bf16[128,4096]{1,0:T(8,128)(2,1)S(1)} %pad_maximum_fusion.6), channel_id=1, source_target_pairs={{0,3},{1,2},{2,1},{3,0},{4,7},{5,6},{6,5},{7,4},{8,11},{9,10},{10,... | collective-permute-start | bytes 3145736 | tf_op jit(solution)/shard_map/ppermute | solution.py:254
  97.8 0.8 collective-permute-start.15
  98.9 1.6 %collective-permute-start.17 = (bf16[128,4096]{1,0:T(8,128)(2,1)S(1)}, bf16[128,4096]{1,0:T(8,128)(2,1)S(1)}, u32[]{:S(2)}, u32[]{:S(2)}) collective-permute-start(bf16[128,4096]{1,0:T(8,128)(2,1)S(1)} %pad_maximum_fusion.8), channel_id=1, source_target_pairs={{0,8},{8,0},{16,24},{24,16},{1,9},{9,1},{17,25},{25,17},{2,10},{10... | collective-permute-start | bytes 3145736 | tf_op jit(solution)/shard_map/ppermute | solution.py:254
  101.2 1.2 collective-permute-start.21
  102.4 16.3 %collective-permute-done.12 = bf16[128,4096]{1,0:T(8,128)(2,1)S(1)} collective-permute-done((bf16[128,4096]{1,0:T(8,128)(2,1)S(1)}, bf16[128,4096]{1,0:T(8,128)(2,1)S(1)}, u32[]{:S(2)}, u32[]{:S(2)}) %collective-permute-start.12) | collective-permute-done | bytes 1048608 | tf_op jit(solution)/shard_map/ppermute | solution.py:254
  119.4 3.8 %collective-permute-start.13 = (bf16[256,4096]{1,0:T(8,128)(2,1)S(1)}, bf16[256,4096]{1,0:T(8,128)(2,1)S(1)}, u32[]{:S(2)}, u32[]{:S(2)}) collective-permute-start(bf16[256,4096]{1,0:T(8,128)(2,1)S(1)} %pad_maximum_fusion.1), channel_id=1, source_target_pairs={{0,4},{4,0},{1,5},{5,1},{2,6},{6,2},{3,7},{7,3},{8,12},{12,8},{9,1... | collective-permute-start | bytes 6291464 | tf_op jit(solution)/shard_map/ppermute | solution.py:250
  123.7 0.5 broadcast_select_fusion.5
  126.0 1.0 collective-permute-done.13
  127.0 0.5 pad_maximum_fusion.rows_ref
  127.5 2.0 %gram.4 = (f32[264,256]{1,0:T(8,128)S(1)}, f32[264,256]{1,0:T(8,128)S(1)}) custom-call(bf16[512,4096]{1,0:T(8,128)(2,1)S(1)} %pad_maximum_fusion.rows_ref, bf16[256,4096]{1,0:T(8,128)(2,1)S(1)} %pad_maximum_fusion.2.cols_ref, f32[8,4096]{1,0:T(8,128)S(1)} %get-tuple-element.33.scale_ref, f32[256,1]{1,0:T(8,128)S(1)} %copy.8.gain_ref), custom_call_target="tpu_custom_call" | custom-call | flops 1073741824 | bytes 6291456 | tf_op jit(solution)/shard_map/gram/pallas_call | solution.py:203
  129.5 2.1 %collective-permute-start.22 = (f32[264,256]{1,0:T(8,128)S(1)}, f32[264,256]{1,0:T(8,128)S(1)}, u32[]{:S(2)}, u32[]{:S(2)}) collective-permute-start(f32[264,256]{1,0:T(8,128)S(1)} %get-tuple-element.38), channel_id=1, source_target_pairs={{0,4},{4,0},{1,5},{5,1},{2,6},{6,2},{3,7},{7,3},{8,12},{12,8},{9,1... | collective-permute-start | bytes 811016 | tf_op jit(solution)/shard_map/ppermute | solution.py:250
  131.5 2.0 %gram.5 = (f32[264,256]{1,0:T(8,128)S(1)}, f32[264,256]{1,0:T(8,128)S(1)}) custom-call(bf16[512,4096]{1,0:T(8,128)(2,1)S(1)} %pad_maximum_fusion.rows_ref, bf16[256,4096]{1,0:T(8,128)(2,1)S(1)} %pad_maximum_fusion.3.cols_ref, f32[8,4096]{1,0:T(8,128)S(1)} %get-tuple-element.33.scale_ref, f32[256,1]{1,0:T(8,128)S(1)} %copy.9.gain_ref), custom_call_target="tpu_custom_call" | custom-call | flops 1073741824 | bytes 6291456 | tf_op jit(solution)/shard_map/gram/pallas_call | solution.py:203
  133.6 2.0 %gram.6 = (f32[264,256]{1,0:T(8,128)S(1)}, f32[264,256]{1,0:T(8,128)S(1)}) custom-call(bf16[512,4096]{1,0:T(8,128)(2,1)S(1)} %pad_maximum_fusion.rows_ref, bf16[256,4096]{1,0:T(8,128)(2,1)S(1)} %pad_maximum_fusion.4.cols_ref, f32[8,4096]{1,0:T(8,128)S(1)} %get-tuple-element.33.scale_ref, f32[256,1]{1,0:T(8,128)S(1)} %copy.10.gain_ref), custom_call_target="tpu_custom_call" | custom-call | flops 1073741824 | bytes 6291456 | tf_op jit(solution)/shard_map/gram/pallas_call | solution.py:203
  135.6 0.6 collective-permute-start.24
  136.2 2.7 %gram.7 = (f32[264,256]{1,0:T(8,128)S(1)}, f32[264,256]{1,0:T(8,128)}) custom-call(bf16[512,4096]{1,0:T(8,128)(2,1)S(1)} %pad_maximum_fusion.rows_ref, bf16[256,4096]{1,0:T(8,128)(2,1)S(1)} %pad_maximum_fusion.5.cols_ref, f32[8,4096]{1,0:T(8,128)S(1)} %get-tuple-element.33.scale_ref, f32[256,1]{1,0:T(8,128)S(1)} %copy.11.gain_ref), custom_call_target="tpu_custom_call" | custom-call | flops 1073741824 | bytes 6291456 | tf_op jit(solution)/shard_map/gram/pallas_call | solution.py:203
  139.7 0.9 collective-permute-done.25.refs_7_
  140.6 2.5 %finish.1 = (f32[1,2048]{1,0:T(1,128)}, f32[256,2048]{1,0:T(8,128)}) custom-call(s32[3]{0:T(128)S(1)} %pad_add_fusion.info_ref, f32[1]{0:T(128)} %bitcast.5.part_ref, f32[264,256]{1,0:T(8,128)S(1)} %get-tuple-element.34.refs_0_, f32[264,256]{1,0:T(8,128)S(1)} %get-tuple-element.35.refs_1_, f32[264,256]{1,0:T(8,128)S(1)} %get-tuple-element.36.refs_2_, ...), custom_call_target="tpu_custom_call" | custom-call | tf_op jit(solution)/shard_map/finish/pallas_call | solution.py:235
  (107 shorter events, 7.9 us)
Async XLA Ops:
  1.3 1.6 %copy-start = (bf16[512,2048]{1,0:T(8,128)(2,1)S(1)}, bf16[512,2048]{1,0:T(8,128)(2,1)}, u32[]{:S(2)}) copy-start(bf16[512,2048]{1,0:T(8,128)(2,1)} %resid_ref.1) | copy-start | bytes 6291460
  3.6 0.7 copy-start.3
  6.9 33.3 %copy-start.2 = (s32[2]{0:T(128)S(1)}, s32[2]{0:T(128)}, u32[]{:S(2)}) copy-start(s32[2]{0:T(128)} %counts_ref.3) | copy-start | bytes 28
  6.9 28.7 %all-to-all-start = ((bf16[32,80,256]{2,1,0:T(8,128)(2,1)}), bf16[32,80,256]{2,1,0:T(8,128)(2,1)S(1)}, u32[]{:S(2)}, u32[]{:S(2)}) async-start(bf16[32,80,256]{2,1,0:T(8,128)(2,1)} %get-tuple-element.23), calls=%async_computation | async-start | bytes 2621440 | tf_op jit(solution)/shard_map/all_to_all | solution.py:270
  16.5 23.7 %collective-permute-start = (bf16[8,80,256]{2,1,0:T(8,128)(2,1)}, bf16[8,80,256]{2,1,0:T(8,128)(2,1)S(1)}, u32[]{:S(2)}, u32[]{:S(2)}) collective-permute-start(bf16[8,80,256]{2,1,0:T(8,128)(2,1)} %get-tuple-element.25), channel_id=1, source_target_pairs={{0,1},{1,0},{2,3},{3,2},{4,5},{5,4},{6,7},{7,6},{8,9},{9,8},{10,11... | collective-permute-start | bytes 983048 | tf_op jit(solution)/shard_map/ppermute | solution.py:254
  17.8 22.4 %collective-permute-start.1 = (bf16[8,80,256]{2,1,0:T(8,128)(2,1)}, bf16[8,80,256]{2,1,0:T(8,128)(2,1)S(1)}, u32[]{:S(2)}, u32[]{:S(2)}) collective-permute-start(bf16[8,80,256]{2,1,0:T(8,128)(2,1)} %get-tuple-element.26), channel_id=1, source_target_pairs={{0,2},{1,3},{2,0},{3,1},{4,6},{5,7},{6,4},{7,5},{8,10},{9,11},{10,... | collective-permute-start | bytes 983048 | tf_op jit(solution)/shard_map/ppermute | solution.py:254
  20.5 19.7 %collective-permute-start.2 = (bf16[8,80,256]{2,1,0:T(8,128)(2,1)S(1)}, bf16[8,80,256]{2,1,0:T(8,128)(2,1)S(1)}, u32[]{:S(2)}, u32[]{:S(2)}) collective-permute-start(bf16[8,80,256]{2,1,0:T(8,128)(2,1)S(1)} %get-tuple-element.27), channel_id=1, source_target_pairs={{0,3},{1,2},{2,1},{3,0},{4,7},{5,6},{6,5},{7,4},{8,11},{9,10},{10,... | collective-permute-start | bytes 983048 | tf_op jit(solution)/shard_map/ppermute | solution.py:254
  38.9 14.9 %collective-permute-start.3 = (bf16[16,4096]{1,0:T(8,128)(2,1)S(1)}, bf16[16,4096]{1,0:T(8,128)(2,1)}, u32[]{:S(2)}, u32[]{:S(2)}) collective-permute-start(bf16[16,4096]{1,0:T(8,128)(2,1)S(1)} %get-tuple-element.28), channel_id=1, source_target_pairs={{0,8},{8,0},{16,24},{24,16},{1,9},{9,1},{17,25},{25,17},{2,10},{10... | collective-permute-start | bytes 393224 | tf_op jit(solution)/shard_map/ppermute | solution.py:254
  42.5 37.2 %all-to-all-start.1 = ((bf16[32,80,256]{2,1,0:T(8,128)(2,1)}), bf16[32,80,256]{2,1,0:T(8,128)(2,1)S(1)}, u32[]{:S(2)}, u32[]{:S(2)}) async-start(bf16[32,80,256]{2,1,0:T(8,128)(2,1)} %panel.1), calls=%async_computation.1 | async-start | bytes 2621440 | tf_op jit(solution)/shard_map/all_to_all | solution.py:272
  48.2 18.7 %collective-permute-start.5 = (bf16[16,4096]{1,0:T(8,128)(2,1)S(1)}, bf16[16,4096]{1,0:T(8,128)(2,1)S(1)}, u32[]{:S(2)}, u32[]{:S(2)}) collective-permute-start(bf16[16,4096]{1,0:T(8,128)(2,1)S(1)} %get-tuple-element.29), channel_id=1, source_target_pairs={{0,32},{32,0},{64,96},{96,64},{1,33},{33,1},{65,97},{97,65},{2,34}... | collective-permute-start | bytes 393224 | tf_op jit(solution)/shard_map/ppermute | solution.py:254
  49.6 20.5 %collective-permute-start.7 = (bf16[16,4096]{1,0:T(8,128)(2,1)S(1)}, bf16[16,4096]{1,0:T(8,128)(2,1)S(1)}, u32[]{:S(2)}, u32[]{:S(2)}) collective-permute-start(bf16[16,4096]{1,0:T(8,128)(2,1)S(1)} %get-tuple-element.30), channel_id=1, source_target_pairs={{0,24},{8,16},{16,8},{24,0},{1,25},{9,17},{17,9},{25,1},{2,26},{10... | collective-permute-start | bytes 393224 | tf_op jit(solution)/shard_map/ppermute | solution.py:254
  52.0 19.7 %collective-permute-start.9 = (bf16[16,4096]{1,0:T(8,128)(2,1)S(1)}, bf16[16,4096]{1,0:T(8,128)(2,1)S(1)}, u32[]{:S(2)}, u32[]{:S(2)}) collective-permute-start(bf16[16,4096]{1,0:T(8,128)(2,1)S(1)} %get-tuple-element.31), channel_id=1, source_target_pairs={{0,96},{32,64},{64,32},{96,0},{1,97},{33,65},{65,33},{97,1},{2,98}... | collective-permute-start | bytes 393224 | tf_op jit(solution)/shard_map/ppermute | solution.py:254
  54.8 18.1 %collective-permute-start.4 = (bf16[32,4096]{1,0:T(8,128)(2,1)S(1)}, bf16[32,4096]{1,0:T(8,128)(2,1)S(1)}, u32[]{:S(2)}, u32[]{:S(2)}) collective-permute-start(bf16[32,4096]{1,0:T(8,128)(2,1)S(1)} %pad_maximum_fusion.15), channel_id=1, source_target_pairs={{0,32},{32,0},{64,96},{96,64},{1,33},{33,1},{65,97},{97,65},{2,34}... | collective-permute-start | bytes 786440 | tf_op jit(solution)/shard_map/ppermute | solution.py:254
  66.9 8.3 %collective-permute-start.6 = (bf16[32,4096]{1,0:T(8,128)(2,1)S(1)}, bf16[32,4096]{1,0:T(8,128)(2,1)S(1)}, u32[]{:S(2)}, u32[]{:S(2)}) collective-permute-start(bf16[32,4096]{1,0:T(8,128)(2,1)S(1)} %pad_maximum_fusion.16), channel_id=1, source_target_pairs={{0,24},{8,16},{16,8},{24,0},{1,25},{9,17},{17,9},{25,1},{2,26},{10... | collective-permute-start | bytes 786440 | tf_op jit(solution)/shard_map/ppermute | solution.py:254
  70.2 8.2 %collective-permute-start.8 = (bf16[32,4096]{1,0:T(8,128)(2,1)S(1)}, bf16[32,4096]{1,0:T(8,128)(2,1)S(1)}, u32[]{:S(2)}, u32[]{:S(2)}) collective-permute-start(bf16[32,4096]{1,0:T(8,128)(2,1)S(1)} %pad_maximum_fusion.17), channel_id=1, source_target_pairs={{0,96},{32,64},{64,32},{96,0},{1,97},{33,65},{65,33},{97,1},{2,98}... | collective-permute-start | bytes 786440 | tf_op jit(solution)/shard_map/ppermute | solution.py:254
  71.8 6.9 %collective-permute-start.10 = (bf16[32,4096]{1,0:T(8,128)(2,1)S(1)}, bf16[32,4096]{1,0:T(8,128)(2,1)S(1)}, u32[]{:S(2)}, u32[]{:S(2)}) collective-permute-start(bf16[32,4096]{1,0:T(8,128)(2,1)S(1)} %pad_maximum_fusion.18), channel_id=1, source_target_pairs={{0,8},{8,0},{16,24},{24,16},{1,9},{9,1},{17,25},{25,17},{2,10},{10... | collective-permute-start | bytes 786440 | tf_op jit(solution)/shard_map/ppermute | solution.py:254
  73.0 5.7 %copy-start.16 = (bf16[32,4096]{1,0:T(8,128)(2,1)}, bf16[32,4096]{1,0:T(8,128)(2,1)S(1)}, u32[]{:S(2)}) copy-start(bf16[32,4096]{1,0:T(8,128)(2,1)S(1)} %get-tuple-element.72) | copy-start | bytes 786436
  73.0 5.7 %copy-start.18 = (bf16[32,4096]{1,0:T(8,128)(2,1)}, bf16[32,4096]{1,0:T(8,128)(2,1)S(1)}, u32[]{:S(2)}) copy-start(bf16[32,4096]{1,0:T(8,128)(2,1)S(1)} %get-tuple-element.73) | copy-start | bytes 786436
  75.3 3.3 %copy-start.12 = (bf16[32,4096]{1,0:T(8,128)(2,1)}, bf16[32,4096]{1,0:T(8,128)(2,1)S(1)}, u32[]{:S(2)}) copy-start(bf16[32,4096]{1,0:T(8,128)(2,1)S(1)} %get-tuple-element.70) | copy-start | bytes 786436
  75.3 3.3 %copy-start.14 = (bf16[32,4096]{1,0:T(8,128)(2,1)}, bf16[32,4096]{1,0:T(8,128)(2,1)S(1)}, u32[]{:S(2)}) copy-start(bf16[32,4096]{1,0:T(8,128)(2,1)S(1)} %get-tuple-element.71) | copy-start | bytes 786436
  78.5 0.7 copy-start.8
  78.5 0.8 copy-start.10
  78.8 0.7 copy-start.4
  78.8 0.8 copy-start.6
  79.7 3.3 %copy-start.20 = (f32[2048]{0:T(1024)S(1)}, f32[2048]{0:T(1024)}, u32[]{:S(2)}) copy-start(f32[2048]{0:T(1024)} %param.5) | copy-start | bytes 24580
  82.6 11.7 %collective-permute-start.11 = (bf16[64,4096]{1,0:T(8,128)(2,1)}, bf16[64,4096]{1,0:T(8,128)(2,1)S(1)}, u32[]{:S(2)}, u32[]{:S(2)}) collective-permute-start(bf16[64,4096]{1,0:T(8,128)(2,1)} %get-tuple-element.32), channel_id=1, source_target_pairs={{0,1},{1,0},{2,3},{3,2},{4,5},{5,4},{6,7},{7,6},{8,9},{9,8},{10,11... | collective-permute-start | bytes 1572872 | tf_op jit(solution)/shard_map/ppermute | solution.py:254
  83.6 13.8 %copy-start.17 = (bf16[32,4096]{1,0:T(8,128)(2,1)S(1)}, bf16[32,4096]{1,0:T(8,128)(2,1)}, u32[]{:S(2)}) copy-start(bf16[32,4096]{1,0:T(8,128)(2,1)} %copy-done.16) | copy-start | bytes 786436
  83.6 13.8 %copy-start.19 = (bf16[32,4096]{1,0:T(8,128)(2,1)S(1)}, bf16[32,4096]{1,0:T(8,128)(2,1)}, u32[]{:S(2)}) copy-start(bf16[32,4096]{1,0:T(8,128)(2,1)} %copy-done.18) | copy-start | bytes 786436
  83.6 13.8 %collective-permute-start.14 = (bf16[64,4096]{1,0:T(8,128)(2,1)S(1)}, bf16[64,4096]{1,0:T(8,128)(2,1)S(1)}, u32[]{:S(2)}, u32[]{:S(2)}) collective-permute-start(bf16[64,4096]{1,0:T(8,128)(2,1)S(1)} %get-tuple-element.86.refs_2_), channel_id=1, source_target_pairs={{0,24},{8,16},{16,8},{24,0},{1,25},{9,17},{17,9},{25,1},{2,26},{10... | collective-permute-start | bytes 1572872 | tf_op jit(solution)/shard_map/ppermute | solution.py:254
  84.5 14.1 %collective-permute-start.16 = (bf16[64,4096]{1,0:T(8,128)(2,1)S(1)}, bf16[64,4096]{1,0:T(8,128)(2,1)S(1)}, u32[]{:S(2)}, u32[]{:S(2)}) collective-permute-start(bf16[64,4096]{1,0:T(8,128)(2,1)S(1)} %get-tuple-element.87.refs_3_), channel_id=1, source_target_pairs={{0,96},{32,64},{64,32},{96,0},{1,97},{33,65},{65,33},{97,1},{2,98}... | collective-permute-start | bytes 1572872 | tf_op jit(solution)/shard_map/ppermute | solution.py:254
  85.2 15.3 %collective-permute-start.18 = (bf16[64,4096]{1,0:T(8,128)(2,1)S(1)}, bf16[64,4096]{1,0:T(8,128)(2,1)S(1)}, u32[]{:S(2)}, u32[]{:S(2)}) collective-permute-start(bf16[64,4096]{1,0:T(8,128)(2,1)S(1)} %get-tuple-element.88.refs_4_), channel_id=1, source_target_pairs={{0,8},{8,0},{16,24},{24,16},{1,9},{9,1},{17,25},{25,17},{2,10},{10... | collective-permute-start | bytes 1572872 | tf_op jit(solution)/shard_map/ppermute | solution.py:254
  85.8 15.1 %collective-permute-start.20 = (bf16[64,4096]{1,0:T(8,128)(2,1)S(1)}, bf16[64,4096]{1,0:T(8,128)(2,1)S(1)}, u32[]{:S(2)}, u32[]{:S(2)}) collective-permute-start(bf16[64,4096]{1,0:T(8,128)(2,1)S(1)} %get-tuple-element.89.refs_5_), channel_id=1, source_target_pairs={{0,32},{32,0},{64,96},{96,64},{1,33},{33,1},{65,97},{97,65},{2,34}... | collective-permute-start | bytes 1572872 | tf_op jit(solution)/shard_map/ppermute | solution.py:254
  95.5 3.0 %copy-start.13 = (bf16[32,4096]{1,0:T(8,128)(2,1)S(1)}, bf16[32,4096]{1,0:T(8,128)(2,1)}, u32[]{:S(2)}) copy-start(bf16[32,4096]{1,0:T(8,128)(2,1)} %copy-done.12) | copy-start | bytes 786436
  95.5 3.0 %copy-start.15 = (bf16[32,4096]{1,0:T(8,128)(2,1)S(1)}, bf16[32,4096]{1,0:T(8,128)(2,1)}, u32[]{:S(2)}) copy-start(bf16[32,4096]{1,0:T(8,128)(2,1)} %copy-done.14) | copy-start | bytes 786436
  95.6 23.1 %collective-permute-start.12 = (bf16[128,4096]{1,0:T(8,128)(2,1)S(1)}, bf16[128,4096]{1,0:T(8,128)(2,1)S(1)}, u32[]{:S(2)}, u32[]{:S(2)}) collective-permute-start(bf16[128,4096]{1,0:T(8,128)(2,1)S(1)} %pad_maximum_fusion.6), channel_id=1, source_target_pairs={{0,3},{1,2},{2,1},{3,0},{4,7},{5,6},{6,5},{7,4},{8,11},{9,10},{10,... | collective-permute-start | bytes 3145736 | tf_op jit(solution)/shard_map/ppermute | solution.py:254
  97.7 2.7 %copy-start.9 = (bf16[32,4096]{1,0:T(8,128)(2,1)S(1)}, bf16[32,4096]{1,0:T(8,128)(2,1)}, u32[]{:S(2)}) copy-start(bf16[32,4096]{1,0:T(8,128)(2,1)} %copy-done.8) | copy-start | bytes 786436
  97.8 2.7 %copy-start.11 = (bf16[32,4096]{1,0:T(8,128)(2,1)S(1)}, bf16[32,4096]{1,0:T(8,128)(2,1)}, u32[]{:S(2)}) copy-start(bf16[32,4096]{1,0:T(8,128)(2,1)} %copy-done.10) | copy-start | bytes 786436
  97.8 25.4 %collective-permute-start.15 = (bf16[128,4096]{1,0:T(8,128)(2,1)S(1)}, bf16[128,4096]{1,0:T(8,128)(2,1)S(1)}, u32[]{:S(2)}, u32[]{:S(2)}) collective-permute-start(bf16[128,4096]{1,0:T(8,128)(2,1)S(1)} %pad_maximum_fusion.7), channel_id=1, source_target_pairs={{0,96},{32,64},{64,32},{96,0},{1,97},{33,65},{65,33},{97,1},{2,98}... | collective-permute-start | bytes 3145736 | tf_op jit(solution)/shard_map/ppermute | solution.py:254
  98.9 2.0 %copy-start.5 = (bf16[32,4096]{1,0:T(8,128)(2,1)S(1)}, bf16[32,4096]{1,0:T(8,128)(2,1)}, u32[]{:S(2)}) copy-start(bf16[32,4096]{1,0:T(8,128)(2,1)} %copy-done.4) | copy-start | bytes 786436
  98.9 2.0 %copy-start.7 = (bf16[32,4096]{1,0:T(8,128)(2,1)S(1)}, bf16[32,4096]{1,0:T(8,128)(2,1)}, u32[]{:S(2)}) copy-start(bf16[32,4096]{1,0:T(8,128)(2,1)} %copy-done.6) | copy-start | bytes 786436
  98.9 24.8 %collective-permute-start.17 = (bf16[128,4096]{1,0:T(8,128)(2,1)S(1)}, bf16[128,4096]{1,0:T(8,128)(2,1)S(1)}, u32[]{:S(2)}, u32[]{:S(2)}) collective-permute-start(bf16[128,4096]{1,0:T(8,128)(2,1)S(1)} %pad_maximum_fusion.8), channel_id=1, source_target_pairs={{0,8},{8,0},{16,24},{24,16},{1,9},{9,1},{17,25},{25,17},{2,10},{10... | collective-permute-start | bytes 3145736 | tf_op jit(solution)/shard_map/ppermute | solution.py:254
  100.8 23.4 %collective-permute-start.19 = (bf16[128,4096]{1,0:T(8,128)(2,1)S(1)}, bf16[128,4096]{1,0:T(8,128)(2,1)S(1)}, u32[]{:S(2)}, u32[]{:S(2)}) collective-permute-start(bf16[128,4096]{1,0:T(8,128)(2,1)S(1)} %pad_maximum_fusion.9), channel_id=1, source_target_pairs={{0,32},{32,0},{64,96},{96,64},{1,33},{33,1},{65,97},{97,65},{2,34}... | collective-permute-start | bytes 3145736 | tf_op jit(solution)/shard_map/ppermute | solution.py:254
  101.2 24.1 %collective-permute-start.21 = (bf16[128,4096]{1,0:T(8,128)(2,1)S(1)}, bf16[128,4096]{1,0:T(8,128)(2,1)S(1)}, u32[]{:S(2)}, u32[]{:S(2)}) collective-permute-start(bf16[128,4096]{1,0:T(8,128)(2,1)S(1)} %pad_maximum_fusion.10), channel_id=1, source_target_pairs={{0,24},{8,16},{16,8},{24,0},{1,25},{9,17},{17,9},{25,1},{2,26},{10... | collective-permute-start | bytes 3145736 | tf_op jit(solution)/shard_map/ppermute | solution.py:254
  119.4 7.6 %collective-permute-start.13 = (bf16[256,4096]{1,0:T(8,128)(2,1)S(1)}, bf16[256,4096]{1,0:T(8,128)(2,1)S(1)}, u32[]{:S(2)}, u32[]{:S(2)}) collective-permute-start(bf16[256,4096]{1,0:T(8,128)(2,1)S(1)} %pad_maximum_fusion.1), channel_id=1, source_target_pairs={{0,4},{4,0},{1,5},{5,1},{2,6},{6,2},{3,7},{7,3},{8,12},{12,8},{9,1... | collective-permute-start | bytes 6291464 | tf_op jit(solution)/shard_map/ppermute | solution.py:250
  129.5 10.2 %collective-permute-start.22 = (f32[264,256]{1,0:T(8,128)S(1)}, f32[264,256]{1,0:T(8,128)S(1)}, u32[]{:S(2)}, u32[]{:S(2)}) collective-permute-start(f32[264,256]{1,0:T(8,128)S(1)} %get-tuple-element.38), channel_id=1, source_target_pairs={{0,4},{4,0},{1,5},{5,1},{2,6},{6,2},{3,7},{7,3},{8,12},{12,8},{9,1... | collective-permute-start | bytes 811016 | tf_op jit(solution)/shard_map/ppermute | solution.py:250
  133.5 6.2 %collective-permute-start.23 = (f32[264,256]{1,0:T(8,128)S(1)}, f32[264,256]{1,0:T(8,128)S(1)}, u32[]{:S(2)}, u32[]{:S(2)}) collective-permute-start(f32[264,256]{1,0:T(8,128)S(1)} %get-tuple-element.39), channel_id=1, source_target_pairs={{0,4},{4,0},{1,5},{5,1},{2,6},{6,2},{3,7},{7,3},{8,12},{12,8},{9,1... | collective-permute-start | bytes 811016 | tf_op jit(solution)/shard_map/ppermute | solution.py:250
  135.6 4.1 %collective-permute-start.24 = (f32[264,256]{1,0:T(8,128)S(1)}, f32[264,256]{1,0:T(8,128)S(1)}, u32[]{:S(2)}, u32[]{:S(2)}) collective-permute-start(f32[264,256]{1,0:T(8,128)S(1)} %get-tuple-element.40), channel_id=1, source_target_pairs={{0,4},{4,0},{1,5},{5,1},{2,6},{6,2},{3,7},{7,3},{8,12},{12,8},{9,1... | collective-permute-start | bytes 811016 | tf_op jit(solution)/shard_map/ppermute | solution.py:250
  138.9 1.8 %collective-permute-start.25 = (f32[264,256]{1,0:T(8,128)}, f32[264,256]{1,0:T(8,128)S(1)}, u32[]{:S(2)}, u32[]{:S(2)}) collective-permute-start(f32[264,256]{1,0:T(8,128)} %get-tuple-element.41), channel_id=1, source_target_pairs={{0,4},{4,0},{1,5},{5,1},{2,6},{6,2},{3,7},{7,3},{8,12},{12,8},{9,1... | collective-permute-start | bytes 811016 | tf_op jit(solution)/shard_map/ppermute | solution.py:250
  (1 other events, 0.7 us)

commit v9 on v8

--- a/solution.py
+++ b/solution.py
@@ -53,16 +53,14 @@
     return slot < jnp.where(slot < half, counts_ref[0], half + counts_ref[1])
 
 
-def pick_kernel(place_ref, index_ref, counts_ref, resid_ref, gain_ref, out_ref, *refs):
-    turn_refs, picked_ref = refs[:4], refs[4]
+def pick_kernel(index_ref, counts_ref, resid_ref, out_ref, picked_ref, sums_ref):
     tokens = resid_ref.shape[0]
     token = lax.broadcasted_iota(jnp.int32, (tokens, SLOTS), 0)
-    kept = jnp.where(live_slots(counts_ref), index_ref[...], -1)
+    live = live_slots(counts_ref)
+    kept = jnp.where(live, index_ref[...], -1)
     one_hot = jnp.where(token == kept, 1.0, 0.0).astype(bf16)
-    live = (counts_ref[0] + counts_ref[1]).astype(f32)
-    extra = jnp.full((EXTRA, SLOTS), live, f32).astype(bf16)
-    for t in range(32):
-        out_ref[t, PIECE:, :] = extra
+    row = lax.broadcasted_iota(jnp.int32, (16, 1), 0)
+    mark = jnp.where(row == 0, jnp.where(live, 0.0, jnp.inf), 0.0).astype(bf16)
     total = jnp.zeros((1, SLOTS), f32)
     for s in range(4):
         product = lax.dot_general(
@@ -78,30 +76,55 @@
             for z in range(4):
                 for x in range(4):
                     at = c * 256 + slot_of(s, x, z) * 16
-                    out_ref[z * 8 + x * 2 + c, s * 16 : (s + 1) * 16, :] = short[at : at + 16, :]
-    row = lax.broadcasted_iota(jnp.int32, (EXTRA, SLOTS), 0)
-    sum_terms = spread(total, row)
-    for k in range(8):
-        terms = jnp.where(row < 3, sum_terms, spread(gain_ref[k : k + 1, :], row - 3)).astype(bf16)
-        for flip, ref in enumerate(turn_refs):
-            first = pl.multiple_of((place_ref[0] ^ flip) * PIECE, PIECE)
-            ref[k, :PIECE, :] = picked_ref[pl.ds(k * 256 + first, PIECE), :]
-            ref[k, PIECE:, :] = terms
-
-
-def pick(place, resid, gain, keep_index, counts):
+                    part = short[at : at + 16, :]
+                    out_ref[z * 8 + x * 2 + c, s * 16 : (s + 1) * 16, :] = part + mark if s == 0 else part
+    sums_ref[...] = jnp.broadcast_to(total, (8, SLOTS))
+
+
+def pick(resid, keep_index, counts):
     vmem = pl.BlockSpec(memory_space=pltpu.VMEM)
     smem = pl.BlockSpec(memory_space=pltpu.SMEM)
     return pl.pallas_call(
         pick_kernel,
-        out_shape=(jax.ShapeDtypeStruct((32, PIECE + EXTRA, SLOTS), bf16),)
-        + (jax.ShapeDtypeStruct((8, PIECE + EXTRA, SLOTS), bf16),) * 4,
-        in_specs=[smem, vmem, smem, vmem, vmem],
-        out_specs=(vmem,) * 5,
-        scratch_shapes=[pltpu.VMEM((WIDTH, SLOTS), bf16)],
+        out_shape=(
+            jax.ShapeDtypeStruct((32, PIECE, SLOTS), bf16),
+            jax.ShapeDtypeStruct((WIDTH, SLOTS), bf16),
+            jax.ShapeDtypeStruct((8, SLOTS), f32),
+        ),
+        in_specs=[vmem, smem, vmem],
+        out_specs=(vmem,) * 3,
         compiler_params=params(16),
         name="pick",
-    )(place, keep_index[None, :], counts, resid, gain)
+    )(keep_index[None, :], counts, resid)
+
+
+def turn_kernel(place_ref, picked_ref, sums_ref, gain_ref, *turn_refs):
+    row = lax.broadcasted_iota(jnp.int32, (EXTRA, SLOTS), 0)
+    sum_terms = spread(sums_ref[:1, :], row)
+    for k in range(8):
+        gain = gain_ref[:, k * 256 : (k + 1) * 256]
+        terms = jnp.where(row < 3, sum_terms, spread(gain, row - 3)).astype(bf16)
+        for flip, ref in enumerate(turn_refs):
+            low, high = panel_rows(place_ref[0] ^ flip)
+            ref[k, :32, :] = picked_ref[pl.ds(k * 256 + low, 32), :]
+            ref[k, 32:PIECE, :] = picked_ref[pl.ds(k * 256 + high, 32), :]
+            ref[k, PIECE:, :] = terms
+
+
+def turn(place, picked, sums, gain):
+    vmem = pl.BlockSpec(memory_space=pltpu.VMEM)
+    return pl.pallas_call(
+        turn_kernel,
+        out_shape=(jax.ShapeDtypeStruct((8, PIECE + EXTRA, SLOTS), bf16),) * 4,
+        in_specs=[pl.BlockSpec(memory_space=pltpu.SMEM)] + [vmem] * 3,
+        out_specs=(vmem,) * 4,
+        compiler_params=params(10),
+        name="turn",
+    )(place, picked, sums, gain)
+
+
+def panel_rows(q):
+    return pl.multiple_of(q * 32, 32), pl.multiple_of(128 + (side(q, 1, False) * 2 + side(q, 3, True)) * 32, 32)
 
 
 def whole_terms(ref, k, first):
@@ -109,33 +132,37 @@
     return terms[first : first + 1, :] + (terms[first + 1 : first + 2, :] + terms[first + 2 : first + 3, :])
 
 
-def panel_kernel(place_ref, counts_ref, t0, t1, t2, t3, out_ref, gain_ref):
+def panel_kernel(place_ref, counts_ref, t0, t1, t2, t3, *refs):
+    out_ref, gain_ref = refs[-2:]
     sums = [whole_terms(ref, 0, 0) for ref in (t0, t1, t2, t3)]
     scale = lax.rsqrt(((sums[0] + sums[2]) + (sums[1] + sums[3])) / 8192 + epsilon)
     row = lax.broadcasted_iota(jnp.int32, (EXTRA, SLOTS), 0)
     extra = spread(jnp.where(live_slots(counts_ref), scale, 0.0), row).astype(bf16)
     y = place_ref[0]
-    first = pl.multiple_of(y * PIECE, PIECE)
+    low, high = panel_rows(y)
     for flip, turn in enumerate((t0, t1, t2, t3)):
         gains = [whole_terms(turn, k, 3) for k in range(8)]
         gain_ref[...] = jnp.concatenate(gains + [jnp.zeros((120, SLOTS), f32)], axis=0).T
         for k in range(8):
-            gain = gain_ref[pl.ds(first, PIECE), :][:, k : k + 1]
-            rows = turn[k, :PIECE, :].astype(f32)
-            out_ref[(y ^ flip) * 8 + k, :PIECE, :] = (rows * scale * gain).astype(bf16)
+            for at, first in ((0, low), (32, high)):
+                gain = gain_ref[pl.ds(first, 32), :][:, k : k + 1]
+                rows = turn[k, at : at + 32, :].astype(f32)
+                out_ref[(y ^ flip) * 8 + k, at : at + 32, :] = (rows * scale * gain).astype(bf16)
             out_ref[(y ^ flip) * 8 + k, PIECE:, :] = extra
 
 
-def panel_pieces(place, counts, turns):
+def panel_pieces(place, counts, turns, after):
     return pl.pallas_call(
         panel_kernel,
         out_shape=jax.ShapeDtypeStruct((32, PIECE + EXTRA, SLOTS), bf16),
-        in_specs=[pl.BlockSpec(memory_space=pltpu.SMEM)] * 2 + [pl.BlockSpec(memory_space=pltpu.VMEM)] * 4,
+        in_specs=[pl.BlockSpec(memory_space=pltpu.SMEM)] * 2
+        + [pl.BlockSpec(memory_space=pltpu.VMEM)] * 4
+        + [pl.BlockSpec(memory_space=pl.ANY)] * len(after),
         out_specs=pl.BlockSpec(memory_space=pltpu.VMEM),
         scratch_shapes=[pltpu.VMEM((SLOTS, 128), f32)],
         compiler_params=params(10),
         name="panel",
-    )(place, counts, *turns)
+    )(place, counts, *turns, *after)
 
 
 def pack_kernel(heights, scales, first_ref, in_ref, *refs):
@@ -149,6 +176,7 @@
         for k in range(group):
             t = g * group + k
             rows = in_ref[t, :n_rows, :].astype(f32)
+            rows = jnp.where(rows < jnp.inf, rows, 0.0)
             first = first_ref[t]
             base = pl.multiple_of((first // 128) * 128, 128)
             wide = jnp.concatenate([rows, jnp.zeros((n_rows, 128), f32)], axis=1)
@@ -168,7 +196,7 @@
         out_refs[-1][...] = jnp.broadcast_to(scale, (8, LIVE))
 
 
-def pack(first, pieces, heights, scales=False, after=()):
+def pack(first, pieces, heights, scales=False):
     vmem = pl.BlockSpec(memory_space=pltpu.VMEM)
     n_rows = PIECE + EXTRA if scales else PIECE
     out_shape = [jax.ShapeDtypeStruct((height, LIVE), bf16) for height in heights]
@@ -177,13 +205,12 @@
     return pl.pallas_call(
         lambda *refs: pack_kernel(heights, scales, *refs),
         out_shape=tuple(out_shape),
-        in_specs=[pl.BlockSpec(memory_space=pltpu.SMEM), vmem]
-        + [pl.BlockSpec(memory_space=pl.ANY)] * len(after),
+        in_specs=[pl.BlockSpec(memory_space=pltpu.SMEM), vmem],
         out_specs=(vmem,) * len(out_shape),
         scratch_shapes=[pltpu.VMEM((n_rows, LIVE + SLOTS + 128), f32)],
         compiler_params=params(10),
         name="pack",
-    )(first, pieces, *after)
+    )(first, pieces)
 
 
 def gram_kernel(rows_ref, cols_ref, scale_ref, gain_ref, own_ref, given_ref):
@@ -266,12 +293,12 @@
 def per_device(resid, norm_gain, keep_index, counts):
     z, x, c, y = (lax.axis_index(a) for a in ("z", "x", "c", "y"))
     place_y = y[None].astype(jnp.int32)
-    pieces, *turns = pick(place_y, resid, norm_gain.reshape(8, SLOTS), keep_index, counts)
+    pieces, picked, sums = pick(resid, keep_index, counts)
     pieces = lax.all_to_all(pieces, TOK, 0, 0, tiled=True)
+    turns = turn(place_y, picked, sums, norm_gain[None, :])
     turns = [turns[0]] + [trade(turns[flip], "y", flip) for flip in (1, 2, 3)]
-    panel = lax.all_to_all(panel_pieces(place_y, counts, turns), TOK, 0, 0, tiled=True)
-
-    loads = pieces[:, PIECE, 0].astype(jnp.int32)
+
+    loads = jnp.sum((pieces[:, 0, :] < jnp.inf).astype(jnp.int32), axis=1)
     first = jnp.cumsum(loads) - loads
     part = 1.0 / jnp.sum(loads).astype(f32)
 
@@ -283,10 +310,13 @@
             which = side(x if axis == "x" else z, flip, axis not in seen)
             streams[s] = meet(streams[s], axis, flip, which)
         if step == 1:
-            rows, scale = pack(first, panel, (PIECE,), scales=True, after=streams)
-
-    rows = meet(rows, "y", 1, side(y, 1, True))
-    rows = meet(rows, "y", 3, side(y, 3, False))
+            panel = panel_pieces(place_y, counts, turns, after=streams)
+            panel = lax.all_to_all(panel, TOK, 0, 0, tiled=True)
+
+    low, high, scale = pack(first, panel, (32, 32), scales=True)
+    low, high = meet(low, "y", 1, side(y, 1, True)), meet(high, "y", 3, side(y, 3, True))
+    low, high = meet(low, "y", 3, side(y, 3, False)), meet(high, "y", 1, side(y, 1, False))
+    rows = join(low, high)
     rows = join(rows, swap(rows))
 
     gains = lax.dynamic_index_in_dim(norm_gain.reshape(4, 2, 256), c, 1, keepdims=False)[:, :, None]

time: 144 us -> 155 us (1.076)
  blocking collectives: 0 us -> 26.4 us
  waiting for transfers between devices: 58.8 us -> 41.1 us
  other arithmetic: 9.32 us -> 18.3 us
  starting transfers between devices: 47.1 us -> 40.5 us
  Pallas kernels: 20.8 us -> 19.1 us
  local copies, waits for them, and re-layouts: 5.04 us -> 6.69 us
    all_to_all x0 -> x1, blocking collectives: none -> 26.4 us  [per_device(): pieces = lax.all_to_all(pieces, TOK, 0, 0, tiled=True)]
    ppermute x21 -> x23, waiting for transfers between devices: 41.7 us -> 31.3 us  [trade(): return lax.ppermute(value, axis, [(i, i ^ flip) for i in range(4)])]
    all_to_all x2 -> x1, waiting for transfers between devices: 15.1 us -> 6.35 us  [per_device(): panel = lax.all_to_all(panel, TOK, 0, 0, tiled=True)]
    select_n x18, other arithmetic: 5.5 us -> 11.1 us  [meet(): jnp.where(which == 0, value, got)]
    ppermute x5, starting transfers between devices: 6.59 us -> 3.01 us  [swap(): return lax.ppermute(value, 'c', [(0, 1), (1, 0)])]
    all_to_all x2 -> x1, starting transfers between devices: 15.2 us -> 12.2 us  [per_device(): panel = lax.all_to_all(panel, TOK, 0, 0, tiled=True)]
    concatenate x17, other arithmetic: 2.27 us -> 5.02 us  [join(): return jnp.concatenate(values, axis=0)]
    squeeze x5, local copies, waits for them, and re-layouts: 0.55 us -> 2.51 us  [per_device(): kept, given = gram(rows, streams[s], scale, gains[s])]
  transfers between devices with their start and end apart: 28 -> 29, of which waited for: 9 -> 14; matrix products, arithmetic and copies ran while one was open for 7% -> 13% of each run, Pallas kernels for 8% -> 7%
where the time goes in v9:
time: 155 us; the launch traced here: 154 us
  waiting for transfers between devices  41.1 us (27%)
  starting transfers between devices  40.5 us (26%)
  blocking collectives  26.4 us (17%)
  Pallas kernels  19.1 us (12%)
  other arithmetic  18.3 us (12%)
  local copies, waits for them, and re-layouts  6.69 us (4%)
  between operations  2.08 us (1%)
    ppermute x23, waiting for transfers between devices, trade(): return lax.ppermute(value, axis, [(i, i ^ flip) for i in range(4)])  31.3 us
    all_to_all x1, blocking collectives, per_device(): pieces = lax.all_to_all(pieces, TOK, 0, 0, tiled=True)  26.4 us
    ppermute x23, starting transfers between devices, trade(): return lax.ppermute(value, axis, [(i, i ^ flip) for i in range(4)])  25.3 us
    all_to_all x1, starting transfers between devices, per_device(): panel = lax.all_to_all(panel, TOK, 0, 0, tiled=True)  12.2 us
    select_n x18, other arithmetic, meet(): jnp.where(which == 0, value, got)  11.1 us
    pallas_call x4, Pallas kernels, gram(): pl.pallas_call(gram_kernel, out_shape=(jax.ShapeDtypeStruct((264, 256), f...  7.86 us
    all_to_all x1, waiting for transfers between devices, per_device(): panel = lax.all_to_all(panel, TOK, 0, 0, tiled=True)  6.35 us
    concatenate x17, other arithmetic, join(): return jnp.concatenate(values, axis=0)  5.02 us
  transfers between devices with their start and end apart: 29, of which 14 were waited for; matrix products, arithmetic and copies ran while one was open for 13% of the time, Pallas kernels for 7%

profile of v9, /device:TPU:1, one launch (start us, length us, event | category | flops | bytes accessed | tf_op | source)
XLA Modules:
  0.0 154.1 jit_solution(7838886237165780997)
XLA Ops:
  0.6 1.6 %copy-done = bf16[512,2048]{1,0:T(8,128)(2,1)S(1)} copy-done((bf16[512,2048]{1,0:T(8,128)(2,1)S(1)}, bf16[512,2048]{1,0:T(8,128)(2,1)}, u32[]{:S(2)}) %copy-start) | copy-done | bytes 2097176
  3.6 1.4 pick.1
  4.9 26.4 %all_to_all.10.refs_1_ = bf16[32,64,256]{2,1,0:T(8,128)(2,1)S(1)} all-to-all(bf16[32,64,256]{2,1,0:T(8,128)(2,1)S(1)} %get-tuple-element.26), channel_id=1, replica_groups=mesh['z'=4,'x'=4,'c'=2,'y'=4] {'z','x','c'}, dimensions={0} | all-to-all | bytes 2097152 | tf_op jit(solution)/shard_map/all_to_all | solution.py:297
  31.3 1.3 fusion
  32.9 1.9 %pack.2 = (bf16[16,4096]{1,0:T(8,128)(2,1)S(1)}, bf16[16,4096]{1,0:T(8,128)(2,1)S(1)}, bf16[16,4096]{1,0:T(8,128)(2,1)S(1)}, bf16[16,4096]{1,0:T(8,128)(2,1)S(1)}) custom-call(s32[32]{0:T(128)S(1)} %sub.3.refs_0_, bf16[32,64,256]{2,1,0:T(8,128)(2,1)S(1)} %all_to_all.10.refs_1_), custom_call_target="tpu_custom_call" | custom-call | tf_op jit(solution)/shard_map/pack/pallas_call | solution.py:205
  35.3 1.0 turn.1
  36.3 1.3 collective-permute-start
  37.6 2.6 %collective-permute-start.1 = (bf16[8,80,256]{2,1,0:T(8,128)(2,1)}, bf16[8,80,256]{2,1,0:T(8,128)(2,1)S(1)}, u32[]{:S(2)}, u32[]{:S(2)}) collective-permute-start(bf16[8,80,256]{2,1,0:T(8,128)(2,1)} %get-tuple-element.31), channel_id=1, source_target_pairs={{0,2},{1,3},{2,0},{3,1},{4,6},{5,7},{6,4},{7,5},{8,10},{9,11},{10,... | collective-permute-start | bytes 983048 | tf_op jit(solution)/shard_map/ppermute | solution.py:281
  44.2 2.8 %collective-permute-done.5 = bf16[16,4096]{1,0:T(8,128)(2,1)S(1)} collective-permute-done((bf16[16,4096]{1,0:T(8,128)(2,1)S(1)}, bf16[16,4096]{1,0:T(8,128)(2,1)S(1)}, u32[]{:S(2)}, u32[]{:S(2)}) %collective-permute-start.5) | collective-permute-done | bytes 131104 | tf_op jit(solution)/shard_map/ppermute | solution.py:281
  48.6 1.1 collective-permute-start.4
  49.7 2.6 %collective-permute-done.9 = bf16[16,4096]{1,0:T(8,128)(2,1)S(1)} collective-permute-done((bf16[16,4096]{1,0:T(8,128)(2,1)S(1)}, bf16[16,4096]{1,0:T(8,128)(2,1)S(1)}, u32[]{:S(2)}, u32[]{:S(2)}) %collective-permute-start.9) | collective-permute-done | bytes 131104 | tf_op jit(solution)/shard_map/ppermute | solution.py:281
  52.3 1.0 collective-permute-start.6
  53.3 1.1 collective-permute-done.4
  54.5 0.9 collective-permute-start.8
  55.5 3.2 %collective-permute-done.6 = bf16[32,4096]{1,0:T(8,128)(2,1)S(1)} collective-permute-done((bf16[32,4096]{1,0:T(8,128)(2,1)S(1)}, bf16[32,4096]{1,0:T(8,128)(2,1)S(1)}, u32[]{:S(2)}, u32[]{:S(2)}) %collective-permute-start.6) | collective-permute-done | bytes 262176 | tf_op jit(solution)/shard_map/ppermute | solution.py:281
  59.2 2.0 %collective-permute-done.8 = bf16[32,4096]{1,0:T(8,128)(2,1)S(1)} collective-permute-done((bf16[32,4096]{1,0:T(8,128)(2,1)S(1)}, bf16[32,4096]{1,0:T(8,128)(2,1)S(1)}, u32[]{:S(2)}, u32[]{:S(2)}) %collective-permute-start.8) | collective-permute-done | bytes 262176 | tf_op jit(solution)/shard_map/ppermute | solution.py:281
  62.0 2.3 %collective-permute-done.10 = bf16[32,4096]{1,0:T(8,128)(2,1)S(1)} collective-permute-done((bf16[32,4096]{1,0:T(8,128)(2,1)S(1)}, bf16[32,4096]{1,0:T(8,128)(2,1)S(1)}, u32[]{:S(2)}, u32[]{:S(2)}) %collective-permute-start.10) | collective-permute-done | bytes 262176 | tf_op jit(solution)/shard_map/ppermute | solution.py:281
  65.4 1.0 collective-permute-start.20
  66.5 2.3 %panel.1 = bf16[32,80,256]{2,1,0:T(8,128)(2,1)} custom-call(s32[1]{0:T(128)} %bitcast.6.place_ref, s32[2]{0:T(128)S(1)} %copy-done.6, bf16[8,80,256]{2,1,0:T(8,128)(2,1)S(1)} %get-tuple-element.29.t0, bf16[8,80,256]{2,1,0:T(8,128)(2,1)S(1)} %collective-permute-done.t1, bf16[8,80,256]{2,1,0:T(8,128)(2,1)S(1)} %collective-permute-done.1.t2, ...), custom_call_target="tpu_custom_call" | custom-call | tf_op jit(solution)/shard_map/panel/pallas_call | solution.py:155
  68.8 12.2 %all-to-all-start.1 = ((bf16[32,80,256]{2,1,0:T(8,128)(2,1)}), bf16[32,80,256]{2,1,0:T(8,128)(2,1)S(1)}, u32[]{:S(2)}, u32[]{:S(2)}) async-start(bf16[32,80,256]{2,1,0:T(8,128)(2,1)} %panel.1), calls=%async_computation.1 | async-start | bytes 2621440 | tf_op jit(solution)/shard_map/all_to_all | solution.py:314
  81.0 1.4 broadcast_select_fusion.15
  82.4 1.2 pad_maximum_fusion.5
  83.7 2.6 %collective-permute-start.17 = (bf16[128,4096]{1,0:T(8,128)(2,1)}, bf16[128,4096]{1,0:T(8,128)(2,1)}, u32[]{:S(2)}, u32[]{:S(2)}) collective-permute-start(bf16[128,4096]{1,0:T(8,128)(2,1)} %pad_maximum_fusion.5), channel_id=1, source_target_pairs={{0,96},{32,64},{64,32},{96,0},{1,97},{33,65},{65,33},{97,1},{2,98}... | collective-permute-start | bytes 3145736 | tf_op jit(solution)/shard_map/ppermute | solution.py:281
  86.3 1.2 broadcast_select_fusion.13
  87.6 1.2 pad_maximum_fusion.6
  88.8 1.2 collective-permute-start.19
  90.0 1.2 broadcast_select_fusion.11
  91.2 1.2 pad_maximum_fusion.7
  92.6 1.2 broadcast_select_fusion.9
  93.8 6.4 %all-to-all-done.1.refs_1_ = bf16[32,80,256]{2,1,0:T(8,128)(2,1)S(1)} async-done(((bf16[32,80,256]{2,1,0:T(8,128)(2,1)}), bf16[32,80,256]{2,1,0:T(8,128)(2,1)S(1)}, u32[]{:S(2)}, u32[]{:S(2)}) %all-to-all-start.1) | async-done | bytes 1310752 | tf_op jit(solution)/shard_map/all_to_all | solution.py:314
  100.1 2.1 %pack.3 = (bf16[32,4096]{1,0:T(8,128)(2,1)S(1)}, bf16[32,4096]{1,0:T(8,128)(2,1)S(1)}, f32[8,4096]{1,0:T(8,128)S(1)}) custom-call(s32[32]{0:T(128)S(1)} %sub.3.refs_0_, bf16[32,80,256]{2,1,0:T(8,128)(2,1)S(1)} %all-to-all-done.1.refs_1_), custom_call_target="tpu_custom_call" | custom-call | tf_op jit(solution)/shard_map/pack/pallas_call | solution.py:205
  102.8 2.7 %collective-permute-start.23 = (bf16[128,4096]{1,0:T(8,128)(2,1)S(1)}, bf16[128,4096]{1,0:T(8,128)(2,1)S(1)}, u32[]{:S(2)}, u32[]{:S(2)}) collective-permute-start(bf16[128,4096]{1,0:T(8,128)(2,1)S(1)} %pad_maximum_fusion.8), channel_id=1, source_target_pairs={{0,24},{8,16},{16,8},{24,0},{1,25},{9,17},{17,9},{25,1},{2,26},{10... | collective-permute-start | bytes 3145736 | tf_op jit(solution)/shard_map/ppermute | solution.py:281
  105.5 2.9 %collective-permute-done.11 = bf16[32,4096]{1,0:T(8,128)(2,1)S(1)} collective-permute-done((bf16[32,4096]{1,0:T(8,128)(2,1)S(1)}, bf16[32,4096]{1,0:T(8,128)(2,1)S(1)}, u32[]{:S(2)}, u32[]{:S(2)}) %collective-permute-start.11) | collective-permute-done | bytes 262176 | tf_op jit(solution)/shard_map/ppermute | solution.py:281
  108.4 2.8 %collective-permute-start.13 = (bf16[32,4096]{1,0:T(8,128)(2,1)S(1)}, bf16[32,4096]{1,0:T(8,128)(2,1)S(1)}, u32[]{:S(2)}, u32[]{:S(2)}) collective-permute-start(bf16[32,4096]{1,0:T(8,128)(2,1)S(1)} %get-tuple-element.38), channel_id=1, source_target_pairs={{0,3},{1,2},{2,1},{3,0},{4,7},{5,6},{6,5},{7,4},{8,11},{9,10},{10,... | collective-permute-start | bytes 786440 | tf_op jit(solution)/shard_map/ppermute | solution.py:281
  111.3 4.1 %collective-permute-done.13 = bf16[32,4096]{1,0:T(8,128)(2,1)S(1)} collective-permute-done((bf16[32,4096]{1,0:T(8,128)(2,1)S(1)}, bf16[32,4096]{1,0:T(8,128)(2,1)S(1)}, u32[]{:S(2)}, u32[]{:S(2)}) %collective-permute-start.13) | collective-permute-done | bytes 262176 | tf_op jit(solution)/shard_map/ppermute | solution.py:281
  115.4 2.7 %collective-permute-start.12 = (bf16[64,4096]{1,0:T(8,128)(2,1)S(1)}, bf16[64,4096]{1,0:T(8,128)(2,1)S(1)}, u32[]{:S(2)}, u32[]{:S(2)}) collective-permute-start(bf16[64,4096]{1,0:T(8,128)(2,1)S(1)} %pad_maximum_fusion.13), channel_id=1, source_target_pairs={{0,3},{1,2},{2,1},{3,0},{4,7},{5,6},{6,5},{7,4},{8,11},{9,10},{10,... | collective-permute-start | bytes 1572872 | tf_op jit(solution)/shard_map/ppermute | solution.py:281
  118.2 3.1 %collective-permute-done.17 = bf16[128,4096]{1,0:T(8,128)(2,1)} collective-permute-done((bf16[128,4096]{1,0:T(8,128)(2,1)}, bf16[128,4096]{1,0:T(8,128)(2,1)}, u32[]{:S(2)}, u32[]{:S(2)}) %collective-permute-start.17) | collective-permute-done | bytes 1048608 | tf_op jit(solution)/shard_map/ppermute | solution.py:281
  121.7 1.7 %broadcast_select_fusion.7 = (bf16[128,4096]{1,0:T(8,128)(2,1)S(1)}, bf16[128,4096]{1,0:T(8,128)(2,1)S(1)}) fusion(bf16[128,4096]{1,0:T(8,128)(2,1)} %collective-permute-done.17, pred[]{:T(512)S(6)} %eq.23, bf16[64,4096]{1,0:T(8,128)(2,1)S(1)} %copy-done.11, bf16[64,4096]{1,0:T(8,128)(2,1)S(1)} %copy-done.9), kind=kLoop, calls=%fused_computation.16 | loop fusion | flops 3145728 | bytes 4194305 | tf_op jit(solution)/shard_map/jit(_where)/select_n | solution.py:290
  123.4 1.8 %broadcast_select_fusion.5 = (bf16[128,4096]{1,0:T(8,128)(2,1)S(1)}, bf16[128,4096]{1,0:T(8,128)(2,1)S(1)}) fusion(bf16[128,4096]{1,0:T(8,128)(2,1)} %collective-permute-done.19, pred[]{:T(512)S(6)} %eq.25, bf16[64,4096]{1,0:T(8,128)(2,1)S(1)} %copy-done.15, bf16[64,4096]{1,0:T(8,128)(2,1)S(1)} %copy-done.13), kind=kLoop, calls=%fused_computation.14 | loop fusion | flops 3145728 | bytes 4194305 | tf_op jit(solution)/shard_map/jit(_where)/select_n | solution.py:290
  125.2 1.7 %broadcast_select_fusion.3 = (bf16[128,4096]{1,0:T(8,128)(2,1)S(1)}, bf16[128,4096]{1,0:T(8,128)(2,1)S(1)}) fusion(bf16[128,4096]{1,0:T(8,128)(2,1)} %collective-permute-done.21, pred[]{:T(512)S(6)} %eq.26, bf16[64,4096]{1,0:T(8,128)(2,1)S(1)} %copy-done.19, bf16[64,4096]{1,0:T(8,128)(2,1)S(1)} %copy-done.17), kind=kLoop, calls=%fused_computation.12 | loop fusion | flops 3145728 | bytes 4194305 | tf_op jit(solution)/shard_map/jit(_where)/select_n | solution.py:290
  127.5 6.6 %collective-permute-done.14 = bf16[64,4096]{1,0:T(8,128)(2,1)S(1)} collective-permute-done((bf16[64,4096]{1,0:T(8,128)(2,1)S(1)}, bf16[64,4096]{1,0:T(8,128)(2,1)S(1)}, u32[]{:S(2)}, u32[]{:S(2)}) %collective-permute-start.14) | collective-permute-done | bytes 524320 | tf_op jit(solution)/shard_map/ppermute | solution.py:281
  134.6 1.7 %collective-permute-start.15 = (bf16[256,4096]{1,0:T(8,128)(2,1)S(1)}, bf16[256,4096]{1,0:T(8,128)(2,1)S(1)}, u32[]{:S(2)}, u32[]{:S(2)}) collective-permute-start(bf16[256,4096]{1,0:T(8,128)(2,1)S(1)} %pad_maximum_fusion), channel_id=1, source_target_pairs={{0,4},{4,0},{1,5},{5,1},{2,6},{6,2},{3,7},{7,3},{8,12},{12,8},{9,1... | collective-permute-start | bytes 6291464 | tf_op jit(solution)/shard_map/ppermute | solution.py:277
  137.3 2.8 %collective-permute-done.15 = bf16[256,4096]{1,0:T(8,128)(2,1)S(1)} collective-permute-done((bf16[256,4096]{1,0:T(8,128)(2,1)S(1)}, bf16[256,4096]{1,0:T(8,128)(2,1)S(1)}, u32[]{:S(2)}, u32[]{:S(2)}) %collective-permute-start.15) | collective-permute-done | bytes 2097184 | tf_op jit(solution)/shard_map/ppermute | solution.py:277
  141.0 2.0 %gram.4 = (f32[264,256]{1,0:T(8,128)S(1)}, f32[264,256]{1,0:T(8,128)S(1)}) custom-call(bf16[512,4096]{1,0:T(8,128)(2,1)S(1)} %constant_dynamic-update-slice_fusion.rows_ref, bf16[256,4096]{1,0:T(8,128)(2,1)S(1)} %pad_maximum_fusion.1.cols_ref, f32[8,4096]{1,0:T(8,128)S(1)} %get-tuple-element.39.scale_ref, f32[256,1]{1,0:T(8,128)S(1)} %copy-done.3), custom_call_target="tpu_custom_call" | custom-call | flops 1073741824 | bytes 6291456 | tf_op jit(solution)/shard_map/gram/pallas_call | solution.py:230
  143.4 2.0 %gram.5 = (f32[264,256]{1,0:T(8,128)S(1)}, f32[264,256]{1,0:T(8,128)S(1)}) custom-call(bf16[512,4096]{1,0:T(8,128)(2,1)S(1)} %constant_dynamic-update-slice_fusion.rows_ref, bf16[256,4096]{1,0:T(8,128)(2,1)S(1)} %pad_maximum_fusion.2.cols_ref, f32[8,4096]{1,0:T(8,128)S(1)} %get-tuple-element.39.scale_ref, f32[256,1]{1,0:T(8,128)S(1)} %copy-done.2), custom_call_target="tpu_custom_call" | custom-call | flops 1073741824 | bytes 6291456 | tf_op jit(solution)/shard_map/gram/pallas_call | solution.py:230
  145.6 2.0 %gram.6 = (f32[264,256]{1,0:T(8,128)S(1)}, f32[264,256]{1,0:T(8,128)S(1)}) custom-call(bf16[512,4096]{1,0:T(8,128)(2,1)S(1)} %constant_dynamic-update-slice_fusion.rows_ref, bf16[256,4096]{1,0:T(8,128)(2,1)S(1)} %pad_maximum_fusion.3.cols_ref, f32[8,4096]{1,0:T(8,128)S(1)} %get-tuple-element.39.scale_ref, f32[256,1]{1,0:T(8,128)S(1)} %copy-done.1), custom_call_target="tpu_custom_call" | custom-call | flops 1073741824 | bytes 6291456 | tf_op jit(solution)/shard_map/gram/pallas_call | solution.py:230
  148.0 2.0 %gram.7 = (f32[264,256]{1,0:T(8,128)S(1)}, f32[264,256]{1,0:T(8,128)S(1)}) custom-call(bf16[512,4096]{1,0:T(8,128)(2,1)S(1)} %constant_dynamic-update-slice_fusion.rows_ref, bf16[256,4096]{1,0:T(8,128)(2,1)S(1)} %pad_maximum_fusion.4.cols_ref, f32[8,4096]{1,0:T(8,128)S(1)} %get-tuple-element.39.scale_ref, f32[256,1]{1,0:T(8,128)S(1)} %copy.11.gain_ref), custom_call_target="tpu_custom_call" | custom-call | flops 1073741824 | bytes 6291456 | tf_op jit(solution)/shard_map/gram/pallas_call | solution.py:230
  151.6 2.5 %finish.1 = (f32[1,2048]{1,0:T(1,128)}, f32[256,2048]{1,0:T(8,128)}) custom-call(s32[3]{0:T(128)S(1)} %pad_add_fusion.info_ref, f32[1]{0:T(128)} %bitcast.4.part_ref, f32[264,256]{1,0:T(8,128)S(1)} %get-tuple-element.40.refs_0_, f32[264,256]{1,0:T(8,128)S(1)} %get-tuple-element.41.refs_1_, f32[264,256]{1,0:T(8,128)S(1)} %get-tuple-element.42.refs_2_, ...), custom_call_target="tpu_custom_call" | custom-call | tf_op jit(solution)/shard_map/finish/pallas_call | solution.py:262
  (141 shorter events, 16.3 us)
Async XLA Ops:
  4.9 30.4 %copy-start.4 = (f32[2048]{0:T(1024)S(1)}, f32[2048]{0:T(1024)}, u32[]{:S(2)}) copy-start(f32[2048]{0:T(1024)} %param.5) | copy-start | bytes 24580
  34.8 8.4 %collective-permute-start.3 = (bf16[16,4096]{1,0:T(8,128)(2,1)S(1)}, bf16[16,4096]{1,0:T(8,128)(2,1)S(1)}, u32[]{:S(2)}, u32[]{:S(2)}) collective-permute-start(bf16[16,4096]{1,0:T(8,128)(2,1)S(1)} %get-tuple-element.33), channel_id=1, source_target_pairs={{0,8},{8,0},{16,24},{24,16},{1,9},{9,1},{17,25},{25,17},{2,10},{10... | collective-permute-start | bytes 393224 | tf_op jit(solution)/shard_map/ppermute | solution.py:281
  36.3 29.1 %collective-permute-start = (bf16[8,80,256]{2,1,0:T(8,128)(2,1)}, bf16[8,80,256]{2,1,0:T(8,128)(2,1)S(1)}, u32[]{:S(2)}, u32[]{:S(2)}) collective-permute-start(bf16[8,80,256]{2,1,0:T(8,128)(2,1)} %get-tuple-element.30), channel_id=1, source_target_pairs={{0,1},{1,0},{2,3},{3,2},{4,5},{5,4},{6,7},{7,6},{8,9},{9,8},{10,11... | collective-permute-start | bytes 983048 | tf_op jit(solution)/shard_map/ppermute | solution.py:281
  37.6 28.8 %collective-permute-start.1 = (bf16[8,80,256]{2,1,0:T(8,128)(2,1)}, bf16[8,80,256]{2,1,0:T(8,128)(2,1)S(1)}, u32[]{:S(2)}, u32[]{:S(2)}) collective-permute-start(bf16[8,80,256]{2,1,0:T(8,128)(2,1)} %get-tuple-element.31), channel_id=1, source_target_pairs={{0,2},{1,3},{2,0},{3,1},{4,6},{5,7},{6,4},{7,5},{8,10},{9,11},{10,... | collective-permute-start | bytes 983048 | tf_op jit(solution)/shard_map/ppermute | solution.py:281
  40.2 26.2 %collective-permute-start.2 = (bf16[8,80,256]{2,1,0:T(8,128)(2,1)}, bf16[8,80,256]{2,1,0:T(8,128)(2,1)S(1)}, u32[]{:S(2)}, u32[]{:S(2)}) collective-permute-start(bf16[8,80,256]{2,1,0:T(8,128)(2,1)} %get-tuple-element.32), channel_id=1, source_target_pairs={{0,3},{1,2},{2,1},{3,0},{4,7},{5,6},{6,5},{7,4},{8,11},{9,10},{10,... | collective-permute-start | bytes 983048 | tf_op jit(solution)/shard_map/ppermute | solution.py:281
  42.8 4.2 %collective-permute-start.5 = (bf16[16,4096]{1,0:T(8,128)(2,1)S(1)}, bf16[16,4096]{1,0:T(8,128)(2,1)S(1)}, u32[]{:S(2)}, u32[]{:S(2)}) collective-permute-start(bf16[16,4096]{1,0:T(8,128)(2,1)S(1)} %get-tuple-element.34), channel_id=1, source_target_pairs={{0,32},{32,0},{64,96},{96,64},{1,33},{33,1},{65,97},{97,65},{2,34}... | collective-permute-start | bytes 393224 | tf_op jit(solution)/shard_map/ppermute | solution.py:281
  43.3 5.3 %collective-permute-start.7 = (bf16[16,4096]{1,0:T(8,128)(2,1)S(1)}, bf16[16,4096]{1,0:T(8,128)(2,1)S(1)}, u32[]{:S(2)}, u32[]{:S(2)}) collective-permute-start(bf16[16,4096]{1,0:T(8,128)(2,1)S(1)} %get-tuple-element.35), channel_id=1, source_target_pairs={{0,24},{8,16},{16,8},{24,0},{1,25},{9,17},{17,9},{25,1},{2,26},{10... | collective-permute-start | bytes 393224 | tf_op jit(solution)/shard_map/ppermute | solution.py:281
  47.0 5.3 %collective-permute-start.9 = (bf16[16,4096]{1,0:T(8,128)(2,1)S(1)}, bf16[16,4096]{1,0:T(8,128)(2,1)S(1)}, u32[]{:S(2)}, u32[]{:S(2)}) collective-permute-start(bf16[16,4096]{1,0:T(8,128)(2,1)S(1)} %get-tuple-element.36), channel_id=1, source_target_pairs={{0,96},{32,64},{64,32},{96,0},{1,97},{33,65},{65,33},{97,1},{2,98}... | collective-permute-start | bytes 393224 | tf_op jit(solution)/shard_map/ppermute | solution.py:281
  48.6 5.9 %collective-permute-start.4 = (bf16[32,4096]{1,0:T(8,128)(2,1)S(1)}, bf16[32,4096]{1,0:T(8,128)(2,1)S(1)}, u32[]{:S(2)}, u32[]{:S(2)}) collective-permute-start(bf16[32,4096]{1,0:T(8,128)(2,1)S(1)} %pad_maximum_fusion.15), channel_id=1, source_target_pairs={{0,32},{32,0},{64,96},{96,64},{1,33},{33,1},{65,97},{97,65},{2,34}... | collective-permute-start | bytes 786440 | tf_op jit(solution)/shard_map/ppermute | solution.py:281
  52.3 6.4 %collective-permute-start.6 = (bf16[32,4096]{1,0:T(8,128)(2,1)S(1)}, bf16[32,4096]{1,0:T(8,128)(2,1)S(1)}, u32[]{:S(2)}, u32[]{:S(2)}) collective-permute-start(bf16[32,4096]{1,0:T(8,128)(2,1)S(1)} %pad_maximum_fusion.16), channel_id=1, source_target_pairs={{0,24},{8,16},{16,8},{24,0},{1,25},{9,17},{17,9},{25,1},{2,26},{10... | collective-permute-start | bytes 786440 | tf_op jit(solution)/shard_map/ppermute | solution.py:281
  54.5 6.7 %collective-permute-start.8 = (bf16[32,4096]{1,0:T(8,128)(2,1)S(1)}, bf16[32,4096]{1,0:T(8,128)(2,1)S(1)}, u32[]{:S(2)}, u32[]{:S(2)}) collective-permute-start(bf16[32,4096]{1,0:T(8,128)(2,1)S(1)} %pad_maximum_fusion.17), channel_id=1, source_target_pairs={{0,96},{32,64},{64,32},{96,0},{1,97},{33,65},{65,33},{97,1},{2,98}... | collective-permute-start | bytes 786440 | tf_op jit(solution)/shard_map/ppermute | solution.py:281
  55.5 9.8 %copy-start.24 = (bf16[32,4096]{1,0:T(8,128)(2,1)}, bf16[32,4096]{1,0:T(8,128)(2,1)S(1)}, u32[]{:S(2)}) copy-start(bf16[32,4096]{1,0:T(8,128)(2,1)S(1)} %get-tuple-element.86) | copy-start | bytes 786436
  55.5 9.8 %copy-start.25 = (bf16[32,4096]{1,0:T(8,128)(2,1)}, bf16[32,4096]{1,0:T(8,128)(2,1)S(1)}, u32[]{:S(2)}) copy-start(bf16[32,4096]{1,0:T(8,128)(2,1)S(1)} %get-tuple-element.87) | copy-start | bytes 786436
  58.8 5.5 %collective-permute-start.10 = (bf16[32,4096]{1,0:T(8,128)(2,1)S(1)}, bf16[32,4096]{1,0:T(8,128)(2,1)S(1)}, u32[]{:S(2)}, u32[]{:S(2)}) collective-permute-start(bf16[32,4096]{1,0:T(8,128)(2,1)S(1)} %pad_maximum_fusion.18), channel_id=1, source_target_pairs={{0,8},{8,0},{16,24},{24,16},{1,9},{9,1},{17,25},{25,17},{2,10},{10... | collective-permute-start | bytes 786440 | tf_op jit(solution)/shard_map/ppermute | solution.py:281
  59.1 6.1 %copy-start.20 = (bf16[32,4096]{1,0:T(8,128)(2,1)}, bf16[32,4096]{1,0:T(8,128)(2,1)S(1)}, u32[]{:S(2)}) copy-start(bf16[32,4096]{1,0:T(8,128)(2,1)S(1)} %get-tuple-element.84) | copy-start | bytes 786436
  59.1 6.1 %copy-start.22 = (bf16[32,4096]{1,0:T(8,128)(2,1)}, bf16[32,4096]{1,0:T(8,128)(2,1)S(1)}, u32[]{:S(2)}) copy-start(bf16[32,4096]{1,0:T(8,128)(2,1)S(1)} %get-tuple-element.85) | copy-start | bytes 786436
  61.2 5.3 %copy-start.6 = (s32[2]{0:T(128)S(1)}, s32[2]{0:T(128)}, u32[]{:S(2)}) copy-start(s32[2]{0:T(128)} %counts_ref.3) | copy-start | bytes 28
  61.2 19.8 %collective-permute-start.16 = (bf16[64,4096]{1,0:T(8,128)(2,1)S(1)}, bf16[64,4096]{1,0:T(8,128)(2,1)}, u32[]{:S(2)}, u32[]{:S(2)}) collective-permute-start(bf16[64,4096]{1,0:T(8,128)(2,1)S(1)} %get-tuple-element.100.refs_0_), channel_id=1, source_target_pairs={{0,24},{8,16},{16,8},{24,0},{1,25},{9,17},{17,9},{25,1},{2,26},{10... | collective-permute-start | bytes 1572872 | tf_op jit(solution)/shard_map/ppermute | solution.py:281
  62.0 4.5 %copy-start.30 = (bf16[32,4096]{1,0:T(8,128)(2,1)}, bf16[32,4096]{1,0:T(8,128)(2,1)S(1)}, u32[]{:S(2)}) copy-start(bf16[32,4096]{1,0:T(8,128)(2,1)S(1)} %get-tuple-element.82) | copy-start | bytes 786436
  62.0 4.5 %copy-start.32 = (bf16[32,4096]{1,0:T(8,128)(2,1)}, bf16[32,4096]{1,0:T(8,128)(2,1)S(1)}, u32[]{:S(2)}) copy-start(bf16[32,4096]{1,0:T(8,128)(2,1)S(1)} %get-tuple-element.83) | copy-start | bytes 786436
  64.3 22.0 %collective-permute-start.18 = (bf16[64,4096]{1,0:T(8,128)(2,1)S(1)}, bf16[64,4096]{1,0:T(8,128)(2,1)}, u32[]{:S(2)}, u32[]{:S(2)}) collective-permute-start(bf16[64,4096]{1,0:T(8,128)(2,1)S(1)} %get-tuple-element.101.refs_1_), channel_id=1, source_target_pairs={{0,96},{32,64},{64,32},{96,0},{1,97},{33,65},{65,33},{97,1},{2,98}... | collective-permute-start | bytes 1572872 | tf_op jit(solution)/shard_map/ppermute | solution.py:281
  65.4 24.6 %collective-permute-start.20 = (bf16[64,4096]{1,0:T(8,128)(2,1)S(1)}, bf16[64,4096]{1,0:T(8,128)(2,1)}, u32[]{:S(2)}, u32[]{:S(2)}) collective-permute-start(bf16[64,4096]{1,0:T(8,128)(2,1)S(1)} %get-tuple-element.102.refs_2_), channel_id=1, source_target_pairs={{0,8},{8,0},{16,24},{24,16},{1,9},{9,1},{17,25},{25,17},{2,10},{10... | collective-permute-start | bytes 1572872 | tf_op jit(solution)/shard_map/ppermute | solution.py:281
  66.4 26.0 %collective-permute-start.22 = (bf16[64,4096]{1,0:T(8,128)(2,1)S(1)}, bf16[64,4096]{1,0:T(8,128)(2,1)}, u32[]{:S(2)}, u32[]{:S(2)}) collective-permute-start(bf16[64,4096]{1,0:T(8,128)(2,1)S(1)} %get-tuple-element.103.refs_3_), channel_id=1, source_target_pairs={{0,32},{32,0},{64,96},{96,64},{1,33},{33,1},{65,97},{97,65},{2,34}... | collective-permute-start | bytes 1572872 | tf_op jit(solution)/shard_map/ppermute | solution.py:281
  68.8 31.3 %all-to-all-start.1 = ((bf16[32,80,256]{2,1,0:T(8,128)(2,1)}), bf16[32,80,256]{2,1,0:T(8,128)(2,1)S(1)}, u32[]{:S(2)}, u32[]{:S(2)}) async-start(bf16[32,80,256]{2,1,0:T(8,128)(2,1)} %panel.1), calls=%async_computation.1 | async-start | bytes 2621440 | tf_op jit(solution)/shard_map/all_to_all | solution.py:314
  81.0 5.3 %copy-start.21 = (bf16[32,4096]{1,0:T(8,128)(2,1)S(1)}, bf16[32,4096]{1,0:T(8,128)(2,1)}, u32[]{:S(2)}) copy-start(bf16[32,4096]{1,0:T(8,128)(2,1)} %copy-done.20) | copy-start | bytes 786436
  81.0 5.3 %copy-start.23 = (bf16[32,4096]{1,0:T(8,128)(2,1)S(1)}, bf16[32,4096]{1,0:T(8,128)(2,1)}, u32[]{:S(2)}) copy-start(bf16[32,4096]{1,0:T(8,128)(2,1)} %copy-done.22) | copy-start | bytes 786436
  82.4 5.1 %copy-start.8 = (bf16[64,4096]{1,0:T(8,128)(2,1)}, bf16[64,4096]{1,0:T(8,128)(2,1)S(1)}, u32[]{:S(2)}) copy-start(bf16[64,4096]{1,0:T(8,128)(2,1)S(1)} %get-tuple-element.74) | copy-start | bytes 1572868
  82.4 5.1 %copy-start.10 = (bf16[64,4096]{1,0:T(8,128)(2,1)}, bf16[64,4096]{1,0:T(8,128)(2,1)S(1)}, u32[]{:S(2)}) copy-start(bf16[64,4096]{1,0:T(8,128)(2,1)S(1)} %get-tuple-element.75) | copy-start | bytes 1572868
  83.6 6.3 %copy-start.31 = (bf16[32,4096]{1,0:T(8,128)(2,1)S(1)}, bf16[32,4096]{1,0:T(8,128)(2,1)}, u32[]{:S(2)}) copy-start(bf16[32,4096]{1,0:T(8,128)(2,1)} %copy-done.30) | copy-start | bytes 786436
  83.6 6.3 %copy-start.33 = (bf16[32,4096]{1,0:T(8,128)(2,1)S(1)}, bf16[32,4096]{1,0:T(8,128)(2,1)}, u32[]{:S(2)}) copy-start(bf16[32,4096]{1,0:T(8,128)(2,1)} %copy-done.32) | copy-start | bytes 786436
  83.7 37.7 %collective-permute-start.17 = (bf16[128,4096]{1,0:T(8,128)(2,1)}, bf16[128,4096]{1,0:T(8,128)(2,1)}, u32[]{:S(2)}, u32[]{:S(2)}) collective-permute-start(bf16[128,4096]{1,0:T(8,128)(2,1)} %pad_maximum_fusion.5), channel_id=1, source_target_pairs={{0,96},{32,64},{64,32},{96,0},{1,97},{33,65},{65,33},{97,1},{2,98}... | collective-permute-start | bytes 3145736 | tf_op jit(solution)/shard_map/ppermute | solution.py:281
  88.8 3.8 %copy-start.29 = (bf16[32,4096]{1,0:T(8,128)(2,1)S(1)}, bf16[32,4096]{1,0:T(8,128)(2,1)}, u32[]{:S(2)}) copy-start(bf16[32,4096]{1,0:T(8,128)(2,1)} %copy-done.28) | copy-start | bytes 786436
  88.8 34.6 %collective-permute-start.19 = (bf16[128,4096]{1,0:T(8,128)(2,1)}, bf16[128,4096]{1,0:T(8,128)(2,1)}, u32[]{:S(2)}, u32[]{:S(2)}) collective-permute-start(bf16[128,4096]{1,0:T(8,128)(2,1)} %pad_maximum_fusion.6), channel_id=1, source_target_pairs={{0,8},{8,0},{16,24},{24,16},{1,9},{9,1},{17,25},{25,17},{2,10},{10... | collective-permute-start | bytes 3145736 | tf_op jit(solution)/shard_map/ppermute | solution.py:281
  92.4 32.8 %collective-permute-start.21 = (bf16[128,4096]{1,0:T(8,128)(2,1)}, bf16[128,4096]{1,0:T(8,128)(2,1)}, u32[]{:S(2)}, u32[]{:S(2)}) collective-permute-start(bf16[128,4096]{1,0:T(8,128)(2,1)} %pad_maximum_fusion.7), channel_id=1, source_target_pairs={{0,32},{32,0},{64,96},{96,64},{1,33},{33,1},{65,97},{97,65},{2,34}... | collective-permute-start | bytes 3145736 | tf_op jit(solution)/shard_map/ppermute | solution.py:281
  102.3 6.1 %collective-permute-start.11 = (bf16[32,4096]{1,0:T(8,128)(2,1)S(1)}, bf16[32,4096]{1,0:T(8,128)(2,1)S(1)}, u32[]{:S(2)}, u32[]{:S(2)}) collective-permute-start(bf16[32,4096]{1,0:T(8,128)(2,1)S(1)} %get-tuple-element.37), channel_id=1, source_target_pairs={{0,1},{1,0},{2,3},{3,2},{4,5},{5,4},{6,7},{7,6},{8,9},{9,8},{10,11... | collective-permute-start | bytes 786440 | tf_op jit(solution)/shard_map/ppermute | solution.py:281
  102.8 33.9 %collective-permute-start.23 = (bf16[128,4096]{1,0:T(8,128)(2,1)S(1)}, bf16[128,4096]{1,0:T(8,128)(2,1)S(1)}, u32[]{:S(2)}, u32[]{:S(2)}) collective-permute-start(bf16[128,4096]{1,0:T(8,128)(2,1)S(1)} %pad_maximum_fusion.8), channel_id=1, source_target_pairs={{0,24},{8,16},{16,8},{24,0},{1,25},{9,17},{17,9},{25,1},{2,26},{10... | collective-permute-start | bytes 3145736 | tf_op jit(solution)/shard_map/ppermute | solution.py:281
  108.4 13.3 %copy-start.9 = (bf16[64,4096]{1,0:T(8,128)(2,1)S(1)}, bf16[64,4096]{1,0:T(8,128)(2,1)}, u32[]{:S(2)}) copy-start(bf16[64,4096]{1,0:T(8,128)(2,1)} %copy-done.8) | copy-start | bytes 1572868
  108.4 13.3 %copy-start.11 = (bf16[64,4096]{1,0:T(8,128)(2,1)S(1)}, bf16[64,4096]{1,0:T(8,128)(2,1)}, u32[]{:S(2)}) copy-start(bf16[64,4096]{1,0:T(8,128)(2,1)} %copy-done.10) | copy-start | bytes 1572868
  108.4 7.0 %collective-permute-start.13 = (bf16[32,4096]{1,0:T(8,128)(2,1)S(1)}, bf16[32,4096]{1,0:T(8,128)(2,1)S(1)}, u32[]{:S(2)}, u32[]{:S(2)}) collective-permute-start(bf16[32,4096]{1,0:T(8,128)(2,1)S(1)} %get-tuple-element.38), channel_id=1, source_target_pairs={{0,3},{1,2},{2,1},{3,0},{4,7},{5,6},{6,5},{7,4},{8,11},{9,10},{10,... | collective-permute-start | bytes 786440 | tf_op jit(solution)/shard_map/ppermute | solution.py:281
  115.4 11.7 %collective-permute-start.12 = (bf16[64,4096]{1,0:T(8,128)(2,1)S(1)}, bf16[64,4096]{1,0:T(8,128)(2,1)S(1)}, u32[]{:S(2)}, u32[]{:S(2)}) collective-permute-start(bf16[64,4096]{1,0:T(8,128)(2,1)S(1)} %pad_maximum_fusion.13), channel_id=1, source_target_pairs={{0,3},{1,2},{2,1},{3,0},{4,7},{5,6},{6,5},{7,4},{8,11},{9,10},{10,... | collective-permute-start | bytes 1572872 | tf_op jit(solution)/shard_map/ppermute | solution.py:281
  118.2 5.2 %copy-start.13 = (bf16[64,4096]{1,0:T(8,128)(2,1)S(1)}, bf16[64,4096]{1,0:T(8,128)(2,1)}, u32[]{:S(2)}) copy-start(bf16[64,4096]{1,0:T(8,128)(2,1)} %copy-done.12) | copy-start | bytes 1572868
  118.2 5.2 %copy-start.15 = (bf16[64,4096]{1,0:T(8,128)(2,1)S(1)}, bf16[64,4096]{1,0:T(8,128)(2,1)}, u32[]{:S(2)}) copy-start(bf16[64,4096]{1,0:T(8,128)(2,1)} %copy-done.14) | copy-start | bytes 1572868
  121.3 12.7 %collective-permute-start.14 = (bf16[64,4096]{1,0:T(8,128)(2,1)S(1)}, bf16[64,4096]{1,0:T(8,128)(2,1)S(1)}, u32[]{:S(2)}, u32[]{:S(2)}) collective-permute-start(bf16[64,4096]{1,0:T(8,128)(2,1)S(1)} %pad_maximum_fusion.14), channel_id=1, source_target_pairs={{0,1},{1,0},{2,3},{3,2},{4,5},{5,4},{6,7},{7,6},{8,9},{9,8},{10,11... | collective-permute-start | bytes 1572872 | tf_op jit(solution)/shard_map/ppermute | solution.py:281
  134.6 5.5 %collective-permute-start.15 = (bf16[256,4096]{1,0:T(8,128)(2,1)S(1)}, bf16[256,4096]{1,0:T(8,128)(2,1)S(1)}, u32[]{:S(2)}, u32[]{:S(2)}) collective-permute-start(bf16[256,4096]{1,0:T(8,128)(2,1)S(1)} %pad_maximum_fusion), channel_id=1, source_target_pairs={{0,4},{4,0},{1,5},{5,1},{2,6},{6,2},{3,7},{7,3},{8,12},{12,8},{9,1... | collective-permute-start | bytes 6291464 | tf_op jit(solution)/shard_map/ppermute | solution.py:277
  142.9 8.0 %collective-permute-start.24 = (f32[264,256]{1,0:T(8,128)S(1)}, f32[264,256]{1,0:T(8,128)S(1)}, u32[]{:S(2)}, u32[]{:S(2)}) collective-permute-start(f32[264,256]{1,0:T(8,128)S(1)} %get-tuple-element.44), channel_id=1, source_target_pairs={{0,4},{4,0},{1,5},{5,1},{2,6},{6,2},{3,7},{7,3},{8,12},{12,8},{9,1... | collective-permute-start | bytes 811016 | tf_op jit(solution)/shard_map/ppermute | solution.py:277
  145.4 5.6 %collective-permute-start.25 = (f32[264,256]{1,0:T(8,128)S(1)}, f32[264,256]{1,0:T(8,128)S(1)}, u32[]{:S(2)}, u32[]{:S(2)}) collective-permute-start(f32[264,256]{1,0:T(8,128)S(1)} %get-tuple-element.45), channel_id=1, source_target_pairs={{0,4},{4,0},{1,5},{5,1},{2,6},{6,2},{3,7},{7,3},{8,12},{12,8},{9,1... | collective-permute-start | bytes 811016 | tf_op jit(solution)/shard_map/ppermute | solution.py:277
  147.6 3.4 %collective-permute-start.26 = (f32[264,256]{1,0:T(8,128)S(1)}, f32[264,256]{1,0:T(8,128)S(1)}, u32[]{:S(2)}, u32[]{:S(2)}) collective-permute-start(f32[264,256]{1,0:T(8,128)S(1)} %get-tuple-element.46), channel_id=1, source_target_pairs={{0,4},{4,0},{1,5},{5,1},{2,6},{6,2},{3,7},{7,3},{8,12},{12,8},{9,1... | collective-permute-start | bytes 811016 | tf_op jit(solution)/shard_map/ppermute | solution.py:277
  150.0 1.6 %collective-permute-start.27 = (f32[264,256]{1,0:T(8,128)S(1)}, f32[264,256]{1,0:T(8,128)S(1)}, u32[]{:S(2)}, u32[]{:S(2)}) collective-permute-start(f32[264,256]{1,0:T(8,128)S(1)} %get-tuple-element.47), channel_id=1, source_target_pairs={{0,4},{4,0},{1,5},{5,1},{2,6},{6,2},{3,7},{7,3},{8,12},{12,8},{9,1... | collective-permute-start | bytes 811016 | tf_op jit(solution)/shard_map/ppermute | solution.py:277
  (15 other events, 28.6 us)

commit v10 on v9

v10 whole, which is shorter than its diff:
```python
import jax
import jax.numpy as jnp
from jax import lax
from jax.experimental import pallas as pl
from jax.experimental.pallas import tpu as pltpu
from jax.sharding import Mesh, PartitionSpec as P

epsilon = 1e-05
TOK = ("z", "x", "c")
SLOTS = 256
LIVE = 4096
WIDTH = 2048
PIECE = 64
LONG = LIVE + 128
MIB = 1024 * 1024
bf16 = jnp.bfloat16
f32 = jnp.float32


def params(mib):
    return pltpu.CompilerParams(vmem_limit_bytes=mib * MIB)


def spread(value, place):
    high = value.astype(bf16).astype(f32)
    middle = (value - high).astype(bf16).astype(f32)
    low = value - high - middle
    rest = jnp.where(place == 2, low, 0.0)
    return jnp.where(place == 0, high, jnp.where(place == 1, middle, rest))


PARTNERS = (("x", 1), ("z", 1), ("x", 3), ("z", 3))


def side(place, flip, first):
    if flip == 1 and not first:
        return (place ^ (place >> 1)) & 1
    return place & 1 if flip == 1 else place >> 1


def slot_of(s, x, z):
    at, seen = 0, []
    for step in range(4):
        axis, flip = PARTNERS[(s + step) % 4]
        at += side(x if axis == "x" else z, flip, axis not in seen) << step
        seen.append(axis)
    return at


def live_slots(counts_ref):
    slot = lax.broadcasted_iota(jnp.int32, (1, SLOTS), 1)
    half = SLOTS // 2
    return slot < jnp.where(slot < half, counts_ref[0], half + counts_ref[1])


def second_place(q):
    return side(q, 1, False) * 2 + side(q, 3, True)


def pick_kernel(index_ref, counts_ref, resid_ref, picked_ref, sums_ref):
    tokens = resid_ref.shape[0]
    token = lax.broadcasted_iota(jnp.int32, (tokens, SLOTS), 0)
    kept = jnp.where(live_slots(counts_ref), index_ref[...], -1)
    one_hot = jnp.where(token == kept, 1.0, 0.0).astype(bf16)
    total = jnp.zeros((1, SLOTS), f32)
    step = 512
    for k in range(WIDTH // step):
        part = lax.dot_general(
            resid_ref[:, k * step : (k + 1) * step],
            one_hot,
            (((0,), (0,)), ((), ())),
            preferred_element_type=f32,
        )
        total += jnp.sum(part * part, axis=0, keepdims=True)
        picked_ref[k * step : (k + 1) * step, :] = part.astype(bf16)
    sums_ref[...] = jnp.broadcast_to(total, sums_ref.shape)


def pick(resid, keep_index, counts):
    vmem = pl.BlockSpec(memory_space=pltpu.VMEM)
    return pl.pallas_call(
        pick_kernel,
        out_shape=(
            jax.ShapeDtypeStruct((WIDTH, SLOTS), bf16),
            jax.ShapeDtypeStruct((8, SLOTS), f32),
        ),
        in_specs=[vmem, pl.BlockSpec(memory_space=pltpu.SMEM), vmem],
        out_specs=(vmem,) * 2,
        compiler_params=params(16),
        name="pick",
    )(keep_index[None, :], counts, resid)


def norm_kernel(counts_ref, picked_ref, gain_ref, s0, s1, s2, s3, out_ref):
    squares = (s0[:1, :] + s2[:1, :]) + (s1[:1, :] + s3[:1, :])
    scale = lax.rsqrt(squares / 8192 + epsilon)
    row = lax.broadcasted_iota(jnp.int32, (32, 1), 0)
    mark = jnp.where(row == 0, jnp.where(live_slots(counts_ref), 0.0, jnp.inf), 0.0).astype(bf16)
    for x in range(4):
        for c in range(2):
            first = (x * 2 + c) * 256
            rows = picked_ref[first : first + 256, :].astype(f32)
            short = (rows * scale * gain_ref[first : first + 256, :]).astype(bf16)
            for z in range(4):
                low, high = z * 32, 128 + second_place(z) * 32
                out_ref[z * 8 + x * 2 + c, :32, :] = short[low : low + 32, :] + mark
                out_ref[z * 8 + x * 2 + c, 32:, :] = short[high : high + 32, :]


def norm(counts, picked, gain, sums):
    return pl.pallas_call(
        norm_kernel,
        out_shape=jax.ShapeDtypeStruct((32, PIECE, SLOTS), bf16),
        in_specs=[pl.BlockSpec(memory_space=pltpu.SMEM)] + [pl.BlockSpec(memory_space=pltpu.VMEM)] * 6,
        out_specs=pl.BlockSpec(memory_space=pltpu.VMEM),
        compiler_params=params(10),
        name="norm",
    )(counts, picked, gain, *sums)


def pack_kernel(first_ref, in_ref, *refs):
    out_refs, acc_ref = refs[:-1], refs[-1]
    acc_ref[...] = jnp.zeros_like(acc_ref)
    group = 4

    def body(g, _):
        moved = []
        for k in range(group):
            t = g * group + k
            rows = in_ref[t].astype(f32)
            rows = jnp.where(rows < jnp.inf, rows, 0.0)
            first = first_ref[t]
            base = pl.multiple_of((first // 128) * 128, 128)
            wide = jnp.concatenate([rows, jnp.zeros((PIECE, 128), f32)], axis=1)
            moved.append((base, pltpu.roll(wide, first - base, 1)))
        for base, rows in moved:
            acc_ref[:, pl.ds(base, SLOTS + 128)] += rows
        return 0

    lax.fori_loop(0, 32 // group, body, 0)
    whole_ref, part_refs = out_refs[0], out_refs[1:]
    rows = acc_ref[:, :LIVE]
    whole_ref[:, :LIVE] = rows.astype(bf16)
    lane = lax.broadcasted_iota(jnp.int32, (PIECE, 128), 1)
    whole_ref[:, LIVE:] = spread(jnp.sum(rows, axis=1, keepdims=True), lane).astype(bf16)
    for k, ref in enumerate(part_refs):
        ref[...] = whole_ref[k * 16 : (k + 1) * 16, :]


def pack(first, pieces):
    vmem = pl.BlockSpec(memory_space=pltpu.VMEM)
    return pl.pallas_call(
        pack_kernel,
        out_shape=(jax.ShapeDtypeStruct((PIECE, LONG), bf16),)
        + (jax.ShapeDtypeStruct((16, LONG), bf16),) * 4,
        in_specs=[pl.BlockSpec(memory_space=pltpu.SMEM), vmem],
        out_specs=(vmem,) * 5,
        scratch_shapes=[pltpu.VMEM((PIECE, LIVE + SLOTS + 128), f32)],
        compiler_params=params(10),
        name="pack",
    )(first, pieces)


def gram_kernel(blocks, rows_ref, *refs):
    streams, (own_ref, given_ref, cols_ref) = refs[:4], refs[4:]
    lane = lax.broadcasted_iota(jnp.int32, (16, 128), 1)
    terms = jnp.where(lane < 3, 1.0, 0.0).astype(bf16)
    for n, x in enumerate(blocks):
        for z in range(4):
            for s in range(4):
                at = (z if s < 2 else 4 + second_place(z)) * 32 + s % 2 * 16
                first = slot_of(s, x, z) * 16
                cols_ref[n * 256 + at : n * 256 + at + 16, :] = streams[s][first : first + 16, :]
        inside = slice(n * 256, (n + 1) * 256)
        product = lax.dot_general(
            rows_ref[:, :LIVE],
            cols_ref[inside, :LIVE],
            (((1,), (1,)), ((), ())),
            preferred_element_type=f32,
        )
        own_ref[:256, inside] = product[:256]
        given_ref[:256, inside] = product[256:]
        sums = lax.dot_general(
            terms, cols_ref[inside, LIVE:], (((1,), (1,)), ((), ())), preferred_element_type=f32
        )
        own_ref[256:, inside] = sums[:8]
        given_ref[256:, inside] = sums[:8]


def gram(blocks, rows, streams):
    vmem = pl.BlockSpec(memory_space=pltpu.VMEM)
    width = 256 * len(blocks)
    return pl.pallas_call(
        lambda *refs: gram_kernel(blocks, *refs),
        out_shape=(jax.ShapeDtypeStruct((264, width), f32),) * 2,
        in_specs=[vmem] * 5,
        out_specs=(vmem,) * 2,
        scratch_shapes=[pltpu.VMEM((width, LONG), bf16)],
        compiler_params=params(10),
        cost_estimate=pl.CostEstimate(
            flops=2 * 512 * width * LIVE, bytes_accessed=6 * 1024 * 1024, transcendentals=0
        ),
        name="gram",
    )(rows, *streams)


def finish_kernel(info_ref, part_ref, *refs):
    own, got, (mean_ref, out_ref) = refs[:2], refs[2:4], refs[4:]
    core, row_first, col_first = info_ref[0], info_ref[1], info_ref[2]
    part = part_ref[0]
    row = row_first + lax.broadcasted_iota(jnp.int32, (256, 256), 0)
    col = col_first + lax.broadcasted_iota(jnp.int32, (256, 256), 1)
    for x in range(4):
        inside = slice(x % 2 * 256, (x % 2 + 1) * 256)
        for ref, which in ((own[x // 2], core), (got[x // 2], 1 - core)):
            at = pl.multiple_of(x * 512 + which * 256, 256)
            out_ref[:, pl.ds(at, 256)] = jnp.where(row <= col + at, ref[:256, inside] * part, 0.0)
            mean_ref[:, pl.ds(at, 256)] = ref[256:264, inside][:1] * part


def finish(info, part, own, got):
    vmem = pl.BlockSpec(memory_space=pltpu.VMEM)
    return pl.pallas_call(
        finish_kernel,
        out_shape=(
            jax.ShapeDtypeStruct((1, WIDTH), f32),
            jax.ShapeDtypeStruct((256, WIDTH), f32),
        ),
        in_specs=[pl.BlockSpec(memory_space=pltpu.SMEM)] * 2 + [vmem] * 4,
        out_specs=(vmem,) * 2,
        compiler_params=params(10),
        name="finish",
    )(info, part, *own, *got)


def swap(value):
    return lax.ppermute(value, "c", [(0, 1), (1, 0)])


def trade(value, axis, flip):
    return lax.ppermute(value, axis, [(i, i ^ flip) for i in range(4)])


def join(*values):
    return jnp.concatenate(values, axis=0)


def meet(value, axis, flip, which):
    got = trade(value, axis, flip)
    return join(jnp.where(which == 0, value, got), jnp.where(which == 0, got, value))


def per_device(resid, norm_gain, keep_index, counts):
    z, x, c, y = (lax.axis_index(a) for a in ("z", "x", "c", "y"))
    picked, sums = pick(resid, keep_index, counts)
    all_sums = [sums] + [trade(sums, "y", flip) for flip in (1, 2, 3)]
    pieces = norm(counts, picked, norm_gain[:, None], all_sums)
    pieces = lax.all_to_all(pieces, TOK, 0, 0, tiled=True)

    loads = jnp.sum((pieces[:, 0, :] < jnp.inf).astype(jnp.int32), axis=1)
    first = jnp.cumsum(loads) - loads
    part = 1.0 / jnp.sum(loads).astype(f32)
    mine, *streams = pack(first, pieces)

    places = [(q, u) for q in range(4) for u in range(4)]
    turned = lax.ppermute(mine, ("z", "y"), [(q * 4 + u, u * 4 + (q ^ u)) for q, u in places])

    for step in range(4):
        for s in range(4):
            axis, flip = PARTNERS[(s + step) % 4]
            seen = [PARTNERS[(s + k) % 4][0] for k in range(step)]
            which = side(x if axis == "x" else z, flip, axis not in seen)
            streams[s] = meet(streams[s], axis, flip, which)

    q = y ^ z
    low, high = turned[:32], turned[32:]
    low, high = meet(low, "y", 1, side(q, 1, True)), meet(high, "y", 3, side(q, 3, True))
    low, high = meet(low, "y", 3, side(q, 3, False)), meet(high, "y", 1, side(q, 1, False))
    rows = join(low, high)
    rows = join(rows, swap(rows))

    own, got = [], []
    for blocks in ((0, 1), (2, 3)):
        kept, given = gram(blocks, rows, streams)
        own.append(kept)
        got.append(swap(given))
    info = jnp.stack([c, (z * 8 + x * 2 + c) * 256, y * WIDTH]).astype(jnp.int32)
    mean, gram_factor = finish(info, part[None], own, got)
    return (mean[0], gram_factor)


def solution(mesh):
    fine = Mesh(mesh.devices.reshape(4, 4, 2, 4), ("z", "x", "c", "y"))
    return jax.shard_map(
        per_device,
        mesh=fine,
        in_specs=(P(TOK, "y"), P("y"), P(TOK), P(TOK)),
        out_specs=(P("y"), P(TOK, "y")),
        check_vma=False,
    )
```

time: 155 us -> 133 us (0.86)
  other arithmetic: 18.3 us -> 6.37 us
  starting transfers between devices: 40.5 us -> 50 us
  waiting for transfers between devices: 41.1 us -> 32.1 us
  Pallas kernels: 19.1 us -> 11.3 us
  local copies, waits for them, and re-layouts: 6.69 us -> 3.7 us
    ppermute x23, starting transfers between devices: 25.3 us -> 40.8 us  [trade(): return lax.ppermute(value, axis, [(i, i ^ flip) for i in range(4)])]
    all_to_all x1 -> x0, starting transfers between devices: 12.2 us -> none  [per_device(): panel = lax.all_to_all(panel, TOK, 0, 0, tiled=True)]
    select_n x18 -> x17, other arithmetic: 11.1 us -> 2.8 us  [meet(): jnp.where(which == 0, value, got)]
    pallas_call x10 -> x6, Pallas kernels: 19.1 us -> 11.3 us  [the longest x2 4.8 us: gram(): pl.pallas_call(lambda *refs: gram_kernel(blocks, *refs), out_shape=(jax.S...]
    all_to_all x1 -> x0, waiting for transfers between devices: 6.35 us -> none  [per_device(): panel = lax.all_to_all(panel, TOK, 0, 0, tiled=True)]
    ppermute x5 -> x3, starting transfers between devices: 3.01 us -> 8.59 us  [swap(): return lax.ppermute(value, 'c', [(0, 1), (1, 0)])]
    concatenate x17, other arithmetic: 5.02 us -> 1.4 us  [join(): return jnp.concatenate(values, axis=0)]
    squeeze x5 -> x0, local copies, waits for them, and re-layouts: 2.51 us -> none  [per_device(): kept, given = gram(rows, streams[s], scale, gains[s])]
  transfers between devices with their start and end apart: 29 -> 27, of which waited for: 14 -> 13; matrix products, arithmetic and copies ran while one was open for 13% -> 4% of each run, Pallas kernels for 7% -> 0%
where the time goes in v10:
time: 133 us; the launch traced here: 132 us
  starting transfers between devices  50 us (38%)
  waiting for transfers between devices  32.1 us (24%)
  blocking collectives  27.3 us (21%)
  Pallas kernels  11.3 us (8%)
  other arithmetic  6.37 us (5%)
  local copies, waits for them, and re-layouts  3.7 us (3%)
  between operations  1.61 us (1%)
    ppermute x23, starting transfers between devices, trade(): return lax.ppermute(value, axis, [(i, i ^ flip) for i in range(4)])  40.8 us
    ppermute x23, waiting for transfers between devices, trade(): return lax.ppermute(value, axis, [(i, i ^ flip) for i in range(4)])  30.6 us
    all_to_all x1, blocking collectives, per_device(): pieces = lax.all_to_all(pieces, TOK, 0, 0, tiled=True)  27.3 us
    ppermute x3, starting transfers between devices, swap(): return lax.ppermute(value, 'c', [(0, 1), (1, 0)])  8.59 us
    pallas_call x2, Pallas kernels, gram(): pl.pallas_call(lambda *refs: gram_kernel(blocks, *refs), out_shape=(jax.S...  4.8 us
    unnamed x10, local copies, waits for them, and re-layouts  2.92 us
    select_n x17, other arithmetic, meet(): jnp.where(which == 0, value, got)  2.8 us
  transfers between devices with their start and end apart: 27, of which 13 were waited for; matrix products, arithmetic and copies ran while one was open for 4% of the time, Pallas kernels for 0%

profile of v10, /device:TPU:1, one launch (start us, length us, event | category | flops | bytes accessed | tf_op | source)
XLA Modules:
  0.0 132.4 jit_solution(405990010988351645)
XLA Ops:
  0.6 1.6 %copy-done = bf16[512,2048]{1,0:T(8,128)(2,1)S(1)} copy-done((bf16[512,2048]{1,0:T(8,128)(2,1)S(1)}, bf16[512,2048]{1,0:T(8,128)(2,1)}, u32[]{:S(2)}) %copy-start) | copy-done | bytes 2097176
  2.2 0.7 copy-done.1
  2.9 0.7 copy-done.3
  3.6 1.3 %pick.1 = (bf16[2048,256]{1,0:T(8,128)(2,1)S(1)}, f32[8,256]{1,0:T(8,128)S(1)}) custom-call(s32[1,256]{1,0:T(1,128)S(1)} %bitcast.8, s32[2]{0:T(128)S(1)} %copy-done.1, bf16[512,2048]{1,0:T(8,128)(2,1)S(1)} %copy-done), custom_call_target="tpu_custom_call" | custom-call | tf_op jit(solution)/shard_map/pick/pallas_call | solution.py:81
  4.9 2.2 %collective-permute-start = (f32[8,256]{1,0:T(8,128)S(1)}, f32[8,256]{1,0:T(8,128)S(1)}, u32[]{:S(2)}, u32[]{:S(2)}) collective-permute-start(f32[8,256]{1,0:T(8,128)S(1)} %get-tuple-element.16.s0), channel_id=1, source_target_pairs={{0,1},{1,0},{2,3},{3,2},{4,5},{5,4},{6,7},{7,6},{8,9},{9,8},{10,11... | collective-permute-start | bytes 24584 | tf_op jit(solution)/shard_map/ppermute | solution.py:241
  7.1 2.6 %collective-permute-start.1 = (f32[8,256]{1,0:T(8,128)S(1)}, f32[8,256]{1,0:T(8,128)S(1)}, u32[]{:S(2)}, u32[]{:S(2)}) collective-permute-start(f32[8,256]{1,0:T(8,128)S(1)} %get-tuple-element.16.s0), channel_id=1, source_target_pairs={{0,2},{1,3},{2,0},{3,1},{4,6},{5,7},{6,4},{7,5},{8,10},{9,11},{10,... | collective-permute-start | bytes 24584 | tf_op jit(solution)/shard_map/ppermute | solution.py:241
  10.1 1.0 collective-permute-done.1.s2
  11.1 2.3 %collective-permute-done.2.s3 = f32[8,256]{1,0:T(8,128)S(1)} collective-permute-done((f32[8,256]{1,0:T(8,128)S(1)}, f32[8,256]{1,0:T(8,128)S(1)}, u32[]{:S(2)}, u32[]{:S(2)}) %collective-permute-start.2) | collective-permute-done | bytes 8224 | tf_op jit(solution)/shard_map/ppermute | solution.py:241
  13.5 0.9 norm.1
  14.3 27.3 %all_to_all.5.in_ref = bf16[32,64,256]{2,1,0:T(8,128)(2,1)S(1)} all-to-all(bf16[32,64,256]{2,1,0:T(8,128)(2,1)S(1)} %norm.1), channel_id=1, replica_groups=mesh['z'=4,'x'=4,'c'=2,'y'=4] {'z','x','c'}, dimensions={0} | all-to-all | bytes 2097152 | tf_op jit(solution)/shard_map/all_to_all | solution.py:258
  41.6 1.3 fusion
  43.2 2.1 %pack.1 = (bf16[64,4224]{1,0:T(8,128)(2,1)S(1)}, bf16[16,4224]{1,0:T(8,128)(2,1)S(1)}, bf16[16,4224]{1,0:T(8,128)(2,1)S(1)}, bf16[16,4224]{1,0:T(8,128)(2,1)S(1)}, bf16[16,4224]{1,0:T(8,128)(2,1)S(1)}) custom-call(s32[32]{0:T(128)S(1)} %sub.3.first_ref, bf16[32,64,256]{2,1,0:T(8,128)(2,1)S(1)} %all_to_all.5.in_ref), custom_call_target="tpu_custom_call" | custom-call | tf_op jit(solution)/shard_map/pack/pallas_call | solution.py:152
  45.2 0.4 collective-permute-start.9
  45.7 0.7 collective-permute-start.3
  46.4 1.7 %collective-permute-start.13 = (bf16[16,4224]{1,0:T(8,128)(2,1)S(1)}, bf16[16,4224]{1,0:T(8,128)(2,1)S(1)}, u32[]{:S(2)}, u32[]{:S(2)}) collective-permute-start(bf16[16,4224]{1,0:T(8,128)(2,1)S(1)} %get-tuple-element.19), channel_id=1, source_target_pairs={{0,32},{32,0},{64,96},{96,64},{1,33},{33,1},{65,97},{97,65},{2,34}... | collective-permute-start | bytes 405512 | tf_op jit(solution)/shard_map/ppermute | solution.py:241
  48.0 0.9 collective-permute-start.17
  49.0 2.6 %collective-permute-start.21 = (bf16[16,4224]{1,0:T(8,128)(2,1)S(1)}, bf16[16,4224]{1,0:T(8,128)(2,1)S(1)}, u32[]{:S(2)}, u32[]{:S(2)}) collective-permute-start(bf16[16,4224]{1,0:T(8,128)(2,1)S(1)} %get-tuple-element.21), channel_id=1, source_target_pairs={{0,96},{32,64},{64,32},{96,0},{1,97},{33,65},{65,33},{97,1},{2,98}... | collective-permute-start | bytes 405512 | tf_op jit(solution)/shard_map/ppermute | solution.py:241
  52.1 1.8 %collective-permute-start.14 = (bf16[32,4224]{1,0:T(8,128)(2,1)S(1)}, bf16[32,4224]{1,0:T(8,128)(2,1)S(1)}, u32[]{:S(2)}, u32[]{:S(2)}) collective-permute-start(bf16[32,4224]{1,0:T(8,128)(2,1)S(1)} %pad_maximum_fusion.16), channel_id=1, source_target_pairs={{0,24},{8,16},{16,8},{24,0},{1,25},{9,17},{17,9},{25,1},{2,26},{10... | collective-permute-start | bytes 811016 | tf_op jit(solution)/shard_map/ppermute | solution.py:241
  53.9 2.3 %collective-permute-start.18 = (bf16[32,4224]{1,0:T(8,128)(2,1)S(1)}, bf16[32,4224]{1,0:T(8,128)(2,1)S(1)}, u32[]{:S(2)}, u32[]{:S(2)}) collective-permute-start(bf16[32,4224]{1,0:T(8,128)(2,1)S(1)} %pad_maximum_fusion.17), channel_id=1, source_target_pairs={{0,96},{32,64},{64,32},{96,0},{1,97},{33,65},{65,33},{97,1},{2,98}... | collective-permute-start | bytes 811016 | tf_op jit(solution)/shard_map/ppermute | solution.py:241
  56.2 1.5 %collective-permute-start.22 = (bf16[32,4224]{1,0:T(8,128)(2,1)S(1)}, bf16[32,4224]{1,0:T(8,128)(2,1)S(1)}, u32[]{:S(2)}, u32[]{:S(2)}) collective-permute-start(bf16[32,4224]{1,0:T(8,128)(2,1)S(1)} %pad_maximum_fusion.18), channel_id=1, source_target_pairs={{0,8},{8,0},{16,24},{24,16},{1,9},{9,1},{17,25},{25,17},{2,10},{10... | collective-permute-start | bytes 811016 | tf_op jit(solution)/shard_map/ppermute | solution.py:241
  57.7 0.4 collective-permute-done.10
  58.2 1.7 %collective-permute-start.11 = (bf16[64,4224]{1,0:T(8,128)(2,1)S(1)}, bf16[64,4224]{1,0:T(8,128)(2,1)S(1)}, u32[]{:S(2)}, u32[]{:S(2)}) collective-permute-start(bf16[64,4224]{1,0:T(8,128)(2,1)S(1)} %pad_maximum_fusion.11), channel_id=1, source_target_pairs={{0,24},{8,16},{16,8},{24,0},{1,25},{9,17},{17,9},{25,1},{2,26},{10... | collective-permute-start | bytes 1622024 | tf_op jit(solution)/shard_map/ppermute | solution.py:241
  60.1 1.3 collective-permute-start.15
  61.5 1.6 %collective-permute-start.19 = (bf16[64,4224]{1,0:T(8,128)(2,1)S(1)}, bf16[64,4224]{1,0:T(8,128)(2,1)S(1)}, u32[]{:S(2)}, u32[]{:S(2)}) collective-permute-start(bf16[64,4224]{1,0:T(8,128)(2,1)S(1)} %pad_maximum_fusion.13), channel_id=1, source_target_pairs={{0,8},{8,0},{16,24},{24,16},{1,9},{9,1},{17,25},{25,17},{2,10},{10... | collective-permute-start | bytes 1622024 | tf_op jit(solution)/shard_map/ppermute | solution.py:241
  63.3 12.5 %collective-permute-start.6 = (bf16[32,4224]{1,0:T(8,128)(2,1)S(1)}, bf16[32,4224]{1,0:T(8,128)(2,1)S(1)}, u32[]{:S(2)}, u32[]{:S(2)}) collective-permute-start(bf16[32,4224]{1,0:T(8,128)(2,1)S(1)} %get-tuple-element.68), channel_id=1, source_target_pairs={{0,3},{1,2},{2,1},{3,0},{4,7},{5,6},{6,5},{7,4},{8,11},{9,10},{10,... | collective-permute-start | bytes 811016 | tf_op jit(solution)/shard_map/ppermute | solution.py:241
  75.7 0.8 collective-permute-start.4
  76.5 4.5 %collective-permute-done.6 = bf16[32,4224]{1,0:T(8,128)(2,1)S(1)} collective-permute-done((bf16[32,4224]{1,0:T(8,128)(2,1)S(1)}, bf16[32,4224]{1,0:T(8,128)(2,1)S(1)}, u32[]{:S(2)}, u32[]{:S(2)}) %collective-permute-start.6) | collective-permute-done | bytes 270368 | tf_op jit(solution)/shard_map/ppermute | solution.py:241
  81.1 0.9 collective-permute-done.4
  82.1 1.6 %collective-permute-start.5 = (bf16[64,4224]{1,0:T(8,128)(2,1)S(1)}, bf16[64,4224]{1,0:T(8,128)(2,1)S(1)}, u32[]{:S(2)}, u32[]{:S(2)}) collective-permute-start(bf16[64,4224]{1,0:T(8,128)(2,1)S(1)} %pad_maximum_fusion.9), channel_id=1, source_target_pairs={{0,3},{1,2},{2,1},{3,0},{4,7},{5,6},{6,5},{7,4},{8,11},{9,10},{10,... | collective-permute-start | bytes 1622024 | tf_op jit(solution)/shard_map/ppermute | solution.py:241
  83.8 1.8 %collective-permute-start.7 = (bf16[64,4224]{1,0:T(8,128)(2,1)S(1)}, bf16[64,4224]{1,0:T(8,128)(2,1)S(1)}, u32[]{:S(2)}, u32[]{:S(2)}) collective-permute-start(bf16[64,4224]{1,0:T(8,128)(2,1)S(1)} %pad_maximum_fusion.10), channel_id=1, source_target_pairs={{0,1},{1,0},{2,3},{3,2},{4,5},{5,4},{6,7},{7,6},{8,9},{9,8},{10,11... | collective-permute-start | bytes 1622024 | tf_op jit(solution)/shard_map/ppermute | solution.py:241
  85.8 1.9 %collective-permute-start.12 = (bf16[128,4224]{1,0:T(8,128)(2,1)S(1)}, bf16[128,4224]{1,0:T(8,128)(2,1)S(1)}, u32[]{:S(2)}, u32[]{:S(2)}) collective-permute-start(bf16[128,4224]{1,0:T(8,128)(2,1)S(1)} %pad_maximum_fusion.5), channel_id=1, source_target_pairs={{0,96},{32,64},{64,32},{96,0},{1,97},{33,65},{65,33},{97,1},{2,98}... | collective-permute-start | bytes 3244040 | tf_op jit(solution)/shard_map/ppermute | solution.py:241
  88.3 4.4 %collective-permute-done.23 = bf16[64,4224]{1,0:T(8,128)(2,1)S(1)} collective-permute-done((bf16[64,4224]{1,0:T(8,128)(2,1)S(1)}, bf16[64,4224]{1,0:T(8,128)(2,1)S(1)}, u32[]{:S(2)}, u32[]{:S(2)}) %collective-permute-start.23) | collective-permute-done | bytes 540704 | tf_op jit(solution)/shard_map/ppermute | solution.py:241
  93.3 1.2 collective-permute-done.5
  94.5 1.0 collective-permute-start.24
  96.3 3.9 %collective-permute-start.8 = (bf16[256,4224]{1,0:T(8,128)(2,1)S(1)}, bf16[256,4224]{1,0:T(8,128)(2,1)S(1)}, u32[]{:S(2)}, u32[]{:S(2)}) collective-permute-start(bf16[256,4224]{1,0:T(8,128)(2,1)S(1)} %pad_maximum_fusion), channel_id=1, source_target_pairs={{0,4},{4,0},{1,5},{5,1},{2,6},{6,2},{3,7},{7,3},{8,12},{12,8},{9,1... | collective-permute-start | bytes 6488072 | tf_op jit(solution)/shard_map/ppermute | solution.py:237
  100.3 10.1 %collective-permute-done.12 = bf16[128,4224]{1,0:T(8,128)(2,1)S(1)} collective-permute-done((bf16[128,4224]{1,0:T(8,128)(2,1)S(1)}, bf16[128,4224]{1,0:T(8,128)(2,1)S(1)}, u32[]{:S(2)}, u32[]{:S(2)}) %collective-permute-start.12) | collective-permute-done | bytes 1081376 | tf_op jit(solution)/shard_map/ppermute | solution.py:241
  110.4 0.4 broadcast_select_fusion.7
  110.7 0.8 collective-permute-done.16
  111.6 0.4 broadcast_select_fusion.5
  112.0 3.1 %collective-permute-done.20 = bf16[128,4224]{1,0:T(8,128)(2,1)S(1)} collective-permute-done((bf16[128,4224]{1,0:T(8,128)(2,1)S(1)}, bf16[128,4224]{1,0:T(8,128)(2,1)S(1)}, u32[]{:S(2)}, u32[]{:S(2)}) %collective-permute-start.20) | collective-permute-done | bytes 1081376 | tf_op jit(solution)/shard_map/ppermute | solution.py:241
  115.1 0.4 broadcast_select_fusion.3
  115.8 1.8 %collective-permute-done.24 = bf16[128,4224]{1,0:T(8,128)(2,1)S(1)} collective-permute-done((bf16[128,4224]{1,0:T(8,128)(2,1)S(1)}, bf16[128,4224]{1,0:T(8,128)(2,1)S(1)}, u32[]{:S(2)}, u32[]{:S(2)}) %collective-permute-start.24) | collective-permute-done | bytes 1081376 | tf_op jit(solution)/shard_map/ppermute | solution.py:241
  118.5 2.4 %gram.2 = (f32[264,512]{1,0:T(8,128)S(1)}, f32[264,512]{1,0:T(8,128)S(1)}) custom-call(bf16[512,4224]{1,0:T(8,128)(2,1)S(1)} %constant_dynamic-update-slice_fusion.refs_0_, bf16[256,4224]{1,0:T(8,128)(2,1)S(1)} %get-tuple-element.78.refs_1_, bf16[256,4224]{1,0:T(8,128)(2,1)S(1)} %get-tuple-element.79.refs_2_, ...), custom_call_target="tpu_custom_call" | custom-call | flops 2147483648 | bytes 6291456 | tf_op jit(solution)/shard_map/gram/pallas_call | solution.py:193
  120.9 2.4 %gram.3 = (f32[264,512]{1,0:T(8,128)S(1)}, f32[264,512]{1,0:T(8,128)S(1)}) custom-call(bf16[512,4224]{1,0:T(8,128)(2,1)S(1)} %constant_dynamic-update-slice_fusion.refs_0_, bf16[256,4224]{1,0:T(8,128)(2,1)S(1)} %get-tuple-element.78.refs_1_, bf16[256,4224]{1,0:T(8,128)(2,1)S(1)} %get-tuple-element.79.refs_2_, ...), custom_call_target="tpu_custom_call" | custom-call | flops 2147483648 | bytes 6291456 | tf_op jit(solution)/shard_map/gram/pallas_call | solution.py:193
  123.3 4.6 %collective-permute-start.25 = (f32[264,512]{1,0:T(8,128)S(1)}, f32[264,512]{1,0:T(8,128)S(1)}, u32[]{:S(2)}, u32[]{:S(2)}) collective-permute-start(f32[264,512]{1,0:T(8,128)S(1)} %get-tuple-element.24), channel_id=1, source_target_pairs={{0,4},{4,0},{1,5},{5,1},{2,6},{6,2},{3,7},{7,3},{8,12},{12,8},{9,1... | collective-permute-start | bytes 1622024 | tf_op jit(solution)/shard_map/ppermute | solution.py:237
  128.7 0.7 collective-permute-done.25.refs_2_
  129.4 0.8 collective-permute-done.26.refs_3_
  130.2 2.2 %finish.1 = (f32[1,2048]{1,0:T(1,128)}, f32[256,2048]{1,0:T(8,128)}) custom-call(s32[3]{0:T(128)S(1)} %pad_add_fusion.info_ref, f32[1]{0:T(128)} %bitcast.5.part_ref, f32[264,512]{1,0:T(8,128)S(1)} %get-tuple-element.22.refs_0_, f32[264,512]{1,0:T(8,128)S(1)} %get-tuple-element.23.refs_1_, f32[264,512]{1,0:T(8,128)S(1)} %collective-permute-done.25.refs_2_, ...), custom_call_target="tpu_custom_call" | custom-call | tf_op jit(solution)/shard_map/finish/pallas_call | solution.py:223
  (70 shorter events, 5.6 us)
Async XLA Ops:
  0.6 1.6 %copy-start = (bf16[512,2048]{1,0:T(8,128)(2,1)S(1)}, bf16[512,2048]{1,0:T(8,128)(2,1)}, u32[]{:S(2)}) copy-start(bf16[512,2048]{1,0:T(8,128)(2,1)} %resid_ref.1) | copy-start | bytes 6291460
  2.2 0.7 copy-start.1
  2.9 0.7 copy-start.3
  3.6 6.2 %copy-start.4 = (f32[2048]{0:T(1024)S(1)}, f32[2048]{0:T(1024)}, u32[]{:S(2)}) copy-start(f32[2048]{0:T(1024)} %param.5) | copy-start | bytes 24580
  3.6 9.9 %copy-start.2 = (s32[2]{0:T(128)S(1)}, s32[2]{0:T(128)}, u32[]{:S(2)}) copy-start(s32[2]{0:T(128)} %counts_ref.3) | copy-start | bytes 28
  4.9 5.2 %collective-permute-start = (f32[8,256]{1,0:T(8,128)S(1)}, f32[8,256]{1,0:T(8,128)S(1)}, u32[]{:S(2)}, u32[]{:S(2)}) collective-permute-start(f32[8,256]{1,0:T(8,128)S(1)} %get-tuple-element.16.s0), channel_id=1, source_target_pairs={{0,1},{1,0},{2,3},{3,2},{4,5},{5,4},{6,7},{7,6},{8,9},{9,8},{10,11... | collective-permute-start | bytes 24584 | tf_op jit(solution)/shard_map/ppermute | solution.py:241
  7.1 4.0 %collective-permute-start.1 = (f32[8,256]{1,0:T(8,128)S(1)}, f32[8,256]{1,0:T(8,128)S(1)}, u32[]{:S(2)}, u32[]{:S(2)}) collective-permute-start(f32[8,256]{1,0:T(8,128)S(1)} %get-tuple-element.16.s0), channel_id=1, source_target_pairs={{0,2},{1,3},{2,0},{3,1},{4,6},{5,7},{6,4},{7,5},{8,10},{9,11},{10,... | collective-permute-start | bytes 24584 | tf_op jit(solution)/shard_map/ppermute | solution.py:241
  9.7 3.7 %collective-permute-start.2 = (f32[8,256]{1,0:T(8,128)S(1)}, f32[8,256]{1,0:T(8,128)S(1)}, u32[]{:S(2)}, u32[]{:S(2)}) collective-permute-start(f32[8,256]{1,0:T(8,128)S(1)} %get-tuple-element.16.s0), channel_id=1, source_target_pairs={{0,3},{1,2},{2,1},{3,0},{4,7},{5,6},{6,5},{7,4},{8,11},{9,10},{10,... | collective-permute-start | bytes 24584 | tf_op jit(solution)/shard_map/ppermute | solution.py:241
  45.2 6.4 %collective-permute-start.9 = (bf16[16,4224]{1,0:T(8,128)(2,1)S(1)}, bf16[16,4224]{1,0:T(8,128)(2,1)S(1)}, u32[]{:S(2)}, u32[]{:S(2)}) collective-permute-start(bf16[16,4224]{1,0:T(8,128)(2,1)S(1)} %get-tuple-element.18), channel_id=1, source_target_pairs={{0,8},{8,0},{16,24},{24,16},{1,9},{9,1},{17,25},{25,17},{2,10},{10... | collective-permute-start | bytes 405512 | tf_op jit(solution)/shard_map/ppermute | solution.py:241
  45.7 17.5 %collective-permute-start.3 = (bf16[64,4224]{1,0:T(8,128)(2,1)S(1)}, bf16[64,4224]{1,0:T(8,128)(2,1)S(1)}, u32[]{:S(2)}, u32[]{:S(2)}) collective-permute-start(bf16[64,4224]{1,0:T(8,128)(2,1)S(1)} %get-tuple-element.17), channel_id=1, source_target_pairs={{0,0},{1,33},{2,66},{3,99},{32,1},{33,32},{34,67},{35,98},{64,2},{... | collective-permute-start | bytes 1622024 | tf_op jit(solution)/shard_map/ppermute | solution.py:266
  46.4 5.6 %collective-permute-start.13 = (bf16[16,4224]{1,0:T(8,128)(2,1)S(1)}, bf16[16,4224]{1,0:T(8,128)(2,1)S(1)}, u32[]{:S(2)}, u32[]{:S(2)}) collective-permute-start(bf16[16,4224]{1,0:T(8,128)(2,1)S(1)} %get-tuple-element.19), channel_id=1, source_target_pairs={{0,32},{32,0},{64,96},{96,64},{1,33},{33,1},{65,97},{97,65},{2,34}... | collective-permute-start | bytes 405512 | tf_op jit(solution)/shard_map/ppermute | solution.py:241
  48.0 5.8 %collective-permute-start.17 = (bf16[16,4224]{1,0:T(8,128)(2,1)S(1)}, bf16[16,4224]{1,0:T(8,128)(2,1)S(1)}, u32[]{:S(2)}, u32[]{:S(2)}) collective-permute-start(bf16[16,4224]{1,0:T(8,128)(2,1)S(1)} %get-tuple-element.20), channel_id=1, source_target_pairs={{0,24},{8,16},{16,8},{24,0},{1,25},{9,17},{17,9},{25,1},{2,26},{10... | collective-permute-start | bytes 405512 | tf_op jit(solution)/shard_map/ppermute | solution.py:241
  49.0 7.2 %collective-permute-start.21 = (bf16[16,4224]{1,0:T(8,128)(2,1)S(1)}, bf16[16,4224]{1,0:T(8,128)(2,1)S(1)}, u32[]{:S(2)}, u32[]{:S(2)}) collective-permute-start(bf16[16,4224]{1,0:T(8,128)(2,1)S(1)} %get-tuple-element.21), channel_id=1, source_target_pairs={{0,96},{32,64},{64,32},{96,0},{1,97},{33,65},{65,33},{97,1},{2,98}... | collective-permute-start | bytes 405512 | tf_op jit(solution)/shard_map/ppermute | solution.py:241
  51.7 6.3 %collective-permute-start.10 = (bf16[32,4224]{1,0:T(8,128)(2,1)S(1)}, bf16[32,4224]{1,0:T(8,128)(2,1)S(1)}, u32[]{:S(2)}, u32[]{:S(2)}) collective-permute-start(bf16[32,4224]{1,0:T(8,128)(2,1)S(1)} %pad_maximum_fusion.15), channel_id=1, source_target_pairs={{0,32},{32,0},{64,96},{96,64},{1,33},{33,1},{65,97},{97,65},{2,34}... | collective-permute-start | bytes 811016 | tf_op jit(solution)/shard_map/ppermute | solution.py:241
  52.1 7.9 %collective-permute-start.14 = (bf16[32,4224]{1,0:T(8,128)(2,1)S(1)}, bf16[32,4224]{1,0:T(8,128)(2,1)S(1)}, u32[]{:S(2)}, u32[]{:S(2)}) collective-permute-start(bf16[32,4224]{1,0:T(8,128)(2,1)S(1)} %pad_maximum_fusion.16), channel_id=1, source_target_pairs={{0,24},{8,16},{16,8},{24,0},{1,25},{9,17},{17,9},{25,1},{2,26},{10... | collective-permute-start | bytes 811016 | tf_op jit(solution)/shard_map/ppermute | solution.py:241
  53.9 7.5 %collective-permute-start.18 = (bf16[32,4224]{1,0:T(8,128)(2,1)S(1)}, bf16[32,4224]{1,0:T(8,128)(2,1)S(1)}, u32[]{:S(2)}, u32[]{:S(2)}) collective-permute-start(bf16[32,4224]{1,0:T(8,128)(2,1)S(1)} %pad_maximum_fusion.17), channel_id=1, source_target_pairs={{0,96},{32,64},{64,32},{96,0},{1,97},{33,65},{65,33},{97,1},{2,98}... | collective-permute-start | bytes 811016 | tf_op jit(solution)/shard_map/ppermute | solution.py:241
  56.2 6.9 %collective-permute-start.22 = (bf16[32,4224]{1,0:T(8,128)(2,1)S(1)}, bf16[32,4224]{1,0:T(8,128)(2,1)S(1)}, u32[]{:S(2)}, u32[]{:S(2)}) collective-permute-start(bf16[32,4224]{1,0:T(8,128)(2,1)S(1)} %pad_maximum_fusion.18), channel_id=1, source_target_pairs={{0,8},{8,0},{16,24},{24,16},{1,9},{9,1},{17,25},{25,17},{2,10},{10... | collective-permute-start | bytes 811016 | tf_op jit(solution)/shard_map/ppermute | solution.py:241
  58.2 25.6 %collective-permute-start.11 = (bf16[64,4224]{1,0:T(8,128)(2,1)S(1)}, bf16[64,4224]{1,0:T(8,128)(2,1)S(1)}, u32[]{:S(2)}, u32[]{:S(2)}) collective-permute-start(bf16[64,4224]{1,0:T(8,128)(2,1)S(1)} %pad_maximum_fusion.11), channel_id=1, source_target_pairs={{0,24},{8,16},{16,8},{24,0},{1,25},{9,17},{17,9},{25,1},{2,26},{10... | collective-permute-start | bytes 1622024 | tf_op jit(solution)/shard_map/ppermute | solution.py:241
  60.1 25.8 %collective-permute-start.15 = (bf16[64,4224]{1,0:T(8,128)(2,1)S(1)}, bf16[64,4224]{1,0:T(8,128)(2,1)S(1)}, u32[]{:S(2)}, u32[]{:S(2)}) collective-permute-start(bf16[64,4224]{1,0:T(8,128)(2,1)S(1)} %pad_maximum_fusion.12), channel_id=1, source_target_pairs={{0,96},{32,64},{64,32},{96,0},{1,97},{33,65},{65,33},{97,1},{2,98}... | collective-permute-start | bytes 1622024 | tf_op jit(solution)/shard_map/ppermute | solution.py:241
  61.5 26.5 %collective-permute-start.19 = (bf16[64,4224]{1,0:T(8,128)(2,1)S(1)}, bf16[64,4224]{1,0:T(8,128)(2,1)S(1)}, u32[]{:S(2)}, u32[]{:S(2)}) collective-permute-start(bf16[64,4224]{1,0:T(8,128)(2,1)S(1)} %pad_maximum_fusion.13), channel_id=1, source_target_pairs={{0,8},{8,0},{16,24},{24,16},{1,9},{9,1},{17,25},{25,17},{2,10},{10... | collective-permute-start | bytes 1622024 | tf_op jit(solution)/shard_map/ppermute | solution.py:241
  63.3 17.8 %collective-permute-start.6 = (bf16[32,4224]{1,0:T(8,128)(2,1)S(1)}, bf16[32,4224]{1,0:T(8,128)(2,1)S(1)}, u32[]{:S(2)}, u32[]{:S(2)}) collective-permute-start(bf16[32,4224]{1,0:T(8,128)(2,1)S(1)} %get-tuple-element.68), channel_id=1, source_target_pairs={{0,3},{1,2},{2,1},{3,0},{4,7},{5,6},{6,5},{7,4},{8,11},{9,10},{10,... | collective-permute-start | bytes 811016 | tf_op jit(solution)/shard_map/ppermute | solution.py:241
  75.7 6.2 %collective-permute-start.4 = (bf16[32,4224]{1,0:T(8,128)(2,1)S(1)}, bf16[32,4224]{1,0:T(8,128)(2,1)S(1)}, u32[]{:S(2)}, u32[]{:S(2)}) collective-permute-start(bf16[32,4224]{1,0:T(8,128)(2,1)S(1)} %get-tuple-element.69), channel_id=1, source_target_pairs={{0,1},{1,0},{2,3},{3,2},{4,5},{5,4},{6,7},{7,6},{8,9},{9,8},{10,11... | collective-permute-start | bytes 811016 | tf_op jit(solution)/shard_map/ppermute | solution.py:241
  81.1 11.7 %collective-permute-start.23 = (bf16[64,4224]{1,0:T(8,128)(2,1)S(1)}, bf16[64,4224]{1,0:T(8,128)(2,1)S(1)}, u32[]{:S(2)}, u32[]{:S(2)}) collective-permute-start(bf16[64,4224]{1,0:T(8,128)(2,1)S(1)} %pad_maximum_fusion.14), channel_id=1, source_target_pairs={{0,32},{32,0},{64,96},{96,64},{1,33},{33,1},{65,97},{97,65},{2,34}... | collective-permute-start | bytes 1622024 | tf_op jit(solution)/shard_map/ppermute | solution.py:241
  82.1 12.4 %collective-permute-start.5 = (bf16[64,4224]{1,0:T(8,128)(2,1)S(1)}, bf16[64,4224]{1,0:T(8,128)(2,1)S(1)}, u32[]{:S(2)}, u32[]{:S(2)}) collective-permute-start(bf16[64,4224]{1,0:T(8,128)(2,1)S(1)} %pad_maximum_fusion.9), channel_id=1, source_target_pairs={{0,3},{1,2},{2,1},{3,0},{4,7},{5,6},{6,5},{7,4},{8,11},{9,10},{10,... | collective-permute-start | bytes 1622024 | tf_op jit(solution)/shard_map/ppermute | solution.py:241
  83.8 12.1 %collective-permute-start.7 = (bf16[64,4224]{1,0:T(8,128)(2,1)S(1)}, bf16[64,4224]{1,0:T(8,128)(2,1)S(1)}, u32[]{:S(2)}, u32[]{:S(2)}) collective-permute-start(bf16[64,4224]{1,0:T(8,128)(2,1)S(1)} %pad_maximum_fusion.10), channel_id=1, source_target_pairs={{0,1},{1,0},{2,3},{3,2},{4,5},{5,4},{6,7},{7,6},{8,9},{9,8},{10,11... | collective-permute-start | bytes 1622024 | tf_op jit(solution)/shard_map/ppermute | solution.py:241
  85.8 24.5 %collective-permute-start.12 = (bf16[128,4224]{1,0:T(8,128)(2,1)S(1)}, bf16[128,4224]{1,0:T(8,128)(2,1)S(1)}, u32[]{:S(2)}, u32[]{:S(2)}) collective-permute-start(bf16[128,4224]{1,0:T(8,128)(2,1)S(1)} %pad_maximum_fusion.5), channel_id=1, source_target_pairs={{0,96},{32,64},{64,32},{96,0},{1,97},{33,65},{65,33},{97,1},{2,98}... | collective-permute-start | bytes 3244040 | tf_op jit(solution)/shard_map/ppermute | solution.py:241
  88.0 23.6 %collective-permute-start.16 = (bf16[128,4224]{1,0:T(8,128)(2,1)S(1)}, bf16[128,4224]{1,0:T(8,128)(2,1)S(1)}, u32[]{:S(2)}, u32[]{:S(2)}) collective-permute-start(bf16[128,4224]{1,0:T(8,128)(2,1)S(1)} %pad_maximum_fusion.6), channel_id=1, source_target_pairs={{0,8},{8,0},{16,24},{24,16},{1,9},{9,1},{17,25},{25,17},{2,10},{10... | collective-permute-start | bytes 3244040 | tf_op jit(solution)/shard_map/ppermute | solution.py:241
  92.7 22.3 %collective-permute-start.20 = (bf16[128,4224]{1,0:T(8,128)(2,1)S(1)}, bf16[128,4224]{1,0:T(8,128)(2,1)S(1)}, u32[]{:S(2)}, u32[]{:S(2)}) collective-permute-start(bf16[128,4224]{1,0:T(8,128)(2,1)S(1)} %pad_maximum_fusion.7), channel_id=1, source_target_pairs={{0,32},{32,0},{64,96},{96,64},{1,33},{33,1},{65,97},{97,65},{2,34}... | collective-permute-start | bytes 3244040 | tf_op jit(solution)/shard_map/ppermute | solution.py:241
  94.5 23.0 %collective-permute-start.24 = (bf16[128,4224]{1,0:T(8,128)(2,1)S(1)}, bf16[128,4224]{1,0:T(8,128)(2,1)S(1)}, u32[]{:S(2)}, u32[]{:S(2)}) collective-permute-start(bf16[128,4224]{1,0:T(8,128)(2,1)S(1)} %pad_maximum_fusion.8), channel_id=1, source_target_pairs={{0,24},{8,16},{16,8},{24,0},{1,25},{9,17},{17,9},{25,1},{2,26},{10... | collective-permute-start | bytes 3244040 | tf_op jit(solution)/shard_map/ppermute | solution.py:241
  96.3 21.9 %collective-permute-start.8 = (bf16[256,4224]{1,0:T(8,128)(2,1)S(1)}, bf16[256,4224]{1,0:T(8,128)(2,1)S(1)}, u32[]{:S(2)}, u32[]{:S(2)}) collective-permute-start(bf16[256,4224]{1,0:T(8,128)(2,1)S(1)} %pad_maximum_fusion), channel_id=1, source_target_pairs={{0,4},{4,0},{1,5},{5,1},{2,6},{6,2},{3,7},{7,3},{8,12},{12,8},{9,1... | collective-permute-start | bytes 6488072 | tf_op jit(solution)/shard_map/ppermute | solution.py:237
  123.3 6.1 %collective-permute-start.25 = (f32[264,512]{1,0:T(8,128)S(1)}, f32[264,512]{1,0:T(8,128)S(1)}, u32[]{:S(2)}, u32[]{:S(2)}) collective-permute-start(f32[264,512]{1,0:T(8,128)S(1)} %get-tuple-element.24), channel_id=1, source_target_pairs={{0,4},{4,0},{1,5},{5,1},{2,6},{6,2},{3,7},{7,3},{8,12},{12,8},{9,1... | collective-permute-start | bytes 1622024 | tf_op jit(solution)/shard_map/ppermute | solution.py:237
  127.9 2.3 %collective-permute-start.26 = (f32[264,512]{1,0:T(8,128)S(1)}, f32[264,512]{1,0:T(8,128)S(1)}, u32[]{:S(2)}, u32[]{:S(2)}) collective-permute-start(f32[264,512]{1,0:T(8,128)S(1)} %get-tuple-element.25), channel_id=1, source_target_pairs={{0,4},{4,0},{1,5},{5,1},{2,6},{6,2},{3,7},{7,3},{8,12},{12,8},{9,1... | collective-permute-start | bytes 1622024 | tf_op jit(solution)/shard_map/ppermute | solution.py:237

commit v11 on v10

--- a/solution.py
+++ b/solution.py
@@ -159,6 +159,24 @@
         compiler_params=params(10),
         name="pack",
     )(first, pieces)
+
+
+def halve_kernel(in_ref, *refs):
+    low_ref, high_ref = refs[-2:]
+    low_ref[...] = in_ref[: PIECE // 2, :]
+    high_ref[...] = in_ref[PIECE // 2 :, :]
+
+
+def halve(value, after):
+    vmem = pl.BlockSpec(memory_space=pltpu.VMEM)
+    return pl.pallas_call(
+        halve_kernel,
+        out_shape=(jax.ShapeDtypeStruct((PIECE // 2, LONG), bf16),) * 2,
+        in_specs=[vmem] + [pl.BlockSpec(memory_space=pl.ANY)] * len(after),
+        out_specs=(vmem,) * 2,
+        compiler_params=params(4),
+        name="halve",
+    )(value, *after)
 
 
 def gram_kernel(blocks, rows_ref, *refs):
@@ -271,9 +289,10 @@
             seen = [PARTNERS[(s + k) % 4][0] for k in range(step)]
             which = side(x if axis == "x" else z, flip, axis not in seen)
             streams[s] = meet(streams[s], axis, flip, which)
+        if step == 2:
+            low, high = halve(turned, after=streams[:1])
 
     q = y ^ z
-    low, high = turned[:32], turned[32:]
     low, high = meet(low, "y", 1, side(q, 1, True)), meet(high, "y", 3, side(q, 3, True))
     low, high = meet(low, "y", 3, side(q, 3, False)), meet(high, "y", 1, side(q, 1, False))
     rows = join(low, high)

time: 133 us -> 137 us (1.030)
  waiting for transfers between devices: 32.1 us -> 40.1 us
  starting transfers between devices: 50 us -> 46.4 us
    ppermute x23, waiting for transfers between devices: 30.6 us -> 36.9 us  [trade(): return lax.ppermute(value, axis, [(i, i ^ flip) for i in range(4)])]
    ppermute x3, starting transfers between devices: 8.59 us -> 5.22 us  [swap(): return lax.ppermute(value, 'c', [(0, 1), (1, 0)])]
    ppermute x3, waiting for transfers between devices: 1.5 us -> 3.18 us  [swap(): return lax.ppermute(value, 'c', [(0, 1), (1, 0)])]
    select_n x17 -> x18, other arithmetic: 2.8 us -> 2.82 us  [meet(): jnp.where(which == 0, value, got)]
  transfers between devices with their start and end apart: 27 -> 27, of which waited for: 13 -> 11; matrix products, arithmetic and copies ran while one was open for 4% -> 4% of each run, Pallas kernels for 0% -> 0%
where the time goes in v11:
time: 137 us
  starting transfers between devices  46.4 us (34%)
  waiting for transfers between devices  40.1 us (29%)
  blocking collectives  27.3 us (20%)
  Pallas kernels  11.3 us (8%)
  other arithmetic  6.36 us (5%)
  local copies, waits for them, and re-layouts  3.66 us (3%)
  between operations  1.62 us (1%)
    ppermute x23, starting transfers between devices, trade(): return lax.ppermute(value, axis, [(i, i ^ flip) for i in range(4)])  40.5 us
    ppermute x23, waiting for transfers between devices, trade(): return lax.ppermute(value, axis, [(i, i ^ flip) for i in range(4)])  36.9 us
    all_to_all x1, blocking collectives, per_device(): pieces = lax.all_to_all(pieces, TOK, 0, 0, tiled=True)  27.3 us
    ppermute x3, starting transfers between devices, swap(): return lax.ppermute(value, 'c', [(0, 1), (1, 0)])  5.22 us
    pallas_call x2, Pallas kernels, gram(): pl.pallas_call(lambda *refs: gram_kernel(blocks, *refs), out_shape=(jax.S...  4.8 us
    ppermute x3, waiting for transfers between devices, swap(): return lax.ppermute(value, 'c', [(0, 1), (1, 0)])  3.18 us
    unnamed x10, local copies, waits for them, and re-layouts  2.92 us
    select_n x18, other arithmetic, meet(): jnp.where(which == 0, value, got)  2.82 us
  transfers between devices with their start and end apart: 27, of which 11 were waited for; matrix products, arithmetic and copies ran while one was open for 4% of the time, Pallas kernels for 0%

profile of v11, /device:TPU:1, one launch (start us, length us, event | category | flops | bytes accessed | tf_op | source)
XLA Modules:
  0.0 136.7 jit_solution(5562465892640727896)
XLA Ops:
  0.6 1.6 %copy-done = bf16[512,2048]{1,0:T(8,128)(2,1)S(1)} copy-done((bf16[512,2048]{1,0:T(8,128)(2,1)S(1)}, bf16[512,2048]{1,0:T(8,128)(2,1)}, u32[]{:S(2)}) %copy-start) | copy-done | bytes 2097176
  2.2 0.7 copy-done.1
  2.9 0.7 copy-done.3
  3.6 1.3 pick.1
  4.9 2.2 %collective-permute-start = (f32[8,256]{1,0:T(8,128)S(1)}, f32[8,256]{1,0:T(8,128)S(1)}, u32[]{:S(2)}, u32[]{:S(2)}) collective-permute-start(f32[8,256]{1,0:T(8,128)S(1)} %get-tuple-element.18.s0), channel_id=1, source_target_pairs={{0,1},{1,0},{2,3},{3,2},{4,5},{5,4},{6,7},{7,6},{8,9},{9,8},{10,11... | collective-permute-start | bytes 24584 | tf_op jit(solution)/shard_map/ppermute | solution.py:259
  7.1 2.6 %collective-permute-start.1 = (f32[8,256]{1,0:T(8,128)S(1)}, f32[8,256]{1,0:T(8,128)S(1)}, u32[]{:S(2)}, u32[]{:S(2)}) collective-permute-start(f32[8,256]{1,0:T(8,128)S(1)} %get-tuple-element.18.s0), channel_id=1, source_target_pairs={{0,2},{1,3},{2,0},{3,1},{4,6},{5,7},{6,4},{7,5},{8,10},{9,11},{10,... | collective-permute-start | bytes 24584 | tf_op jit(solution)/shard_map/ppermute | solution.py:259
  9.7 0.4 copy.7.gain_ref
  10.1 1.0 collective-permute-done.1.s2
  11.1 2.3 %collective-permute-done.2.s3 = f32[8,256]{1,0:T(8,128)S(1)} collective-permute-done((f32[8,256]{1,0:T(8,128)S(1)}, f32[8,256]{1,0:T(8,128)S(1)}, u32[]{:S(2)}, u32[]{:S(2)}) %collective-permute-start.2) | collective-permute-done | bytes 8224 | tf_op jit(solution)/shard_map/ppermute | solution.py:259
  13.5 0.9 norm.1
  14.3 27.3 %all_to_all.5.in_ref = bf16[32,64,256]{2,1,0:T(8,128)(2,1)S(1)} all-to-all(bf16[32,64,256]{2,1,0:T(8,128)(2,1)S(1)} %norm.1), channel_id=1, replica_groups=mesh['z'=4,'x'=4,'c'=2,'y'=4] {'z','x','c'}, dimensions={0} | all-to-all | bytes 2097152 | tf_op jit(solution)/shard_map/all_to_all | solution.py:276
  41.6 1.2 fusion
  43.1 2.1 %pack.1 = (bf16[64,4224]{1,0:T(8,128)(2,1)S(1)}, bf16[16,4224]{1,0:T(8,128)(2,1)S(1)}, bf16[16,4224]{1,0:T(8,128)(2,1)S(1)}, bf16[16,4224]{1,0:T(8,128)(2,1)S(1)}, bf16[16,4224]{1,0:T(8,128)(2,1)S(1)}) custom-call(s32[32]{0:T(128)S(1)} %sub.3.first_ref, bf16[32,64,256]{2,1,0:T(8,128)(2,1)S(1)} %all_to_all.5.in_ref), custom_call_target="tpu_custom_call" | custom-call | tf_op jit(solution)/shard_map/pack/pallas_call | solution.py:152
  45.2 0.4 collective-permute-start.4
  45.6 0.7 collective-permute-start.3
  46.3 1.7 %collective-permute-start.13 = (bf16[16,4224]{1,0:T(8,128)(2,1)S(1)}, bf16[16,4224]{1,0:T(8,128)(2,1)S(1)}, u32[]{:S(2)}, u32[]{:S(2)}) collective-permute-start(bf16[16,4224]{1,0:T(8,128)(2,1)S(1)} %get-tuple-element.23), channel_id=1, source_target_pairs={{0,32},{32,0},{64,96},{96,64},{1,33},{33,1},{65,97},{97,65},{2,34}... | collective-permute-start | bytes 405512 | tf_op jit(solution)/shard_map/ppermute | solution.py:259
  48.0 0.9 collective-permute-start.17
  48.9 2.6 %collective-permute-start.21 = (bf16[16,4224]{1,0:T(8,128)(2,1)S(1)}, bf16[16,4224]{1,0:T(8,128)(2,1)S(1)}, u32[]{:S(2)}, u32[]{:S(2)}) collective-permute-start(bf16[16,4224]{1,0:T(8,128)(2,1)S(1)} %get-tuple-element.25), channel_id=1, source_target_pairs={{0,96},{32,64},{64,32},{96,0},{1,97},{33,65},{65,33},{97,1},{2,98}... | collective-permute-start | bytes 405512 | tf_op jit(solution)/shard_map/ppermute | solution.py:259
  52.0 1.8 %collective-permute-start.14 = (bf16[32,4224]{1,0:T(8,128)(2,1)S(1)}, bf16[32,4224]{1,0:T(8,128)(2,1)S(1)}, u32[]{:S(2)}, u32[]{:S(2)}) collective-permute-start(bf16[32,4224]{1,0:T(8,128)(2,1)S(1)} %pad_maximum_fusion.16), channel_id=1, source_target_pairs={{0,24},{8,16},{16,8},{24,0},{1,25},{9,17},{17,9},{25,1},{2,26},{10... | collective-permute-start | bytes 811016 | tf_op jit(solution)/shard_map/ppermute | solution.py:259
  53.8 2.3 %collective-permute-start.18 = (bf16[32,4224]{1,0:T(8,128)(2,1)S(1)}, bf16[32,4224]{1,0:T(8,128)(2,1)S(1)}, u32[]{:S(2)}, u32[]{:S(2)}) collective-permute-start(bf16[32,4224]{1,0:T(8,128)(2,1)S(1)} %pad_maximum_fusion.17), channel_id=1, source_target_pairs={{0,96},{32,64},{64,32},{96,0},{1,97},{33,65},{65,33},{97,1},{2,98}... | collective-permute-start | bytes 811016 | tf_op jit(solution)/shard_map/ppermute | solution.py:259
  56.2 1.5 %collective-permute-start.22 = (bf16[32,4224]{1,0:T(8,128)(2,1)S(1)}, bf16[32,4224]{1,0:T(8,128)(2,1)S(1)}, u32[]{:S(2)}, u32[]{:S(2)}) collective-permute-start(bf16[32,4224]{1,0:T(8,128)(2,1)S(1)} %pad_maximum_fusion.18), channel_id=1, source_target_pairs={{0,8},{8,0},{16,24},{24,16},{1,9},{9,1},{17,25},{25,17},{2,10},{10... | collective-permute-start | bytes 811016 | tf_op jit(solution)/shard_map/ppermute | solution.py:259
  57.6 0.4 collective-permute-done.5
  58.2 1.7 %collective-permute-start.6 = (bf16[64,4224]{1,0:T(8,128)(2,1)S(1)}, bf16[64,4224]{1,0:T(8,128)(2,1)S(1)}, u32[]{:S(2)}, u32[]{:S(2)}) collective-permute-start(bf16[64,4224]{1,0:T(8,128)(2,1)S(1)} %pad_maximum_fusion.9), channel_id=1, source_target_pairs={{0,24},{8,16},{16,8},{24,0},{1,25},{9,17},{17,9},{25,1},{2,26},{10... | collective-permute-start | bytes 1622024 | tf_op jit(solution)/shard_map/ppermute | solution.py:259
  60.0 1.3 collective-permute-start.15
  61.5 1.6 %collective-permute-start.19 = (bf16[64,4224]{1,0:T(8,128)(2,1)S(1)}, bf16[64,4224]{1,0:T(8,128)(2,1)S(1)}, u32[]{:S(2)}, u32[]{:S(2)}) collective-permute-start(bf16[64,4224]{1,0:T(8,128)(2,1)S(1)} %pad_maximum_fusion.13), channel_id=1, source_target_pairs={{0,8},{8,0},{16,24},{24,16},{1,9},{9,1},{17,25},{25,17},{2,10},{10... | collective-permute-start | bytes 1622024 | tf_op jit(solution)/shard_map/ppermute | solution.py:259
  63.3 7.3 %collective-permute-done.6 = bf16[64,4224]{1,0:T(8,128)(2,1)S(1)} collective-permute-done((bf16[64,4224]{1,0:T(8,128)(2,1)S(1)}, bf16[64,4224]{1,0:T(8,128)(2,1)S(1)}, u32[]{:S(2)}, u32[]{:S(2)}) %collective-permute-start.6) | collective-permute-done | bytes 540704 | tf_op jit(solution)/shard_map/ppermute | solution.py:259
  70.9 3.6 %collective-permute-start.12 = (bf16[128,4224]{1,0:T(8,128)(2,1)S(1)}, bf16[128,4224]{1,0:T(8,128)(2,1)S(1)}, u32[]{:S(2)}, u32[]{:S(2)}) collective-permute-start(bf16[128,4224]{1,0:T(8,128)(2,1)S(1)} %pad_maximum_fusion.5.refs_0_), channel_id=1, source_target_pairs={{0,96},{32,64},{64,32},{96,0},{1,97},{33,65},{65,33},{97,1},{2,98}... | collective-permute-start | bytes 3244040 | tf_op jit(solution)/shard_map/ppermute | solution.py:259
  74.6 13.2 %collective-permute-start.7 = (bf16[32,4224]{1,0:T(8,128)(2,1)S(1)}, bf16[32,4224]{1,0:T(8,128)(2,1)S(1)}, u32[]{:S(2)}, u32[]{:S(2)}) collective-permute-start(bf16[32,4224]{1,0:T(8,128)(2,1)S(1)} %get-tuple-element.21), channel_id=1, source_target_pairs={{0,1},{1,0},{2,3},{3,2},{4,5},{5,4},{6,7},{7,6},{8,9},{9,8},{10,11... | collective-permute-start | bytes 811016 | tf_op jit(solution)/shard_map/ppermute | solution.py:259
  87.8 1.0 collective-permute-start.9
  89.9 3.2 %collective-permute-done.7 = bf16[32,4224]{1,0:T(8,128)(2,1)S(1)} collective-permute-done((bf16[32,4224]{1,0:T(8,128)(2,1)S(1)}, bf16[32,4224]{1,0:T(8,128)(2,1)S(1)}, u32[]{:S(2)}, u32[]{:S(2)}) %collective-permute-start.7) | collective-permute-done | bytes 270368 | tf_op jit(solution)/shard_map/ppermute | solution.py:259
  93.1 0.7 collective-permute-start.24
  93.9 1.3 collective-permute-done.9
  95.2 0.7 collective-permute-start.8
  96.0 11.5 %collective-permute-done.8 = bf16[64,4224]{1,0:T(8,128)(2,1)S(1)} collective-permute-done((bf16[64,4224]{1,0:T(8,128)(2,1)S(1)}, bf16[64,4224]{1,0:T(8,128)(2,1)S(1)}, u32[]{:S(2)}, u32[]{:S(2)}) %collective-permute-start.8) | collective-permute-done | bytes 540704 | tf_op jit(solution)/shard_map/ppermute | solution.py:259
  107.8 9.8 %collective-permute-done.10 = bf16[64,4224]{1,0:T(8,128)(2,1)S(1)} collective-permute-done((bf16[64,4224]{1,0:T(8,128)(2,1)S(1)}, bf16[64,4224]{1,0:T(8,128)(2,1)S(1)}, u32[]{:S(2)}, u32[]{:S(2)}) %collective-permute-start.10) | collective-permute-done | bytes 540704 | tf_op jit(solution)/shard_map/ppermute | solution.py:259
  118.1 4.6 %collective-permute-start.11 = (bf16[256,4224]{1,0:T(8,128)(2,1)S(1)}, bf16[256,4224]{1,0:T(8,128)(2,1)S(1)}, u32[]{:S(2)}, u32[]{:S(2)}) collective-permute-start(bf16[256,4224]{1,0:T(8,128)(2,1)S(1)} %pad_maximum_fusion), channel_id=1, source_target_pairs={{0,4},{4,0},{1,5},{5,1},{2,6},{6,2},{3,7},{7,3},{8,12},{12,8},{9,1... | collective-permute-start | bytes 6488072 | tf_op jit(solution)/shard_map/ppermute | solution.py:255
  122.8 0.4 broadcast_select_fusion.7
  123.1 0.4 broadcast_select_fusion.5
  123.5 0.4 broadcast_select_fusion.3
  123.9 0.3 pad_maximum_fusion.1
  124.2 0.4 broadcast_select_fusion.1
  124.9 1.7 %collective-permute-done.11 = bf16[256,4224]{1,0:T(8,128)(2,1)S(1)} collective-permute-done((bf16[256,4224]{1,0:T(8,128)(2,1)S(1)}, bf16[256,4224]{1,0:T(8,128)(2,1)S(1)}, u32[]{:S(2)}, u32[]{:S(2)}) %collective-permute-start.11) | collective-permute-done | bytes 2162720 | tf_op jit(solution)/shard_map/ppermute | solution.py:255
  126.9 2.4 %gram.2 = (f32[264,512]{1,0:T(8,128)S(1)}, f32[264,512]{1,0:T(8,128)S(1)}) custom-call(bf16[512,4224]{1,0:T(8,128)(2,1)S(1)} %constant_dynamic-update-slice_fusion.refs_0_, bf16[256,4224]{1,0:T(8,128)(2,1)S(1)} %get-tuple-element.78.refs_1_, bf16[256,4224]{1,0:T(8,128)(2,1)S(1)} %get-tuple-element.79.refs_2_, ...), custom_call_target="tpu_custom_call" | custom-call | flops 2147483648 | bytes 6291456 | tf_op jit(solution)/shard_map/gram/pallas_call | solution.py:211
  129.3 2.4 %gram.3 = (f32[264,512]{1,0:T(8,128)S(1)}, f32[264,512]{1,0:T(8,128)S(1)}) custom-call(bf16[512,4224]{1,0:T(8,128)(2,1)S(1)} %constant_dynamic-update-slice_fusion.refs_0_, bf16[256,4224]{1,0:T(8,128)(2,1)S(1)} %get-tuple-element.78.refs_1_, bf16[256,4224]{1,0:T(8,128)(2,1)S(1)} %get-tuple-element.79.refs_2_, ...), custom_call_target="tpu_custom_call" | custom-call | flops 2147483648 | bytes 6291456 | tf_op jit(solution)/shard_map/gram/pallas_call | solution.py:211
  131.7 0.5 collective-permute-start.25
  133.1 0.7 collective-permute-done.25.refs_2_
  133.7 0.8 collective-permute-done.26.refs_3_
  134.5 2.2 %finish.1 = (f32[1,2048]{1,0:T(1,128)}, f32[256,2048]{1,0:T(8,128)}) custom-call(s32[3]{0:T(128)S(1)} %pad_add_fusion.info_ref, f32[1]{0:T(128)} %bitcast.5.part_ref, f32[264,512]{1,0:T(8,128)S(1)} %get-tuple-element.26.refs_0_, f32[264,512]{1,0:T(8,128)S(1)} %get-tuple-element.27.refs_1_, f32[264,512]{1,0:T(8,128)S(1)} %collective-permute-done.25.refs_2_, ...), custom_call_target="tpu_custom_call" | custom-call | tf_op jit(solution)/shard_map/finish/pallas_call | solution.py:241
  (71 shorter events, 4.6 us)
Async XLA Ops:
  0.6 1.6 %copy-start = (bf16[512,2048]{1,0:T(8,128)(2,1)S(1)}, bf16[512,2048]{1,0:T(8,128)(2,1)}, u32[]{:S(2)}) copy-start(bf16[512,2048]{1,0:T(8,128)(2,1)} %resid_ref.1) | copy-start | bytes 6291460
  2.2 0.7 copy-start.1
  2.9 0.7 copy-start.3
  3.6 6.2 %copy-start.4 = (f32[2048]{0:T(1024)S(1)}, f32[2048]{0:T(1024)}, u32[]{:S(2)}) copy-start(f32[2048]{0:T(1024)} %param.5) | copy-start | bytes 24580
  3.6 9.9 %copy-start.2 = (s32[2]{0:T(128)S(1)}, s32[2]{0:T(128)}, u32[]{:S(2)}) copy-start(s32[2]{0:T(128)} %counts_ref.3) | copy-start | bytes 28
  4.9 5.2 %collective-permute-start = (f32[8,256]{1,0:T(8,128)S(1)}, f32[8,256]{1,0:T(8,128)S(1)}, u32[]{:S(2)}, u32[]{:S(2)}) collective-permute-start(f32[8,256]{1,0:T(8,128)S(1)} %get-tuple-element.18.s0), channel_id=1, source_target_pairs={{0,1},{1,0},{2,3},{3,2},{4,5},{5,4},{6,7},{7,6},{8,9},{9,8},{10,11... | collective-permute-start | bytes 24584 | tf_op jit(solution)/shard_map/ppermute | solution.py:259
  7.1 4.0 %collective-permute-start.1 = (f32[8,256]{1,0:T(8,128)S(1)}, f32[8,256]{1,0:T(8,128)S(1)}, u32[]{:S(2)}, u32[]{:S(2)}) collective-permute-start(f32[8,256]{1,0:T(8,128)S(1)} %get-tuple-element.18.s0), channel_id=1, source_target_pairs={{0,2},{1,3},{2,0},{3,1},{4,6},{5,7},{6,4},{7,5},{8,10},{9,11},{10,... | collective-permute-start | bytes 24584 | tf_op jit(solution)/shard_map/ppermute | solution.py:259
  9.7 3.7 %collective-permute-start.2 = (f32[8,256]{1,0:T(8,128)S(1)}, f32[8,256]{1,0:T(8,128)S(1)}, u32[]{:S(2)}, u32[]{:S(2)}) collective-permute-start(f32[8,256]{1,0:T(8,128)S(1)} %get-tuple-element.18.s0), channel_id=1, source_target_pairs={{0,3},{1,2},{2,1},{3,0},{4,7},{5,6},{6,5},{7,4},{8,11},{9,10},{10,... | collective-permute-start | bytes 24584 | tf_op jit(solution)/shard_map/ppermute | solution.py:259
  45.2 6.4 %collective-permute-start.4 = (bf16[16,4224]{1,0:T(8,128)(2,1)S(1)}, bf16[16,4224]{1,0:T(8,128)(2,1)S(1)}, u32[]{:S(2)}, u32[]{:S(2)}) collective-permute-start(bf16[16,4224]{1,0:T(8,128)(2,1)S(1)} %get-tuple-element.20), channel_id=1, source_target_pairs={{0,8},{8,0},{16,24},{24,16},{1,9},{9,1},{17,25},{25,17},{2,10},{10... | collective-permute-start | bytes 405512 | tf_op jit(solution)/shard_map/ppermute | solution.py:259
  45.6 28.9 %collective-permute-start.3 = (bf16[64,4224]{1,0:T(8,128)(2,1)S(1)}, bf16[64,4224]{1,0:T(8,128)(2,1)S(1)}, u32[]{:S(2)}, u32[]{:S(2)}) collective-permute-start(bf16[64,4224]{1,0:T(8,128)(2,1)S(1)} %get-tuple-element.19), channel_id=1, source_target_pairs={{0,0},{1,33},{2,66},{3,99},{32,1},{33,32},{34,67},{35,98},{64,2},{... | collective-permute-start | bytes 1622024 | tf_op jit(solution)/shard_map/ppermute | solution.py:284
  46.3 5.6 %collective-permute-start.13 = (bf16[16,4224]{1,0:T(8,128)(2,1)S(1)}, bf16[16,4224]{1,0:T(8,128)(2,1)S(1)}, u32[]{:S(2)}, u32[]{:S(2)}) collective-permute-start(bf16[16,4224]{1,0:T(8,128)(2,1)S(1)} %get-tuple-element.23), channel_id=1, source_target_pairs={{0,32},{32,0},{64,96},{96,64},{1,33},{33,1},{65,97},{97,65},{2,34}... | collective-permute-start | bytes 405512 | tf_op jit(solution)/shard_map/ppermute | solution.py:259
  48.0 5.8 %collective-permute-start.17 = (bf16[16,4224]{1,0:T(8,128)(2,1)S(1)}, bf16[16,4224]{1,0:T(8,128)(2,1)S(1)}, u32[]{:S(2)}, u32[]{:S(2)}) collective-permute-start(bf16[16,4224]{1,0:T(8,128)(2,1)S(1)} %get-tuple-element.24), channel_id=1, source_target_pairs={{0,24},{8,16},{16,8},{24,0},{1,25},{9,17},{17,9},{25,1},{2,26},{10... | collective-permute-start | bytes 405512 | tf_op jit(solution)/shard_map/ppermute | solution.py:259
  48.9 7.2 %collective-permute-start.21 = (bf16[16,4224]{1,0:T(8,128)(2,1)S(1)}, bf16[16,4224]{1,0:T(8,128)(2,1)S(1)}, u32[]{:S(2)}, u32[]{:S(2)}) collective-permute-start(bf16[16,4224]{1,0:T(8,128)(2,1)S(1)} %get-tuple-element.25), channel_id=1, source_target_pairs={{0,96},{32,64},{64,32},{96,0},{1,97},{33,65},{65,33},{97,1},{2,98}... | collective-permute-start | bytes 405512 | tf_op jit(solution)/shard_map/ppermute | solution.py:259
  51.7 6.3 %collective-permute-start.5 = (bf16[32,4224]{1,0:T(8,128)(2,1)S(1)}, bf16[32,4224]{1,0:T(8,128)(2,1)S(1)}, u32[]{:S(2)}, u32[]{:S(2)}) collective-permute-start(bf16[32,4224]{1,0:T(8,128)(2,1)S(1)} %pad_maximum_fusion.15), channel_id=1, source_target_pairs={{0,32},{32,0},{64,96},{96,64},{1,33},{33,1},{65,97},{97,65},{2,34}... | collective-permute-start | bytes 811016 | tf_op jit(solution)/shard_map/ppermute | solution.py:259
  52.0 7.9 %collective-permute-start.14 = (bf16[32,4224]{1,0:T(8,128)(2,1)S(1)}, bf16[32,4224]{1,0:T(8,128)(2,1)S(1)}, u32[]{:S(2)}, u32[]{:S(2)}) collective-permute-start(bf16[32,4224]{1,0:T(8,128)(2,1)S(1)} %pad_maximum_fusion.16), channel_id=1, source_target_pairs={{0,24},{8,16},{16,8},{24,0},{1,25},{9,17},{17,9},{25,1},{2,26},{10... | collective-permute-start | bytes 811016 | tf_op jit(solution)/shard_map/ppermute | solution.py:259
  53.8 7.5 %collective-permute-start.18 = (bf16[32,4224]{1,0:T(8,128)(2,1)S(1)}, bf16[32,4224]{1,0:T(8,128)(2,1)S(1)}, u32[]{:S(2)}, u32[]{:S(2)}) collective-permute-start(bf16[32,4224]{1,0:T(8,128)(2,1)S(1)} %pad_maximum_fusion.17), channel_id=1, source_target_pairs={{0,96},{32,64},{64,32},{96,0},{1,97},{33,65},{65,33},{97,1},{2,98}... | collective-permute-start | bytes 811016 | tf_op jit(solution)/shard_map/ppermute | solution.py:259
  56.2 6.9 %collective-permute-start.22 = (bf16[32,4224]{1,0:T(8,128)(2,1)S(1)}, bf16[32,4224]{1,0:T(8,128)(2,1)S(1)}, u32[]{:S(2)}, u32[]{:S(2)}) collective-permute-start(bf16[32,4224]{1,0:T(8,128)(2,1)S(1)} %pad_maximum_fusion.18), channel_id=1, source_target_pairs={{0,8},{8,0},{16,24},{24,16},{1,9},{9,1},{17,25},{25,17},{2,10},{10... | collective-permute-start | bytes 811016 | tf_op jit(solution)/shard_map/ppermute | solution.py:259
  58.2 12.4 %collective-permute-start.6 = (bf16[64,4224]{1,0:T(8,128)(2,1)S(1)}, bf16[64,4224]{1,0:T(8,128)(2,1)S(1)}, u32[]{:S(2)}, u32[]{:S(2)}) collective-permute-start(bf16[64,4224]{1,0:T(8,128)(2,1)S(1)} %pad_maximum_fusion.9), channel_id=1, source_target_pairs={{0,24},{8,16},{16,8},{24,0},{1,25},{9,17},{17,9},{25,1},{2,26},{10... | collective-permute-start | bytes 1622024 | tf_op jit(solution)/shard_map/ppermute | solution.py:259
  60.0 27.8 %collective-permute-start.15 = (bf16[64,4224]{1,0:T(8,128)(2,1)S(1)}, bf16[64,4224]{1,0:T(8,128)(2,1)S(1)}, u32[]{:S(2)}, u32[]{:S(2)}) collective-permute-start(bf16[64,4224]{1,0:T(8,128)(2,1)S(1)} %pad_maximum_fusion.12), channel_id=1, source_target_pairs={{0,96},{32,64},{64,32},{96,0},{1,97},{33,65},{65,33},{97,1},{2,98}... | collective-permute-start | bytes 1622024 | tf_op jit(solution)/shard_map/ppermute | solution.py:259
  61.5 27.6 %collective-permute-start.19 = (bf16[64,4224]{1,0:T(8,128)(2,1)S(1)}, bf16[64,4224]{1,0:T(8,128)(2,1)S(1)}, u32[]{:S(2)}, u32[]{:S(2)}) collective-permute-start(bf16[64,4224]{1,0:T(8,128)(2,1)S(1)} %pad_maximum_fusion.13), channel_id=1, source_target_pairs={{0,8},{8,0},{16,24},{24,16},{1,9},{9,1},{17,25},{25,17},{2,10},{10... | collective-permute-start | bytes 1622024 | tf_op jit(solution)/shard_map/ppermute | solution.py:259
  63.2 26.2 %collective-permute-start.23 = (bf16[64,4224]{1,0:T(8,128)(2,1)S(1)}, bf16[64,4224]{1,0:T(8,128)(2,1)S(1)}, u32[]{:S(2)}, u32[]{:S(2)}) collective-permute-start(bf16[64,4224]{1,0:T(8,128)(2,1)S(1)} %pad_maximum_fusion.14), channel_id=1, source_target_pairs={{0,32},{32,0},{64,96},{96,64},{1,33},{33,1},{65,97},{97,65},{2,34}... | collective-permute-start | bytes 1622024 | tf_op jit(solution)/shard_map/ppermute | solution.py:259
  70.9 51.9 %collective-permute-start.12 = (bf16[128,4224]{1,0:T(8,128)(2,1)S(1)}, bf16[128,4224]{1,0:T(8,128)(2,1)S(1)}, u32[]{:S(2)}, u32[]{:S(2)}) collective-permute-start(bf16[128,4224]{1,0:T(8,128)(2,1)S(1)} %pad_maximum_fusion.5.refs_0_), channel_id=1, source_target_pairs={{0,96},{32,64},{64,32},{96,0},{1,97},{33,65},{65,33},{97,1},{2,98}... | collective-permute-start | bytes 3244040 | tf_op jit(solution)/shard_map/ppermute | solution.py:259
  74.6 18.5 %collective-permute-start.7 = (bf16[32,4224]{1,0:T(8,128)(2,1)S(1)}, bf16[32,4224]{1,0:T(8,128)(2,1)S(1)}, u32[]{:S(2)}, u32[]{:S(2)}) collective-permute-start(bf16[32,4224]{1,0:T(8,128)(2,1)S(1)} %get-tuple-element.21), channel_id=1, source_target_pairs={{0,1},{1,0},{2,3},{3,2},{4,5},{5,4},{6,7},{7,6},{8,9},{9,8},{10,11... | collective-permute-start | bytes 811016 | tf_op jit(solution)/shard_map/ppermute | solution.py:259
  87.8 7.4 %collective-permute-start.9 = (bf16[32,4224]{1,0:T(8,128)(2,1)S(1)}, bf16[32,4224]{1,0:T(8,128)(2,1)S(1)}, u32[]{:S(2)}, u32[]{:S(2)}) collective-permute-start(bf16[32,4224]{1,0:T(8,128)(2,1)S(1)} %get-tuple-element.22), channel_id=1, source_target_pairs={{0,3},{1,2},{2,1},{3,0},{4,7},{5,6},{6,5},{7,4},{8,11},{9,10},{10,... | collective-permute-start | bytes 811016 | tf_op jit(solution)/shard_map/ppermute | solution.py:259
  89.0 34.1 %collective-permute-start.16 = (bf16[128,4224]{1,0:T(8,128)(2,1)S(1)}, bf16[128,4224]{1,0:T(8,128)(2,1)S(1)}, u32[]{:S(2)}, u32[]{:S(2)}) collective-permute-start(bf16[128,4224]{1,0:T(8,128)(2,1)S(1)} %pad_maximum_fusion.6), channel_id=1, source_target_pairs={{0,8},{8,0},{16,24},{24,16},{1,9},{9,1},{17,25},{25,17},{2,10},{10... | collective-permute-start | bytes 3244040 | tf_op jit(solution)/shard_map/ppermute | solution.py:259
  89.4 34.1 %collective-permute-start.20 = (bf16[128,4224]{1,0:T(8,128)(2,1)S(1)}, bf16[128,4224]{1,0:T(8,128)(2,1)S(1)}, u32[]{:S(2)}, u32[]{:S(2)}) collective-permute-start(bf16[128,4224]{1,0:T(8,128)(2,1)S(1)} %pad_maximum_fusion.7), channel_id=1, source_target_pairs={{0,32},{32,0},{64,96},{96,64},{1,33},{33,1},{65,97},{97,65},{2,34}... | collective-permute-start | bytes 3244040 | tf_op jit(solution)/shard_map/ppermute | solution.py:259
  93.1 31.1 %collective-permute-start.24 = (bf16[128,4224]{1,0:T(8,128)(2,1)S(1)}, bf16[128,4224]{1,0:T(8,128)(2,1)S(1)}, u32[]{:S(2)}, u32[]{:S(2)}) collective-permute-start(bf16[128,4224]{1,0:T(8,128)(2,1)S(1)} %pad_maximum_fusion.8), channel_id=1, source_target_pairs={{0,24},{8,16},{16,8},{24,0},{1,25},{9,17},{17,9},{25,1},{2,26},{10... | collective-permute-start | bytes 3244040 | tf_op jit(solution)/shard_map/ppermute | solution.py:259
  95.2 12.3 %collective-permute-start.8 = (bf16[64,4224]{1,0:T(8,128)(2,1)S(1)}, bf16[64,4224]{1,0:T(8,128)(2,1)S(1)}, u32[]{:S(2)}, u32[]{:S(2)}) collective-permute-start(bf16[64,4224]{1,0:T(8,128)(2,1)S(1)} %pad_maximum_fusion.10), channel_id=1, source_target_pairs={{0,3},{1,2},{2,1},{3,0},{4,7},{5,6},{6,5},{7,4},{8,11},{9,10},{10,... | collective-permute-start | bytes 1622024 | tf_op jit(solution)/shard_map/ppermute | solution.py:259
  107.5 10.1 %collective-permute-start.10 = (bf16[64,4224]{1,0:T(8,128)(2,1)S(1)}, bf16[64,4224]{1,0:T(8,128)(2,1)S(1)}, u32[]{:S(2)}, u32[]{:S(2)}) collective-permute-start(bf16[64,4224]{1,0:T(8,128)(2,1)S(1)} %pad_maximum_fusion.11), channel_id=1, source_target_pairs={{0,1},{1,0},{2,3},{3,2},{4,5},{5,4},{6,7},{7,6},{8,9},{9,8},{10,11... | collective-permute-start | bytes 1622024 | tf_op jit(solution)/shard_map/ppermute | solution.py:259
  118.1 8.5 %collective-permute-start.11 = (bf16[256,4224]{1,0:T(8,128)(2,1)S(1)}, bf16[256,4224]{1,0:T(8,128)(2,1)S(1)}, u32[]{:S(2)}, u32[]{:S(2)}) collective-permute-start(bf16[256,4224]{1,0:T(8,128)(2,1)S(1)} %pad_maximum_fusion), channel_id=1, source_target_pairs={{0,4},{4,0},{1,5},{5,1},{2,6},{6,2},{3,7},{7,3},{8,12},{12,8},{9,1... | collective-permute-start | bytes 6488072 | tf_op jit(solution)/shard_map/ppermute | solution.py:255
  131.7 2.0 %collective-permute-start.25 = (f32[264,512]{1,0:T(8,128)S(1)}, f32[264,512]{1,0:T(8,128)S(1)}, u32[]{:S(2)}, u32[]{:S(2)}) collective-permute-start(f32[264,512]{1,0:T(8,128)S(1)} %get-tuple-element.28), channel_id=1, source_target_pairs={{0,4},{4,0},{1,5},{5,1},{2,6},{6,2},{3,7},{7,3},{8,12},{12,8},{9,1... | collective-permute-start | bytes 1622024 | tf_op jit(solution)/shard_map/ppermute | solution.py:255
  132.2 2.3 %collective-permute-start.26 = (f32[264,512]{1,0:T(8,128)S(1)}, f32[264,512]{1,0:T(8,128)S(1)}, u32[]{:S(2)}, u32[]{:S(2)}) collective-permute-start(f32[264,512]{1,0:T(8,128)S(1)} %get-tuple-element.29), channel_id=1, source_target_pairs={{0,4},{4,0},{1,5},{5,1},{2,6},{6,2},{3,7},{7,3},{8,12},{12,8},{9,1... | collective-permute-start | bytes 1622024 | tf_op jit(solution)/shard_map/ppermute | solution.py:255

commit v12 on v10

--- a/solution.py
+++ b/solution.py
@@ -51,10 +51,6 @@
     slot = lax.broadcasted_iota(jnp.int32, (1, SLOTS), 1)
     half = SLOTS // 2
     return slot < jnp.where(slot < half, counts_ref[0], half + counts_ref[1])
-
-
-def second_place(q):
-    return side(q, 1, False) * 2 + side(q, 3, True)
 
 
 def pick_kernel(index_ref, counts_ref, resid_ref, picked_ref, sums_ref):
@@ -94,7 +90,7 @@
 def norm_kernel(counts_ref, picked_ref, gain_ref, s0, s1, s2, s3, out_ref):
     squares = (s0[:1, :] + s2[:1, :]) + (s1[:1, :] + s3[:1, :])
     scale = lax.rsqrt(squares / 8192 + epsilon)
-    row = lax.broadcasted_iota(jnp.int32, (32, 1), 0)
+    row = lax.broadcasted_iota(jnp.int32, (PIECE, 1), 0)
     mark = jnp.where(row == 0, jnp.where(live_slots(counts_ref), 0.0, jnp.inf), 0.0).astype(bf16)
     for x in range(4):
         for c in range(2):
@@ -102,9 +98,7 @@
             rows = picked_ref[first : first + 256, :].astype(f32)
             short = (rows * scale * gain_ref[first : first + 256, :]).astype(bf16)
             for z in range(4):
-                low, high = z * 32, 128 + second_place(z) * 32
-                out_ref[z * 8 + x * 2 + c, :32, :] = short[low : low + 32, :] + mark
-                out_ref[z * 8 + x * 2 + c, 32:, :] = short[high : high + 32, :]
+                out_ref[z * 8 + x * 2 + c] = short[z * PIECE : (z + 1) * PIECE, :] + mark
 
 
 def norm(counts, picked, gain, sums):
@@ -161,6 +155,22 @@
     )(first, pieces)
 
 
+def behind_kernel(in_ref, *refs):
+    refs[-1][...] = in_ref[...]
+
+
+def behind(value, after):
+    vmem = pl.BlockSpec(memory_space=pltpu.VMEM)
+    return pl.pallas_call(
+        behind_kernel,
+        out_shape=jax.ShapeDtypeStruct(value.shape, value.dtype),
+        in_specs=[vmem] + [pl.BlockSpec(memory_space=pl.ANY)] * len(after),
+        out_specs=vmem,
+        compiler_params=params(4),
+        name="behind",
+    )(value, *after)
+
+
 def gram_kernel(blocks, rows_ref, *refs):
     streams, (own_ref, given_ref, cols_ref) = refs[:4], refs[4:]
     lane = lax.broadcasted_iota(jnp.int32, (16, 128), 1)
@@ -168,7 +178,7 @@
     for n, x in enumerate(blocks):
         for z in range(4):
             for s in range(4):
-                at = (z if s < 2 else 4 + second_place(z)) * 32 + s % 2 * 16
+                at = z * PIECE + s * 16
                 first = slot_of(s, x, z) * 16
                 cols_ref[n * 256 + at : n * 256 + at + 16, :] = streams[s][first : first + 16, :]
         inside = slice(n * 256, (n + 1) * 256)
@@ -262,21 +272,23 @@
     part = 1.0 / jnp.sum(loads).astype(f32)
     mine, *streams = pack(first, pieces)
 
-    places = [(q, u) for q in range(4) for u in range(4)]
-    turned = lax.ppermute(mine, ("z", "y"), [(q * 4 + u, u * 4 + (q ^ u)) for q, u in places])
-
     for step in range(4):
         for s in range(4):
             axis, flip = PARTNERS[(s + step) % 4]
             seen = [PARTNERS[(s + k) % 4][0] for k in range(step)]
             which = side(x if axis == "x" else z, flip, axis not in seen)
             streams[s] = meet(streams[s], axis, flip, which)
+        if step == 0:
+            places = [(q, u) for q in range(4) for u in range(4)]
+            turned = lax.ppermute(
+                behind(mine, streams), ("z", "y"), [(q * 4 + u, u * 4 + (q ^ u)) for q, u in places]
+            )
+        if step == 1:
+            rows = behind(turned, streams)
 
     q = y ^ z
-    low, high = turned[:32], turned[32:]
-    low, high = meet(low, "y", 1, side(q, 1, True)), meet(high, "y", 3, side(q, 3, True))
-    low, high = meet(low, "y", 3, side(q, 3, False)), meet(high, "y", 1, side(q, 1, False))
-    rows = join(low, high)
+    rows = meet(rows, "y", 1, side(q, 1, True))
+    rows = meet(rows, "y", 3, side(q, 3, False))
     rows = join(rows, swap(rows))
 
     own, got = [], []

time: 133 us -> 130 us (0.977)
  starting transfers between devices: 50 us -> 41.2 us
  waiting for transfers between devices: 32.1 us -> 38.3 us
    ppermute x3, starting transfers between devices: 8.59 us -> 2.44 us  [swap(): return lax.ppermute(value, 'c', [(0, 1), (1, 0)])]
    ppermute x3, waiting for transfers between devices: 1.5 us -> 4.64 us  [swap(): return lax.ppermute(value, 'c', [(0, 1), (1, 0)])]
    ppermute x23 -> x21, waiting for transfers between devices: 30.6 us -> 33.7 us  [trade(): return lax.ppermute(value, axis, [(i, i ^ flip) for i in range(4)])]
    ppermute x23 -> x21, starting transfers between devices: 40.8 us -> 38 us  [trade(): return lax.ppermute(value, axis, [(i, i ^ flip) for i in range(4)])]
    select_n x17 -> x18, other arithmetic: 2.8 us -> 3.21 us  [meet(): jnp.where(which == 0, value, got)]
  transfers between devices with their start and end apart: 27 -> 25, of which waited for: 13 -> 15; matrix products, arithmetic and copies ran while one was open for 4% -> 4% of each run, Pallas kernels for 0% -> 0%
where the time goes in v12:
time: 130 us
  starting transfers between devices  41.2 us (32%)
  waiting for transfers between devices  38.3 us (29%)
  blocking collectives  27.3 us (21%)
  Pallas kernels  11.4 us (9%)
  other arithmetic  6.63 us (5%)
  local copies, waits for them, and re-layouts  3.38 us (3%)
  between operations  1.61 us (1%)
    ppermute x21, starting transfers between devices, trade(): return lax.ppermute(value, axis, [(i, i ^ flip) for i in range(4)])  38 us
    ppermute x21, waiting for transfers between devices, trade(): return lax.ppermute(value, axis, [(i, i ^ flip) for i in range(4)])  33.7 us
    all_to_all x1, blocking collectives, per_device(): pieces = lax.all_to_all(pieces, TOK, 0, 0, tiled=True)  27.3 us
    pallas_call x2, Pallas kernels, gram(): pl.pallas_call(lambda *refs: gram_kernel(blocks, *refs), out_shape=(jax.S...  4.8 us
    ppermute x3, waiting for transfers between devices, swap(): return lax.ppermute(value, 'c', [(0, 1), (1, 0)])  4.64 us
    select_n x18, other arithmetic, meet(): jnp.where(which == 0, value, got)  3.21 us
    unnamed x10, local copies, waits for them, and re-layouts  2.92 us
  transfers between devices with their start and end apart: 25, of which 15 were waited for; matrix products, arithmetic and copies ran while one was open for 4% of the time, Pallas kernels for 0%

profile of v12, /device:TPU:1, one launch (start us, length us, event | category | flops | bytes accessed | tf_op | source)
XLA Modules:
  0.0 129.7 jit_solution(84291501009395402)
XLA Ops:
  0.6 1.6 %copy-done = bf16[512,2048]{1,0:T(8,128)(2,1)S(1)} copy-done((bf16[512,2048]{1,0:T(8,128)(2,1)S(1)}, bf16[512,2048]{1,0:T(8,128)(2,1)}, u32[]{:S(2)}) %copy-start) | copy-done | bytes 2097176
  2.2 0.7 copy-done.1
  2.9 0.7 copy-done.3
  3.6 1.3 %pick.1 = (bf16[2048,256]{1,0:T(8,128)(2,1)S(1)}, f32[8,256]{1,0:T(8,128)S(1)}) custom-call(s32[1,256]{1,0:T(1,128)S(1)} %bitcast.8, s32[2]{0:T(128)S(1)} %copy-done.1, bf16[512,2048]{1,0:T(8,128)(2,1)S(1)} %copy-done), custom_call_target="tpu_custom_call" | custom-call | tf_op jit(solution)/shard_map/pick/pallas_call | solution.py:77
  4.9 2.2 %collective-permute-start = (f32[8,256]{1,0:T(8,128)S(1)}, f32[8,256]{1,0:T(8,128)S(1)}, u32[]{:S(2)}, u32[]{:S(2)}) collective-permute-start(f32[8,256]{1,0:T(8,128)S(1)} %get-tuple-element.16.s0), channel_id=1, source_target_pairs={{0,1},{1,0},{2,3},{3,2},{4,5},{5,4},{6,7},{7,6},{8,9},{9,8},{10,11... | collective-permute-start | bytes 24584 | tf_op jit(solution)/shard_map/ppermute | solution.py:251
  7.1 2.6 %collective-permute-start.1 = (f32[8,256]{1,0:T(8,128)S(1)}, f32[8,256]{1,0:T(8,128)S(1)}, u32[]{:S(2)}, u32[]{:S(2)}) collective-permute-start(f32[8,256]{1,0:T(8,128)S(1)} %get-tuple-element.16.s0), channel_id=1, source_target_pairs={{0,2},{1,3},{2,0},{3,1},{4,6},{5,7},{6,4},{7,5},{8,10},{9,11},{10,... | collective-permute-start | bytes 24584 | tf_op jit(solution)/shard_map/ppermute | solution.py:251
  10.1 1.0 collective-permute-done.1.s2
  11.1 2.3 %collective-permute-done.2.s3 = f32[8,256]{1,0:T(8,128)S(1)} collective-permute-done((f32[8,256]{1,0:T(8,128)S(1)}, f32[8,256]{1,0:T(8,128)S(1)}, u32[]{:S(2)}, u32[]{:S(2)}) %collective-permute-start.2) | collective-permute-done | bytes 8224 | tf_op jit(solution)/shard_map/ppermute | solution.py:251
  13.5 0.9 norm.1
  14.3 27.3 %all_to_all.5.in_ref = bf16[32,64,256]{2,1,0:T(8,128)(2,1)S(1)} all-to-all(bf16[32,64,256]{2,1,0:T(8,128)(2,1)S(1)} %norm.1), channel_id=1, replica_groups=mesh['z'=4,'x'=4,'c'=2,'y'=4] {'z','x','c'}, dimensions={0} | all-to-all | bytes 2097152 | tf_op jit(solution)/shard_map/all_to_all | solution.py:268
  41.6 1.2 fusion
  43.1 2.0 %pack.1 = (bf16[64,4224]{1,0:T(8,128)(2,1)S(1)}, bf16[16,4224]{1,0:T(8,128)(2,1)S(1)}, bf16[16,4224]{1,0:T(8,128)(2,1)S(1)}, bf16[16,4224]{1,0:T(8,128)(2,1)S(1)}, bf16[16,4224]{1,0:T(8,128)(2,1)S(1)}) custom-call(s32[32]{0:T(128)S(1)} %sub.3.first_ref, bf16[32,64,256]{2,1,0:T(8,128)(2,1)S(1)} %all_to_all.5.in_ref), custom_call_target="tpu_custom_call" | custom-call | tf_op jit(solution)/shard_map/pack/pallas_call | solution.py:146
  45.2 0.4 collective-permute-start.3
  45.6 0.4 collective-permute-start.4
  46.0 1.0 collective-permute-start.5
  47.0 0.6 collective-permute-start.6
  47.6 2.4 %collective-permute-done.3 = bf16[16,4224]{1,0:T(8,128)(2,1)S(1)} collective-permute-done((bf16[16,4224]{1,0:T(8,128)(2,1)S(1)}, bf16[16,4224]{1,0:T(8,128)(2,1)S(1)}, u32[]{:S(2)}, u32[]{:S(2)}) %collective-permute-start.3) | collective-permute-done | bytes 135200 | tf_op jit(solution)/shard_map/ppermute | solution.py:251
  50.2 1.2 collective-permute-start.8
  51.4 1.2 collective-permute-start.9
  52.8 1.0 collective-permute-start.10
  53.8 0.4 collective-permute-start.11
  54.2 0.7 collective-permute-start.7
  54.9 1.9 %collective-permute-done.8 = bf16[32,4224]{1,0:T(8,128)(2,1)S(1)} collective-permute-done((bf16[32,4224]{1,0:T(8,128)(2,1)S(1)}, bf16[32,4224]{1,0:T(8,128)(2,1)S(1)}, u32[]{:S(2)}, u32[]{:S(2)}) %collective-permute-start.8) | collective-permute-done | bytes 270368 | tf_op jit(solution)/shard_map/ppermute | solution.py:251
  57.0 2.3 %collective-permute-start.15 = (bf16[64,4224]{1,0:T(8,128)(2,1)S(1)}, bf16[64,4224]{1,0:T(8,128)(2,1)S(1)}, u32[]{:S(2)}, u32[]{:S(2)}) collective-permute-start(bf16[64,4224]{1,0:T(8,128)(2,1)S(1)} %pad_maximum_fusion.11.refs_0_), channel_id=1, source_target_pairs={{0,24},{8,16},{16,8},{24,0},{1,25},{9,17},{17,9},{25,1},{2,26},{10... | collective-permute-start | bytes 1622024 | tf_op jit(solution)/shard_map/ppermute | solution.py:251
  59.8 1.4 %collective-permute-start.17 = (bf16[64,4224]{1,0:T(8,128)(2,1)S(1)}, bf16[64,4224]{1,0:T(8,128)(2,1)S(1)}, u32[]{:S(2)}, u32[]{:S(2)}) collective-permute-start(bf16[64,4224]{1,0:T(8,128)(2,1)S(1)} %pad_maximum_fusion.12.refs_1_), channel_id=1, source_target_pairs={{0,96},{32,64},{64,32},{96,0},{1,97},{33,65},{65,33},{97,1},{2,98}... | collective-permute-start | bytes 1622024 | tf_op jit(solution)/shard_map/ppermute | solution.py:251
  61.3 0.7 collective-permute-start.19
  62.4 6.7 %collective-permute-start.12 = (bf16[64,4224]{1,0:T(8,128)(2,1)S(1)}, bf16[64,4224]{1,0:T(8,128)(2,1)S(1)}, u32[]{:S(2)}, u32[]{:S(2)}) collective-permute-start(bf16[64,4224]{1,0:T(8,128)(2,1)S(1)} %behind.3), channel_id=1, source_target_pairs={{0,1},{1,0},{2,3},{3,2},{4,5},{5,4},{6,7},{7,6},{8,9},{9,8},{10,11... | collective-permute-start | bytes 1622024 | tf_op jit(solution)/shard_map/ppermute | solution.py:251
  69.1 0.9 collective-permute-done.15
  70.3 1.7 %collective-permute-start.16 = (bf16[128,4224]{1,0:T(8,128)(2,1)S(1)}, bf16[128,4224]{1,0:T(8,128)(2,1)S(1)}, u32[]{:S(2)}, u32[]{:S(2)}) collective-permute-start(bf16[128,4224]{1,0:T(8,128)(2,1)S(1)} %pad_maximum_fusion.7), channel_id=1, source_target_pairs={{0,96},{32,64},{64,32},{96,0},{1,97},{33,65},{65,33},{97,1},{2,98}... | collective-permute-start | bytes 3244040 | tf_op jit(solution)/shard_map/ppermute | solution.py:251
  72.0 0.8 collective-permute-done.17
  73.1 2.2 %collective-permute-start.18 = (bf16[128,4224]{1,0:T(8,128)(2,1)S(1)}, bf16[128,4224]{1,0:T(8,128)(2,1)S(1)}, u32[]{:S(2)}, u32[]{:S(2)}) collective-permute-start(bf16[128,4224]{1,0:T(8,128)(2,1)S(1)} %pad_maximum_fusion.8), channel_id=1, source_target_pairs={{0,8},{8,0},{16,24},{24,16},{1,9},{9,1},{17,25},{25,17},{2,10},{10... | collective-permute-start | bytes 3244040 | tf_op jit(solution)/shard_map/ppermute | solution.py:251
  76.0 1.0 collective-permute-start.22
  76.9 2.4 %collective-permute-done.12 = bf16[64,4224]{1,0:T(8,128)(2,1)S(1)} collective-permute-done((bf16[64,4224]{1,0:T(8,128)(2,1)S(1)}, bf16[64,4224]{1,0:T(8,128)(2,1)S(1)}, u32[]{:S(2)}, u32[]{:S(2)}) %collective-permute-start.12) | collective-permute-done | bytes 540704 | tf_op jit(solution)/shard_map/ppermute | solution.py:251
  79.5 10.5 %collective-permute-start.13 = (bf16[128,4224]{1,0:T(8,128)(2,1)S(1)}, bf16[128,4224]{1,0:T(8,128)(2,1)S(1)}, u32[]{:S(2)}, u32[]{:S(2)}) collective-permute-start(bf16[128,4224]{1,0:T(8,128)(2,1)S(1)} %pad_maximum_fusion.6), channel_id=1, source_target_pairs={{0,3},{1,2},{2,1},{3,0},{4,7},{5,6},{6,5},{7,4},{8,11},{9,10},{10,... | collective-permute-start | bytes 3244040 | tf_op jit(solution)/shard_map/ppermute | solution.py:251
  90.1 5.9 %collective-permute-done.16 = bf16[128,4224]{1,0:T(8,128)(2,1)S(1)} collective-permute-done((bf16[128,4224]{1,0:T(8,128)(2,1)S(1)}, bf16[128,4224]{1,0:T(8,128)(2,1)S(1)}, u32[]{:S(2)}, u32[]{:S(2)}) %collective-permute-start.16) | collective-permute-done | bytes 1081376 | tf_op jit(solution)/shard_map/ppermute | solution.py:251
  96.3 0.4 broadcast_select_fusion.5
  97.0 1.5 %collective-permute-done.20 = bf16[128,4224]{1,0:T(8,128)(2,1)S(1)} collective-permute-done((bf16[128,4224]{1,0:T(8,128)(2,1)S(1)}, bf16[128,4224]{1,0:T(8,128)(2,1)S(1)}, u32[]{:S(2)}, u32[]{:S(2)}) %collective-permute-start.20) | collective-permute-done | bytes 1081376 | tf_op jit(solution)/shard_map/ppermute | solution.py:251
  98.8 14.3 %collective-permute-done.13 = bf16[128,4224]{1,0:T(8,128)(2,1)S(1)} collective-permute-done((bf16[128,4224]{1,0:T(8,128)(2,1)S(1)}, bf16[128,4224]{1,0:T(8,128)(2,1)S(1)}, u32[]{:S(2)}, u32[]{:S(2)}) %collective-permute-start.13) | collective-permute-done | bytes 1081376 | tf_op jit(solution)/shard_map/ppermute | solution.py:251
  113.6 1.8 %collective-permute-start.14 = (bf16[256,4224]{1,0:T(8,128)(2,1)S(1)}, bf16[256,4224]{1,0:T(8,128)(2,1)S(1)}, u32[]{:S(2)}, u32[]{:S(2)}) collective-permute-start(bf16[256,4224]{1,0:T(8,128)(2,1)S(1)} %pad_maximum_fusion.1), channel_id=1, source_target_pairs={{0,4},{4,0},{1,5},{5,1},{2,6},{6,2},{3,7},{7,3},{8,12},{12,8},{9,1... | collective-permute-start | bytes 6488072 | tf_op jit(solution)/shard_map/ppermute | solution.py:247
  115.6 0.4 broadcast_select_fusion.1
  116.2 3.2 %collective-permute-done.14 = bf16[256,4224]{1,0:T(8,128)(2,1)S(1)} collective-permute-done((bf16[256,4224]{1,0:T(8,128)(2,1)S(1)}, bf16[256,4224]{1,0:T(8,128)(2,1)S(1)}, u32[]{:S(2)}, u32[]{:S(2)}) %collective-permute-start.14) | collective-permute-done | bytes 2162720 | tf_op jit(solution)/shard_map/ppermute | solution.py:247
  119.4 0.6 pad_maximum_fusion.refs_0_
  119.9 2.4 %gram.2 = (f32[264,512]{1,0:T(8,128)S(1)}, f32[264,512]{1,0:T(8,128)S(1)}) custom-call(bf16[512,4224]{1,0:T(8,128)(2,1)S(1)} %pad_maximum_fusion.refs_0_, bf16[256,4224]{1,0:T(8,128)(2,1)S(1)} %pad_maximum_fusion.2.refs_1_, bf16[256,4224]{1,0:T(8,128)(2,1)S(1)} %pad_maximum_fusion.3.refs_2_, bf16[256,4224]{1,0:T(8,128)(2,1)S(1)} %pad_maximum_fusion.4.refs_3_, ...), custom_call_target="tpu_custom_call" | custom-call | flops 2147483648 | bytes 6291456 | tf_op jit(solution)/shard_map/gram/pallas_call | solution.py:203
  122.3 2.4 %gram.3 = (f32[264,512]{1,0:T(8,128)S(1)}, f32[264,512]{1,0:T(8,128)S(1)}) custom-call(bf16[512,4224]{1,0:T(8,128)(2,1)S(1)} %pad_maximum_fusion.refs_0_, bf16[256,4224]{1,0:T(8,128)(2,1)S(1)} %pad_maximum_fusion.2.refs_1_, bf16[256,4224]{1,0:T(8,128)(2,1)S(1)} %pad_maximum_fusion.3.refs_2_, bf16[256,4224]{1,0:T(8,128)(2,1)S(1)} %pad_maximum_fusion.4.refs_3_, ...), custom_call_target="tpu_custom_call" | custom-call | flops 2147483648 | bytes 6291456 | tf_op jit(solution)/shard_map/gram/pallas_call | solution.py:203
  124.7 0.5 collective-permute-start.23
  126.1 0.7 collective-permute-done.23.refs_2_
  126.8 0.8 collective-permute-done.24.refs_3_
  127.5 2.2 %finish.1 = (f32[1,2048]{1,0:T(1,128)}, f32[256,2048]{1,0:T(8,128)}) custom-call(s32[3]{0:T(128)S(1)} %pad_add_fusion.info_ref, f32[1]{0:T(128)} %bitcast.5.part_ref, f32[264,512]{1,0:T(8,128)S(1)} %get-tuple-element.22.refs_0_, f32[264,512]{1,0:T(8,128)S(1)} %get-tuple-element.23.refs_1_, f32[264,512]{1,0:T(8,128)S(1)} %collective-permute-done.23.refs_2_, ...), custom_call_target="tpu_custom_call" | custom-call | tf_op jit(solution)/shard_map/finish/pallas_call | solution.py:233
  (63 shorter events, 5.5 us)
Async XLA Ops:
  0.6 1.6 %copy-start = (bf16[512,2048]{1,0:T(8,128)(2,1)S(1)}, bf16[512,2048]{1,0:T(8,128)(2,1)}, u32[]{:S(2)}) copy-start(bf16[512,2048]{1,0:T(8,128)(2,1)} %resid_ref.1) | copy-start | bytes 6291460
  2.2 0.7 copy-start.1
  2.9 0.7 copy-start.3
  3.6 6.2 %copy-start.4 = (f32[2048]{0:T(1024)S(1)}, f32[2048]{0:T(1024)}, u32[]{:S(2)}) copy-start(f32[2048]{0:T(1024)} %param.5) | copy-start | bytes 24580
  3.6 9.9 %copy-start.2 = (s32[2]{0:T(128)S(1)}, s32[2]{0:T(128)}, u32[]{:S(2)}) copy-start(s32[2]{0:T(128)} %counts_ref.3) | copy-start | bytes 28
  4.9 5.2 %collective-permute-start = (f32[8,256]{1,0:T(8,128)S(1)}, f32[8,256]{1,0:T(8,128)S(1)}, u32[]{:S(2)}, u32[]{:S(2)}) collective-permute-start(f32[8,256]{1,0:T(8,128)S(1)} %get-tuple-element.16.s0), channel_id=1, source_target_pairs={{0,1},{1,0},{2,3},{3,2},{4,5},{5,4},{6,7},{7,6},{8,9},{9,8},{10,11... | collective-permute-start | bytes 24584 | tf_op jit(solution)/shard_map/ppermute | solution.py:251
  7.1 4.0 %collective-permute-start.1 = (f32[8,256]{1,0:T(8,128)S(1)}, f32[8,256]{1,0:T(8,128)S(1)}, u32[]{:S(2)}, u32[]{:S(2)}) collective-permute-start(f32[8,256]{1,0:T(8,128)S(1)} %get-tuple-element.16.s0), channel_id=1, source_target_pairs={{0,2},{1,3},{2,0},{3,1},{4,6},{5,7},{6,4},{7,5},{8,10},{9,11},{10,... | collective-permute-start | bytes 24584 | tf_op jit(solution)/shard_map/ppermute | solution.py:251
  9.7 3.7 %collective-permute-start.2 = (f32[8,256]{1,0:T(8,128)S(1)}, f32[8,256]{1,0:T(8,128)S(1)}, u32[]{:S(2)}, u32[]{:S(2)}) collective-permute-start(f32[8,256]{1,0:T(8,128)S(1)} %get-tuple-element.16.s0), channel_id=1, source_target_pairs={{0,3},{1,2},{2,1},{3,0},{4,7},{5,6},{6,5},{7,4},{8,11},{9,10},{10,... | collective-permute-start | bytes 24584 | tf_op jit(solution)/shard_map/ppermute | solution.py:251
  45.2 4.8 %collective-permute-start.3 = (bf16[16,4224]{1,0:T(8,128)(2,1)S(1)}, bf16[16,4224]{1,0:T(8,128)(2,1)S(1)}, u32[]{:S(2)}, u32[]{:S(2)}) collective-permute-start(bf16[16,4224]{1,0:T(8,128)(2,1)S(1)} %get-tuple-element.18), channel_id=1, source_target_pairs={{0,8},{8,0},{16,24},{24,16},{1,9},{9,1},{17,25},{25,17},{2,10},{10... | collective-permute-start | bytes 405512 | tf_op jit(solution)/shard_map/ppermute | solution.py:251
  45.6 4.5 %collective-permute-start.4 = (bf16[16,4224]{1,0:T(8,128)(2,1)S(1)}, bf16[16,4224]{1,0:T(8,128)(2,1)S(1)}, u32[]{:S(2)}, u32[]{:S(2)}) collective-permute-start(bf16[16,4224]{1,0:T(8,128)(2,1)S(1)} %get-tuple-element.19), channel_id=1, source_target_pairs={{0,32},{32,0},{64,96},{96,64},{1,33},{33,1},{65,97},{97,65},{2,34}... | collective-permute-start | bytes 405512 | tf_op jit(solution)/shard_map/ppermute | solution.py:251
  46.0 6.6 %collective-permute-start.5 = (bf16[16,4224]{1,0:T(8,128)(2,1)S(1)}, bf16[16,4224]{1,0:T(8,128)(2,1)S(1)}, u32[]{:S(2)}, u32[]{:S(2)}) collective-permute-start(bf16[16,4224]{1,0:T(8,128)(2,1)S(1)} %get-tuple-element.20), channel_id=1, source_target_pairs={{0,24},{8,16},{16,8},{24,0},{1,25},{9,17},{17,9},{25,1},{2,26},{10... | collective-permute-start | bytes 405512 | tf_op jit(solution)/shard_map/ppermute | solution.py:251
  47.0 5.6 %collective-permute-start.6 = (bf16[16,4224]{1,0:T(8,128)(2,1)S(1)}, bf16[16,4224]{1,0:T(8,128)(2,1)S(1)}, u32[]{:S(2)}, u32[]{:S(2)}) collective-permute-start(bf16[16,4224]{1,0:T(8,128)(2,1)S(1)} %get-tuple-element.21), channel_id=1, source_target_pairs={{0,96},{32,64},{64,32},{96,0},{1,97},{33,65},{65,33},{97,1},{2,98}... | collective-permute-start | bytes 405512 | tf_op jit(solution)/shard_map/ppermute | solution.py:251
  50.2 6.6 %collective-permute-start.8 = (bf16[32,4224]{1,0:T(8,128)(2,1)S(1)}, bf16[32,4224]{1,0:T(8,128)(2,1)S(1)}, u32[]{:S(2)}, u32[]{:S(2)}) collective-permute-start(bf16[32,4224]{1,0:T(8,128)(2,1)S(1)} %get-tuple-element.66.refs_0_), channel_id=1, source_target_pairs={{0,32},{32,0},{64,96},{96,64},{1,33},{33,1},{65,97},{97,65},{2,34}... | collective-permute-start | bytes 811016 | tf_op jit(solution)/shard_map/ppermute | solution.py:251
  51.4 8.2 %collective-permute-start.9 = (bf16[32,4224]{1,0:T(8,128)(2,1)S(1)}, bf16[32,4224]{1,0:T(8,128)(2,1)S(1)}, u32[]{:S(2)}, u32[]{:S(2)}) collective-permute-start(bf16[32,4224]{1,0:T(8,128)(2,1)S(1)} %get-tuple-element.67.refs_1_), channel_id=1, source_target_pairs={{0,24},{8,16},{16,8},{24,0},{1,25},{9,17},{17,9},{25,1},{2,26},{10... | collective-permute-start | bytes 811016 | tf_op jit(solution)/shard_map/ppermute | solution.py:251
  52.8 8.4 %collective-permute-start.10 = (bf16[32,4224]{1,0:T(8,128)(2,1)S(1)}, bf16[32,4224]{1,0:T(8,128)(2,1)S(1)}, u32[]{:S(2)}, u32[]{:S(2)}) collective-permute-start(bf16[32,4224]{1,0:T(8,128)(2,1)S(1)} %get-tuple-element.68.refs_2_), channel_id=1, source_target_pairs={{0,96},{32,64},{64,32},{96,0},{1,97},{33,65},{65,33},{97,1},{2,98}... | collective-permute-start | bytes 811016 | tf_op jit(solution)/shard_map/ppermute | solution.py:251
  53.8 8.3 %collective-permute-start.11 = (bf16[32,4224]{1,0:T(8,128)(2,1)S(1)}, bf16[32,4224]{1,0:T(8,128)(2,1)S(1)}, u32[]{:S(2)}, u32[]{:S(2)}) collective-permute-start(bf16[32,4224]{1,0:T(8,128)(2,1)S(1)} %get-tuple-element.69.refs_3_), channel_id=1, source_target_pairs={{0,8},{8,0},{16,24},{24,16},{1,9},{9,1},{17,25},{25,17},{2,10},{10... | collective-permute-start | bytes 811016 | tf_op jit(solution)/shard_map/ppermute | solution.py:251
  54.2 8.1 %collective-permute-start.7 = (bf16[64,4224]{1,0:T(8,128)(2,1)S(1)}, bf16[64,4224]{1,0:T(8,128)(2,1)S(1)}, u32[]{:S(2)}, u32[]{:S(2)}) collective-permute-start(bf16[64,4224]{1,0:T(8,128)(2,1)S(1)} %behind.2), channel_id=1, source_target_pairs={{0,0},{1,33},{2,66},{3,99},{32,1},{33,32},{34,67},{35,98},{64,2},{... | collective-permute-start | bytes 1622024 | tf_op jit(solution)/shard_map/ppermute | solution.py:283
  57.0 13.0 %collective-permute-start.15 = (bf16[64,4224]{1,0:T(8,128)(2,1)S(1)}, bf16[64,4224]{1,0:T(8,128)(2,1)S(1)}, u32[]{:S(2)}, u32[]{:S(2)}) collective-permute-start(bf16[64,4224]{1,0:T(8,128)(2,1)S(1)} %pad_maximum_fusion.11.refs_0_), channel_id=1, source_target_pairs={{0,24},{8,16},{16,8},{24,0},{1,25},{9,17},{17,9},{25,1},{2,26},{10... | collective-permute-start | bytes 1622024 | tf_op jit(solution)/shard_map/ppermute | solution.py:251
  59.8 13.0 %collective-permute-start.17 = (bf16[64,4224]{1,0:T(8,128)(2,1)S(1)}, bf16[64,4224]{1,0:T(8,128)(2,1)S(1)}, u32[]{:S(2)}, u32[]{:S(2)}) collective-permute-start(bf16[64,4224]{1,0:T(8,128)(2,1)S(1)} %pad_maximum_fusion.12.refs_1_), channel_id=1, source_target_pairs={{0,96},{32,64},{64,32},{96,0},{1,97},{33,65},{65,33},{97,1},{2,98}... | collective-permute-start | bytes 1622024 | tf_op jit(solution)/shard_map/ppermute | solution.py:251
  61.3 14.0 %collective-permute-start.19 = (bf16[64,4224]{1,0:T(8,128)(2,1)S(1)}, bf16[64,4224]{1,0:T(8,128)(2,1)S(1)}, u32[]{:S(2)}, u32[]{:S(2)}) collective-permute-start(bf16[64,4224]{1,0:T(8,128)(2,1)S(1)} %pad_maximum_fusion.13.refs_2_), channel_id=1, source_target_pairs={{0,8},{8,0},{16,24},{24,16},{1,9},{9,1},{17,25},{25,17},{2,10},{10... | collective-permute-start | bytes 1622024 | tf_op jit(solution)/shard_map/ppermute | solution.py:251
  62.2 13.5 %collective-permute-start.21 = (bf16[64,4224]{1,0:T(8,128)(2,1)S(1)}, bf16[64,4224]{1,0:T(8,128)(2,1)S(1)}, u32[]{:S(2)}, u32[]{:S(2)}) collective-permute-start(bf16[64,4224]{1,0:T(8,128)(2,1)S(1)} %pad_maximum_fusion.14.refs_3_), channel_id=1, source_target_pairs={{0,32},{32,0},{64,96},{96,64},{1,33},{33,1},{65,97},{97,65},{2,34}... | collective-permute-start | bytes 1622024 | tf_op jit(solution)/shard_map/ppermute | solution.py:251
  62.4 16.9 %collective-permute-start.12 = (bf16[64,4224]{1,0:T(8,128)(2,1)S(1)}, bf16[64,4224]{1,0:T(8,128)(2,1)S(1)}, u32[]{:S(2)}, u32[]{:S(2)}) collective-permute-start(bf16[64,4224]{1,0:T(8,128)(2,1)S(1)} %behind.3), channel_id=1, source_target_pairs={{0,1},{1,0},{2,3},{3,2},{4,5},{5,4},{6,7},{7,6},{8,9},{9,8},{10,11... | collective-permute-start | bytes 1622024 | tf_op jit(solution)/shard_map/ppermute | solution.py:251
  70.3 25.6 %collective-permute-start.16 = (bf16[128,4224]{1,0:T(8,128)(2,1)S(1)}, bf16[128,4224]{1,0:T(8,128)(2,1)S(1)}, u32[]{:S(2)}, u32[]{:S(2)}) collective-permute-start(bf16[128,4224]{1,0:T(8,128)(2,1)S(1)} %pad_maximum_fusion.7), channel_id=1, source_target_pairs={{0,96},{32,64},{64,32},{96,0},{1,97},{33,65},{65,33},{97,1},{2,98}... | collective-permute-start | bytes 3244040 | tf_op jit(solution)/shard_map/ppermute | solution.py:251
  73.1 23.2 %collective-permute-start.18 = (bf16[128,4224]{1,0:T(8,128)(2,1)S(1)}, bf16[128,4224]{1,0:T(8,128)(2,1)S(1)}, u32[]{:S(2)}, u32[]{:S(2)}) collective-permute-start(bf16[128,4224]{1,0:T(8,128)(2,1)S(1)} %pad_maximum_fusion.8), channel_id=1, source_target_pairs={{0,8},{8,0},{16,24},{24,16},{1,9},{9,1},{17,25},{25,17},{2,10},{10... | collective-permute-start | bytes 3244040 | tf_op jit(solution)/shard_map/ppermute | solution.py:251
  75.6 22.9 %collective-permute-start.20 = (bf16[128,4224]{1,0:T(8,128)(2,1)S(1)}, bf16[128,4224]{1,0:T(8,128)(2,1)S(1)}, u32[]{:S(2)}, u32[]{:S(2)}) collective-permute-start(bf16[128,4224]{1,0:T(8,128)(2,1)S(1)} %pad_maximum_fusion.9), channel_id=1, source_target_pairs={{0,32},{32,0},{64,96},{96,64},{1,33},{33,1},{65,97},{97,65},{2,34}... | collective-permute-start | bytes 3244040 | tf_op jit(solution)/shard_map/ppermute | solution.py:251
  76.0 39.7 %collective-permute-start.22 = (bf16[128,4224]{1,0:T(8,128)(2,1)S(1)}, bf16[128,4224]{1,0:T(8,128)(2,1)S(1)}, u32[]{:S(2)}, u32[]{:S(2)}) collective-permute-start(bf16[128,4224]{1,0:T(8,128)(2,1)S(1)} %pad_maximum_fusion.10), channel_id=1, source_target_pairs={{0,24},{8,16},{16,8},{24,0},{1,25},{9,17},{17,9},{25,1},{2,26},{10... | collective-permute-start | bytes 3244040 | tf_op jit(solution)/shard_map/ppermute | solution.py:251
  79.5 33.6 %collective-permute-start.13 = (bf16[128,4224]{1,0:T(8,128)(2,1)S(1)}, bf16[128,4224]{1,0:T(8,128)(2,1)S(1)}, u32[]{:S(2)}, u32[]{:S(2)}) collective-permute-start(bf16[128,4224]{1,0:T(8,128)(2,1)S(1)} %pad_maximum_fusion.6), channel_id=1, source_target_pairs={{0,3},{1,2},{2,1},{3,0},{4,7},{5,6},{6,5},{7,4},{8,11},{9,10},{10,... | collective-permute-start | bytes 3244040 | tf_op jit(solution)/shard_map/ppermute | solution.py:251
  113.6 5.7 %collective-permute-start.14 = (bf16[256,4224]{1,0:T(8,128)(2,1)S(1)}, bf16[256,4224]{1,0:T(8,128)(2,1)S(1)}, u32[]{:S(2)}, u32[]{:S(2)}) collective-permute-start(bf16[256,4224]{1,0:T(8,128)(2,1)S(1)} %pad_maximum_fusion.1), channel_id=1, source_target_pairs={{0,4},{4,0},{1,5},{5,1},{2,6},{6,2},{3,7},{7,3},{8,12},{12,8},{9,1... | collective-permute-start | bytes 6488072 | tf_op jit(solution)/shard_map/ppermute | solution.py:247
  124.7 2.0 %collective-permute-start.23 = (f32[264,512]{1,0:T(8,128)S(1)}, f32[264,512]{1,0:T(8,128)S(1)}, u32[]{:S(2)}, u32[]{:S(2)}) collective-permute-start(f32[264,512]{1,0:T(8,128)S(1)} %get-tuple-element.24), channel_id=1, source_target_pairs={{0,4},{4,0},{1,5},{5,1},{2,6},{6,2},{3,7},{7,3},{8,12},{12,8},{9,1... | collective-permute-start | bytes 1622024 | tf_op jit(solution)/shard_map/ppermute | solution.py:247
  125.2 2.3 %collective-permute-start.24 = (f32[264,512]{1,0:T(8,128)S(1)}, f32[264,512]{1,0:T(8,128)S(1)}, u32[]{:S(2)}, u32[]{:S(2)}) collective-permute-start(f32[264,512]{1,0:T(8,128)S(1)} %get-tuple-element.25), channel_id=1, source_target_pairs={{0,4},{4,0},{1,5},{5,1},{2,6},{6,2},{3,7},{7,3},{8,12},{12,8},{9,1... | collective-permute-start | bytes 1622024 | tf_op jit(solution)/shard_map/ppermute | solution.py:247

commit v13 on v12

--- a/solution.py
+++ b/solution.py
@@ -132,23 +132,23 @@
         return 0
 
     lax.fori_loop(0, 32 // group, body, 0)
-    whole_ref, part_refs = out_refs[0], out_refs[1:]
-    rows = acc_ref[:, :LIVE]
-    whole_ref[:, :LIVE] = rows.astype(bf16)
-    lane = lax.broadcasted_iota(jnp.int32, (PIECE, 128), 1)
-    whole_ref[:, LIVE:] = spread(jnp.sum(rows, axis=1, keepdims=True), lane).astype(bf16)
-    for k, ref in enumerate(part_refs):
-        ref[...] = whole_ref[k * 16 : (k + 1) * 16, :]
+    for k, ref in enumerate(out_refs[2:]):
+        rows = acc_ref[k * 16 : (k + 1) * 16, :LIVE]
+        lane = lax.broadcasted_iota(jnp.int32, (16, 128), 1)
+        sums = spread(jnp.sum(rows, axis=1, keepdims=True), lane)
+        for into in (ref, out_refs[k // 2].at[pl.ds(k % 2 * 16, 16)]):
+            into[:, :LIVE] = rows.astype(bf16)
+            into[:, LIVE:] = sums.astype(bf16)
 
 
 def pack(first, pieces):
     vmem = pl.BlockSpec(memory_space=pltpu.VMEM)
     return pl.pallas_call(
         pack_kernel,
-        out_shape=(jax.ShapeDtypeStruct((PIECE, LONG), bf16),)
+        out_shape=(jax.ShapeDtypeStruct((32, LONG), bf16),) * 2
         + (jax.ShapeDtypeStruct((16, LONG), bf16),) * 4,
         in_specs=[pl.BlockSpec(memory_space=pltpu.SMEM), vmem],
-        out_specs=(vmem,) * 5,
+        out_specs=(vmem,) * 6,
         scratch_shapes=[pltpu.VMEM((PIECE, LIVE + SLOTS + 128), f32)],
         compiler_params=params(10),
         name="pack",
@@ -270,7 +270,8 @@
     loads = jnp.sum((pieces[:, 0, :] < jnp.inf).astype(jnp.int32), axis=1)
     first = jnp.cumsum(loads) - loads
     part = 1.0 / jnp.sum(loads).astype(f32)
-    mine, *streams = pack(first, pieces)
+    *halves, s0, s1, s2, s3 = pack(first, pieces)
+    streams, turned = [s0, s1, s2, s3], []
 
     for step in range(4):
         for s in range(4):
@@ -278,13 +279,17 @@
             seen = [PARTNERS[(s + k) % 4][0] for k in range(step)]
             which = side(x if axis == "x" else z, flip, axis not in seen)
             streams[s] = meet(streams[s], axis, flip, which)
-        if step == 0:
+        if step < 2:
             places = [(q, u) for q in range(4) for u in range(4)]
-            turned = lax.ppermute(
-                behind(mine, streams), ("z", "y"), [(q * 4 + u, u * 4 + (q ^ u)) for q, u in places]
+            turned.append(
+                lax.ppermute(
+                    behind(halves[step], streams[:1]),
+                    ("z", "y"),
+                    [(q * 4 + u, u * 4 + (q ^ u)) for q, u in places],
+                )
             )
         if step == 1:
-            rows = behind(turned, streams)
+            rows = behind(join(*turned), streams)
 
     q = y ^ z
     rows = meet(rows, "y", 1, side(q, 1, True))

time: 130 us -> 131 us (level)
  waiting for transfers between devices: 38.3 us -> 40.4 us
    ppermute x21, starting transfers between devices: 38 us -> 35.6 us  [trade(): return lax.ppermute(value, axis, [(i, i ^ flip) for i in range(4)])]
    ppermute x21, waiting for transfers between devices: 33.7 us -> 36 us  [trade(): return lax.ppermute(value, axis, [(i, i ^ flip) for i in range(4)])]
  transfers between devices with their start and end apart: 25 -> 26, of which waited for: 15 -> 13; matrix products, arithmetic and copies ran while one was open for 4% -> 4% of each run, Pallas kernels for 0% -> 0%
where the time goes in v13:
time: 131 us
  waiting for transfers between devices  40.4 us (31%)
  starting transfers between devices  40 us (31%)
  blocking collectives  27.3 us (21%)
  Pallas kernels  11.4 us (9%)
  other arithmetic  6.75 us (5%)
  local copies, waits for them, and re-layouts  3.38 us (3%)
  between operations  1.72 us (1%)
    ppermute x21, waiting for transfers between devices, trade(): return lax.ppermute(value, axis, [(i, i ^ flip) for i in range(4)])  36 us
    ppermute x21, starting transfers between devices, trade(): return lax.ppermute(value, axis, [(i, i ^ flip) for i in range(4)])  35.6 us
    all_to_all x1, blocking collectives, per_device(): pieces = lax.all_to_all(pieces, TOK, 0, 0, tiled=True)  27.3 us
    pallas_call x2, Pallas kernels, gram(): pl.pallas_call(lambda *refs: gram_kernel(blocks, *refs), out_shape=(jax.S...  4.8 us
    ppermute x3, waiting for transfers between devices, swap(): return lax.ppermute(value, 'c', [(0, 1), (1, 0)])  4.44 us
    select_n x18, other arithmetic, meet(): jnp.where(which == 0, value, got)  3.21 us
    ppermute x3, starting transfers between devices, swap(): return lax.ppermute(value, 'c', [(0, 1), (1, 0)])  3.02 us
    unnamed x10, local copies, waits for them, and re-layouts  2.92 us
  transfers between devices with their start and end apart: 26, of which 13 were waited for; matrix products, arithmetic and copies ran while one was open for 4% of the time, Pallas kernels for 0%

profile of v13, /device:TPU:1, one launch (start us, length us, event | category | flops | bytes accessed | tf_op | source)
XLA Modules:
  0.0 130.9 jit_solution(14435551156464604961)
XLA Ops:
  0.6 1.6 %copy-done = bf16[512,2048]{1,0:T(8,128)(2,1)S(1)} copy-done((bf16[512,2048]{1,0:T(8,128)(2,1)S(1)}, bf16[512,2048]{1,0:T(8,128)(2,1)}, u32[]{:S(2)}) %copy-start) | copy-done | bytes 2097176
  2.2 0.7 copy-done.1
  2.9 0.7 copy-done.3
  3.6 1.3 %pick.1 = (bf16[2048,256]{1,0:T(8,128)(2,1)S(1)}, f32[8,256]{1,0:T(8,128)S(1)}) custom-call(s32[1,256]{1,0:T(1,128)S(1)} %bitcast.8, s32[2]{0:T(128)S(1)} %copy-done.1, bf16[512,2048]{1,0:T(8,128)(2,1)S(1)} %copy-done), custom_call_target="tpu_custom_call" | custom-call | tf_op jit(solution)/shard_map/pick/pallas_call | solution.py:77
  4.9 2.2 %collective-permute-start = (f32[8,256]{1,0:T(8,128)S(1)}, f32[8,256]{1,0:T(8,128)S(1)}, u32[]{:S(2)}, u32[]{:S(2)}) collective-permute-start(f32[8,256]{1,0:T(8,128)S(1)} %get-tuple-element.17.s0), channel_id=1, source_target_pairs={{0,1},{1,0},{2,3},{3,2},{4,5},{5,4},{6,7},{7,6},{8,9},{9,8},{10,11... | collective-permute-start | bytes 24584 | tf_op jit(solution)/shard_map/ppermute | solution.py:251
  7.1 2.6 %collective-permute-start.1 = (f32[8,256]{1,0:T(8,128)S(1)}, f32[8,256]{1,0:T(8,128)S(1)}, u32[]{:S(2)}, u32[]{:S(2)}) collective-permute-start(f32[8,256]{1,0:T(8,128)S(1)} %get-tuple-element.17.s0), channel_id=1, source_target_pairs={{0,2},{1,3},{2,0},{3,1},{4,6},{5,7},{6,4},{7,5},{8,10},{9,11},{10,... | collective-permute-start | bytes 24584 | tf_op jit(solution)/shard_map/ppermute | solution.py:251
  10.1 1.0 collective-permute-done.1.s2
  11.1 2.3 %collective-permute-done.2.s3 = f32[8,256]{1,0:T(8,128)S(1)} collective-permute-done((f32[8,256]{1,0:T(8,128)S(1)}, f32[8,256]{1,0:T(8,128)S(1)}, u32[]{:S(2)}, u32[]{:S(2)}) %collective-permute-start.2) | collective-permute-done | bytes 8224 | tf_op jit(solution)/shard_map/ppermute | solution.py:251
  13.5 0.9 norm.1
  14.3 27.3 %all_to_all.5.in_ref = bf16[32,64,256]{2,1,0:T(8,128)(2,1)S(1)} all-to-all(bf16[32,64,256]{2,1,0:T(8,128)(2,1)S(1)} %norm.1), channel_id=1, replica_groups=mesh['z'=4,'x'=4,'c'=2,'y'=4] {'z','x','c'}, dimensions={0} | all-to-all | bytes 2097152 | tf_op jit(solution)/shard_map/all_to_all | solution.py:268
  41.6 1.3 fusion
  43.2 2.1 %pack.1 = (bf16[32,4224]{1,0:T(8,128)(2,1)S(1)}, bf16[32,4224]{1,0:T(8,128)(2,1)S(1)}, bf16[16,4224]{1,0:T(8,128)(2,1)S(1)}, bf16[16,4224]{1,0:T(8,128)(2,1)S(1)...) custom-call(s32[32]{0:T(128)S(1)} %sub.3.first_ref, bf16[32,64,256]{2,1,0:T(8,128)(2,1)S(1)} %all_to_all.5.in_ref), custom_call_target="tpu_custom_call" | custom-call | tf_op jit(solution)/shard_map/pack/pallas_call | solution.py:146
  45.2 0.4 collective-permute-start.3
  45.7 0.4 collective-permute-start.7
  46.1 1.0 collective-permute-start.9
  47.1 0.6 collective-permute-start.11
  47.7 2.4 %collective-permute-done.3 = bf16[16,4224]{1,0:T(8,128)(2,1)S(1)} collective-permute-done((bf16[16,4224]{1,0:T(8,128)(2,1)S(1)}, bf16[16,4224]{1,0:T(8,128)(2,1)S(1)}, u32[]{:S(2)}, u32[]{:S(2)}) %collective-permute-start.3) | collective-permute-done | bytes 135200 | tf_op jit(solution)/shard_map/ppermute | solution.py:251
  50.2 0.5 collective-permute-start.5
  50.7 0.7 collective-permute-start.4
  51.5 2.0 %collective-permute-start.8 = (bf16[32,4224]{1,0:T(8,128)(2,1)S(1)}, bf16[32,4224]{1,0:T(8,128)(2,1)S(1)}, u32[]{:S(2)}, u32[]{:S(2)}) collective-permute-start(bf16[32,4224]{1,0:T(8,128)(2,1)S(1)} %pad_maximum_fusion.17), channel_id=1, source_target_pairs={{0,24},{8,16},{16,8},{24,0},{1,25},{9,17},{17,9},{25,1},{2,26},{10... | collective-permute-start | bytes 811016 | tf_op jit(solution)/shard_map/ppermute | solution.py:251
  53.6 3.6 %collective-permute-start.10 = (bf16[32,4224]{1,0:T(8,128)(2,1)S(1)}, bf16[32,4224]{1,0:T(8,128)(2,1)S(1)}, u32[]{:S(2)}, u32[]{:S(2)}) collective-permute-start(bf16[32,4224]{1,0:T(8,128)(2,1)S(1)} %pad_maximum_fusion.18), channel_id=1, source_target_pairs={{0,96},{32,64},{64,32},{96,0},{1,97},{33,65},{65,33},{97,1},{2,98}... | collective-permute-start | bytes 811016 | tf_op jit(solution)/shard_map/ppermute | solution.py:251
  57.5 2.7 %collective-permute-start.16 = (bf16[64,4224]{1,0:T(8,128)(2,1)S(1)}, bf16[64,4224]{1,0:T(8,128)(2,1)S(1)}, u32[]{:S(2)}, u32[]{:S(2)}) collective-permute-start(bf16[64,4224]{1,0:T(8,128)(2,1)S(1)} %pad_maximum_fusion.11.refs_0_), channel_id=1, source_target_pairs={{0,24},{8,16},{16,8},{24,0},{1,25},{9,17},{17,9},{25,1},{2,26},{10... | collective-permute-start | bytes 1622024 | tf_op jit(solution)/shard_map/ppermute | solution.py:251
  60.3 3.5 %collective-permute-done.12 = bf16[32,4224]{1,0:T(8,128)(2,1)S(1)} collective-permute-done((bf16[32,4224]{1,0:T(8,128)(2,1)S(1)}, bf16[32,4224]{1,0:T(8,128)(2,1)S(1)}, u32[]{:S(2)}, u32[]{:S(2)}) %collective-permute-start.12) | collective-permute-done | bytes 270368 | tf_op jit(solution)/shard_map/ppermute | solution.py:251
  63.7 0.7 collective-permute-start.6
  64.6 3.5 %collective-permute-start.22 = (bf16[64,4224]{1,0:T(8,128)(2,1)S(1)}, bf16[64,4224]{1,0:T(8,128)(2,1)S(1)}, u32[]{:S(2)}, u32[]{:S(2)}) collective-permute-start(bf16[64,4224]{1,0:T(8,128)(2,1)S(1)} %pad_maximum_fusion.15.refs_3_), channel_id=1, source_target_pairs={{0,32},{32,0},{64,96},{96,64},{1,33},{33,1},{65,97},{97,65},{2,34}... | collective-permute-start | bytes 1622024 | tf_op jit(solution)/shard_map/ppermute | solution.py:251
  68.3 3.2 %collective-permute-start.18 = (bf16[64,4224]{1,0:T(8,128)(2,1)S(1)}, bf16[64,4224]{1,0:T(8,128)(2,1)S(1)}, u32[]{:S(2)}, u32[]{:S(2)}) collective-permute-start(bf16[64,4224]{1,0:T(8,128)(2,1)S(1)} %get-tuple-element.68.refs_1_), channel_id=1, source_target_pairs={{0,96},{32,64},{64,32},{96,0},{1,97},{33,65},{65,33},{97,1},{2,98}... | collective-permute-start | bytes 1622024 | tf_op jit(solution)/shard_map/ppermute | solution.py:251
  71.7 2.3 %collective-permute-start.13 = (bf16[64,4224]{1,0:T(8,128)(2,1)S(1)}, bf16[64,4224]{1,0:T(8,128)(2,1)S(1)}, u32[]{:S(2)}, u32[]{:S(2)}) collective-permute-start(bf16[64,4224]{1,0:T(8,128)(2,1)S(1)} %behind.5), channel_id=1, source_target_pairs={{0,1},{1,0},{2,3},{3,2},{4,5},{5,4},{6,7},{7,6},{8,9},{9,8},{10,11... | collective-permute-start | bytes 1622024 | tf_op jit(solution)/shard_map/ppermute | solution.py:251
  74.2 2.8 %collective-permute-start.17 = (bf16[128,4224]{1,0:T(8,128)(2,1)S(1)}, bf16[128,4224]{1,0:T(8,128)(2,1)S(1)}, u32[]{:S(2)}, u32[]{:S(2)}) collective-permute-start(bf16[128,4224]{1,0:T(8,128)(2,1)S(1)} %pad_maximum_fusion.7), channel_id=1, source_target_pairs={{0,96},{32,64},{64,32},{96,0},{1,97},{33,65},{65,33},{97,1},{2,98}... | collective-permute-start | bytes 3244040 | tf_op jit(solution)/shard_map/ppermute | solution.py:251
  77.1 1.5 %collective-permute-done.22 = bf16[64,4224]{1,0:T(8,128)(2,1)S(1)} collective-permute-done((bf16[64,4224]{1,0:T(8,128)(2,1)S(1)}, bf16[64,4224]{1,0:T(8,128)(2,1)S(1)}, u32[]{:S(2)}, u32[]{:S(2)}) %collective-permute-start.22) | collective-permute-done | bytes 540704 | tf_op jit(solution)/shard_map/ppermute | solution.py:251
  78.9 3.1 %collective-permute-done.18 = bf16[64,4224]{1,0:T(8,128)(2,1)S(1)} collective-permute-done((bf16[64,4224]{1,0:T(8,128)(2,1)S(1)}, bf16[64,4224]{1,0:T(8,128)(2,1)S(1)}, u32[]{:S(2)}, u32[]{:S(2)}) %collective-permute-start.18) | collective-permute-done | bytes 540704 | tf_op jit(solution)/shard_map/ppermute | solution.py:251
  82.4 1.0 collective-permute-done.20
  84.0 7.2 %collective-permute-start.14 = (bf16[128,4224]{1,0:T(8,128)(2,1)S(1)}, bf16[128,4224]{1,0:T(8,128)(2,1)S(1)}, u32[]{:S(2)}, u32[]{:S(2)}) collective-permute-start(bf16[128,4224]{1,0:T(8,128)(2,1)S(1)} %pad_maximum_fusion.6), channel_id=1, source_target_pairs={{0,3},{1,2},{2,1},{3,0},{4,7},{5,6},{6,5},{7,4},{8,11},{9,10},{10,... | collective-permute-start | bytes 3244040 | tf_op jit(solution)/shard_map/ppermute | solution.py:251
  91.2 12.9 %collective-permute-done.19 = bf16[128,4224]{1,0:T(8,128)(2,1)S(1)} collective-permute-done((bf16[128,4224]{1,0:T(8,128)(2,1)S(1)}, bf16[128,4224]{1,0:T(8,128)(2,1)S(1)}, u32[]{:S(2)}, u32[]{:S(2)}) %collective-permute-start.19) | collective-permute-done | bytes 1081376 | tf_op jit(solution)/shard_map/ppermute | solution.py:251
  104.7 0.5 collective-permute-done.17
  105.2 0.4 broadcast_select_fusion.7
  105.6 0.4 broadcast_select_fusion.3
  105.9 7.7 %collective-permute-done.14 = bf16[128,4224]{1,0:T(8,128)(2,1)S(1)} collective-permute-done((bf16[128,4224]{1,0:T(8,128)(2,1)S(1)}, bf16[128,4224]{1,0:T(8,128)(2,1)S(1)}, u32[]{:S(2)}, u32[]{:S(2)}) %collective-permute-start.14) | collective-permute-done | bytes 1081376 | tf_op jit(solution)/shard_map/ppermute | solution.py:251
  113.7 0.4 broadcast_select_fusion.9
  114.2 2.4 %collective-permute-start.15 = (bf16[256,4224]{1,0:T(8,128)(2,1)S(1)}, bf16[256,4224]{1,0:T(8,128)(2,1)S(1)}, u32[]{:S(2)}, u32[]{:S(2)}) collective-permute-start(bf16[256,4224]{1,0:T(8,128)(2,1)S(1)} %pad_maximum_fusion.1), channel_id=1, source_target_pairs={{0,4},{4,0},{1,5},{5,1},{2,6},{6,2},{3,7},{7,3},{8,12},{12,8},{9,1... | collective-permute-start | bytes 6488072 | tf_op jit(solution)/shard_map/ppermute | solution.py:247
  116.8 0.4 broadcast_select_fusion.1
  117.5 3.0 %collective-permute-done.15 = bf16[256,4224]{1,0:T(8,128)(2,1)S(1)} collective-permute-done((bf16[256,4224]{1,0:T(8,128)(2,1)S(1)}, bf16[256,4224]{1,0:T(8,128)(2,1)S(1)}, u32[]{:S(2)}, u32[]{:S(2)}) %collective-permute-start.15) | collective-permute-done | bytes 2162720 | tf_op jit(solution)/shard_map/ppermute | solution.py:247
  120.5 0.6 pad_maximum_fusion.refs_0_
  121.1 2.4 %gram.2 = (f32[264,512]{1,0:T(8,128)S(1)}, f32[264,512]{1,0:T(8,128)S(1)}) custom-call(bf16[512,4224]{1,0:T(8,128)(2,1)S(1)} %pad_maximum_fusion.refs_0_, bf16[256,4224]{1,0:T(8,128)(2,1)S(1)} %get-tuple-element.70.refs_1_, bf16[256,4224]{1,0:T(8,128)(2,1)S(1)} %pad_maximum_fusion.3.refs_2_, bf16[256,4224]{1,0:T(8,128)(2,1)S(1)} %pad_maximum_fusion.4.refs_3_, ...), custom_call_target="tpu_custom_call" | custom-call | flops 2147483648 | bytes 6291456 | tf_op jit(solution)/shard_map/gram/pallas_call | solution.py:203
  123.5 2.4 %gram.3 = (f32[264,512]{1,0:T(8,128)S(1)}, f32[264,512]{1,0:T(8,128)S(1)}) custom-call(bf16[512,4224]{1,0:T(8,128)(2,1)S(1)} %pad_maximum_fusion.refs_0_, bf16[256,4224]{1,0:T(8,128)(2,1)S(1)} %get-tuple-element.70.refs_1_, bf16[256,4224]{1,0:T(8,128)(2,1)S(1)} %pad_maximum_fusion.3.refs_2_, bf16[256,4224]{1,0:T(8,128)(2,1)S(1)} %pad_maximum_fusion.4.refs_3_, ...), custom_call_target="tpu_custom_call" | custom-call | flops 2147483648 | bytes 6291456 | tf_op jit(solution)/shard_map/gram/pallas_call | solution.py:203
  125.9 0.5 collective-permute-start.24
  127.3 0.6 collective-permute-done.24.refs_2_
  127.9 0.8 collective-permute-done.25.refs_3_
  128.7 2.2 %finish.1 = (f32[1,2048]{1,0:T(1,128)}, f32[256,2048]{1,0:T(8,128)}) custom-call(s32[3]{0:T(128)S(1)} %pad_add_fusion.info_ref, f32[1]{0:T(128)} %bitcast.5.part_ref, f32[264,512]{1,0:T(8,128)S(1)} %get-tuple-element.24.refs_0_, f32[264,512]{1,0:T(8,128)S(1)} %get-tuple-element.25.refs_1_, f32[264,512]{1,0:T(8,128)S(1)} %collective-permute-done.24.refs_2_, ...), custom_call_target="tpu_custom_call" | custom-call | tf_op jit(solution)/shard_map/finish/pallas_call | solution.py:233
  (67 shorter events, 4.5 us)
Async XLA Ops:
  0.6 1.6 %copy-start = (bf16[512,2048]{1,0:T(8,128)(2,1)S(1)}, bf16[512,2048]{1,0:T(8,128)(2,1)}, u32[]{:S(2)}) copy-start(bf16[512,2048]{1,0:T(8,128)(2,1)} %resid_ref.1) | copy-start | bytes 6291460
  2.2 0.7 copy-start.1
  2.9 0.7 copy-start.3
  3.6 6.2 %copy-start.4 = (f32[2048]{0:T(1024)S(1)}, f32[2048]{0:T(1024)}, u32[]{:S(2)}) copy-start(f32[2048]{0:T(1024)} %param.5) | copy-start | bytes 24580
  3.6 9.9 %copy-start.2 = (s32[2]{0:T(128)S(1)}, s32[2]{0:T(128)}, u32[]{:S(2)}) copy-start(s32[2]{0:T(128)} %counts_ref.3) | copy-start | bytes 28
  4.9 5.2 %collective-permute-start = (f32[8,256]{1,0:T(8,128)S(1)}, f32[8,256]{1,0:T(8,128)S(1)}, u32[]{:S(2)}, u32[]{:S(2)}) collective-permute-start(f32[8,256]{1,0:T(8,128)S(1)} %get-tuple-element.17.s0), channel_id=1, source_target_pairs={{0,1},{1,0},{2,3},{3,2},{4,5},{5,4},{6,7},{7,6},{8,9},{9,8},{10,11... | collective-permute-start | bytes 24584 | tf_op jit(solution)/shard_map/ppermute | solution.py:251
  7.1 4.0 %collective-permute-start.1 = (f32[8,256]{1,0:T(8,128)S(1)}, f32[8,256]{1,0:T(8,128)S(1)}, u32[]{:S(2)}, u32[]{:S(2)}) collective-permute-start(f32[8,256]{1,0:T(8,128)S(1)} %get-tuple-element.17.s0), channel_id=1, source_target_pairs={{0,2},{1,3},{2,0},{3,1},{4,6},{5,7},{6,4},{7,5},{8,10},{9,11},{10,... | collective-permute-start | bytes 24584 | tf_op jit(solution)/shard_map/ppermute | solution.py:251
  9.7 3.7 %collective-permute-start.2 = (f32[8,256]{1,0:T(8,128)S(1)}, f32[8,256]{1,0:T(8,128)S(1)}, u32[]{:S(2)}, u32[]{:S(2)}) collective-permute-start(f32[8,256]{1,0:T(8,128)S(1)} %get-tuple-element.17.s0), channel_id=1, source_target_pairs={{0,3},{1,2},{2,1},{3,0},{4,7},{5,6},{6,5},{7,4},{8,11},{9,10},{10,... | collective-permute-start | bytes 24584 | tf_op jit(solution)/shard_map/ppermute | solution.py:251
  45.2 4.9 %collective-permute-start.3 = (bf16[16,4224]{1,0:T(8,128)(2,1)S(1)}, bf16[16,4224]{1,0:T(8,128)(2,1)S(1)}, u32[]{:S(2)}, u32[]{:S(2)}) collective-permute-start(bf16[16,4224]{1,0:T(8,128)(2,1)S(1)} %get-tuple-element.19), channel_id=1, source_target_pairs={{0,8},{8,0},{16,24},{24,16},{1,9},{9,1},{17,25},{25,17},{2,10},{10... | collective-permute-start | bytes 405512 | tf_op jit(solution)/shard_map/ppermute | solution.py:251
  45.7 5.7 %collective-permute-start.7 = (bf16[16,4224]{1,0:T(8,128)(2,1)S(1)}, bf16[16,4224]{1,0:T(8,128)(2,1)S(1)}, u32[]{:S(2)}, u32[]{:S(2)}) collective-permute-start(bf16[16,4224]{1,0:T(8,128)(2,1)S(1)} %get-tuple-element.21), channel_id=1, source_target_pairs={{0,32},{32,0},{64,96},{96,64},{1,33},{33,1},{65,97},{97,65},{2,34}... | collective-permute-start | bytes 405512 | tf_op jit(solution)/shard_map/ppermute | solution.py:251
  46.1 7.4 %collective-permute-start.9 = (bf16[16,4224]{1,0:T(8,128)(2,1)S(1)}, bf16[16,4224]{1,0:T(8,128)(2,1)S(1)}, u32[]{:S(2)}, u32[]{:S(2)}) collective-permute-start(bf16[16,4224]{1,0:T(8,128)(2,1)S(1)} %get-tuple-element.22), channel_id=1, source_target_pairs={{0,24},{8,16},{16,8},{24,0},{1,25},{9,17},{17,9},{25,1},{2,26},{10... | collective-permute-start | bytes 405512 | tf_op jit(solution)/shard_map/ppermute | solution.py:251
  47.1 10.1 %collective-permute-start.11 = (bf16[16,4224]{1,0:T(8,128)(2,1)S(1)}, bf16[16,4224]{1,0:T(8,128)(2,1)S(1)}, u32[]{:S(2)}, u32[]{:S(2)}) collective-permute-start(bf16[16,4224]{1,0:T(8,128)(2,1)S(1)} %get-tuple-element.23), channel_id=1, source_target_pairs={{0,96},{32,64},{64,32},{96,0},{1,97},{33,65},{65,33},{97,1},{2,98}... | collective-permute-start | bytes 405512 | tf_op jit(solution)/shard_map/ppermute | solution.py:251
  50.2 7.2 %collective-permute-start.5 = (bf16[32,4224]{1,0:T(8,128)(2,1)S(1)}, bf16[32,4224]{1,0:T(8,128)(2,1)S(1)}, u32[]{:S(2)}, u32[]{:S(2)}) collective-permute-start(bf16[32,4224]{1,0:T(8,128)(2,1)S(1)} %pad_maximum_fusion.16.refs_0_), channel_id=1, source_target_pairs={{0,32},{32,0},{64,96},{96,64},{1,33},{33,1},{65,97},{97,65},{2,34}... | collective-permute-start | bytes 811016 | tf_op jit(solution)/shard_map/ppermute | solution.py:251
  50.7 20.9 %collective-permute-start.4 = (bf16[32,4224]{1,0:T(8,128)(2,1)S(1)}, bf16[32,4224]{1,0:T(8,128)(2,1)S(1)}, u32[]{:S(2)}, u32[]{:S(2)}) collective-permute-start(bf16[32,4224]{1,0:T(8,128)(2,1)S(1)} %behind.3), channel_id=1, source_target_pairs={{0,0},{1,33},{2,66},{3,99},{32,1},{33,32},{34,67},{35,98},{64,2},{... | collective-permute-start | bytes 811016 | tf_op jit(solution)/shard_map/ppermute | solution.py:285
  51.5 13.1 %collective-permute-start.8 = (bf16[32,4224]{1,0:T(8,128)(2,1)S(1)}, bf16[32,4224]{1,0:T(8,128)(2,1)S(1)}, u32[]{:S(2)}, u32[]{:S(2)}) collective-permute-start(bf16[32,4224]{1,0:T(8,128)(2,1)S(1)} %pad_maximum_fusion.17), channel_id=1, source_target_pairs={{0,24},{8,16},{16,8},{24,0},{1,25},{9,17},{17,9},{25,1},{2,26},{10... | collective-permute-start | bytes 811016 | tf_op jit(solution)/shard_map/ppermute | solution.py:251
  53.6 14.6 %collective-permute-start.10 = (bf16[32,4224]{1,0:T(8,128)(2,1)S(1)}, bf16[32,4224]{1,0:T(8,128)(2,1)S(1)}, u32[]{:S(2)}, u32[]{:S(2)}) collective-permute-start(bf16[32,4224]{1,0:T(8,128)(2,1)S(1)} %pad_maximum_fusion.18), channel_id=1, source_target_pairs={{0,96},{32,64},{64,32},{96,0},{1,97},{33,65},{65,33},{97,1},{2,98}... | collective-permute-start | bytes 811016 | tf_op jit(solution)/shard_map/ppermute | solution.py:251
  57.3 6.5 %collective-permute-start.12 = (bf16[32,4224]{1,0:T(8,128)(2,1)S(1)}, bf16[32,4224]{1,0:T(8,128)(2,1)S(1)}, u32[]{:S(2)}, u32[]{:S(2)}) collective-permute-start(bf16[32,4224]{1,0:T(8,128)(2,1)S(1)} %pad_maximum_fusion.19), channel_id=1, source_target_pairs={{0,8},{8,0},{16,24},{24,16},{1,9},{9,1},{17,25},{25,17},{2,10},{10... | collective-permute-start | bytes 811016 | tf_op jit(solution)/shard_map/ppermute | solution.py:251
  57.5 16.4 %collective-permute-start.16 = (bf16[64,4224]{1,0:T(8,128)(2,1)S(1)}, bf16[64,4224]{1,0:T(8,128)(2,1)S(1)}, u32[]{:S(2)}, u32[]{:S(2)}) collective-permute-start(bf16[64,4224]{1,0:T(8,128)(2,1)S(1)} %pad_maximum_fusion.11.refs_0_), channel_id=1, source_target_pairs={{0,24},{8,16},{16,8},{24,0},{1,25},{9,17},{17,9},{25,1},{2,26},{10... | collective-permute-start | bytes 1622024 | tf_op jit(solution)/shard_map/ppermute | solution.py:251
  63.7 7.9 %collective-permute-start.6 = (bf16[32,4224]{1,0:T(8,128)(2,1)S(1)}, bf16[32,4224]{1,0:T(8,128)(2,1)S(1)}, u32[]{:S(2)}, u32[]{:S(2)}) collective-permute-start(bf16[32,4224]{1,0:T(8,128)(2,1)S(1)} %behind.4), channel_id=1, source_target_pairs={{0,0},{1,33},{2,66},{3,99},{32,1},{33,32},{34,67},{35,98},{64,2},{... | collective-permute-start | bytes 811016 | tf_op jit(solution)/shard_map/ppermute | solution.py:285
  64.6 14.0 %collective-permute-start.22 = (bf16[64,4224]{1,0:T(8,128)(2,1)S(1)}, bf16[64,4224]{1,0:T(8,128)(2,1)S(1)}, u32[]{:S(2)}, u32[]{:S(2)}) collective-permute-start(bf16[64,4224]{1,0:T(8,128)(2,1)S(1)} %pad_maximum_fusion.15.refs_3_), channel_id=1, source_target_pairs={{0,32},{32,0},{64,96},{96,64},{1,33},{33,1},{65,97},{97,65},{2,34}... | collective-permute-start | bytes 1622024 | tf_op jit(solution)/shard_map/ppermute | solution.py:251
  68.3 13.7 %collective-permute-start.18 = (bf16[64,4224]{1,0:T(8,128)(2,1)S(1)}, bf16[64,4224]{1,0:T(8,128)(2,1)S(1)}, u32[]{:S(2)}, u32[]{:S(2)}) collective-permute-start(bf16[64,4224]{1,0:T(8,128)(2,1)S(1)} %get-tuple-element.68.refs_1_), channel_id=1, source_target_pairs={{0,96},{32,64},{64,32},{96,0},{1,97},{33,65},{65,33},{97,1},{2,98}... | collective-permute-start | bytes 1622024 | tf_op jit(solution)/shard_map/ppermute | solution.py:251
  71.6 11.8 %collective-permute-start.20 = (bf16[64,4224]{1,0:T(8,128)(2,1)S(1)}, bf16[64,4224]{1,0:T(8,128)(2,1)S(1)}, u32[]{:S(2)}, u32[]{:S(2)}) collective-permute-start(bf16[64,4224]{1,0:T(8,128)(2,1)S(1)} %get-tuple-element.69.refs_2_), channel_id=1, source_target_pairs={{0,8},{8,0},{16,24},{24,16},{1,9},{9,1},{17,25},{25,17},{2,10},{10... | collective-permute-start | bytes 1622024 | tf_op jit(solution)/shard_map/ppermute | solution.py:251
  71.7 12.1 %collective-permute-start.13 = (bf16[64,4224]{1,0:T(8,128)(2,1)S(1)}, bf16[64,4224]{1,0:T(8,128)(2,1)S(1)}, u32[]{:S(2)}, u32[]{:S(2)}) collective-permute-start(bf16[64,4224]{1,0:T(8,128)(2,1)S(1)} %behind.5), channel_id=1, source_target_pairs={{0,1},{1,0},{2,3},{3,2},{4,5},{5,4},{6,7},{7,6},{8,9},{9,8},{10,11... | collective-permute-start | bytes 1622024 | tf_op jit(solution)/shard_map/ppermute | solution.py:251
  74.2 30.9 %collective-permute-start.17 = (bf16[128,4224]{1,0:T(8,128)(2,1)S(1)}, bf16[128,4224]{1,0:T(8,128)(2,1)S(1)}, u32[]{:S(2)}, u32[]{:S(2)}) collective-permute-start(bf16[128,4224]{1,0:T(8,128)(2,1)S(1)} %pad_maximum_fusion.7), channel_id=1, source_target_pairs={{0,96},{32,64},{64,32},{96,0},{1,97},{33,65},{65,33},{97,1},{2,98}... | collective-permute-start | bytes 3244040 | tf_op jit(solution)/shard_map/ppermute | solution.py:251
  78.8 38.0 %collective-permute-start.23 = (bf16[128,4224]{1,0:T(8,128)(2,1)S(1)}, bf16[128,4224]{1,0:T(8,128)(2,1)S(1)}, u32[]{:S(2)}, u32[]{:S(2)}) collective-permute-start(bf16[128,4224]{1,0:T(8,128)(2,1)S(1)} %pad_maximum_fusion.10), channel_id=1, source_target_pairs={{0,24},{8,16},{16,8},{24,0},{1,25},{9,17},{17,9},{25,1},{2,26},{10... | collective-permute-start | bytes 3244040 | tf_op jit(solution)/shard_map/ppermute | solution.py:251
  82.3 21.9 %collective-permute-start.19 = (bf16[128,4224]{1,0:T(8,128)(2,1)S(1)}, bf16[128,4224]{1,0:T(8,128)(2,1)S(1)}, u32[]{:S(2)}, u32[]{:S(2)}) collective-permute-start(bf16[128,4224]{1,0:T(8,128)(2,1)S(1)} %pad_maximum_fusion.8), channel_id=1, source_target_pairs={{0,8},{8,0},{16,24},{24,16},{1,9},{9,1},{17,25},{25,17},{2,10},{10... | collective-permute-start | bytes 3244040 | tf_op jit(solution)/shard_map/ppermute | solution.py:251
  83.7 21.9 %collective-permute-start.21 = (bf16[128,4224]{1,0:T(8,128)(2,1)S(1)}, bf16[128,4224]{1,0:T(8,128)(2,1)S(1)}, u32[]{:S(2)}, u32[]{:S(2)}) collective-permute-start(bf16[128,4224]{1,0:T(8,128)(2,1)S(1)} %pad_maximum_fusion.9), channel_id=1, source_target_pairs={{0,32},{32,0},{64,96},{96,64},{1,33},{33,1},{65,97},{97,65},{2,34}... | collective-permute-start | bytes 3244040 | tf_op jit(solution)/shard_map/ppermute | solution.py:251
  84.0 29.7 %collective-permute-start.14 = (bf16[128,4224]{1,0:T(8,128)(2,1)S(1)}, bf16[128,4224]{1,0:T(8,128)(2,1)S(1)}, u32[]{:S(2)}, u32[]{:S(2)}) collective-permute-start(bf16[128,4224]{1,0:T(8,128)(2,1)S(1)} %pad_maximum_fusion.6), channel_id=1, source_target_pairs={{0,3},{1,2},{2,1},{3,0},{4,7},{5,6},{6,5},{7,4},{8,11},{9,10},{10,... | collective-permute-start | bytes 3244040 | tf_op jit(solution)/shard_map/ppermute | solution.py:251
  114.2 6.3 %collective-permute-start.15 = (bf16[256,4224]{1,0:T(8,128)(2,1)S(1)}, bf16[256,4224]{1,0:T(8,128)(2,1)S(1)}, u32[]{:S(2)}, u32[]{:S(2)}) collective-permute-start(bf16[256,4224]{1,0:T(8,128)(2,1)S(1)} %pad_maximum_fusion.1), channel_id=1, source_target_pairs={{0,4},{4,0},{1,5},{5,1},{2,6},{6,2},{3,7},{7,3},{8,12},{12,8},{9,1... | collective-permute-start | bytes 6488072 | tf_op jit(solution)/shard_map/ppermute | solution.py:247
  125.9 2.0 %collective-permute-start.24 = (f32[264,512]{1,0:T(8,128)S(1)}, f32[264,512]{1,0:T(8,128)S(1)}, u32[]{:S(2)}, u32[]{:S(2)}) collective-permute-start(f32[264,512]{1,0:T(8,128)S(1)} %get-tuple-element.26), channel_id=1, source_target_pairs={{0,4},{4,0},{1,5},{5,1},{2,6},{6,2},{3,7},{7,3},{8,12},{12,8},{9,1... | collective-permute-start | bytes 1622024 | tf_op jit(solution)/shard_map/ppermute | solution.py:247
  126.3 2.3 %collective-permute-start.25 = (f32[264,512]{1,0:T(8,128)S(1)}, f32[264,512]{1,0:T(8,128)S(1)}, u32[]{:S(2)}, u32[]{:S(2)}) collective-permute-start(f32[264,512]{1,0:T(8,128)S(1)} %get-tuple-element.27), channel_id=1, source_target_pairs={{0,4},{4,0},{1,5},{5,1},{2,6},{6,2},{3,7},{7,3},{8,12},{12,8},{9,1... | collective-permute-start | bytes 1622024 | tf_op jit(solution)/shard_map/ppermute | solution.py:247

commit v14 on v13

--- a/solution.py
+++ b/solution.py
@@ -90,7 +90,7 @@
 def norm_kernel(counts_ref, picked_ref, gain_ref, s0, s1, s2, s3, out_ref):
     squares = (s0[:1, :] + s2[:1, :]) + (s1[:1, :] + s3[:1, :])
     scale = lax.rsqrt(squares / 8192 + epsilon)
-    row = lax.broadcasted_iota(jnp.int32, (PIECE, 1), 0)
+    row = lax.broadcasted_iota(jnp.int32, (32, 1), 0)
     mark = jnp.where(row == 0, jnp.where(live_slots(counts_ref), 0.0, jnp.inf), 0.0).astype(bf16)
     for x in range(4):
         for c in range(2):
@@ -98,7 +98,9 @@
             rows = picked_ref[first : first + 256, :].astype(f32)
             short = (rows * scale * gain_ref[first : first + 256, :]).astype(bf16)
             for z in range(4):
-                out_ref[z * 8 + x * 2 + c] = short[z * PIECE : (z + 1) * PIECE, :] + mark
+                low, high = z * PIECE, (z ^ 2) * PIECE + 32
+                out_ref[z * 8 + x * 2 + c, :32, :] = short[low : low + 32, :] + mark
+                out_ref[z * 8 + x * 2 + c, 32:, :] = short[high : high + 32, :]
 
 
 def norm(counts, picked, gain, sums):
@@ -178,7 +180,7 @@
     for n, x in enumerate(blocks):
         for z in range(4):
             for s in range(4):
-                at = z * PIECE + s * 16
+                at = (z if s < 2 else z ^ 2) * PIECE + s * 16
                 first = slot_of(s, x, z) * 16
                 cols_ref[n * 256 + at : n * 256 + at + 16, :] = streams[s][first : first + 16, :]
         inside = slice(n * 256, (n + 1) * 256)
@@ -273,21 +275,20 @@
     *halves, s0, s1, s2, s3 = pack(first, pieces)
     streams, turned = [s0, s1, s2, s3], []
 
+    def send(half, turn):
+        places = [(q, u) for q in range(4) for u in range(4)]
+        return lax.ppermute(half, ("z", "y"), [(q * 4 + u, u * 4 + (q ^ u ^ turn)) for q, u in places])
+
+    turned.append(send(halves[0], 0))
+
     for step in range(4):
         for s in range(4):
             axis, flip = PARTNERS[(s + step) % 4]
             seen = [PARTNERS[(s + k) % 4][0] for k in range(step)]
             which = side(x if axis == "x" else z, flip, axis not in seen)
             streams[s] = meet(streams[s], axis, flip, which)
-        if step < 2:
-            places = [(q, u) for q in range(4) for u in range(4)]
-            turned.append(
-                lax.ppermute(
-                    behind(halves[step], streams[:1]),
-                    ("z", "y"),
-                    [(q * 4 + u, u * 4 + (q ^ u)) for q, u in places],
-                )
-            )
+        if step == 0:
+            turned.append(send(behind(halves[1], streams[:1]), 2))
         if step == 1:
             rows = behind(join(*turned), streams)
 

time: 131 us -> 135 us (1.031)
  local copies, waits for them, and re-layouts: 3.38 us -> 5.23 us
    ppermute x2, starting transfers between devices: 1.34 us -> 10.4 us  [send(): lax.ppermute(half, ('z', 'y'), [(q * 4 + u, u * 4 + (q ^ u ^ turn)) for q...]
    ppermute x21, starting transfers between devices: 35.6 us -> 27.7 us  [trade(): return lax.ppermute(value, axis, [(i, i ^ flip) for i in range(4)])]
    unnamed x10 -> x30, local copies, waits for them, and re-layouts: 2.92 us -> 4.78 us
  transfers between devices with their start and end apart: 26 -> 26, of which waited for: 13 -> 10; matrix products, arithmetic and copies ran while one was open for 4% -> 5% of each run, Pallas kernels for 0% -> 0%
where the time goes in v14:
time: 135 us; the launch traced here: 134 us
  starting transfers between devices  40.9 us (30%)
  waiting for transfers between devices  40.2 us (30%)
  blocking collectives  27.3 us (20%)
  Pallas kernels  11.4 us (8%)
  other arithmetic  7.75 us (6%)
  local copies, waits for them, and re-layouts  5.23 us (4%)
  between operations  1.81 us (1%)
    ppermute x21, waiting for transfers between devices, trade(): return lax.ppermute(value, axis, [(i, i ^ flip) for i in range(4)])  37 us
    ppermute x21, starting transfers between devices, trade(): return lax.ppermute(value, axis, [(i, i ^ flip) for i in range(4)])  27.7 us
    all_to_all x1, blocking collectives, per_device(): pieces = lax.all_to_all(pieces, TOK, 0, 0, tiled=True)  27.3 us
    ppermute x2, starting transfers between devices, send(): lax.ppermute(half, ('z', 'y'), [(q * 4 + u, u * 4 + (q ^ u ^ turn)) for q...  10.4 us
    pallas_call x2, Pallas kernels, gram(): pl.pallas_call(lambda *refs: gram_kernel(blocks, *refs), out_shape=(jax.S...  4.8 us
    unnamed x30, local copies, waits for them, and re-layouts  4.78 us
    select_n x18, other arithmetic, meet(): jnp.where(which == 0, value, got)  4.26 us
    ppermute x3, waiting for transfers between devices, swap(): return lax.ppermute(value, 'c', [(0, 1), (1, 0)])  3.17 us
  transfers between devices with their start and end apart: 26, of which 10 were waited for; matrix products, arithmetic and copies ran while one was open for 5% of the time, Pallas kernels for 0%

profile of v14, /device:TPU:1, one launch (start us, length us, event | category | flops | bytes accessed | tf_op | source)
XLA Modules:
  0.0 134.5 jit_solution(3647443239974092356)
XLA Ops:
  0.6 1.6 %copy-done = bf16[512,2048]{1,0:T(8,128)(2,1)S(1)} copy-done((bf16[512,2048]{1,0:T(8,128)(2,1)S(1)}, bf16[512,2048]{1,0:T(8,128)(2,1)}, u32[]{:S(2)}) %copy-start) | copy-done | bytes 2097176
  2.2 0.7 copy-done.1
  2.9 0.7 copy-done.3
  3.6 1.3 pick.1
  4.9 2.2 %collective-permute-start = (f32[8,256]{1,0:T(8,128)S(1)}, f32[8,256]{1,0:T(8,128)S(1)}, u32[]{:S(2)}, u32[]{:S(2)}) collective-permute-start(f32[8,256]{1,0:T(8,128)S(1)} %get-tuple-element.17.s0), channel_id=1, source_target_pairs={{0,1},{1,0},{2,3},{3,2},{4,5},{5,4},{6,7},{7,6},{8,9},{9,8},{10,11... | collective-permute-start | bytes 24584 | tf_op jit(solution)/shard_map/ppermute | solution.py:253
  7.1 2.6 %collective-permute-start.1 = (f32[8,256]{1,0:T(8,128)S(1)}, f32[8,256]{1,0:T(8,128)S(1)}, u32[]{:S(2)}, u32[]{:S(2)}) collective-permute-start(f32[8,256]{1,0:T(8,128)S(1)} %get-tuple-element.17.s0), channel_id=1, source_target_pairs={{0,2},{1,3},{2,0},{3,1},{4,6},{5,7},{6,4},{7,5},{8,10},{9,11},{10,... | collective-permute-start | bytes 24584 | tf_op jit(solution)/shard_map/ppermute | solution.py:253
  9.7 0.4 copy.7.gain_ref
  10.1 1.0 collective-permute-done.1.s2
  11.1 2.3 %collective-permute-done.2.s3 = f32[8,256]{1,0:T(8,128)S(1)} collective-permute-done((f32[8,256]{1,0:T(8,128)S(1)}, f32[8,256]{1,0:T(8,128)S(1)}, u32[]{:S(2)}, u32[]{:S(2)}) %collective-permute-start.2) | collective-permute-done | bytes 8224 | tf_op jit(solution)/shard_map/ppermute | solution.py:253
  13.5 0.9 norm.1
  14.3 27.3 %all_to_all.5.in_ref = bf16[32,64,256]{2,1,0:T(8,128)(2,1)S(1)} all-to-all(bf16[32,64,256]{2,1,0:T(8,128)(2,1)S(1)} %norm.1), channel_id=1, replica_groups=mesh['z'=4,'x'=4,'c'=2,'y'=4] {'z','x','c'}, dimensions={0} | all-to-all | bytes 2097152 | tf_op jit(solution)/shard_map/all_to_all | solution.py:270
  41.6 1.2 fusion
  43.1 2.1 %pack.1 = (bf16[32,4224]{1,0:T(8,128)(2,1)S(1)}, bf16[32,4224]{1,0:T(8,128)(2,1)S(1)}, bf16[16,4224]{1,0:T(8,128)(2,1)S(1)}, bf16[16,4224]{1,0:T(8,128)(2,1)S(1)...) custom-call(s32[32]{0:T(128)S(1)} %sub.3.first_ref, bf16[32,64,256]{2,1,0:T(8,128)(2,1)S(1)} %all_to_all.5.in_ref), custom_call_target="tpu_custom_call" | custom-call | tf_op jit(solution)/shard_map/pack/pallas_call | solution.py:148
  45.2 0.4 collective-permute-start.4
  45.6 0.7 collective-permute-start.3
  46.3 1.7 %collective-permute-start.7 = (bf16[16,4224]{1,0:T(8,128)(2,1)S(1)}, bf16[16,4224]{1,0:T(8,128)(2,1)S(1)}, u32[]{:S(2)}, u32[]{:S(2)}) collective-permute-start(bf16[16,4224]{1,0:T(8,128)(2,1)S(1)} %get-tuple-element.21), channel_id=1, source_target_pairs={{0,32},{32,0},{64,96},{96,64},{1,33},{33,1},{65,97},{97,65},{2,34}... | collective-permute-start | bytes 405512 | tf_op jit(solution)/shard_map/ppermute | solution.py:253
  48.0 0.9 collective-permute-start.9
  48.9 2.6 %collective-permute-start.11 = (bf16[16,4224]{1,0:T(8,128)(2,1)S(1)}, bf16[16,4224]{1,0:T(8,128)(2,1)S(1)}, u32[]{:S(2)}, u32[]{:S(2)}) collective-permute-start(bf16[16,4224]{1,0:T(8,128)(2,1)S(1)} %get-tuple-element.23), channel_id=1, source_target_pairs={{0,96},{32,64},{64,32},{96,0},{1,97},{33,65},{65,33},{97,1},{2,98}... | collective-permute-start | bytes 405512 | tf_op jit(solution)/shard_map/ppermute | solution.py:253
  52.0 9.7 %collective-permute-start.5 = (bf16[32,4224]{1,0:T(8,128)(2,1)S(1)}, bf16[32,4224]{1,0:T(8,128)(2,1)S(1)}, u32[]{:S(2)}, u32[]{:S(2)}) collective-permute-start(bf16[32,4224]{1,0:T(8,128)(2,1)S(1)} %behind.2), channel_id=1, source_target_pairs={{0,2},{1,35},{2,64},{3,97},{32,3},{33,34},{34,65},{35,96},{64,0},{... | collective-permute-start | bytes 811016 | tf_op jit(solution)/shard_map/ppermute | solution.py:280
  61.7 0.6 collective-permute-start.8
  62.4 2.1 %collective-permute-start.10 = (bf16[32,4224]{1,0:T(8,128)(2,1)S(1)}, bf16[32,4224]{1,0:T(8,128)(2,1)S(1)}, u32[]{:S(2)}, u32[]{:S(2)}) collective-permute-start(bf16[32,4224]{1,0:T(8,128)(2,1)S(1)} %pad_maximum_fusion.18), channel_id=1, source_target_pairs={{0,96},{32,64},{64,32},{96,0},{1,97},{33,65},{65,33},{97,1},{2,98}... | collective-permute-start | bytes 811016 | tf_op jit(solution)/shard_map/ppermute | solution.py:253
  64.6 1.0 collective-permute-start.12
  65.6 4.6 %collective-permute-done.8 = bf16[32,4224]{1,0:T(8,128)(2,1)S(1)} collective-permute-done((bf16[32,4224]{1,0:T(8,128)(2,1)S(1)}, bf16[32,4224]{1,0:T(8,128)(2,1)S(1)}, u32[]{:S(2)}, u32[]{:S(2)}) %collective-permute-start.8) | collective-permute-done | bytes 270368 | tf_op jit(solution)/shard_map/ppermute | solution.py:253
  70.4 0.6 collective-permute-done.10
  71.3 0.4 copy-done.4
  72.0 6.3 %collective-permute-start.13 = (bf16[64,4224]{1,0:T(8,128)(2,1)S(1)}, bf16[64,4224]{1,0:T(8,128)(2,1)}, u32[]{:S(2)}, u32[]{:S(2)}) collective-permute-start(bf16[64,4224]{1,0:T(8,128)(2,1)S(1)} %behind.3), channel_id=1, source_target_pairs={{0,1},{1,0},{2,3},{3,2},{4,5},{5,4},{6,7},{7,6},{8,9},{9,8},{10,11... | collective-permute-start | bytes 1622024 | tf_op jit(solution)/shard_map/ppermute | solution.py:253
  78.3 0.8 collective-permute-start.16
  79.1 2.8 %collective-permute-start.18 = (bf16[64,4224]{1,0:T(8,128)(2,1)S(1)}, bf16[64,4224]{1,0:T(8,128)(2,1)S(1)}, u32[]{:S(2)}, u32[]{:S(2)}) collective-permute-start(bf16[64,4224]{1,0:T(8,128)(2,1)S(1)} %get-tuple-element.69.refs_1_), channel_id=1, source_target_pairs={{0,96},{32,64},{64,32},{96,0},{1,97},{33,65},{65,33},{97,1},{2,98}... | collective-permute-start | bytes 1622024 | tf_op jit(solution)/shard_map/ppermute | solution.py:253
  81.9 8.7 %collective-permute-done.13 = bf16[64,4224]{1,0:T(8,128)(2,1)} collective-permute-done((bf16[64,4224]{1,0:T(8,128)(2,1)S(1)}, bf16[64,4224]{1,0:T(8,128)(2,1)}, u32[]{:S(2)}, u32[]{:S(2)}) %collective-permute-start.13) | collective-permute-done | bytes 540704 | tf_op jit(solution)/shard_map/ppermute | solution.py:253
  90.6 1.1 broadcast_select_fusion.19
  92.0 0.6 collective-permute-done.16
  93.2 0.7 copy-done.7
  94.3 0.6 collective-permute-start.19
  95.8 2.5 %collective-permute-start.23 = (bf16[128,4224]{1,0:T(8,128)(2,1)S(1)}, bf16[128,4224]{1,0:T(8,128)(2,1)S(1)}, u32[]{:S(2)}, u32[]{:S(2)}) collective-permute-start(bf16[128,4224]{1,0:T(8,128)(2,1)S(1)} %pad_maximum_fusion.10), channel_id=1, source_target_pairs={{0,24},{8,16},{16,8},{24,0},{1,25},{9,17},{17,9},{25,1},{2,26},{10... | collective-permute-start | bytes 3244040 | tf_op jit(solution)/shard_map/ppermute | solution.py:253
  98.3 19.2 %collective-permute-done.14 = bf16[128,4224]{1,0:T(8,128)(2,1)S(1)} collective-permute-done((bf16[128,4224]{1,0:T(8,128)(2,1)S(1)}, bf16[128,4224]{1,0:T(8,128)(2,1)S(1)}, u32[]{:S(2)}, u32[]{:S(2)}) %collective-permute-start.14) | collective-permute-done | bytes 1081376 | tf_op jit(solution)/shard_map/ppermute | solution.py:253
  118.0 2.2 %collective-permute-start.15 = (bf16[256,4224]{1,0:T(8,128)(2,1)S(1)}, bf16[256,4224]{1,0:T(8,128)(2,1)S(1)}, u32[]{:S(2)}, u32[]{:S(2)}) collective-permute-start(bf16[256,4224]{1,0:T(8,128)(2,1)S(1)} %pad_maximum_fusion.1), channel_id=1, source_target_pairs={{0,4},{4,0},{1,5},{5,1},{2,6},{6,2},{3,7},{7,3},{8,12},{12,8},{9,1... | collective-permute-start | bytes 6488072 | tf_op jit(solution)/shard_map/ppermute | solution.py:249
  120.2 0.4 broadcast_select_fusion.7
  120.8 0.4 broadcast_select_fusion.5
  121.2 0.4 broadcast_select_fusion.3
  121.9 0.4 broadcast_select_fusion.1
  122.4 1.7 %collective-permute-done.15 = bf16[256,4224]{1,0:T(8,128)(2,1)S(1)} collective-permute-done((bf16[256,4224]{1,0:T(8,128)(2,1)S(1)}, bf16[256,4224]{1,0:T(8,128)(2,1)S(1)}, u32[]{:S(2)}, u32[]{:S(2)}) %collective-permute-start.15) | collective-permute-done | bytes 2162720 | tf_op jit(solution)/shard_map/ppermute | solution.py:249
  124.1 0.6 pad_maximum_fusion.refs_0_
  124.7 2.4 %gram.2 = (f32[264,512]{1,0:T(8,128)S(1)}, f32[264,512]{1,0:T(8,128)S(1)}) custom-call(bf16[512,4224]{1,0:T(8,128)(2,1)S(1)} %pad_maximum_fusion.refs_0_, bf16[256,4224]{1,0:T(8,128)(2,1)S(1)} %pad_maximum_fusion.2.refs_1_, bf16[256,4224]{1,0:T(8,128)(2,1)S(1)} %pad_maximum_fusion.3.refs_2_, bf16[256,4224]{1,0:T(8,128)(2,1)S(1)} %pad_maximum_fusion.4.refs_3_, ...), custom_call_target="tpu_custom_call" | custom-call | flops 2147483648 | bytes 6291456 | tf_op jit(solution)/shard_map/gram/pallas_call | solution.py:205
  127.1 2.4 %gram.3 = (f32[264,512]{1,0:T(8,128)S(1)}, f32[264,512]{1,0:T(8,128)S(1)}) custom-call(bf16[512,4224]{1,0:T(8,128)(2,1)S(1)} %pad_maximum_fusion.refs_0_, bf16[256,4224]{1,0:T(8,128)(2,1)S(1)} %pad_maximum_fusion.2.refs_1_, bf16[256,4224]{1,0:T(8,128)(2,1)S(1)} %pad_maximum_fusion.3.refs_2_, bf16[256,4224]{1,0:T(8,128)(2,1)S(1)} %pad_maximum_fusion.4.refs_3_, ...), custom_call_target="tpu_custom_call" | custom-call | flops 2147483648 | bytes 6291456 | tf_op jit(solution)/shard_map/gram/pallas_call | solution.py:205
  129.5 0.5 collective-permute-start.24
  130.8 0.7 collective-permute-done.24.refs_2_
  131.5 0.8 collective-permute-done.25.refs_3_
  132.3 2.2 %finish.1 = (f32[1,2048]{1,0:T(1,128)}, f32[256,2048]{1,0:T(8,128)}) custom-call(s32[3]{0:T(128)S(1)} %pad_add_fusion.info_ref, f32[1]{0:T(128)} %bitcast.5.part_ref, f32[264,512]{1,0:T(8,128)S(1)} %get-tuple-element.24.refs_0_, f32[264,512]{1,0:T(8,128)S(1)} %get-tuple-element.25.refs_1_, f32[264,512]{1,0:T(8,128)S(1)} %collective-permute-done.24.refs_2_, ...), custom_call_target="tpu_custom_call" | custom-call | tf_op jit(solution)/shard_map/finish/pallas_call | solution.py:235
  (86 shorter events, 4.9 us)
Async XLA Ops:
  0.6 1.6 %copy-start = (bf16[512,2048]{1,0:T(8,128)(2,1)S(1)}, bf16[512,2048]{1,0:T(8,128)(2,1)}, u32[]{:S(2)}) copy-start(bf16[512,2048]{1,0:T(8,128)(2,1)} %resid_ref.1) | copy-start | bytes 6291460
  2.2 0.7 copy-start.1
  2.9 0.7 copy-start.3
  3.6 6.2 %copy-start.14 = (f32[2048]{0:T(1024)S(1)}, f32[2048]{0:T(1024)}, u32[]{:S(2)}) copy-start(f32[2048]{0:T(1024)} %param.5) | copy-start | bytes 24580
  3.6 9.9 %copy-start.2 = (s32[2]{0:T(128)S(1)}, s32[2]{0:T(128)}, u32[]{:S(2)}) copy-start(s32[2]{0:T(128)} %counts_ref.3) | copy-start | bytes 28
  4.9 5.2 %collective-permute-start = (f32[8,256]{1,0:T(8,128)S(1)}, f32[8,256]{1,0:T(8,128)S(1)}, u32[]{:S(2)}, u32[]{:S(2)}) collective-permute-start(f32[8,256]{1,0:T(8,128)S(1)} %get-tuple-element.17.s0), channel_id=1, source_target_pairs={{0,1},{1,0},{2,3},{3,2},{4,5},{5,4},{6,7},{7,6},{8,9},{9,8},{10,11... | collective-permute-start | bytes 24584 | tf_op jit(solution)/shard_map/ppermute | solution.py:253
  7.1 4.0 %collective-permute-start.1 = (f32[8,256]{1,0:T(8,128)S(1)}, f32[8,256]{1,0:T(8,128)S(1)}, u32[]{:S(2)}, u32[]{:S(2)}) collective-permute-start(f32[8,256]{1,0:T(8,128)S(1)} %get-tuple-element.17.s0), channel_id=1, source_target_pairs={{0,2},{1,3},{2,0},{3,1},{4,6},{5,7},{6,4},{7,5},{8,10},{9,11},{10,... | collective-permute-start | bytes 24584 | tf_op jit(solution)/shard_map/ppermute | solution.py:253
  9.7 3.7 %collective-permute-start.2 = (f32[8,256]{1,0:T(8,128)S(1)}, f32[8,256]{1,0:T(8,128)S(1)}, u32[]{:S(2)}, u32[]{:S(2)}) collective-permute-start(f32[8,256]{1,0:T(8,128)S(1)} %get-tuple-element.17.s0), channel_id=1, source_target_pairs={{0,3},{1,2},{2,1},{3,0},{4,7},{5,6},{6,5},{7,4},{8,11},{9,10},{10,... | collective-permute-start | bytes 24584 | tf_op jit(solution)/shard_map/ppermute | solution.py:253
  45.2 6.4 %collective-permute-start.4 = (bf16[16,4224]{1,0:T(8,128)(2,1)S(1)}, bf16[16,4224]{1,0:T(8,128)(2,1)S(1)}, u32[]{:S(2)}, u32[]{:S(2)}) collective-permute-start(bf16[16,4224]{1,0:T(8,128)(2,1)S(1)} %get-tuple-element.20), channel_id=1, source_target_pairs={{0,8},{8,0},{16,24},{24,16},{1,9},{9,1},{17,25},{25,17},{2,10},{10... | collective-permute-start | bytes 405512 | tf_op jit(solution)/shard_map/ppermute | solution.py:253
  45.6 26.2 %collective-permute-start.3 = (bf16[32,4224]{1,0:T(8,128)(2,1)S(1)}, bf16[32,4224]{1,0:T(8,128)(2,1)S(1)}, u32[]{:S(2)}, u32[]{:S(2)}) collective-permute-start(bf16[32,4224]{1,0:T(8,128)(2,1)S(1)} %get-tuple-element.18), channel_id=1, source_target_pairs={{0,0},{1,33},{2,66},{3,99},{32,1},{33,32},{34,67},{35,98},{64,2},{... | collective-permute-start | bytes 811016 | tf_op jit(solution)/shard_map/ppermute | solution.py:280
  46.3 5.6 %collective-permute-start.7 = (bf16[16,4224]{1,0:T(8,128)(2,1)S(1)}, bf16[16,4224]{1,0:T(8,128)(2,1)S(1)}, u32[]{:S(2)}, u32[]{:S(2)}) collective-permute-start(bf16[16,4224]{1,0:T(8,128)(2,1)S(1)} %get-tuple-element.21), channel_id=1, source_target_pairs={{0,32},{32,0},{64,96},{96,64},{1,33},{33,1},{65,97},{97,65},{2,34}... | collective-permute-start | bytes 405512 | tf_op jit(solution)/shard_map/ppermute | solution.py:253
  48.0 13.7 %collective-permute-start.9 = (bf16[16,4224]{1,0:T(8,128)(2,1)S(1)}, bf16[16,4224]{1,0:T(8,128)(2,1)S(1)}, u32[]{:S(2)}, u32[]{:S(2)}) collective-permute-start(bf16[16,4224]{1,0:T(8,128)(2,1)S(1)} %get-tuple-element.22), channel_id=1, source_target_pairs={{0,24},{8,16},{16,8},{24,0},{1,25},{9,17},{17,9},{25,1},{2,26},{10... | collective-permute-start | bytes 405512 | tf_op jit(solution)/shard_map/ppermute | solution.py:253
  48.9 13.4 %collective-permute-start.11 = (bf16[16,4224]{1,0:T(8,128)(2,1)S(1)}, bf16[16,4224]{1,0:T(8,128)(2,1)S(1)}, u32[]{:S(2)}, u32[]{:S(2)}) collective-permute-start(bf16[16,4224]{1,0:T(8,128)(2,1)S(1)} %get-tuple-element.23), channel_id=1, source_target_pairs={{0,96},{32,64},{64,32},{96,0},{1,97},{33,65},{65,33},{97,1},{2,98}... | collective-permute-start | bytes 405512 | tf_op jit(solution)/shard_map/ppermute | solution.py:253
  51.7 12.9 %collective-permute-start.6 = (bf16[32,4224]{1,0:T(8,128)(2,1)S(1)}, bf16[32,4224]{1,0:T(8,128)(2,1)S(1)}, u32[]{:S(2)}, u32[]{:S(2)}) collective-permute-start(bf16[32,4224]{1,0:T(8,128)(2,1)S(1)} %pad_maximum_fusion.16.refs_0_), channel_id=1, source_target_pairs={{0,32},{32,0},{64,96},{96,64},{1,33},{33,1},{65,97},{97,65},{2,34}... | collective-permute-start | bytes 811016 | tf_op jit(solution)/shard_map/ppermute | solution.py:253
  52.0 19.9 %collective-permute-start.5 = (bf16[32,4224]{1,0:T(8,128)(2,1)S(1)}, bf16[32,4224]{1,0:T(8,128)(2,1)S(1)}, u32[]{:S(2)}, u32[]{:S(2)}) collective-permute-start(bf16[32,4224]{1,0:T(8,128)(2,1)S(1)} %behind.2), channel_id=1, source_target_pairs={{0,2},{1,35},{2,64},{3,97},{32,3},{33,34},{34,65},{35,96},{64,0},{... | collective-permute-start | bytes 811016 | tf_op jit(solution)/shard_map/ppermute | solution.py:280
  61.7 8.5 %collective-permute-start.8 = (bf16[32,4224]{1,0:T(8,128)(2,1)S(1)}, bf16[32,4224]{1,0:T(8,128)(2,1)S(1)}, u32[]{:S(2)}, u32[]{:S(2)}) collective-permute-start(bf16[32,4224]{1,0:T(8,128)(2,1)S(1)} %pad_maximum_fusion.17), channel_id=1, source_target_pairs={{0,24},{8,16},{16,8},{24,0},{1,25},{9,17},{17,9},{25,1},{2,26},{10... | collective-permute-start | bytes 811016 | tf_op jit(solution)/shard_map/ppermute | solution.py:253
  62.4 8.6 %collective-permute-start.10 = (bf16[32,4224]{1,0:T(8,128)(2,1)S(1)}, bf16[32,4224]{1,0:T(8,128)(2,1)S(1)}, u32[]{:S(2)}, u32[]{:S(2)}) collective-permute-start(bf16[32,4224]{1,0:T(8,128)(2,1)S(1)} %pad_maximum_fusion.18), channel_id=1, source_target_pairs={{0,96},{32,64},{64,32},{96,0},{1,97},{33,65},{65,33},{97,1},{2,98}... | collective-permute-start | bytes 811016 | tf_op jit(solution)/shard_map/ppermute | solution.py:253
  64.6 6.7 %collective-permute-start.12 = (bf16[32,4224]{1,0:T(8,128)(2,1)S(1)}, bf16[32,4224]{1,0:T(8,128)(2,1)S(1)}, u32[]{:S(2)}, u32[]{:S(2)}) collective-permute-start(bf16[32,4224]{1,0:T(8,128)(2,1)S(1)} %pad_maximum_fusion.19), channel_id=1, source_target_pairs={{0,8},{8,0},{16,24},{24,16},{1,9},{9,1},{17,25},{25,17},{2,10},{10... | collective-permute-start | bytes 811016 | tf_op jit(solution)/shard_map/ppermute | solution.py:253
  65.6 5.5 %copy-start.10 = (bf16[32,4224]{1,0:T(8,128)(2,1)}, bf16[32,4224]{1,0:T(8,128)(2,1)S(1)}, u32[]{:S(2)}) copy-start(bf16[32,4224]{1,0:T(8,128)(2,1)S(1)} %get-tuple-element.58) | copy-start | bytes 811012
  65.6 5.5 %copy-start.12 = (bf16[32,4224]{1,0:T(8,128)(2,1)}, bf16[32,4224]{1,0:T(8,128)(2,1)S(1)}, u32[]{:S(2)}) copy-start(bf16[32,4224]{1,0:T(8,128)(2,1)S(1)} %get-tuple-element.59) | copy-start | bytes 811012
  70.4 0.8 copy-start.6
  70.4 0.8 copy-start.8
  71.1 0.7 copy-start.4
  72.0 18.7 %collective-permute-start.13 = (bf16[64,4224]{1,0:T(8,128)(2,1)S(1)}, bf16[64,4224]{1,0:T(8,128)(2,1)}, u32[]{:S(2)}, u32[]{:S(2)}) collective-permute-start(bf16[64,4224]{1,0:T(8,128)(2,1)S(1)} %behind.3), channel_id=1, source_target_pairs={{0,1},{1,0},{2,3},{3,2},{4,5},{5,4},{6,7},{7,6},{8,9},{9,8},{10,11... | collective-permute-start | bytes 1622024 | tf_op jit(solution)/shard_map/ppermute | solution.py:253
  78.3 14.2 %collective-permute-start.16 = (bf16[64,4224]{1,0:T(8,128)(2,1)S(1)}, bf16[64,4224]{1,0:T(8,128)(2,1)S(1)}, u32[]{:S(2)}, u32[]{:S(2)}) collective-permute-start(bf16[64,4224]{1,0:T(8,128)(2,1)S(1)} %get-tuple-element.68.refs_0_), channel_id=1, source_target_pairs={{0,24},{8,16},{16,8},{24,0},{1,25},{9,17},{17,9},{25,1},{2,26},{10... | collective-permute-start | bytes 1622024 | tf_op jit(solution)/shard_map/ppermute | solution.py:253
  79.1 14.1 %collective-permute-start.18 = (bf16[64,4224]{1,0:T(8,128)(2,1)S(1)}, bf16[64,4224]{1,0:T(8,128)(2,1)S(1)}, u32[]{:S(2)}, u32[]{:S(2)}) collective-permute-start(bf16[64,4224]{1,0:T(8,128)(2,1)S(1)} %get-tuple-element.69.refs_1_), channel_id=1, source_target_pairs={{0,96},{32,64},{64,32},{96,0},{1,97},{33,65},{65,33},{97,1},{2,98}... | collective-permute-start | bytes 1622024 | tf_op jit(solution)/shard_map/ppermute | solution.py:253
  81.9 13.0 %collective-permute-start.20 = (bf16[64,4224]{1,0:T(8,128)(2,1)S(1)}, bf16[64,4224]{1,0:T(8,128)(2,1)S(1)}, u32[]{:S(2)}, u32[]{:S(2)}) collective-permute-start(bf16[64,4224]{1,0:T(8,128)(2,1)S(1)} %get-tuple-element.70.refs_2_), channel_id=1, source_target_pairs={{0,8},{8,0},{16,24},{24,16},{1,9},{9,1},{17,25},{25,17},{2,10},{10... | collective-permute-start | bytes 1622024 | tf_op jit(solution)/shard_map/ppermute | solution.py:253
  81.9 13.6 %collective-permute-start.22 = (bf16[64,4224]{1,0:T(8,128)(2,1)S(1)}, bf16[64,4224]{1,0:T(8,128)(2,1)S(1)}, u32[]{:S(2)}, u32[]{:S(2)}) collective-permute-start(bf16[64,4224]{1,0:T(8,128)(2,1)S(1)} %get-tuple-element.71.refs_3_), channel_id=1, source_target_pairs={{0,32},{32,0},{64,96},{96,64},{1,33},{33,1},{65,97},{97,65},{2,34}... | collective-permute-start | bytes 1622024 | tf_op jit(solution)/shard_map/ppermute | solution.py:253
  91.8 1.0 copy-start.11
  91.8 1.0 copy-start.13
  91.9 25.6 %collective-permute-start.14 = (bf16[128,4224]{1,0:T(8,128)(2,1)S(1)}, bf16[128,4224]{1,0:T(8,128)(2,1)S(1)}, u32[]{:S(2)}, u32[]{:S(2)}) collective-permute-start(bf16[128,4224]{1,0:T(8,128)(2,1)S(1)} %pad_maximum_fusion.6), channel_id=1, source_target_pairs={{0,3},{1,2},{2,1},{3,0},{4,7},{5,6},{6,5},{7,4},{8,11},{9,10},{10,... | collective-permute-start | bytes 3244040 | tf_op jit(solution)/shard_map/ppermute | solution.py:253
  93.0 1.0 copy-start.7
  93.0 1.0 copy-start.9
  93.1 27.1 %collective-permute-start.17 = (bf16[128,4224]{1,0:T(8,128)(2,1)S(1)}, bf16[128,4224]{1,0:T(8,128)(2,1)S(1)}, u32[]{:S(2)}, u32[]{:S(2)}) collective-permute-start(bf16[128,4224]{1,0:T(8,128)(2,1)S(1)} %pad_maximum_fusion.7), channel_id=1, source_target_pairs={{0,96},{32,64},{64,32},{96,0},{1,97},{33,65},{65,33},{97,1},{2,98}... | collective-permute-start | bytes 3244040 | tf_op jit(solution)/shard_map/ppermute | solution.py:253
  94.2 1.0 copy-start.5
  94.3 26.4 %collective-permute-start.19 = (bf16[128,4224]{1,0:T(8,128)(2,1)S(1)}, bf16[128,4224]{1,0:T(8,128)(2,1)S(1)}, u32[]{:S(2)}, u32[]{:S(2)}) collective-permute-start(bf16[128,4224]{1,0:T(8,128)(2,1)S(1)} %pad_maximum_fusion.8), channel_id=1, source_target_pairs={{0,8},{8,0},{16,24},{24,16},{1,9},{9,1},{17,25},{25,17},{2,10},{10... | collective-permute-start | bytes 3244040 | tf_op jit(solution)/shard_map/ppermute | solution.py:253
  95.5 25.7 %collective-permute-start.21 = (bf16[128,4224]{1,0:T(8,128)(2,1)S(1)}, bf16[128,4224]{1,0:T(8,128)(2,1)S(1)}, u32[]{:S(2)}, u32[]{:S(2)}) collective-permute-start(bf16[128,4224]{1,0:T(8,128)(2,1)S(1)} %pad_maximum_fusion.9), channel_id=1, source_target_pairs={{0,32},{32,0},{64,96},{96,64},{1,33},{33,1},{65,97},{97,65},{2,34}... | collective-permute-start | bytes 3244040 | tf_op jit(solution)/shard_map/ppermute | solution.py:253
  95.8 26.0 %collective-permute-start.23 = (bf16[128,4224]{1,0:T(8,128)(2,1)S(1)}, bf16[128,4224]{1,0:T(8,128)(2,1)S(1)}, u32[]{:S(2)}, u32[]{:S(2)}) collective-permute-start(bf16[128,4224]{1,0:T(8,128)(2,1)S(1)} %pad_maximum_fusion.10), channel_id=1, source_target_pairs={{0,24},{8,16},{16,8},{24,0},{1,25},{9,17},{17,9},{25,1},{2,26},{10... | collective-permute-start | bytes 3244040 | tf_op jit(solution)/shard_map/ppermute | solution.py:253
  118.0 6.1 %collective-permute-start.15 = (bf16[256,4224]{1,0:T(8,128)(2,1)S(1)}, bf16[256,4224]{1,0:T(8,128)(2,1)S(1)}, u32[]{:S(2)}, u32[]{:S(2)}) collective-permute-start(bf16[256,4224]{1,0:T(8,128)(2,1)S(1)} %pad_maximum_fusion.1), channel_id=1, source_target_pairs={{0,4},{4,0},{1,5},{5,1},{2,6},{6,2},{3,7},{7,3},{8,12},{12,8},{9,1... | collective-permute-start | bytes 6488072 | tf_op jit(solution)/shard_map/ppermute | solution.py:249
  129.5 2.0 %collective-permute-start.24 = (f32[264,512]{1,0:T(8,128)S(1)}, f32[264,512]{1,0:T(8,128)S(1)}, u32[]{:S(2)}, u32[]{:S(2)}) collective-permute-start(f32[264,512]{1,0:T(8,128)S(1)} %get-tuple-element.26), channel_id=1, source_target_pairs={{0,4},{4,0},{1,5},{5,1},{2,6},{6,2},{3,7},{7,3},{8,12},{12,8},{9,1... | collective-permute-start | bytes 1622024 | tf_op jit(solution)/shard_map/ppermute | solution.py:249
  129.9 2.3 %collective-permute-start.25 = (f32[264,512]{1,0:T(8,128)S(1)}, f32[264,512]{1,0:T(8,128)S(1)}, u32[]{:S(2)}, u32[]{:S(2)}) collective-permute-start(f32[264,512]{1,0:T(8,128)S(1)} %get-tuple-element.27), channel_id=1, source_target_pairs={{0,4},{4,0},{1,5},{5,1},{2,6},{6,2},{3,7},{7,3},{8,12},{12,8},{9,1... | collective-permute-start | bytes 1622024 | tf_op jit(solution)/shard_map/ppermute | solution.py:249

commit v15 on v14

--- a/solution.py
+++ b/solution.py
@@ -273,13 +273,11 @@
     first = jnp.cumsum(loads) - loads
     part = 1.0 / jnp.sum(loads).astype(f32)
     *halves, s0, s1, s2, s3 = pack(first, pieces)
-    streams, turned = [s0, s1, s2, s3], []
+    streams = [s0, s1, s2, s3]
 
     def send(half, turn):
         places = [(q, u) for q in range(4) for u in range(4)]
         return lax.ppermute(half, ("z", "y"), [(q * 4 + u, u * 4 + (q ^ u ^ turn)) for q, u in places])
-
-    turned.append(send(halves[0], 0))
 
     for step in range(4):
         for s in range(4):
@@ -288,9 +286,9 @@
             which = side(x if axis == "x" else z, flip, axis not in seen)
             streams[s] = meet(streams[s], axis, flip, which)
         if step == 0:
-            turned.append(send(behind(halves[1], streams[:1]), 2))
-        if step == 1:
-            rows = behind(join(*turned), streams)
+            turned = [send(behind(half, streams), turn) for half, turn in zip(halves, (0, 2))]
+        if step == 2:
+            rows = behind(join(*turned), streams[:1])
 
     q = y ^ z
     rows = meet(rows, "y", 1, side(q, 1, True))

time: 135 us -> 131 us (0.970)
  starting transfers between devices: 40.9 us -> 37 us
  waiting for transfers between devices: 40.2 us -> 42.3 us
  local copies, waits for them, and re-layouts: 5.23 us -> 3.38 us
    ppermute x2, starting transfers between devices: 10.4 us -> 2.59 us  [send(): lax.ppermute(half, ('z', 'y'), [(q * 4 + u, u * 4 + (q ^ u ^ turn)) for q...]
    ppermute x3, starting transfers between devices: 2.79 us -> 6.14 us  [swap(): return lax.ppermute(value, 'c', [(0, 1), (1, 0)])]
    unnamed x30 -> x10, local copies, waits for them, and re-layouts: 4.78 us -> 2.92 us
    ppermute x3, waiting for transfers between devices: 3.17 us -> 4.59 us  [swap(): return lax.ppermute(value, 'c', [(0, 1), (1, 0)])]
  transfers between devices with their start and end apart: 26 -> 26, of which waited for: 10 -> 13; matrix products, arithmetic and copies ran while one was open for 5% -> 4% of each run, Pallas kernels for 0% -> 0%
where the time goes in v15:
time: 131 us; the launch traced here: 130 us
  waiting for transfers between devices  42.3 us (32%)
  starting transfers between devices  37 us (28%)
  blocking collectives  27.3 us (21%)
  Pallas kernels  11.4 us (9%)
  other arithmetic  6.73 us (5%)
  local copies, waits for them, and re-layouts  3.38 us (3%)
  between operations  1.75 us (1%)
    ppermute x21, waiting for transfers between devices, trade(): return lax.ppermute(value, axis, [(i, i ^ flip) for i in range(4)])  37.7 us
    ppermute x21, starting transfers between devices, trade(): return lax.ppermute(value, axis, [(i, i ^ flip) for i in range(4)])  28.3 us
    all_to_all x1, blocking collectives, per_device(): pieces = lax.all_to_all(pieces, TOK, 0, 0, tiled=True)  27.3 us
    ppermute x3, starting transfers between devices, swap(): return lax.ppermute(value, 'c', [(0, 1), (1, 0)])  6.14 us
    pallas_call x2, Pallas kernels, gram(): pl.pallas_call(lambda *refs: gram_kernel(blocks, *refs), out_shape=(jax.S...  4.8 us
    ppermute x3, waiting for transfers between devices, swap(): return lax.ppermute(value, 'c', [(0, 1), (1, 0)])  4.59 us
    select_n x18, other arithmetic, meet(): jnp.where(which == 0, value, got)  3.21 us
    unnamed x10, local copies, waits for them, and re-layouts  2.92 us
  transfers between devices with their start and end apart: 26, of which 13 were waited for; matrix products, arithmetic and copies ran while one was open for 4% of the time, Pallas kernels for 0%

profile of v15, /device:TPU:1, one launch (start us, length us, event | category | flops | bytes accessed | tf_op | source)
XLA Modules:
  0.0 129.8 jit_solution(1961592280025736315)
XLA Ops:
  0.6 1.6 %copy-done = bf16[512,2048]{1,0:T(8,128)(2,1)S(1)} copy-done((bf16[512,2048]{1,0:T(8,128)(2,1)S(1)}, bf16[512,2048]{1,0:T(8,128)(2,1)}, u32[]{:S(2)}) %copy-start) | copy-done | bytes 2097176
  2.2 0.7 copy-done.1
  2.9 0.7 copy-done.3
  3.6 1.3 %pick.1 = (bf16[2048,256]{1,0:T(8,128)(2,1)S(1)}, f32[8,256]{1,0:T(8,128)S(1)}) custom-call(s32[1,256]{1,0:T(1,128)S(1)} %bitcast.8, s32[2]{0:T(128)S(1)} %copy-done.1, bf16[512,2048]{1,0:T(8,128)(2,1)S(1)} %copy-done), custom_call_target="tpu_custom_call" | custom-call | tf_op jit(solution)/shard_map/pick/pallas_call | solution.py:77
  4.9 2.2 %collective-permute-start = (f32[8,256]{1,0:T(8,128)S(1)}, f32[8,256]{1,0:T(8,128)S(1)}, u32[]{:S(2)}, u32[]{:S(2)}) collective-permute-start(f32[8,256]{1,0:T(8,128)S(1)} %get-tuple-element.17.s0), channel_id=1, source_target_pairs={{0,1},{1,0},{2,3},{3,2},{4,5},{5,4},{6,7},{7,6},{8,9},{9,8},{10,11... | collective-permute-start | bytes 24584 | tf_op jit(solution)/shard_map/ppermute | solution.py:253
  7.1 2.6 %collective-permute-start.1 = (f32[8,256]{1,0:T(8,128)S(1)}, f32[8,256]{1,0:T(8,128)S(1)}, u32[]{:S(2)}, u32[]{:S(2)}) collective-permute-start(f32[8,256]{1,0:T(8,128)S(1)} %get-tuple-element.17.s0), channel_id=1, source_target_pairs={{0,2},{1,3},{2,0},{3,1},{4,6},{5,7},{6,4},{7,5},{8,10},{9,11},{10,... | collective-permute-start | bytes 24584 | tf_op jit(solution)/shard_map/ppermute | solution.py:253
  10.1 1.0 collective-permute-done.1.s2
  11.1 2.3 %collective-permute-done.2.s3 = f32[8,256]{1,0:T(8,128)S(1)} collective-permute-done((f32[8,256]{1,0:T(8,128)S(1)}, f32[8,256]{1,0:T(8,128)S(1)}, u32[]{:S(2)}, u32[]{:S(2)}) %collective-permute-start.2) | collective-permute-done | bytes 8224 | tf_op jit(solution)/shard_map/ppermute | solution.py:253
  13.5 0.9 norm.1
  14.3 27.3 %all_to_all.5.in_ref = bf16[32,64,256]{2,1,0:T(8,128)(2,1)S(1)} all-to-all(bf16[32,64,256]{2,1,0:T(8,128)(2,1)S(1)} %norm.1), channel_id=1, replica_groups=mesh['z'=4,'x'=4,'c'=2,'y'=4] {'z','x','c'}, dimensions={0} | all-to-all | bytes 2097152 | tf_op jit(solution)/shard_map/all_to_all | solution.py:270
  41.6 1.3 fusion
  43.2 2.1 %pack.1 = (bf16[32,4224]{1,0:T(8,128)(2,1)S(1)}, bf16[32,4224]{1,0:T(8,128)(2,1)S(1)}, bf16[16,4224]{1,0:T(8,128)(2,1)S(1)}, bf16[16,4224]{1,0:T(8,128)(2,1)S(1)...) custom-call(s32[32]{0:T(128)S(1)} %sub.3.first_ref, bf16[32,64,256]{2,1,0:T(8,128)(2,1)S(1)} %all_to_all.5.in_ref), custom_call_target="tpu_custom_call" | custom-call | tf_op jit(solution)/shard_map/pack/pallas_call | solution.py:148
  45.2 0.4 collective-permute-start.3
  45.7 0.4 collective-permute-start.4
  46.1 1.0 collective-permute-start.5
  47.1 0.6 collective-permute-start.6
  47.7 2.4 %collective-permute-done.3 = bf16[16,4224]{1,0:T(8,128)(2,1)S(1)} collective-permute-done((bf16[16,4224]{1,0:T(8,128)(2,1)S(1)}, bf16[16,4224]{1,0:T(8,128)(2,1)S(1)}, u32[]{:S(2)}, u32[]{:S(2)}) %collective-permute-start.3) | collective-permute-done | bytes 135200 | tf_op jit(solution)/shard_map/ppermute | solution.py:253
  50.3 1.2 collective-permute-start.9
  51.5 1.2 collective-permute-start.15
  52.8 1.0 collective-permute-start.18
  53.8 0.4 collective-permute-start.21
  54.3 1.9 %collective-permute-start.8 = (bf16[32,4224]{1,0:T(8,128)(2,1)S(1)}, bf16[32,4224]{1,0:T(8,128)(2,1)S(1)}, u32[]{:S(2)}, u32[]{:S(2)}) collective-permute-start(bf16[32,4224]{1,0:T(8,128)(2,1)S(1)} %behind.4), channel_id=1, source_target_pairs={{0,2},{1,35},{2,64},{3,97},{32,3},{33,34},{34,65},{35,96},{64,0},{... | collective-permute-start | bytes 811016 | tf_op jit(solution)/shard_map/ppermute | solution.py:280
  56.3 0.6 collective-permute-done.9
  56.9 0.7 collective-permute-start.7
  57.7 2.0 %collective-permute-done.15 = bf16[32,4224]{1,0:T(8,128)(2,1)S(1)} collective-permute-done((bf16[32,4224]{1,0:T(8,128)(2,1)S(1)}, bf16[32,4224]{1,0:T(8,128)(2,1)S(1)}, u32[]{:S(2)}, u32[]{:S(2)}) %collective-permute-start.15) | collective-permute-done | bytes 270368 | tf_op jit(solution)/shard_map/ppermute | solution.py:253
  59.7 1.4 %collective-permute-start.10 = (bf16[64,4224]{1,0:T(8,128)(2,1)S(1)}, bf16[64,4224]{1,0:T(8,128)(2,1)S(1)}, u32[]{:S(2)}, u32[]{:S(2)}) collective-permute-start(bf16[64,4224]{1,0:T(8,128)(2,1)S(1)} %pad_maximum_fusion.12), channel_id=1, source_target_pairs={{0,24},{8,16},{16,8},{24,0},{1,25},{9,17},{17,9},{25,1},{2,26},{10... | collective-permute-start | bytes 1622024 | tf_op jit(solution)/shard_map/ppermute | solution.py:253
  61.2 3.7 %collective-permute-start.16 = (bf16[64,4224]{1,0:T(8,128)(2,1)S(1)}, bf16[64,4224]{1,0:T(8,128)(2,1)S(1)}, u32[]{:S(2)}, u32[]{:S(2)}) collective-permute-start(bf16[64,4224]{1,0:T(8,128)(2,1)S(1)} %pad_maximum_fusion.13), channel_id=1, source_target_pairs={{0,96},{32,64},{64,32},{96,0},{1,97},{33,65},{65,33},{97,1},{2,98}... | collective-permute-start | bytes 1622024 | tf_op jit(solution)/shard_map/ppermute | solution.py:253
  65.1 2.7 %collective-permute-start.19 = (bf16[64,4224]{1,0:T(8,128)(2,1)S(1)}, bf16[64,4224]{1,0:T(8,128)(2,1)S(1)}, u32[]{:S(2)}, u32[]{:S(2)}) collective-permute-start(bf16[64,4224]{1,0:T(8,128)(2,1)S(1)} %pad_maximum_fusion.14), channel_id=1, source_target_pairs={{0,8},{8,0},{16,24},{24,16},{1,9},{9,1},{17,25},{25,17},{2,10},{10... | collective-permute-start | bytes 1622024 | tf_op jit(solution)/shard_map/ppermute | solution.py:253
  68.1 4.7 %collective-permute-done.10 = bf16[64,4224]{1,0:T(8,128)(2,1)S(1)} collective-permute-done((bf16[64,4224]{1,0:T(8,128)(2,1)S(1)}, bf16[64,4224]{1,0:T(8,128)(2,1)S(1)}, u32[]{:S(2)}, u32[]{:S(2)}) %collective-permute-start.10) | collective-permute-done | bytes 540704 | tf_op jit(solution)/shard_map/ppermute | solution.py:253
  73.1 3.7 %collective-permute-start.14 = (bf16[128,4224]{1,0:T(8,128)(2,1)S(1)}, bf16[128,4224]{1,0:T(8,128)(2,1)S(1)}, u32[]{:S(2)}, u32[]{:S(2)}) collective-permute-start(bf16[128,4224]{1,0:T(8,128)(2,1)S(1)} %pad_maximum_fusion.6.refs_0_), channel_id=1, source_target_pairs={{0,96},{32,64},{64,32},{96,0},{1,97},{33,65},{65,33},{97,1},{2,98}... | collective-permute-start | bytes 3244040 | tf_op jit(solution)/shard_map/ppermute | solution.py:253
  77.2 3.5 %collective-permute-start.17 = (bf16[128,4224]{1,0:T(8,128)(2,1)S(1)}, bf16[128,4224]{1,0:T(8,128)(2,1)S(1)}, u32[]{:S(2)}, u32[]{:S(2)}) collective-permute-start(bf16[128,4224]{1,0:T(8,128)(2,1)S(1)} %pad_maximum_fusion.8), channel_id=1, source_target_pairs={{0,8},{8,0},{16,24},{24,16},{1,9},{9,1},{17,25},{25,17},{2,10},{10... | collective-permute-start | bytes 3244040 | tf_op jit(solution)/shard_map/ppermute | solution.py:253
  81.3 0.9 collective-permute-start.23
  82.2 4.8 %collective-permute-done.11 = bf16[64,4224]{1,0:T(8,128)(2,1)S(1)} collective-permute-done((bf16[64,4224]{1,0:T(8,128)(2,1)S(1)}, bf16[64,4224]{1,0:T(8,128)(2,1)S(1)}, u32[]{:S(2)}, u32[]{:S(2)}) %collective-permute-start.11) | collective-permute-done | bytes 540704 | tf_op jit(solution)/shard_map/ppermute | solution.py:253
  87.2 1.0 collective-permute-start.12
  88.2 13.0 %collective-permute-done.14 = bf16[128,4224]{1,0:T(8,128)(2,1)S(1)} collective-permute-done((bf16[128,4224]{1,0:T(8,128)(2,1)S(1)}, bf16[128,4224]{1,0:T(8,128)(2,1)S(1)}, u32[]{:S(2)}, u32[]{:S(2)}) %collective-permute-start.14) | collective-permute-done | bytes 1081376 | tf_op jit(solution)/shard_map/ppermute | solution.py:253
  101.6 0.4 broadcast_select_fusion.5
  102.3 0.4 broadcast_select_fusion.3
  102.7 6.8 %collective-permute-done.12 = bf16[128,4224]{1,0:T(8,128)(2,1)S(1)} collective-permute-done((bf16[128,4224]{1,0:T(8,128)(2,1)S(1)}, bf16[128,4224]{1,0:T(8,128)(2,1)S(1)}, u32[]{:S(2)}, u32[]{:S(2)}) %collective-permute-start.12) | collective-permute-done | bytes 1081376 | tf_op jit(solution)/shard_map/ppermute | solution.py:253
  110.0 5.6 %collective-permute-start.13 = (bf16[256,4224]{1,0:T(8,128)(2,1)S(1)}, bf16[256,4224]{1,0:T(8,128)(2,1)S(1)}, u32[]{:S(2)}, u32[]{:S(2)}) collective-permute-start(bf16[256,4224]{1,0:T(8,128)(2,1)S(1)} %pad_maximum_fusion.1), channel_id=1, source_target_pairs={{0,4},{4,0},{1,5},{5,1},{2,6},{6,2},{3,7},{7,3},{8,12},{12,8},{9,1... | collective-permute-start | bytes 6488072 | tf_op jit(solution)/shard_map/ppermute | solution.py:249
  115.7 0.4 broadcast_select_fusion.1
  116.2 3.2 %collective-permute-done.13 = bf16[256,4224]{1,0:T(8,128)(2,1)S(1)} collective-permute-done((bf16[256,4224]{1,0:T(8,128)(2,1)S(1)}, bf16[256,4224]{1,0:T(8,128)(2,1)S(1)}, u32[]{:S(2)}, u32[]{:S(2)}) %collective-permute-start.13) | collective-permute-done | bytes 2162720 | tf_op jit(solution)/shard_map/ppermute | solution.py:249
  119.4 0.6 pad_maximum_fusion.refs_0_
  120.0 2.4 %gram.2 = (f32[264,512]{1,0:T(8,128)S(1)}, f32[264,512]{1,0:T(8,128)S(1)}) custom-call(bf16[512,4224]{1,0:T(8,128)(2,1)S(1)} %pad_maximum_fusion.refs_0_, bf16[256,4224]{1,0:T(8,128)(2,1)S(1)} %pad_maximum_fusion.2.refs_1_, bf16[256,4224]{1,0:T(8,128)(2,1)S(1)} %pad_maximum_fusion.3.refs_2_, bf16[256,4224]{1,0:T(8,128)(2,1)S(1)} %pad_maximum_fusion.4.refs_3_, ...), custom_call_target="tpu_custom_call" | custom-call | flops 2147483648 | bytes 6291456 | tf_op jit(solution)/shard_map/gram/pallas_call | solution.py:205
  122.4 2.4 %gram.3 = (f32[264,512]{1,0:T(8,128)S(1)}, f32[264,512]{1,0:T(8,128)S(1)}) custom-call(bf16[512,4224]{1,0:T(8,128)(2,1)S(1)} %pad_maximum_fusion.refs_0_, bf16[256,4224]{1,0:T(8,128)(2,1)S(1)} %pad_maximum_fusion.2.refs_1_, bf16[256,4224]{1,0:T(8,128)(2,1)S(1)} %pad_maximum_fusion.3.refs_2_, bf16[256,4224]{1,0:T(8,128)(2,1)S(1)} %pad_maximum_fusion.4.refs_3_, ...), custom_call_target="tpu_custom_call" | custom-call | flops 2147483648 | bytes 6291456 | tf_op jit(solution)/shard_map/gram/pallas_call | solution.py:205
  124.8 0.5 collective-permute-start.24
  126.2 0.6 collective-permute-done.24.refs_2_
  126.8 0.8 collective-permute-done.25.refs_3_
  127.6 2.2 %finish.1 = (f32[1,2048]{1,0:T(1,128)}, f32[256,2048]{1,0:T(8,128)}) custom-call(s32[3]{0:T(128)S(1)} %pad_add_fusion.info_ref, f32[1]{0:T(128)} %bitcast.5.part_ref, f32[264,512]{1,0:T(8,128)S(1)} %get-tuple-element.24.refs_0_, f32[264,512]{1,0:T(8,128)S(1)} %get-tuple-element.25.refs_1_, f32[264,512]{1,0:T(8,128)S(1)} %collective-permute-done.24.refs_2_, ...), custom_call_target="tpu_custom_call" | custom-call | tf_op jit(solution)/shard_map/finish/pallas_call | solution.py:235
  (67 shorter events, 4.8 us)
Async XLA Ops:
  0.6 1.6 %copy-start = (bf16[512,2048]{1,0:T(8,128)(2,1)S(1)}, bf16[512,2048]{1,0:T(8,128)(2,1)}, u32[]{:S(2)}) copy-start(bf16[512,2048]{1,0:T(8,128)(2,1)} %resid_ref.1) | copy-start | bytes 6291460
  2.2 0.7 copy-start.1
  2.9 0.7 copy-start.3
  3.6 6.2 %copy-start.4 = (f32[2048]{0:T(1024)S(1)}, f32[2048]{0:T(1024)}, u32[]{:S(2)}) copy-start(f32[2048]{0:T(1024)} %param.5) | copy-start | bytes 24580
  3.6 9.9 %copy-start.2 = (s32[2]{0:T(128)S(1)}, s32[2]{0:T(128)}, u32[]{:S(2)}) copy-start(s32[2]{0:T(128)} %counts_ref.3) | copy-start | bytes 28
  4.9 5.2 %collective-permute-start = (f32[8,256]{1,0:T(8,128)S(1)}, f32[8,256]{1,0:T(8,128)S(1)}, u32[]{:S(2)}, u32[]{:S(2)}) collective-permute-start(f32[8,256]{1,0:T(8,128)S(1)} %get-tuple-element.17.s0), channel_id=1, source_target_pairs={{0,1},{1,0},{2,3},{3,2},{4,5},{5,4},{6,7},{7,6},{8,9},{9,8},{10,11... | collective-permute-start | bytes 24584 | tf_op jit(solution)/shard_map/ppermute | solution.py:253
  7.1 4.0 %collective-permute-start.1 = (f32[8,256]{1,0:T(8,128)S(1)}, f32[8,256]{1,0:T(8,128)S(1)}, u32[]{:S(2)}, u32[]{:S(2)}) collective-permute-start(f32[8,256]{1,0:T(8,128)S(1)} %get-tuple-element.17.s0), channel_id=1, source_target_pairs={{0,2},{1,3},{2,0},{3,1},{4,6},{5,7},{6,4},{7,5},{8,10},{9,11},{10,... | collective-permute-start | bytes 24584 | tf_op jit(solution)/shard_map/ppermute | solution.py:253
  9.7 3.7 %collective-permute-start.2 = (f32[8,256]{1,0:T(8,128)S(1)}, f32[8,256]{1,0:T(8,128)S(1)}, u32[]{:S(2)}, u32[]{:S(2)}) collective-permute-start(f32[8,256]{1,0:T(8,128)S(1)} %get-tuple-element.17.s0), channel_id=1, source_target_pairs={{0,3},{1,2},{2,1},{3,0},{4,7},{5,6},{6,5},{7,4},{8,11},{9,10},{10,... | collective-permute-start | bytes 24584 | tf_op jit(solution)/shard_map/ppermute | solution.py:253
  45.2 4.9 %collective-permute-start.3 = (bf16[16,4224]{1,0:T(8,128)(2,1)S(1)}, bf16[16,4224]{1,0:T(8,128)(2,1)S(1)}, u32[]{:S(2)}, u32[]{:S(2)}) collective-permute-start(bf16[16,4224]{1,0:T(8,128)(2,1)S(1)} %get-tuple-element.19), channel_id=1, source_target_pairs={{0,8},{8,0},{16,24},{24,16},{1,9},{9,1},{17,25},{25,17},{2,10},{10... | collective-permute-start | bytes 405512 | tf_op jit(solution)/shard_map/ppermute | solution.py:253
  45.7 4.5 %collective-permute-start.4 = (bf16[16,4224]{1,0:T(8,128)(2,1)S(1)}, bf16[16,4224]{1,0:T(8,128)(2,1)S(1)}, u32[]{:S(2)}, u32[]{:S(2)}) collective-permute-start(bf16[16,4224]{1,0:T(8,128)(2,1)S(1)} %get-tuple-element.20), channel_id=1, source_target_pairs={{0,32},{32,0},{64,96},{96,64},{1,33},{33,1},{65,97},{97,65},{2,34}... | collective-permute-start | bytes 405512 | tf_op jit(solution)/shard_map/ppermute | solution.py:253
  46.1 6.6 %collective-permute-start.5 = (bf16[16,4224]{1,0:T(8,128)(2,1)S(1)}, bf16[16,4224]{1,0:T(8,128)(2,1)S(1)}, u32[]{:S(2)}, u32[]{:S(2)}) collective-permute-start(bf16[16,4224]{1,0:T(8,128)(2,1)S(1)} %get-tuple-element.21), channel_id=1, source_target_pairs={{0,24},{8,16},{16,8},{24,0},{1,25},{9,17},{17,9},{25,1},{2,26},{10... | collective-permute-start | bytes 405512 | tf_op jit(solution)/shard_map/ppermute | solution.py:253
  47.1 5.7 %collective-permute-start.6 = (bf16[16,4224]{1,0:T(8,128)(2,1)S(1)}, bf16[16,4224]{1,0:T(8,128)(2,1)S(1)}, u32[]{:S(2)}, u32[]{:S(2)}) collective-permute-start(bf16[16,4224]{1,0:T(8,128)(2,1)S(1)} %get-tuple-element.22), channel_id=1, source_target_pairs={{0,96},{32,64},{64,32},{96,0},{1,97},{33,65},{65,33},{97,1},{2,98}... | collective-permute-start | bytes 405512 | tf_op jit(solution)/shard_map/ppermute | solution.py:253
  50.3 6.6 %collective-permute-start.9 = (bf16[32,4224]{1,0:T(8,128)(2,1)S(1)}, bf16[32,4224]{1,0:T(8,128)(2,1)S(1)}, u32[]{:S(2)}, u32[]{:S(2)}) collective-permute-start(bf16[32,4224]{1,0:T(8,128)(2,1)S(1)} %get-tuple-element.68.refs_0_), channel_id=1, source_target_pairs={{0,32},{32,0},{64,96},{96,64},{1,33},{33,1},{65,97},{97,65},{2,34}... | collective-permute-start | bytes 811016 | tf_op jit(solution)/shard_map/ppermute | solution.py:253
  51.5 8.2 %collective-permute-start.15 = (bf16[32,4224]{1,0:T(8,128)(2,1)S(1)}, bf16[32,4224]{1,0:T(8,128)(2,1)S(1)}, u32[]{:S(2)}, u32[]{:S(2)}) collective-permute-start(bf16[32,4224]{1,0:T(8,128)(2,1)S(1)} %get-tuple-element.69.refs_1_), channel_id=1, source_target_pairs={{0,24},{8,16},{16,8},{24,0},{1,25},{9,17},{17,9},{25,1},{2,26},{10... | collective-permute-start | bytes 811016 | tf_op jit(solution)/shard_map/ppermute | solution.py:253
  52.8 8.4 %collective-permute-start.18 = (bf16[32,4224]{1,0:T(8,128)(2,1)S(1)}, bf16[32,4224]{1,0:T(8,128)(2,1)S(1)}, u32[]{:S(2)}, u32[]{:S(2)}) collective-permute-start(bf16[32,4224]{1,0:T(8,128)(2,1)S(1)} %get-tuple-element.70.refs_2_), channel_id=1, source_target_pairs={{0,96},{32,64},{64,32},{96,0},{1,97},{33,65},{65,33},{97,1},{2,98}... | collective-permute-start | bytes 811016 | tf_op jit(solution)/shard_map/ppermute | solution.py:253
  53.8 11.3 %collective-permute-start.21 = (bf16[32,4224]{1,0:T(8,128)(2,1)S(1)}, bf16[32,4224]{1,0:T(8,128)(2,1)S(1)}, u32[]{:S(2)}, u32[]{:S(2)}) collective-permute-start(bf16[32,4224]{1,0:T(8,128)(2,1)S(1)} %get-tuple-element.71.refs_3_), channel_id=1, source_target_pairs={{0,8},{8,0},{16,24},{24,16},{1,9},{9,1},{17,25},{25,17},{2,10},{10... | collective-permute-start | bytes 811016 | tf_op jit(solution)/shard_map/ppermute | solution.py:253
  54.3 13.6 %collective-permute-start.8 = (bf16[32,4224]{1,0:T(8,128)(2,1)S(1)}, bf16[32,4224]{1,0:T(8,128)(2,1)S(1)}, u32[]{:S(2)}, u32[]{:S(2)}) collective-permute-start(bf16[32,4224]{1,0:T(8,128)(2,1)S(1)} %behind.4), channel_id=1, source_target_pairs={{0,2},{1,35},{2,64},{3,97},{32,3},{33,34},{34,65},{35,96},{64,0},{... | collective-permute-start | bytes 811016 | tf_op jit(solution)/shard_map/ppermute | solution.py:280
  56.9 11.1 %collective-permute-start.7 = (bf16[32,4224]{1,0:T(8,128)(2,1)S(1)}, bf16[32,4224]{1,0:T(8,128)(2,1)S(1)}, u32[]{:S(2)}, u32[]{:S(2)}) collective-permute-start(bf16[32,4224]{1,0:T(8,128)(2,1)S(1)} %behind.3), channel_id=1, source_target_pairs={{0,0},{1,33},{2,66},{3,99},{32,1},{33,32},{34,67},{35,98},{64,2},{... | collective-permute-start | bytes 811016 | tf_op jit(solution)/shard_map/ppermute | solution.py:280
  59.7 13.1 %collective-permute-start.10 = (bf16[64,4224]{1,0:T(8,128)(2,1)S(1)}, bf16[64,4224]{1,0:T(8,128)(2,1)S(1)}, u32[]{:S(2)}, u32[]{:S(2)}) collective-permute-start(bf16[64,4224]{1,0:T(8,128)(2,1)S(1)} %pad_maximum_fusion.12), channel_id=1, source_target_pairs={{0,24},{8,16},{16,8},{24,0},{1,25},{9,17},{17,9},{25,1},{2,26},{10... | collective-permute-start | bytes 1622024 | tf_op jit(solution)/shard_map/ppermute | solution.py:253
  61.2 15.7 %collective-permute-start.16 = (bf16[64,4224]{1,0:T(8,128)(2,1)S(1)}, bf16[64,4224]{1,0:T(8,128)(2,1)S(1)}, u32[]{:S(2)}, u32[]{:S(2)}) collective-permute-start(bf16[64,4224]{1,0:T(8,128)(2,1)S(1)} %pad_maximum_fusion.13), channel_id=1, source_target_pairs={{0,96},{32,64},{64,32},{96,0},{1,97},{33,65},{65,33},{97,1},{2,98}... | collective-permute-start | bytes 1622024 | tf_op jit(solution)/shard_map/ppermute | solution.py:253
  65.1 15.5 %collective-permute-start.19 = (bf16[64,4224]{1,0:T(8,128)(2,1)S(1)}, bf16[64,4224]{1,0:T(8,128)(2,1)S(1)}, u32[]{:S(2)}, u32[]{:S(2)}) collective-permute-start(bf16[64,4224]{1,0:T(8,128)(2,1)S(1)} %pad_maximum_fusion.14), channel_id=1, source_target_pairs={{0,8},{8,0},{16,24},{24,16},{1,9},{9,1},{17,25},{25,17},{2,10},{10... | collective-permute-start | bytes 1622024 | tf_op jit(solution)/shard_map/ppermute | solution.py:253
  67.9 13.1 %collective-permute-start.22 = (bf16[64,4224]{1,0:T(8,128)(2,1)S(1)}, bf16[64,4224]{1,0:T(8,128)(2,1)S(1)}, u32[]{:S(2)}, u32[]{:S(2)}) collective-permute-start(bf16[64,4224]{1,0:T(8,128)(2,1)S(1)} %pad_maximum_fusion.15), channel_id=1, source_target_pairs={{0,32},{32,0},{64,96},{96,64},{1,33},{33,1},{65,97},{97,65},{2,34}... | collective-permute-start | bytes 1622024 | tf_op jit(solution)/shard_map/ppermute | solution.py:253
  73.1 28.2 %collective-permute-start.14 = (bf16[128,4224]{1,0:T(8,128)(2,1)S(1)}, bf16[128,4224]{1,0:T(8,128)(2,1)S(1)}, u32[]{:S(2)}, u32[]{:S(2)}) collective-permute-start(bf16[128,4224]{1,0:T(8,128)(2,1)S(1)} %pad_maximum_fusion.6.refs_0_), channel_id=1, source_target_pairs={{0,96},{32,64},{64,32},{96,0},{1,97},{33,65},{65,33},{97,1},{2,98}... | collective-permute-start | bytes 3244040 | tf_op jit(solution)/shard_map/ppermute | solution.py:253
  76.8 10.2 %collective-permute-start.11 = (bf16[64,4224]{1,0:T(8,128)(2,1)S(1)}, bf16[64,4224]{1,0:T(8,128)(2,1)S(1)}, u32[]{:S(2)}, u32[]{:S(2)}) collective-permute-start(bf16[64,4224]{1,0:T(8,128)(2,1)S(1)} %behind.5), channel_id=1, source_target_pairs={{0,1},{1,0},{2,3},{3,2},{4,5},{5,4},{6,7},{7,6},{8,9},{9,8},{10,11... | collective-permute-start | bytes 1622024 | tf_op jit(solution)/shard_map/ppermute | solution.py:253
  77.2 24.4 %collective-permute-start.17 = (bf16[128,4224]{1,0:T(8,128)(2,1)S(1)}, bf16[128,4224]{1,0:T(8,128)(2,1)S(1)}, u32[]{:S(2)}, u32[]{:S(2)}) collective-permute-start(bf16[128,4224]{1,0:T(8,128)(2,1)S(1)} %pad_maximum_fusion.8), channel_id=1, source_target_pairs={{0,8},{8,0},{16,24},{24,16},{1,9},{9,1},{17,25},{25,17},{2,10},{10... | collective-permute-start | bytes 3244040 | tf_op jit(solution)/shard_map/ppermute | solution.py:253
  80.9 21.4 %collective-permute-start.20 = (bf16[128,4224]{1,0:T(8,128)(2,1)S(1)}, bf16[128,4224]{1,0:T(8,128)(2,1)S(1)}, u32[]{:S(2)}, u32[]{:S(2)}) collective-permute-start(bf16[128,4224]{1,0:T(8,128)(2,1)S(1)} %pad_maximum_fusion.9), channel_id=1, source_target_pairs={{0,32},{32,0},{64,96},{96,64},{1,33},{33,1},{65,97},{97,65},{2,34}... | collective-permute-start | bytes 3244040 | tf_op jit(solution)/shard_map/ppermute | solution.py:253
  81.3 34.4 %collective-permute-start.23 = (bf16[128,4224]{1,0:T(8,128)(2,1)S(1)}, bf16[128,4224]{1,0:T(8,128)(2,1)S(1)}, u32[]{:S(2)}, u32[]{:S(2)}) collective-permute-start(bf16[128,4224]{1,0:T(8,128)(2,1)S(1)} %pad_maximum_fusion.10), channel_id=1, source_target_pairs={{0,24},{8,16},{16,8},{24,0},{1,25},{9,17},{17,9},{25,1},{2,26},{10... | collective-permute-start | bytes 3244040 | tf_op jit(solution)/shard_map/ppermute | solution.py:253
  87.2 22.3 %collective-permute-start.12 = (bf16[128,4224]{1,0:T(8,128)(2,1)S(1)}, bf16[128,4224]{1,0:T(8,128)(2,1)S(1)}, u32[]{:S(2)}, u32[]{:S(2)}) collective-permute-start(bf16[128,4224]{1,0:T(8,128)(2,1)S(1)} %pad_maximum_fusion.7), channel_id=1, source_target_pairs={{0,3},{1,2},{2,1},{3,0},{4,7},{5,6},{6,5},{7,4},{8,11},{9,10},{10,... | collective-permute-start | bytes 3244040 | tf_op jit(solution)/shard_map/ppermute | solution.py:253
  110.0 9.4 %collective-permute-start.13 = (bf16[256,4224]{1,0:T(8,128)(2,1)S(1)}, bf16[256,4224]{1,0:T(8,128)(2,1)S(1)}, u32[]{:S(2)}, u32[]{:S(2)}) collective-permute-start(bf16[256,4224]{1,0:T(8,128)(2,1)S(1)} %pad_maximum_fusion.1), channel_id=1, source_target_pairs={{0,4},{4,0},{1,5},{5,1},{2,6},{6,2},{3,7},{7,3},{8,12},{12,8},{9,1... | collective-permute-start | bytes 6488072 | tf_op jit(solution)/shard_map/ppermute | solution.py:249
  124.8 2.0 %collective-permute-start.24 = (f32[264,512]{1,0:T(8,128)S(1)}, f32[264,512]{1,0:T(8,128)S(1)}, u32[]{:S(2)}, u32[]{:S(2)}) collective-permute-start(f32[264,512]{1,0:T(8,128)S(1)} %get-tuple-element.26), channel_id=1, source_target_pairs={{0,4},{4,0},{1,5},{5,1},{2,6},{6,2},{3,7},{7,3},{8,12},{12,8},{9,1... | collective-permute-start | bytes 1622024 | tf_op jit(solution)/shard_map/ppermute | solution.py:249
  125.3 2.3 %collective-permute-start.25 = (f32[264,512]{1,0:T(8,128)S(1)}, f32[264,512]{1,0:T(8,128)S(1)}, u32[]{:S(2)}, u32[]{:S(2)}) collective-permute-start(f32[264,512]{1,0:T(8,128)S(1)} %get-tuple-element.27), channel_id=1, source_target_pairs={{0,4},{4,0},{1,5},{5,1},{2,6},{6,2},{3,7},{7,3},{8,12},{12,8},{9,1... | collective-permute-start | bytes 1622024 | tf_op jit(solution)/shard_map/ppermute | solution.py:249

commit v16 on v14

--- a/solution.py
+++ b/solution.py
@@ -273,13 +273,11 @@
     first = jnp.cumsum(loads) - loads
     part = 1.0 / jnp.sum(loads).astype(f32)
     *halves, s0, s1, s2, s3 = pack(first, pieces)
-    streams, turned = [s0, s1, s2, s3], []
+    streams = [s0, s1, s2, s3]
 
     def send(half, turn):
         places = [(q, u) for q in range(4) for u in range(4)]
         return lax.ppermute(half, ("z", "y"), [(q * 4 + u, u * 4 + (q ^ u ^ turn)) for q, u in places])
-
-    turned.append(send(halves[0], 0))
 
     for step in range(4):
         for s in range(4):
@@ -288,7 +286,7 @@
             which = side(x if axis == "x" else z, flip, axis not in seen)
             streams[s] = meet(streams[s], axis, flip, which)
         if step == 0:
-            turned.append(send(behind(halves[1], streams[:1]), 2))
+            turned = [send(behind(halves[0], streams[:1]), 0), send(behind(halves[1], streams), 2)]
         if step == 1:
             rows = behind(join(*turned), streams)
 

time: 135 us -> 125 us (0.926)
  waiting for transfers between devices: 40.2 us -> 33 us
  starting transfers between devices: 40.9 us -> 37.7 us
    ppermute x21, waiting for transfers between devices: 37 us -> 27.4 us  [trade(): return lax.ppermute(value, axis, [(i, i ^ flip) for i in range(4)])]
    ppermute x2, starting transfers between devices: 10.4 us -> 2.59 us  [send(): lax.ppermute(half, ('z', 'y'), [(q * 4 + u, u * 4 + (q ^ u ^ turn)) for q...]
    ppermute x3, starting transfers between devices: 2.79 us -> 7.46 us  [swap(): return lax.ppermute(value, 'c', [(0, 1), (1, 0)])]
    ppermute x2, waiting for transfers between devices: 0.01 us -> 2.38 us  [send(): lax.ppermute(half, ('z', 'y'), [(q * 4 + u, u * 4 + (q ^ u ^ turn)) for q...]
  transfers between devices with their start and end apart: 26 -> 26, of which waited for: 10 -> 13; matrix products, arithmetic and copies ran while one was open for 5% -> 5% of each run, Pallas kernels for 0% -> 0%
where the time goes in v16:
time: 125 us
  starting transfers between devices  37.7 us (30%)
  waiting for transfers between devices  33 us (26%)
  blocking collectives  27.3 us (22%)
  Pallas kernels  11.4 us (9%)
  other arithmetic  7.71 us (6%)
  local copies, waits for them, and re-layouts  6.22 us (5%)
  between operations  1.78 us (1%)
    ppermute x21, starting transfers between devices, trade(): return lax.ppermute(value, axis, [(i, i ^ flip) for i in range(4)])  27.6 us
    ppermute x21, waiting for transfers between devices, trade(): return lax.ppermute(value, axis, [(i, i ^ flip) for i in range(4)])  27.4 us
    all_to_all x1, blocking collectives, per_device(): pieces = lax.all_to_all(pieces, TOK, 0, 0, tiled=True)  27.3 us
    ppermute x3, starting transfers between devices, swap(): return lax.ppermute(value, 'c', [(0, 1), (1, 0)])  7.46 us
    unnamed x30, local copies, waits for them, and re-layouts  5.77 us
    pallas_call x2, Pallas kernels, gram(): pl.pallas_call(lambda *refs: gram_kernel(blocks, *refs), out_shape=(jax.S...  4.8 us
    select_n x18, other arithmetic, meet(): jnp.where(which == 0, value, got)  4.26 us
    ppermute x3, waiting for transfers between devices, swap(): return lax.ppermute(value, 'c', [(0, 1), (1, 0)])  3.21 us
  transfers between devices with their start and end apart: 26, of which 13 were waited for; matrix products, arithmetic and copies ran while one was open for 5% of the time, Pallas kernels for 0%

profile of v16, /device:TPU:1, one launch (start us, length us, event | category | flops | bytes accessed | tf_op | source)
XLA Modules:
  0.0 125.0 jit_solution(12401592142572491159)
XLA Ops:
  0.6 1.6 %copy-done = bf16[512,2048]{1,0:T(8,128)(2,1)S(1)} copy-done((bf16[512,2048]{1,0:T(8,128)(2,1)S(1)}, bf16[512,2048]{1,0:T(8,128)(2,1)}, u32[]{:S(2)}) %copy-start) | copy-done | bytes 2097176
  2.2 0.7 copy-done.1
  2.9 0.7 copy-done.3
  3.6 1.3 %pick.1 = (bf16[2048,256]{1,0:T(8,128)(2,1)S(1)}, f32[8,256]{1,0:T(8,128)S(1)}) custom-call(s32[1,256]{1,0:T(1,128)S(1)} %bitcast.8, s32[2]{0:T(128)S(1)} %copy-done.1, bf16[512,2048]{1,0:T(8,128)(2,1)S(1)} %copy-done), custom_call_target="tpu_custom_call" | custom-call | tf_op jit(solution)/shard_map/pick/pallas_call | solution.py:77
  4.9 2.2 %collective-permute-start = (f32[8,256]{1,0:T(8,128)S(1)}, f32[8,256]{1,0:T(8,128)S(1)}, u32[]{:S(2)}, u32[]{:S(2)}) collective-permute-start(f32[8,256]{1,0:T(8,128)S(1)} %get-tuple-element.17.s0), channel_id=1, source_target_pairs={{0,1},{1,0},{2,3},{3,2},{4,5},{5,4},{6,7},{7,6},{8,9},{9,8},{10,11... | collective-permute-start | bytes 24584 | tf_op jit(solution)/shard_map/ppermute | solution.py:253
  7.1 2.6 %collective-permute-start.1 = (f32[8,256]{1,0:T(8,128)S(1)}, f32[8,256]{1,0:T(8,128)S(1)}, u32[]{:S(2)}, u32[]{:S(2)}) collective-permute-start(f32[8,256]{1,0:T(8,128)S(1)} %get-tuple-element.17.s0), channel_id=1, source_target_pairs={{0,2},{1,3},{2,0},{3,1},{4,6},{5,7},{6,4},{7,5},{8,10},{9,11},{10,... | collective-permute-start | bytes 24584 | tf_op jit(solution)/shard_map/ppermute | solution.py:253
  10.1 1.0 collective-permute-done.1.s2
  11.1 2.3 %collective-permute-done.2.s3 = f32[8,256]{1,0:T(8,128)S(1)} collective-permute-done((f32[8,256]{1,0:T(8,128)S(1)}, f32[8,256]{1,0:T(8,128)S(1)}, u32[]{:S(2)}, u32[]{:S(2)}) %collective-permute-start.2) | collective-permute-done | bytes 8224 | tf_op jit(solution)/shard_map/ppermute | solution.py:253
  13.5 0.9 norm.1
  14.3 27.3 %all_to_all.5.in_ref = bf16[32,64,256]{2,1,0:T(8,128)(2,1)S(1)} all-to-all(bf16[32,64,256]{2,1,0:T(8,128)(2,1)S(1)} %norm.1), channel_id=1, replica_groups=mesh['z'=4,'x'=4,'c'=2,'y'=4] {'z','x','c'}, dimensions={0} | all-to-all | bytes 2097152 | tf_op jit(solution)/shard_map/all_to_all | solution.py:270
  41.6 1.2 fusion
  43.1 2.1 %pack.1 = (bf16[32,4224]{1,0:T(8,128)(2,1)S(1)}, bf16[32,4224]{1,0:T(8,128)(2,1)S(1)}, bf16[16,4224]{1,0:T(8,128)(2,1)S(1)}, bf16[16,4224]{1,0:T(8,128)(2,1)S(1)...) custom-call(s32[32]{0:T(128)S(1)} %sub.3.first_ref, bf16[32,64,256]{2,1,0:T(8,128)(2,1)S(1)} %all_to_all.5.in_ref), custom_call_target="tpu_custom_call" | custom-call | tf_op jit(solution)/shard_map/pack/pallas_call | solution.py:148
  45.2 0.4 collective-permute-start.3
  46.0 1.0 collective-permute-start.6
  47.0 0.6 collective-permute-start.7
  47.7 2.4 %collective-permute-done.3 = bf16[16,4224]{1,0:T(8,128)(2,1)S(1)} collective-permute-done((bf16[16,4224]{1,0:T(8,128)(2,1)S(1)}, bf16[16,4224]{1,0:T(8,128)(2,1)S(1)}, u32[]{:S(2)}, u32[]{:S(2)}) %collective-permute-start.3) | collective-permute-done | bytes 135200 | tf_op jit(solution)/shard_map/ppermute | solution.py:253
  50.3 1.2 collective-permute-start.9
  51.5 1.2 collective-permute-start.10
  52.8 1.0 collective-permute-start.11
  53.8 0.4 collective-permute-start.12
  54.2 1.9 %collective-permute-start.8 = (bf16[32,4224]{1,0:T(8,128)(2,1)S(1)}, bf16[32,4224]{1,0:T(8,128)(2,1)S(1)}, u32[]{:S(2)}, u32[]{:S(2)}) collective-permute-start(bf16[32,4224]{1,0:T(8,128)(2,1)S(1)} %behind.4), channel_id=1, source_target_pairs={{0,2},{1,35},{2,64},{3,97},{32,3},{33,34},{34,65},{35,96},{64,0},{... | collective-permute-start | bytes 811016 | tf_op jit(solution)/shard_map/ppermute | solution.py:280
  56.2 0.6 collective-permute-done.9
  56.8 0.7 collective-permute-start.4
  57.7 0.6 copy-done.10
  58.3 1.3 %collective-permute-done.10 = bf16[32,4224]{1,0:T(8,128)(2,1)S(1)} collective-permute-done((bf16[32,4224]{1,0:T(8,128)(2,1)S(1)}, bf16[32,4224]{1,0:T(8,128)(2,1)S(1)}, u32[]{:S(2)}, u32[]{:S(2)}) %collective-permute-start.10) | collective-permute-done | bytes 270368 | tf_op jit(solution)/shard_map/ppermute | solution.py:253
  59.8 0.6 collective-permute-done.11
  60.7 0.5 copy-done.4
  61.3 2.4 %collective-permute-done.8 = bf16[32,4224]{1,0:T(8,128)(2,1)S(1)} collective-permute-done((bf16[32,4224]{1,0:T(8,128)(2,1)S(1)}, bf16[32,4224]{1,0:T(8,128)(2,1)S(1)}, u32[]{:S(2)}, u32[]{:S(2)}) %collective-permute-start.8) | collective-permute-done | bytes 270368 | tf_op jit(solution)/shard_map/ppermute | solution.py:280
  63.8 3.2 %collective-permute-start.13 = (bf16[64,4224]{1,0:T(8,128)(2,1)S(1)}, bf16[64,4224]{1,0:T(8,128)(2,1)}, u32[]{:S(2)}, u32[]{:S(2)}) collective-permute-start(bf16[64,4224]{1,0:T(8,128)(2,1)S(1)} %behind.5), channel_id=1, source_target_pairs={{0,1},{1,0},{2,3},{3,2},{4,5},{5,4},{6,7},{7,6},{8,9},{9,8},{10,11... | collective-permute-start | bytes 1622024 | tf_op jit(solution)/shard_map/ppermute | solution.py:253
  66.9 2.6 %collective-permute-start.16 = (bf16[64,4224]{1,0:T(8,128)(2,1)S(1)}, bf16[64,4224]{1,0:T(8,128)(2,1)S(1)}, u32[]{:S(2)}, u32[]{:S(2)}) collective-permute-start(bf16[64,4224]{1,0:T(8,128)(2,1)S(1)} %pad_maximum_fusion.12.refs_0_), channel_id=1, source_target_pairs={{0,24},{8,16},{16,8},{24,0},{1,25},{9,17},{17,9},{25,1},{2,26},{10... | collective-permute-start | bytes 1622024 | tf_op jit(solution)/shard_map/ppermute | solution.py:253
  69.5 1.5 %collective-permute-start.18 = (bf16[64,4224]{1,0:T(8,128)(2,1)S(1)}, bf16[64,4224]{1,0:T(8,128)(2,1)S(1)}, u32[]{:S(2)}, u32[]{:S(2)}) collective-permute-start(bf16[64,4224]{1,0:T(8,128)(2,1)S(1)} %pad_maximum_fusion.13.refs_1_), channel_id=1, source_target_pairs={{0,96},{32,64},{64,32},{96,0},{1,97},{33,65},{65,33},{97,1},{2,98}... | collective-permute-start | bytes 1622024 | tf_op jit(solution)/shard_map/ppermute | solution.py:253
  71.0 0.7 collective-permute-start.20
  71.7 4.2 %collective-permute-done.13 = bf16[64,4224]{1,0:T(8,128)(2,1)} collective-permute-done((bf16[64,4224]{1,0:T(8,128)(2,1)S(1)}, bf16[64,4224]{1,0:T(8,128)(2,1)}, u32[]{:S(2)}, u32[]{:S(2)}) %collective-permute-start.13) | collective-permute-done | bytes 540704 | tf_op jit(solution)/shard_map/ppermute | solution.py:253
  75.9 1.1 broadcast_select_fusion.19
  77.2 6.7 %collective-permute-start.14 = (bf16[128,4224]{1,0:T(8,128)(2,1)S(1)}, bf16[128,4224]{1,0:T(8,128)(2,1)S(1)}, u32[]{:S(2)}, u32[]{:S(2)}) collective-permute-start(bf16[128,4224]{1,0:T(8,128)(2,1)S(1)} %pad_maximum_fusion.6), channel_id=1, source_target_pairs={{0,3},{1,2},{2,1},{3,0},{4,7},{5,6},{6,5},{7,4},{8,11},{9,10},{10,... | collective-permute-start | bytes 3244040 | tf_op jit(solution)/shard_map/ppermute | solution.py:253
  84.2 0.7 copy-done.7
  85.4 0.8 copy-done.5
  86.9 1.5 %collective-permute-start.23 = (bf16[128,4224]{1,0:T(8,128)(2,1)S(1)}, bf16[128,4224]{1,0:T(8,128)(2,1)S(1)}, u32[]{:S(2)}, u32[]{:S(2)}) collective-permute-start(bf16[128,4224]{1,0:T(8,128)(2,1)S(1)} %pad_maximum_fusion.10), channel_id=1, source_target_pairs={{0,24},{8,16},{16,8},{24,0},{1,25},{9,17},{17,9},{25,1},{2,26},{10... | collective-permute-start | bytes 3244040 | tf_op jit(solution)/shard_map/ppermute | solution.py:253
  88.5 14.9 %collective-permute-done.14 = bf16[128,4224]{1,0:T(8,128)(2,1)S(1)} collective-permute-done((bf16[128,4224]{1,0:T(8,128)(2,1)S(1)}, bf16[128,4224]{1,0:T(8,128)(2,1)S(1)}, u32[]{:S(2)}, u32[]{:S(2)}) %collective-permute-start.14) | collective-permute-done | bytes 1081376 | tf_op jit(solution)/shard_map/ppermute | solution.py:253
  103.9 5.5 %collective-permute-start.15 = (bf16[256,4224]{1,0:T(8,128)(2,1)S(1)}, bf16[256,4224]{1,0:T(8,128)(2,1)S(1)}, u32[]{:S(2)}, u32[]{:S(2)}) collective-permute-start(bf16[256,4224]{1,0:T(8,128)(2,1)S(1)} %pad_maximum_fusion.1), channel_id=1, source_target_pairs={{0,4},{4,0},{1,5},{5,1},{2,6},{6,2},{3,7},{7,3},{8,12},{12,8},{9,1... | collective-permute-start | bytes 6488072 | tf_op jit(solution)/shard_map/ppermute | solution.py:249
  111.6 1.7 %collective-permute-done.15 = bf16[256,4224]{1,0:T(8,128)(2,1)S(1)} collective-permute-done((bf16[256,4224]{1,0:T(8,128)(2,1)S(1)}, bf16[256,4224]{1,0:T(8,128)(2,1)S(1)}, u32[]{:S(2)}, u32[]{:S(2)}) %collective-permute-start.15) | collective-permute-done | bytes 2162720 | tf_op jit(solution)/shard_map/ppermute | solution.py:249
  113.3 0.6 pad_maximum_fusion.refs_0_
  113.9 2.4 %gram.2 = (f32[264,512]{1,0:T(8,128)S(1)}, f32[264,512]{1,0:T(8,128)S(1)}) custom-call(bf16[512,4224]{1,0:T(8,128)(2,1)S(1)} %pad_maximum_fusion.refs_0_, bf16[256,4224]{1,0:T(8,128)(2,1)S(1)} %pad_maximum_fusion.2.refs_1_, bf16[256,4224]{1,0:T(8,128)(2,1)S(1)} %pad_maximum_fusion.3.refs_2_, bf16[256,4224]{1,0:T(8,128)(2,1)S(1)} %pad_maximum_fusion.4.refs_3_, ...), custom_call_target="tpu_custom_call" | custom-call | flops 2147483648 | bytes 6291456 | tf_op jit(solution)/shard_map/gram/pallas_call | solution.py:205
  116.3 2.4 %gram.3 = (f32[264,512]{1,0:T(8,128)S(1)}, f32[264,512]{1,0:T(8,128)S(1)}) custom-call(bf16[512,4224]{1,0:T(8,128)(2,1)S(1)} %pad_maximum_fusion.refs_0_, bf16[256,4224]{1,0:T(8,128)(2,1)S(1)} %pad_maximum_fusion.2.refs_1_, bf16[256,4224]{1,0:T(8,128)(2,1)S(1)} %pad_maximum_fusion.3.refs_2_, bf16[256,4224]{1,0:T(8,128)(2,1)S(1)} %pad_maximum_fusion.4.refs_3_, ...), custom_call_target="tpu_custom_call" | custom-call | flops 2147483648 | bytes 6291456 | tf_op jit(solution)/shard_map/gram/pallas_call | solution.py:205
  118.7 1.8 %collective-permute-start.24 = (f32[264,512]{1,0:T(8,128)S(1)}, f32[264,512]{1,0:T(8,128)S(1)}, u32[]{:S(2)}, u32[]{:S(2)}) collective-permute-start(f32[264,512]{1,0:T(8,128)S(1)} %get-tuple-element.26), channel_id=1, source_target_pairs={{0,4},{4,0},{1,5},{5,1},{2,6},{6,2},{3,7},{7,3},{8,12},{12,8},{9,1... | collective-permute-start | bytes 1622024 | tf_op jit(solution)/shard_map/ppermute | solution.py:249
  121.3 0.7 collective-permute-done.24.refs_2_
  122.1 0.8 collective-permute-done.25.refs_3_
  122.8 2.2 %finish.1 = (f32[1,2048]{1,0:T(1,128)}, f32[256,2048]{1,0:T(8,128)}) custom-call(s32[3]{0:T(128)S(1)} %pad_add_fusion.info_ref, f32[1]{0:T(128)} %bitcast.5.part_ref, f32[264,512]{1,0:T(8,128)S(1)} %get-tuple-element.24.refs_0_, f32[264,512]{1,0:T(8,128)S(1)} %get-tuple-element.25.refs_1_, f32[264,512]{1,0:T(8,128)S(1)} %collective-permute-done.24.refs_2_, ...), custom_call_target="tpu_custom_call" | custom-call | tf_op jit(solution)/shard_map/finish/pallas_call | solution.py:235
  (87 shorter events, 6.4 us)
Async XLA Ops:
  0.6 1.6 %copy-start = (bf16[512,2048]{1,0:T(8,128)(2,1)S(1)}, bf16[512,2048]{1,0:T(8,128)(2,1)}, u32[]{:S(2)}) copy-start(bf16[512,2048]{1,0:T(8,128)(2,1)} %resid_ref.1) | copy-start | bytes 6291460
  2.2 0.7 copy-start.1
  2.9 0.7 copy-start.3
  3.6 6.2 %copy-start.14 = (f32[2048]{0:T(1024)S(1)}, f32[2048]{0:T(1024)}, u32[]{:S(2)}) copy-start(f32[2048]{0:T(1024)} %param.5) | copy-start | bytes 24580
  3.6 9.9 %copy-start.2 = (s32[2]{0:T(128)S(1)}, s32[2]{0:T(128)}, u32[]{:S(2)}) copy-start(s32[2]{0:T(128)} %counts_ref.3) | copy-start | bytes 28
  4.9 5.2 %collective-permute-start = (f32[8,256]{1,0:T(8,128)S(1)}, f32[8,256]{1,0:T(8,128)S(1)}, u32[]{:S(2)}, u32[]{:S(2)}) collective-permute-start(f32[8,256]{1,0:T(8,128)S(1)} %get-tuple-element.17.s0), channel_id=1, source_target_pairs={{0,1},{1,0},{2,3},{3,2},{4,5},{5,4},{6,7},{7,6},{8,9},{9,8},{10,11... | collective-permute-start | bytes 24584 | tf_op jit(solution)/shard_map/ppermute | solution.py:253
  7.1 4.0 %collective-permute-start.1 = (f32[8,256]{1,0:T(8,128)S(1)}, f32[8,256]{1,0:T(8,128)S(1)}, u32[]{:S(2)}, u32[]{:S(2)}) collective-permute-start(f32[8,256]{1,0:T(8,128)S(1)} %get-tuple-element.17.s0), channel_id=1, source_target_pairs={{0,2},{1,3},{2,0},{3,1},{4,6},{5,7},{6,4},{7,5},{8,10},{9,11},{10,... | collective-permute-start | bytes 24584 | tf_op jit(solution)/shard_map/ppermute | solution.py:253
  9.7 3.7 %collective-permute-start.2 = (f32[8,256]{1,0:T(8,128)S(1)}, f32[8,256]{1,0:T(8,128)S(1)}, u32[]{:S(2)}, u32[]{:S(2)}) collective-permute-start(f32[8,256]{1,0:T(8,128)S(1)} %get-tuple-element.17.s0), channel_id=1, source_target_pairs={{0,3},{1,2},{2,1},{3,0},{4,7},{5,6},{6,5},{7,4},{8,11},{9,10},{10,... | collective-permute-start | bytes 24584 | tf_op jit(solution)/shard_map/ppermute | solution.py:253
  45.2 4.9 %collective-permute-start.3 = (bf16[16,4224]{1,0:T(8,128)(2,1)S(1)}, bf16[16,4224]{1,0:T(8,128)(2,1)S(1)}, u32[]{:S(2)}, u32[]{:S(2)}) collective-permute-start(bf16[16,4224]{1,0:T(8,128)(2,1)S(1)} %get-tuple-element.19), channel_id=1, source_target_pairs={{0,8},{8,0},{16,24},{24,16},{1,9},{9,1},{17,25},{25,17},{2,10},{10... | collective-permute-start | bytes 405512 | tf_op jit(solution)/shard_map/ppermute | solution.py:253
  45.6 4.5 %collective-permute-start.5 = (bf16[16,4224]{1,0:T(8,128)(2,1)S(1)}, bf16[16,4224]{1,0:T(8,128)(2,1)S(1)}, u32[]{:S(2)}, u32[]{:S(2)}) collective-permute-start(bf16[16,4224]{1,0:T(8,128)(2,1)S(1)} %get-tuple-element.21), channel_id=1, source_target_pairs={{0,32},{32,0},{64,96},{96,64},{1,33},{33,1},{65,97},{97,65},{2,34}... | collective-permute-start | bytes 405512 | tf_op jit(solution)/shard_map/ppermute | solution.py:253
  46.0 6.6 %collective-permute-start.6 = (bf16[16,4224]{1,0:T(8,128)(2,1)S(1)}, bf16[16,4224]{1,0:T(8,128)(2,1)S(1)}, u32[]{:S(2)}, u32[]{:S(2)}) collective-permute-start(bf16[16,4224]{1,0:T(8,128)(2,1)S(1)} %get-tuple-element.22), channel_id=1, source_target_pairs={{0,24},{8,16},{16,8},{24,0},{1,25},{9,17},{17,9},{25,1},{2,26},{10... | collective-permute-start | bytes 405512 | tf_op jit(solution)/shard_map/ppermute | solution.py:253
  47.0 5.7 %collective-permute-start.7 = (bf16[16,4224]{1,0:T(8,128)(2,1)S(1)}, bf16[16,4224]{1,0:T(8,128)(2,1)S(1)}, u32[]{:S(2)}, u32[]{:S(2)}) collective-permute-start(bf16[16,4224]{1,0:T(8,128)(2,1)S(1)} %get-tuple-element.23), channel_id=1, source_target_pairs={{0,96},{32,64},{64,32},{96,0},{1,97},{33,65},{65,33},{97,1},{2,98}... | collective-permute-start | bytes 405512 | tf_op jit(solution)/shard_map/ppermute | solution.py:253
  50.3 6.6 %collective-permute-start.9 = (bf16[32,4224]{1,0:T(8,128)(2,1)S(1)}, bf16[32,4224]{1,0:T(8,128)(2,1)S(1)}, u32[]{:S(2)}, u32[]{:S(2)}) collective-permute-start(bf16[32,4224]{1,0:T(8,128)(2,1)S(1)} %get-tuple-element.68.refs_0_), channel_id=1, source_target_pairs={{0,32},{32,0},{64,96},{96,64},{1,33},{33,1},{65,97},{97,65},{2,34}... | collective-permute-start | bytes 811016 | tf_op jit(solution)/shard_map/ppermute | solution.py:253
  51.5 8.2 %collective-permute-start.10 = (bf16[32,4224]{1,0:T(8,128)(2,1)S(1)}, bf16[32,4224]{1,0:T(8,128)(2,1)S(1)}, u32[]{:S(2)}, u32[]{:S(2)}) collective-permute-start(bf16[32,4224]{1,0:T(8,128)(2,1)S(1)} %get-tuple-element.69.refs_1_), channel_id=1, source_target_pairs={{0,24},{8,16},{16,8},{24,0},{1,25},{9,17},{17,9},{25,1},{2,26},{10... | collective-permute-start | bytes 811016 | tf_op jit(solution)/shard_map/ppermute | solution.py:253
  52.8 7.6 %collective-permute-start.11 = (bf16[32,4224]{1,0:T(8,128)(2,1)S(1)}, bf16[32,4224]{1,0:T(8,128)(2,1)S(1)}, u32[]{:S(2)}, u32[]{:S(2)}) collective-permute-start(bf16[32,4224]{1,0:T(8,128)(2,1)S(1)} %get-tuple-element.70.refs_2_), channel_id=1, source_target_pairs={{0,96},{32,64},{64,32},{96,0},{1,97},{33,65},{65,33},{97,1},{2,98}... | collective-permute-start | bytes 811016 | tf_op jit(solution)/shard_map/ppermute | solution.py:253
  53.8 6.8 %collective-permute-start.12 = (bf16[32,4224]{1,0:T(8,128)(2,1)S(1)}, bf16[32,4224]{1,0:T(8,128)(2,1)S(1)}, u32[]{:S(2)}, u32[]{:S(2)}) collective-permute-start(bf16[32,4224]{1,0:T(8,128)(2,1)S(1)} %get-tuple-element.71.refs_3_), channel_id=1, source_target_pairs={{0,8},{8,0},{16,24},{24,16},{1,9},{9,1},{17,25},{25,17},{2,10},{10... | collective-permute-start | bytes 811016 | tf_op jit(solution)/shard_map/ppermute | solution.py:253
  54.2 9.4 %collective-permute-start.8 = (bf16[32,4224]{1,0:T(8,128)(2,1)S(1)}, bf16[32,4224]{1,0:T(8,128)(2,1)S(1)}, u32[]{:S(2)}, u32[]{:S(2)}) collective-permute-start(bf16[32,4224]{1,0:T(8,128)(2,1)S(1)} %behind.4), channel_id=1, source_target_pairs={{0,2},{1,35},{2,64},{3,97},{32,3},{33,34},{34,65},{35,96},{64,0},{... | collective-permute-start | bytes 811016 | tf_op jit(solution)/shard_map/ppermute | solution.py:280
  56.8 6.8 %collective-permute-start.4 = (bf16[32,4224]{1,0:T(8,128)(2,1)S(1)}, bf16[32,4224]{1,0:T(8,128)(2,1)S(1)}, u32[]{:S(2)}, u32[]{:S(2)}) collective-permute-start(bf16[32,4224]{1,0:T(8,128)(2,1)S(1)} %behind.3), channel_id=1, source_target_pairs={{0,0},{1,33},{2,66},{3,99},{32,1},{33,32},{34,67},{35,98},{64,2},{... | collective-permute-start | bytes 811016 | tf_op jit(solution)/shard_map/ppermute | solution.py:280
  57.6 0.7 copy-start.10
  57.6 2.1 %copy-start.12 = (bf16[32,4224]{1,0:T(8,128)(2,1)}, bf16[32,4224]{1,0:T(8,128)(2,1)S(1)}, u32[]{:S(2)}) copy-start(bf16[32,4224]{1,0:T(8,128)(2,1)S(1)} %get-tuple-element.59) | copy-start | bytes 811012
  59.8 0.7 copy-start.6
  59.8 0.8 copy-start.8
  60.6 0.7 copy-start.4
  63.8 12.1 %collective-permute-start.13 = (bf16[64,4224]{1,0:T(8,128)(2,1)S(1)}, bf16[64,4224]{1,0:T(8,128)(2,1)}, u32[]{:S(2)}, u32[]{:S(2)}) collective-permute-start(bf16[64,4224]{1,0:T(8,128)(2,1)S(1)} %behind.5), channel_id=1, source_target_pairs={{0,1},{1,0},{2,3},{3,2},{4,5},{5,4},{6,7},{7,6},{8,9},{9,8},{10,11... | collective-permute-start | bytes 1622024 | tf_op jit(solution)/shard_map/ppermute | solution.py:253
  66.9 16.9 %collective-permute-start.16 = (bf16[64,4224]{1,0:T(8,128)(2,1)S(1)}, bf16[64,4224]{1,0:T(8,128)(2,1)S(1)}, u32[]{:S(2)}, u32[]{:S(2)}) collective-permute-start(bf16[64,4224]{1,0:T(8,128)(2,1)S(1)} %pad_maximum_fusion.12.refs_0_), channel_id=1, source_target_pairs={{0,24},{8,16},{16,8},{24,0},{1,25},{9,17},{17,9},{25,1},{2,26},{10... | collective-permute-start | bytes 1622024 | tf_op jit(solution)/shard_map/ppermute | solution.py:253
  69.5 14.7 %collective-permute-start.18 = (bf16[64,4224]{1,0:T(8,128)(2,1)S(1)}, bf16[64,4224]{1,0:T(8,128)(2,1)S(1)}, u32[]{:S(2)}, u32[]{:S(2)}) collective-permute-start(bf16[64,4224]{1,0:T(8,128)(2,1)S(1)} %pad_maximum_fusion.13.refs_1_), channel_id=1, source_target_pairs={{0,96},{32,64},{64,32},{96,0},{1,97},{33,65},{65,33},{97,1},{2,98}... | collective-permute-start | bytes 1622024 | tf_op jit(solution)/shard_map/ppermute | solution.py:253
  71.0 14.4 %collective-permute-start.20 = (bf16[64,4224]{1,0:T(8,128)(2,1)S(1)}, bf16[64,4224]{1,0:T(8,128)(2,1)S(1)}, u32[]{:S(2)}, u32[]{:S(2)}) collective-permute-start(bf16[64,4224]{1,0:T(8,128)(2,1)S(1)} %pad_maximum_fusion.14.refs_2_), channel_id=1, source_target_pairs={{0,8},{8,0},{16,24},{24,16},{1,9},{9,1},{17,25},{25,17},{2,10},{10... | collective-permute-start | bytes 1622024 | tf_op jit(solution)/shard_map/ppermute | solution.py:253
  71.7 14.9 %collective-permute-start.22 = (bf16[64,4224]{1,0:T(8,128)(2,1)S(1)}, bf16[64,4224]{1,0:T(8,128)(2,1)S(1)}, u32[]{:S(2)}, u32[]{:S(2)}) collective-permute-start(bf16[64,4224]{1,0:T(8,128)(2,1)S(1)} %pad_maximum_fusion.15.refs_3_), channel_id=1, source_target_pairs={{0,32},{32,0},{64,96},{96,64},{1,33},{33,1},{65,97},{97,65},{2,34}... | collective-permute-start | bytes 1622024 | tf_op jit(solution)/shard_map/ppermute | solution.py:253
  77.0 6.8 %copy-start.11 = (bf16[32,4224]{1,0:T(8,128)(2,1)S(1)}, bf16[32,4224]{1,0:T(8,128)(2,1)}, u32[]{:S(2)}) copy-start(bf16[32,4224]{1,0:T(8,128)(2,1)} %copy-done.10) | copy-start | bytes 811012
  77.1 6.8 %copy-start.13 = (bf16[32,4224]{1,0:T(8,128)(2,1)S(1)}, bf16[32,4224]{1,0:T(8,128)(2,1)}, u32[]{:S(2)}) copy-start(bf16[32,4224]{1,0:T(8,128)(2,1)} %copy-done.12) | copy-start | bytes 811012
  77.2 26.2 %collective-permute-start.14 = (bf16[128,4224]{1,0:T(8,128)(2,1)S(1)}, bf16[128,4224]{1,0:T(8,128)(2,1)S(1)}, u32[]{:S(2)}, u32[]{:S(2)}) collective-permute-start(bf16[128,4224]{1,0:T(8,128)(2,1)S(1)} %pad_maximum_fusion.6), channel_id=1, source_target_pairs={{0,3},{1,2},{2,1},{3,0},{4,7},{5,6},{6,5},{7,4},{8,11},{9,10},{10,... | collective-permute-start | bytes 3244040 | tf_op jit(solution)/shard_map/ppermute | solution.py:253
  84.0 1.0 copy-start.7
  84.0 1.0 copy-start.9
  84.1 25.3 %collective-permute-start.17 = (bf16[128,4224]{1,0:T(8,128)(2,1)S(1)}, bf16[128,4224]{1,0:T(8,128)(2,1)S(1)}, u32[]{:S(2)}, u32[]{:S(2)}) collective-permute-start(bf16[128,4224]{1,0:T(8,128)(2,1)S(1)} %pad_maximum_fusion.7), channel_id=1, source_target_pairs={{0,96},{32,64},{64,32},{96,0},{1,97},{33,65},{65,33},{97,1},{2,98}... | collective-permute-start | bytes 3244040 | tf_op jit(solution)/shard_map/ppermute | solution.py:253
  85.2 1.0 copy-start.5
  85.3 24.6 %collective-permute-start.19 = (bf16[128,4224]{1,0:T(8,128)(2,1)S(1)}, bf16[128,4224]{1,0:T(8,128)(2,1)S(1)}, u32[]{:S(2)}, u32[]{:S(2)}) collective-permute-start(bf16[128,4224]{1,0:T(8,128)(2,1)S(1)} %pad_maximum_fusion.8), channel_id=1, source_target_pairs={{0,8},{8,0},{16,24},{24,16},{1,9},{9,1},{17,25},{25,17},{2,10},{10... | collective-permute-start | bytes 3244040 | tf_op jit(solution)/shard_map/ppermute | solution.py:253
  86.5 23.9 %collective-permute-start.21 = (bf16[128,4224]{1,0:T(8,128)(2,1)S(1)}, bf16[128,4224]{1,0:T(8,128)(2,1)S(1)}, u32[]{:S(2)}, u32[]{:S(2)}) collective-permute-start(bf16[128,4224]{1,0:T(8,128)(2,1)S(1)} %pad_maximum_fusion.9), channel_id=1, source_target_pairs={{0,32},{32,0},{64,96},{96,64},{1,33},{33,1},{65,97},{97,65},{2,34}... | collective-permute-start | bytes 3244040 | tf_op jit(solution)/shard_map/ppermute | solution.py:253
  86.9 24.1 %collective-permute-start.23 = (bf16[128,4224]{1,0:T(8,128)(2,1)S(1)}, bf16[128,4224]{1,0:T(8,128)(2,1)S(1)}, u32[]{:S(2)}, u32[]{:S(2)}) collective-permute-start(bf16[128,4224]{1,0:T(8,128)(2,1)S(1)} %pad_maximum_fusion.10), channel_id=1, source_target_pairs={{0,24},{8,16},{16,8},{24,0},{1,25},{9,17},{17,9},{25,1},{2,26},{10... | collective-permute-start | bytes 3244040 | tf_op jit(solution)/shard_map/ppermute | solution.py:253
  103.9 9.4 %collective-permute-start.15 = (bf16[256,4224]{1,0:T(8,128)(2,1)S(1)}, bf16[256,4224]{1,0:T(8,128)(2,1)S(1)}, u32[]{:S(2)}, u32[]{:S(2)}) collective-permute-start(bf16[256,4224]{1,0:T(8,128)(2,1)S(1)} %pad_maximum_fusion.1), channel_id=1, source_target_pairs={{0,4},{4,0},{1,5},{5,1},{2,6},{6,2},{3,7},{7,3},{8,12},{12,8},{9,1... | collective-permute-start | bytes 6488072 | tf_op jit(solution)/shard_map/ppermute | solution.py:249
  118.7 3.4 %collective-permute-start.24 = (f32[264,512]{1,0:T(8,128)S(1)}, f32[264,512]{1,0:T(8,128)S(1)}, u32[]{:S(2)}, u32[]{:S(2)}) collective-permute-start(f32[264,512]{1,0:T(8,128)S(1)} %get-tuple-element.26), channel_id=1, source_target_pairs={{0,4},{4,0},{1,5},{5,1},{2,6},{6,2},{3,7},{7,3},{8,12},{12,8},{9,1... | collective-permute-start | bytes 1622024 | tf_op jit(solution)/shard_map/ppermute | solution.py:249
  120.5 2.3 %collective-permute-start.25 = (f32[264,512]{1,0:T(8,128)S(1)}, f32[264,512]{1,0:T(8,128)S(1)}, u32[]{:S(2)}, u32[]{:S(2)}) collective-permute-start(f32[264,512]{1,0:T(8,128)S(1)} %get-tuple-element.27), channel_id=1, source_target_pairs={{0,4},{4,0},{1,5},{5,1},{2,6},{6,2},{3,7},{7,3},{8,12},{12,8},{9,1... | collective-permute-start | bytes 1622024 | tf_op jit(solution)/shard_map/ppermute | solution.py:249

commit v17 on v16

--- a/solution.py
+++ b/solution.py
@@ -47,16 +47,17 @@
     return at
 
 
-def live_slots(counts_ref):
+def live_slots(kept_ref):
     slot = lax.broadcasted_iota(jnp.int32, (1, SLOTS), 1)
     half = SLOTS // 2
-    return slot < jnp.where(slot < half, counts_ref[0], half + counts_ref[1])
-
-
-def pick_kernel(index_ref, counts_ref, resid_ref, picked_ref, sums_ref):
+    counts = kept_ref[:, SLOTS : SLOTS + 128]
+    return slot < jnp.where(slot < half, counts[:, 0:1], half + counts[:, 1:2])
+
+
+def pick_kernel(kept_ref, resid_ref, picked_ref, sums_ref):
     tokens = resid_ref.shape[0]
     token = lax.broadcasted_iota(jnp.int32, (tokens, SLOTS), 0)
-    kept = jnp.where(live_slots(counts_ref), index_ref[...], -1)
+    kept = jnp.where(live_slots(kept_ref), kept_ref[:, :SLOTS], -1)
     one_hot = jnp.where(token == kept, 1.0, 0.0).astype(bf16)
     total = jnp.zeros((1, SLOTS), f32)
     step = 512
@@ -72,7 +73,7 @@
     sums_ref[...] = jnp.broadcast_to(total, sums_ref.shape)
 
 
-def pick(resid, keep_index, counts):
+def pick(resid, kept):
     vmem = pl.BlockSpec(memory_space=pltpu.VMEM)
     return pl.pallas_call(
         pick_kernel,
@@ -80,18 +81,18 @@
             jax.ShapeDtypeStruct((WIDTH, SLOTS), bf16),
             jax.ShapeDtypeStruct((8, SLOTS), f32),
         ),
-        in_specs=[vmem, pl.BlockSpec(memory_space=pltpu.SMEM), vmem],
+        in_specs=[vmem] * 2,
         out_specs=(vmem,) * 2,
         compiler_params=params(16),
         name="pick",
-    )(keep_index[None, :], counts, resid)
-
-
-def norm_kernel(counts_ref, picked_ref, gain_ref, s0, s1, s2, s3, out_ref):
+    )(kept, resid)
+
+
+def norm_kernel(kept_ref, picked_ref, gain_ref, s0, s1, s2, s3, out_ref):
     squares = (s0[:1, :] + s2[:1, :]) + (s1[:1, :] + s3[:1, :])
     scale = lax.rsqrt(squares / 8192 + epsilon)
     row = lax.broadcasted_iota(jnp.int32, (32, 1), 0)
-    mark = jnp.where(row == 0, jnp.where(live_slots(counts_ref), 0.0, jnp.inf), 0.0).astype(bf16)
+    mark = jnp.where(row == 0, jnp.where(live_slots(kept_ref), 0.0, jnp.inf), 0.0).astype(bf16)
     for x in range(4):
         for c in range(2):
             first = (x * 2 + c) * 256
@@ -103,15 +104,15 @@
                 out_ref[z * 8 + x * 2 + c, 32:, :] = short[high : high + 32, :]
 
 
-def norm(counts, picked, gain, sums):
+def norm(kept, picked, gain, sums):
     return pl.pallas_call(
         norm_kernel,
         out_shape=jax.ShapeDtypeStruct((32, PIECE, SLOTS), bf16),
-        in_specs=[pl.BlockSpec(memory_space=pltpu.SMEM)] + [pl.BlockSpec(memory_space=pltpu.VMEM)] * 6,
+        in_specs=[pl.BlockSpec(memory_space=pltpu.VMEM)] * 7,
         out_specs=pl.BlockSpec(memory_space=pltpu.VMEM),
         compiler_params=params(10),
         name="norm",
-    )(counts, picked, gain, *sums)
+    )(kept, picked, gain, *sums)
 
 
 def pack_kernel(first_ref, in_ref, *refs):
@@ -166,7 +167,7 @@
     return pl.pallas_call(
         behind_kernel,
         out_shape=jax.ShapeDtypeStruct(value.shape, value.dtype),
-        in_specs=[vmem] + [pl.BlockSpec(memory_space=pl.ANY)] * len(after),
+        in_specs=[vmem] * (1 + len(after)),
         out_specs=vmem,
         compiler_params=params(4),
         name="behind",
@@ -264,9 +265,10 @@
 
 def per_device(resid, norm_gain, keep_index, counts):
     z, x, c, y = (lax.axis_index(a) for a in ("z", "x", "c", "y"))
-    picked, sums = pick(resid, keep_index, counts)
+    kept = jnp.concatenate([keep_index, counts, jnp.zeros((126,), jnp.int32)])[None, :]
+    picked, sums = pick(resid, kept)
     all_sums = [sums] + [trade(sums, "y", flip) for flip in (1, 2, 3)]
-    pieces = norm(counts, picked, norm_gain[:, None], all_sums)
+    pieces = norm(kept, picked, norm_gain[:, None], all_sums)
     pieces = lax.all_to_all(pieces, TOK, 0, 0, tiled=True)
 
     loads = jnp.sum((pieces[:, 0, :] < jnp.inf).astype(jnp.int32), axis=1)
@@ -288,11 +290,10 @@
         if step == 0:
             turned = [send(behind(halves[0], streams[:1]), 0), send(behind(halves[1], streams), 2)]
         if step == 1:
-            rows = behind(join(*turned), streams)
-
-    q = y ^ z
-    rows = meet(rows, "y", 1, side(q, 1, True))
-    rows = meet(rows, "y", 3, side(q, 3, False))
+            rows = meet(behind(join(*turned), streams), "y", 1, side(y ^ z, 1, True))
+        if step == 2:
+            rows = meet(behind(rows, streams), "y", 3, side(y ^ z, 3, False))
+
     rows = join(rows, swap(rows))
 
     own, got = [], []

time: 125 us -> 138 us (1.10)
  other arithmetic: 7.71 us -> 14.1 us
  waiting for transfers between devices: 33 us -> 38.1 us
  local copies, waits for them, and re-layouts: 6.22 us -> 10.2 us
  starting transfers between devices: 37.7 us -> 34.1 us
    ppermute x21, waiting for transfers between devices: 27.4 us -> 34.8 us  [trade(): return lax.ppermute(value, axis, [(i, i ^ flip) for i in range(4)])]
    ppermute x21, starting transfers between devices: 27.6 us -> 20.3 us  [trade(): return lax.ppermute(value, axis, [(i, i ^ flip) for i in range(4)])]
    concatenate x18, other arithmetic: 1.97 us -> 6.16 us  [join(): return jnp.concatenate(values, axis=0)]
    unnamed x30 -> x58, local copies, waits for them, and re-layouts: 5.77 us -> 9.74 us
    ppermute x2, starting transfers between devices: 2.59 us -> 5.6 us  [send(): lax.ppermute(half, ('z', 'y'), [(q * 4 + u, u * 4 + (q ^ u ^ turn)) for q...]
    pallas_call x3 -> x4, Pallas kernels: 0.08 us -> 2.28 us  [behind(): pl.pallas_call(behind_kernel, out_shape=jax.ShapeDtypeStruct(value.shape,...]
    ppermute x3, waiting for transfers between devices: 3.21 us -> 1.49 us  [swap(): return lax.ppermute(value, 'c', [(0, 1), (1, 0)])]
    select_n x18, other arithmetic: 4.26 us -> 5.65 us  [meet(): jnp.where(which == 0, value, got)]
  transfers between devices with their start and end apart: 26 -> 26, of which waited for: 13 -> 10; matrix products, arithmetic and copies ran while one was open for 5% -> 6% of each run, Pallas kernels for 0% -> 0%
where the time goes in v17:
time: 138 us
  waiting for transfers between devices  38.1 us (28%)
  starting transfers between devices  34.1 us (25%)
  blocking collectives  27 us (20%)
  other arithmetic  14.1 us (10%)
  Pallas kernels  12.5 us (9%)
  local copies, waits for them, and re-layouts  10.2 us (7%)
  between operations  1.88 us (1%)
    ppermute x21, waiting for transfers between devices, trade(): return lax.ppermute(value, axis, [(i, i ^ flip) for i in range(4)])  34.8 us
    all_to_all x1, blocking collectives, per_device(): pieces = lax.all_to_all(pieces, TOK, 0, 0, tiled=True)  27 us
    ppermute x21, starting transfers between devices, trade(): return lax.ppermute(value, axis, [(i, i ^ flip) for i in range(4)])  20.3 us
    unnamed x58, local copies, waits for them, and re-layouts  9.74 us
    ppermute x3, starting transfers between devices, swap(): return lax.ppermute(value, 'c', [(0, 1), (1, 0)])  8.2 us
    concatenate x18, other arithmetic, join(): return jnp.concatenate(values, axis=0)  6.16 us
    select_n x18, other arithmetic, meet(): jnp.where(which == 0, value, got)  5.65 us
    ppermute x2, starting transfers between devices, send(): lax.ppermute(half, ('z', 'y'), [(q * 4 + u, u * 4 + (q ^ u ^ turn)) for q...  5.6 us
  transfers between devices with their start and end apart: 26, of which 10 were waited for; matrix products, arithmetic and copies ran while one was open for 6% of the time, Pallas kernels for 0%

profile of v17, /device:TPU:1, one launch (start us, length us, event | category | flops | bytes accessed | tf_op | source)
XLA Modules:
  0.0 137.9 jit_solution(17935703370950040936)
XLA Ops:
  0.6 0.8 pad_add_fusion
  1.4 1.6 %copy-done.1 = bf16[512,2048]{1,0:T(8,128)(2,1)S(1)} copy-done((bf16[512,2048]{1,0:T(8,128)(2,1)S(1)}, bf16[512,2048]{1,0:T(8,128)(2,1)}, u32[]{:S(2)}) %copy-start.1) | copy-done | bytes 2097176
  3.0 0.8 pick.1
  3.8 3.6 %collective-permute-start.2 = (f32[8,256]{1,0:T(8,128)S(1)}, f32[8,256]{1,0:T(8,128)S(1)}, u32[]{:S(2)}, u32[]{:S(2)}) collective-permute-start(f32[8,256]{1,0:T(8,128)S(1)} %get-tuple-element.17.s0), channel_id=1, source_target_pairs={{0,3},{1,2},{2,1},{3,0},{4,7},{5,6},{6,5},{7,4},{8,11},{9,10},{10,... | collective-permute-start | bytes 24584 | tf_op jit(solution)/shard_map/ppermute | solution.py:254
  8.5 3.0 %collective-permute-done.1.s2 = f32[8,256]{1,0:T(8,128)S(1)} collective-permute-done((f32[8,256]{1,0:T(8,128)S(1)}, f32[8,256]{1,0:T(8,128)S(1)}, u32[]{:S(2)}, u32[]{:S(2)}) %collective-permute-start.1) | collective-permute-done | bytes 8224 | tf_op jit(solution)/shard_map/ppermute | solution.py:254
  11.8 27.0 %all_to_all.5.in_ref = bf16[32,64,256]{2,1,0:T(8,128)(2,1)S(1)} all-to-all(bf16[32,64,256]{2,1,0:T(8,128)(2,1)S(1)} %norm.1), channel_id=1, replica_groups=mesh['z'=4,'x'=4,'c'=2,'y'=4] {'z','x','c'}, dimensions={0} | all-to-all | bytes 2097152 | tf_op jit(solution)/shard_map/all_to_all | solution.py:272
  38.9 1.2 fusion
  40.4 2.1 %pack.1 = (bf16[32,4224]{1,0:T(8,128)(2,1)S(1)}, bf16[32,4224]{1,0:T(8,128)(2,1)S(1)}, bf16[16,4224]{1,0:T(8,128)(2,1)S(1)}, bf16[16,4224]{1,0:T(8,128)(2,1)S(1)...) custom-call(s32[32]{0:T(128)S(1)} %sub.3.first_ref, bf16[32,64,256]{2,1,0:T(8,128)(2,1)S(1)} %all_to_all.5.in_ref), custom_call_target="tpu_custom_call" | custom-call | tf_op jit(solution)/shard_map/pack/pallas_call | solution.py:149
  42.4 1.4 collective-permute-start.6
  44.1 0.6 collective-permute-start.7
  44.7 3.8 %collective-permute-done.6 = bf16[16,4224]{1,0:T(8,128)(2,1)S(1)} collective-permute-done((bf16[16,4224]{1,0:T(8,128)(2,1)S(1)}, bf16[16,4224]{1,0:T(8,128)(2,1)S(1)}, u32[]{:S(2)}, u32[]{:S(2)}) %collective-permute-start.6) | collective-permute-done | bytes 135200 | tf_op jit(solution)/shard_map/ppermute | solution.py:254
  48.5 1.3 collective-permute-done.7
  50.0 0.6 collective-permute-start.11
  50.5 1.2 collective-permute-start.12
  51.9 2.0 %collective-permute-start.10 = (bf16[32,4224]{1,0:T(8,128)(2,1)S(1)}, bf16[32,4224]{1,0:T(8,128)(2,1)S(1)}, u32[]{:S(2)}, u32[]{:S(2)}) collective-permute-start(bf16[32,4224]{1,0:T(8,128)(2,1)S(1)} %get-tuple-element.69.refs_1_), channel_id=1, source_target_pairs={{0,24},{8,16},{16,8},{24,0},{1,25},{9,17},{17,9},{25,1},{2,26},{10... | collective-permute-start | bytes 811016 | tf_op jit(solution)/shard_map/ppermute | solution.py:254
  54.0 0.7 collective-permute-start.4
  54.7 2.0 %collective-permute-done.12 = bf16[32,4224]{1,0:T(8,128)(2,1)S(1)} collective-permute-done((bf16[32,4224]{1,0:T(8,128)(2,1)S(1)}, bf16[32,4224]{1,0:T(8,128)(2,1)S(1)}, u32[]{:S(2)}, u32[]{:S(2)}) %collective-permute-start.12) | collective-permute-done | bytes 270368 | tf_op jit(solution)/shard_map/ppermute | solution.py:254
  56.7 4.9 %collective-permute-start.8 = (bf16[32,4224]{1,0:T(8,128)(2,1)S(1)}, bf16[32,4224]{1,0:T(8,128)(2,1)S(1)}, u32[]{:S(2)}, u32[]{:S(2)}) collective-permute-start(bf16[32,4224]{1,0:T(8,128)(2,1)S(1)} %behind.5), channel_id=1, source_target_pairs={{0,2},{1,35},{2,64},{3,97},{32,3},{33,34},{34,65},{35,96},{64,0},{... | collective-permute-start | bytes 811016 | tf_op jit(solution)/shard_map/ppermute | solution.py:282
  62.0 0.5 copy-done.18
  62.7 0.6 copy-done.20
  63.4 0.9 pad_maximum_fusion.13.refs_1_
  64.3 1.9 %collective-permute-done.8 = bf16[32,4224]{1,0:T(8,128)(2,1)S(1)} collective-permute-done((bf16[32,4224]{1,0:T(8,128)(2,1)S(1)}, bf16[32,4224]{1,0:T(8,128)(2,1)S(1)}, u32[]{:S(2)}, u32[]{:S(2)}) %collective-permute-start.8) | collective-permute-done | bytes 270368 | tf_op jit(solution)/shard_map/ppermute | solution.py:282
  66.2 1.1 behind.6
  67.3 0.5 collective-permute-start.13
  67.8 5.2 %collective-permute-start.15 = (bf16[64,4224]{1,0:T(8,128)(2,1)}, bf16[64,4224]{1,0:T(8,128)(2,1)S(1)}, u32[]{:S(2)}, u32[]{:S(2)}) collective-permute-start(bf16[64,4224]{1,0:T(8,128)(2,1)} %pad_maximum_fusion.13.refs_1_), channel_id=1, source_target_pairs={{0,96},{32,64},{64,32},{96,0},{1,97},{33,65},{65,33},{97,1},{2,98}... | collective-permute-start | bytes 1622024 | tf_op jit(solution)/shard_map/ppermute | solution.py:254
  72.9 0.7 collective-permute-start.14
  73.8 3.6 %collective-permute-done.13 = bf16[64,4224]{1,0:T(8,128)(2,1)} collective-permute-done((bf16[64,4224]{1,0:T(8,128)(2,1)S(1)}, bf16[64,4224]{1,0:T(8,128)(2,1)}, u32[]{:S(2)}, u32[]{:S(2)}) %collective-permute-start.13) | collective-permute-done | bytes 540704 | tf_op jit(solution)/shard_map/ppermute | solution.py:254
  77.4 1.1 broadcast_select_fusion.19
  78.6 3.7 %collective-permute-done.17 = bf16[64,4224]{1,0:T(8,128)(2,1)S(1)} collective-permute-done((bf16[64,4224]{1,0:T(8,128)(2,1)S(1)}, bf16[64,4224]{1,0:T(8,128)(2,1)S(1)}, u32[]{:S(2)}, u32[]{:S(2)}) %collective-permute-start.17) | collective-permute-done | bytes 540704 | tf_op jit(solution)/shard_map/ppermute | solution.py:254
  82.6 0.7 copy-done.2
  84.0 0.7 copy-done.6
  85.6 0.7 copy-done.10
  87.2 0.7 copy-done.14
  88.2 1.2 behind.7
  89.6 1.4 collective-permute-start.21
  90.9 2.0 %collective-permute-start.20 = (bf16[128,4224]{1,0:T(8,128)(2,1)S(1)}, bf16[128,4224]{1,0:T(8,128)(2,1)S(1)}, u32[]{:S(2)}, u32[]{:S(2)}) collective-permute-start(bf16[128,4224]{1,0:T(8,128)(2,1)S(1)} %pad_maximum_fusion.7.refs_0_), channel_id=1, source_target_pairs={{0,96},{32,64},{64,32},{96,0},{1,97},{33,65},{65,33},{97,1},{2,98}... | collective-permute-start | bytes 3244040 | tf_op jit(solution)/shard_map/ppermute | solution.py:254
  93.0 17.4 %collective-permute-done.18 = bf16[128,4224]{1,0:T(8,128)(2,1)} collective-permute-done((bf16[128,4224]{1,0:T(8,128)(2,1)}, bf16[128,4224]{1,0:T(8,128)(2,1)}, u32[]{:S(2)}, u32[]{:S(2)}) %collective-permute-start.18) | collective-permute-done | bytes 1081376 | tf_op jit(solution)/shard_map/ppermute | solution.py:254
  110.4 1.8 %broadcast_select_fusion.9 = (bf16[128,4224]{1,0:T(8,128)(2,1)S(1)}, bf16[128,4224]{1,0:T(8,128)(2,1)S(1)}) fusion(bf16[128,4224]{1,0:T(8,128)(2,1)} %behind.7, bf16[128,4224]{1,0:T(8,128)(2,1)} %collective-permute-done.18, pred[]{:T(512)S(6)} %eq.16), kind=kLoop, calls=%fused_computation.20 | loop fusion | flops 1081344 | bytes 4325377 | tf_op jit(solution)/shard_map/jit(_where)/select_n | solution.py:263
  112.3 7.3 %collective-permute-start.19 = (bf16[256,4224]{1,0:T(8,128)(2,1)S(1)}, bf16[256,4224]{1,0:T(8,128)(2,1)}, u32[]{:S(2)}, u32[]{:S(2)}) collective-permute-start(bf16[256,4224]{1,0:T(8,128)(2,1)S(1)} %pad_maximum_fusion.1), channel_id=1, source_target_pairs={{0,4},{4,0},{1,5},{5,1},{2,6},{6,2},{3,7},{7,3},{8,12},{12,8},{9,1... | collective-permute-start | bytes 6488072 | tf_op jit(solution)/shard_map/ppermute | solution.py:250
  120.1 0.8 copy-done.11
  122.3 0.9 copy-done.3
  123.8 3.9 %pad_maximum_fusion.refs_0_ = bf16[512,4224]{1,0:T(8,128)(2,1)S(1)} fusion(bf16[256,4224]{1,0:T(8,128)(2,1)} %collective-permute-done.19, bf16[128,4224]{1,0:T(8,128)(2,1)S(1)} %get-tuple-element.41, bf16[128,4224]{1,0:T(8,128)(2,1)S(1)} %get-tuple-element.40), kind=kLoop, calls=%fused_computation | loop fusion | flops 12976128 | bytes 8650752 | tf_op jit(solution)/shard_map/concatenate | solution.py:258
  127.7 2.4 %gram.3 = (f32[264,512]{1,0:T(8,128)S(1)}, f32[264,512]{1,0:T(8,128)S(1)}) custom-call(bf16[512,4224]{1,0:T(8,128)(2,1)S(1)} %pad_maximum_fusion.refs_0_, bf16[256,4224]{1,0:T(8,128)(2,1)S(1)} %pad_maximum_fusion.2.refs_1_, bf16[256,4224]{1,0:T(8,128)(2,1)S(1)} %pad_maximum_fusion.3.refs_2_, bf16[256,4224]{1,0:T(8,128)(2,1)S(1)} %pad_maximum_fusion.4.refs_3_, ...), custom_call_target="tpu_custom_call" | custom-call | flops 2147483648 | bytes 6291456 | tf_op jit(solution)/shard_map/gram/pallas_call | solution.py:206
  130.1 2.4 %gram.2 = (f32[264,512]{1,0:T(8,128)S(1)}, f32[264,512]{1,0:T(8,128)S(1)}) custom-call(bf16[512,4224]{1,0:T(8,128)(2,1)S(1)} %pad_maximum_fusion.refs_0_, bf16[256,4224]{1,0:T(8,128)(2,1)S(1)} %pad_maximum_fusion.2.refs_1_, bf16[256,4224]{1,0:T(8,128)(2,1)S(1)} %pad_maximum_fusion.3.refs_2_, bf16[256,4224]{1,0:T(8,128)(2,1)S(1)} %pad_maximum_fusion.4.refs_3_, ...), custom_call_target="tpu_custom_call" | custom-call | flops 2147483648 | bytes 6291456 | tf_op jit(solution)/shard_map/gram/pallas_call | solution.py:206
  132.5 0.8 collective-permute-start.25
  134.2 0.7 collective-permute-done.25.refs_3_
  134.9 0.8 collective-permute-done.24.refs_2_
  135.7 2.2 %finish.1 = (f32[1,2048]{1,0:T(1,128)}, f32[256,2048]{1,0:T(8,128)}) custom-call(s32[3]{0:T(128)S(1)} %pad_add_fusion.1.info_ref, f32[1]{0:T(128)} %bitcast.4.part_ref, f32[264,512]{1,0:T(8,128)S(1)} %get-tuple-element.24.refs_0_, f32[264,512]{1,0:T(8,128)S(1)} %get-tuple-element.25.refs_1_, f32[264,512]{1,0:T(8,128)S(1)} %collective-permute-done.24.refs_2_, ...), custom_call_target="tpu_custom_call" | custom-call | tf_op jit(solution)/shard_map/finish/pallas_call | solution.py:236
  (119 shorter events, 9.1 us)
Async XLA Ops:
  0.6 7.5 %copy-start.28 = (f32[2048]{0:T(1024)S(1)}, f32[2048]{0:T(1024)}, u32[]{:S(2)}) copy-start(f32[2048]{0:T(1024)} %param.5) | copy-start | bytes 24580
  1.4 1.6 %copy-start.1 = (bf16[512,2048]{1,0:T(8,128)(2,1)S(1)}, bf16[512,2048]{1,0:T(8,128)(2,1)}, u32[]{:S(2)}) copy-start(bf16[512,2048]{1,0:T(8,128)(2,1)} %resid_ref.1) | copy-start | bytes 6291460
  3.8 4.7 %collective-permute-start.2 = (f32[8,256]{1,0:T(8,128)S(1)}, f32[8,256]{1,0:T(8,128)S(1)}, u32[]{:S(2)}, u32[]{:S(2)}) collective-permute-start(f32[8,256]{1,0:T(8,128)S(1)} %get-tuple-element.17.s0), channel_id=1, source_target_pairs={{0,3},{1,2},{2,1},{3,0},{4,7},{5,6},{6,5},{7,4},{8,11},{9,10},{10,... | collective-permute-start | bytes 24584 | tf_op jit(solution)/shard_map/ppermute | solution.py:254
  7.5 4.0 %collective-permute-start.1 = (f32[8,256]{1,0:T(8,128)S(1)}, f32[8,256]{1,0:T(8,128)S(1)}, u32[]{:S(2)}, u32[]{:S(2)}) collective-permute-start(f32[8,256]{1,0:T(8,128)S(1)} %get-tuple-element.17.s0), channel_id=1, source_target_pairs={{0,2},{1,3},{2,0},{3,1},{4,6},{5,7},{6,4},{7,5},{8,10},{9,11},{10,... | collective-permute-start | bytes 24584 | tf_op jit(solution)/shard_map/ppermute | solution.py:254
  7.8 3.7 %collective-permute-start = (f32[8,256]{1,0:T(8,128)S(1)}, f32[8,256]{1,0:T(8,128)S(1)}, u32[]{:S(2)}, u32[]{:S(2)}) collective-permute-start(f32[8,256]{1,0:T(8,128)S(1)} %get-tuple-element.17.s0), channel_id=1, source_target_pairs={{0,1},{1,0},{2,3},{3,2},{4,5},{5,4},{6,7},{7,6},{8,9},{9,8},{10,11... | collective-permute-start | bytes 24584 | tf_op jit(solution)/shard_map/ppermute | solution.py:254
  42.4 6.1 %collective-permute-start.6 = (bf16[16,4224]{1,0:T(8,128)(2,1)S(1)}, bf16[16,4224]{1,0:T(8,128)(2,1)S(1)}, u32[]{:S(2)}, u32[]{:S(2)}) collective-permute-start(bf16[16,4224]{1,0:T(8,128)(2,1)S(1)} %get-tuple-element.22), channel_id=1, source_target_pairs={{0,24},{8,16},{16,8},{24,0},{1,25},{9,17},{17,9},{25,1},{2,26},{10... | collective-permute-start | bytes 405512 | tf_op jit(solution)/shard_map/ppermute | solution.py:254
  43.8 8.0 %collective-permute-start.3 = (bf16[16,4224]{1,0:T(8,128)(2,1)S(1)}, bf16[16,4224]{1,0:T(8,128)(2,1)S(1)}, u32[]{:S(2)}, u32[]{:S(2)}) collective-permute-start(bf16[16,4224]{1,0:T(8,128)(2,1)S(1)} %get-tuple-element.19), channel_id=1, source_target_pairs={{0,8},{8,0},{16,24},{24,16},{1,9},{9,1},{17,25},{25,17},{2,10},{10... | collective-permute-start | bytes 405512 | tf_op jit(solution)/shard_map/ppermute | solution.py:254
  43.8 8.0 %collective-permute-start.5 = (bf16[16,4224]{1,0:T(8,128)(2,1)S(1)}, bf16[16,4224]{1,0:T(8,128)(2,1)S(1)}, u32[]{:S(2)}, u32[]{:S(2)}) collective-permute-start(bf16[16,4224]{1,0:T(8,128)(2,1)S(1)} %get-tuple-element.21), channel_id=1, source_target_pairs={{0,32},{32,0},{64,96},{96,64},{1,33},{33,1},{65,97},{97,65},{2,34}... | collective-permute-start | bytes 405512 | tf_op jit(solution)/shard_map/ppermute | solution.py:254
  44.1 5.7 %collective-permute-start.7 = (bf16[16,4224]{1,0:T(8,128)(2,1)S(1)}, bf16[16,4224]{1,0:T(8,128)(2,1)S(1)}, u32[]{:S(2)}, u32[]{:S(2)}) collective-permute-start(bf16[16,4224]{1,0:T(8,128)(2,1)S(1)} %get-tuple-element.23), channel_id=1, source_target_pairs={{0,96},{32,64},{64,32},{96,0},{1,97},{33,65},{65,33},{97,1},{2,98}... | collective-permute-start | bytes 405512 | tf_op jit(solution)/shard_map/ppermute | solution.py:254
  50.0 11.8 %collective-permute-start.11 = (bf16[32,4224]{1,0:T(8,128)(2,1)S(1)}, bf16[32,4224]{1,0:T(8,128)(2,1)S(1)}, u32[]{:S(2)}, u32[]{:S(2)}) collective-permute-start(bf16[32,4224]{1,0:T(8,128)(2,1)S(1)} %get-tuple-element.70.refs_2_), channel_id=1, source_target_pairs={{0,96},{32,64},{64,32},{96,0},{1,97},{33,65},{65,33},{97,1},{2,98}... | collective-permute-start | bytes 811016 | tf_op jit(solution)/shard_map/ppermute | solution.py:254
  50.5 6.1 %collective-permute-start.12 = (bf16[32,4224]{1,0:T(8,128)(2,1)S(1)}, bf16[32,4224]{1,0:T(8,128)(2,1)S(1)}, u32[]{:S(2)}, u32[]{:S(2)}) collective-permute-start(bf16[32,4224]{1,0:T(8,128)(2,1)S(1)} %get-tuple-element.71.refs_3_), channel_id=1, source_target_pairs={{0,8},{8,0},{16,24},{24,16},{1,9},{9,1},{17,25},{25,17},{2,10},{10... | collective-permute-start | bytes 811016 | tf_op jit(solution)/shard_map/ppermute | solution.py:254
  51.9 10.7 %collective-permute-start.10 = (bf16[32,4224]{1,0:T(8,128)(2,1)S(1)}, bf16[32,4224]{1,0:T(8,128)(2,1)S(1)}, u32[]{:S(2)}, u32[]{:S(2)}) collective-permute-start(bf16[32,4224]{1,0:T(8,128)(2,1)S(1)} %get-tuple-element.69.refs_1_), channel_id=1, source_target_pairs={{0,24},{8,16},{16,8},{24,0},{1,25},{9,17},{17,9},{25,1},{2,26},{10... | collective-permute-start | bytes 811016 | tf_op jit(solution)/shard_map/ppermute | solution.py:254
  53.9 8.0 %collective-permute-start.9 = (bf16[32,4224]{1,0:T(8,128)(2,1)S(1)}, bf16[32,4224]{1,0:T(8,128)(2,1)S(1)}, u32[]{:S(2)}, u32[]{:S(2)}) collective-permute-start(bf16[32,4224]{1,0:T(8,128)(2,1)S(1)} %get-tuple-element.68.refs_0_), channel_id=1, source_target_pairs={{0,32},{32,0},{64,96},{96,64},{1,33},{33,1},{65,97},{97,65},{2,34}... | collective-permute-start | bytes 811016 | tf_op jit(solution)/shard_map/ppermute | solution.py:254
  54.0 10.3 %collective-permute-start.4 = (bf16[32,4224]{1,0:T(8,128)(2,1)S(1)}, bf16[32,4224]{1,0:T(8,128)(2,1)S(1)}, u32[]{:S(2)}, u32[]{:S(2)}) collective-permute-start(bf16[32,4224]{1,0:T(8,128)(2,1)S(1)} %behind.4), channel_id=1, source_target_pairs={{0,0},{1,33},{2,66},{3,99},{32,1},{33,32},{34,67},{35,98},{64,2},{... | collective-permute-start | bytes 811016 | tf_op jit(solution)/shard_map/ppermute | solution.py:282
  56.7 9.5 %collective-permute-start.8 = (bf16[32,4224]{1,0:T(8,128)(2,1)S(1)}, bf16[32,4224]{1,0:T(8,128)(2,1)S(1)}, u32[]{:S(2)}, u32[]{:S(2)}) collective-permute-start(bf16[32,4224]{1,0:T(8,128)(2,1)S(1)} %behind.5), channel_id=1, source_target_pairs={{0,2},{1,35},{2,64},{3,97},{32,3},{33,34},{34,65},{35,96},{64,0},{... | collective-permute-start | bytes 811016 | tf_op jit(solution)/shard_map/ppermute | solution.py:282
  63.4 0.9 copy-start.26
  63.4 2.8 %copy-start.24 = (bf16[32,4224]{1,0:T(8,128)(2,1)}, bf16[32,4224]{1,0:T(8,128)(2,1)S(1)}, u32[]{:S(2)}) copy-start(bf16[32,4224]{1,0:T(8,128)(2,1)S(1)} %get-tuple-element.56) | copy-start | bytes 811012
  67.3 10.1 %collective-permute-start.13 = (bf16[64,4224]{1,0:T(8,128)(2,1)S(1)}, bf16[64,4224]{1,0:T(8,128)(2,1)}, u32[]{:S(2)}, u32[]{:S(2)}) collective-permute-start(bf16[64,4224]{1,0:T(8,128)(2,1)S(1)} %behind.6), channel_id=1, source_target_pairs={{0,1},{1,0},{2,3},{3,2},{4,5},{5,4},{6,7},{7,6},{8,9},{9,8},{10,11... | collective-permute-start | bytes 1622024 | tf_op jit(solution)/shard_map/ppermute | solution.py:254
  67.8 18.7 %collective-permute-start.15 = (bf16[64,4224]{1,0:T(8,128)(2,1)}, bf16[64,4224]{1,0:T(8,128)(2,1)S(1)}, u32[]{:S(2)}, u32[]{:S(2)}) collective-permute-start(bf16[64,4224]{1,0:T(8,128)(2,1)} %pad_maximum_fusion.13.refs_1_), channel_id=1, source_target_pairs={{0,96},{32,64},{64,32},{96,0},{1,97},{33,65},{65,33},{97,1},{2,98}... | collective-permute-start | bytes 1622024 | tf_op jit(solution)/shard_map/ppermute | solution.py:254
  72.9 12.0 %collective-permute-start.14 = (bf16[64,4224]{1,0:T(8,128)(2,1)S(1)}, bf16[64,4224]{1,0:T(8,128)(2,1)S(1)}, u32[]{:S(2)}, u32[]{:S(2)}) collective-permute-start(bf16[64,4224]{1,0:T(8,128)(2,1)S(1)} %pad_maximum_fusion.12.refs_0_), channel_id=1, source_target_pairs={{0,24},{8,16},{16,8},{24,0},{1,25},{9,17},{17,9},{25,1},{2,26},{10... | collective-permute-start | bytes 1622024 | tf_op jit(solution)/shard_map/ppermute | solution.py:254
  73.7 9.8 %collective-permute-start.16 = (bf16[64,4224]{1,0:T(8,128)(2,1)S(1)}, bf16[64,4224]{1,0:T(8,128)(2,1)S(1)}, u32[]{:S(2)}, u32[]{:S(2)}) collective-permute-start(bf16[64,4224]{1,0:T(8,128)(2,1)S(1)} %pad_maximum_fusion.14.refs_2_), channel_id=1, source_target_pairs={{0,8},{8,0},{16,24},{24,16},{1,9},{9,1},{17,25},{25,17},{2,10},{10... | collective-permute-start | bytes 1622024 | tf_op jit(solution)/shard_map/ppermute | solution.py:254
  73.7 8.6 %collective-permute-start.17 = (bf16[64,4224]{1,0:T(8,128)(2,1)S(1)}, bf16[64,4224]{1,0:T(8,128)(2,1)S(1)}, u32[]{:S(2)}, u32[]{:S(2)}) collective-permute-start(bf16[64,4224]{1,0:T(8,128)(2,1)S(1)} %pad_maximum_fusion.15.refs_3_), channel_id=1, source_target_pairs={{0,32},{32,0},{64,96},{96,64},{1,33},{33,1},{65,97},{97,65},{2,34}... | collective-permute-start | bytes 1622024 | tf_op jit(solution)/shard_map/ppermute | solution.py:254
  82.5 1.0 copy-start.4
  82.5 1.2 copy-start.19
  83.9 1.0 copy-start.8
  83.9 1.2 copy-start.21
  83.9 1.4 %copy-start.23 = (bf16[32,4224]{1,0:T(8,128)(2,1)S(1)}, bf16[32,4224]{1,0:T(8,128)(2,1)}, u32[]{:S(2)}) copy-start(bf16[32,4224]{1,0:T(8,128)(2,1)} %copy-done.22) | copy-start | bytes 811012
  85.5 1.0 copy-start.12
  85.5 1.2 copy-start.25
  85.5 1.4 %copy-start.27 = (bf16[32,4224]{1,0:T(8,128)(2,1)S(1)}, bf16[32,4224]{1,0:T(8,128)(2,1)}, u32[]{:S(2)}) copy-start(bf16[32,4224]{1,0:T(8,128)(2,1)} %copy-done.26) | copy-start | bytes 811012
  87.2 1.0 copy-start.16
  88.2 1.4 copy-start
  89.6 20.8 %collective-permute-start.18 = (bf16[128,4224]{1,0:T(8,128)(2,1)}, bf16[128,4224]{1,0:T(8,128)(2,1)}, u32[]{:S(2)}, u32[]{:S(2)}) collective-permute-start(bf16[128,4224]{1,0:T(8,128)(2,1)} %behind.7), channel_id=1, source_target_pairs={{0,3},{1,2},{2,1},{3,0},{4,7},{5,6},{6,5},{7,4},{8,11},{9,10},{10,... | collective-permute-start | bytes 3244040 | tf_op jit(solution)/shard_map/ppermute | solution.py:254
  89.6 30.0 %collective-permute-start.21 = (bf16[128,4224]{1,0:T(8,128)(2,1)}, bf16[128,4224]{1,0:T(8,128)(2,1)S(1)}, u32[]{:S(2)}, u32[]{:S(2)}) collective-permute-start(bf16[128,4224]{1,0:T(8,128)(2,1)} %copy-done), channel_id=1, source_target_pairs={{0,8},{8,0},{16,24},{24,16},{1,9},{9,1},{17,25},{25,17},{2,10},{10... | collective-permute-start | bytes 3244040 | tf_op jit(solution)/shard_map/ppermute | solution.py:254
  90.9 29.2 %collective-permute-start.20 = (bf16[128,4224]{1,0:T(8,128)(2,1)S(1)}, bf16[128,4224]{1,0:T(8,128)(2,1)S(1)}, u32[]{:S(2)}, u32[]{:S(2)}) collective-permute-start(bf16[128,4224]{1,0:T(8,128)(2,1)S(1)} %pad_maximum_fusion.7.refs_0_), channel_id=1, source_target_pairs={{0,96},{32,64},{64,32},{96,0},{1,97},{33,65},{65,33},{97,1},{2,98}... | collective-permute-start | bytes 3244040 | tf_op jit(solution)/shard_map/ppermute | solution.py:254
  92.9 28.6 %collective-permute-start.22 = (bf16[128,4224]{1,0:T(8,128)(2,1)S(1)}, bf16[128,4224]{1,0:T(8,128)(2,1)S(1)}, u32[]{:S(2)}, u32[]{:S(2)}) collective-permute-start(bf16[128,4224]{1,0:T(8,128)(2,1)S(1)} %pad_maximum_fusion.9.refs_2_), channel_id=1, source_target_pairs={{0,32},{32,0},{64,96},{96,64},{1,33},{33,1},{65,97},{97,65},{2,34}... | collective-permute-start | bytes 3244040 | tf_op jit(solution)/shard_map/ppermute | solution.py:254
  92.9 29.3 %collective-permute-start.23 = (bf16[128,4224]{1,0:T(8,128)(2,1)S(1)}, bf16[128,4224]{1,0:T(8,128)(2,1)S(1)}, u32[]{:S(2)}, u32[]{:S(2)}) collective-permute-start(bf16[128,4224]{1,0:T(8,128)(2,1)S(1)} %pad_maximum_fusion.10.refs_3_), channel_id=1, source_target_pairs={{0,24},{8,16},{16,8},{24,0},{1,25},{9,17},{17,9},{25,1},{2,26},{10... | collective-permute-start | bytes 3244040 | tf_op jit(solution)/shard_map/ppermute | solution.py:254
  112.1 7.4 %copy-start.15 = (bf16[64,4224]{1,0:T(8,128)(2,1)S(1)}, bf16[64,4224]{1,0:T(8,128)(2,1)}, u32[]{:S(2)}) copy-start(bf16[64,4224]{1,0:T(8,128)(2,1)} %copy-done.14) | copy-start | bytes 1622020
  112.1 7.4 %copy-start.17 = (bf16[64,4224]{1,0:T(8,128)(2,1)S(1)}, bf16[64,4224]{1,0:T(8,128)(2,1)}, u32[]{:S(2)}) copy-start(bf16[64,4224]{1,0:T(8,128)(2,1)} %copy-done.16) | copy-start | bytes 1622020
  112.3 11.5 %collective-permute-start.19 = (bf16[256,4224]{1,0:T(8,128)(2,1)S(1)}, bf16[256,4224]{1,0:T(8,128)(2,1)}, u32[]{:S(2)}, u32[]{:S(2)}) collective-permute-start(bf16[256,4224]{1,0:T(8,128)(2,1)S(1)} %pad_maximum_fusion.1), channel_id=1, source_target_pairs={{0,4},{4,0},{1,5},{5,1},{2,6},{6,2},{3,7},{7,3},{8,12},{12,8},{9,1... | collective-permute-start | bytes 6488072 | tf_op jit(solution)/shard_map/ppermute | solution.py:250
  119.9 1.0 copy-start.11
  119.9 1.2 copy-start.13
  120.1 1.4 %copy-start.7 = (bf16[64,4224]{1,0:T(8,128)(2,1)S(1)}, bf16[64,4224]{1,0:T(8,128)(2,1)}, u32[]{:S(2)}) copy-start(bf16[64,4224]{1,0:T(8,128)(2,1)} %copy-done.6) | copy-start | bytes 1622020
  120.1 1.4 %copy-start.9 = (bf16[64,4224]{1,0:T(8,128)(2,1)S(1)}, bf16[64,4224]{1,0:T(8,128)(2,1)}, u32[]{:S(2)}) copy-start(bf16[64,4224]{1,0:T(8,128)(2,1)} %copy-done.8) | copy-start | bytes 1622020
  122.1 1.0 copy-start.3
  122.1 1.2 copy-start.5
  132.5 2.4 %collective-permute-start.25 = (f32[264,512]{1,0:T(8,128)S(1)}, f32[264,512]{1,0:T(8,128)S(1)}, u32[]{:S(2)}, u32[]{:S(2)}) collective-permute-start(f32[264,512]{1,0:T(8,128)S(1)} %get-tuple-element.27), channel_id=1, source_target_pairs={{0,4},{4,0},{1,5},{5,1},{2,6},{6,2},{3,7},{7,3},{8,12},{12,8},{9,1... | collective-permute-start | bytes 1622024 | tf_op jit(solution)/shard_map/ppermute | solution.py:250
  133.3 2.3 %collective-permute-start.24 = (f32[264,512]{1,0:T(8,128)S(1)}, f32[264,512]{1,0:T(8,128)S(1)}, u32[]{:S(2)}, u32[]{:S(2)}) collective-permute-start(f32[264,512]{1,0:T(8,128)S(1)} %get-tuple-element.26), channel_id=1, source_target_pairs={{0,4},{4,0},{1,5},{5,1},{2,6},{6,2},{3,7},{7,3},{8,12},{12,8},{9,1... | collective-permute-start | bytes 1622024 | tf_op jit(solution)/shard_map/ppermute | solution.py:250
  (7 other events, 5.5 us)

commit v18 on v17

--- a/solution.py
+++ b/solution.py
@@ -287,13 +287,14 @@
             seen = [PARTNERS[(s + k) % 4][0] for k in range(step)]
             which = side(x if axis == "x" else z, flip, axis not in seen)
             streams[s] = meet(streams[s], axis, flip, which)
+        marks = [value[:16, :128] for value in streams]
         if step == 0:
-            turned = [send(behind(halves[0], streams[:1]), 0), send(behind(halves[1], streams), 2)]
+            turned = [send(behind(halves[0], marks[:1]), 0), send(behind(halves[1], marks), 2)]
         if step == 1:
-            rows = meet(behind(join(*turned), streams), "y", 1, side(y ^ z, 1, True))
-        if step == 2:
-            rows = meet(behind(rows, streams), "y", 3, side(y ^ z, 3, False))
-
+            rows = behind(join(*turned), [swap(join(*marks))])
+
+    rows = meet(rows, "y", 1, side(y ^ z, 1, True))
+    rows = meet(rows, "y", 3, side(y ^ z, 3, False))
     rows = join(rows, swap(rows))
 
     own, got = [], []

time: 138 us -> 130 us (0.942)
  waiting for transfers between devices: 38.1 us -> 50.3 us
  local copies, waits for them, and re-layouts: 10.2 us -> 2.07 us
  other arithmetic: 14.1 us -> 7.54 us
  starting transfers between devices: 34.1 us -> 31 us
  Pallas kernels: 12.5 us -> 10.3 us
    ppermute x21, waiting for transfers between devices: 34.8 us -> 46 us  [trade(): return lax.ppermute(value, axis, [(i, i ^ flip) for i in range(4)])]
    unnamed x58 -> x4, local copies, waits for them, and re-layouts: 9.74 us -> 1.59 us
    ppermute x21, starting transfers between devices: 20.3 us -> 15.2 us  [trade(): return lax.ppermute(value, axis, [(i, i ^ flip) for i in range(4)])]
    concatenate x18 -> x19, other arithmetic: 6.16 us -> 2 us  [join(): return jnp.concatenate(values, axis=0)]
    ppermute x3 -> x4, starting transfers between devices: 8.2 us -> 11.4 us  [swap(): return lax.ppermute(value, 'c', [(0, 1), (1, 0)])]
    select_n x18 -> x10, other arithmetic: 5.65 us -> 2.76 us  [meet(): jnp.where(which == 0, value, got)]
    ppermute x3 -> x4, waiting for transfers between devices: 1.49 us -> 4.33 us  [swap(): return lax.ppermute(value, 'c', [(0, 1), (1, 0)])]
    pallas_call x4 -> x3, Pallas kernels: 2.28 us -> 0.08 us  [behind(): pl.pallas_call(behind_kernel, out_shape=jax.ShapeDtypeStruct(value.shape,...]
  transfers between devices with their start and end apart: 26 -> 27, of which waited for: 10 -> 10; matrix products, arithmetic and copies ran while one was open for 6% -> 4% of each run, Pallas kernels for 0% -> 0%
where the time goes in v18:
time: 130 us
  waiting for transfers between devices  50.3 us (39%)
  starting transfers between devices  31 us (24%)
  blocking collectives  27 us (21%)
  Pallas kernels  10.3 us (8%)
  other arithmetic  7.54 us (6%)
  local copies, waits for them, and re-layouts  2.07 us (2%)
  between operations  1.81 us (1%)
    ppermute x21, waiting for transfers between devices, trade(): return lax.ppermute(value, axis, [(i, i ^ flip) for i in range(4)])  46 us
    all_to_all x1, blocking collectives, per_device(): pieces = lax.all_to_all(pieces, TOK, 0, 0, tiled=True)  27 us
    ppermute x21, starting transfers between devices, trade(): return lax.ppermute(value, axis, [(i, i ^ flip) for i in range(4)])  15.2 us
    ppermute x4, starting transfers between devices, swap(): return lax.ppermute(value, 'c', [(0, 1), (1, 0)])  11.4 us
    pallas_call x2, Pallas kernels, gram(): pl.pallas_call(lambda *refs: gram_kernel(blocks, *refs), out_shape=(jax.S...  4.8 us
    ppermute x4, waiting for transfers between devices, swap(): return lax.ppermute(value, 'c', [(0, 1), (1, 0)])  4.33 us
    ppermute x2, starting transfers between devices, send(): lax.ppermute(half, ('z', 'y'), [(q * 4 + u, u * 4 + (q ^ u ^ turn)) for q...  4.33 us
    select_n x10, other arithmetic, meet(): jnp.where(which == 0, value, got)  2.76 us
  transfers between devices with their start and end apart: 27, of which 10 were waited for; matrix products, arithmetic and copies ran while one was open for 4% of the time, Pallas kernels for 0%

profile of v18, /device:TPU:1, one launch (start us, length us, event | category | flops | bytes accessed | tf_op | source)
XLA Modules:
  0.0 130.0 jit_solution(18128725859633396662)
XLA Ops:
  0.6 0.8 pad_add_fusion
  1.4 1.6 %copy-done = bf16[512,2048]{1,0:T(8,128)(2,1)S(1)} copy-done((bf16[512,2048]{1,0:T(8,128)(2,1)S(1)}, bf16[512,2048]{1,0:T(8,128)(2,1)}, u32[]{:S(2)}) %copy-start) | copy-done | bytes 2097176
  3.0 0.8 pick.1
  3.9 3.6 %collective-permute-start.2 = (f32[8,256]{1,0:T(8,128)S(1)}, f32[8,256]{1,0:T(8,128)S(1)}, u32[]{:S(2)}, u32[]{:S(2)}) collective-permute-start(f32[8,256]{1,0:T(8,128)S(1)} %get-tuple-element.17.s0), channel_id=1, source_target_pairs={{0,3},{1,2},{2,1},{3,0},{4,7},{5,6},{6,5},{7,4},{8,11},{9,10},{10,... | collective-permute-start | bytes 24584 | tf_op jit(solution)/shard_map/ppermute | solution.py:254
  7.5 0.4 collective-permute-start.1
  7.9 0.3 collective-permute-start
  8.2 0.4 copy.7.gain_ref
  8.6 3.0 %collective-permute-done.1.s2 = f32[8,256]{1,0:T(8,128)S(1)} collective-permute-done((f32[8,256]{1,0:T(8,128)S(1)}, f32[8,256]{1,0:T(8,128)S(1)}, u32[]{:S(2)}, u32[]{:S(2)}) %collective-permute-start.1) | collective-permute-done | bytes 8224 | tf_op jit(solution)/shard_map/ppermute | solution.py:254
  11.5 0.3 norm.1
  11.9 27.0 %all_to_all.5.in_ref = bf16[32,64,256]{2,1,0:T(8,128)(2,1)S(1)} all-to-all(bf16[32,64,256]{2,1,0:T(8,128)(2,1)S(1)} %norm.1), channel_id=1, replica_groups=mesh['z'=4,'x'=4,'c'=2,'y'=4] {'z','x','c'}, dimensions={0} | all-to-all | bytes 2097152 | tf_op jit(solution)/shard_map/all_to_all | solution.py:272
  38.9 1.2 fusion
  40.4 2.1 %pack.1 = (bf16[32,4224]{1,0:T(8,128)(2,1)S(1)}, bf16[32,4224]{1,0:T(8,128)(2,1)S(1)}, bf16[16,4224]{1,0:T(8,128)(2,1)S(1)}, bf16[16,4224]{1,0:T(8,128)(2,1)S(1)...) custom-call(s32[32]{0:T(128)S(1)} %sub.3.first_ref, bf16[32,64,256]{2,1,0:T(8,128)(2,1)S(1)} %all_to_all.5.in_ref), custom_call_target="tpu_custom_call" | custom-call | tf_op jit(solution)/shard_map/pack/pallas_call | solution.py:149
  42.5 0.4 collective-permute-start.3
  42.9 0.4 collective-permute-start.5
  43.3 1.0 collective-permute-start.6
  44.3 0.6 collective-permute-start.7
  44.9 2.4 %collective-permute-done.3 = bf16[16,4224]{1,0:T(8,128)(2,1)S(1)} collective-permute-done((bf16[16,4224]{1,0:T(8,128)(2,1)S(1)}, bf16[16,4224]{1,0:T(8,128)(2,1)S(1)}, u32[]{:S(2)}, u32[]{:S(2)}) %collective-permute-start.3) | collective-permute-done | bytes 135200 | tf_op jit(solution)/shard_map/ppermute | solution.py:254
  47.4 0.5 collective-permute-start.9
  47.9 1.8 %collective-permute-done.7 = bf16[16,4224]{1,0:T(8,128)(2,1)S(1)} collective-permute-done((bf16[16,4224]{1,0:T(8,128)(2,1)S(1)}, bf16[16,4224]{1,0:T(8,128)(2,1)S(1)}, u32[]{:S(2)}, u32[]{:S(2)}) %collective-permute-start.7) | collective-permute-done | bytes 135200 | tf_op jit(solution)/shard_map/ppermute | solution.py:254
  49.9 2.2 %collective-permute-start.10 = (bf16[32,4224]{1,0:T(8,128)(2,1)S(1)}, bf16[32,4224]{1,0:T(8,128)(2,1)S(1)}, u32[]{:S(2)}, u32[]{:S(2)}) collective-permute-start(bf16[32,4224]{1,0:T(8,128)(2,1)S(1)} %pad_maximum_fusion.17), channel_id=1, source_target_pairs={{0,24},{8,16},{16,8},{24,0},{1,25},{9,17},{17,9},{25,1},{2,26},{10... | collective-permute-start | bytes 811016 | tf_op jit(solution)/shard_map/ppermute | solution.py:254
  52.1 1.4 %collective-permute-start.11 = (bf16[32,4224]{1,0:T(8,128)(2,1)S(1)}, bf16[32,4224]{1,0:T(8,128)(2,1)S(1)}, u32[]{:S(2)}, u32[]{:S(2)}) collective-permute-start(bf16[32,4224]{1,0:T(8,128)(2,1)S(1)} %pad_maximum_fusion.18), channel_id=1, source_target_pairs={{0,96},{32,64},{64,32},{96,0},{1,97},{33,65},{65,33},{97,1},{2,98}... | collective-permute-start | bytes 811016 | tf_op jit(solution)/shard_map/ppermute | solution.py:254
  53.6 3.7 %collective-permute-start.8 = (bf16[32,4224]{1,0:T(8,128)(2,1)S(1)}, bf16[32,4224]{1,0:T(8,128)(2,1)S(1)}, u32[]{:S(2)}, u32[]{:S(2)}) collective-permute-start(bf16[32,4224]{1,0:T(8,128)(2,1)S(1)} %behind.4), channel_id=1, source_target_pairs={{0,2},{1,35},{2,64},{3,97},{32,3},{33,34},{34,65},{35,96},{64,0},{... | collective-permute-start | bytes 811016 | tf_op jit(solution)/shard_map/ppermute | solution.py:282
  57.3 0.7 collective-permute-start.4
  58.2 1.5 %collective-permute-done.11 = bf16[32,4224]{1,0:T(8,128)(2,1)S(1)} collective-permute-done((bf16[32,4224]{1,0:T(8,128)(2,1)S(1)}, bf16[32,4224]{1,0:T(8,128)(2,1)S(1)}, u32[]{:S(2)}, u32[]{:S(2)}) %collective-permute-start.11) | collective-permute-done | bytes 270368 | tf_op jit(solution)/shard_map/ppermute | solution.py:254
  60.0 8.4 %collective-permute-start.13 = (bf16[64,128]{1,0:T(8,128)(2,1)S(1)}, bf16[64,128]{1,0:T(8,128)(2,1)S(1)}, u32[]{:S(2)}, u32[]{:S(2)}) collective-permute-start(bf16[64,128]{1,0:T(8,128)(2,1)S(1)} %pad_maximum_fusion.20), channel_id=1, source_target_pairs={{0,4},{4,0},{1,5},{5,1},{2,6},{6,2},{3,7},{7,3},{8,12},{12,8},{9,1... | collective-permute-start | bytes 49160 | tf_op jit(solution)/shard_map/ppermute | solution.py:250
  68.6 0.6 collective-permute-start.17
  69.2 1.0 collective-permute-start.19
  70.4 13.3 %collective-permute-done.17 = bf16[64,4224]{1,0:T(8,128)(2,1)S(1)} collective-permute-done((bf16[64,4224]{1,0:T(8,128)(2,1)S(1)}, bf16[64,4224]{1,0:T(8,128)(2,1)S(1)}, u32[]{:S(2)}, u32[]{:S(2)}) %collective-permute-start.17) | collective-permute-done | bytes 540704 | tf_op jit(solution)/shard_map/ppermute | solution.py:254
  84.0 1.5 %collective-permute-start.18 = (bf16[128,4224]{1,0:T(8,128)(2,1)S(1)}, bf16[128,4224]{1,0:T(8,128)(2,1)S(1)}, u32[]{:S(2)}, u32[]{:S(2)}) collective-permute-start(bf16[128,4224]{1,0:T(8,128)(2,1)S(1)} %pad_maximum_fusion.7), channel_id=1, source_target_pairs={{0,96},{32,64},{64,32},{96,0},{1,97},{33,65},{65,33},{97,1},{2,98}... | collective-permute-start | bytes 3244040 | tf_op jit(solution)/shard_map/ppermute | solution.py:254
  86.6 0.7 collective-permute-start.24
  87.7 22.2 %collective-permute-done.18 = bf16[128,4224]{1,0:T(8,128)(2,1)S(1)} collective-permute-done((bf16[128,4224]{1,0:T(8,128)(2,1)S(1)}, bf16[128,4224]{1,0:T(8,128)(2,1)S(1)}, u32[]{:S(2)}, u32[]{:S(2)}) %collective-permute-start.18) | collective-permute-done | bytes 1081376 | tf_op jit(solution)/shard_map/ppermute | solution.py:254
  109.9 0.4 broadcast_select_fusion.7
  110.3 0.4 broadcast_select_fusion.5
  110.7 0.4 broadcast_select_fusion.3
  111.1 1.7 %collective-permute-done.15 = bf16[128,4224]{1,0:T(8,128)(2,1)S(1)} collective-permute-done((bf16[128,4224]{1,0:T(8,128)(2,1)S(1)}, bf16[128,4224]{1,0:T(8,128)(2,1)S(1)}, u32[]{:S(2)}, u32[]{:S(2)}) %collective-permute-start.15) | collective-permute-done | bytes 1081376 | tf_op jit(solution)/shard_map/ppermute | solution.py:254
  112.9 0.4 broadcast_select_fusion.9
  113.4 2.4 %collective-permute-start.16 = (bf16[256,4224]{1,0:T(8,128)(2,1)S(1)}, bf16[256,4224]{1,0:T(8,128)(2,1)S(1)}, u32[]{:S(2)}, u32[]{:S(2)}) collective-permute-start(bf16[256,4224]{1,0:T(8,128)(2,1)S(1)} %pad_maximum_fusion.1), channel_id=1, source_target_pairs={{0,4},{4,0},{1,5},{5,1},{2,6},{6,2},{3,7},{7,3},{8,12},{12,8},{9,1... | collective-permute-start | bytes 6488072 | tf_op jit(solution)/shard_map/ppermute | solution.py:250
  115.8 0.3 pad_maximum_fusion.2
  116.1 0.4 broadcast_select_fusion.1
  116.5 0.3 pad_maximum_fusion.4
  116.8 2.9 %collective-permute-done.16 = bf16[256,4224]{1,0:T(8,128)(2,1)S(1)} collective-permute-done((bf16[256,4224]{1,0:T(8,128)(2,1)S(1)}, bf16[256,4224]{1,0:T(8,128)(2,1)S(1)}, u32[]{:S(2)}, u32[]{:S(2)}) %collective-permute-start.16) | collective-permute-done | bytes 2162720 | tf_op jit(solution)/shard_map/ppermute | solution.py:250
  119.7 0.6 pad_maximum_fusion.refs_0_
  120.2 2.4 %gram.3 = (f32[264,512]{1,0:T(8,128)S(1)}, f32[264,512]{1,0:T(8,128)S(1)}) custom-call(bf16[512,4224]{1,0:T(8,128)(2,1)S(1)} %pad_maximum_fusion.refs_0_, bf16[256,4224]{1,0:T(8,128)(2,1)S(1)} %get-tuple-element.68.refs_1_, bf16[256,4224]{1,0:T(8,128)(2,1)S(1)} %get-tuple-element.69.refs_2_, bf16[256,4224]{1,0:T(8,128)(2,1)S(1)} %get-tuple-element.70.refs_3_, ...), custom_call_target="tpu_custom_call" | custom-call | flops 2147483648 | bytes 6291456 | tf_op jit(solution)/shard_map/gram/pallas_call | solution.py:206
  122.6 2.4 %gram.2 = (f32[264,512]{1,0:T(8,128)S(1)}, f32[264,512]{1,0:T(8,128)S(1)}) custom-call(bf16[512,4224]{1,0:T(8,128)(2,1)S(1)} %pad_maximum_fusion.refs_0_, bf16[256,4224]{1,0:T(8,128)(2,1)S(1)} %get-tuple-element.68.refs_1_, bf16[256,4224]{1,0:T(8,128)(2,1)S(1)} %get-tuple-element.69.refs_2_, bf16[256,4224]{1,0:T(8,128)(2,1)S(1)} %get-tuple-element.70.refs_3_, ...), custom_call_target="tpu_custom_call" | custom-call | flops 2147483648 | bytes 6291456 | tf_op jit(solution)/shard_map/gram/pallas_call | solution.py:206
  125.0 0.5 collective-permute-start.26
  126.4 0.7 collective-permute-done.26.refs_3_
  127.1 0.8 collective-permute-done.25.refs_2_
  127.8 2.2 %finish.1 = (f32[1,2048]{1,0:T(1,128)}, f32[256,2048]{1,0:T(8,128)}) custom-call(s32[3]{0:T(128)S(1)} %pad_add_fusion.1.info_ref, f32[1]{0:T(128)} %bitcast.4.part_ref, f32[264,512]{1,0:T(8,128)S(1)} %get-tuple-element.24.refs_0_, f32[264,512]{1,0:T(8,128)S(1)} %get-tuple-element.25.refs_1_, f32[264,512]{1,0:T(8,128)S(1)} %collective-permute-done.25.refs_2_, ...), custom_call_target="tpu_custom_call" | custom-call | tf_op jit(solution)/shard_map/finish/pallas_call | solution.py:236
  (75 shorter events, 3.4 us)
Async XLA Ops:
  0.6 7.6 %copy-start.1 = (f32[2048]{0:T(1024)S(1)}, f32[2048]{0:T(1024)}, u32[]{:S(2)}) copy-start(f32[2048]{0:T(1024)} %param.5) | copy-start | bytes 24580
  1.4 1.6 %copy-start = (bf16[512,2048]{1,0:T(8,128)(2,1)S(1)}, bf16[512,2048]{1,0:T(8,128)(2,1)}, u32[]{:S(2)}) copy-start(bf16[512,2048]{1,0:T(8,128)(2,1)} %resid_ref.1) | copy-start | bytes 6291460
  3.9 4.7 %collective-permute-start.2 = (f32[8,256]{1,0:T(8,128)S(1)}, f32[8,256]{1,0:T(8,128)S(1)}, u32[]{:S(2)}, u32[]{:S(2)}) collective-permute-start(f32[8,256]{1,0:T(8,128)S(1)} %get-tuple-element.17.s0), channel_id=1, source_target_pairs={{0,3},{1,2},{2,1},{3,0},{4,7},{5,6},{6,5},{7,4},{8,11},{9,10},{10,... | collective-permute-start | bytes 24584 | tf_op jit(solution)/shard_map/ppermute | solution.py:254
  7.5 4.0 %collective-permute-start.1 = (f32[8,256]{1,0:T(8,128)S(1)}, f32[8,256]{1,0:T(8,128)S(1)}, u32[]{:S(2)}, u32[]{:S(2)}) collective-permute-start(f32[8,256]{1,0:T(8,128)S(1)} %get-tuple-element.17.s0), channel_id=1, source_target_pairs={{0,2},{1,3},{2,0},{3,1},{4,6},{5,7},{6,4},{7,5},{8,10},{9,11},{10,... | collective-permute-start | bytes 24584 | tf_op jit(solution)/shard_map/ppermute | solution.py:254
  7.9 3.7 %collective-permute-start = (f32[8,256]{1,0:T(8,128)S(1)}, f32[8,256]{1,0:T(8,128)S(1)}, u32[]{:S(2)}, u32[]{:S(2)}) collective-permute-start(f32[8,256]{1,0:T(8,128)S(1)} %get-tuple-element.17.s0), channel_id=1, source_target_pairs={{0,1},{1,0},{2,3},{3,2},{4,5},{5,4},{6,7},{7,6},{8,9},{9,8},{10,11... | collective-permute-start | bytes 24584 | tf_op jit(solution)/shard_map/ppermute | solution.py:254
  42.5 4.9 %collective-permute-start.3 = (bf16[16,4224]{1,0:T(8,128)(2,1)S(1)}, bf16[16,4224]{1,0:T(8,128)(2,1)S(1)}, u32[]{:S(2)}, u32[]{:S(2)}) collective-permute-start(bf16[16,4224]{1,0:T(8,128)(2,1)S(1)} %get-tuple-element.19), channel_id=1, source_target_pairs={{0,8},{8,0},{16,24},{24,16},{1,9},{9,1},{17,25},{25,17},{2,10},{10... | collective-permute-start | bytes 405512 | tf_op jit(solution)/shard_map/ppermute | solution.py:254
  42.9 6.9 %collective-permute-start.5 = (bf16[16,4224]{1,0:T(8,128)(2,1)S(1)}, bf16[16,4224]{1,0:T(8,128)(2,1)S(1)}, u32[]{:S(2)}, u32[]{:S(2)}) collective-permute-start(bf16[16,4224]{1,0:T(8,128)(2,1)S(1)} %get-tuple-element.21), channel_id=1, source_target_pairs={{0,32},{32,0},{64,96},{96,64},{1,33},{33,1},{65,97},{97,65},{2,34}... | collective-permute-start | bytes 405512 | tf_op jit(solution)/shard_map/ppermute | solution.py:254
  43.3 6.4 %collective-permute-start.6 = (bf16[16,4224]{1,0:T(8,128)(2,1)S(1)}, bf16[16,4224]{1,0:T(8,128)(2,1)S(1)}, u32[]{:S(2)}, u32[]{:S(2)}) collective-permute-start(bf16[16,4224]{1,0:T(8,128)(2,1)S(1)} %get-tuple-element.22), channel_id=1, source_target_pairs={{0,24},{8,16},{16,8},{24,0},{1,25},{9,17},{17,9},{25,1},{2,26},{10... | collective-permute-start | bytes 405512 | tf_op jit(solution)/shard_map/ppermute | solution.py:254
  44.3 5.4 %collective-permute-start.7 = (bf16[16,4224]{1,0:T(8,128)(2,1)S(1)}, bf16[16,4224]{1,0:T(8,128)(2,1)S(1)}, u32[]{:S(2)}, u32[]{:S(2)}) collective-permute-start(bf16[16,4224]{1,0:T(8,128)(2,1)S(1)} %get-tuple-element.23), channel_id=1, source_target_pairs={{0,96},{32,64},{64,32},{96,0},{1,97},{33,65},{65,33},{97,1},{2,98}... | collective-permute-start | bytes 405512 | tf_op jit(solution)/shard_map/ppermute | solution.py:254
  47.4 9.9 %collective-permute-start.9 = (bf16[32,4224]{1,0:T(8,128)(2,1)S(1)}, bf16[32,4224]{1,0:T(8,128)(2,1)S(1)}, u32[]{:S(2)}, u32[]{:S(2)}) collective-permute-start(bf16[32,4224]{1,0:T(8,128)(2,1)S(1)} %pad_maximum_fusion.16), channel_id=1, source_target_pairs={{0,32},{32,0},{64,96},{96,64},{1,33},{33,1},{65,97},{97,65},{2,34}... | collective-permute-start | bytes 811016 | tf_op jit(solution)/shard_map/ppermute | solution.py:254
  49.9 8.1 %collective-permute-start.10 = (bf16[32,4224]{1,0:T(8,128)(2,1)S(1)}, bf16[32,4224]{1,0:T(8,128)(2,1)S(1)}, u32[]{:S(2)}, u32[]{:S(2)}) collective-permute-start(bf16[32,4224]{1,0:T(8,128)(2,1)S(1)} %pad_maximum_fusion.17), channel_id=1, source_target_pairs={{0,24},{8,16},{16,8},{24,0},{1,25},{9,17},{17,9},{25,1},{2,26},{10... | collective-permute-start | bytes 811016 | tf_op jit(solution)/shard_map/ppermute | solution.py:254
  52.1 7.5 %collective-permute-start.11 = (bf16[32,4224]{1,0:T(8,128)(2,1)S(1)}, bf16[32,4224]{1,0:T(8,128)(2,1)S(1)}, u32[]{:S(2)}, u32[]{:S(2)}) collective-permute-start(bf16[32,4224]{1,0:T(8,128)(2,1)S(1)} %pad_maximum_fusion.18), channel_id=1, source_target_pairs={{0,96},{32,64},{64,32},{96,0},{1,97},{33,65},{65,33},{97,1},{2,98}... | collective-permute-start | bytes 811016 | tf_op jit(solution)/shard_map/ppermute | solution.py:254
  53.5 6.3 %collective-permute-start.12 = (bf16[32,4224]{1,0:T(8,128)(2,1)S(1)}, bf16[32,4224]{1,0:T(8,128)(2,1)S(1)}, u32[]{:S(2)}, u32[]{:S(2)}) collective-permute-start(bf16[32,4224]{1,0:T(8,128)(2,1)S(1)} %pad_maximum_fusion.19), channel_id=1, source_target_pairs={{0,8},{8,0},{16,24},{24,16},{1,9},{9,1},{17,25},{25,17},{2,10},{10... | collective-permute-start | bytes 811016 | tf_op jit(solution)/shard_map/ppermute | solution.py:254
  53.6 16.5 %collective-permute-start.8 = (bf16[32,4224]{1,0:T(8,128)(2,1)S(1)}, bf16[32,4224]{1,0:T(8,128)(2,1)S(1)}, u32[]{:S(2)}, u32[]{:S(2)}) collective-permute-start(bf16[32,4224]{1,0:T(8,128)(2,1)S(1)} %behind.4), channel_id=1, source_target_pairs={{0,2},{1,35},{2,64},{3,97},{32,3},{33,34},{34,65},{35,96},{64,0},{... | collective-permute-start | bytes 811016 | tf_op jit(solution)/shard_map/ppermute | solution.py:282
  57.3 12.9 %collective-permute-start.4 = (bf16[32,4224]{1,0:T(8,128)(2,1)S(1)}, bf16[32,4224]{1,0:T(8,128)(2,1)S(1)}, u32[]{:S(2)}, u32[]{:S(2)}) collective-permute-start(bf16[32,4224]{1,0:T(8,128)(2,1)S(1)} %behind.3), channel_id=1, source_target_pairs={{0,0},{1,33},{2,66},{3,99},{32,1},{33,32},{34,67},{35,98},{64,2},{... | collective-permute-start | bytes 811016 | tf_op jit(solution)/shard_map/ppermute | solution.py:282
  60.0 10.3 %collective-permute-start.13 = (bf16[64,128]{1,0:T(8,128)(2,1)S(1)}, bf16[64,128]{1,0:T(8,128)(2,1)S(1)}, u32[]{:S(2)}, u32[]{:S(2)}) collective-permute-start(bf16[64,128]{1,0:T(8,128)(2,1)S(1)} %pad_maximum_fusion.20), channel_id=1, source_target_pairs={{0,4},{4,0},{1,5},{5,1},{2,6},{6,2},{3,7},{7,3},{8,12},{12,8},{9,1... | collective-permute-start | bytes 49160 | tf_op jit(solution)/shard_map/ppermute | solution.py:250
  68.6 15.2 %collective-permute-start.17 = (bf16[64,4224]{1,0:T(8,128)(2,1)S(1)}, bf16[64,4224]{1,0:T(8,128)(2,1)S(1)}, u32[]{:S(2)}, u32[]{:S(2)}) collective-permute-start(bf16[64,4224]{1,0:T(8,128)(2,1)S(1)} %pad_maximum_fusion.12), channel_id=1, source_target_pairs={{0,24},{8,16},{16,8},{24,0},{1,25},{9,17},{17,9},{25,1},{2,26},{10... | collective-permute-start | bytes 1622024 | tf_op jit(solution)/shard_map/ppermute | solution.py:254
  69.2 16.3 %collective-permute-start.19 = (bf16[64,4224]{1,0:T(8,128)(2,1)S(1)}, bf16[64,4224]{1,0:T(8,128)(2,1)S(1)}, u32[]{:S(2)}, u32[]{:S(2)}) collective-permute-start(bf16[64,4224]{1,0:T(8,128)(2,1)S(1)} %pad_maximum_fusion.13), channel_id=1, source_target_pairs={{0,96},{32,64},{64,32},{96,0},{1,97},{33,65},{65,33},{97,1},{2,98}... | collective-permute-start | bytes 1622024 | tf_op jit(solution)/shard_map/ppermute | solution.py:254
  70.1 15.7 %collective-permute-start.21 = (bf16[64,4224]{1,0:T(8,128)(2,1)S(1)}, bf16[64,4224]{1,0:T(8,128)(2,1)S(1)}, u32[]{:S(2)}, u32[]{:S(2)}) collective-permute-start(bf16[64,4224]{1,0:T(8,128)(2,1)S(1)} %pad_maximum_fusion.14), channel_id=1, source_target_pairs={{0,8},{8,0},{16,24},{24,16},{1,9},{9,1},{17,25},{25,17},{2,10},{10... | collective-permute-start | bytes 1622024 | tf_op jit(solution)/shard_map/ppermute | solution.py:254
  70.1 16.1 %collective-permute-start.23 = (bf16[64,4224]{1,0:T(8,128)(2,1)S(1)}, bf16[64,4224]{1,0:T(8,128)(2,1)S(1)}, u32[]{:S(2)}, u32[]{:S(2)}) collective-permute-start(bf16[64,4224]{1,0:T(8,128)(2,1)S(1)} %pad_maximum_fusion.15), channel_id=1, source_target_pairs={{0,32},{32,0},{64,96},{96,64},{1,33},{33,1},{65,97},{97,65},{2,34}... | collective-permute-start | bytes 1622024 | tf_op jit(solution)/shard_map/ppermute | solution.py:254
  70.3 16.9 %collective-permute-start.14 = (bf16[64,4224]{1,0:T(8,128)(2,1)S(1)}, bf16[64,4224]{1,0:T(8,128)(2,1)S(1)}, u32[]{:S(2)}, u32[]{:S(2)}) collective-permute-start(bf16[64,4224]{1,0:T(8,128)(2,1)S(1)} %behind.5), channel_id=1, source_target_pairs={{0,1},{1,0},{2,3},{3,2},{4,5},{5,4},{6,7},{7,6},{8,9},{9,8},{10,11... | collective-permute-start | bytes 1622024 | tf_op jit(solution)/shard_map/ppermute | solution.py:254
  84.0 25.9 %collective-permute-start.18 = (bf16[128,4224]{1,0:T(8,128)(2,1)S(1)}, bf16[128,4224]{1,0:T(8,128)(2,1)S(1)}, u32[]{:S(2)}, u32[]{:S(2)}) collective-permute-start(bf16[128,4224]{1,0:T(8,128)(2,1)S(1)} %pad_maximum_fusion.7), channel_id=1, source_target_pairs={{0,96},{32,64},{64,32},{96,0},{1,97},{33,65},{65,33},{97,1},{2,98}... | collective-permute-start | bytes 3244040 | tf_op jit(solution)/shard_map/ppermute | solution.py:254
  85.8 24.5 %collective-permute-start.20 = (bf16[128,4224]{1,0:T(8,128)(2,1)S(1)}, bf16[128,4224]{1,0:T(8,128)(2,1)S(1)}, u32[]{:S(2)}, u32[]{:S(2)}) collective-permute-start(bf16[128,4224]{1,0:T(8,128)(2,1)S(1)} %pad_maximum_fusion.8), channel_id=1, source_target_pairs={{0,8},{8,0},{16,24},{24,16},{1,9},{9,1},{17,25},{25,17},{2,10},{10... | collective-permute-start | bytes 3244040 | tf_op jit(solution)/shard_map/ppermute | solution.py:254
  86.2 24.5 %collective-permute-start.22 = (bf16[128,4224]{1,0:T(8,128)(2,1)S(1)}, bf16[128,4224]{1,0:T(8,128)(2,1)S(1)}, u32[]{:S(2)}, u32[]{:S(2)}) collective-permute-start(bf16[128,4224]{1,0:T(8,128)(2,1)S(1)} %pad_maximum_fusion.9), channel_id=1, source_target_pairs={{0,32},{32,0},{64,96},{96,64},{1,33},{33,1},{65,97},{97,65},{2,34}... | collective-permute-start | bytes 3244040 | tf_op jit(solution)/shard_map/ppermute | solution.py:254
  86.6 29.5 %collective-permute-start.24 = (bf16[128,4224]{1,0:T(8,128)(2,1)S(1)}, bf16[128,4224]{1,0:T(8,128)(2,1)S(1)}, u32[]{:S(2)}, u32[]{:S(2)}) collective-permute-start(bf16[128,4224]{1,0:T(8,128)(2,1)S(1)} %pad_maximum_fusion.10), channel_id=1, source_target_pairs={{0,24},{8,16},{16,8},{24,0},{1,25},{9,17},{17,9},{25,1},{2,26},{10... | collective-permute-start | bytes 3244040 | tf_op jit(solution)/shard_map/ppermute | solution.py:254
  87.4 25.4 %collective-permute-start.15 = (bf16[128,4224]{1,0:T(8,128)(2,1)S(1)}, bf16[128,4224]{1,0:T(8,128)(2,1)S(1)}, u32[]{:S(2)}, u32[]{:S(2)}) collective-permute-start(bf16[128,4224]{1,0:T(8,128)(2,1)S(1)} %pad_maximum_fusion.6), channel_id=1, source_target_pairs={{0,3},{1,2},{2,1},{3,0},{4,7},{5,6},{6,5},{7,4},{8,11},{9,10},{10,... | collective-permute-start | bytes 3244040 | tf_op jit(solution)/shard_map/ppermute | solution.py:254
  113.4 6.3 %collective-permute-start.16 = (bf16[256,4224]{1,0:T(8,128)(2,1)S(1)}, bf16[256,4224]{1,0:T(8,128)(2,1)S(1)}, u32[]{:S(2)}, u32[]{:S(2)}) collective-permute-start(bf16[256,4224]{1,0:T(8,128)(2,1)S(1)} %pad_maximum_fusion.1), channel_id=1, source_target_pairs={{0,4},{4,0},{1,5},{5,1},{2,6},{6,2},{3,7},{7,3},{8,12},{12,8},{9,1... | collective-permute-start | bytes 6488072 | tf_op jit(solution)/shard_map/ppermute | solution.py:250
  125.0 2.0 %collective-permute-start.26 = (f32[264,512]{1,0:T(8,128)S(1)}, f32[264,512]{1,0:T(8,128)S(1)}, u32[]{:S(2)}, u32[]{:S(2)}) collective-permute-start(f32[264,512]{1,0:T(8,128)S(1)} %get-tuple-element.27), channel_id=1, source_target_pairs={{0,4},{4,0},{1,5},{5,1},{2,6},{6,2},{3,7},{7,3},{8,12},{12,8},{9,1... | collective-permute-start | bytes 1622024 | tf_op jit(solution)/shard_map/ppermute | solution.py:250
  125.5 2.3 %collective-permute-start.25 = (f32[264,512]{1,0:T(8,128)S(1)}, f32[264,512]{1,0:T(8,128)S(1)}, u32[]{:S(2)}, u32[]{:S(2)}) collective-permute-start(f32[264,512]{1,0:T(8,128)S(1)} %get-tuple-element.26), channel_id=1, source_target_pairs={{0,4},{4,0},{1,5},{5,1},{2,6},{6,2},{3,7},{7,3},{8,12},{12,8},{9,1... | collective-permute-start | bytes 1622024 | tf_op jit(solution)/shard_map/ppermute | solution.py:250

commit v19 on v17

--- a/solution.py
+++ b/solution.py
@@ -167,7 +167,7 @@
     return pl.pallas_call(
         behind_kernel,
         out_shape=jax.ShapeDtypeStruct(value.shape, value.dtype),
-        in_specs=[vmem] * (1 + len(after)),
+        in_specs=[vmem] + [pl.BlockSpec(memory_space=pl.ANY)] * len(after),
         out_specs=vmem,
         compiler_params=params(4),
         name="behind",
@@ -290,10 +290,11 @@
         if step == 0:
             turned = [send(behind(halves[0], streams[:1]), 0), send(behind(halves[1], streams), 2)]
         if step == 1:
-            rows = meet(behind(join(*turned), streams), "y", 1, side(y ^ z, 1, True))
-        if step == 2:
-            rows = meet(behind(rows, streams), "y", 3, side(y ^ z, 3, False))
-
+            rows = behind(join(*turned), streams)
+
+    q = y ^ z
+    rows = meet(rows, "y", 1, side(q, 1, True))
+    rows = meet(rows, "y", 3, side(q, 3, False))
     rows = join(rows, swap(rows))
 
     own, got = [], []

time: 138 us -> 124 us (0.90)
  other arithmetic: 14.1 us -> 8.5 us
  local copies, waits for them, and re-layouts: 10.2 us -> 4.92 us
  waiting for transfers between devices: 38.1 us -> 32.9 us
  starting transfers between devices: 34.1 us -> 37.7 us
  Pallas kernels: 12.5 us -> 10.3 us
    ppermute x21, waiting for transfers between devices: 34.8 us -> 27.4 us  [trade(): return lax.ppermute(value, axis, [(i, i ^ flip) for i in range(4)])]
    ppermute x21, starting transfers between devices: 20.3 us -> 27.6 us  [trade(): return lax.ppermute(value, axis, [(i, i ^ flip) for i in range(4)])]
    unnamed x58 -> x24, local copies, waits for them, and re-layouts: 9.74 us -> 4.46 us
    concatenate x18, other arithmetic: 6.16 us -> 1.97 us  [join(): return jnp.concatenate(values, axis=0)]
    ppermute x2, starting transfers between devices: 5.6 us -> 2.59 us  [send(): lax.ppermute(half, ('z', 'y'), [(q * 4 + u, u * 4 + (q ^ u ^ turn)) for q...]
    pallas_call x4 -> x3, Pallas kernels: 2.28 us -> 0.08 us  [behind(): pl.pallas_call(behind_kernel, out_shape=jax.ShapeDtypeStruct(value.shape,...]
    ppermute x3, waiting for transfers between devices: 1.49 us -> 3.2 us  [swap(): return lax.ppermute(value, 'c', [(0, 1), (1, 0)])]
    select_n x18, other arithmetic: 5.65 us -> 4.26 us  [meet(): jnp.where(which == 0, value, got)]
  transfers between devices with their start and end apart: 26 -> 26, of which waited for: 10 -> 13; matrix products, arithmetic and copies ran while one was open for 6% -> 5% of each run, Pallas kernels for 0% -> 0%
where the time goes in v19:
time: 124 us; the launch traced here: 123 us
  starting transfers between devices  37.7 us (30%)
  waiting for transfers between devices  32.9 us (27%)
  blocking collectives  27.3 us (22%)
  Pallas kernels  10.3 us (8%)
  other arithmetic  8.5 us (7%)
  local copies, waits for them, and re-layouts  4.92 us (4%)
  between operations  1.79 us (1%)
    ppermute x21, starting transfers between devices, trade(): return lax.ppermute(value, axis, [(i, i ^ flip) for i in range(4)])  27.6 us
    ppermute x21, waiting for transfers between devices, trade(): return lax.ppermute(value, axis, [(i, i ^ flip) for i in range(4)])  27.4 us
    all_to_all x1, blocking collectives, per_device(): pieces = lax.all_to_all(pieces, TOK, 0, 0, tiled=True)  27.3 us
    ppermute x3, starting transfers between devices, swap(): return lax.ppermute(value, 'c', [(0, 1), (1, 0)])  7.46 us
    pallas_call x2, Pallas kernels, gram(): pl.pallas_call(lambda *refs: gram_kernel(blocks, *refs), out_shape=(jax.S...  4.8 us
    unnamed x24, local copies, waits for them, and re-layouts  4.46 us
    select_n x18, other arithmetic, meet(): jnp.where(which == 0, value, got)  4.26 us
    ppermute x3, waiting for transfers between devices, swap(): return lax.ppermute(value, 'c', [(0, 1), (1, 0)])  3.2 us
  transfers between devices with their start and end apart: 26, of which 13 were waited for; matrix products, arithmetic and copies ran while one was open for 5% of the time, Pallas kernels for 0%

profile of v19, /device:TPU:1, one launch (start us, length us, event | category | flops | bytes accessed | tf_op | source)
XLA Modules:
  0.0 123.5 jit_solution(12653997314362411747)
XLA Ops:
  0.6 0.8 pad_add_fusion
  1.4 1.6 %copy-done = bf16[512,2048]{1,0:T(8,128)(2,1)S(1)} copy-done((bf16[512,2048]{1,0:T(8,128)(2,1)S(1)}, bf16[512,2048]{1,0:T(8,128)(2,1)}, u32[]{:S(2)}) %copy-start) | copy-done | bytes 2097176
  3.0 0.8 pick.1
  3.9 2.2 %collective-permute-start = (f32[8,256]{1,0:T(8,128)S(1)}, f32[8,256]{1,0:T(8,128)S(1)}, u32[]{:S(2)}, u32[]{:S(2)}) collective-permute-start(f32[8,256]{1,0:T(8,128)S(1)} %get-tuple-element.17.s0), channel_id=1, source_target_pairs={{0,1},{1,0},{2,3},{3,2},{4,5},{5,4},{6,7},{7,6},{8,9},{9,8},{10,11... | collective-permute-start | bytes 24584 | tf_op jit(solution)/shard_map/ppermute | solution.py:254
  6.1 2.6 %collective-permute-start.1 = (f32[8,256]{1,0:T(8,128)S(1)}, f32[8,256]{1,0:T(8,128)S(1)}, u32[]{:S(2)}, u32[]{:S(2)}) collective-permute-start(f32[8,256]{1,0:T(8,128)S(1)} %get-tuple-element.17.s0), channel_id=1, source_target_pairs={{0,2},{1,3},{2,0},{3,1},{4,6},{5,7},{6,4},{7,5},{8,10},{9,11},{10,... | collective-permute-start | bytes 24584 | tf_op jit(solution)/shard_map/ppermute | solution.py:254
  9.1 1.0 collective-permute-done.1.s2
  10.1 2.3 %collective-permute-done.2.s3 = f32[8,256]{1,0:T(8,128)S(1)} collective-permute-done((f32[8,256]{1,0:T(8,128)S(1)}, f32[8,256]{1,0:T(8,128)S(1)}, u32[]{:S(2)}, u32[]{:S(2)}) %collective-permute-start.2) | collective-permute-done | bytes 8224 | tf_op jit(solution)/shard_map/ppermute | solution.py:254
  12.8 27.3 %all_to_all.5.in_ref = bf16[32,64,256]{2,1,0:T(8,128)(2,1)S(1)} all-to-all(bf16[32,64,256]{2,1,0:T(8,128)(2,1)S(1)} %norm.1), channel_id=1, replica_groups=mesh['z'=4,'x'=4,'c'=2,'y'=4] {'z','x','c'}, dimensions={0} | all-to-all | bytes 2097152 | tf_op jit(solution)/shard_map/all_to_all | solution.py:272
  40.0 1.2 %fusion = (s32[32]{0:T(128)S(1)}, s32[]{:T(128)}) fusion(bf16[32,64,256]{2,1,0:T(8,128)(2,1)S(1)} %all_to_all.5.in_ref), kind=kLoop, calls=%fused_computation.58 | loop fusion | flops 32735 | bytes 16516 | tf_op jit(solution)/shard_map/reduce_sum | solution.py:274
  41.5 2.1 %pack.1 = (bf16[32,4224]{1,0:T(8,128)(2,1)S(1)}, bf16[32,4224]{1,0:T(8,128)(2,1)S(1)}, bf16[16,4224]{1,0:T(8,128)(2,1)S(1)}, bf16[16,4224]{1,0:T(8,128)(2,1)S(1)...) custom-call(s32[32]{0:T(128)S(1)} %sub.3.first_ref, bf16[32,64,256]{2,1,0:T(8,128)(2,1)S(1)} %all_to_all.5.in_ref), custom_call_target="tpu_custom_call" | custom-call | tf_op jit(solution)/shard_map/pack/pallas_call | solution.py:149
  43.6 0.4 collective-permute-start.3
  44.1 0.4 collective-permute-start.5
  44.4 1.0 collective-permute-start.6
  45.4 0.6 collective-permute-start.7
  46.1 2.4 %collective-permute-done.3 = bf16[16,4224]{1,0:T(8,128)(2,1)S(1)} collective-permute-done((bf16[16,4224]{1,0:T(8,128)(2,1)S(1)}, bf16[16,4224]{1,0:T(8,128)(2,1)S(1)}, u32[]{:S(2)}, u32[]{:S(2)}) %collective-permute-start.3) | collective-permute-done | bytes 135200 | tf_op jit(solution)/shard_map/ppermute | solution.py:254
  48.7 1.2 collective-permute-start.9
  49.9 1.2 collective-permute-start.10
  51.2 1.0 collective-permute-start.11
  52.2 0.4 collective-permute-start.12
  52.7 1.9 %collective-permute-start.8 = (bf16[32,4224]{1,0:T(8,128)(2,1)S(1)}, bf16[32,4224]{1,0:T(8,128)(2,1)S(1)}, u32[]{:S(2)}, u32[]{:S(2)}) collective-permute-start(bf16[32,4224]{1,0:T(8,128)(2,1)S(1)} %behind.4), channel_id=1, source_target_pairs={{0,2},{1,35},{2,64},{3,97},{32,3},{33,34},{34,65},{35,96},{64,0},{... | collective-permute-start | bytes 811016 | tf_op jit(solution)/shard_map/ppermute | solution.py:282
  54.6 0.6 collective-permute-done.9
  55.3 0.7 collective-permute-start.4
  56.1 0.6 copy-done.7
  56.7 1.3 %collective-permute-done.10 = bf16[32,4224]{1,0:T(8,128)(2,1)S(1)} collective-permute-done((bf16[32,4224]{1,0:T(8,128)(2,1)S(1)}, bf16[32,4224]{1,0:T(8,128)(2,1)S(1)}, u32[]{:S(2)}, u32[]{:S(2)}) %collective-permute-start.10) | collective-permute-done | bytes 270368 | tf_op jit(solution)/shard_map/ppermute | solution.py:254
  58.2 0.6 collective-permute-done.11
  59.1 0.5 copy-done.1
  59.7 2.4 %collective-permute-done.8 = bf16[32,4224]{1,0:T(8,128)(2,1)S(1)} collective-permute-done((bf16[32,4224]{1,0:T(8,128)(2,1)S(1)}, bf16[32,4224]{1,0:T(8,128)(2,1)S(1)}, u32[]{:S(2)}, u32[]{:S(2)}) %collective-permute-start.8) | collective-permute-done | bytes 270368 | tf_op jit(solution)/shard_map/ppermute | solution.py:282
  62.2 3.2 %collective-permute-start.13 = (bf16[64,4224]{1,0:T(8,128)(2,1)S(1)}, bf16[64,4224]{1,0:T(8,128)(2,1)}, u32[]{:S(2)}, u32[]{:S(2)}) collective-permute-start(bf16[64,4224]{1,0:T(8,128)(2,1)S(1)} %behind.5), channel_id=1, source_target_pairs={{0,1},{1,0},{2,3},{3,2},{4,5},{5,4},{6,7},{7,6},{8,9},{9,8},{10,11... | collective-permute-start | bytes 1622024 | tf_op jit(solution)/shard_map/ppermute | solution.py:254
  65.3 2.6 %collective-permute-start.16 = (bf16[64,4224]{1,0:T(8,128)(2,1)S(1)}, bf16[64,4224]{1,0:T(8,128)(2,1)S(1)}, u32[]{:S(2)}, u32[]{:S(2)}) collective-permute-start(bf16[64,4224]{1,0:T(8,128)(2,1)S(1)} %pad_maximum_fusion.12.refs_0_), channel_id=1, source_target_pairs={{0,24},{8,16},{16,8},{24,0},{1,25},{9,17},{17,9},{25,1},{2,26},{10... | collective-permute-start | bytes 1622024 | tf_op jit(solution)/shard_map/ppermute | solution.py:254
  67.9 1.5 %collective-permute-start.18 = (bf16[64,4224]{1,0:T(8,128)(2,1)S(1)}, bf16[64,4224]{1,0:T(8,128)(2,1)S(1)}, u32[]{:S(2)}, u32[]{:S(2)}) collective-permute-start(bf16[64,4224]{1,0:T(8,128)(2,1)S(1)} %pad_maximum_fusion.13.refs_1_), channel_id=1, source_target_pairs={{0,96},{32,64},{64,32},{96,0},{1,97},{33,65},{65,33},{97,1},{2,98}... | collective-permute-start | bytes 1622024 | tf_op jit(solution)/shard_map/ppermute | solution.py:254
  69.4 0.7 collective-permute-start.20
  70.2 4.1 %collective-permute-done.13 = bf16[64,4224]{1,0:T(8,128)(2,1)} collective-permute-done((bf16[64,4224]{1,0:T(8,128)(2,1)S(1)}, bf16[64,4224]{1,0:T(8,128)(2,1)}, u32[]{:S(2)}, u32[]{:S(2)}) %collective-permute-start.13) | collective-permute-done | bytes 540704 | tf_op jit(solution)/shard_map/ppermute | solution.py:254
  74.3 1.1 broadcast_select_fusion.19
  75.6 6.7 %collective-permute-start.14 = (bf16[128,4224]{1,0:T(8,128)(2,1)S(1)}, bf16[128,4224]{1,0:T(8,128)(2,1)S(1)}, u32[]{:S(2)}, u32[]{:S(2)}) collective-permute-start(bf16[128,4224]{1,0:T(8,128)(2,1)S(1)} %pad_maximum_fusion.6), channel_id=1, source_target_pairs={{0,3},{1,2},{2,1},{3,0},{4,7},{5,6},{6,5},{7,4},{8,11},{9,10},{10,... | collective-permute-start | bytes 3244040 | tf_op jit(solution)/shard_map/ppermute | solution.py:254
  82.6 0.7 copy-done.4
  83.9 0.8 copy-done.2
  85.3 1.5 %collective-permute-start.23 = (bf16[128,4224]{1,0:T(8,128)(2,1)S(1)}, bf16[128,4224]{1,0:T(8,128)(2,1)S(1)}, u32[]{:S(2)}, u32[]{:S(2)}) collective-permute-start(bf16[128,4224]{1,0:T(8,128)(2,1)S(1)} %pad_maximum_fusion.10), channel_id=1, source_target_pairs={{0,24},{8,16},{16,8},{24,0},{1,25},{9,17},{17,9},{25,1},{2,26},{10... | collective-permute-start | bytes 3244040 | tf_op jit(solution)/shard_map/ppermute | solution.py:254
  86.9 14.9 %collective-permute-done.14 = bf16[128,4224]{1,0:T(8,128)(2,1)S(1)} collective-permute-done((bf16[128,4224]{1,0:T(8,128)(2,1)S(1)}, bf16[128,4224]{1,0:T(8,128)(2,1)S(1)}, u32[]{:S(2)}, u32[]{:S(2)}) %collective-permute-start.14) | collective-permute-done | bytes 1081376 | tf_op jit(solution)/shard_map/ppermute | solution.py:254
  102.3 5.5 %collective-permute-start.15 = (bf16[256,4224]{1,0:T(8,128)(2,1)S(1)}, bf16[256,4224]{1,0:T(8,128)(2,1)S(1)}, u32[]{:S(2)}, u32[]{:S(2)}) collective-permute-start(bf16[256,4224]{1,0:T(8,128)(2,1)S(1)} %pad_maximum_fusion.1), channel_id=1, source_target_pairs={{0,4},{4,0},{1,5},{5,1},{2,6},{6,2},{3,7},{7,3},{8,12},{12,8},{9,1... | collective-permute-start | bytes 6488072 | tf_op jit(solution)/shard_map/ppermute | solution.py:250
  108.4 0.4 broadcast_select_fusion.5
  110.0 1.7 %collective-permute-done.15 = bf16[256,4224]{1,0:T(8,128)(2,1)S(1)} collective-permute-done((bf16[256,4224]{1,0:T(8,128)(2,1)S(1)}, bf16[256,4224]{1,0:T(8,128)(2,1)S(1)}, u32[]{:S(2)}, u32[]{:S(2)}) %collective-permute-start.15) | collective-permute-done | bytes 2162720 | tf_op jit(solution)/shard_map/ppermute | solution.py:250
  111.7 0.6 pad_maximum_fusion.refs_0_
  112.3 2.4 %gram.2 = (f32[264,512]{1,0:T(8,128)S(1)}, f32[264,512]{1,0:T(8,128)S(1)}) custom-call(bf16[512,4224]{1,0:T(8,128)(2,1)S(1)} %pad_maximum_fusion.refs_0_, bf16[256,4224]{1,0:T(8,128)(2,1)S(1)} %pad_maximum_fusion.2.refs_1_, bf16[256,4224]{1,0:T(8,128)(2,1)S(1)} %pad_maximum_fusion.3.refs_2_, bf16[256,4224]{1,0:T(8,128)(2,1)S(1)} %pad_maximum_fusion.4.refs_3_, ...), custom_call_target="tpu_custom_call" | custom-call | flops 2147483648 | bytes 6291456 | tf_op jit(solution)/shard_map/gram/pallas_call | solution.py:206
  114.7 2.4 %gram.3 = (f32[264,512]{1,0:T(8,128)S(1)}, f32[264,512]{1,0:T(8,128)S(1)}) custom-call(bf16[512,4224]{1,0:T(8,128)(2,1)S(1)} %pad_maximum_fusion.refs_0_, bf16[256,4224]{1,0:T(8,128)(2,1)S(1)} %pad_maximum_fusion.2.refs_1_, bf16[256,4224]{1,0:T(8,128)(2,1)S(1)} %pad_maximum_fusion.3.refs_2_, bf16[256,4224]{1,0:T(8,128)(2,1)S(1)} %pad_maximum_fusion.4.refs_3_, ...), custom_call_target="tpu_custom_call" | custom-call | flops 2147483648 | bytes 6291456 | tf_op jit(solution)/shard_map/gram/pallas_call | solution.py:206
  117.1 1.8 %collective-permute-start.24 = (f32[264,512]{1,0:T(8,128)S(1)}, f32[264,512]{1,0:T(8,128)S(1)}, u32[]{:S(2)}, u32[]{:S(2)}) collective-permute-start(f32[264,512]{1,0:T(8,128)S(1)} %get-tuple-element.26), channel_id=1, source_target_pairs={{0,4},{4,0},{1,5},{5,1},{2,6},{6,2},{3,7},{7,3},{8,12},{12,8},{9,1... | collective-permute-start | bytes 1622024 | tf_op jit(solution)/shard_map/ppermute | solution.py:250
  119.8 0.7 collective-permute-done.24.refs_2_
  120.5 0.8 collective-permute-done.25.refs_3_
  121.3 2.2 %finish.1 = (f32[1,2048]{1,0:T(1,128)}, f32[256,2048]{1,0:T(8,128)}) custom-call(s32[3]{0:T(128)S(1)} %pad_add_fusion.1.info_ref, f32[1]{0:T(128)} %bitcast.4.part_ref, f32[264,512]{1,0:T(8,128)S(1)} %get-tuple-element.24.refs_0_, f32[264,512]{1,0:T(8,128)S(1)} %get-tuple-element.25.refs_1_, f32[264,512]{1,0:T(8,128)S(1)} %collective-permute-done.24.refs_2_, ...), custom_call_target="tpu_custom_call" | custom-call | tf_op jit(solution)/shard_map/finish/pallas_call | solution.py:236
  (84 shorter events, 6.0 us)
Async XLA Ops:
  0.6 8.1 %copy-start.11 = (f32[2048]{0:T(1024)S(1)}, f32[2048]{0:T(1024)}, u32[]{:S(2)}) copy-start(f32[2048]{0:T(1024)} %param.5) | copy-start | bytes 24580
  1.4 1.6 %copy-start = (bf16[512,2048]{1,0:T(8,128)(2,1)S(1)}, bf16[512,2048]{1,0:T(8,128)(2,1)}, u32[]{:S(2)}) copy-start(bf16[512,2048]{1,0:T(8,128)(2,1)} %resid_ref.1) | copy-start | bytes 6291460
  3.9 5.2 %collective-permute-start = (f32[8,256]{1,0:T(8,128)S(1)}, f32[8,256]{1,0:T(8,128)S(1)}, u32[]{:S(2)}, u32[]{:S(2)}) collective-permute-start(f32[8,256]{1,0:T(8,128)S(1)} %get-tuple-element.17.s0), channel_id=1, source_target_pairs={{0,1},{1,0},{2,3},{3,2},{4,5},{5,4},{6,7},{7,6},{8,9},{9,8},{10,11... | collective-permute-start | bytes 24584 | tf_op jit(solution)/shard_map/ppermute | solution.py:254
  6.1 4.0 %collective-permute-start.1 = (f32[8,256]{1,0:T(8,128)S(1)}, f32[8,256]{1,0:T(8,128)S(1)}, u32[]{:S(2)}, u32[]{:S(2)}) collective-permute-start(f32[8,256]{1,0:T(8,128)S(1)} %get-tuple-element.17.s0), channel_id=1, source_target_pairs={{0,2},{1,3},{2,0},{3,1},{4,6},{5,7},{6,4},{7,5},{8,10},{9,11},{10,... | collective-permute-start | bytes 24584 | tf_op jit(solution)/shard_map/ppermute | solution.py:254
  8.7 3.7 %collective-permute-start.2 = (f32[8,256]{1,0:T(8,128)S(1)}, f32[8,256]{1,0:T(8,128)S(1)}, u32[]{:S(2)}, u32[]{:S(2)}) collective-permute-start(f32[8,256]{1,0:T(8,128)S(1)} %get-tuple-element.17.s0), channel_id=1, source_target_pairs={{0,3},{1,2},{2,1},{3,0},{4,7},{5,6},{6,5},{7,4},{8,11},{9,10},{10,... | collective-permute-start | bytes 24584 | tf_op jit(solution)/shard_map/ppermute | solution.py:254
  43.6 4.9 %collective-permute-start.3 = (bf16[16,4224]{1,0:T(8,128)(2,1)S(1)}, bf16[16,4224]{1,0:T(8,128)(2,1)S(1)}, u32[]{:S(2)}, u32[]{:S(2)}) collective-permute-start(bf16[16,4224]{1,0:T(8,128)(2,1)S(1)} %get-tuple-element.19), channel_id=1, source_target_pairs={{0,8},{8,0},{16,24},{24,16},{1,9},{9,1},{17,25},{25,17},{2,10},{10... | collective-permute-start | bytes 405512 | tf_op jit(solution)/shard_map/ppermute | solution.py:254
  44.1 4.5 %collective-permute-start.5 = (bf16[16,4224]{1,0:T(8,128)(2,1)S(1)}, bf16[16,4224]{1,0:T(8,128)(2,1)S(1)}, u32[]{:S(2)}, u32[]{:S(2)}) collective-permute-start(bf16[16,4224]{1,0:T(8,128)(2,1)S(1)} %get-tuple-element.21), channel_id=1, source_target_pairs={{0,32},{32,0},{64,96},{96,64},{1,33},{33,1},{65,97},{97,65},{2,34}... | collective-permute-start | bytes 405512 | tf_op jit(solution)/shard_map/ppermute | solution.py:254
  44.4 6.6 %collective-permute-start.6 = (bf16[16,4224]{1,0:T(8,128)(2,1)S(1)}, bf16[16,4224]{1,0:T(8,128)(2,1)S(1)}, u32[]{:S(2)}, u32[]{:S(2)}) collective-permute-start(bf16[16,4224]{1,0:T(8,128)(2,1)S(1)} %get-tuple-element.22), channel_id=1, source_target_pairs={{0,24},{8,16},{16,8},{24,0},{1,25},{9,17},{17,9},{25,1},{2,26},{10... | collective-permute-start | bytes 405512 | tf_op jit(solution)/shard_map/ppermute | solution.py:254
  45.4 5.7 %collective-permute-start.7 = (bf16[16,4224]{1,0:T(8,128)(2,1)S(1)}, bf16[16,4224]{1,0:T(8,128)(2,1)S(1)}, u32[]{:S(2)}, u32[]{:S(2)}) collective-permute-start(bf16[16,4224]{1,0:T(8,128)(2,1)S(1)} %get-tuple-element.23), channel_id=1, source_target_pairs={{0,96},{32,64},{64,32},{96,0},{1,97},{33,65},{65,33},{97,1},{2,98}... | collective-permute-start | bytes 405512 | tf_op jit(solution)/shard_map/ppermute | solution.py:254
  48.7 6.6 %collective-permute-start.9 = (bf16[32,4224]{1,0:T(8,128)(2,1)S(1)}, bf16[32,4224]{1,0:T(8,128)(2,1)S(1)}, u32[]{:S(2)}, u32[]{:S(2)}) collective-permute-start(bf16[32,4224]{1,0:T(8,128)(2,1)S(1)} %get-tuple-element.68.refs_0_), channel_id=1, source_target_pairs={{0,32},{32,0},{64,96},{96,64},{1,33},{33,1},{65,97},{97,65},{2,34}... | collective-permute-start | bytes 811016 | tf_op jit(solution)/shard_map/ppermute | solution.py:254
  49.9 8.2 %collective-permute-start.10 = (bf16[32,4224]{1,0:T(8,128)(2,1)S(1)}, bf16[32,4224]{1,0:T(8,128)(2,1)S(1)}, u32[]{:S(2)}, u32[]{:S(2)}) collective-permute-start(bf16[32,4224]{1,0:T(8,128)(2,1)S(1)} %get-tuple-element.69.refs_1_), channel_id=1, source_target_pairs={{0,24},{8,16},{16,8},{24,0},{1,25},{9,17},{17,9},{25,1},{2,26},{10... | collective-permute-start | bytes 811016 | tf_op jit(solution)/shard_map/ppermute | solution.py:254
  51.2 7.6 %collective-permute-start.11 = (bf16[32,4224]{1,0:T(8,128)(2,1)S(1)}, bf16[32,4224]{1,0:T(8,128)(2,1)S(1)}, u32[]{:S(2)}, u32[]{:S(2)}) collective-permute-start(bf16[32,4224]{1,0:T(8,128)(2,1)S(1)} %get-tuple-element.70.refs_2_), channel_id=1, source_target_pairs={{0,96},{32,64},{64,32},{96,0},{1,97},{33,65},{65,33},{97,1},{2,98}... | collective-permute-start | bytes 811016 | tf_op jit(solution)/shard_map/ppermute | solution.py:254
  52.2 6.8 %collective-permute-start.12 = (bf16[32,4224]{1,0:T(8,128)(2,1)S(1)}, bf16[32,4224]{1,0:T(8,128)(2,1)S(1)}, u32[]{:S(2)}, u32[]{:S(2)}) collective-permute-start(bf16[32,4224]{1,0:T(8,128)(2,1)S(1)} %get-tuple-element.71.refs_3_), channel_id=1, source_target_pairs={{0,8},{8,0},{16,24},{24,16},{1,9},{9,1},{17,25},{25,17},{2,10},{10... | collective-permute-start | bytes 811016 | tf_op jit(solution)/shard_map/ppermute | solution.py:254
  52.7 9.4 %collective-permute-start.8 = (bf16[32,4224]{1,0:T(8,128)(2,1)S(1)}, bf16[32,4224]{1,0:T(8,128)(2,1)S(1)}, u32[]{:S(2)}, u32[]{:S(2)}) collective-permute-start(bf16[32,4224]{1,0:T(8,128)(2,1)S(1)} %behind.4), channel_id=1, source_target_pairs={{0,2},{1,35},{2,64},{3,97},{32,3},{33,34},{34,65},{35,96},{64,0},{... | collective-permute-start | bytes 811016 | tf_op jit(solution)/shard_map/ppermute | solution.py:282
  55.3 6.8 %collective-permute-start.4 = (bf16[32,4224]{1,0:T(8,128)(2,1)S(1)}, bf16[32,4224]{1,0:T(8,128)(2,1)S(1)}, u32[]{:S(2)}, u32[]{:S(2)}) collective-permute-start(bf16[32,4224]{1,0:T(8,128)(2,1)S(1)} %behind.3), channel_id=1, source_target_pairs={{0,0},{1,33},{2,66},{3,99},{32,1},{33,32},{34,67},{35,98},{64,2},{... | collective-permute-start | bytes 811016 | tf_op jit(solution)/shard_map/ppermute | solution.py:282
  56.0 0.7 copy-start.7
  56.0 2.1 %copy-start.9 = (bf16[32,4224]{1,0:T(8,128)(2,1)}, bf16[32,4224]{1,0:T(8,128)(2,1)S(1)}, u32[]{:S(2)}) copy-start(bf16[32,4224]{1,0:T(8,128)(2,1)S(1)} %get-tuple-element.59) | copy-start | bytes 811012
  58.2 0.7 copy-start.3
  58.2 0.8 copy-start.5
  59.0 0.7 copy-start.1
  62.2 12.1 %collective-permute-start.13 = (bf16[64,4224]{1,0:T(8,128)(2,1)S(1)}, bf16[64,4224]{1,0:T(8,128)(2,1)}, u32[]{:S(2)}, u32[]{:S(2)}) collective-permute-start(bf16[64,4224]{1,0:T(8,128)(2,1)S(1)} %behind.5), channel_id=1, source_target_pairs={{0,1},{1,0},{2,3},{3,2},{4,5},{5,4},{6,7},{7,6},{8,9},{9,8},{10,11... | collective-permute-start | bytes 1622024 | tf_op jit(solution)/shard_map/ppermute | solution.py:254
  65.3 16.9 %collective-permute-start.16 = (bf16[64,4224]{1,0:T(8,128)(2,1)S(1)}, bf16[64,4224]{1,0:T(8,128)(2,1)S(1)}, u32[]{:S(2)}, u32[]{:S(2)}) collective-permute-start(bf16[64,4224]{1,0:T(8,128)(2,1)S(1)} %pad_maximum_fusion.12.refs_0_), channel_id=1, source_target_pairs={{0,24},{8,16},{16,8},{24,0},{1,25},{9,17},{17,9},{25,1},{2,26},{10... | collective-permute-start | bytes 1622024 | tf_op jit(solution)/shard_map/ppermute | solution.py:254
  67.9 14.7 %collective-permute-start.18 = (bf16[64,4224]{1,0:T(8,128)(2,1)S(1)}, bf16[64,4224]{1,0:T(8,128)(2,1)S(1)}, u32[]{:S(2)}, u32[]{:S(2)}) collective-permute-start(bf16[64,4224]{1,0:T(8,128)(2,1)S(1)} %pad_maximum_fusion.13.refs_1_), channel_id=1, source_target_pairs={{0,96},{32,64},{64,32},{96,0},{1,97},{33,65},{65,33},{97,1},{2,98}... | collective-permute-start | bytes 1622024 | tf_op jit(solution)/shard_map/ppermute | solution.py:254
  69.4 14.4 %collective-permute-start.20 = (bf16[64,4224]{1,0:T(8,128)(2,1)S(1)}, bf16[64,4224]{1,0:T(8,128)(2,1)S(1)}, u32[]{:S(2)}, u32[]{:S(2)}) collective-permute-start(bf16[64,4224]{1,0:T(8,128)(2,1)S(1)} %pad_maximum_fusion.14.refs_2_), channel_id=1, source_target_pairs={{0,8},{8,0},{16,24},{24,16},{1,9},{9,1},{17,25},{25,17},{2,10},{10... | collective-permute-start | bytes 1622024 | tf_op jit(solution)/shard_map/ppermute | solution.py:254
  70.2 14.9 %collective-permute-start.22 = (bf16[64,4224]{1,0:T(8,128)(2,1)S(1)}, bf16[64,4224]{1,0:T(8,128)(2,1)S(1)}, u32[]{:S(2)}, u32[]{:S(2)}) collective-permute-start(bf16[64,4224]{1,0:T(8,128)(2,1)S(1)} %pad_maximum_fusion.15.refs_3_), channel_id=1, source_target_pairs={{0,32},{32,0},{64,96},{96,64},{1,33},{33,1},{65,97},{97,65},{2,34}... | collective-permute-start | bytes 1622024 | tf_op jit(solution)/shard_map/ppermute | solution.py:254
  75.4 6.8 %copy-start.8 = (bf16[32,4224]{1,0:T(8,128)(2,1)S(1)}, bf16[32,4224]{1,0:T(8,128)(2,1)}, u32[]{:S(2)}) copy-start(bf16[32,4224]{1,0:T(8,128)(2,1)} %copy-done.7) | copy-start | bytes 811012
  75.5 6.8 %copy-start.10 = (bf16[32,4224]{1,0:T(8,128)(2,1)S(1)}, bf16[32,4224]{1,0:T(8,128)(2,1)}, u32[]{:S(2)}) copy-start(bf16[32,4224]{1,0:T(8,128)(2,1)} %copy-done.9) | copy-start | bytes 811012
  75.6 26.2 %collective-permute-start.14 = (bf16[128,4224]{1,0:T(8,128)(2,1)S(1)}, bf16[128,4224]{1,0:T(8,128)(2,1)S(1)}, u32[]{:S(2)}, u32[]{:S(2)}) collective-permute-start(bf16[128,4224]{1,0:T(8,128)(2,1)S(1)} %pad_maximum_fusion.6), channel_id=1, source_target_pairs={{0,3},{1,2},{2,1},{3,0},{4,7},{5,6},{6,5},{7,4},{8,11},{9,10},{10,... | collective-permute-start | bytes 3244040 | tf_op jit(solution)/shard_map/ppermute | solution.py:254
  82.4 1.0 copy-start.4
  82.4 1.0 copy-start.6
  82.5 25.3 %collective-permute-start.17 = (bf16[128,4224]{1,0:T(8,128)(2,1)S(1)}, bf16[128,4224]{1,0:T(8,128)(2,1)S(1)}, u32[]{:S(2)}, u32[]{:S(2)}) collective-permute-start(bf16[128,4224]{1,0:T(8,128)(2,1)S(1)} %pad_maximum_fusion.7), channel_id=1, source_target_pairs={{0,96},{32,64},{64,32},{96,0},{1,97},{33,65},{65,33},{97,1},{2,98}... | collective-permute-start | bytes 3244040 | tf_op jit(solution)/shard_map/ppermute | solution.py:254
  83.7 1.0 copy-start.2
  83.8 24.6 %collective-permute-start.19 = (bf16[128,4224]{1,0:T(8,128)(2,1)S(1)}, bf16[128,4224]{1,0:T(8,128)(2,1)S(1)}, u32[]{:S(2)}, u32[]{:S(2)}) collective-permute-start(bf16[128,4224]{1,0:T(8,128)(2,1)S(1)} %pad_maximum_fusion.8), channel_id=1, source_target_pairs={{0,8},{8,0},{16,24},{24,16},{1,9},{9,1},{17,25},{25,17},{2,10},{10... | collective-permute-start | bytes 3244040 | tf_op jit(solution)/shard_map/ppermute | solution.py:254
  84.9 23.9 %collective-permute-start.21 = (bf16[128,4224]{1,0:T(8,128)(2,1)S(1)}, bf16[128,4224]{1,0:T(8,128)(2,1)S(1)}, u32[]{:S(2)}, u32[]{:S(2)}) collective-permute-start(bf16[128,4224]{1,0:T(8,128)(2,1)S(1)} %pad_maximum_fusion.9), channel_id=1, source_target_pairs={{0,32},{32,0},{64,96},{96,64},{1,33},{33,1},{65,97},{97,65},{2,34}... | collective-permute-start | bytes 3244040 | tf_op jit(solution)/shard_map/ppermute | solution.py:254
  85.3 24.1 %collective-permute-start.23 = (bf16[128,4224]{1,0:T(8,128)(2,1)S(1)}, bf16[128,4224]{1,0:T(8,128)(2,1)S(1)}, u32[]{:S(2)}, u32[]{:S(2)}) collective-permute-start(bf16[128,4224]{1,0:T(8,128)(2,1)S(1)} %pad_maximum_fusion.10), channel_id=1, source_target_pairs={{0,24},{8,16},{16,8},{24,0},{1,25},{9,17},{17,9},{25,1},{2,26},{10... | collective-permute-start | bytes 3244040 | tf_op jit(solution)/shard_map/ppermute | solution.py:254
  102.3 9.4 %collective-permute-start.15 = (bf16[256,4224]{1,0:T(8,128)(2,1)S(1)}, bf16[256,4224]{1,0:T(8,128)(2,1)S(1)}, u32[]{:S(2)}, u32[]{:S(2)}) collective-permute-start(bf16[256,4224]{1,0:T(8,128)(2,1)S(1)} %pad_maximum_fusion.1), channel_id=1, source_target_pairs={{0,4},{4,0},{1,5},{5,1},{2,6},{6,2},{3,7},{7,3},{8,12},{12,8},{9,1... | collective-permute-start | bytes 6488072 | tf_op jit(solution)/shard_map/ppermute | solution.py:250
  117.1 3.4 %collective-permute-start.24 = (f32[264,512]{1,0:T(8,128)S(1)}, f32[264,512]{1,0:T(8,128)S(1)}, u32[]{:S(2)}, u32[]{:S(2)}) collective-permute-start(f32[264,512]{1,0:T(8,128)S(1)} %get-tuple-element.26), channel_id=1, source_target_pairs={{0,4},{4,0},{1,5},{5,1},{2,6},{6,2},{3,7},{7,3},{8,12},{12,8},{9,1... | collective-permute-start | bytes 1622024 | tf_op jit(solution)/shard_map/ppermute | solution.py:250
  118.9 2.3 %collective-permute-start.25 = (f32[264,512]{1,0:T(8,128)S(1)}, f32[264,512]{1,0:T(8,128)S(1)}, u32[]{:S(2)}, u32[]{:S(2)}) collective-permute-start(f32[264,512]{1,0:T(8,128)S(1)} %get-tuple-element.27), channel_id=1, source_target_pairs={{0,4},{4,0},{1,5},{5,1},{2,6},{6,2},{3,7},{7,3},{8,12},{12,8},{9,1... | collective-permute-start | bytes 1622024 | tf_op jit(solution)/shard_map/ppermute | solution.py:250

commit v20 on v17

--- a/solution.py
+++ b/solution.py
@@ -167,7 +167,7 @@
     return pl.pallas_call(
         behind_kernel,
         out_shape=jax.ShapeDtypeStruct(value.shape, value.dtype),
-        in_specs=[vmem] * (1 + len(after)),
+        in_specs=[vmem] + [pl.BlockSpec(memory_space=pl.ANY)] * len(after),
         out_specs=vmem,
         compiler_params=params(4),
         name="behind",
@@ -219,16 +219,31 @@
 
 def finish_kernel(info_ref, part_ref, *refs):
     own, got, (mean_ref, out_ref) = refs[:2], refs[2:4], refs[4:]
-    core, row_first, col_first = info_ref[0], info_ref[1], info_ref[2]
+    core, row_block, col_block = info_ref[0], info_ref[1], info_ref[2]
     part = part_ref[0]
-    row = row_first + lax.broadcasted_iota(jnp.int32, (256, 256), 0)
-    col = col_first + lax.broadcasted_iota(jnp.int32, (256, 256), 1)
+
+    def put(ref, inside, block):
+        at = pl.multiple_of(block * 256, 256)
+        mean_ref[:, pl.ds(at, 256)] = ref[256:264, inside][:1] * part
+
+        @pl.when(col_block + block > row_block)
+        def _():
+            out_ref[:, pl.ds(at, 256)] = ref[:256, inside] * part
+
+        @pl.when(col_block + block == row_block)
+        def _():
+            row = lax.broadcasted_iota(jnp.int32, (256, 256), 0)
+            col = lax.broadcasted_iota(jnp.int32, (256, 256), 1)
+            out_ref[:, pl.ds(at, 256)] = jnp.where(row <= col, ref[:256, inside] * part, 0.0)
+
+        @pl.when(col_block + block < row_block)
+        def _():
+            out_ref[:, pl.ds(at, 256)] = jnp.zeros((256, 256), f32)
+
     for x in range(4):
         inside = slice(x % 2 * 256, (x % 2 + 1) * 256)
-        for ref, which in ((own[x // 2], core), (got[x // 2], 1 - core)):
-            at = pl.multiple_of(x * 512 + which * 256, 256)
-            out_ref[:, pl.ds(at, 256)] = jnp.where(row <= col + at, ref[:256, inside] * part, 0.0)
-            mean_ref[:, pl.ds(at, 256)] = ref[256:264, inside][:1] * part
+        put(own[x // 2], inside, x * 2 + core)
+        put(got[x // 2], inside, x * 2 + 1 - core)
 
 
 def finish(info, part, own, got):
@@ -288,11 +303,13 @@
             which = side(x if axis == "x" else z, flip, axis not in seen)
             streams[s] = meet(streams[s], axis, flip, which)
         if step == 0:
-            turned = [send(behind(halves[0], streams[:1]), 0), send(behind(halves[1], streams), 2)]
+            low_t = send(behind(halves[0], streams[:1]), 0)
+        if step == 0:
+            high_t = send(behind(halves[1], streams), 2)
         if step == 1:
-            rows = meet(behind(join(*turned), streams), "y", 1, side(y ^ z, 1, True))
+            rows = meet(behind(join(low_t, high_t), streams), "y", 1, side(y ^ z, 1, True))
         if step == 2:
-            rows = meet(behind(rows, streams), "y", 3, side(y ^ z, 3, False))
+            rows = meet(behind(rows, streams[:1]), "y", 3, side(y ^ z, 3, False))
 
     rows = join(rows, swap(rows))
 
@@ -301,7 +318,7 @@
         kept, given = gram(blocks, rows, streams)
         own.append(kept)
         got.append(swap(given))
-    info = jnp.stack([c, (z * 8 + x * 2 + c) * 256, y * WIDTH]).astype(jnp.int32)
+    info = jnp.stack([c, z * 8 + x * 2 + c, y * 8]).astype(jnp.int32)
     mean, gram_factor = finish(info, part[None], own, got)
     return (mean[0], gram_factor)
 

time: 138 us -> 122 us (0.88)
  local copies, waits for them, and re-layouts: 10.2 us -> 2.05 us
  other arithmetic: 14.1 us -> 7.32 us
  starting transfers between devices: 34.1 us -> 36.7 us
  Pallas kernels: 12.5 us -> 10.3 us
  waiting for transfers between devices: 38.1 us -> 36.7 us
    ppermute x21, starting transfers between devices: 20.3 us -> 29.2 us  [trade(): return lax.ppermute(value, axis, [(i, i ^ flip) for i in range(4)])]
    unnamed x58 -> x4, local copies, waits for them, and re-layouts: 9.74 us -> 1.59 us
    concatenate x18, other arithmetic: 6.16 us -> 2.01 us  [join(): return jnp.concatenate(values, axis=0)]
    ppermute x3, starting transfers between devices: 8.2 us -> 4.86 us  [swap(): return lax.ppermute(value, 'c', [(0, 1), (1, 0)])]
    ppermute x2, starting transfers between devices: 5.6 us -> 2.59 us  [send(): lax.ppermute(half, ('z', 'y'), [(q * 4 + u, u * 4 + (q ^ u ^ turn)) for q...]
    select_n x18, other arithmetic: 5.65 us -> 3.07 us  [meet(): jnp.where(which == 0, value, got)]
    pallas_call x4, Pallas kernels: 2.28 us -> 0.15 us  [behind(): pl.pallas_call(behind_kernel, out_shape=jax.ShapeDtypeStruct(value.shape,...]
    ppermute x2, waiting for transfers between devices: 1.86 us -> 0.01 us  [send(): lax.ppermute(half, ('z', 'y'), [(q * 4 + u, u * 4 + (q ^ u ^ turn)) for q...]
  transfers between devices with their start and end apart: 26 -> 26, of which waited for: 10 -> 12; matrix products, arithmetic and copies ran while one was open for 6% -> 4% of each run, Pallas kernels for 0% -> 0%
where the time goes in v20:
time: 122 us
  starting transfers between devices  36.7 us (30%)
  waiting for transfers between devices  36.7 us (30%)
  blocking collectives  27.3 us (22%)
  Pallas kernels  10.3 us (8%)
  other arithmetic  7.32 us (6%)
  local copies, waits for them, and re-layouts  2.05 us (2%)
  between operations  1.67 us (1%)
    ppermute x21, waiting for transfers between devices, trade(): return lax.ppermute(value, axis, [(i, i ^ flip) for i in range(4)])  33.5 us
    ppermute x21, starting transfers between devices, trade(): return lax.ppermute(value, axis, [(i, i ^ flip) for i in range(4)])  29.2 us
    all_to_all x1, blocking collectives, per_device(): pieces = lax.all_to_all(pieces, TOK, 0, 0, tiled=True)  27.3 us
    ppermute x3, starting transfers between devices, swap(): return lax.ppermute(value, 'c', [(0, 1), (1, 0)])  4.86 us
    pallas_call x2, Pallas kernels, gram(): pl.pallas_call(lambda *refs: gram_kernel(blocks, *refs), out_shape=(jax.S...  4.8 us
    ppermute x3, waiting for transfers between devices, swap(): return lax.ppermute(value, 'c', [(0, 1), (1, 0)])  3.21 us
    select_n x18, other arithmetic, meet(): jnp.where(which == 0, value, got)  3.07 us
    ppermute x2, starting transfers between devices, send(): lax.ppermute(half, ('z', 'y'), [(q * 4 + u, u * 4 + (q ^ u ^ turn)) for q...  2.59 us
  transfers between devices with their start and end apart: 26, of which 12 were waited for; matrix products, arithmetic and copies ran while one was open for 4% of the time, Pallas kernels for 0%

profile of v20, /device:TPU:1, one launch (start us, length us, event | category | flops | bytes accessed | tf_op | source)
XLA Modules:
  0.0 122.0 jit_solution(6201522067448259195)
XLA Ops:
  0.6 0.8 pad_add_fusion
  1.4 1.6 %copy-done = bf16[512,2048]{1,0:T(8,128)(2,1)S(1)} copy-done((bf16[512,2048]{1,0:T(8,128)(2,1)S(1)}, bf16[512,2048]{1,0:T(8,128)(2,1)}, u32[]{:S(2)}) %copy-start) | copy-done | bytes 2097176
  3.0 0.8 pick.1
  3.9 2.2 %collective-permute-start = (f32[8,256]{1,0:T(8,128)S(1)}, f32[8,256]{1,0:T(8,128)S(1)}, u32[]{:S(2)}, u32[]{:S(2)}) collective-permute-start(f32[8,256]{1,0:T(8,128)S(1)} %get-tuple-element.17.s0), channel_id=1, source_target_pairs={{0,1},{1,0},{2,3},{3,2},{4,5},{5,4},{6,7},{7,6},{8,9},{9,8},{10,11... | collective-permute-start | bytes 24584 | tf_op jit(solution)/shard_map/ppermute | solution.py:269
  6.1 2.6 %collective-permute-start.1 = (f32[8,256]{1,0:T(8,128)S(1)}, f32[8,256]{1,0:T(8,128)S(1)}, u32[]{:S(2)}, u32[]{:S(2)}) collective-permute-start(f32[8,256]{1,0:T(8,128)S(1)} %get-tuple-element.17.s0), channel_id=1, source_target_pairs={{0,2},{1,3},{2,0},{3,1},{4,6},{5,7},{6,4},{7,5},{8,10},{9,11},{10,... | collective-permute-start | bytes 24584 | tf_op jit(solution)/shard_map/ppermute | solution.py:269
  8.7 0.4 copy.7.gain_ref
  9.1 1.0 collective-permute-done.1.s2
  10.1 2.3 %collective-permute-done.2.s3 = f32[8,256]{1,0:T(8,128)S(1)} collective-permute-done((f32[8,256]{1,0:T(8,128)S(1)}, f32[8,256]{1,0:T(8,128)S(1)}, u32[]{:S(2)}, u32[]{:S(2)}) %collective-permute-start.2) | collective-permute-done | bytes 8224 | tf_op jit(solution)/shard_map/ppermute | solution.py:269
  12.4 0.3 norm.1
  12.8 27.3 %all_to_all.5.in_ref = bf16[32,64,256]{2,1,0:T(8,128)(2,1)S(1)} all-to-all(bf16[32,64,256]{2,1,0:T(8,128)(2,1)S(1)} %norm.1), channel_id=1, replica_groups=mesh['z'=4,'x'=4,'c'=2,'y'=4] {'z','x','c'}, dimensions={0} | all-to-all | bytes 2097152 | tf_op jit(solution)/shard_map/all_to_all | solution.py:287
  40.0 1.2 %fusion = (s32[32]{0:T(128)S(1)}, s32[]{:T(128)}) fusion(bf16[32,64,256]{2,1,0:T(8,128)(2,1)S(1)} %all_to_all.5.in_ref), kind=kLoop, calls=%fused_computation.58 | loop fusion | flops 32735 | bytes 16516 | tf_op jit(solution)/shard_map/reduce_sum | solution.py:289
  41.5 2.1 %pack.1 = (bf16[32,4224]{1,0:T(8,128)(2,1)S(1)}, bf16[32,4224]{1,0:T(8,128)(2,1)S(1)}, bf16[16,4224]{1,0:T(8,128)(2,1)S(1)}, bf16[16,4224]{1,0:T(8,128)(2,1)S(1)...) custom-call(s32[32]{0:T(128)S(1)} %sub.3.first_ref, bf16[32,64,256]{2,1,0:T(8,128)(2,1)S(1)} %all_to_all.5.in_ref), custom_call_target="tpu_custom_call" | custom-call | tf_op jit(solution)/shard_map/pack/pallas_call | solution.py:149
  43.6 0.4 collective-permute-start.3
  44.0 0.4 collective-permute-start.5
  44.4 1.0 collective-permute-start.6
  45.4 0.6 collective-permute-start.7
  46.1 2.4 %collective-permute-done.3 = bf16[16,4224]{1,0:T(8,128)(2,1)S(1)} collective-permute-done((bf16[16,4224]{1,0:T(8,128)(2,1)S(1)}, bf16[16,4224]{1,0:T(8,128)(2,1)S(1)}, u32[]{:S(2)}, u32[]{:S(2)}) %collective-permute-start.3) | collective-permute-done | bytes 135200 | tf_op jit(solution)/shard_map/ppermute | solution.py:269
  48.7 1.2 collective-permute-start.9
  49.9 1.2 collective-permute-start.10
  51.2 1.0 collective-permute-start.11
  52.2 0.4 collective-permute-start.12
  52.6 1.9 %collective-permute-start.8 = (bf16[32,4224]{1,0:T(8,128)(2,1)S(1)}, bf16[32,4224]{1,0:T(8,128)(2,1)S(1)}, u32[]{:S(2)}, u32[]{:S(2)}) collective-permute-start(bf16[32,4224]{1,0:T(8,128)(2,1)S(1)} %behind.5), channel_id=1, source_target_pairs={{0,2},{1,35},{2,64},{3,97},{32,3},{33,34},{34,65},{35,96},{64,0},{... | collective-permute-start | bytes 811016 | tf_op jit(solution)/shard_map/ppermute | solution.py:297
  54.6 0.6 collective-permute-done.9
  55.2 0.7 collective-permute-start.4
  56.1 2.0 %collective-permute-done.10 = bf16[32,4224]{1,0:T(8,128)(2,1)S(1)} collective-permute-done((bf16[32,4224]{1,0:T(8,128)(2,1)S(1)}, bf16[32,4224]{1,0:T(8,128)(2,1)S(1)}, u32[]{:S(2)}, u32[]{:S(2)}) %collective-permute-start.10) | collective-permute-done | bytes 270368 | tf_op jit(solution)/shard_map/ppermute | solution.py:269
  58.1 1.4 %collective-permute-start.14 = (bf16[64,4224]{1,0:T(8,128)(2,1)S(1)}, bf16[64,4224]{1,0:T(8,128)(2,1)S(1)}, u32[]{:S(2)}, u32[]{:S(2)}) collective-permute-start(bf16[64,4224]{1,0:T(8,128)(2,1)S(1)} %pad_maximum_fusion.12.refs_0_), channel_id=1, source_target_pairs={{0,24},{8,16},{16,8},{24,0},{1,25},{9,17},{17,9},{25,1},{2,26},{10... | collective-permute-start | bytes 1622024 | tf_op jit(solution)/shard_map/ppermute | solution.py:269
  59.6 3.7 %collective-permute-start.18 = (bf16[64,4224]{1,0:T(8,128)(2,1)S(1)}, bf16[64,4224]{1,0:T(8,128)(2,1)S(1)}, u32[]{:S(2)}, u32[]{:S(2)}) collective-permute-start(bf16[64,4224]{1,0:T(8,128)(2,1)S(1)} %pad_maximum_fusion.13.refs_1_), channel_id=1, source_target_pairs={{0,96},{32,64},{64,32},{96,0},{1,97},{33,65},{65,33},{97,1},{2,98}... | collective-permute-start | bytes 1622024 | tf_op jit(solution)/shard_map/ppermute | solution.py:269
  63.5 2.7 %collective-permute-start.20 = (bf16[64,4224]{1,0:T(8,128)(2,1)S(1)}, bf16[64,4224]{1,0:T(8,128)(2,1)S(1)}, u32[]{:S(2)}, u32[]{:S(2)}) collective-permute-start(bf16[64,4224]{1,0:T(8,128)(2,1)S(1)} %pad_maximum_fusion.14.refs_2_), channel_id=1, source_target_pairs={{0,8},{8,0},{16,24},{24,16},{1,9},{9,1},{17,25},{25,17},{2,10},{10... | collective-permute-start | bytes 1622024 | tf_op jit(solution)/shard_map/ppermute | solution.py:269
  66.6 4.5 %collective-permute-done.14 = bf16[64,4224]{1,0:T(8,128)(2,1)S(1)} collective-permute-done((bf16[64,4224]{1,0:T(8,128)(2,1)S(1)}, bf16[64,4224]{1,0:T(8,128)(2,1)S(1)}, u32[]{:S(2)}, u32[]{:S(2)}) %collective-permute-start.14) | collective-permute-done | bytes 540704 | tf_op jit(solution)/shard_map/ppermute | solution.py:269
  71.4 3.7 %collective-permute-start.17 = (bf16[128,4224]{1,0:T(8,128)(2,1)S(1)}, bf16[128,4224]{1,0:T(8,128)(2,1)S(1)}, u32[]{:S(2)}, u32[]{:S(2)}) collective-permute-start(bf16[128,4224]{1,0:T(8,128)(2,1)S(1)} %pad_maximum_fusion.7.refs_0_), channel_id=1, source_target_pairs={{0,96},{32,64},{64,32},{96,0},{1,97},{33,65},{65,33},{97,1},{2,98}... | collective-permute-start | bytes 3244040 | tf_op jit(solution)/shard_map/ppermute | solution.py:269
  75.1 1.7 %collective-permute-done.13 = bf16[64,4224]{1,0:T(8,128)(2,1)S(1)} collective-permute-done((bf16[64,4224]{1,0:T(8,128)(2,1)S(1)}, bf16[64,4224]{1,0:T(8,128)(2,1)S(1)}, u32[]{:S(2)}, u32[]{:S(2)}) %collective-permute-start.13) | collective-permute-done | bytes 540704 | tf_op jit(solution)/shard_map/ppermute | solution.py:269
  77.1 5.3 %collective-permute-start.15 = (bf16[128,4224]{1,0:T(8,128)(2,1)S(1)}, bf16[128,4224]{1,0:T(8,128)(2,1)S(1)}, u32[]{:S(2)}, u32[]{:S(2)}) collective-permute-start(bf16[128,4224]{1,0:T(8,128)(2,1)S(1)} %behind.7), channel_id=1, source_target_pairs={{0,3},{1,2},{2,1},{3,0},{4,7},{5,6},{6,5},{7,4},{8,11},{9,10},{10,... | collective-permute-start | bytes 3244040 | tf_op jit(solution)/shard_map/ppermute | solution.py:269
  83.4 1.0 collective-permute-start.23
  84.4 18.8 %collective-permute-done.15 = bf16[128,4224]{1,0:T(8,128)(2,1)S(1)} collective-permute-done((bf16[128,4224]{1,0:T(8,128)(2,1)S(1)}, bf16[128,4224]{1,0:T(8,128)(2,1)S(1)}, u32[]{:S(2)}, u32[]{:S(2)}) %collective-permute-start.15) | collective-permute-done | bytes 1081376 | tf_op jit(solution)/shard_map/ppermute | solution.py:269
  103.2 0.2 broadcast_select_fusion.9
  103.6 4.3 %collective-permute-start.16 = (bf16[256,4224]{1,0:T(8,128)(2,1)S(1)}, bf16[256,4224]{1,0:T(8,128)(2,1)S(1)}, u32[]{:S(2)}, u32[]{:S(2)}) collective-permute-start(bf16[256,4224]{1,0:T(8,128)(2,1)S(1)} %pad_maximum_fusion.1), channel_id=1, source_target_pairs={{0,4},{4,0},{1,5},{5,1},{2,6},{6,2},{3,7},{7,3},{8,12},{12,8},{9,1... | collective-permute-start | bytes 6488072 | tf_op jit(solution)/shard_map/ppermute | solution.py:265
  107.8 0.4 broadcast_select_fusion.7
  108.4 0.4 broadcast_select_fusion.5
  108.8 0.4 broadcast_select_fusion.3
  109.5 0.4 broadcast_select_fusion.1
  110.0 1.7 %collective-permute-done.16 = bf16[256,4224]{1,0:T(8,128)(2,1)S(1)} collective-permute-done((bf16[256,4224]{1,0:T(8,128)(2,1)S(1)}, bf16[256,4224]{1,0:T(8,128)(2,1)S(1)}, u32[]{:S(2)}, u32[]{:S(2)}) %collective-permute-start.16) | collective-permute-done | bytes 2162720 | tf_op jit(solution)/shard_map/ppermute | solution.py:265
  111.7 0.6 pad_maximum_fusion.refs_0_
  112.3 2.4 %gram.2 = (f32[264,512]{1,0:T(8,128)S(1)}, f32[264,512]{1,0:T(8,128)S(1)}) custom-call(bf16[512,4224]{1,0:T(8,128)(2,1)S(1)} %pad_maximum_fusion.refs_0_, bf16[256,4224]{1,0:T(8,128)(2,1)S(1)} %pad_maximum_fusion.2.refs_1_, bf16[256,4224]{1,0:T(8,128)(2,1)S(1)} %pad_maximum_fusion.3.refs_2_, bf16[256,4224]{1,0:T(8,128)(2,1)S(1)} %pad_maximum_fusion.4.refs_3_, ...), custom_call_target="tpu_custom_call" | custom-call | flops 2147483648 | bytes 6291456 | tf_op jit(solution)/shard_map/gram/pallas_call | solution.py:206
  114.7 2.4 %gram.3 = (f32[264,512]{1,0:T(8,128)S(1)}, f32[264,512]{1,0:T(8,128)S(1)}) custom-call(bf16[512,4224]{1,0:T(8,128)(2,1)S(1)} %pad_maximum_fusion.refs_0_, bf16[256,4224]{1,0:T(8,128)(2,1)S(1)} %pad_maximum_fusion.2.refs_1_, bf16[256,4224]{1,0:T(8,128)(2,1)S(1)} %pad_maximum_fusion.3.refs_2_, bf16[256,4224]{1,0:T(8,128)(2,1)S(1)} %pad_maximum_fusion.4.refs_3_, ...), custom_call_target="tpu_custom_call" | custom-call | flops 2147483648 | bytes 6291456 | tf_op jit(solution)/shard_map/gram/pallas_call | solution.py:206
  117.1 0.5 collective-permute-start.24
  118.4 0.7 collective-permute-done.24.refs_2_
  119.1 0.8 collective-permute-done.25.refs_3_
  119.9 2.1 %finish.1 = (f32[1,2048]{1,0:T(1,128)}, f32[256,2048]{1,0:T(8,128)}) custom-call(s32[3]{0:T(128)S(1)} %pad_add_fusion.1.info_ref, f32[1]{0:T(128)} %bitcast.4.part_ref, f32[264,512]{1,0:T(8,128)S(1)} %get-tuple-element.24.refs_0_, f32[264,512]{1,0:T(8,128)S(1)} %get-tuple-element.25.refs_1_, f32[264,512]{1,0:T(8,128)S(1)} %collective-permute-done.24.refs_2_, ...), custom_call_target="tpu_custom_call" | custom-call | tf_op jit(solution)/shard_map/finish/pallas_call | solution.py:251
  (65 shorter events, 3.9 us)
Async XLA Ops:
  0.6 8.1 %copy-start.1 = (f32[2048]{0:T(1024)S(1)}, f32[2048]{0:T(1024)}, u32[]{:S(2)}) copy-start(f32[2048]{0:T(1024)} %param.5) | copy-start | bytes 24580
  1.4 1.6 %copy-start = (bf16[512,2048]{1,0:T(8,128)(2,1)S(1)}, bf16[512,2048]{1,0:T(8,128)(2,1)}, u32[]{:S(2)}) copy-start(bf16[512,2048]{1,0:T(8,128)(2,1)} %resid_ref.1) | copy-start | bytes 6291460
  3.9 5.2 %collective-permute-start = (f32[8,256]{1,0:T(8,128)S(1)}, f32[8,256]{1,0:T(8,128)S(1)}, u32[]{:S(2)}, u32[]{:S(2)}) collective-permute-start(f32[8,256]{1,0:T(8,128)S(1)} %get-tuple-element.17.s0), channel_id=1, source_target_pairs={{0,1},{1,0},{2,3},{3,2},{4,5},{5,4},{6,7},{7,6},{8,9},{9,8},{10,11... | collective-permute-start | bytes 24584 | tf_op jit(solution)/shard_map/ppermute | solution.py:269
  6.1 4.0 %collective-permute-start.1 = (f32[8,256]{1,0:T(8,128)S(1)}, f32[8,256]{1,0:T(8,128)S(1)}, u32[]{:S(2)}, u32[]{:S(2)}) collective-permute-start(f32[8,256]{1,0:T(8,128)S(1)} %get-tuple-element.17.s0), channel_id=1, source_target_pairs={{0,2},{1,3},{2,0},{3,1},{4,6},{5,7},{6,4},{7,5},{8,10},{9,11},{10,... | collective-permute-start | bytes 24584 | tf_op jit(solution)/shard_map/ppermute | solution.py:269
  8.7 3.7 %collective-permute-start.2 = (f32[8,256]{1,0:T(8,128)S(1)}, f32[8,256]{1,0:T(8,128)S(1)}, u32[]{:S(2)}, u32[]{:S(2)}) collective-permute-start(f32[8,256]{1,0:T(8,128)S(1)} %get-tuple-element.17.s0), channel_id=1, source_target_pairs={{0,3},{1,2},{2,1},{3,0},{4,7},{5,6},{6,5},{7,4},{8,11},{9,10},{10,... | collective-permute-start | bytes 24584 | tf_op jit(solution)/shard_map/ppermute | solution.py:269
  43.6 4.9 %collective-permute-start.3 = (bf16[16,4224]{1,0:T(8,128)(2,1)S(1)}, bf16[16,4224]{1,0:T(8,128)(2,1)S(1)}, u32[]{:S(2)}, u32[]{:S(2)}) collective-permute-start(bf16[16,4224]{1,0:T(8,128)(2,1)S(1)} %get-tuple-element.19), channel_id=1, source_target_pairs={{0,8},{8,0},{16,24},{24,16},{1,9},{9,1},{17,25},{25,17},{2,10},{10... | collective-permute-start | bytes 405512 | tf_op jit(solution)/shard_map/ppermute | solution.py:269
  44.0 4.5 %collective-permute-start.5 = (bf16[16,4224]{1,0:T(8,128)(2,1)S(1)}, bf16[16,4224]{1,0:T(8,128)(2,1)S(1)}, u32[]{:S(2)}, u32[]{:S(2)}) collective-permute-start(bf16[16,4224]{1,0:T(8,128)(2,1)S(1)} %get-tuple-element.21), channel_id=1, source_target_pairs={{0,32},{32,0},{64,96},{96,64},{1,33},{33,1},{65,97},{97,65},{2,34}... | collective-permute-start | bytes 405512 | tf_op jit(solution)/shard_map/ppermute | solution.py:269
  44.4 6.6 %collective-permute-start.6 = (bf16[16,4224]{1,0:T(8,128)(2,1)S(1)}, bf16[16,4224]{1,0:T(8,128)(2,1)S(1)}, u32[]{:S(2)}, u32[]{:S(2)}) collective-permute-start(bf16[16,4224]{1,0:T(8,128)(2,1)S(1)} %get-tuple-element.22), channel_id=1, source_target_pairs={{0,24},{8,16},{16,8},{24,0},{1,25},{9,17},{17,9},{25,1},{2,26},{10... | collective-permute-start | bytes 405512 | tf_op jit(solution)/shard_map/ppermute | solution.py:269
  45.4 5.6 %collective-permute-start.7 = (bf16[16,4224]{1,0:T(8,128)(2,1)S(1)}, bf16[16,4224]{1,0:T(8,128)(2,1)S(1)}, u32[]{:S(2)}, u32[]{:S(2)}) collective-permute-start(bf16[16,4224]{1,0:T(8,128)(2,1)S(1)} %get-tuple-element.23), channel_id=1, source_target_pairs={{0,96},{32,64},{64,32},{96,0},{1,97},{33,65},{65,33},{97,1},{2,98}... | collective-permute-start | bytes 405512 | tf_op jit(solution)/shard_map/ppermute | solution.py:269
  48.7 6.6 %collective-permute-start.9 = (bf16[32,4224]{1,0:T(8,128)(2,1)S(1)}, bf16[32,4224]{1,0:T(8,128)(2,1)S(1)}, u32[]{:S(2)}, u32[]{:S(2)}) collective-permute-start(bf16[32,4224]{1,0:T(8,128)(2,1)S(1)} %get-tuple-element.68.refs_0_), channel_id=1, source_target_pairs={{0,32},{32,0},{64,96},{96,64},{1,33},{33,1},{65,97},{97,65},{2,34}... | collective-permute-start | bytes 811016 | tf_op jit(solution)/shard_map/ppermute | solution.py:269
  49.9 8.2 %collective-permute-start.10 = (bf16[32,4224]{1,0:T(8,128)(2,1)S(1)}, bf16[32,4224]{1,0:T(8,128)(2,1)S(1)}, u32[]{:S(2)}, u32[]{:S(2)}) collective-permute-start(bf16[32,4224]{1,0:T(8,128)(2,1)S(1)} %get-tuple-element.69.refs_1_), channel_id=1, source_target_pairs={{0,24},{8,16},{16,8},{24,0},{1,25},{9,17},{17,9},{25,1},{2,26},{10... | collective-permute-start | bytes 811016 | tf_op jit(solution)/shard_map/ppermute | solution.py:269
  51.2 8.4 %collective-permute-start.11 = (bf16[32,4224]{1,0:T(8,128)(2,1)S(1)}, bf16[32,4224]{1,0:T(8,128)(2,1)S(1)}, u32[]{:S(2)}, u32[]{:S(2)}) collective-permute-start(bf16[32,4224]{1,0:T(8,128)(2,1)S(1)} %get-tuple-element.70.refs_2_), channel_id=1, source_target_pairs={{0,96},{32,64},{64,32},{96,0},{1,97},{33,65},{65,33},{97,1},{2,98}... | collective-permute-start | bytes 811016 | tf_op jit(solution)/shard_map/ppermute | solution.py:269
  52.2 11.3 %collective-permute-start.12 = (bf16[32,4224]{1,0:T(8,128)(2,1)S(1)}, bf16[32,4224]{1,0:T(8,128)(2,1)S(1)}, u32[]{:S(2)}, u32[]{:S(2)}) collective-permute-start(bf16[32,4224]{1,0:T(8,128)(2,1)S(1)} %get-tuple-element.71.refs_3_), channel_id=1, source_target_pairs={{0,8},{8,0},{16,24},{24,16},{1,9},{9,1},{17,25},{25,17},{2,10},{10... | collective-permute-start | bytes 811016 | tf_op jit(solution)/shard_map/ppermute | solution.py:269
  52.6 13.6 %collective-permute-start.8 = (bf16[32,4224]{1,0:T(8,128)(2,1)S(1)}, bf16[32,4224]{1,0:T(8,128)(2,1)S(1)}, u32[]{:S(2)}, u32[]{:S(2)}) collective-permute-start(bf16[32,4224]{1,0:T(8,128)(2,1)S(1)} %behind.5), channel_id=1, source_target_pairs={{0,2},{1,35},{2,64},{3,97},{32,3},{33,34},{34,65},{35,96},{64,0},{... | collective-permute-start | bytes 811016 | tf_op jit(solution)/shard_map/ppermute | solution.py:297
  55.2 11.1 %collective-permute-start.4 = (bf16[32,4224]{1,0:T(8,128)(2,1)S(1)}, bf16[32,4224]{1,0:T(8,128)(2,1)S(1)}, u32[]{:S(2)}, u32[]{:S(2)}) collective-permute-start(bf16[32,4224]{1,0:T(8,128)(2,1)S(1)} %behind.4), channel_id=1, source_target_pairs={{0,0},{1,33},{2,66},{3,99},{32,1},{33,32},{34,67},{35,98},{64,2},{... | collective-permute-start | bytes 811016 | tf_op jit(solution)/shard_map/ppermute | solution.py:297
  58.1 13.1 %collective-permute-start.14 = (bf16[64,4224]{1,0:T(8,128)(2,1)S(1)}, bf16[64,4224]{1,0:T(8,128)(2,1)S(1)}, u32[]{:S(2)}, u32[]{:S(2)}) collective-permute-start(bf16[64,4224]{1,0:T(8,128)(2,1)S(1)} %pad_maximum_fusion.12.refs_0_), channel_id=1, source_target_pairs={{0,24},{8,16},{16,8},{24,0},{1,25},{9,17},{17,9},{25,1},{2,26},{10... | collective-permute-start | bytes 1622024 | tf_op jit(solution)/shard_map/ppermute | solution.py:269
  59.6 22.8 %collective-permute-start.18 = (bf16[64,4224]{1,0:T(8,128)(2,1)S(1)}, bf16[64,4224]{1,0:T(8,128)(2,1)S(1)}, u32[]{:S(2)}, u32[]{:S(2)}) collective-permute-start(bf16[64,4224]{1,0:T(8,128)(2,1)S(1)} %pad_maximum_fusion.13.refs_1_), channel_id=1, source_target_pairs={{0,96},{32,64},{64,32},{96,0},{1,97},{33,65},{65,33},{97,1},{2,98}... | collective-permute-start | bytes 1622024 | tf_op jit(solution)/shard_map/ppermute | solution.py:269
  63.5 19.3 %collective-permute-start.20 = (bf16[64,4224]{1,0:T(8,128)(2,1)S(1)}, bf16[64,4224]{1,0:T(8,128)(2,1)S(1)}, u32[]{:S(2)}, u32[]{:S(2)}) collective-permute-start(bf16[64,4224]{1,0:T(8,128)(2,1)S(1)} %pad_maximum_fusion.14.refs_2_), channel_id=1, source_target_pairs={{0,8},{8,0},{16,24},{24,16},{1,9},{9,1},{17,25},{25,17},{2,10},{10... | collective-permute-start | bytes 1622024 | tf_op jit(solution)/shard_map/ppermute | solution.py:269
  66.3 16.9 %collective-permute-start.22 = (bf16[64,4224]{1,0:T(8,128)(2,1)S(1)}, bf16[64,4224]{1,0:T(8,128)(2,1)S(1)}, u32[]{:S(2)}, u32[]{:S(2)}) collective-permute-start(bf16[64,4224]{1,0:T(8,128)(2,1)S(1)} %pad_maximum_fusion.15.refs_3_), channel_id=1, source_target_pairs={{0,32},{32,0},{64,96},{96,64},{1,33},{33,1},{65,97},{97,65},{2,34}... | collective-permute-start | bytes 1622024 | tf_op jit(solution)/shard_map/ppermute | solution.py:269
  66.5 10.3 %collective-permute-start.13 = (bf16[64,4224]{1,0:T(8,128)(2,1)S(1)}, bf16[64,4224]{1,0:T(8,128)(2,1)S(1)}, u32[]{:S(2)}, u32[]{:S(2)}) collective-permute-start(bf16[64,4224]{1,0:T(8,128)(2,1)S(1)} %behind.6), channel_id=1, source_target_pairs={{0,1},{1,0},{2,3},{3,2},{4,5},{5,4},{6,7},{7,6},{8,9},{9,8},{10,11... | collective-permute-start | bytes 1622024 | tf_op jit(solution)/shard_map/ppermute | solution.py:269
  71.4 36.4 %collective-permute-start.17 = (bf16[128,4224]{1,0:T(8,128)(2,1)S(1)}, bf16[128,4224]{1,0:T(8,128)(2,1)S(1)}, u32[]{:S(2)}, u32[]{:S(2)}) collective-permute-start(bf16[128,4224]{1,0:T(8,128)(2,1)S(1)} %pad_maximum_fusion.7.refs_0_), channel_id=1, source_target_pairs={{0,96},{32,64},{64,32},{96,0},{1,97},{33,65},{65,33},{97,1},{2,98}... | collective-permute-start | bytes 3244040 | tf_op jit(solution)/shard_map/ppermute | solution.py:269
  77.1 26.1 %collective-permute-start.15 = (bf16[128,4224]{1,0:T(8,128)(2,1)S(1)}, bf16[128,4224]{1,0:T(8,128)(2,1)S(1)}, u32[]{:S(2)}, u32[]{:S(2)}) collective-permute-start(bf16[128,4224]{1,0:T(8,128)(2,1)S(1)} %behind.7), channel_id=1, source_target_pairs={{0,3},{1,2},{2,1},{3,0},{4,7},{5,6},{6,5},{7,4},{8,11},{9,10},{10,... | collective-permute-start | bytes 3244040 | tf_op jit(solution)/shard_map/ppermute | solution.py:269
  82.7 25.7 %collective-permute-start.19 = (bf16[128,4224]{1,0:T(8,128)(2,1)S(1)}, bf16[128,4224]{1,0:T(8,128)(2,1)S(1)}, u32[]{:S(2)}, u32[]{:S(2)}) collective-permute-start(bf16[128,4224]{1,0:T(8,128)(2,1)S(1)} %pad_maximum_fusion.8), channel_id=1, source_target_pairs={{0,8},{8,0},{16,24},{24,16},{1,9},{9,1},{17,25},{25,17},{2,10},{10... | collective-permute-start | bytes 3244040 | tf_op jit(solution)/shard_map/ppermute | solution.py:269
  83.0 25.7 %collective-permute-start.21 = (bf16[128,4224]{1,0:T(8,128)(2,1)S(1)}, bf16[128,4224]{1,0:T(8,128)(2,1)S(1)}, u32[]{:S(2)}, u32[]{:S(2)}) collective-permute-start(bf16[128,4224]{1,0:T(8,128)(2,1)S(1)} %pad_maximum_fusion.9), channel_id=1, source_target_pairs={{0,32},{32,0},{64,96},{96,64},{1,33},{33,1},{65,97},{97,65},{2,34}... | collective-permute-start | bytes 3244040 | tf_op jit(solution)/shard_map/ppermute | solution.py:269
  83.4 26.0 %collective-permute-start.23 = (bf16[128,4224]{1,0:T(8,128)(2,1)S(1)}, bf16[128,4224]{1,0:T(8,128)(2,1)S(1)}, u32[]{:S(2)}, u32[]{:S(2)}) collective-permute-start(bf16[128,4224]{1,0:T(8,128)(2,1)S(1)} %pad_maximum_fusion.10), channel_id=1, source_target_pairs={{0,24},{8,16},{16,8},{24,0},{1,25},{9,17},{17,9},{25,1},{2,26},{10... | collective-permute-start | bytes 3244040 | tf_op jit(solution)/shard_map/ppermute | solution.py:269
  103.6 8.2 %collective-permute-start.16 = (bf16[256,4224]{1,0:T(8,128)(2,1)S(1)}, bf16[256,4224]{1,0:T(8,128)(2,1)S(1)}, u32[]{:S(2)}, u32[]{:S(2)}) collective-permute-start(bf16[256,4224]{1,0:T(8,128)(2,1)S(1)} %pad_maximum_fusion.1), channel_id=1, source_target_pairs={{0,4},{4,0},{1,5},{5,1},{2,6},{6,2},{3,7},{7,3},{8,12},{12,8},{9,1... | collective-permute-start | bytes 6488072 | tf_op jit(solution)/shard_map/ppermute | solution.py:265
  117.1 2.0 %collective-permute-start.24 = (f32[264,512]{1,0:T(8,128)S(1)}, f32[264,512]{1,0:T(8,128)S(1)}, u32[]{:S(2)}, u32[]{:S(2)}) collective-permute-start(f32[264,512]{1,0:T(8,128)S(1)} %get-tuple-element.26), channel_id=1, source_target_pairs={{0,4},{4,0},{1,5},{5,1},{2,6},{6,2},{3,7},{7,3},{8,12},{12,8},{9,1... | collective-permute-start | bytes 1622024 | tf_op jit(solution)/shard_map/ppermute | solution.py:265
  117.6 2.3 %collective-permute-start.25 = (f32[264,512]{1,0:T(8,128)S(1)}, f32[264,512]{1,0:T(8,128)S(1)}, u32[]{:S(2)}, u32[]{:S(2)}) collective-permute-start(f32[264,512]{1,0:T(8,128)S(1)} %get-tuple-element.27), channel_id=1, source_target_pairs={{0,4},{4,0},{1,5},{5,1},{2,6},{6,2},{3,7},{7,3},{8,12},{12,8},{9,1... | collective-permute-start | bytes 1622024 | tf_op jit(solution)/shard_map/ppermute | solution.py:265

commit v21 on v20

--- a/solution.py
+++ b/solution.py
@@ -174,91 +174,112 @@
     )(value, *after)
 
 
-def gram_kernel(blocks, rows_ref, *refs):
-    streams, (own_ref, given_ref, cols_ref) = refs[:4], refs[4:]
+def gram_kernel(rows_ref, *refs):
+    streams, (out_ref, cols_ref) = refs[:4], refs[4:]
     lane = lax.broadcasted_iota(jnp.int32, (16, 128), 1)
     terms = jnp.where(lane < 3, 1.0, 0.0).astype(bf16)
-    for n, x in enumerate(blocks):
+    for x in range(4):
         for z in range(4):
             for s in range(4):
-                at = (z if s < 2 else z ^ 2) * PIECE + s * 16
+                at = x * 256 + (z if s < 2 else z ^ 2) * PIECE + s * 16
                 first = slot_of(s, x, z) * 16
-                cols_ref[n * 256 + at : n * 256 + at + 16, :] = streams[s][first : first + 16, :]
-        inside = slice(n * 256, (n + 1) * 256)
-        product = lax.dot_general(
+                cols_ref[at : at + 16, :] = streams[s][first : first + 16, :]
+        inside = slice(x * 256, (x + 1) * 256)
+        out_ref[:256, inside] = lax.dot_general(
             rows_ref[:, :LIVE],
             cols_ref[inside, :LIVE],
             (((1,), (1,)), ((), ())),
             preferred_element_type=f32,
         )
-        own_ref[:256, inside] = product[:256]
-        given_ref[:256, inside] = product[256:]
-        sums = lax.dot_general(
+        out_ref[256:, inside] = lax.dot_general(
             terms, cols_ref[inside, LIVE:], (((1,), (1,)), ((), ())), preferred_element_type=f32
-        )
-        own_ref[256:, inside] = sums[:8]
-        given_ref[256:, inside] = sums[:8]
-
-
-def gram(blocks, rows, streams):
-    vmem = pl.BlockSpec(memory_space=pltpu.VMEM)
-    width = 256 * len(blocks)
-    return pl.pallas_call(
-        lambda *refs: gram_kernel(blocks, *refs),
-        out_shape=(jax.ShapeDtypeStruct((264, width), f32),) * 2,
+        )[:8]
+
+
+def gram(rows, streams):
+    vmem = pl.BlockSpec(memory_space=pltpu.VMEM)
+    return pl.pallas_call(
+        gram_kernel,
+        out_shape=jax.ShapeDtypeStruct((264, 1024), f32),
         in_specs=[vmem] * 5,
-        out_specs=(vmem,) * 2,
-        scratch_shapes=[pltpu.VMEM((width, LONG), bf16)],
-        compiler_params=params(10),
+        out_specs=vmem,
+        scratch_shapes=[pltpu.VMEM((1024, LONG), bf16)],
+        compiler_params=params(14),
         cost_estimate=pl.CostEstimate(
-            flops=2 * 512 * width * LIVE, bytes_accessed=6 * 1024 * 1024, transcendentals=0
+            flops=2 * 256 * 1024 * LIVE, bytes_accessed=10 * 1024 * 1024, transcendentals=0
         ),
         name="gram",
     )(rows, *streams)
 
 
-def finish_kernel(info_ref, part_ref, *refs):
-    own, got, (mean_ref, out_ref) = refs[:2], refs[2:4], refs[4:]
-    core, row_block, col_block = info_ref[0], info_ref[1], info_ref[2]
+def put_blocks(info_ref, part_ref, core, ref, out_hbm, buffer, sem):
+    row_block, col_block = info_ref[1], info_ref[2]
     part = part_ref[0]
-
-    def put(ref, inside, block):
-        at = pl.multiple_of(block * 256, 256)
-        mean_ref[:, pl.ds(at, 256)] = ref[256:264, inside][:1] * part
+    copies = []
+    for x in range(4):
+        inside = slice(x * 256, (x + 1) * 256)
+        block = x * 2 + core
 
         @pl.when(col_block + block > row_block)
         def _():
-            out_ref[:, pl.ds(at, 256)] = ref[:256, inside] * part
+            buffer[x] = ref[:256, inside] * part
 
         @pl.when(col_block + block == row_block)
         def _():
             row = lax.broadcasted_iota(jnp.int32, (256, 256), 0)
             col = lax.broadcasted_iota(jnp.int32, (256, 256), 1)
-            out_ref[:, pl.ds(at, 256)] = jnp.where(row <= col, ref[:256, inside] * part, 0.0)
+            buffer[x] = jnp.where(row <= col, ref[:256, inside] * part, 0.0)
 
         @pl.when(col_block + block < row_block)
         def _():
-            out_ref[:, pl.ds(at, 256)] = jnp.zeros((256, 256), f32)
-
+            buffer[x] = jnp.zeros((256, 256), f32)
+
+        target = out_hbm.at[:, pl.ds(pl.multiple_of(block * 256, 256), 256)]
+        copies.append(pltpu.make_async_copy(buffer.at[x], target, sem.at[x]))
+        copies[-1].start()
+    for copy in copies:
+        copy.wait()
+
+
+def own_kernel(info_ref, part_ref, own_ref, out_hbm, buffer, sem):
+    put_blocks(info_ref, part_ref, info_ref[0], own_ref, out_hbm, buffer, sem)
+
+
+def rest_kernel(info_ref, part_ref, own_ref, got_ref, in_hbm, mean_ref, out_hbm, buffer, sem):
+    core = info_ref[0]
     for x in range(4):
-        inside = slice(x % 2 * 256, (x % 2 + 1) * 256)
-        put(own[x // 2], inside, x * 2 + core)
-        put(got[x // 2], inside, x * 2 + 1 - core)
+        inside = slice(x * 256, (x + 1) * 256)
+        for ref, which in ((own_ref, core), (got_ref, 1 - core)):
+            at = pl.multiple_of(x * 512 + which * 256, 256)
+            mean_ref[:, pl.ds(at, 256)] = ref[256:264, inside][:1] * part_ref[0]
+    put_blocks(info_ref, part_ref, 1 - core, got_ref, out_hbm, buffer, sem)
 
 
 def finish(info, part, own, got):
     vmem = pl.BlockSpec(memory_space=pltpu.VMEM)
-    return pl.pallas_call(
-        finish_kernel,
-        out_shape=(
-            jax.ShapeDtypeStruct((1, WIDTH), f32),
-            jax.ShapeDtypeStruct((256, WIDTH), f32),
-        ),
-        in_specs=[pl.BlockSpec(memory_space=pltpu.SMEM)] * 2 + [vmem] * 4,
-        out_specs=(vmem,) * 2,
-        compiler_params=params(10),
-        name="finish",
-    )(info, part, *own, *got)
+    smem = pl.BlockSpec(memory_space=pltpu.SMEM)
+    hbm = pl.BlockSpec(memory_space=pl.ANY)
+    shape = jax.ShapeDtypeStruct((256, WIDTH), f32)
+    scratch = [pltpu.VMEM((4, 256, 256), f32), pltpu.SemaphoreType.DMA((4,))]
+    half = pl.pallas_call(
+        own_kernel,
+        out_shape=shape,
+        in_specs=[smem, smem, vmem],
+        out_specs=hbm,
+        scratch_shapes=scratch,
+        compiler_params=params(6),
+        name="own_blocks",
+    )(info, part, own)
+    return pl.pallas_call(
+        rest_kernel,
+        out_shape=(jax.ShapeDtypeStruct((1, WIDTH), f32), shape),
+        in_specs=[smem, smem, vmem, vmem, hbm],
+        out_specs=(vmem, hbm),
+        scratch_shapes=scratch,
+        input_output_aliases={4: 1},
+        compiler_params=params(6),
+        name="other_blocks",
+    )(info, part, own, got, half)
 
 
 def swap(value):
@@ -311,13 +332,8 @@
         if step == 2:
             rows = meet(behind(rows, streams[:1]), "y", 3, side(y ^ z, 3, False))
 
-    rows = join(rows, swap(rows))
-
-    own, got = [], []
-    for blocks in ((0, 1), (2, 3)):
-        kept, given = gram(blocks, rows, streams)
-        own.append(kept)
-        got.append(swap(given))
+    got = swap(gram(swap(rows), streams))
+    own = gram(rows, streams)
     info = jnp.stack([c, z * 8 + x * 2 + c, y * 8]).astype(jnp.int32)
     mean, gram_factor = finish(info, part[None], own, got)
     return (mean[0], gram_factor)

time: 122 us -> 129 us (1.057)
  local copies, waits for them, and re-layouts: 2.05 us -> 8.5 us
  Pallas kernels: 10.3 us -> 12.7 us
  waiting for transfers between devices: 36.7 us -> 35.2 us
    unnamed x4 -> x20, local copies, waits for them, and re-layouts: 1.59 us -> 8.04 us
    pallas_call x3 -> x4, Pallas kernels: 6.92 us -> 9.32 us  [the longest x2 4.86 us: gram(): pl.pallas_call(gram_kernel, out_shape=jax.ShapeDtypeStruct((264, 1024), f...]
    ppermute x3 -> x2, waiting for transfers between devices: 3.21 us -> 1.67 us  [swap(): return lax.ppermute(value, 'c', [(0, 1), (1, 0)])]
    ppermute x3 -> x2, starting transfers between devices: 4.86 us -> 4.73 us  [swap(): return lax.ppermute(value, 'c', [(0, 1), (1, 0)])]
  transfers between devices with their start and end apart: 26 -> 25, of which waited for: 12 -> 10; matrix products, arithmetic and copies ran while one was open for 4% -> 4% of each run, Pallas kernels for 0% -> 3%
where the time goes in v21:
time: 129 us
  starting transfers between devices  36.5 us (28%)
  waiting for transfers between devices  35.2 us (27%)
  blocking collectives  27.3 us (21%)
  Pallas kernels  12.7 us (10%)
  local copies, waits for them, and re-layouts  8.5 us (7%)
  other arithmetic  6.81 us (5%)
  between operations  1.99 us (2%)
    ppermute x21, waiting for transfers between devices, trade(): return lax.ppermute(value, axis, [(i, i ^ flip) for i in range(4)])  33.5 us
    ppermute x21, starting transfers between devices, trade(): return lax.ppermute(value, axis, [(i, i ^ flip) for i in range(4)])  29.2 us
    all_to_all x1, blocking collectives, per_device(): pieces = lax.all_to_all(pieces, TOK, 0, 0, tiled=True)  27.3 us
    unnamed x20, local copies, waits for them, and re-layouts  8.04 us
    pallas_call x2, Pallas kernels, gram(): pl.pallas_call(gram_kernel, out_shape=jax.ShapeDtypeStruct((264, 1024), f...  4.86 us
    ppermute x2, starting transfers between devices, swap(): return lax.ppermute(value, 'c', [(0, 1), (1, 0)])  4.73 us
    select_n x18, other arithmetic, meet(): jnp.where(which == 0, value, got)  3.07 us
    pallas_call x1, Pallas kernels, finish(): pl.pallas_call(rest_kernel, out_shape=(jax.ShapeDtypeStruct((1, WIDTH), f...  2.88 us
  transfers between devices with their start and end apart: 25, of which 10 were waited for; matrix products, arithmetic and copies ran while one was open for 4% of the time, Pallas kernels for 3%

profile of v21, /device:TPU:1, one launch (start us, length us, event | category | flops | bytes accessed | tf_op | source)
XLA Modules:
  0.0 129.0 jit_solution(10078627646183401918)
XLA Ops:
  0.6 0.8 pad_add_fusion
  1.4 1.6 %copy-done.8 = bf16[512,2048]{1,0:T(8,128)(2,1)S(1)} copy-done((bf16[512,2048]{1,0:T(8,128)(2,1)S(1)}, bf16[512,2048]{1,0:T(8,128)(2,1)}, u32[]{:S(2)}) %copy-start.8) | copy-done | bytes 2097176
  3.0 0.8 pick.1
  3.9 2.2 %collective-permute-start = (f32[8,256]{1,0:T(8,128)S(1)}, f32[8,256]{1,0:T(8,128)S(1)}, u32[]{:S(2)}, u32[]{:S(2)}) collective-permute-start(f32[8,256]{1,0:T(8,128)S(1)} %get-tuple-element.13.s0), channel_id=1, source_target_pairs={{0,1},{1,0},{2,3},{3,2},{4,5},{5,4},{6,7},{7,6},{8,9},{9,8},{10,11... | collective-permute-start | bytes 24584 | tf_op jit(solution)/shard_map/ppermute | solution.py:290
  6.1 2.6 %collective-permute-start.1 = (f32[8,256]{1,0:T(8,128)S(1)}, f32[8,256]{1,0:T(8,128)S(1)}, u32[]{:S(2)}, u32[]{:S(2)}) collective-permute-start(f32[8,256]{1,0:T(8,128)S(1)} %get-tuple-element.13.s0), channel_id=1, source_target_pairs={{0,2},{1,3},{2,0},{3,1},{4,6},{5,7},{6,4},{7,5},{8,10},{9,11},{10,... | collective-permute-start | bytes 24584 | tf_op jit(solution)/shard_map/ppermute | solution.py:290
  8.7 0.4 copy.8.gain_ref
  9.1 1.0 collective-permute-done.1.s2
  10.1 2.3 %collective-permute-done.2.s3 = f32[8,256]{1,0:T(8,128)S(1)} collective-permute-done((f32[8,256]{1,0:T(8,128)S(1)}, f32[8,256]{1,0:T(8,128)S(1)}, u32[]{:S(2)}, u32[]{:S(2)}) %collective-permute-start.2) | collective-permute-done | bytes 8224 | tf_op jit(solution)/shard_map/ppermute | solution.py:290
  12.8 27.3 %all_to_all.5.in_ref = bf16[32,64,256]{2,1,0:T(8,128)(2,1)S(1)} all-to-all(bf16[32,64,256]{2,1,0:T(8,128)(2,1)S(1)} %norm.1), channel_id=1, replica_groups=mesh['z'=4,'x'=4,'c'=2,'y'=4] {'z','x','c'}, dimensions={0} | all-to-all | bytes 2097152 | tf_op jit(solution)/shard_map/all_to_all | solution.py:308
  40.0 1.3 fusion
  41.6 2.1 %pack.1 = (bf16[32,4224]{1,0:T(8,128)(2,1)S(1)}, bf16[32,4224]{1,0:T(8,128)(2,1)S(1)}, bf16[16,4224]{1,0:T(8,128)(2,1)S(1)}, bf16[16,4224]{1,0:T(8,128)(2,1)S(1)...) custom-call(s32[32]{0:T(128)S(1)} %sub.3.first_ref, bf16[32,64,256]{2,1,0:T(8,128)(2,1)S(1)} %all_to_all.5.in_ref), custom_call_target="tpu_custom_call" | custom-call | tf_op jit(solution)/shard_map/pack/pallas_call | solution.py:149
  43.7 0.4 collective-permute-start.3
  44.1 0.4 collective-permute-start.5
  44.5 1.0 collective-permute-start.6
  45.5 0.6 collective-permute-start.7
  46.1 2.4 %collective-permute-done.3 = bf16[16,4224]{1,0:T(8,128)(2,1)S(1)} collective-permute-done((bf16[16,4224]{1,0:T(8,128)(2,1)S(1)}, bf16[16,4224]{1,0:T(8,128)(2,1)S(1)}, u32[]{:S(2)}, u32[]{:S(2)}) %collective-permute-start.3) | collective-permute-done | bytes 135200 | tf_op jit(solution)/shard_map/ppermute | solution.py:290
  48.7 1.2 collective-permute-start.9
  49.9 1.2 collective-permute-start.10
  51.2 1.0 collective-permute-start.11
  52.2 0.4 collective-permute-start.12
  52.7 1.9 %collective-permute-start.8 = (bf16[32,4224]{1,0:T(8,128)(2,1)S(1)}, bf16[32,4224]{1,0:T(8,128)(2,1)S(1)}, u32[]{:S(2)}, u32[]{:S(2)}) collective-permute-start(bf16[32,4224]{1,0:T(8,128)(2,1)S(1)} %behind.5), channel_id=1, source_target_pairs={{0,2},{1,35},{2,64},{3,97},{32,3},{33,34},{34,65},{35,96},{64,0},{... | collective-permute-start | bytes 811016 | tf_op jit(solution)/shard_map/ppermute | solution.py:318
  54.7 0.6 collective-permute-done.9
  55.3 0.7 collective-permute-start.4
  56.1 2.0 %collective-permute-done.10 = bf16[32,4224]{1,0:T(8,128)(2,1)S(1)} collective-permute-done((bf16[32,4224]{1,0:T(8,128)(2,1)S(1)}, bf16[32,4224]{1,0:T(8,128)(2,1)S(1)}, u32[]{:S(2)}, u32[]{:S(2)}) %collective-permute-start.10) | collective-permute-done | bytes 270368 | tf_op jit(solution)/shard_map/ppermute | solution.py:290
  58.1 1.4 %collective-permute-start.14 = (bf16[64,4224]{1,0:T(8,128)(2,1)S(1)}, bf16[64,4224]{1,0:T(8,128)(2,1)S(1)}, u32[]{:S(2)}, u32[]{:S(2)}) collective-permute-start(bf16[64,4224]{1,0:T(8,128)(2,1)S(1)} %pad_maximum_fusion.11.refs_0_), channel_id=1, source_target_pairs={{0,24},{8,16},{16,8},{24,0},{1,25},{9,17},{17,9},{25,1},{2,26},{10... | collective-permute-start | bytes 1622024 | tf_op jit(solution)/shard_map/ppermute | solution.py:290
  59.6 3.7 %collective-permute-start.17 = (bf16[64,4224]{1,0:T(8,128)(2,1)S(1)}, bf16[64,4224]{1,0:T(8,128)(2,1)S(1)}, u32[]{:S(2)}, u32[]{:S(2)}) collective-permute-start(bf16[64,4224]{1,0:T(8,128)(2,1)S(1)} %pad_maximum_fusion.12.refs_1_), channel_id=1, source_target_pairs={{0,96},{32,64},{64,32},{96,0},{1,97},{33,65},{65,33},{97,1},{2,98}... | collective-permute-start | bytes 1622024 | tf_op jit(solution)/shard_map/ppermute | solution.py:290
  63.5 2.7 %collective-permute-start.19 = (bf16[64,4224]{1,0:T(8,128)(2,1)S(1)}, bf16[64,4224]{1,0:T(8,128)(2,1)S(1)}, u32[]{:S(2)}, u32[]{:S(2)}) collective-permute-start(bf16[64,4224]{1,0:T(8,128)(2,1)S(1)} %pad_maximum_fusion.13.refs_2_), channel_id=1, source_target_pairs={{0,8},{8,0},{16,24},{24,16},{1,9},{9,1},{17,25},{25,17},{2,10},{10... | collective-permute-start | bytes 1622024 | tf_op jit(solution)/shard_map/ppermute | solution.py:290
  66.6 4.5 %collective-permute-done.14 = bf16[64,4224]{1,0:T(8,128)(2,1)S(1)} collective-permute-done((bf16[64,4224]{1,0:T(8,128)(2,1)S(1)}, bf16[64,4224]{1,0:T(8,128)(2,1)S(1)}, u32[]{:S(2)}, u32[]{:S(2)}) %collective-permute-start.14) | collective-permute-done | bytes 540704 | tf_op jit(solution)/shard_map/ppermute | solution.py:290
  71.5 3.7 %collective-permute-start.16 = (bf16[128,4224]{1,0:T(8,128)(2,1)S(1)}, bf16[128,4224]{1,0:T(8,128)(2,1)S(1)}, u32[]{:S(2)}, u32[]{:S(2)}) collective-permute-start(bf16[128,4224]{1,0:T(8,128)(2,1)S(1)} %pad_maximum_fusion.6.refs_0_), channel_id=1, source_target_pairs={{0,96},{32,64},{64,32},{96,0},{1,97},{33,65},{65,33},{97,1},{2,98}... | collective-permute-start | bytes 3244040 | tf_op jit(solution)/shard_map/ppermute | solution.py:290
  75.2 1.7 %collective-permute-done.13 = bf16[64,4224]{1,0:T(8,128)(2,1)S(1)} collective-permute-done((bf16[64,4224]{1,0:T(8,128)(2,1)S(1)}, bf16[64,4224]{1,0:T(8,128)(2,1)S(1)}, u32[]{:S(2)}, u32[]{:S(2)}) %collective-permute-start.13) | collective-permute-done | bytes 540704 | tf_op jit(solution)/shard_map/ppermute | solution.py:290
  77.2 5.3 %collective-permute-start.15 = (bf16[128,4224]{1,0:T(8,128)(2,1)S(1)}, bf16[128,4224]{1,0:T(8,128)(2,1)S(1)}, u32[]{:S(2)}, u32[]{:S(2)}) collective-permute-start(bf16[128,4224]{1,0:T(8,128)(2,1)S(1)} %behind.7), channel_id=1, source_target_pairs={{0,3},{1,2},{2,1},{3,0},{4,7},{5,6},{6,5},{7,4},{8,11},{9,10},{10,... | collective-permute-start | bytes 3244040 | tf_op jit(solution)/shard_map/ppermute | solution.py:290
  83.5 1.0 collective-permute-start.22
  84.5 18.8 %collective-permute-done.15 = bf16[128,4224]{1,0:T(8,128)(2,1)S(1)} collective-permute-done((bf16[128,4224]{1,0:T(8,128)(2,1)S(1)}, bf16[128,4224]{1,0:T(8,128)(2,1)S(1)}, u32[]{:S(2)}, u32[]{:S(2)}) %collective-permute-start.15) | collective-permute-done | bytes 1081376 | tf_op jit(solution)/shard_map/ppermute | solution.py:290
  103.6 4.3 %collective-permute-start.23 = (bf16[256,4224]{1,0:T(8,128)(2,1)S(1)}, bf16[256,4224]{1,0:T(8,128)(2,1)S(1)}, u32[]{:S(2)}, u32[]{:S(2)}) collective-permute-start(bf16[256,4224]{1,0:T(8,128)(2,1)S(1)} %pad_maximum_fusion.rows_ref), channel_id=1, source_target_pairs={{0,4},{4,0},{1,5},{5,1},{2,6},{6,2},{3,7},{7,3},{8,12},{12,8},{9,1... | collective-permute-start | bytes 6488072 | tf_op jit(solution)/shard_map/ppermute | solution.py:286
  107.9 0.4 broadcast_select_fusion.7
  108.5 0.4 broadcast_select_fusion.5
  108.9 0.4 broadcast_select_fusion.3
  109.6 0.4 broadcast_select_fusion.1
  110.1 1.7 %collective-permute-done.23.rows_ref = bf16[256,4224]{1,0:T(8,128)(2,1)S(1)} collective-permute-done((bf16[256,4224]{1,0:T(8,128)(2,1)S(1)}, bf16[256,4224]{1,0:T(8,128)(2,1)S(1)}, u32[]{:S(2)}, u32[]{:S(2)}) %collective-permute-start.23) | collective-permute-done | bytes 2162720 | tf_op jit(solution)/shard_map/ppermute | solution.py:286
  111.8 2.4 %gram.3 = f32[264,1024]{1,0:T(8,128)S(1)} custom-call(bf16[256,4224]{1,0:T(8,128)(2,1)S(1)} %collective-permute-done.23.rows_ref, bf16[256,4224]{1,0:T(8,128)(2,1)S(1)} %pad_maximum_fusion.1.refs_0_, bf16[256,4224]{1,0:T(8,128)(2,1)S(1)} %pad_maximum_fusion.2.refs_1_, bf16[256,4224]{1,0:T(8,128)(2,1)S(1)} %pad_maximum_fusion.3.refs_2_, ...), custom_call_target="tpu_custom_call" | custom-call | flops 2147483648 | bytes 10485760 | tf_op jit(solution)/shard_map/gram/pallas_call | solution.py:201
  114.2 0.5 collective-permute-start.24
  115.5 1.6 %copy-done.1 = bf16[256,4224]{1,0:T(8,128)(2,1)S(1)} copy-done((bf16[256,4224]{1,0:T(8,128)(2,1)S(1)}, bf16[256,4224]{1,0:T(8,128)(2,1)}, u32[]{:S(2)}) %copy-start.1) | copy-done | bytes 2162712
  117.1 1.6 %copy-done.3 = bf16[256,4224]{1,0:T(8,128)(2,1)S(1)} copy-done((bf16[256,4224]{1,0:T(8,128)(2,1)S(1)}, bf16[256,4224]{1,0:T(8,128)(2,1)}, u32[]{:S(2)}) %copy-start.3) | copy-done | bytes 2162712
  118.7 1.6 %copy-done.5 = bf16[256,4224]{1,0:T(8,128)(2,1)S(1)} copy-done((bf16[256,4224]{1,0:T(8,128)(2,1)S(1)}, bf16[256,4224]{1,0:T(8,128)(2,1)}, u32[]{:S(2)}) %copy-start.5) | copy-done | bytes 2162712
  120.3 1.6 %copy-done.7 = bf16[256,4224]{1,0:T(8,128)(2,1)S(1)} copy-done((bf16[256,4224]{1,0:T(8,128)(2,1)S(1)}, bf16[256,4224]{1,0:T(8,128)(2,1)}, u32[]{:S(2)}) %copy-start.7) | copy-done | bytes 2162712
  121.9 2.4 %gram.2.own_ref = f32[264,1024]{1,0:T(8,128)S(1)} custom-call(bf16[256,4224]{1,0:T(8,128)(2,1)S(1)} %copy-done.7, bf16[256,4224]{1,0:T(8,128)(2,1)S(1)} %pad_maximum_fusion.1.refs_0_, bf16[256,4224]{1,0:T(8,128)(2,1)S(1)} %copy-done.1, bf16[256,4224]{1,0:T(8,128)(2,1)S(1)} %copy-done.3, bf16[256,4224]{1,0:T(8,128)(2,1)S(1)} %copy-done.5), custom_call_target="tpu_custom_call" | custom-call | flops 2147483648 | bytes 10485760 | tf_op jit(solution)/shard_map/gram/pallas_call | solution.py:201
  124.3 1.6 %own_blocks.1.in_hbm = f32[256,2048]{1,0:T(8,128)} custom-call(s32[3]{0:T(128)S(1)} %pad_add_fusion.1.info_ref, f32[1]{0:T(128)} %bitcast.4.part_ref, f32[264,1024]{1,0:T(8,128)S(1)} %gram.2.own_ref), custom_call_target="tpu_custom_call" | custom-call | tf_op jit(solution)/shard_map/own_blocks/pallas_call | solution.py:264
  125.9 2.9 %other_blocks.1 = (f32[1,2048]{1,0:T(1,128)}, f32[256,2048]{1,0:T(8,128)}) custom-call(s32[3]{0:T(128)S(1)} %pad_add_fusion.1.info_ref, f32[1]{0:T(128)} %bitcast.4.part_ref, f32[264,1024]{1,0:T(8,128)S(1)} %gram.2.own_ref, f32[264,1024]{1,0:T(8,128)} %collective-permute-done.24.got_ref, f32[256,2048]{1,0:T(8,128)} %own_blocks.1.in_hbm), custom_call_target="tpu_custom_call", output_to_operand_aliasing={{1}: (4, {})} | custom-call | tf_op jit(solution)/shard_map/other_blocks/pallas_call | solution.py:273
  (79 shorter events, 4.4 us)
Async XLA Ops:
  0.6 8.1 %copy-start.9 = (f32[2048]{0:T(1024)S(1)}, f32[2048]{0:T(1024)}, u32[]{:S(2)}) copy-start(f32[2048]{0:T(1024)} %param.5) | copy-start | bytes 24580
  1.4 1.6 %copy-start.8 = (bf16[512,2048]{1,0:T(8,128)(2,1)S(1)}, bf16[512,2048]{1,0:T(8,128)(2,1)}, u32[]{:S(2)}) copy-start(bf16[512,2048]{1,0:T(8,128)(2,1)} %resid_ref.1) | copy-start | bytes 6291460
  3.9 5.2 %collective-permute-start = (f32[8,256]{1,0:T(8,128)S(1)}, f32[8,256]{1,0:T(8,128)S(1)}, u32[]{:S(2)}, u32[]{:S(2)}) collective-permute-start(f32[8,256]{1,0:T(8,128)S(1)} %get-tuple-element.13.s0), channel_id=1, source_target_pairs={{0,1},{1,0},{2,3},{3,2},{4,5},{5,4},{6,7},{7,6},{8,9},{9,8},{10,11... | collective-permute-start | bytes 24584 | tf_op jit(solution)/shard_map/ppermute | solution.py:290
  6.1 4.0 %collective-permute-start.1 = (f32[8,256]{1,0:T(8,128)S(1)}, f32[8,256]{1,0:T(8,128)S(1)}, u32[]{:S(2)}, u32[]{:S(2)}) collective-permute-start(f32[8,256]{1,0:T(8,128)S(1)} %get-tuple-element.13.s0), channel_id=1, source_target_pairs={{0,2},{1,3},{2,0},{3,1},{4,6},{5,7},{6,4},{7,5},{8,10},{9,11},{10,... | collective-permute-start | bytes 24584 | tf_op jit(solution)/shard_map/ppermute | solution.py:290
  8.7 3.7 %collective-permute-start.2 = (f32[8,256]{1,0:T(8,128)S(1)}, f32[8,256]{1,0:T(8,128)S(1)}, u32[]{:S(2)}, u32[]{:S(2)}) collective-permute-start(f32[8,256]{1,0:T(8,128)S(1)} %get-tuple-element.13.s0), channel_id=1, source_target_pairs={{0,3},{1,2},{2,1},{3,0},{4,7},{5,6},{6,5},{7,4},{8,11},{9,10},{10,... | collective-permute-start | bytes 24584 | tf_op jit(solution)/shard_map/ppermute | solution.py:290
  43.7 4.9 %collective-permute-start.3 = (bf16[16,4224]{1,0:T(8,128)(2,1)S(1)}, bf16[16,4224]{1,0:T(8,128)(2,1)S(1)}, u32[]{:S(2)}, u32[]{:S(2)}) collective-permute-start(bf16[16,4224]{1,0:T(8,128)(2,1)S(1)} %get-tuple-element.15), channel_id=1, source_target_pairs={{0,8},{8,0},{16,24},{24,16},{1,9},{9,1},{17,25},{25,17},{2,10},{10... | collective-permute-start | bytes 405512 | tf_op jit(solution)/shard_map/ppermute | solution.py:290
  44.1 4.5 %collective-permute-start.5 = (bf16[16,4224]{1,0:T(8,128)(2,1)S(1)}, bf16[16,4224]{1,0:T(8,128)(2,1)S(1)}, u32[]{:S(2)}, u32[]{:S(2)}) collective-permute-start(bf16[16,4224]{1,0:T(8,128)(2,1)S(1)} %get-tuple-element.17), channel_id=1, source_target_pairs={{0,32},{32,0},{64,96},{96,64},{1,33},{33,1},{65,97},{97,65},{2,34}... | collective-permute-start | bytes 405512 | tf_op jit(solution)/shard_map/ppermute | solution.py:290
  44.5 6.6 %collective-permute-start.6 = (bf16[16,4224]{1,0:T(8,128)(2,1)S(1)}, bf16[16,4224]{1,0:T(8,128)(2,1)S(1)}, u32[]{:S(2)}, u32[]{:S(2)}) collective-permute-start(bf16[16,4224]{1,0:T(8,128)(2,1)S(1)} %get-tuple-element.18), channel_id=1, source_target_pairs={{0,24},{8,16},{16,8},{24,0},{1,25},{9,17},{17,9},{25,1},{2,26},{10... | collective-permute-start | bytes 405512 | tf_op jit(solution)/shard_map/ppermute | solution.py:290
  45.5 5.6 %collective-permute-start.7 = (bf16[16,4224]{1,0:T(8,128)(2,1)S(1)}, bf16[16,4224]{1,0:T(8,128)(2,1)S(1)}, u32[]{:S(2)}, u32[]{:S(2)}) collective-permute-start(bf16[16,4224]{1,0:T(8,128)(2,1)S(1)} %get-tuple-element.19), channel_id=1, source_target_pairs={{0,96},{32,64},{64,32},{96,0},{1,97},{33,65},{65,33},{97,1},{2,98}... | collective-permute-start | bytes 405512 | tf_op jit(solution)/shard_map/ppermute | solution.py:290
  48.7 6.6 %collective-permute-start.9 = (bf16[32,4224]{1,0:T(8,128)(2,1)S(1)}, bf16[32,4224]{1,0:T(8,128)(2,1)S(1)}, u32[]{:S(2)}, u32[]{:S(2)}) collective-permute-start(bf16[32,4224]{1,0:T(8,128)(2,1)S(1)} %get-tuple-element.60.refs_0_), channel_id=1, source_target_pairs={{0,32},{32,0},{64,96},{96,64},{1,33},{33,1},{65,97},{97,65},{2,34}... | collective-permute-start | bytes 811016 | tf_op jit(solution)/shard_map/ppermute | solution.py:290
  49.9 8.2 %collective-permute-start.10 = (bf16[32,4224]{1,0:T(8,128)(2,1)S(1)}, bf16[32,4224]{1,0:T(8,128)(2,1)S(1)}, u32[]{:S(2)}, u32[]{:S(2)}) collective-permute-start(bf16[32,4224]{1,0:T(8,128)(2,1)S(1)} %get-tuple-element.61.refs_1_), channel_id=1, source_target_pairs={{0,24},{8,16},{16,8},{24,0},{1,25},{9,17},{17,9},{25,1},{2,26},{10... | collective-permute-start | bytes 811016 | tf_op jit(solution)/shard_map/ppermute | solution.py:290
  51.2 8.4 %collective-permute-start.11 = (bf16[32,4224]{1,0:T(8,128)(2,1)S(1)}, bf16[32,4224]{1,0:T(8,128)(2,1)S(1)}, u32[]{:S(2)}, u32[]{:S(2)}) collective-permute-start(bf16[32,4224]{1,0:T(8,128)(2,1)S(1)} %get-tuple-element.62.refs_2_), channel_id=1, source_target_pairs={{0,96},{32,64},{64,32},{96,0},{1,97},{33,65},{65,33},{97,1},{2,98}... | collective-permute-start | bytes 811016 | tf_op jit(solution)/shard_map/ppermute | solution.py:290
  52.2 11.3 %collective-permute-start.12 = (bf16[32,4224]{1,0:T(8,128)(2,1)S(1)}, bf16[32,4224]{1,0:T(8,128)(2,1)S(1)}, u32[]{:S(2)}, u32[]{:S(2)}) collective-permute-start(bf16[32,4224]{1,0:T(8,128)(2,1)S(1)} %get-tuple-element.63.refs_3_), channel_id=1, source_target_pairs={{0,8},{8,0},{16,24},{24,16},{1,9},{9,1},{17,25},{25,17},{2,10},{10... | collective-permute-start | bytes 811016 | tf_op jit(solution)/shard_map/ppermute | solution.py:290
  52.7 13.6 %collective-permute-start.8 = (bf16[32,4224]{1,0:T(8,128)(2,1)S(1)}, bf16[32,4224]{1,0:T(8,128)(2,1)S(1)}, u32[]{:S(2)}, u32[]{:S(2)}) collective-permute-start(bf16[32,4224]{1,0:T(8,128)(2,1)S(1)} %behind.5), channel_id=1, source_target_pairs={{0,2},{1,35},{2,64},{3,97},{32,3},{33,34},{34,65},{35,96},{64,0},{... | collective-permute-start | bytes 811016 | tf_op jit(solution)/shard_map/ppermute | solution.py:318
  55.3 11.1 %collective-permute-start.4 = (bf16[32,4224]{1,0:T(8,128)(2,1)S(1)}, bf16[32,4224]{1,0:T(8,128)(2,1)S(1)}, u32[]{:S(2)}, u32[]{:S(2)}) collective-permute-start(bf16[32,4224]{1,0:T(8,128)(2,1)S(1)} %behind.4), channel_id=1, source_target_pairs={{0,0},{1,33},{2,66},{3,99},{32,1},{33,32},{34,67},{35,98},{64,2},{... | collective-permute-start | bytes 811016 | tf_op jit(solution)/shard_map/ppermute | solution.py:318
  58.1 13.1 %collective-permute-start.14 = (bf16[64,4224]{1,0:T(8,128)(2,1)S(1)}, bf16[64,4224]{1,0:T(8,128)(2,1)S(1)}, u32[]{:S(2)}, u32[]{:S(2)}) collective-permute-start(bf16[64,4224]{1,0:T(8,128)(2,1)S(1)} %pad_maximum_fusion.11.refs_0_), channel_id=1, source_target_pairs={{0,24},{8,16},{16,8},{24,0},{1,25},{9,17},{17,9},{25,1},{2,26},{10... | collective-permute-start | bytes 1622024 | tf_op jit(solution)/shard_map/ppermute | solution.py:290
  59.6 22.8 %collective-permute-start.17 = (bf16[64,4224]{1,0:T(8,128)(2,1)S(1)}, bf16[64,4224]{1,0:T(8,128)(2,1)S(1)}, u32[]{:S(2)}, u32[]{:S(2)}) collective-permute-start(bf16[64,4224]{1,0:T(8,128)(2,1)S(1)} %pad_maximum_fusion.12.refs_1_), channel_id=1, source_target_pairs={{0,96},{32,64},{64,32},{96,0},{1,97},{33,65},{65,33},{97,1},{2,98}... | collective-permute-start | bytes 1622024 | tf_op jit(solution)/shard_map/ppermute | solution.py:290
  63.5 19.3 %collective-permute-start.19 = (bf16[64,4224]{1,0:T(8,128)(2,1)S(1)}, bf16[64,4224]{1,0:T(8,128)(2,1)S(1)}, u32[]{:S(2)}, u32[]{:S(2)}) collective-permute-start(bf16[64,4224]{1,0:T(8,128)(2,1)S(1)} %pad_maximum_fusion.13.refs_2_), channel_id=1, source_target_pairs={{0,8},{8,0},{16,24},{24,16},{1,9},{9,1},{17,25},{25,17},{2,10},{10... | collective-permute-start | bytes 1622024 | tf_op jit(solution)/shard_map/ppermute | solution.py:290
  66.3 16.9 %collective-permute-start.21 = (bf16[64,4224]{1,0:T(8,128)(2,1)S(1)}, bf16[64,4224]{1,0:T(8,128)(2,1)S(1)}, u32[]{:S(2)}, u32[]{:S(2)}) collective-permute-start(bf16[64,4224]{1,0:T(8,128)(2,1)S(1)} %pad_maximum_fusion.14.refs_3_), channel_id=1, source_target_pairs={{0,32},{32,0},{64,96},{96,64},{1,33},{33,1},{65,97},{97,65},{2,34}... | collective-permute-start | bytes 1622024 | tf_op jit(solution)/shard_map/ppermute | solution.py:290
  66.5 10.3 %collective-permute-start.13 = (bf16[64,4224]{1,0:T(8,128)(2,1)S(1)}, bf16[64,4224]{1,0:T(8,128)(2,1)S(1)}, u32[]{:S(2)}, u32[]{:S(2)}) collective-permute-start(bf16[64,4224]{1,0:T(8,128)(2,1)S(1)} %behind.6), channel_id=1, source_target_pairs={{0,1},{1,0},{2,3},{3,2},{4,5},{5,4},{6,7},{7,6},{8,9},{9,8},{10,11... | collective-permute-start | bytes 1622024 | tf_op jit(solution)/shard_map/ppermute | solution.py:290
  71.5 36.4 %collective-permute-start.16 = (bf16[128,4224]{1,0:T(8,128)(2,1)S(1)}, bf16[128,4224]{1,0:T(8,128)(2,1)S(1)}, u32[]{:S(2)}, u32[]{:S(2)}) collective-permute-start(bf16[128,4224]{1,0:T(8,128)(2,1)S(1)} %pad_maximum_fusion.6.refs_0_), channel_id=1, source_target_pairs={{0,96},{32,64},{64,32},{96,0},{1,97},{33,65},{65,33},{97,1},{2,98}... | collective-permute-start | bytes 3244040 | tf_op jit(solution)/shard_map/ppermute | solution.py:290
  77.2 26.1 %collective-permute-start.15 = (bf16[128,4224]{1,0:T(8,128)(2,1)S(1)}, bf16[128,4224]{1,0:T(8,128)(2,1)S(1)}, u32[]{:S(2)}, u32[]{:S(2)}) collective-permute-start(bf16[128,4224]{1,0:T(8,128)(2,1)S(1)} %behind.7), channel_id=1, source_target_pairs={{0,3},{1,2},{2,1},{3,0},{4,7},{5,6},{6,5},{7,4},{8,11},{9,10},{10,... | collective-permute-start | bytes 3244040 | tf_op jit(solution)/shard_map/ppermute | solution.py:290
  82.7 25.7 %collective-permute-start.18 = (bf16[128,4224]{1,0:T(8,128)(2,1)S(1)}, bf16[128,4224]{1,0:T(8,128)(2,1)S(1)}, u32[]{:S(2)}, u32[]{:S(2)}) collective-permute-start(bf16[128,4224]{1,0:T(8,128)(2,1)S(1)} %pad_maximum_fusion.7), channel_id=1, source_target_pairs={{0,8},{8,0},{16,24},{24,16},{1,9},{9,1},{17,25},{25,17},{2,10},{10... | collective-permute-start | bytes 3244040 | tf_op jit(solution)/shard_map/ppermute | solution.py:290
  83.1 25.7 %collective-permute-start.20 = (bf16[128,4224]{1,0:T(8,128)(2,1)S(1)}, bf16[128,4224]{1,0:T(8,128)(2,1)S(1)}, u32[]{:S(2)}, u32[]{:S(2)}) collective-permute-start(bf16[128,4224]{1,0:T(8,128)(2,1)S(1)} %pad_maximum_fusion.8), channel_id=1, source_target_pairs={{0,32},{32,0},{64,96},{96,64},{1,33},{33,1},{65,97},{97,65},{2,34}... | collective-permute-start | bytes 3244040 | tf_op jit(solution)/shard_map/ppermute | solution.py:290
  83.5 26.1 %collective-permute-start.22 = (bf16[128,4224]{1,0:T(8,128)(2,1)S(1)}, bf16[128,4224]{1,0:T(8,128)(2,1)S(1)}, u32[]{:S(2)}, u32[]{:S(2)}) collective-permute-start(bf16[128,4224]{1,0:T(8,128)(2,1)S(1)} %pad_maximum_fusion.9), channel_id=1, source_target_pairs={{0,24},{8,16},{16,8},{24,0},{1,25},{9,17},{17,9},{25,1},{2,26},{10... | collective-permute-start | bytes 3244040 | tf_op jit(solution)/shard_map/ppermute | solution.py:290
  103.6 4.7 %copy-start.6 = (bf16[256,4224]{1,0:T(8,128)(2,1)}, bf16[256,4224]{1,0:T(8,128)(2,1)S(1)}, u32[]{:S(2)}) copy-start(bf16[256,4224]{1,0:T(8,128)(2,1)S(1)} %pad_maximum_fusion.rows_ref) | copy-start | bytes 6488068
  103.6 8.2 %collective-permute-start.23 = (bf16[256,4224]{1,0:T(8,128)(2,1)S(1)}, bf16[256,4224]{1,0:T(8,128)(2,1)S(1)}, u32[]{:S(2)}, u32[]{:S(2)}) collective-permute-start(bf16[256,4224]{1,0:T(8,128)(2,1)S(1)} %pad_maximum_fusion.rows_ref), channel_id=1, source_target_pairs={{0,4},{4,0},{1,5},{5,1},{2,6},{6,2},{3,7},{7,3},{8,12},{12,8},{9,1... | collective-permute-start | bytes 6488072 | tf_op jit(solution)/shard_map/ppermute | solution.py:286
  109.4 2.4 %copy-start = (bf16[256,4224]{1,0:T(8,128)(2,1)}, bf16[256,4224]{1,0:T(8,128)(2,1)S(1)}, u32[]{:S(2)}) copy-start(bf16[256,4224]{1,0:T(8,128)(2,1)S(1)} %pad_maximum_fusion.2.refs_1_) | copy-start | bytes 6488068
  109.5 2.2 %copy-start.2 = (bf16[256,4224]{1,0:T(8,128)(2,1)}, bf16[256,4224]{1,0:T(8,128)(2,1)S(1)}, u32[]{:S(2)}) copy-start(bf16[256,4224]{1,0:T(8,128)(2,1)S(1)} %pad_maximum_fusion.3.refs_2_) | copy-start | bytes 6488068
  110.1 4.1 %copy-start.4 = (bf16[256,4224]{1,0:T(8,128)(2,1)}, bf16[256,4224]{1,0:T(8,128)(2,1)S(1)}, u32[]{:S(2)}) copy-start(bf16[256,4224]{1,0:T(8,128)(2,1)S(1)} %pad_maximum_fusion.4.refs_3_) | copy-start | bytes 6488068
  114.2 11.7 %collective-permute-start.24 = (f32[264,1024]{1,0:T(8,128)S(1)}, f32[264,1024]{1,0:T(8,128)}, u32[]{:S(2)}, u32[]{:S(2)}) collective-permute-start(f32[264,1024]{1,0:T(8,128)S(1)} %gram.3), channel_id=1, source_target_pairs={{0,4},{4,0},{1,5},{5,1},{2,6},{6,2},{3,7},{7,3},{8,12},{12,8},{9,1... | collective-permute-start | bytes 3244040 | tf_op jit(solution)/shard_map/ppermute | solution.py:286
  115.5 1.6 %copy-start.1 = (bf16[256,4224]{1,0:T(8,128)(2,1)S(1)}, bf16[256,4224]{1,0:T(8,128)(2,1)}, u32[]{:S(2)}) copy-start(bf16[256,4224]{1,0:T(8,128)(2,1)} %copy-done) | copy-start | bytes 6488068
  117.1 1.6 %copy-start.3 = (bf16[256,4224]{1,0:T(8,128)(2,1)S(1)}, bf16[256,4224]{1,0:T(8,128)(2,1)}, u32[]{:S(2)}) copy-start(bf16[256,4224]{1,0:T(8,128)(2,1)} %copy-done.2) | copy-start | bytes 6488068
  118.7 1.6 %copy-start.5 = (bf16[256,4224]{1,0:T(8,128)(2,1)S(1)}, bf16[256,4224]{1,0:T(8,128)(2,1)}, u32[]{:S(2)}) copy-start(bf16[256,4224]{1,0:T(8,128)(2,1)} %copy-done.4) | copy-start | bytes 6488068
  120.3 1.6 %copy-start.7 = (bf16[256,4224]{1,0:T(8,128)(2,1)S(1)}, bf16[256,4224]{1,0:T(8,128)(2,1)}, u32[]{:S(2)}) copy-start(bf16[256,4224]{1,0:T(8,128)(2,1)} %copy-done.6) | copy-start | bytes 6488068

commit v22 on v20

--- a/solution.py
+++ b/solution.py
@@ -174,51 +174,46 @@
     )(value, *after)
 
 
-def gram_kernel(blocks, rows_ref, *refs):
-    streams, (own_ref, given_ref, cols_ref) = refs[:4], refs[4:]
+def gram_kernel(rows_ref, *refs):
+    streams, (out_ref, cols_ref) = refs[:4], refs[4:]
     lane = lax.broadcasted_iota(jnp.int32, (16, 128), 1)
     terms = jnp.where(lane < 3, 1.0, 0.0).astype(bf16)
-    for n, x in enumerate(blocks):
+    for x in range(4):
         for z in range(4):
             for s in range(4):
                 at = (z if s < 2 else z ^ 2) * PIECE + s * 16
                 first = slot_of(s, x, z) * 16
-                cols_ref[n * 256 + at : n * 256 + at + 16, :] = streams[s][first : first + 16, :]
-        inside = slice(n * 256, (n + 1) * 256)
-        product = lax.dot_general(
+                cols_ref[x % 2, at : at + 16, :] = streams[s][first : first + 16, :]
+        inside = slice(x * 256, (x + 1) * 256)
+        out_ref[:256, inside] = lax.dot_general(
             rows_ref[:, :LIVE],
-            cols_ref[inside, :LIVE],
+            cols_ref[x % 2, :, :LIVE],
             (((1,), (1,)), ((), ())),
             preferred_element_type=f32,
         )
-        own_ref[:256, inside] = product[:256]
-        given_ref[:256, inside] = product[256:]
-        sums = lax.dot_general(
-            terms, cols_ref[inside, LIVE:], (((1,), (1,)), ((), ())), preferred_element_type=f32
-        )
-        own_ref[256:, inside] = sums[:8]
-        given_ref[256:, inside] = sums[:8]
-
-
-def gram(blocks, rows, streams):
-    vmem = pl.BlockSpec(memory_space=pltpu.VMEM)
-    width = 256 * len(blocks)
-    return pl.pallas_call(
-        lambda *refs: gram_kernel(blocks, *refs),
-        out_shape=(jax.ShapeDtypeStruct((264, width), f32),) * 2,
+        out_ref[256:, inside] = lax.dot_general(
+            terms, cols_ref[x % 2, :, LIVE:], (((1,), (1,)), ((), ())), preferred_element_type=f32
+        )[:8]
+
+
+def gram(rows, streams):
+    vmem = pl.BlockSpec(memory_space=pltpu.VMEM)
+    return pl.pallas_call(
+        gram_kernel,
+        out_shape=jax.ShapeDtypeStruct((264, 1024), f32),
         in_specs=[vmem] * 5,
-        out_specs=(vmem,) * 2,
-        scratch_shapes=[pltpu.VMEM((width, LONG), bf16)],
-        compiler_params=params(10),
+        out_specs=vmem,
+        scratch_shapes=[pltpu.VMEM((2, 256, LONG), bf16)],
+        compiler_params=params(8),
         cost_estimate=pl.CostEstimate(
-            flops=2 * 512 * width * LIVE, bytes_accessed=6 * 1024 * 1024, transcendentals=0
+            flops=2 * 256 * 1024 * LIVE, bytes_accessed=10 * 1024 * 1024, transcendentals=0
         ),
         name="gram",
     )(rows, *streams)
 
 
 def finish_kernel(info_ref, part_ref, *refs):
-    own, got, (mean_ref, out_ref) = refs[:2], refs[2:4], refs[4:]
+    own_ref, got_ref, mean_ref, out_ref = refs
     core, row_block, col_block = info_ref[0], info_ref[1], info_ref[2]
     part = part_ref[0]
 
@@ -241,9 +236,9 @@
             out_ref[:, pl.ds(at, 256)] = jnp.zeros((256, 256), f32)
 
     for x in range(4):
-        inside = slice(x % 2 * 256, (x % 2 + 1) * 256)
-        put(own[x // 2], inside, x * 2 + core)
-        put(got[x // 2], inside, x * 2 + 1 - core)
+        inside = slice(x * 256, (x + 1) * 256)
+        put(own_ref, inside, x * 2 + core)
+        put(got_ref, inside, x * 2 + 1 - core)
 
 
 def finish(info, part, own, got):
@@ -254,11 +249,11 @@
             jax.ShapeDtypeStruct((1, WIDTH), f32),
             jax.ShapeDtypeStruct((256, WIDTH), f32),
         ),
-        in_specs=[pl.BlockSpec(memory_space=pltpu.SMEM)] * 2 + [vmem] * 4,
+        in_specs=[pl.BlockSpec(memory_space=pltpu.SMEM)] * 2 + [vmem] * 2,
         out_specs=(vmem,) * 2,
         compiler_params=params(10),
         name="finish",
-    )(info, part, *own, *got)
+    )(info, part, own, got)
 
 
 def swap(value):
@@ -311,13 +306,8 @@
         if step == 2:
             rows = meet(behind(rows, streams[:1]), "y", 3, side(y ^ z, 3, False))
 
-    rows = join(rows, swap(rows))
-
-    own, got = [], []
-    for blocks in ((0, 1), (2, 3)):
-        kept, given = gram(blocks, rows, streams)
-        own.append(kept)
-        got.append(swap(given))
+    got = swap(gram(swap(rows), streams))
+    own = gram(rows, streams)
     info = jnp.stack([c, z * 8 + x * 2 + c, y * 8]).astype(jnp.int32)
     mean, gram_factor = finish(info, part[None], own, got)
     return (mean[0], gram_factor)

time: 122 us -> 129 us (1.057)
  local copies, waits for them, and re-layouts: 2.05 us -> 8.5 us
  starting transfers between devices: 36.7 us -> 31 us
  waiting for transfers between devices: 36.7 us -> 42.2 us
    ppermute x21, starting transfers between devices: 29.2 us -> 20.4 us  [trade(): return lax.ppermute(value, axis, [(i, i ^ flip) for i in range(4)])]
    unnamed x4 -> x20, local copies, waits for them, and re-layouts: 1.59 us -> 8.04 us
    ppermute x21, waiting for transfers between devices: 33.5 us -> 38.7 us  [trade(): return lax.ppermute(value, axis, [(i, i ^ flip) for i in range(4)])]
    ppermute x2, starting transfers between devices: 2.59 us -> 5.94 us  [send(): lax.ppermute(half, ('z', 'y'), [(q * 4 + u, u * 4 + (q ^ u ^ turn)) for q...]
    ppermute x2, waiting for transfers between devices: 0.01 us -> 1.8 us  [send(): lax.ppermute(half, ('z', 'y'), [(q * 4 + u, u * 4 + (q ^ u ^ turn)) for q...]
    ppermute x3 -> x2, waiting for transfers between devices: 3.21 us -> 1.71 us  [swap(): return lax.ppermute(value, 'c', [(0, 1), (1, 0)])]
    ppermute x3 -> x2, starting transfers between devices: 4.86 us -> 4.72 us  [swap(): return lax.ppermute(value, 'c', [(0, 1), (1, 0)])]
  transfers between devices with their start and end apart: 26 -> 25, of which waited for: 12 -> 11; matrix products, arithmetic and copies ran while one was open for 4% -> 4% of each run, Pallas kernels for 0% -> 2%
where the time goes in v22:
time: 129 us
  waiting for transfers between devices  42.2 us (33%)
  starting transfers between devices  31 us (24%)
  blocking collectives  27 us (21%)
  Pallas kernels  11.2 us (9%)
  local copies, waits for them, and re-layouts  8.5 us (7%)
  other arithmetic  6.81 us (5%)
  between operations  1.79 us (1%)
    ppermute x21, waiting for transfers between devices, trade(): return lax.ppermute(value, axis, [(i, i ^ flip) for i in range(4)])  38.7 us
    all_to_all x1, blocking collectives, per_device(): pieces = lax.all_to_all(pieces, TOK, 0, 0, tiled=True)  27 us
    ppermute x21, starting transfers between devices, trade(): return lax.ppermute(value, axis, [(i, i ^ flip) for i in range(4)])  20.4 us
    unnamed x20, local copies, waits for them, and re-layouts  8.04 us
    ppermute x2, starting transfers between devices, send(): lax.ppermute(half, ('z', 'y'), [(q * 4 + u, u * 4 + (q ^ u ^ turn)) for q...  5.94 us
    pallas_call x2, Pallas kernels, gram(): pl.pallas_call(gram_kernel, out_shape=jax.ShapeDtypeStruct((264, 1024), f...  4.96 us
    ppermute x2, starting transfers between devices, swap(): return lax.ppermute(value, 'c', [(0, 1), (1, 0)])  4.72 us
    select_n x18, other arithmetic, meet(): jnp.where(which == 0, value, got)  3.09 us
  transfers between devices with their start and end apart: 25, of which 11 were waited for; matrix products, arithmetic and copies ran while one was open for 4% of the time, Pallas kernels for 2%

profile of v22, /device:TPU:1, one launch (start us, length us, event | category | flops | bytes accessed | tf_op | source)
XLA Modules:
  0.0 128.6 jit_solution(2075057193185399785)
XLA Ops:
  0.6 0.8 pad_add_fusion
  1.4 1.6 %copy-done.8 = bf16[512,2048]{1,0:T(8,128)(2,1)S(1)} copy-done((bf16[512,2048]{1,0:T(8,128)(2,1)S(1)}, bf16[512,2048]{1,0:T(8,128)(2,1)}, u32[]{:S(2)}) %copy-start.8) | copy-done | bytes 2097176
  3.0 0.8 pick.1
  3.9 3.6 %collective-permute-start.2 = (f32[8,256]{1,0:T(8,128)S(1)}, f32[8,256]{1,0:T(8,128)S(1)}, u32[]{:S(2)}, u32[]{:S(2)}) collective-permute-start(f32[8,256]{1,0:T(8,128)S(1)} %get-tuple-element.13.s0), channel_id=1, source_target_pairs={{0,3},{1,2},{2,1},{3,0},{4,7},{5,6},{6,5},{7,4},{8,11},{9,10},{10,... | collective-permute-start | bytes 24584 | tf_op jit(solution)/shard_map/ppermute | solution.py:264
  7.5 0.4 collective-permute-start.1
  7.9 0.3 collective-permute-start
  8.2 0.4 copy.7.gain_ref
  8.6 3.0 %collective-permute-done.1.s2 = f32[8,256]{1,0:T(8,128)S(1)} collective-permute-done((f32[8,256]{1,0:T(8,128)S(1)}, f32[8,256]{1,0:T(8,128)S(1)}, u32[]{:S(2)}, u32[]{:S(2)}) %collective-permute-start.1) | collective-permute-done | bytes 8224 | tf_op jit(solution)/shard_map/ppermute | solution.py:264
  11.5 0.3 norm.1
  11.9 27.0 %all_to_all.5.in_ref = bf16[32,64,256]{2,1,0:T(8,128)(2,1)S(1)} all-to-all(bf16[32,64,256]{2,1,0:T(8,128)(2,1)S(1)} %norm.1), channel_id=1, replica_groups=mesh['z'=4,'x'=4,'c'=2,'y'=4] {'z','x','c'}, dimensions={0} | all-to-all | bytes 2097152 | tf_op jit(solution)/shard_map/all_to_all | solution.py:282
  38.9 1.3 fusion
  40.4 2.1 %pack.1 = (bf16[32,4224]{1,0:T(8,128)(2,1)S(1)}, bf16[32,4224]{1,0:T(8,128)(2,1)S(1)}, bf16[16,4224]{1,0:T(8,128)(2,1)S(1)}, bf16[16,4224]{1,0:T(8,128)(2,1)S(1)...) custom-call(s32[32]{0:T(128)S(1)} %sub.3.first_ref, bf16[32,64,256]{2,1,0:T(8,128)(2,1)S(1)} %all_to_all.5.in_ref), custom_call_target="tpu_custom_call" | custom-call | tf_op jit(solution)/shard_map/pack/pallas_call | solution.py:149
  42.5 0.4 collective-permute-start.3
  42.9 0.4 collective-permute-start.5
  43.3 1.0 collective-permute-start.6
  44.3 0.6 collective-permute-start.7
  45.0 2.4 %collective-permute-done.3 = bf16[16,4224]{1,0:T(8,128)(2,1)S(1)} collective-permute-done((bf16[16,4224]{1,0:T(8,128)(2,1)S(1)}, bf16[16,4224]{1,0:T(8,128)(2,1)S(1)}, u32[]{:S(2)}, u32[]{:S(2)}) %collective-permute-start.3) | collective-permute-done | bytes 135200 | tf_op jit(solution)/shard_map/ppermute | solution.py:264
  47.6 1.7 %collective-permute-start.10 = (bf16[32,4224]{1,0:T(8,128)(2,1)S(1)}, bf16[32,4224]{1,0:T(8,128)(2,1)S(1)}, u32[]{:S(2)}, u32[]{:S(2)}) collective-permute-start(bf16[32,4224]{1,0:T(8,128)(2,1)S(1)} %get-tuple-element.61.refs_1_), channel_id=1, source_target_pairs={{0,24},{8,16},{16,8},{24,0},{1,25},{9,17},{17,9},{25,1},{2,26},{10... | collective-permute-start | bytes 811016 | tf_op jit(solution)/shard_map/ppermute | solution.py:264
  49.8 1.3 %collective-permute-start.11 = (bf16[32,4224]{1,0:T(8,128)(2,1)S(1)}, bf16[32,4224]{1,0:T(8,128)(2,1)S(1)}, u32[]{:S(2)}, u32[]{:S(2)}) collective-permute-start(bf16[32,4224]{1,0:T(8,128)(2,1)S(1)} %get-tuple-element.62.refs_2_), channel_id=1, source_target_pairs={{0,96},{32,64},{64,32},{96,0},{1,97},{33,65},{65,33},{97,1},{2,98}... | collective-permute-start | bytes 811016 | tf_op jit(solution)/shard_map/ppermute | solution.py:264
  51.1 0.3 collective-permute-start.12
  51.6 0.7 collective-permute-start.4
  52.3 3.1 %collective-permute-done.10 = bf16[32,4224]{1,0:T(8,128)(2,1)S(1)} collective-permute-done((bf16[32,4224]{1,0:T(8,128)(2,1)S(1)}, bf16[32,4224]{1,0:T(8,128)(2,1)S(1)}, u32[]{:S(2)}, u32[]{:S(2)}) %collective-permute-start.10) | collective-permute-done | bytes 270368 | tf_op jit(solution)/shard_map/ppermute | solution.py:264
  55.4 5.3 %collective-permute-start.8 = (bf16[32,4224]{1,0:T(8,128)(2,1)S(1)}, bf16[32,4224]{1,0:T(8,128)(2,1)S(1)}, u32[]{:S(2)}, u32[]{:S(2)}) collective-permute-start(bf16[32,4224]{1,0:T(8,128)(2,1)S(1)} %behind.5), channel_id=1, source_target_pairs={{0,2},{1,35},{2,64},{3,97},{32,3},{33,34},{34,65},{35,96},{64,0},{... | collective-permute-start | bytes 811016 | tf_op jit(solution)/shard_map/ppermute | solution.py:292
  61.0 1.2 collective-permute-start.14
  62.4 0.7 collective-permute-start.19
  63.2 0.4 collective-permute-start.21
  63.7 1.8 %collective-permute-done.8 = bf16[32,4224]{1,0:T(8,128)(2,1)S(1)} collective-permute-done((bf16[32,4224]{1,0:T(8,128)(2,1)S(1)}, bf16[32,4224]{1,0:T(8,128)(2,1)S(1)}, u32[]{:S(2)}, u32[]{:S(2)}) %collective-permute-start.8) | collective-permute-done | bytes 270368 | tf_op jit(solution)/shard_map/ppermute | solution.py:292
  65.6 1.5 %collective-permute-start.13 = (bf16[64,4224]{1,0:T(8,128)(2,1)S(1)}, bf16[64,4224]{1,0:T(8,128)(2,1)S(1)}, u32[]{:S(2)}, u32[]{:S(2)}) collective-permute-start(bf16[64,4224]{1,0:T(8,128)(2,1)S(1)} %behind.6), channel_id=1, source_target_pairs={{0,1},{1,0},{2,3},{3,2},{4,5},{5,4},{6,7},{7,6},{8,9},{9,8},{10,11... | collective-permute-start | bytes 1622024 | tf_op jit(solution)/shard_map/ppermute | solution.py:264
  67.0 6.3 %collective-permute-done.14 = bf16[64,4224]{1,0:T(8,128)(2,1)S(1)} collective-permute-done((bf16[64,4224]{1,0:T(8,128)(2,1)S(1)}, bf16[64,4224]{1,0:T(8,128)(2,1)S(1)}, u32[]{:S(2)}, u32[]{:S(2)}) %collective-permute-start.14) | collective-permute-done | bytes 540704 | tf_op jit(solution)/shard_map/ppermute | solution.py:264
  73.7 2.5 %collective-permute-start.16 = (bf16[128,4224]{1,0:T(8,128)(2,1)S(1)}, bf16[128,4224]{1,0:T(8,128)(2,1)S(1)}, u32[]{:S(2)}, u32[]{:S(2)}) collective-permute-start(bf16[128,4224]{1,0:T(8,128)(2,1)S(1)} %pad_maximum_fusion.6.refs_0_), channel_id=1, source_target_pairs={{0,96},{32,64},{64,32},{96,0},{1,97},{33,65},{65,33},{97,1},{2,98}... | collective-permute-start | bytes 3244040 | tf_op jit(solution)/shard_map/ppermute | solution.py:264
  76.4 2.9 %collective-permute-done.17 = bf16[64,4224]{1,0:T(8,128)(2,1)S(1)} collective-permute-done((bf16[64,4224]{1,0:T(8,128)(2,1)S(1)}, bf16[64,4224]{1,0:T(8,128)(2,1)S(1)}, u32[]{:S(2)}, u32[]{:S(2)}) %collective-permute-start.17) | collective-permute-done | bytes 540704 | tf_op jit(solution)/shard_map/ppermute | solution.py:264
  80.0 1.1 collective-permute-start.20
  81.3 2.6 %collective-permute-start.22 = (bf16[128,4224]{1,0:T(8,128)(2,1)S(1)}, bf16[128,4224]{1,0:T(8,128)(2,1)S(1)}, u32[]{:S(2)}, u32[]{:S(2)}) collective-permute-start(bf16[128,4224]{1,0:T(8,128)(2,1)S(1)} %pad_maximum_fusion.9), channel_id=1, source_target_pairs={{0,24},{8,16},{16,8},{24,0},{1,25},{9,17},{17,9},{25,1},{2,26},{10... | collective-permute-start | bytes 3244040 | tf_op jit(solution)/shard_map/ppermute | solution.py:264
  83.9 20.6 %collective-permute-done.15 = bf16[128,4224]{1,0:T(8,128)(2,1)S(1)} collective-permute-done((bf16[128,4224]{1,0:T(8,128)(2,1)S(1)}, bf16[128,4224]{1,0:T(8,128)(2,1)S(1)}, u32[]{:S(2)}, u32[]{:S(2)}) %collective-permute-start.15) | collective-permute-done | bytes 1081376 | tf_op jit(solution)/shard_map/ppermute | solution.py:264
  104.9 4.3 %collective-permute-start.23 = (bf16[256,4224]{1,0:T(8,128)(2,1)S(1)}, bf16[256,4224]{1,0:T(8,128)(2,1)S(1)}, u32[]{:S(2)}, u32[]{:S(2)}) collective-permute-start(bf16[256,4224]{1,0:T(8,128)(2,1)S(1)} %pad_maximum_fusion.rows_ref), channel_id=1, source_target_pairs={{0,4},{4,0},{1,5},{5,1},{2,6},{6,2},{3,7},{7,3},{8,12},{12,8},{9,1... | collective-permute-start | bytes 6488072 | tf_op jit(solution)/shard_map/ppermute | solution.py:260
  109.2 0.4 broadcast_select_fusion.5
  109.7 0.4 broadcast_select_fusion.3
  110.1 0.4 broadcast_select_fusion.1
  110.8 0.4 broadcast_select_fusion.7
  111.3 1.7 %collective-permute-done.23.rows_ref = bf16[256,4224]{1,0:T(8,128)(2,1)S(1)} collective-permute-done((bf16[256,4224]{1,0:T(8,128)(2,1)S(1)}, bf16[256,4224]{1,0:T(8,128)(2,1)S(1)}, u32[]{:S(2)}, u32[]{:S(2)}) %collective-permute-start.23) | collective-permute-done | bytes 2162720 | tf_op jit(solution)/shard_map/ppermute | solution.py:260
  113.1 2.5 %gram.3 = f32[264,1024]{1,0:T(8,128)S(1)} custom-call(bf16[256,4224]{1,0:T(8,128)(2,1)S(1)} %collective-permute-done.23.rows_ref, bf16[256,4224]{1,0:T(8,128)(2,1)S(1)} %pad_maximum_fusion.1.refs_0_, bf16[256,4224]{1,0:T(8,128)(2,1)S(1)} %pad_maximum_fusion.2.refs_1_, bf16[256,4224]{1,0:T(8,128)(2,1)S(1)} %pad_maximum_fusion.3.refs_2_, ...), custom_call_target="tpu_custom_call" | custom-call | flops 2147483648 | bytes 10485760 | tf_op jit(solution)/shard_map/gram/pallas_call | solution.py:201
  115.6 0.5 collective-permute-start.24
  116.8 1.6 %copy-done.1 = bf16[256,4224]{1,0:T(8,128)(2,1)S(1)} copy-done((bf16[256,4224]{1,0:T(8,128)(2,1)S(1)}, bf16[256,4224]{1,0:T(8,128)(2,1)}, u32[]{:S(2)}) %copy-start.1) | copy-done | bytes 2162712
  118.4 1.6 %copy-done.3 = bf16[256,4224]{1,0:T(8,128)(2,1)S(1)} copy-done((bf16[256,4224]{1,0:T(8,128)(2,1)S(1)}, bf16[256,4224]{1,0:T(8,128)(2,1)}, u32[]{:S(2)}) %copy-start.3) | copy-done | bytes 2162712
  120.0 1.6 %copy-done.5 = bf16[256,4224]{1,0:T(8,128)(2,1)S(1)} copy-done((bf16[256,4224]{1,0:T(8,128)(2,1)S(1)}, bf16[256,4224]{1,0:T(8,128)(2,1)}, u32[]{:S(2)}) %copy-start.5) | copy-done | bytes 2162712
  121.7 1.6 %copy-done.7 = bf16[256,4224]{1,0:T(8,128)(2,1)S(1)} copy-done((bf16[256,4224]{1,0:T(8,128)(2,1)S(1)}, bf16[256,4224]{1,0:T(8,128)(2,1)}, u32[]{:S(2)}) %copy-start.7) | copy-done | bytes 2162712
  123.3 2.5 %gram.2.refs_0_ = f32[264,1024]{1,0:T(8,128)S(1)} custom-call(bf16[256,4224]{1,0:T(8,128)(2,1)S(1)} %copy-done.7, bf16[256,4224]{1,0:T(8,128)(2,1)S(1)} %copy-done.5, bf16[256,4224]{1,0:T(8,128)(2,1)S(1)} %pad_maximum_fusion.2.refs_1_, bf16[256,4224]{1,0:T(8,128)(2,1)S(1)} %copy-done.1, bf16[256,4224]{1,0:T(8,128)(2,1)S(1)} %copy-done.3), custom_call_target="tpu_custom_call" | custom-call | flops 2147483648 | bytes 10485760 | tf_op jit(solution)/shard_map/gram/pallas_call | solution.py:201
  125.7 2.8 %finish.1 = (f32[1,2048]{1,0:T(1,128)}, f32[256,2048]{1,0:T(8,128)}) custom-call(s32[3]{0:T(128)S(1)} %pad_add_fusion.1.info_ref, f32[1]{0:T(128)} %bitcast.4.part_ref, f32[264,1024]{1,0:T(8,128)S(1)} %gram.2.refs_0_, f32[264,1024]{1,0:T(8,128)} %collective-permute-done.24.refs_1_), custom_call_target="tpu_custom_call" | custom-call | tf_op jit(solution)/shard_map/finish/pallas_call | solution.py:246
  (78 shorter events, 4.4 us)
Async XLA Ops:
  0.6 7.6 %copy-start.9 = (f32[2048]{0:T(1024)S(1)}, f32[2048]{0:T(1024)}, u32[]{:S(2)}) copy-start(f32[2048]{0:T(1024)} %param.5) | copy-start | bytes 24580
  1.4 1.6 %copy-start.8 = (bf16[512,2048]{1,0:T(8,128)(2,1)S(1)}, bf16[512,2048]{1,0:T(8,128)(2,1)}, u32[]{:S(2)}) copy-start(bf16[512,2048]{1,0:T(8,128)(2,1)} %resid_ref.1) | copy-start | bytes 6291460
  3.9 4.7 %collective-permute-start.2 = (f32[8,256]{1,0:T(8,128)S(1)}, f32[8,256]{1,0:T(8,128)S(1)}, u32[]{:S(2)}, u32[]{:S(2)}) collective-permute-start(f32[8,256]{1,0:T(8,128)S(1)} %get-tuple-element.13.s0), channel_id=1, source_target_pairs={{0,3},{1,2},{2,1},{3,0},{4,7},{5,6},{6,5},{7,4},{8,11},{9,10},{10,... | collective-permute-start | bytes 24584 | tf_op jit(solution)/shard_map/ppermute | solution.py:264
  7.5 4.0 %collective-permute-start.1 = (f32[8,256]{1,0:T(8,128)S(1)}, f32[8,256]{1,0:T(8,128)S(1)}, u32[]{:S(2)}, u32[]{:S(2)}) collective-permute-start(f32[8,256]{1,0:T(8,128)S(1)} %get-tuple-element.13.s0), channel_id=1, source_target_pairs={{0,2},{1,3},{2,0},{3,1},{4,6},{5,7},{6,4},{7,5},{8,10},{9,11},{10,... | collective-permute-start | bytes 24584 | tf_op jit(solution)/shard_map/ppermute | solution.py:264
  7.9 3.7 %collective-permute-start = (f32[8,256]{1,0:T(8,128)S(1)}, f32[8,256]{1,0:T(8,128)S(1)}, u32[]{:S(2)}, u32[]{:S(2)}) collective-permute-start(f32[8,256]{1,0:T(8,128)S(1)} %get-tuple-element.13.s0), channel_id=1, source_target_pairs={{0,1},{1,0},{2,3},{3,2},{4,5},{5,4},{6,7},{7,6},{8,9},{9,8},{10,11... | collective-permute-start | bytes 24584 | tf_op jit(solution)/shard_map/ppermute | solution.py:264
  42.5 4.9 %collective-permute-start.3 = (bf16[16,4224]{1,0:T(8,128)(2,1)S(1)}, bf16[16,4224]{1,0:T(8,128)(2,1)S(1)}, u32[]{:S(2)}, u32[]{:S(2)}) collective-permute-start(bf16[16,4224]{1,0:T(8,128)(2,1)S(1)} %get-tuple-element.15), channel_id=1, source_target_pairs={{0,8},{8,0},{16,24},{24,16},{1,9},{9,1},{17,25},{25,17},{2,10},{10... | collective-permute-start | bytes 405512 | tf_op jit(solution)/shard_map/ppermute | solution.py:264
  42.9 4.5 %collective-permute-start.5 = (bf16[16,4224]{1,0:T(8,128)(2,1)S(1)}, bf16[16,4224]{1,0:T(8,128)(2,1)S(1)}, u32[]{:S(2)}, u32[]{:S(2)}) collective-permute-start(bf16[16,4224]{1,0:T(8,128)(2,1)S(1)} %get-tuple-element.17), channel_id=1, source_target_pairs={{0,32},{32,0},{64,96},{96,64},{1,33},{33,1},{65,97},{97,65},{2,34}... | collective-permute-start | bytes 405512 | tf_op jit(solution)/shard_map/ppermute | solution.py:264
  43.3 6.2 %collective-permute-start.6 = (bf16[16,4224]{1,0:T(8,128)(2,1)S(1)}, bf16[16,4224]{1,0:T(8,128)(2,1)S(1)}, u32[]{:S(2)}, u32[]{:S(2)}) collective-permute-start(bf16[16,4224]{1,0:T(8,128)(2,1)S(1)} %get-tuple-element.18), channel_id=1, source_target_pairs={{0,24},{8,16},{16,8},{24,0},{1,25},{9,17},{17,9},{25,1},{2,26},{10... | collective-permute-start | bytes 405512 | tf_op jit(solution)/shard_map/ppermute | solution.py:264
  44.3 5.4 %collective-permute-start.7 = (bf16[16,4224]{1,0:T(8,128)(2,1)S(1)}, bf16[16,4224]{1,0:T(8,128)(2,1)S(1)}, u32[]{:S(2)}, u32[]{:S(2)}) collective-permute-start(bf16[16,4224]{1,0:T(8,128)(2,1)S(1)} %get-tuple-element.19), channel_id=1, source_target_pairs={{0,96},{32,64},{64,32},{96,0},{1,97},{33,65},{65,33},{97,1},{2,98}... | collective-permute-start | bytes 405512 | tf_op jit(solution)/shard_map/ppermute | solution.py:264
  47.6 7.8 %collective-permute-start.10 = (bf16[32,4224]{1,0:T(8,128)(2,1)S(1)}, bf16[32,4224]{1,0:T(8,128)(2,1)S(1)}, u32[]{:S(2)}, u32[]{:S(2)}) collective-permute-start(bf16[32,4224]{1,0:T(8,128)(2,1)S(1)} %get-tuple-element.61.refs_1_), channel_id=1, source_target_pairs={{0,24},{8,16},{16,8},{24,0},{1,25},{9,17},{17,9},{25,1},{2,26},{10... | collective-permute-start | bytes 811016 | tf_op jit(solution)/shard_map/ppermute | solution.py:264
  49.8 11.2 %collective-permute-start.11 = (bf16[32,4224]{1,0:T(8,128)(2,1)S(1)}, bf16[32,4224]{1,0:T(8,128)(2,1)S(1)}, u32[]{:S(2)}, u32[]{:S(2)}) collective-permute-start(bf16[32,4224]{1,0:T(8,128)(2,1)S(1)} %get-tuple-element.62.refs_2_), channel_id=1, source_target_pairs={{0,96},{32,64},{64,32},{96,0},{1,97},{33,65},{65,33},{97,1},{2,98}... | collective-permute-start | bytes 811016 | tf_op jit(solution)/shard_map/ppermute | solution.py:264
  51.1 11.3 %collective-permute-start.12 = (bf16[32,4224]{1,0:T(8,128)(2,1)S(1)}, bf16[32,4224]{1,0:T(8,128)(2,1)S(1)}, u32[]{:S(2)}, u32[]{:S(2)}) collective-permute-start(bf16[32,4224]{1,0:T(8,128)(2,1)S(1)} %get-tuple-element.63.refs_3_), channel_id=1, source_target_pairs={{0,8},{8,0},{16,24},{24,16},{1,9},{9,1},{17,25},{25,17},{2,10},{10... | collective-permute-start | bytes 811016 | tf_op jit(solution)/shard_map/ppermute | solution.py:264
  51.4 9.3 %collective-permute-start.9 = (bf16[32,4224]{1,0:T(8,128)(2,1)S(1)}, bf16[32,4224]{1,0:T(8,128)(2,1)S(1)}, u32[]{:S(2)}, u32[]{:S(2)}) collective-permute-start(bf16[32,4224]{1,0:T(8,128)(2,1)S(1)} %get-tuple-element.60.refs_0_), channel_id=1, source_target_pairs={{0,32},{32,0},{64,96},{96,64},{1,33},{33,1},{65,97},{97,65},{2,34}... | collective-permute-start | bytes 811016 | tf_op jit(solution)/shard_map/ppermute | solution.py:264
  51.6 11.6 %collective-permute-start.4 = (bf16[32,4224]{1,0:T(8,128)(2,1)S(1)}, bf16[32,4224]{1,0:T(8,128)(2,1)S(1)}, u32[]{:S(2)}, u32[]{:S(2)}) collective-permute-start(bf16[32,4224]{1,0:T(8,128)(2,1)S(1)} %behind.4), channel_id=1, source_target_pairs={{0,0},{1,33},{2,66},{3,99},{32,1},{33,32},{34,67},{35,98},{64,2},{... | collective-permute-start | bytes 811016 | tf_op jit(solution)/shard_map/ppermute | solution.py:292
  55.4 10.1 %collective-permute-start.8 = (bf16[32,4224]{1,0:T(8,128)(2,1)S(1)}, bf16[32,4224]{1,0:T(8,128)(2,1)S(1)}, u32[]{:S(2)}, u32[]{:S(2)}) collective-permute-start(bf16[32,4224]{1,0:T(8,128)(2,1)S(1)} %behind.5), channel_id=1, source_target_pairs={{0,2},{1,35},{2,64},{3,97},{32,3},{33,34},{34,65},{35,96},{64,0},{... | collective-permute-start | bytes 811016 | tf_op jit(solution)/shard_map/ppermute | solution.py:292
  60.8 18.5 %collective-permute-start.17 = (bf16[64,4224]{1,0:T(8,128)(2,1)S(1)}, bf16[64,4224]{1,0:T(8,128)(2,1)S(1)}, u32[]{:S(2)}, u32[]{:S(2)}) collective-permute-start(bf16[64,4224]{1,0:T(8,128)(2,1)S(1)} %pad_maximum_fusion.12.refs_1_), channel_id=1, source_target_pairs={{0,96},{32,64},{64,32},{96,0},{1,97},{33,65},{65,33},{97,1},{2,98}... | collective-permute-start | bytes 1622024 | tf_op jit(solution)/shard_map/ppermute | solution.py:264
  61.0 12.3 %collective-permute-start.14 = (bf16[64,4224]{1,0:T(8,128)(2,1)S(1)}, bf16[64,4224]{1,0:T(8,128)(2,1)S(1)}, u32[]{:S(2)}, u32[]{:S(2)}) collective-permute-start(bf16[64,4224]{1,0:T(8,128)(2,1)S(1)} %pad_maximum_fusion.11.refs_0_), channel_id=1, source_target_pairs={{0,24},{8,16},{16,8},{24,0},{1,25},{9,17},{17,9},{25,1},{2,26},{10... | collective-permute-start | bytes 1622024 | tf_op jit(solution)/shard_map/ppermute | solution.py:264
  62.4 17.3 %collective-permute-start.19 = (bf16[64,4224]{1,0:T(8,128)(2,1)S(1)}, bf16[64,4224]{1,0:T(8,128)(2,1)S(1)}, u32[]{:S(2)}, u32[]{:S(2)}) collective-permute-start(bf16[64,4224]{1,0:T(8,128)(2,1)S(1)} %pad_maximum_fusion.13.refs_2_), channel_id=1, source_target_pairs={{0,8},{8,0},{16,24},{24,16},{1,9},{9,1},{17,25},{25,17},{2,10},{10... | collective-permute-start | bytes 1622024 | tf_op jit(solution)/shard_map/ppermute | solution.py:264
  63.2 17.8 %collective-permute-start.21 = (bf16[64,4224]{1,0:T(8,128)(2,1)S(1)}, bf16[64,4224]{1,0:T(8,128)(2,1)S(1)}, u32[]{:S(2)}, u32[]{:S(2)}) collective-permute-start(bf16[64,4224]{1,0:T(8,128)(2,1)S(1)} %pad_maximum_fusion.14.refs_3_), channel_id=1, source_target_pairs={{0,32},{32,0},{64,96},{96,64},{1,33},{33,1},{65,97},{97,65},{2,34}... | collective-permute-start | bytes 1622024 | tf_op jit(solution)/shard_map/ppermute | solution.py:264
  65.6 10.6 %collective-permute-start.13 = (bf16[64,4224]{1,0:T(8,128)(2,1)S(1)}, bf16[64,4224]{1,0:T(8,128)(2,1)S(1)}, u32[]{:S(2)}, u32[]{:S(2)}) collective-permute-start(bf16[64,4224]{1,0:T(8,128)(2,1)S(1)} %behind.6), channel_id=1, source_target_pairs={{0,1},{1,0},{2,3},{3,2},{4,5},{5,4},{6,7},{7,6},{8,9},{9,8},{10,11... | collective-permute-start | bytes 1622024 | tf_op jit(solution)/shard_map/ppermute | solution.py:264
  73.7 37.1 %collective-permute-start.16 = (bf16[128,4224]{1,0:T(8,128)(2,1)S(1)}, bf16[128,4224]{1,0:T(8,128)(2,1)S(1)}, u32[]{:S(2)}, u32[]{:S(2)}) collective-permute-start(bf16[128,4224]{1,0:T(8,128)(2,1)S(1)} %pad_maximum_fusion.6.refs_0_), channel_id=1, source_target_pairs={{0,96},{32,64},{64,32},{96,0},{1,97},{33,65},{65,33},{97,1},{2,98}... | collective-permute-start | bytes 3244040 | tf_op jit(solution)/shard_map/ppermute | solution.py:264
  79.6 29.6 %collective-permute-start.18 = (bf16[128,4224]{1,0:T(8,128)(2,1)S(1)}, bf16[128,4224]{1,0:T(8,128)(2,1)S(1)}, u32[]{:S(2)}, u32[]{:S(2)}) collective-permute-start(bf16[128,4224]{1,0:T(8,128)(2,1)S(1)} %pad_maximum_fusion.7), channel_id=1, source_target_pairs={{0,8},{8,0},{16,24},{24,16},{1,9},{9,1},{17,25},{25,17},{2,10},{10... | collective-permute-start | bytes 3244040 | tf_op jit(solution)/shard_map/ppermute | solution.py:264
  80.0 29.8 %collective-permute-start.20 = (bf16[128,4224]{1,0:T(8,128)(2,1)S(1)}, bf16[128,4224]{1,0:T(8,128)(2,1)S(1)}, u32[]{:S(2)}, u32[]{:S(2)}) collective-permute-start(bf16[128,4224]{1,0:T(8,128)(2,1)S(1)} %pad_maximum_fusion.8), channel_id=1, source_target_pairs={{0,32},{32,0},{64,96},{96,64},{1,33},{33,1},{65,97},{97,65},{2,34}... | collective-permute-start | bytes 3244040 | tf_op jit(solution)/shard_map/ppermute | solution.py:264
  81.0 23.5 %collective-permute-start.15 = (bf16[128,4224]{1,0:T(8,128)(2,1)S(1)}, bf16[128,4224]{1,0:T(8,128)(2,1)S(1)}, u32[]{:S(2)}, u32[]{:S(2)}) collective-permute-start(bf16[128,4224]{1,0:T(8,128)(2,1)S(1)} %behind.7), channel_id=1, source_target_pairs={{0,3},{1,2},{2,1},{3,0},{4,7},{5,6},{6,5},{7,4},{8,11},{9,10},{10,... | collective-permute-start | bytes 3244040 | tf_op jit(solution)/shard_map/ppermute | solution.py:264
  81.3 28.8 %collective-permute-start.22 = (bf16[128,4224]{1,0:T(8,128)(2,1)S(1)}, bf16[128,4224]{1,0:T(8,128)(2,1)S(1)}, u32[]{:S(2)}, u32[]{:S(2)}) collective-permute-start(bf16[128,4224]{1,0:T(8,128)(2,1)S(1)} %pad_maximum_fusion.9), channel_id=1, source_target_pairs={{0,24},{8,16},{16,8},{24,0},{1,25},{9,17},{17,9},{25,1},{2,26},{10... | collective-permute-start | bytes 3244040 | tf_op jit(solution)/shard_map/ppermute | solution.py:264
  104.9 4.6 %copy-start.6 = (bf16[256,4224]{1,0:T(8,128)(2,1)}, bf16[256,4224]{1,0:T(8,128)(2,1)S(1)}, u32[]{:S(2)}) copy-start(bf16[256,4224]{1,0:T(8,128)(2,1)S(1)} %pad_maximum_fusion.rows_ref) | copy-start | bytes 6488068
  104.9 8.1 %collective-permute-start.23 = (bf16[256,4224]{1,0:T(8,128)(2,1)S(1)}, bf16[256,4224]{1,0:T(8,128)(2,1)S(1)}, u32[]{:S(2)}, u32[]{:S(2)}) collective-permute-start(bf16[256,4224]{1,0:T(8,128)(2,1)S(1)} %pad_maximum_fusion.rows_ref), channel_id=1, source_target_pairs={{0,4},{4,0},{1,5},{5,1},{2,6},{6,2},{3,7},{7,3},{8,12},{12,8},{9,1... | collective-permute-start | bytes 6488072 | tf_op jit(solution)/shard_map/ppermute | solution.py:260
  110.6 2.4 %copy-start = (bf16[256,4224]{1,0:T(8,128)(2,1)}, bf16[256,4224]{1,0:T(8,128)(2,1)S(1)}, u32[]{:S(2)}) copy-start(bf16[256,4224]{1,0:T(8,128)(2,1)S(1)} %pad_maximum_fusion.3.refs_2_) | copy-start | bytes 6488068
  110.8 2.3 %copy-start.2 = (bf16[256,4224]{1,0:T(8,128)(2,1)}, bf16[256,4224]{1,0:T(8,128)(2,1)S(1)}, u32[]{:S(2)}) copy-start(bf16[256,4224]{1,0:T(8,128)(2,1)S(1)} %pad_maximum_fusion.4.refs_3_) | copy-start | bytes 6488068
  111.3 4.2 %copy-start.4 = (bf16[256,4224]{1,0:T(8,128)(2,1)}, bf16[256,4224]{1,0:T(8,128)(2,1)S(1)}, u32[]{:S(2)}) copy-start(bf16[256,4224]{1,0:T(8,128)(2,1)S(1)} %pad_maximum_fusion.1.refs_0_) | copy-start | bytes 6488068
  115.6 10.1 %collective-permute-start.24 = (f32[264,1024]{1,0:T(8,128)S(1)}, f32[264,1024]{1,0:T(8,128)}, u32[]{:S(2)}, u32[]{:S(2)}) collective-permute-start(f32[264,1024]{1,0:T(8,128)S(1)} %gram.3), channel_id=1, source_target_pairs={{0,4},{4,0},{1,5},{5,1},{2,6},{6,2},{3,7},{7,3},{8,12},{12,8},{9,1... | collective-permute-start | bytes 3244040 | tf_op jit(solution)/shard_map/ppermute | solution.py:260
  116.8 1.6 %copy-start.1 = (bf16[256,4224]{1,0:T(8,128)(2,1)S(1)}, bf16[256,4224]{1,0:T(8,128)(2,1)}, u32[]{:S(2)}) copy-start(bf16[256,4224]{1,0:T(8,128)(2,1)} %copy-done) | copy-start | bytes 6488068
  118.4 1.6 %copy-start.3 = (bf16[256,4224]{1,0:T(8,128)(2,1)S(1)}, bf16[256,4224]{1,0:T(8,128)(2,1)}, u32[]{:S(2)}) copy-start(bf16[256,4224]{1,0:T(8,128)(2,1)} %copy-done.2) | copy-start | bytes 6488068
  120.0 1.6 %copy-start.5 = (bf16[256,4224]{1,0:T(8,128)(2,1)S(1)}, bf16[256,4224]{1,0:T(8,128)(2,1)}, u32[]{:S(2)}) copy-start(bf16[256,4224]{1,0:T(8,128)(2,1)} %copy-done.4) | copy-start | bytes 6488068
  121.7 1.6 %copy-start.7 = (bf16[256,4224]{1,0:T(8,128)(2,1)S(1)}, bf16[256,4224]{1,0:T(8,128)(2,1)}, u32[]{:S(2)}) copy-start(bf16[256,4224]{1,0:T(8,128)(2,1)} %copy-done.6) | copy-start | bytes 6488068

commit v23 on v20

--- a/solution.py
+++ b/solution.py
@@ -174,7 +174,7 @@
     )(value, *after)
 
 
-def gram_kernel(blocks, rows_ref, *refs):
+def gram_kernel(blocks, rows_ref, other_ref, *refs):
     streams, (own_ref, given_ref, cols_ref) = refs[:4], refs[4:]
     lane = lax.broadcasted_iota(jnp.int32, (16, 128), 1)
     terms = jnp.where(lane < 3, 1.0, 0.0).astype(bf16)
@@ -185,14 +185,13 @@
                 first = slot_of(s, x, z) * 16
                 cols_ref[n * 256 + at : n * 256 + at + 16, :] = streams[s][first : first + 16, :]
         inside = slice(n * 256, (n + 1) * 256)
-        product = lax.dot_general(
-            rows_ref[:, :LIVE],
-            cols_ref[inside, :LIVE],
-            (((1,), (1,)), ((), ())),
-            preferred_element_type=f32,
-        )
-        own_ref[:256, inside] = product[:256]
-        given_ref[:256, inside] = product[256:]
+        for left_ref, into_ref in ((rows_ref, own_ref), (other_ref, given_ref)):
+            into_ref[:256, inside] = lax.dot_general(
+                left_ref[:, :LIVE],
+                cols_ref[inside, :LIVE],
+                (((1,), (1,)), ((), ())),
+                preferred_element_type=f32,
+            )
         sums = lax.dot_general(
             terms, cols_ref[inside, LIVE:], (((1,), (1,)), ((), ())), preferred_element_type=f32
         )
@@ -200,13 +199,13 @@
         given_ref[256:, inside] = sums[:8]
 
 
-def gram(blocks, rows, streams):
+def gram(blocks, rows, other, streams):
     vmem = pl.BlockSpec(memory_space=pltpu.VMEM)
     width = 256 * len(blocks)
     return pl.pallas_call(
         lambda *refs: gram_kernel(blocks, *refs),
         out_shape=(jax.ShapeDtypeStruct((264, width), f32),) * 2,
-        in_specs=[vmem] * 5,
+        in_specs=[vmem] * 6,
         out_specs=(vmem,) * 2,
         scratch_shapes=[pltpu.VMEM((width, LONG), bf16)],
         compiler_params=params(10),
@@ -214,7 +213,7 @@
             flops=2 * 512 * width * LIVE, bytes_accessed=6 * 1024 * 1024, transcendentals=0
         ),
         name="gram",
-    )(rows, *streams)
+    )(rows, other, *streams)
 
 
 def finish_kernel(info_ref, part_ref, *refs):
@@ -311,11 +310,11 @@
         if step == 2:
             rows = meet(behind(rows, streams[:1]), "y", 3, side(y ^ z, 3, False))
 
-    rows = join(rows, swap(rows))
+    other = swap(rows)
 
     own, got = [], []
     for blocks in ((0, 1), (2, 3)):
-        kept, given = gram(blocks, rows, streams)
+        kept, given = gram(blocks, rows, other, streams)
         own.append(kept)
         got.append(swap(given))
     info = jnp.stack([c, z * 8 + x * 2 + c, y * 8]).astype(jnp.int32)

time: 122 us -> 123 us (level)
  waiting for transfers between devices: 36.7 us -> 43.4 us
  starting transfers between devices: 36.7 us -> 31.3 us
    ppermute x21, starting transfers between devices: 29.2 us -> 20.4 us  [trade(): return lax.ppermute(value, axis, [(i, i ^ flip) for i in range(4)])]
    ppermute x21, waiting for transfers between devices: 33.5 us -> 38.7 us  [trade(): return lax.ppermute(value, axis, [(i, i ^ flip) for i in range(4)])]
    ppermute x2, starting transfers between devices: 2.59 us -> 5.94 us  [send(): lax.ppermute(half, ('z', 'y'), [(q * 4 + u, u * 4 + (q ^ u ^ turn)) for q...]
    ppermute x2, waiting for transfers between devices: 0.01 us -> 1.8 us  [send(): lax.ppermute(half, ('z', 'y'), [(q * 4 + u, u * 4 + (q ^ u ^ turn)) for q...]
  transfers between devices with their start and end apart: 26 -> 26, of which waited for: 12 -> 12; matrix products, arithmetic and copies ran while one was open for 4% -> 4% of each run, Pallas kernels for 0% -> 2%
where the time goes in v23:
time: 123 us; the launch traced here: 122 us
  waiting for transfers between devices  43.4 us (35%)
  starting transfers between devices  31.3 us (25%)
  blocking collectives  27 us (22%)
  Pallas kernels  10.4 us (8%)
  other arithmetic  6.68 us (5%)
  local copies, waits for them, and re-layouts  2.05 us (2%)
  between operations  1.65 us (1%)
    ppermute x21, waiting for transfers between devices, trade(): return lax.ppermute(value, axis, [(i, i ^ flip) for i in range(4)])  38.7 us
    all_to_all x1, blocking collectives, per_device(): pieces = lax.all_to_all(pieces, TOK, 0, 0, tiled=True)  27 us
    ppermute x21, starting transfers between devices, trade(): return lax.ppermute(value, axis, [(i, i ^ flip) for i in range(4)])  20.4 us
    ppermute x2, starting transfers between devices, send(): lax.ppermute(half, ('z', 'y'), [(q * 4 + u, u * 4 + (q ^ u ^ turn)) for q...  5.94 us
    ppermute x3, starting transfers between devices, swap(): return lax.ppermute(value, 'c', [(0, 1), (1, 0)])  4.95 us
    pallas_call x2, Pallas kernels, gram(): pl.pallas_call(lambda *refs: gram_kernel(blocks, *refs), out_shape=(jax.S...  4.88 us
    select_n x18, other arithmetic, meet(): jnp.where(which == 0, value, got)  3.02 us
    ppermute x3, waiting for transfers between devices, swap(): return lax.ppermute(value, 'c', [(0, 1), (1, 0)])  2.85 us
  transfers between devices with their start and end apart: 26, of which 12 were waited for; matrix products, arithmetic and copies ran while one was open for 4% of the time, Pallas kernels for 2%

profile of v23, /device:TPU:1, one launch (start us, length us, event | category | flops | bytes accessed | tf_op | source)
XLA Modules:
  0.0 122.4 jit_solution(5042083109652632928)
XLA Ops:
  0.6 0.8 pad_add_fusion
  1.4 1.6 %copy-done = bf16[512,2048]{1,0:T(8,128)(2,1)S(1)} copy-done((bf16[512,2048]{1,0:T(8,128)(2,1)S(1)}, bf16[512,2048]{1,0:T(8,128)(2,1)}, u32[]{:S(2)}) %copy-start) | copy-done | bytes 2097176
  3.0 0.8 pick.1
  3.9 3.6 %collective-permute-start.2 = (f32[8,256]{1,0:T(8,128)S(1)}, f32[8,256]{1,0:T(8,128)S(1)}, u32[]{:S(2)}, u32[]{:S(2)}) collective-permute-start(f32[8,256]{1,0:T(8,128)S(1)} %get-tuple-element.17.s0), channel_id=1, source_target_pairs={{0,3},{1,2},{2,1},{3,0},{4,7},{5,6},{6,5},{7,4},{8,11},{9,10},{10,... | collective-permute-start | bytes 24584 | tf_op jit(solution)/shard_map/ppermute | solution.py:268
  7.5 0.4 collective-permute-start.1
  7.9 0.3 collective-permute-start
  8.2 0.4 copy.7.gain_ref
  8.6 3.0 %collective-permute-done.1.s2 = f32[8,256]{1,0:T(8,128)S(1)} collective-permute-done((f32[8,256]{1,0:T(8,128)S(1)}, f32[8,256]{1,0:T(8,128)S(1)}, u32[]{:S(2)}, u32[]{:S(2)}) %collective-permute-start.1) | collective-permute-done | bytes 8224 | tf_op jit(solution)/shard_map/ppermute | solution.py:268
  11.5 0.3 norm.1
  11.9 27.0 %all_to_all.5.in_ref = bf16[32,64,256]{2,1,0:T(8,128)(2,1)S(1)} all-to-all(bf16[32,64,256]{2,1,0:T(8,128)(2,1)S(1)} %norm.1), channel_id=1, replica_groups=mesh['z'=4,'x'=4,'c'=2,'y'=4] {'z','x','c'}, dimensions={0} | all-to-all | bytes 2097152 | tf_op jit(solution)/shard_map/all_to_all | solution.py:286
  38.9 1.2 fusion
  40.4 2.1 %pack.1 = (bf16[32,4224]{1,0:T(8,128)(2,1)S(1)}, bf16[32,4224]{1,0:T(8,128)(2,1)S(1)}, bf16[16,4224]{1,0:T(8,128)(2,1)S(1)}, bf16[16,4224]{1,0:T(8,128)(2,1)S(1)...) custom-call(s32[32]{0:T(128)S(1)} %sub.3.first_ref, bf16[32,64,256]{2,1,0:T(8,128)(2,1)S(1)} %all_to_all.5.in_ref), custom_call_target="tpu_custom_call" | custom-call | tf_op jit(solution)/shard_map/pack/pallas_call | solution.py:149
  42.4 0.4 collective-permute-start.3
  42.9 0.4 collective-permute-start.5
  43.3 1.0 collective-permute-start.6
  44.3 0.6 collective-permute-start.7
  44.9 2.4 %collective-permute-done.3 = bf16[16,4224]{1,0:T(8,128)(2,1)S(1)} collective-permute-done((bf16[16,4224]{1,0:T(8,128)(2,1)S(1)}, bf16[16,4224]{1,0:T(8,128)(2,1)S(1)}, u32[]{:S(2)}, u32[]{:S(2)}) %collective-permute-start.3) | collective-permute-done | bytes 135200 | tf_op jit(solution)/shard_map/ppermute | solution.py:268
  47.5 1.7 %collective-permute-start.10 = (bf16[32,4224]{1,0:T(8,128)(2,1)S(1)}, bf16[32,4224]{1,0:T(8,128)(2,1)S(1)}, u32[]{:S(2)}, u32[]{:S(2)}) collective-permute-start(bf16[32,4224]{1,0:T(8,128)(2,1)S(1)} %get-tuple-element.69.refs_1_), channel_id=1, source_target_pairs={{0,24},{8,16},{16,8},{24,0},{1,25},{9,17},{17,9},{25,1},{2,26},{10... | collective-permute-start | bytes 811016 | tf_op jit(solution)/shard_map/ppermute | solution.py:268
  49.2 0.2 collective-permute-done.6
  49.7 1.3 %collective-permute-start.11 = (bf16[32,4224]{1,0:T(8,128)(2,1)S(1)}, bf16[32,4224]{1,0:T(8,128)(2,1)S(1)}, u32[]{:S(2)}, u32[]{:S(2)}) collective-permute-start(bf16[32,4224]{1,0:T(8,128)(2,1)S(1)} %get-tuple-element.70.refs_2_), channel_id=1, source_target_pairs={{0,96},{32,64},{64,32},{96,0},{1,97},{33,65},{65,33},{97,1},{2,98}... | collective-permute-start | bytes 811016 | tf_op jit(solution)/shard_map/ppermute | solution.py:268
  51.0 0.3 collective-permute-start.12
  51.5 0.7 collective-permute-start.4
  52.2 3.1 %collective-permute-done.10 = bf16[32,4224]{1,0:T(8,128)(2,1)S(1)} collective-permute-done((bf16[32,4224]{1,0:T(8,128)(2,1)S(1)}, bf16[32,4224]{1,0:T(8,128)(2,1)S(1)}, u32[]{:S(2)}, u32[]{:S(2)}) %collective-permute-start.10) | collective-permute-done | bytes 270368 | tf_op jit(solution)/shard_map/ppermute | solution.py:268
  55.3 5.3 %collective-permute-start.8 = (bf16[32,4224]{1,0:T(8,128)(2,1)S(1)}, bf16[32,4224]{1,0:T(8,128)(2,1)S(1)}, u32[]{:S(2)}, u32[]{:S(2)}) collective-permute-start(bf16[32,4224]{1,0:T(8,128)(2,1)S(1)} %behind.5), channel_id=1, source_target_pairs={{0,2},{1,35},{2,64},{3,97},{32,3},{33,34},{34,65},{35,96},{64,0},{... | collective-permute-start | bytes 811016 | tf_op jit(solution)/shard_map/ppermute | solution.py:296
  61.0 1.2 collective-permute-start.14
  62.3 0.7 collective-permute-start.20
  63.2 0.4 collective-permute-start.22
  63.6 1.8 %collective-permute-done.8 = bf16[32,4224]{1,0:T(8,128)(2,1)S(1)} collective-permute-done((bf16[32,4224]{1,0:T(8,128)(2,1)S(1)}, bf16[32,4224]{1,0:T(8,128)(2,1)S(1)}, u32[]{:S(2)}, u32[]{:S(2)}) %collective-permute-start.8) | collective-permute-done | bytes 270368 | tf_op jit(solution)/shard_map/ppermute | solution.py:296
  65.5 1.5 %collective-permute-start.13 = (bf16[64,4224]{1,0:T(8,128)(2,1)S(1)}, bf16[64,4224]{1,0:T(8,128)(2,1)S(1)}, u32[]{:S(2)}, u32[]{:S(2)}) collective-permute-start(bf16[64,4224]{1,0:T(8,128)(2,1)S(1)} %behind.6), channel_id=1, source_target_pairs={{0,1},{1,0},{2,3},{3,2},{4,5},{5,4},{6,7},{7,6},{8,9},{9,8},{10,11... | collective-permute-start | bytes 1622024 | tf_op jit(solution)/shard_map/ppermute | solution.py:268
  67.0 6.3 %collective-permute-done.14 = bf16[64,4224]{1,0:T(8,128)(2,1)S(1)} collective-permute-done((bf16[64,4224]{1,0:T(8,128)(2,1)S(1)}, bf16[64,4224]{1,0:T(8,128)(2,1)S(1)}, u32[]{:S(2)}, u32[]{:S(2)}) %collective-permute-start.14) | collective-permute-done | bytes 540704 | tf_op jit(solution)/shard_map/ppermute | solution.py:268
  73.6 2.5 %collective-permute-start.17 = (bf16[128,4224]{1,0:T(8,128)(2,1)S(1)}, bf16[128,4224]{1,0:T(8,128)(2,1)S(1)}, u32[]{:S(2)}, u32[]{:S(2)}) collective-permute-start(bf16[128,4224]{1,0:T(8,128)(2,1)S(1)} %pad_maximum_fusion.6.refs_0_), channel_id=1, source_target_pairs={{0,96},{32,64},{64,32},{96,0},{1,97},{33,65},{65,33},{97,1},{2,98}... | collective-permute-start | bytes 3244040 | tf_op jit(solution)/shard_map/ppermute | solution.py:268
  76.3 2.9 %collective-permute-done.18 = bf16[64,4224]{1,0:T(8,128)(2,1)S(1)} collective-permute-done((bf16[64,4224]{1,0:T(8,128)(2,1)S(1)}, bf16[64,4224]{1,0:T(8,128)(2,1)S(1)}, u32[]{:S(2)}, u32[]{:S(2)}) %collective-permute-start.18) | collective-permute-done | bytes 540704 | tf_op jit(solution)/shard_map/ppermute | solution.py:268
  79.9 1.1 collective-permute-start.21
  81.2 2.6 %collective-permute-start.23 = (bf16[128,4224]{1,0:T(8,128)(2,1)S(1)}, bf16[128,4224]{1,0:T(8,128)(2,1)S(1)}, u32[]{:S(2)}, u32[]{:S(2)}) collective-permute-start(bf16[128,4224]{1,0:T(8,128)(2,1)S(1)} %pad_maximum_fusion.9), channel_id=1, source_target_pairs={{0,24},{8,16},{16,8},{24,0},{1,25},{9,17},{17,9},{25,1},{2,26},{10... | collective-permute-start | bytes 3244040 | tf_op jit(solution)/shard_map/ppermute | solution.py:268
  83.8 20.6 %collective-permute-done.15 = bf16[128,4224]{1,0:T(8,128)(2,1)S(1)} collective-permute-done((bf16[128,4224]{1,0:T(8,128)(2,1)S(1)}, bf16[128,4224]{1,0:T(8,128)(2,1)S(1)}, u32[]{:S(2)}, u32[]{:S(2)}) %collective-permute-start.15) | collective-permute-done | bytes 1081376 | tf_op jit(solution)/shard_map/ppermute | solution.py:268
  104.4 0.2 broadcast_select_fusion.9
  104.8 4.3 %collective-permute-start.16 = (bf16[256,4224]{1,0:T(8,128)(2,1)S(1)}, bf16[256,4224]{1,0:T(8,128)(2,1)S(1)}, u32[]{:S(2)}, u32[]{:S(2)}) collective-permute-start(bf16[256,4224]{1,0:T(8,128)(2,1)S(1)} %pad_maximum_fusion.refs_0_), channel_id=1, source_target_pairs={{0,4},{4,0},{1,5},{5,1},{2,6},{6,2},{3,7},{7,3},{8,12},{12,8},{9,1... | collective-permute-start | bytes 6488072 | tf_op jit(solution)/shard_map/ppermute | solution.py:264
  109.1 0.4 broadcast_select_fusion.5
  109.6 0.4 broadcast_select_fusion.3
  110.0 0.4 broadcast_select_fusion.1
  110.7 0.4 broadcast_select_fusion.7
  111.2 1.7 %collective-permute-done.16.refs_1_ = bf16[256,4224]{1,0:T(8,128)(2,1)S(1)} collective-permute-done((bf16[256,4224]{1,0:T(8,128)(2,1)S(1)}, bf16[256,4224]{1,0:T(8,128)(2,1)S(1)}, u32[]{:S(2)}, u32[]{:S(2)}) %collective-permute-start.16) | collective-permute-done | bytes 2162720 | tf_op jit(solution)/shard_map/ppermute | solution.py:264
  112.9 2.4 %gram.3 = (f32[264,512]{1,0:T(8,128)S(1)}, f32[264,512]{1,0:T(8,128)S(1)}) custom-call(bf16[256,4224]{1,0:T(8,128)(2,1)S(1)} %pad_maximum_fusion.refs_0_, bf16[256,4224]{1,0:T(8,128)(2,1)S(1)} %collective-permute-done.16.refs_1_, bf16[256,4224]{1,0:T(8,128)(2,1)S(1)} %pad_maximum_fusion.1.refs_2_, bf16[256,4224]{1,0:T(8,128)(2,1)S(1)} %pad_maximum_fusion.2.refs_3_, ...), custom_call_target="tpu_custom_call" | custom-call | flops 2147483648 | bytes 6291456 | tf_op jit(solution)/shard_map/gram/pallas_call | solution.py:205
  115.4 0.5 collective-permute-start.25
  115.8 2.4 %gram.2 = (f32[264,512]{1,0:T(8,128)S(1)}, f32[264,512]{1,0:T(8,128)S(1)}) custom-call(bf16[256,4224]{1,0:T(8,128)(2,1)S(1)} %pad_maximum_fusion.refs_0_, bf16[256,4224]{1,0:T(8,128)(2,1)S(1)} %collective-permute-done.16.refs_1_, bf16[256,4224]{1,0:T(8,128)(2,1)S(1)} %pad_maximum_fusion.1.refs_2_, bf16[256,4224]{1,0:T(8,128)(2,1)S(1)} %pad_maximum_fusion.2.refs_3_, ...), custom_call_target="tpu_custom_call" | custom-call | flops 2147483648 | bytes 6291456 | tf_op jit(solution)/shard_map/gram/pallas_call | solution.py:205
  118.3 0.2 collective-permute-start.24
  119.2 1.1 collective-permute-done.24.refs_2_
  120.3 2.1 %finish.1 = (f32[1,2048]{1,0:T(1,128)}, f32[256,2048]{1,0:T(8,128)}) custom-call(s32[3]{0:T(128)S(1)} %pad_add_fusion.1.info_ref, f32[1]{0:T(128)} %bitcast.4.part_ref, f32[264,512]{1,0:T(8,128)S(1)} %get-tuple-element.24.refs_0_, f32[264,512]{1,0:T(8,128)S(1)} %get-tuple-element.25.refs_1_, f32[264,512]{1,0:T(8,128)S(1)} %collective-permute-done.24.refs_2_, ...), custom_call_target="tpu_custom_call" | custom-call | tf_op jit(solution)/shard_map/finish/pallas_call | solution.py:250
  (64 shorter events, 3.9 us)
Async XLA Ops:
  0.6 7.6 %copy-start.1 = (f32[2048]{0:T(1024)S(1)}, f32[2048]{0:T(1024)}, u32[]{:S(2)}) copy-start(f32[2048]{0:T(1024)} %param.5) | copy-start | bytes 24580
  1.4 1.6 %copy-start = (bf16[512,2048]{1,0:T(8,128)(2,1)S(1)}, bf16[512,2048]{1,0:T(8,128)(2,1)}, u32[]{:S(2)}) copy-start(bf16[512,2048]{1,0:T(8,128)(2,1)} %resid_ref.1) | copy-start | bytes 6291460
  3.9 4.7 %collective-permute-start.2 = (f32[8,256]{1,0:T(8,128)S(1)}, f32[8,256]{1,0:T(8,128)S(1)}, u32[]{:S(2)}, u32[]{:S(2)}) collective-permute-start(f32[8,256]{1,0:T(8,128)S(1)} %get-tuple-element.17.s0), channel_id=1, source_target_pairs={{0,3},{1,2},{2,1},{3,0},{4,7},{5,6},{6,5},{7,4},{8,11},{9,10},{10,... | collective-permute-start | bytes 24584 | tf_op jit(solution)/shard_map/ppermute | solution.py:268
  7.5 4.0 %collective-permute-start.1 = (f32[8,256]{1,0:T(8,128)S(1)}, f32[8,256]{1,0:T(8,128)S(1)}, u32[]{:S(2)}, u32[]{:S(2)}) collective-permute-start(f32[8,256]{1,0:T(8,128)S(1)} %get-tuple-element.17.s0), channel_id=1, source_target_pairs={{0,2},{1,3},{2,0},{3,1},{4,6},{5,7},{6,4},{7,5},{8,10},{9,11},{10,... | collective-permute-start | bytes 24584 | tf_op jit(solution)/shard_map/ppermute | solution.py:268
  7.9 3.7 %collective-permute-start = (f32[8,256]{1,0:T(8,128)S(1)}, f32[8,256]{1,0:T(8,128)S(1)}, u32[]{:S(2)}, u32[]{:S(2)}) collective-permute-start(f32[8,256]{1,0:T(8,128)S(1)} %get-tuple-element.17.s0), channel_id=1, source_target_pairs={{0,1},{1,0},{2,3},{3,2},{4,5},{5,4},{6,7},{7,6},{8,9},{9,8},{10,11... | collective-permute-start | bytes 24584 | tf_op jit(solution)/shard_map/ppermute | solution.py:268
  42.4 4.9 %collective-permute-start.3 = (bf16[16,4224]{1,0:T(8,128)(2,1)S(1)}, bf16[16,4224]{1,0:T(8,128)(2,1)S(1)}, u32[]{:S(2)}, u32[]{:S(2)}) collective-permute-start(bf16[16,4224]{1,0:T(8,128)(2,1)S(1)} %get-tuple-element.19), channel_id=1, source_target_pairs={{0,8},{8,0},{16,24},{24,16},{1,9},{9,1},{17,25},{25,17},{2,10},{10... | collective-permute-start | bytes 405512 | tf_op jit(solution)/shard_map/ppermute | solution.py:268
  42.9 4.5 %collective-permute-start.5 = (bf16[16,4224]{1,0:T(8,128)(2,1)S(1)}, bf16[16,4224]{1,0:T(8,128)(2,1)S(1)}, u32[]{:S(2)}, u32[]{:S(2)}) collective-permute-start(bf16[16,4224]{1,0:T(8,128)(2,1)S(1)} %get-tuple-element.21), channel_id=1, source_target_pairs={{0,32},{32,0},{64,96},{96,64},{1,33},{33,1},{65,97},{97,65},{2,34}... | collective-permute-start | bytes 405512 | tf_op jit(solution)/shard_map/ppermute | solution.py:268
  43.3 6.2 %collective-permute-start.6 = (bf16[16,4224]{1,0:T(8,128)(2,1)S(1)}, bf16[16,4224]{1,0:T(8,128)(2,1)S(1)}, u32[]{:S(2)}, u32[]{:S(2)}) collective-permute-start(bf16[16,4224]{1,0:T(8,128)(2,1)S(1)} %get-tuple-element.22), channel_id=1, source_target_pairs={{0,24},{8,16},{16,8},{24,0},{1,25},{9,17},{17,9},{25,1},{2,26},{10... | collective-permute-start | bytes 405512 | tf_op jit(solution)/shard_map/ppermute | solution.py:268
  44.3 5.4 %collective-permute-start.7 = (bf16[16,4224]{1,0:T(8,128)(2,1)S(1)}, bf16[16,4224]{1,0:T(8,128)(2,1)S(1)}, u32[]{:S(2)}, u32[]{:S(2)}) collective-permute-start(bf16[16,4224]{1,0:T(8,128)(2,1)S(1)} %get-tuple-element.23), channel_id=1, source_target_pairs={{0,96},{32,64},{64,32},{96,0},{1,97},{33,65},{65,33},{97,1},{2,98}... | collective-permute-start | bytes 405512 | tf_op jit(solution)/shard_map/ppermute | solution.py:268
  47.5 7.8 %collective-permute-start.10 = (bf16[32,4224]{1,0:T(8,128)(2,1)S(1)}, bf16[32,4224]{1,0:T(8,128)(2,1)S(1)}, u32[]{:S(2)}, u32[]{:S(2)}) collective-permute-start(bf16[32,4224]{1,0:T(8,128)(2,1)S(1)} %get-tuple-element.69.refs_1_), channel_id=1, source_target_pairs={{0,24},{8,16},{16,8},{24,0},{1,25},{9,17},{17,9},{25,1},{2,26},{10... | collective-permute-start | bytes 811016 | tf_op jit(solution)/shard_map/ppermute | solution.py:268
  49.7 11.2 %collective-permute-start.11 = (bf16[32,4224]{1,0:T(8,128)(2,1)S(1)}, bf16[32,4224]{1,0:T(8,128)(2,1)S(1)}, u32[]{:S(2)}, u32[]{:S(2)}) collective-permute-start(bf16[32,4224]{1,0:T(8,128)(2,1)S(1)} %get-tuple-element.70.refs_2_), channel_id=1, source_target_pairs={{0,96},{32,64},{64,32},{96,0},{1,97},{33,65},{65,33},{97,1},{2,98}... | collective-permute-start | bytes 811016 | tf_op jit(solution)/shard_map/ppermute | solution.py:268
  51.0 11.3 %collective-permute-start.12 = (bf16[32,4224]{1,0:T(8,128)(2,1)S(1)}, bf16[32,4224]{1,0:T(8,128)(2,1)S(1)}, u32[]{:S(2)}, u32[]{:S(2)}) collective-permute-start(bf16[32,4224]{1,0:T(8,128)(2,1)S(1)} %get-tuple-element.71.refs_3_), channel_id=1, source_target_pairs={{0,8},{8,0},{16,24},{24,16},{1,9},{9,1},{17,25},{25,17},{2,10},{10... | collective-permute-start | bytes 811016 | tf_op jit(solution)/shard_map/ppermute | solution.py:268
  51.4 9.4 %collective-permute-start.9 = (bf16[32,4224]{1,0:T(8,128)(2,1)S(1)}, bf16[32,4224]{1,0:T(8,128)(2,1)S(1)}, u32[]{:S(2)}, u32[]{:S(2)}) collective-permute-start(bf16[32,4224]{1,0:T(8,128)(2,1)S(1)} %get-tuple-element.68.refs_0_), channel_id=1, source_target_pairs={{0,32},{32,0},{64,96},{96,64},{1,33},{33,1},{65,97},{97,65},{2,34}... | collective-permute-start | bytes 811016 | tf_op jit(solution)/shard_map/ppermute | solution.py:268
  51.5 11.6 %collective-permute-start.4 = (bf16[32,4224]{1,0:T(8,128)(2,1)S(1)}, bf16[32,4224]{1,0:T(8,128)(2,1)S(1)}, u32[]{:S(2)}, u32[]{:S(2)}) collective-permute-start(bf16[32,4224]{1,0:T(8,128)(2,1)S(1)} %behind.4), channel_id=1, source_target_pairs={{0,0},{1,33},{2,66},{3,99},{32,1},{33,32},{34,67},{35,98},{64,2},{... | collective-permute-start | bytes 811016 | tf_op jit(solution)/shard_map/ppermute | solution.py:296
  55.3 10.1 %collective-permute-start.8 = (bf16[32,4224]{1,0:T(8,128)(2,1)S(1)}, bf16[32,4224]{1,0:T(8,128)(2,1)S(1)}, u32[]{:S(2)}, u32[]{:S(2)}) collective-permute-start(bf16[32,4224]{1,0:T(8,128)(2,1)S(1)} %behind.5), channel_id=1, source_target_pairs={{0,2},{1,35},{2,64},{3,97},{32,3},{33,34},{34,65},{35,96},{64,0},{... | collective-permute-start | bytes 811016 | tf_op jit(solution)/shard_map/ppermute | solution.py:296
  60.7 18.5 %collective-permute-start.18 = (bf16[64,4224]{1,0:T(8,128)(2,1)S(1)}, bf16[64,4224]{1,0:T(8,128)(2,1)S(1)}, u32[]{:S(2)}, u32[]{:S(2)}) collective-permute-start(bf16[64,4224]{1,0:T(8,128)(2,1)S(1)} %pad_maximum_fusion.12.refs_1_), channel_id=1, source_target_pairs={{0,96},{32,64},{64,32},{96,0},{1,97},{33,65},{65,33},{97,1},{2,98}... | collective-permute-start | bytes 1622024 | tf_op jit(solution)/shard_map/ppermute | solution.py:268
  61.0 12.3 %collective-permute-start.14 = (bf16[64,4224]{1,0:T(8,128)(2,1)S(1)}, bf16[64,4224]{1,0:T(8,128)(2,1)S(1)}, u32[]{:S(2)}, u32[]{:S(2)}) collective-permute-start(bf16[64,4224]{1,0:T(8,128)(2,1)S(1)} %pad_maximum_fusion.11.refs_0_), channel_id=1, source_target_pairs={{0,24},{8,16},{16,8},{24,0},{1,25},{9,17},{17,9},{25,1},{2,26},{10... | collective-permute-start | bytes 1622024 | tf_op jit(solution)/shard_map/ppermute | solution.py:268
  62.3 17.3 %collective-permute-start.20 = (bf16[64,4224]{1,0:T(8,128)(2,1)S(1)}, bf16[64,4224]{1,0:T(8,128)(2,1)S(1)}, u32[]{:S(2)}, u32[]{:S(2)}) collective-permute-start(bf16[64,4224]{1,0:T(8,128)(2,1)S(1)} %pad_maximum_fusion.13.refs_2_), channel_id=1, source_target_pairs={{0,8},{8,0},{16,24},{24,16},{1,9},{9,1},{17,25},{25,17},{2,10},{10... | collective-permute-start | bytes 1622024 | tf_op jit(solution)/shard_map/ppermute | solution.py:268
  63.2 17.8 %collective-permute-start.22 = (bf16[64,4224]{1,0:T(8,128)(2,1)S(1)}, bf16[64,4224]{1,0:T(8,128)(2,1)S(1)}, u32[]{:S(2)}, u32[]{:S(2)}) collective-permute-start(bf16[64,4224]{1,0:T(8,128)(2,1)S(1)} %pad_maximum_fusion.14.refs_3_), channel_id=1, source_target_pairs={{0,32},{32,0},{64,96},{96,64},{1,33},{33,1},{65,97},{97,65},{2,34}... | collective-permute-start | bytes 1622024 | tf_op jit(solution)/shard_map/ppermute | solution.py:268
  65.5 10.5 %collective-permute-start.13 = (bf16[64,4224]{1,0:T(8,128)(2,1)S(1)}, bf16[64,4224]{1,0:T(8,128)(2,1)S(1)}, u32[]{:S(2)}, u32[]{:S(2)}) collective-permute-start(bf16[64,4224]{1,0:T(8,128)(2,1)S(1)} %behind.6), channel_id=1, source_target_pairs={{0,1},{1,0},{2,3},{3,2},{4,5},{5,4},{6,7},{7,6},{8,9},{9,8},{10,11... | collective-permute-start | bytes 1622024 | tf_op jit(solution)/shard_map/ppermute | solution.py:268
  73.6 37.1 %collective-permute-start.17 = (bf16[128,4224]{1,0:T(8,128)(2,1)S(1)}, bf16[128,4224]{1,0:T(8,128)(2,1)S(1)}, u32[]{:S(2)}, u32[]{:S(2)}) collective-permute-start(bf16[128,4224]{1,0:T(8,128)(2,1)S(1)} %pad_maximum_fusion.6.refs_0_), channel_id=1, source_target_pairs={{0,96},{32,64},{64,32},{96,0},{1,97},{33,65},{65,33},{97,1},{2,98}... | collective-permute-start | bytes 3244040 | tf_op jit(solution)/shard_map/ppermute | solution.py:268
  79.5 29.6 %collective-permute-start.19 = (bf16[128,4224]{1,0:T(8,128)(2,1)S(1)}, bf16[128,4224]{1,0:T(8,128)(2,1)S(1)}, u32[]{:S(2)}, u32[]{:S(2)}) collective-permute-start(bf16[128,4224]{1,0:T(8,128)(2,1)S(1)} %pad_maximum_fusion.7), channel_id=1, source_target_pairs={{0,8},{8,0},{16,24},{24,16},{1,9},{9,1},{17,25},{25,17},{2,10},{10... | collective-permute-start | bytes 3244040 | tf_op jit(solution)/shard_map/ppermute | solution.py:268
  79.9 29.7 %collective-permute-start.21 = (bf16[128,4224]{1,0:T(8,128)(2,1)S(1)}, bf16[128,4224]{1,0:T(8,128)(2,1)S(1)}, u32[]{:S(2)}, u32[]{:S(2)}) collective-permute-start(bf16[128,4224]{1,0:T(8,128)(2,1)S(1)} %pad_maximum_fusion.8), channel_id=1, source_target_pairs={{0,32},{32,0},{64,96},{96,64},{1,33},{33,1},{65,97},{97,65},{2,34}... | collective-permute-start | bytes 3244040 | tf_op jit(solution)/shard_map/ppermute | solution.py:268
  80.9 23.5 %collective-permute-start.15 = (bf16[128,4224]{1,0:T(8,128)(2,1)S(1)}, bf16[128,4224]{1,0:T(8,128)(2,1)S(1)}, u32[]{:S(2)}, u32[]{:S(2)}) collective-permute-start(bf16[128,4224]{1,0:T(8,128)(2,1)S(1)} %behind.7), channel_id=1, source_target_pairs={{0,3},{1,2},{2,1},{3,0},{4,7},{5,6},{6,5},{7,4},{8,11},{9,10},{10,... | collective-permute-start | bytes 3244040 | tf_op jit(solution)/shard_map/ppermute | solution.py:268
  81.2 28.8 %collective-permute-start.23 = (bf16[128,4224]{1,0:T(8,128)(2,1)S(1)}, bf16[128,4224]{1,0:T(8,128)(2,1)S(1)}, u32[]{:S(2)}, u32[]{:S(2)}) collective-permute-start(bf16[128,4224]{1,0:T(8,128)(2,1)S(1)} %pad_maximum_fusion.9), channel_id=1, source_target_pairs={{0,24},{8,16},{16,8},{24,0},{1,25},{9,17},{17,9},{25,1},{2,26},{10... | collective-permute-start | bytes 3244040 | tf_op jit(solution)/shard_map/ppermute | solution.py:268
  104.8 8.2 %collective-permute-start.16 = (bf16[256,4224]{1,0:T(8,128)(2,1)S(1)}, bf16[256,4224]{1,0:T(8,128)(2,1)S(1)}, u32[]{:S(2)}, u32[]{:S(2)}) collective-permute-start(bf16[256,4224]{1,0:T(8,128)(2,1)S(1)} %pad_maximum_fusion.refs_0_), channel_id=1, source_target_pairs={{0,4},{4,0},{1,5},{5,1},{2,6},{6,2},{3,7},{7,3},{8,12},{12,8},{9,1... | collective-permute-start | bytes 6488072 | tf_op jit(solution)/shard_map/ppermute | solution.py:264
  115.4 3.8 %collective-permute-start.25 = (f32[264,512]{1,0:T(8,128)S(1)}, f32[264,512]{1,0:T(8,128)S(1)}, u32[]{:S(2)}, u32[]{:S(2)}) collective-permute-start(f32[264,512]{1,0:T(8,128)S(1)} %get-tuple-element.27), channel_id=1, source_target_pairs={{0,4},{4,0},{1,5},{5,1},{2,6},{6,2},{3,7},{7,3},{8,12},{12,8},{9,1... | collective-permute-start | bytes 1622024 | tf_op jit(solution)/shard_map/ppermute | solution.py:264
  118.3 2.0 %collective-permute-start.24 = (f32[264,512]{1,0:T(8,128)S(1)}, f32[264,512]{1,0:T(8,128)S(1)}, u32[]{:S(2)}, u32[]{:S(2)}) collective-permute-start(f32[264,512]{1,0:T(8,128)S(1)} %get-tuple-element.26), channel_id=1, source_target_pairs={{0,4},{4,0},{1,5},{5,1},{2,6},{6,2},{3,7},{7,3},{8,12},{12,8},{9,1... | collective-permute-start | bytes 1622024 | tf_op jit(solution)/shard_map/ppermute | solution.py:264
